TPU v7x, 32 devices: a whole 2x2x4 slice. The times are simulated.
32 devices in a mesh: dp: 8 (over z, y), group: 4 (over x, core).
Axes of the slice: x: 2, y: 2, z: 4, core: 2. Of those that a mesh axis runs over, the one named last changes fastest.
Arguments:
- patches: bfloat16 [192, 144, 640], P(('dp', 'group')), may hold values from -6 to 6
- vis_index: int32 [192, 3, 48], P(('dp', 'group')), may hold values from 0 to 143, as said below
- vis_count: int32 [192, 3], P(('dp', 'group')), may hold values from 24 to 48, as said below
- w_stem: bfloat16 [640, 1024], replicated, may hold values from -0.375 to 0.375
- ln_gain: float32 [1024], replicated, may hold values from 0.5 to 1.5
- w_qkv: bfloat16 [1024, 3, 1024], P('dp', None, 'group'), may hold values from -7.5 to 7.5
- w_out: bfloat16 [1024, 1024], P('group', 'dp'), may hold values from -0.1875 to 0.1875
- out_grad: bfloat16 [192, 3, 48, 1024], P(('dp', 'group')), may hold values from -6 to 6
Outputs:
- output: bfloat16 [192, 3, 48, 1024], P(('dp', 'group'))
- grad_w_stem: float32 [640, 1024], replicated
- grad_w_qkv: float32 [1024, 3, 1024], P('dp', None, 'group')
- grad_w_out: float32 [1024, 1024], P('group', 'dp')
Inputs may be any that keep to these rules, and one draw needn't show every extreme that they name: `vis_index`: for each scene and band group the 48 entries are distinct patch numbers; only the first vis_count entries are visible tokens, the rest are padding. `vis_count`: equals 48 for at least one scene and band group of every draw.
All inputs are finite; a program needn't handle non-finite values.
Results may differ from a plain program's by a relative error of at most 0.0025.
The roundings to bfloat16 on the way count: a program that leaves them out, or rounds other values in their place, can miss the bound.
Values may be sent and summed in bfloat16 or wider, within the bound.
No kernel may reach another device: no remote copies, remote signals or barrier semaphores. Data moves between devices by JAX's collectives and lax.ppermute only.
A program may use at most 192 MiB of HBM per device.

v0:
```python
import jax
import jax.numpy as jnp
from jax import lax
from jax.sharding import PartitionSpec as P

D = 1024
HD = 64
GROUPS = 3
CAP = 48
GRID = 12
PIX = 64


GROUP_BANDS = ((0, 4), (4, 8), (8, 10))
NORM_EPS = 1e-06


def encodings(patch_ids, group_id):
    quarter = D // 4
    half_width = D // 2
    row_freq = jnp.power(10000.0, -jnp.arange(quarter, dtype=jnp.float32) / quarter)
    group_freq = jnp.power(10000.0, -jnp.arange(half_width, dtype=jnp.float32) / half_width)
    row_at = (patch_ids // GRID).astype(jnp.float32)[..., None] * row_freq
    col_at = (patch_ids % GRID).astype(jnp.float32)[..., None] * row_freq
    spatial = jnp.concatenate(
        [jnp.sin(row_at), jnp.cos(row_at), jnp.sin(col_at), jnp.cos(col_at)], axis=-1
    )
    group_at = float(group_id) * group_freq
    return spatial + jnp.concatenate([jnp.sin(group_at), jnp.cos(group_at)])


def embed_tokens(patches, vis_index, w_stem):
    scene_count = patches.shape[0]
    flat_ids = vis_index.reshape(scene_count, GROUPS * CAP)
    picked = jnp.take_along_axis(patches, flat_ids[:, :, None], axis=1)
    pieces = []
    for group_id, (band_start, band_end) in enumerate(GROUP_BANDS):
        columns = picked[
            :, group_id * CAP : (group_id + 1) * CAP, band_start * PIX : band_end * PIX
        ]
        weights = w_stem[band_start * PIX : band_end * PIX]
        summed = jnp.einsum("str,rd->std", columns, weights, preferred_element_type=jnp.float32)
        pieces.append((summed + encodings(vis_index[:, group_id], group_id)).astype(jnp.bfloat16))
    return (jnp.stack(pieces, axis=1), picked)


def layer_norm(embedded, ln_gain):
    values = embedded.astype(jnp.float32)
    centre = jnp.mean(values, axis=-1, keepdims=True)
    spread = jnp.mean(jnp.square(values - centre), axis=-1, keepdims=True)
    inv_std = lax.rsqrt(spread + NORM_EPS)
    centred = (values - centre) * inv_std
    return ((centred * ln_gain).astype(jnp.bfloat16), centred, inv_std)


def norm_back(grad_normed, centred, inv_std, ln_gain):
    scaled = grad_normed * ln_gain
    first_mean = jnp.mean(scaled, axis=-1, keepdims=True)
    second_mean = jnp.mean(scaled * centred, axis=-1, keepdims=True)
    return inv_std * (scaled - first_mean - centred * second_mean)


def attend_forward(normed, key_flags, w_cols):
    scene_count, token_count, _ = normed.shape
    width = w_cols.shape[2]
    head_count = width // HD
    qkv = jnp.einsum("ntd,dcw->ntcw", normed, w_cols, preferred_element_type=jnp.float32).astype(
        jnp.bfloat16
    )
    query_rows = qkv[:, :, 0].reshape(scene_count, token_count, head_count, HD)
    key_rows = qkv[:, :, 1].reshape(scene_count, token_count, head_count, HD)
    value_rows = qkv[:, :, 2].reshape(scene_count, token_count, head_count, HD)
    scores = jnp.einsum(
        "nqhe,nkhe->nhqk", query_rows, key_rows, preferred_element_type=jnp.float32
    ) * HD ** (-0.5)
    scores = jnp.where(key_flags[:, None, None, :], scores, -1e30)
    row_top = jnp.max(scores, axis=-1, keepdims=True)
    lifted = jnp.exp(scores - row_top)
    attn_probs = lifted / jnp.sum(lifted, axis=-1, keepdims=True)
    probs_half = attn_probs.astype(jnp.bfloat16)
    context = jnp.einsum(
        "nhqk,nkhe->nqhe", probs_half, value_rows, preferred_element_type=jnp.float32
    )
    context = context.astype(jnp.bfloat16).reshape(scene_count, token_count, width)
    return (qkv, attn_probs, probs_half, context)


def attend_backward(grad_rows, normed, w_cols, w_head_rows, qkv, attn_probs, probs_half, context):
    scene_count, token_count, _ = normed.shape
    width = w_cols.shape[2]
    head_count = width // HD
    grad_out_w = jnp.einsum("ntw,ntd->wd", context, grad_rows, preferred_element_type=jnp.float32)
    grad_context = jnp.einsum(
        "ntd,wd->ntw", grad_rows, w_head_rows, preferred_element_type=jnp.float32
    )
    grad_context = grad_context.astype(jnp.bfloat16).reshape(
        scene_count, token_count, head_count, HD
    )
    query_rows = qkv[:, :, 0].reshape(scene_count, token_count, head_count, HD)
    key_rows = qkv[:, :, 1].reshape(scene_count, token_count, head_count, HD)
    value_rows = qkv[:, :, 2].reshape(scene_count, token_count, head_count, HD)
    grad_probs = jnp.einsum(
        "nqhe,nkhe->nhqk", grad_context, value_rows, preferred_element_type=jnp.float32
    )
    grad_value = jnp.einsum(
        "nhqk,nqhe->nkhe", probs_half, grad_context, preferred_element_type=jnp.float32
    ).astype(jnp.bfloat16)
    inner = jnp.sum(attn_probs * grad_probs, axis=-1, keepdims=True)
    grad_score = (attn_probs * (grad_probs - inner) * HD ** (-0.5)).astype(jnp.bfloat16)
    grad_query = jnp.einsum(
        "nhqk,nkhe->nqhe", grad_score, key_rows, preferred_element_type=jnp.float32
    ).astype(jnp.bfloat16)
    grad_key = jnp.einsum(
        "nhqk,nqhe->nkhe", grad_score, query_rows, preferred_element_type=jnp.float32
    ).astype(jnp.bfloat16)
    grad_qkv = jnp.stack(
        [
            grad_query.reshape(scene_count, token_count, width),
            grad_key.reshape(scene_count, token_count, width),
            grad_value.reshape(scene_count, token_count, width),
        ],
        axis=2,
    )
    grad_qkv_w = jnp.einsum("ntd,ntcw->dcw", normed, grad_qkv, preferred_element_type=jnp.float32)
    return (grad_qkv_w, grad_out_w, grad_qkv)


def stem_grads(picked, grad_in):
    pieces = []
    for group_id, (band_start, band_end) in enumerate(GROUP_BANDS):
        columns = picked[
            :, group_id * CAP : (group_id + 1) * CAP, band_start * PIX : band_end * PIX
        ]
        pieces.append(
            jnp.einsum(
                "str,std->rd", columns, grad_in[:, group_id], preferred_element_type=jnp.float32
            )
        )
    return jnp.concatenate(pieces, axis=0)


def on_device(patches, vis_index, vis_count, w_stem, ln_gain, w_qkv, w_out, out_grad):
    scene_count = patches.shape[0]
    token_count = GROUPS * CAP
    embedded, picked = embed_tokens(patches, vis_index, w_stem)
    live_slots = lax.broadcasted_iota(jnp.int32, (1, 1, CAP), 2) < vis_count[:, :, None]
    normed, centred, inv_std = layer_norm(embedded, ln_gain)
    normed_rows = normed.reshape(scene_count, token_count, D)
    key_flags = live_slots.reshape(scene_count, token_count)
    grad_live = jnp.where(live_slots[..., None], out_grad, jnp.zeros((), jnp.bfloat16))
    grad_rows = grad_live.reshape(scene_count, token_count, D)
    wq_rows, wo_rows = (
        lax.all_gather(w_qkv, "dp", axis=0, tiled=True),
        lax.all_gather(w_out, "dp", axis=1, tiled=True),
    )
    wq_full, wo_full = (
        lax.all_gather(wq_rows, "group", axis=2, tiled=True),
        lax.all_gather(wo_rows, "group", axis=0, tiled=True),
    )
    qkv, attn_probs, probs_half, context = attend_forward(normed_rows, key_flags, wq_full)
    mixed = jnp.einsum("ntw,wd->ntd", context, wo_full, preferred_element_type=jnp.float32)
    full_qkv_w, full_out_w, grad_qkv = attend_backward(
        grad_rows, normed_rows, wq_full, wo_full, qkv, attn_probs, probs_half, context
    )
    grad_normed = jnp.einsum("ntcw,dcw->ntd", grad_qkv, wq_full, preferred_element_type=jnp.float32)
    grad_qkv_w, grad_out_w = (
        lax.psum_scatter(full_qkv_w, "group", scatter_dimension=2, tiled=True),
        lax.psum_scatter(full_out_w, "group", scatter_dimension=0, tiled=True),
    )
    grad_w_qkv, grad_w_out = (
        lax.psum_scatter(grad_qkv_w, "dp", scatter_dimension=0, tiled=True),
        lax.psum_scatter(grad_out_w, "dp", scatter_dimension=1, tiled=True),
    )
    mixed = mixed.reshape(scene_count, GROUPS, CAP, D)
    output = jnp.where(live_slots[..., None], embedded.astype(jnp.float32) + mixed, 0.0).astype(
        jnp.bfloat16
    )
    grad_normed = grad_normed.reshape(scene_count, GROUPS, CAP, D)
    grad_in = (
        grad_live.astype(jnp.float32) + norm_back(grad_normed, centred, inv_std, ln_gain)
    ).astype(jnp.bfloat16)
    stem_local = stem_grads(picked, grad_in)
    grad_w_stem = lax.psum(stem_local, ("dp", "group"))
    return (output, grad_w_stem, grad_w_qkv, grad_w_out)


def solution(mesh):
    return jax.shard_map(
        on_device,
        mesh=mesh,
        in_specs=(
            P(("dp", "group"), None, None),
            P(("dp", "group"), None, None),
            P(("dp", "group"), None),
            P(),
            P(),
            P("dp", None, "group"),
            P("group", "dp"),
            P(("dp", "group"), None, None, None),
        ),
        out_specs=(
            P(("dp", "group"), None, None, None),
            P(),
            P("dp", None, "group"),
            P("group", "dp"),
        ),
        check_vma=False,
    )
```

profile of v0, /device:TPU:0, one launch (start us, length us, event | category | flops | bytes accessed | tf_op | source)
XLA Modules:
  0.0 670.3 jit_solution(13740511633145533200)
XLA Ops:
  8.0 32.7 %all_gather.14 = bf16[256,1024]{1,0:T(8,128)(2,1)} all-gather(bf16[256,128]{1,0:T(8,128)(2,1)} %param.14), channel_id=1, replica_groups=mesh['dp'=8,'group'=4] {'dp'}, dimensions={1}, use_global_device_ids=true | all-gather | bytes 589824 | tf_op jit(solution)/shard_map/all_gather | solution.py:154
  40.7 18.5 %all-gather.4.cloned.1.call-done = bf16[1024,3,256]{2,0,1:T(8,128)(2,1)} async-done(((bf16[128,3,256]{2,0,1:T(8,128)(2,1)}), bf16[1024,3,256]{2,0,1:T(8,128)(2,1)}) %all-gather.4.cloned.1.call-update) | async-done | bytes 1572880 | tf_op jit(solution)/shard_map/all_gather | solution.py:153
  63.6 11.5 %gather_fusion = bf16[864,640]{1,0:T(8,128)(2,1)S(1)} fusion(bf16[6,144,640]{2,1,0:T(8,128)(2,1)S(1)} %copy-done, s32[864]{0:T(1024)S(1)} %reshape.261), kind=kCustom, calls=%fused_computation | custom fusion | bytes 2218752 | tf_op jit(solution)/shard_map/jit(take_along_axis)/gather | solution.py:35
  75.7 6.2 multiply_sine_fusion.5
  87.1 4.8 fusion.55
  91.9 4.4 copy.117
  96.4 34.6 %all-gather.6.cloned.1.call-done = bf16[1024,3,1024]{2,0,1:T(8,128)(2,1)} async-done(((bf16[1024,3,256]{2,0,1:T(8,128)(2,1)}), bf16[1024,3,1024]{2,0,1:T(8,128)(2,1)}) %all-gather.6.cloned.1.call-update) | async-done | bytes 6291472 | tf_op jit(solution)/shard_map/all_gather | solution.py:157
  131.0 9.0 %fusion.32 = bf16[6,144,3,1024]{3,1,2,0:T(8,128)(2,1)S(1)} fusion(bf16[1024,3,1024]{2,0,1:T(8,128)(2,1)} %all-gather.6.cloned.1.call-done, f32[6,144,1024]{2,1,0:T(8,128)} %fusion.21, f32[1024]{0:T(1024)S(1)} %copy-done.21), kind=kOutput, calls=%fused_computation.42 | convolution fusion | flops 5440241664 | bytes 15142912 | tf_op jit(solution)/shard_map/ntd,dcw->ntcw/dot_general | solution.py:67
  142.3 4.4 copy.116
  146.7 4.4 copy.115
  151.1 2.7 copy.114
  153.9 11.4 %fusion.134 = (f32[6,16,144]{2,1,0:T(8,128)S(1)}, f32[6,16,144,144]{2,3,1,0:T(8,128)}) fusion(pred[6,144]{1,0:T(8,128)(4,1)S(1)} %broadcast_compare_fusion, bf16[6,144,16,64]{1,3,2,0:T(8,128)(2,1)} %bitcast.210, bf16[6,144,16,64]{1,3,2,0:T(8,128)(2,1)} %bitcast.208), kind=kOutput, calls=%fused_computation.183 | convolution fusion | flops 262766736 | bytes 11557728 | tf_op jit(solution)/shard_map/sub | solution.py:78
  165.3 7.4 %fusion.43 = bf16[6,16,64,144]{3,2,1,0:T(8,128)(2,1)S(1)} fusion(bf16[6,144,16,64]{1,3,2,0:T(8,128)(2,1)} %bitcast.202, f32[6,16,144,144]{2,3,1,0:T(8,128)} %get-tuple-element.53, f32[6,16,144]{2,1,0:T(8,128)S(1)} %get-tuple-element.52), kind=kOutput, calls=%fused_computation.47 | convolution fusion | flops 259670016 | bytes 11556864 | tf_op jit(solution)/shard_map/nhqk,nkhe->nqhe/dot_general | solution.py:81
  174.3 4.5 convolution_bitcast_fusion.1
  178.8 10.6 %fusion.46 = bf16[6,16,64,144]{3,2,1,0:T(8,128)(2,1)} fusion(bf16[6,144,16,64]{1,3,2,0:T(8,128)(2,1)} %bitcast.200, f32[6,16,144,144]{2,3,1,0:T(8,128)} %get-tuple-element.53, f32[6,16,144]{2,1,0:T(8,128)S(1)} %get-tuple-element.52), kind=kOutput, calls=%fused_computation.48 | convolution fusion | flops 259670016 | bytes 11556864 | tf_op jit(solution)/shard_map/nhqk,nqhe->nkhe/dot_general | solution.py:105
  189.4 3.4 copy.97
  192.8 10.7 %fusion.135 = f32[6,16,144,144]{2,3,1,0:T(8,128)} fusion(bf16[6,144,16,64]{1,3,2,0:T(8,128)(2,1)} %bitcast.201, bf16[6,144,16,64]{1,3,2,0:T(8,128)(2,1)} %bitcast.203), kind=kOutput, calls=%fused_computation.184 | convolution fusion | flops 254803968 | bytes 11501568 | tf_op jit(solution)/shard_map/nqhe,nkhe->nhqk/dot_general | solution.py:102
  203.5 24.3 %fusion.40 = bf16[6,16,64,144]{3,2,1,0:T(8,128)(2,1)} fusion(bf16[6,144,16,64]{1,3,2,0:T(8,128)(2,1)} %bitcast.211, f32[6,16,144,144]{2,3,1,0:T(8,128)} %fusion.135, f32[6,16,144,144]{2,3,1,0:T(8,128)} %get-tuple-element.53, f32[6,16,144]{2,1,0:T(8,128)S(1)} %get-tuple-element.52), kind=kOutput, calls=%fused_computation.46 | convolution fusion | flops 269637248 | bytes 19519488 | tf_op jit(solution)/shard_map/nhqk,nqhe->nkhe/dot_general | solution.py:113
  227.8 4.3 copy.96
  232.1 24.1 %fusion.37 = bf16[6,16,64,144]{3,2,1,0:T(8,128)(2,1)} fusion(bf16[6,144,16,64]{1,3,2,0:T(8,128)(2,1)} %bitcast.209, f32[6,16,144,144]{2,3,1,0:T(8,128)} %fusion.135, f32[6,16,144,144]{2,3,1,0:T(8,128)} %get-tuple-element.53, f32[6,16,144]{2,1,0:T(8,128)S(1)} %get-tuple-element.52), kind=kOutput, calls=%fused_computation.45 | convolution fusion | flops 269637248 | bytes 19519488 | tf_op jit(solution)/shard_map/nhqk,nkhe->nqhe/dot_general | solution.py:110
  256.2 4.4 copy.95
  260.6 12.2 %convolution_bitcast_fusion = f32[1024,3,1024]{2,0,1:T(8,128)} fusion(bf16[6,144,1,1024]{3,1,2,0:T(8,128)(2,1)S(1)} %copy.97, bf16[6,144,1,1024]{3,1,2,0:T(8,128)(2,1)} %copy.96, bf16[6,144,1,1024]{3,1,2,0:T(8,128)(2,1)} %copy.95, f32[6,144,1024]{2,1,0:T(8,128)} %fusion.21, f32[1024]{0:T(1024)S(1)} %copy-done.21), kind=kOutput, calls=%fused_computation.22 | convolution fusion | flops 5453512704 | bytes 21434368 | tf_op jit(solution)/shard_map/ntd,ntcw->dcw/dot_general | solution.py:124
  273.0 12.1 %fusion.31 = (f32[6,144]{1,0:T(8,128)S(1)}, f32[6,144]{1,0:T(8,128)S(1)}, f32[6,144,1024,1]{2,1,3,0:T(8,128)}) fusion(f32[1024]{0:T(1024)S(1)} %copy-done.21, f32[6,144,1024]{2,1,0:T(8,128)} %fusion.21, bf16[1024,3,1024]{2,0,1:T(8,128)(2,1)} %all-gather.6.cloned.1.call-done, bf16[6,144,1,1024]{3,1,2,0:T(8,128)(2,1)} %copy-done.12, ...), kind=kOutput, calls=%fused_computation.40 | convolution fusion | flops 5444663296 | bytes 18688768 | tf_op jit(solution)/shard_map/ntcw,dcw->ntd/dot_general | solution.py:165
  285.3 4.8 fusion.26
  296.7 75.3 %reduce-scatter.5.cloned.1.call-done = f32[1024,3,256]{2,0,1:T(8,128)} async-done(((f32[1024,3,1024]{2,0,1:T(8,128)}), f32[1024,3,256]{2,0,1:T(8,128)}) %reduce-scatter.5.cloned.1.call-update) | async-done | bytes 3145744 | tf_op jit(solution)/shard_map/reduce_scatter | solution.py:167
  372.0 6.5 copy.83
  378.5 5.9 dot_general.62
  384.4 4.2 select_convert_fusion
  390.0 125.0 %all-reduce.2.cloned.1.call-done = f32[640,1024]{1,0:T(8,128)} async-done(((f32[640,1024]{1,0:T(8,128)}), f32[640,1024]{1,0:T(8,128)}) %all-reduce.2.cloned.1.call-update) | async-done | bytes 2621456 | tf_op jit(solution)/shard_map/psum | solution.py:183
  515.0 66.3 %reduce-scatter.11.cloned.1.call-done = f32[256,128]{1,0:T(8,128)} async-done(((f32[256,1024]{1,0:T(8,128)}), f32[256,128]{1,0:T(8,128)}) %reduce-scatter.11.cloned.1.call-update) | async-done | bytes 131088 | tf_op jit(solution)/shard_map/reduce_scatter | solution.py:172
  581.3 78.4 %reduce-scatter.7.cloned.1.call-done = f32[128,3,256]{2,0,1:T(8,128)} async-done(((f32[1024,3,256]{2,0,1:T(8,128)}), f32[128,3,256]{2,0,1:T(8,128)}) %reduce-scatter.7.cloned.1.call-update) | async-done | bytes 393232 | tf_op jit(solution)/shard_map/reduce_scatter | solution.py:171
  659.7 3.6 copy.245
  (116 shorter events, 22.9 us)
Async XLA Ops:
  7.2 56.4 %copy-start = (bf16[6,144,640]{2,1,0:T(8,128)(2,1)S(1)}, bf16[6,144,640]{2,1,0:T(8,128)(2,1)}, u32[]{:S(2)}) copy-start(bf16[6,144,640]{2,1,0:T(8,128)(2,1)} %param.8) | copy-start | bytes 3317764
  7.2 54.9 %copy-start.8 = (bf16[6,3,48,1024]{3,2,1,0:T(8,128)(2,1)S(1)}, bf16[6,3,48,1024]{3,2,1,0:T(8,128)(2,1)}, u32[]{:S(2)}) copy-start(bf16[6,3,48,1024]{3,2,1,0:T(8,128)(2,1)} %param.15) | copy-start | bytes 5308420
  7.2 52.0 %all-gather.4.cloned.1.call-start = ((), (), s32[]{:S(2)}) async-start(), calls=%async_computation.4 | async-start | bytes 1769472 | tf_op jit(solution)/shard_map/all_gather | solution.py:153
  7.9 79.1 %all-gather.8.cloned.1.call-start = ((), (), s32[]{:S(2)}) async-start(), calls=%async_computation.6 | async-start | bytes 2621440 | tf_op jit(solution)/shard_map/all_gather | solution.py:158
  40.7 90.3 %all-gather.6.cloned.1.call-start = ((), (), s32[]{:S(2)}) async-start(), calls=%async_computation.5 | async-start | bytes 7864320 | tf_op jit(solution)/shard_map/all_gather | solution.py:157
  59.2 236.7 %reduce-scatter.9.cloned.1.call-start = ((), (), s32[]{:S(2)}) async-start(), calls=%async_computation.10 | async-start | bytes 5242880 | tf_op jit(solution)/shard_map/reduce_scatter | solution.py:168
  61.8 1.8 copy-start.19
  63.6 11.7 %copy-start.18 = (s32[6,3,48]{2,1,0:T(4,128)S(1)}, s32[6,3,48]{2,1,0:T(4,128)}, u32[]{:S(2)}) copy-start(s32[6,3,48]{2,1,0:T(4,128)} %param.9) | copy-start | bytes 10372
  75.1 6.8 %copy-start.22 = (bf16[640,1024]{1,0:T(8,128)(2,1)S(1)}, bf16[640,1024]{1,0:T(8,128)(2,1)}, u32[]{:S(2)}) copy-start(bf16[640,1024]{1,0:T(8,128)(2,1)} %param.11) | copy-start | bytes 3932164
  75.6 6.9 %copy-start.13 = (bf16[6,144,640]{2,1,0:T(8,128)(2,1)}, bf16[6,144,640]{2,1,0:T(8,128)(2,1)S(1)}, u32[]{:S(2)}) copy-start(bf16[6,144,640]{2,1,0:T(8,128)(2,1)S(1)} %broadcast_select_fusion) | copy-start | bytes 3317764
  82.2 1.9 copy-start.2
  82.5 1.5 copy-start.4
  82.9 1.5 copy-start.6
  83.2 1.1 copy-start.14
  83.9 1.0 copy-start.16
  84.9 2.2 copy-start.10
  91.9 39.1 %copy-start.21 = (f32[1024]{0:T(1024)S(1)}, f32[1024]{0:T(1024)}, u32[]{:S(2)}) copy-start(f32[1024]{0:T(1024)} %param.12) | copy-start | bytes 12292
  165.2 9.0 %copy-start.11 = (bf16[6,3,48,1024]{3,2,1,0:T(8,128)(2,1)S(1)}, bf16[6,3,48,1024]{3,2,1,0:T(8,128)(2,1)}, u32[]{:S(2)}) copy-start(bf16[6,3,48,1024]{3,2,1,0:T(8,128)(2,1)} %copy.86) | copy-start | bytes 5308420
  172.7 1.6 copy-start.9
  178.8 193.2 %reduce-scatter.5.cloned.1.call-start = ((), (), s32[]{:S(2)}) async-start(), calls=%async_computation.8 | async-start | bytes 15728640 | tf_op jit(solution)/shard_map/reduce_scatter | solution.py:167
  192.8 67.8 %copy-start.12 = (bf16[6,144,1,1024]{3,1,2,0:T(8,128)(2,1)}, bf16[6,144,1,1024]{3,1,2,0:T(8,128)(2,1)S(1)}, u32[]{:S(2)}) copy-start(bf16[6,144,1,1024]{3,1,2,0:T(8,128)(2,1)S(1)} %copy.97) | copy-start | bytes 5308420
  272.9 12.4 %copy-start.3 = (bf16[6,1,48,1024]{3,2,0,1:T(8,128)(2,1)S(1)}, bf16[6,1,48,1024]{3,2,0,1:T(8,128)(2,1)}, u32[]{:S(2)}) copy-start(bf16[6,1,48,1024]{3,2,0,1:T(8,128)(2,1)} %copy-done.2) | copy-start | bytes 1769476
  272.9 12.4 %copy-start.5 = (bf16[6,1,48,1024]{3,2,0,1:T(8,128)(2,1)S(1)}, bf16[6,1,48,1024]{3,2,0,1:T(8,128)(2,1)}, u32[]{:S(2)}) copy-start(bf16[6,1,48,1024]{3,2,0,1:T(8,128)(2,1)} %copy-done.4) | copy-start | bytes 1769476
  272.9 12.3 %copy-start.7 = (bf16[6,1,48,1024]{3,2,0,1:T(8,128)(2,1)S(1)}, bf16[6,1,48,1024]{3,2,0,1:T(8,128)(2,1)}, u32[]{:S(2)}) copy-start(bf16[6,1,48,1024]{3,2,0,1:T(8,128)(2,1)} %copy-done.6) | copy-start | bytes 1769476
  272.9 12.3 %copy-start.15 = (f32[6,3,48]{2,0,1:T(8,128)S(1)}, f32[6,3,48]{2,0,1:T(8,128)}, u32[]{:S(2)}) copy-start(f32[6,3,48]{2,0,1:T(8,128)} %copy-done.14) | copy-start | bytes 10372
  272.9 12.3 %copy-start.17 = (f32[6,3,48]{2,0,1:T(8,128)S(1)}, f32[6,3,48]{2,0,1:T(8,128)}, u32[]{:S(2)}) copy-start(f32[6,3,48]{2,0,1:T(8,128)} %copy-done.16) | copy-start | bytes 10372
  272.9 12.3 %copy-start.20 = (pred[6,3,48]{2,0,1:T(8,128)(4,1)S(1)}, pred[6,3,48]{2,0,1:T(8,128)(4,1)}, u32[]{:S(2)}) copy-start(pred[6,3,48]{2,0,1:T(8,128)(4,1)} %copy-done.19) | copy-start | bytes 2596
  272.9 242.0 %all-reduce.2.cloned.1.call-start = ((), (), s32[]{:S(2)}) async-start(), calls=%async_computation.7 | async-start | bytes 5242880 | tf_op jit(solution)/shard_map/psum | solution.py:183
  295.9 285.4 %reduce-scatter.11.cloned.1.call-start = ((), (), s32[]{:S(2)}) async-start(), calls=%async_computation.11 | async-start | bytes 1179648 | tf_op jit(solution)/shard_map/reduce_scatter | solution.py:172
  296.6 363.1 %reduce-scatter.7.cloned.1.call-start = ((), (), s32[]{:S(2)}) async-start(), calls=%async_computation.9 | async-start | bytes 3538944 | tf_op jit(solution)/shard_map/reduce_scatter | solution.py:171
  388.6 274.6 %copy-start.1 = (bf16[6,144,640]{2,1,0:T(8,128)(2,1)S(1)}, bf16[6,144,640]{2,1,0:T(8,128)(2,1)}, u32[]{:S(2)}) copy-start(bf16[6,144,640]{2,1,0:T(8,128)(2,1)} %param.8) | copy-start | bytes 3317764
Sparse Core Ops, SparseCore 0:
  10.2 48.9 all-gather.3
  60.7 21.3 all-gather.7
  83.7 47.2 all-gather.5
  178.9 44.4 reduce-scatter.8
  273.0 98.9 reduce-scatter.4
  378.8 136.1 all-reduce.1
  519.0 62.2 reduce-scatter.10
  585.9 73.7 reduce-scatter.6
where the time goes:
time: 675 us; the launch traced here: 670 us
  waiting for transfers between devices  400 us (59%)
  matrix products  140 us (21%)
  local copies, waits for them, and re-layouts  65.9 us (10%)
  blocking collectives  32.7 us (5%)
  other arithmetic  16.8 us (2%)
  between operations  14.9 us (2%)
    psum x1, waiting for transfers between devices, on_device(): grad_w_stem = lax.psum(stem_local, ('dp', 'group'))  125 us
    reduce_scatter x1, waiting for transfers between devices, on_device(): lax.psum_scatter(grad_qkv_w, 'dp', scatter_dimension=0, tiled=True)  78.4 us
    reduce_scatter x1, waiting for transfers between devices, on_device(): lax.psum_scatter(full_qkv_w, 'group', scatter_dimension=2, tiled=True)  75.3 us
    reduce_scatter x1, waiting for transfers between devices, on_device(): lax.psum_scatter(grad_out_w, 'dp', scatter_dimension=1, tiled=True)  66.3 us
    all_gather x1, waiting for transfers between devices, on_device(): lax.all_gather(wq_rows, 'group', axis=2, tiled=True)  34.6 us
    all_gather x1, blocking collectives, on_device(): lax.all_gather(w_out, 'dp', axis=1, tiled=True)  32.7 us
    dot_general x1, matrix products, attend_backward(): jnp.einsum('nhqk,nqhe->nkhe', grad_score, query_rows, preferred_element_t...  24.3 us
    dot_general x1, matrix products, attend_backward(): jnp.einsum('nhqk,nkhe->nqhe', grad_score, key_rows, preferred_element_typ...  24.1 us
  transfers between devices with their start and end apart: 8, of which 6 were waited for; matrix products, arithmetic and copies ran while one was open for 26% of the time, Pallas kernels for 0%

commit v1 on v0

v1 whole, which is shorter than its diff:
```python
import functools

import jax
import jax.numpy as jnp
from jax import lax
from jax.experimental import pallas as pl
from jax.experimental.pallas import tpu as pltpu
from jax.sharding import PartitionSpec as P

D = 1024
HD = 64
GROUPS = 3
CAP = 48
GRID = 12
PIX = 64
TOK = GROUPS * CAP
PAIR = 128
GROUP_BANDS = ((0, 4), (4, 8), (8, 10))
NORM_EPS = 1e-06
F32 = jnp.float32
BF16 = jnp.bfloat16
VMEM_LIMIT = 48 * 1024 * 1024


def dot_nn(a, b):
    return lax.dot_general(a, b, (((1,), (0,)), ((), ())), preferred_element_type=F32)


def dot_nt(a, b):
    return lax.dot_general(a, b, (((1,), (1,)), ((), ())), preferred_element_type=F32)


def dot_tn(a, b):
    return lax.dot_general(a, b, (((0,), (0,)), ((), ())), preferred_element_type=F32)


def live_column(c0, c1, c2):
    row = lax.broadcasted_iota(jnp.int32, (TOK, 1), 0)
    return (
        (row < c0)
        | ((row >= CAP) & (row < CAP + c1))
        | ((row >= 2 * CAP) & (row < 2 * CAP + c2))
    )


def params():
    return pltpu.CompilerParams(vmem_limit_bytes=VMEM_LIMIT)


def cost(flops, nbytes):
    return pl.CostEstimate(flops=int(flops), bytes_accessed=int(nbytes), transcendentals=0)


def stem_kernel(
    cnt_ref, idx_ref, patch_ref, w_ref, gain_ref, table_ref, genc_ref, og_ref,
    emb_ref, normed_ref, gl_ref, cols_ref, parts,
):
    step = pl.program_id(0)
    scenes = patch_ref.shape[0]

    @pl.when(step == 0)
    def _():
        whole = table_ref[...]
        high = whole.astype(BF16)
        rest = whole - high.astype(F32)
        mid = rest.astype(BF16)
        low = (rest - mid.astype(F32)).astype(BF16)
        parts[0] = high
        parts[1] = mid
        parts[2] = low

    patch_iota = lax.broadcasted_iota(jnp.int32, (TOK, table_ref.shape[0]), 1)
    picked, placed = [], []
    for s in range(scenes):
        onehot = (idx_ref[s] == patch_iota).astype(F32).astype(BF16)
        picked.append(dot_nn(onehot, patch_ref[s]).astype(BF16))
        placed.append(
            (dot_nn(onehot, parts[0]) + dot_nn(onehot, parts[1])) + dot_nn(onehot, parts[2])
        )
        live = live_column(
            cnt_ref[step * scenes + s, 0], cnt_ref[step * scenes + s, 1], cnt_ref[step * scenes + s, 2]
        )
        gl_ref[s] = jnp.where(live, og_ref[s].astype(F32), 0.0).astype(BF16)
    for g, (start, end) in enumerate(GROUP_BANDS):
        rows = slice(g * CAP, (g + 1) * CAP)
        columns = jnp.concatenate([p[rows, start * PIX : end * PIX] for p in picked], axis=0)
        summed = dot_nn(columns, w_ref[start * PIX : end * PIX, :])
        width = (end - start) * PIX
        for s in range(scenes):
            values = summed[s * CAP : (s + 1) * CAP] + (placed[s][rows] + genc_ref[g : g + 1, :])
            emb = values.astype(BF16)
            emb_ref[s, rows, :] = emb
            x = emb.astype(F32)
            centre = jnp.mean(x, axis=-1, keepdims=True)
            dev = x - centre
            spread = jnp.mean(dev * dev, axis=-1, keepdims=True)
            centred = dev * lax.rsqrt(spread + NORM_EPS)
            normed_ref[s, rows, :] = (centred * gain_ref[...]).astype(BF16)
            cols_ref[s, rows, :width] = columns[s * CAP : (s + 1) * CAP]
            if width < cols_ref.shape[2]:
                cols_ref[s, rows, width:] = jnp.zeros((CAP, cols_ref.shape[2] - width), BF16)


def stem_call(counts, index_col, patches, w_stem, gain, table, genc, out_grad):
    scenes, patch_count, width = patches.shape
    block = 3 if scenes % 3 == 0 else 1
    col_width = max(e - s for s, e in GROUP_BANDS) * PIX
    per = lambda shape: pl.BlockSpec((block,) + shape, lambda i: (i, 0, 0))
    whole = lambda a: pl.BlockSpec(a.shape, lambda i: (0,) * a.ndim)
    rows = jax.ShapeDtypeStruct((scenes, TOK, D), BF16)
    return pl.pallas_call(
        stem_kernel,
        grid=(scenes // block,),
        in_specs=[
            pl.BlockSpec(memory_space=pltpu.SMEM),
            per((TOK, 1)),
            per((patch_count, width)),
            whole(w_stem),
            whole(gain),
            whole(table),
            whole(genc),
            per((TOK, D)),
        ],
        out_specs=[per((TOK, D)), per((TOK, D)), per((TOK, D)), per((TOK, col_width))],
        out_shape=[rows, rows, rows, jax.ShapeDtypeStruct((scenes, TOK, col_width), BF16)],
        scratch_shapes=[pltpu.VMEM((3,) + table.shape, BF16)],
        compiler_params=params(),
        cost_estimate=cost(8e9, 12e6),
        name="stem_norm",
    )(counts, index_col, patches, w_stem, gain, table, genc, out_grad)


def attention_kernel(cnt_ref, na_ref, nb_ref, ga_ref, gb_ref, p_ref, out_ref, n_s, g_s, qkv):
    half, step = pl.program_id(0), pl.program_id(1)
    rows = n_s.shape[0]
    scenes = rows // TOK
    width = p_ref.shape[1] // 4

    @pl.when(half == 0)
    def _():
        n_s[...] = na_ref[...]
        g_s[...] = ga_ref[...]

    @pl.when(half != 0)
    def _():
        n_s[...] = nb_ref[...]
        g_s[...] = gb_ref[...]

    qkv[:, : 3 * width] = dot_nn(n_s[...], p_ref[:, : 3 * width]).astype(BF16)
    qkv[:, 3 * width :] = dot_nn(g_s[...], p_ref[:, 3 * width :]).astype(BF16)
    lane = lax.broadcasted_iota(jnp.int32, (1, PAIR), 1)
    masks = [
        (lane // HD == h).astype(F32).astype(BF16) for h in range(PAIR // HD)
    ]

    def scene_body(s, _):
        base = pl.multiple_of(s * TOK, 16)
        at = pl.ds(base, TOK)
        scene = step * scenes + s
        live = live_column(cnt_ref[half, scene, 0], cnt_ref[half, scene, 1], cnt_ref[half, scene, 2])
        bias = jnp.where(live, 0.0, -1e30)
        for pair in range(width // PAIR):
            cols = [slice(part * width + pair * PAIR, part * width + (pair + 1) * PAIR) for part in range(4)]
            q, k, v, dc = [qkv[at, c] for c in cols]
            gq = gk = gv = ctx = None
            for mask in masks:
                qm = q * (mask * jnp.asarray(HD ** (-0.5), BF16))
                km, vm, dcm = k * mask, v * mask, dc * mask
                scores = dot_nt(k, qm) + bias
                lifted = jnp.exp(scores - jnp.max(scores, axis=0, keepdims=True))
                probs = lifted * (1.0 / jnp.sum(lifted, axis=0, keepdims=True))
                half_probs = probs.astype(BF16)
                grad_probs = dot_nt(v, dcm)
                inner = jnp.sum(probs * grad_probs, axis=0, keepdims=True)
                grad_score = (probs * (grad_probs - inner)).astype(BF16)
                new = (
                    dot_tn(grad_score, km),
                    dot_nn(grad_score, qm),
                    dot_nn(half_probs, dcm),
                    dot_tn(half_probs, vm),
                )
                if gq is None:
                    gq, gk, gv, ctx = new
                else:
                    gq, gk, gv, ctx = gq + new[0], gk + new[1], gv + new[2], ctx + new[3]
            out_ref[at, cols[0]] = (gq * HD ** (-0.5)).astype(BF16)
            out_ref[at, cols[1]] = gk.astype(BF16)
            out_ref[at, cols[2]] = gv.astype(BF16)
            out_ref[at, cols[3]] = ctx.astype(BF16)
        return 0

    lax.fori_loop(0, scenes, scene_body, 0)


def attention_call(counts, na, nb, ga, gb, packed):
    tokens = na.shape[0]
    rows = 3 * TOK if tokens % (3 * TOK) == 0 else TOK
    steps = tokens // rows
    first = pl.BlockSpec((rows, D), lambda h, i: (jnp.where(h == 0, i, steps - 1), 0))
    second = pl.BlockSpec((rows, D), lambda h, i: (jnp.where(h == 0, 0, i), 0))
    return pl.pallas_call(
        attention_kernel,
        grid=(2, steps),
        in_specs=[
            pl.BlockSpec(memory_space=pltpu.SMEM),
            first, second, first, second,
            pl.BlockSpec(packed.shape, lambda h, i: (0, 0)),
        ],
        out_specs=pl.BlockSpec((rows, packed.shape[1]), lambda h, i: (h * steps + i, 0)),
        out_shape=jax.ShapeDtypeStruct((2 * tokens, packed.shape[1]), BF16),
        scratch_shapes=[
            pltpu.VMEM((rows, D), BF16),
            pltpu.VMEM((rows, D), BF16),
            pltpu.VMEM((rows, packed.shape[1]), BF16),
        ],
        compiler_params=params(),
        cost_estimate=cost(22e9, 14e6),
        name="attention",
    )(counts, na, nb, ga, gb, packed)


def weight_grad_kernel(na_ref, nb_ref, ga_ref, gb_ref, pack_ref, out_ref):
    half, step = pl.program_id(0), pl.program_id(1)
    width = pack_ref.shape[1] // 4

    @pl.when((half == 0) & (step == 0))
    def _():
        out_ref[...] = jnp.zeros_like(out_ref)

    def add(n_ref, g_ref):
        out_ref[:, : 3 * width] += dot_tn(n_ref[...], pack_ref[:, : 3 * width])
        out_ref[:, 3 * width :] += dot_tn(g_ref[...], pack_ref[:, 3 * width :])

    pl.when(half == 0)(lambda: add(na_ref, ga_ref))
    pl.when(half != 0)(lambda: add(nb_ref, gb_ref))


def weight_grad_call(na, nb, ga, gb, pack):
    tokens = na.shape[0]
    rows = 3 * TOK if tokens % (3 * TOK) == 0 else TOK
    steps = tokens // rows
    first = pl.BlockSpec((rows, D), lambda h, i: (jnp.where(h == 0, i, steps - 1), 0))
    second = pl.BlockSpec((rows, D), lambda h, i: (jnp.where(h == 0, 0, i), 0))
    return pl.pallas_call(
        weight_grad_kernel,
        grid=(2, steps),
        in_specs=[
            first, second, first, second,
            pl.BlockSpec((rows, pack.shape[1]), lambda h, i: (h * steps + i, 0)),
        ],
        out_specs=pl.BlockSpec((D, pack.shape[1]), lambda h, i: (0, 0)),
        out_shape=jax.ShapeDtypeStruct((D, pack.shape[1]), F32),
        compiler_params=params(),
        cost_estimate=cost(4e9, 15e6),
        name="weight_grad",
    )(na, nb, ga, gb, pack)


def back_kernel(blocks, first_col, last_col, out_dtype, *refs):
    packs, weights, out_ref = refs[:blocks], refs[blocks : 2 * blocks], refs[2 * blocks]
    total = None
    for pack_ref, w_ref in zip(packs, weights):
        new = dot_nt(pack_ref[...], w_ref[:, first_col:last_col])
        total = new if total is None else total + new
    out_ref[...] = total.astype(out_dtype)


def back_call(packs, weights, half, context, out_dtype):
    blocks = len(packs)
    tokens = packs[0].shape[0] // 2
    rows = 3 * TOK if tokens % (3 * TOK) == 0 else TOK
    steps = tokens // rows
    width = packs[0].shape[1] // 4
    span = (3 * width, 4 * width) if context else (0, 3 * width)
    if context:
        pack_spec = pl.BlockSpec((rows, width), lambda i: (half * steps + i, 3))
    else:
        pack_spec = pl.BlockSpec((rows, 3 * width), lambda i: (half * steps + i, 0))
    return pl.pallas_call(
        functools.partial(back_kernel, blocks, span[0], span[1], out_dtype),
        grid=(steps,),
        in_specs=[pack_spec] * blocks + [pl.BlockSpec(w.shape, lambda i: (0, 0)) for w in weights],
        out_specs=pl.BlockSpec((rows, D), lambda i: (i, 0)),
        out_shape=jax.ShapeDtypeStruct((tokens, D), out_dtype),
        compiler_params=params(),
        cost_estimate=cost(3e9, 10e6),
        name="back_context" if context else "back_qkv",
    )(*packs, *weights)


def tail_kernel(
    blocks, cnt_ref, recv_ref, emb_ref, gl_ref, cols_ref, gain_ref, *refs
):
    packs, weights, out_ref = refs[:blocks], refs[blocks : 2 * blocks], refs[2 * blocks]
    step = pl.program_id(0)
    rows = emb_ref.shape[0]
    scenes = rows // TOK

    @pl.when(step == 0)
    def _():
        out_ref[...] = jnp.zeros_like(out_ref)

    grad_normed = recv_ref[...]
    for pack_ref, w_ref in zip(packs, weights):
        grad_normed = grad_normed + dot_nt(pack_ref[...], w_ref[:, : pack_ref.shape[1]])
    x = emb_ref[...].astype(F32)
    dev = x - jnp.mean(x, axis=-1, keepdims=True)
    inv_std = lax.rsqrt(jnp.mean(dev * dev, axis=-1, keepdims=True) + NORM_EPS)
    centred = dev * inv_std
    scaled = grad_normed * gain_ref[...]
    first_mean = jnp.mean(scaled, axis=-1, keepdims=True)
    second_mean = jnp.mean(scaled * centred, axis=-1, keepdims=True)
    back = inv_std * (scaled - first_mean - centred * second_mean)
    grad_in = (gl_ref[...].astype(F32) + back).astype(BF16)
    for g, (start, end) in enumerate(GROUP_BANDS):
        at = [slice(s * TOK + g * CAP, s * TOK + (g + 1) * CAP) for s in range(scenes)]
        columns = jnp.concatenate([cols_ref[a, : (end - start) * PIX] for a in at], axis=0)
        grads = jnp.concatenate([grad_in[a] for a in at], axis=0)
        out_ref[start * PIX : end * PIX, :] += dot_tn(columns, grads)


def tail_call(counts, recv, emb, gl, cols, gain, packs, weights):
    blocks = len(packs)
    tokens = emb.shape[0]
    rows = 3 * TOK if tokens % (3 * TOK) == 0 else TOK
    width = packs[0].shape[1] // 4
    per = lambda a: pl.BlockSpec((rows, a.shape[1]), lambda i: (i, 0))
    return pl.pallas_call(
        functools.partial(tail_kernel, blocks),
        grid=(tokens // rows,),
        in_specs=[pl.BlockSpec(memory_space=pltpu.SMEM), per(recv), per(emb), per(gl), per(cols)]
        + [pl.BlockSpec(gain.shape, lambda i: (0, 0))]
        + [pl.BlockSpec((rows, 3 * width), lambda i: (i, 0))] * blocks
        + [pl.BlockSpec(w.shape, lambda i: (0, 0)) for w in weights],
        out_specs=pl.BlockSpec((GROUP_BANDS[-1][1] * PIX, D), lambda i: (0, 0)),
        out_shape=jax.ShapeDtypeStruct((GROUP_BANDS[-1][1] * PIX, D), F32),
        compiler_params=params(),
        cost_estimate=cost(5e9, 18e6),
        name="tail",
    )(counts, recv, emb, gl, cols, gain, *packs, *weights)


def output_kernel(blocks, cnt_ref, recv_ref, emb_ref, *refs):
    packs, weights, out_ref = refs[:blocks], refs[blocks : 2 * blocks], refs[2 * blocks]
    step = pl.program_id(0)
    scenes = emb_ref.shape[0] // TOK
    mixed = recv_ref[...].astype(F32)
    for pack_ref, w_ref in zip(packs, weights):
        mixed = mixed + dot_nt(pack_ref[...], w_ref[:, 3 * pack_ref.shape[1] :])
    total = emb_ref[...].astype(F32) + mixed
    for s in range(scenes):
        scene = step * scenes + s
        live = live_column(cnt_ref[scene, 0], cnt_ref[scene, 1], cnt_ref[scene, 2])
        at = slice(s * TOK, (s + 1) * TOK)
        out_ref[at, :] = jnp.where(live, total[at], 0.0).astype(BF16)


def output_call(counts, recv, emb, packs, weights):
    blocks = len(packs)
    tokens = emb.shape[0]
    rows = 3 * TOK if tokens % (3 * TOK) == 0 else TOK
    width = packs[0].shape[1] // 4
    per = lambda a: pl.BlockSpec((rows, a.shape[1]), lambda i: (i, 0))
    return pl.pallas_call(
        functools.partial(output_kernel, blocks),
        grid=(tokens // rows,),
        in_specs=[pl.BlockSpec(memory_space=pltpu.SMEM), per(recv), per(emb)]
        + [pl.BlockSpec((rows, width), lambda i: (i, 3))] * blocks
        + [pl.BlockSpec(w.shape, lambda i: (0, 0)) for w in weights],
        out_specs=per(emb),
        out_shape=jax.ShapeDtypeStruct(emb.shape, BF16),
        compiler_params=params(),
        cost_estimate=cost(1e9, 10e6),
        name="layer_output",
    )(counts, recv, emb, *packs, *weights)


def swap(x, axis, size, bit):
    return lax.ppermute(x, axis, [(i, i ^ bit) for i in range(size)])


def ring_order(size):
    return list(range(0, size, 2)) + list(range(size - 1, 0, -2)) if size % 2 == 0 else list(range(size))


def ring_gather(x, axis, size):
    order = ring_order(size)
    place = [order.index(i) for i in range(size)]
    forward = [(order[i], order[(i + 1) % size]) for i in range(size)]
    backward = [(order[(i + 1) % size], order[i]) for i in range(size)]
    here = jnp.array(place, jnp.int32)[lax.axis_index(axis)]
    owners = jnp.array(order, jnp.int32)
    rows = x.shape[0]
    full = jnp.zeros((size * rows,) + x.shape[1:], x.dtype)

    def put(full, block, distance):
        owner = owners[(here + distance + size) % size]
        return lax.dynamic_update_slice_in_dim(full, block, owner * rows, 0)

    full = put(full, x, 0)
    ahead = behind = x
    for s in range(1, size // 2 + 1):
        ahead = lax.ppermute(ahead, axis, forward)
        full = put(full, ahead, -s)
        if s <= (size - 1) // 2:
            behind = lax.ppermute(behind, axis, backward)
            full = put(full, behind, s)
    return full


def reduce_rows(x, axis, size, chunks):
    rows = x.shape[0] // size
    cols = x.shape[1] // chunks
    me = lax.axis_index(axis)
    low, high = me % 2, me // 2
    count = size // 2
    out = []
    for c in range(chunks):
        part = x[:, c * cols : (c + 1) * cols].reshape(count, 2, rows, cols)
        send = lax.dynamic_index_in_dim(part, 1 - low, 1, keepdims=False).astype(BF16)
        keep = lax.dynamic_index_in_dim(part, low, 1, keepdims=False)
        part = keep + swap(send, axis, size, 1).astype(F32)
        total = lax.dynamic_index_in_dim(part, high, 0, keepdims=False)
        for j in range(1, count):
            away = lax.dynamic_index_in_dim(part, high ^ j, 0, keepdims=False).astype(BF16)
            total = total + swap(away, axis, size, 2 * j).astype(F32)
        out.append(total)
    return jnp.concatenate(out, axis=1)


def sum_stem(x, dp, group):
    core = lax.axis_index("group") % 2
    far = lax.axis_index("group") // 2
    low = lax.axis_index("dp") % 2
    high = lax.axis_index("dp") // 2
    fars, highs = group // 2, dp // 2
    rows = x.shape[0] // 2
    own = lax.dynamic_slice_in_dim(x, core * rows, rows, 0)
    other = lax.dynamic_slice_in_dim(x, (1 - core) * rows, rows, 0)
    own = own + swap(other, "group", group, 1)
    small = rows // (2 * fars)
    mine = far * 2 + low
    total = lax.dynamic_slice_in_dim(own, mine * small, small, 0)

    def hop(block, f, b):
        if f:
            block_axis = [
                ((d, g), (d ^ b, g ^ (2 * f))) for d in range(dp) for g in range(group)
            ]
            pairs = [(s[0] * group + s[1], t[0] * group + t[1]) for s, t in block_axis]
            return lax.ppermute(block, ("dp", "group"), pairs)
        return swap(block, "dp", dp, b)

    hops = [(f, b) for f in range(fars) for b in range(2) if f or b]
    for f, b in hops:
        target = (far ^ f) * 2 + (low ^ b)
        away = lax.dynamic_slice_in_dim(own, target * small, small, 0).astype(BF16)
        total = total + hop(away, f, b).astype(F32)
    cols = x.shape[1] // highs
    part = lax.dynamic_slice_in_dim(total, high * cols, cols, 1)
    for j in range(1, highs):
        away = lax.dynamic_slice_in_dim(total, (high ^ j) * cols, cols, 1)
        part = part + swap(away, "dp", dp, 2 * j)
    part = part.astype(BF16)
    line = jnp.zeros((small, x.shape[1]), BF16)
    line = lax.dynamic_update_slice_in_dim(line, part, high * cols, 1)
    for j in range(1, highs):
        line = lax.dynamic_update_slice_in_dim(
            line, swap(part, "dp", dp, 2 * j), (high ^ j) * cols, 1
        )
    block = jnp.zeros((rows, x.shape[1]), BF16)
    block = lax.dynamic_update_slice_in_dim(block, line, mine * small, 0)
    for f, b in hops:
        target = (far ^ f) * 2 + (low ^ b)
        block = lax.dynamic_update_slice_in_dim(block, hop(line, f, b), target * small, 0)
    partner = swap(block, "group", group, 1)
    whole = jnp.zeros(x.shape, BF16)
    whole = lax.dynamic_update_slice_in_dim(whole, block, core * rows, 0)
    whole = lax.dynamic_update_slice_in_dim(whole, partner, (1 - core) * rows, 0)
    return whole.astype(F32)


def spatial_table(patch_count):
    quarter = D // 4
    half_width = D // 2
    row_freq = jnp.power(10000.0, -jnp.arange(quarter, dtype=F32) / quarter)
    group_freq = jnp.power(10000.0, -jnp.arange(half_width, dtype=F32) / half_width)
    at = jnp.arange(GRID).astype(F32)[:, None] * row_freq
    both = jnp.concatenate([jnp.sin(at), jnp.cos(at)], axis=-1)
    rows = patch_count // GRID
    by_row = jnp.broadcast_to(both[:rows, None], (rows, GRID, 2 * quarter))
    by_col = jnp.broadcast_to(both[None], (rows, GRID, 2 * quarter))
    table = jnp.concatenate([by_row, by_col], axis=-1).reshape(patch_count, D)
    group_at = jnp.arange(GROUPS).astype(F32)[:, None] * group_freq
    return table, jnp.concatenate([jnp.sin(group_at), jnp.cos(group_at)], axis=-1)


def on_device(dp, group, patches, vis_index, vis_count, w_stem, ln_gain, w_qkv, w_out, out_grad):
    scenes = patches.shape[0]
    tokens = scenes * TOK
    width = w_qkv.shape[2]
    fars = group // 2

    shard = jnp.concatenate([w_qkv.reshape(w_qkv.shape[0], 3 * width), w_out.T], axis=1)
    shards = [shard] + [swap(shard, "group", group, 2 * f) for f in range(1, fars)]
    weights = [ring_gather(s, "dp", dp) for s in shards]

    counts = vis_count.astype(jnp.int32)
    both_counts = jnp.stack([counts, swap(counts, "group", group, 1)])
    table, genc = spatial_table(patches.shape[1])
    gain = ln_gain.reshape(1, D)
    emb, normed, gl, cols = stem_call(
        counts,
        vis_index.reshape(scenes, TOK, 1),
        patches,
        w_stem,
        gain,
        table,
        genc,
        out_grad.reshape(scenes, TOK, D),
    )
    emb, normed, gl = [a.reshape(tokens, D) for a in (emb, normed, gl)]
    cols = cols.reshape(tokens, cols.shape[2])
    normed_far = swap(normed, "group", group, 1)
    gl_far = swap(gl, "group", group, 1)

    packs, grads = [], []
    for f in range(fars):
        packs.append(attention_call(both_counts, normed, normed_far, gl, gl_far, weights[f]))
        grads.append(weight_grad_call(normed, normed_far, gl, gl_far, packs[f]))
    shares = [reduce_rows(g, "dp", dp, 2) for g in grads]
    total = shares[0]
    for f in range(1, fars):
        total = total + swap(shares[f].astype(BF16), "group", group, 2 * f).astype(F32)
    grad_w_qkv = total[:, : 3 * width].reshape(total.shape[0], 3, width)
    grad_w_out = total[:, 3 * width :].T

    back_far = swap(back_call(packs, weights, 1, False, F32), "group", group, 1)
    mixed_far = swap(back_call(packs, weights, 1, True, BF16), "group", group, 1)
    stem_local = tail_call(counts, back_far, emb, gl, cols, gain, packs, weights)
    grad_w_stem = sum_stem(stem_local, dp, group)
    output = output_call(counts, mixed_far, emb, packs, weights)
    return (output.reshape(scenes, GROUPS, CAP, D), grad_w_stem, grad_w_qkv, grad_w_out)


def solution(mesh):
    sizes = dict(mesh.shape)
    return jax.shard_map(
        functools.partial(on_device, sizes["dp"], sizes["group"]),
        mesh=mesh,
        in_specs=(
            P(("dp", "group"), None, None),
            P(("dp", "group"), None, None),
            P(("dp", "group"), None),
            P(),
            P(),
            P("dp", None, "group"),
            P("group", "dp"),
            P(("dp", "group"), None, None, None),
        ),
        out_specs=(
            P(("dp", "group"), None, None, None),
            P(),
            P("dp", None, "group"),
            P("group", "dp"),
        ),
        check_vma=False,
    )
```

time: 675 us -> 303 us (0.45)
  waiting for transfers between devices: 400 us -> 67.1 us
  matrix products: 140 us -> 0 us
  Pallas kernels: 0 us -> 95.4 us
  starting transfers between devices: 0.32 us -> 61.6 us
  blocking collectives: 32.7 us -> 0 us
  other arithmetic: 16.8 us -> 8.38 us
  local copies, waits for them, and re-layouts: 65.9 us -> 57.7 us
    reduce_scatter x4 -> x0, waiting for transfers between devices: 220 us -> none  [the longest x1 78.4 us: on_device(): lax.psum_scatter(grad_qkv_w, 'dp', scatter_dimension=0, tiled=True)]
    dot_general x17 -> x0, matrix products: 129 us -> none  [the longest x1 24.3 us: attend_backward(): jnp.einsum('nhqk,nqhe->nkhe', grad_score, query_rows, preferred_element_t...]
    psum x1 -> x0, waiting for transfers between devices: 125 us -> none  [on_device(): grad_w_stem = lax.psum(stem_local, ('dp', 'group'))]
    pallas_call x0 -> x9, Pallas kernels: none -> 95.4 us  [the longest x2 45.3 us: attention_call(): pl.pallas_call(attention_kernel, grid=(2, steps), in_specs=[pl.BlockSpec(...]
    ppermute x0 -> x51, waiting for transfers between devices: none -> 67.1 us  [the longest x33 40.1 us: swap(): return lax.ppermute(x, axis, [(i, i ^ bit) for i in range(size)])]
    ppermute x0 -> x51, starting transfers between devices: none -> 61.6 us  [the longest x33 36.6 us: swap(): return lax.ppermute(x, axis, [(i, i ^ bit) for i in range(size)])]
    all_gather x3 -> x0, waiting for transfers between devices: 53.1 us -> none  [the longest x1 34.6 us: on_device(): lax.all_gather(wq_rows, 'group', axis=2, tiled=True)]
    all_gather x1 -> x0, blocking collectives: 32.7 us -> none  [on_device(): lax.all_gather(w_out, 'dp', axis=1, tiled=True)]
  transfers between devices with their start and end apart: 8 -> 51, of which waited for: 6 -> 25; matrix products, arithmetic and copies ran while one was open for 26% -> 15% of each run, Pallas kernels for 0% -> 15%
where the time goes in v1:
time: 303 us; the launch traced here: 302 us
  Pallas kernels  95.4 us (31%)
  waiting for transfers between devices  67.1 us (22%)
  starting transfers between devices  61.6 us (20%)
  local copies, waits for them, and re-layouts  57.7 us (19%)
  between operations  11.6 us (4%)
  other arithmetic  8.38 us (3%)
    pallas_call x2, Pallas kernels, attention_call(): pl.pallas_call(attention_kernel, grid=(2, steps), in_specs=[pl.BlockSpec(...  45.3 us
    ppermute x33, waiting for transfers between devices, swap(): return lax.ppermute(x, axis, [(i, i ^ bit) for i in range(size)])  40.1 us
    ppermute x33, starting transfers between devices, swap(): return lax.ppermute(x, axis, [(i, i ^ bit) for i in range(size)])  36.6 us
    unnamed x66, local copies, waits for them, and re-layouts  24.5 us
    pallas_call x2, Pallas kernels, weight_grad_call(): pl.pallas_call(weight_grad_kernel, grid=(2, steps), in_specs=[first, seco...  19.5 us
    ppermute x8, waiting for transfers between devices, ring_gather(): ahead = lax.ppermute(ahead, axis, forward)  18 us
    dynamic_slice x8, local copies, waits for them, and re-layouts, reduce_rows(): keep = lax.dynamic_index_in_dim(part, low, 1, keepdims=False)  13.8 us
    ppermute x8, starting transfers between devices, ring_gather(): ahead = lax.ppermute(ahead, axis, forward)  13 us
  transfers between devices with their start and end apart: 51, of which 25 were waited for; matrix products, arithmetic and copies ran while one was open for 15% of the time, Pallas kernels for 15%

profile of v1, /device:TPU:0, one launch (start us, length us, event | category | flops | bytes accessed | tf_op | source)
XLA Modules:
  0.0 301.8 jit_solution(13818923408237563434)
XLA Ops:
  12.7 2.9 collective-permute-start.10
  21.2 6.3 %stem_norm.1 = (bf16[6,144,1024]{2,1,0:T(8,128)(2,1)S(1)}, bf16[6,144,1024]{2,1,0:T(8,128)(2,1)}, bf16[6,144,1024]{2,1,0:T(8,128)(2,1)}, bf16[6,144,256]{2,1,0:T(8,128)(2,1)S(1)}) custom-call(s32[6,3]{1,0:T(8,128)S(1)} %copy.76.cnt_ref, s32[6,144,1]{2,1,0:T(8,128)S(1)} %reshape.170.idx_ref, bf16[6,144,640]{2,1,0:T(8,128)(2,1)S(1)} %copy-done.18, ...), custom_call_target="tpu_custom_call" | custom-call | flops 8000000000 | bytes 12000000 | tf_op jit(solution)/shard_map/stem_norm/pallas_call | solution.py:111
  41.6 2.4 collective-permute-done.11
  68.8 4.1 %collective-permute-done.9 = bf16[128,1024]{1,0:T(8,128)(2,1)S(1)} collective-permute-done((bf16[128,1024]{1,0:T(8,128)(2,1)S(1)}, bf16[128,1024]{1,0:T(8,128)(2,1)S(1)}, u32[]{:S(2)}, u32[]{:S(2)}) %collective-permute-start.9) | collective-permute-done | bytes 262176 | tf_op jit(solution)/shard_map/ppermute | solution.py:403
  73.0 4.4 %collective-permute-done.17 = bf16[128,1024]{1,0:T(8,128)(2,1)S(1)} collective-permute-done((bf16[128,1024]{1,0:T(8,128)(2,1)S(1)}, bf16[128,1024]{1,0:T(8,128)(2,1)S(1)}, u32[]{:S(2)}, u32[]{:S(2)}) %collective-permute-start.17) | collective-permute-done | bytes 262176 | tf_op jit(solution)/shard_map/ppermute | solution.py:403
  78.7 22.6 %attention.3.refs_1_.pack_ref = bf16[1728,1024]{1,0:T(8,128)(2,1)} custom-call(s32[2,6,3]{2,1,0:T(8,128)S(1)} %pad_add_fusion.cnt_ref, bf16[864,1024]{1,0:T(8,128)(2,1)S(1)} %bitcast.115, bf16[864,1024]{1,0:T(8,128)(2,1)} %collective-permute-done.1.nb_ref, bf16[864,1024]{1,0:T(8,128)(2,1)S(1)} %bitcast.107, bf16[864,1024]{1,0:T(8,128)(2,1)} %collective-permute-done.2.gb_ref, ...), custom_call_target="tpu_custom_call" | custom-call | flops 22000001024 | bytes 14000000 | tf_op jit(solution)/shard_map/attention/pallas_call | solution.py:201
  101.4 22.6 %attention.2.refs_0_.pack_ref = bf16[1728,1024]{1,0:T(8,128)(2,1)} custom-call(s32[2,6,3]{2,1,0:T(8,128)S(1)} %pad_add_fusion.cnt_ref, bf16[864,1024]{1,0:T(8,128)(2,1)S(1)} %bitcast.116, bf16[864,1024]{1,0:T(8,128)(2,1)} %collective-permute-done.1.nb_ref, bf16[864,1024]{1,0:T(8,128)(2,1)S(1)} %bitcast.108, bf16[864,1024]{1,0:T(8,128)(2,1)} %collective-permute-done.2.gb_ref, ...), custom_call_target="tpu_custom_call" | custom-call | flops 22000001024 | bytes 14000000 | tf_op jit(solution)/shard_map/attention/pallas_call | solution.py:201
  125.6 5.8 %back_qkv.1 = f32[864,1024]{1,0:T(8,128)} custom-call(bf16[1728,1024]{1,0:T(8,128)(2,1)} %attention.2.refs_0_.pack_ref, bf16[1728,1024]{1,0:T(8,128)(2,1)} %attention.3.refs_1_.pack_ref, bf16[1024,1024]{1,0:T(8,128)(2,1)S(1)} %copy-done.1, bf16[1024,1024]{1,0:T(8,128)(2,1)S(1)} %copy-done.4), custom_call_target="tpu_custom_call" | custom-call | flops 3000000000 | bytes 10000000 | tf_op jit(solution)/shard_map/back_qkv/pallas_call | solution.py:279
  131.4 9.7 %weight_grad.3 = f32[1024,1024]{1,0:T(8,128)} custom-call(bf16[864,1024]{1,0:T(8,128)(2,1)S(1)} %bitcast.117, bf16[864,1024]{1,0:T(8,128)(2,1)} %collective-permute-done.1.nb_ref, bf16[864,1024]{1,0:T(8,128)(2,1)S(1)} %bitcast.109, bf16[864,1024]{1,0:T(8,128)(2,1)} %collective-permute-done.2.gb_ref, bf16[1728,1024]{1,0:T(8,128)(2,1)} %attention.3.refs_1_.pack_ref), custom_call_target="tpu_custom_call" | custom-call | flops 4000000000 | bytes 15000000 | tf_op jit(solution)/shard_map/weight_grad/pallas_call | solution.py:244
  141.2 2.7 fusion.22
  149.9 2.3 constant_dynamic-slice_fusion.8
  152.1 2.6 copy.82
  154.7 2.1 copy.90
  157.3 2.3 constant_dynamic-slice_fusion.10
  159.5 2.5 copy.84
  162.1 9.7 %weight_grad.2 = f32[1024,1024]{1,0:T(8,128)} custom-call(bf16[864,1024]{1,0:T(8,128)(2,1)S(1)} %bitcast.118, bf16[864,1024]{1,0:T(8,128)(2,1)} %collective-permute-done.1.nb_ref, bf16[864,1024]{1,0:T(8,128)(2,1)S(1)} %bitcast.110, bf16[864,1024]{1,0:T(8,128)(2,1)} %collective-permute-done.2.gb_ref, bf16[1728,1024]{1,0:T(8,128)(2,1)} %attention.2.refs_0_.pack_ref), custom_call_target="tpu_custom_call" | custom-call | flops 4000000000 | bytes 15000000 | tf_op jit(solution)/shard_map/weight_grad/pallas_call | solution.py:244
  171.8 2.7 fusion.23
  187.6 3.5 %back_context.1 = bf16[864,1024]{1,0:T(8,128)(2,1)} custom-call(bf16[1728,1024]{1,0:T(8,128)(2,1)} %attention.2.refs_0_.pack_ref, bf16[1728,1024]{1,0:T(8,128)(2,1)} %attention.3.refs_1_.pack_ref, bf16[1024,1024]{1,0:T(8,128)(2,1)S(1)} %copy-done.2, bf16[1024,1024]{1,0:T(8,128)(2,1)S(1)} %copy-done.5), custom_call_target="tpu_custom_call" | custom-call | flops 3000000000 | bytes 10000000 | tf_op jit(solution)/shard_map/back_context/pallas_call | solution.py:279
  195.7 10.3 %tail.1 = f32[640,1024]{1,0:T(8,128)} custom-call(s32[6,3]{1,0:T(8,128)S(1)} %copy.76.cnt_ref, f32[864,1024]{1,0:T(8,128)} %collective-permute-done.19.recv_ref, bf16[864,1024]{1,0:T(8,128)(2,1)S(1)} %bitcast.112, bf16[864,1024]{1,0:T(8,128)(2,1)S(1)} %bitcast.111, bf16[864,256]{1,0:T(8,128)(2,1)S(1)} %bitcast.119, f32[1,1024]{1,0:T(1,128)S(1)} %bitcast.121, ...), custom_call_target="tpu_custom_call" | custom-call | flops 5000000000 | bytes 18000000 | tf_op jit(solution)/shard_map/tail/pallas_call | solution.py:328
  209.1 2.7 collective-permute-start.36
  215.5 5.8 %collective-permute-done.36 = bf16[128,512]{0,1:T(8,128)(2,1)S(1)} collective-permute-done((bf16[128,512]{0,1:T(8,128)(2,1)S(1)}, bf16[128,512]{0,1:T(8,128)(2,1)S(1)}, u32[]{:S(2)}, u32[]{:S(2)}) %collective-permute-start.36) | collective-permute-done | bytes 131104 | tf_op jit(solution)/shard_map/ppermute | solution.py:379
  221.4 3.2 %collective-permute-start.45 = (bf16[128,512]{0,1:T(8,128)(2,1)S(1)}, bf16[128,512]{0,1:T(8,128)(2,1)S(1)}, u32[]{:S(2)}, u32[]{:S(2)}) collective-permute-start(bf16[128,512]{0,1:T(8,128)(2,1)S(1)} %get-tuple-element.34), channel_id=1, source_target_pairs={{0,24},{4,28},{8,16},{12,20},{16,8},{20,12},{24,0},{28,4},{1,25},{... | collective-permute-start | bytes 393224 | tf_op jit(solution)/shard_map/ppermute | solution.py:379
  224.6 8.0 %collective-permute-start.47 = (bf16[128,512]{0,1:T(8,128)(2,1)S(1)}, bf16[128,512]{0,1:T(8,128)(2,1)S(1)}, u32[]{:S(2)}, u32[]{:S(2)}) collective-permute-start(bf16[128,512]{0,1:T(8,128)(2,1)S(1)} %get-tuple-element.36), channel_id=1, source_target_pairs={{0,8},{4,12},{8,0},{12,4},{16,24},{20,28},{24,16},{28,20},{1,9},{5... | collective-permute-start | bytes 393224 | tf_op jit(solution)/shard_map/ppermute | solution.py:379
  236.6 2.6 collective-permute-done.21
  245.5 4.3 %collective-permute-done.48 = bf16[128,512]{0,1:T(8,128)(2,1)S(1)} collective-permute-done((bf16[128,512]{0,1:T(8,128)(2,1)S(1)}, bf16[128,512]{0,1:T(8,128)(2,1)S(1)}, u32[]{:S(2)}, u32[]{:S(2)}) %collective-permute-start.48) | collective-permute-done | bytes 131104 | tf_op jit(solution)/shard_map/ppermute | solution.py:379
  254.8 5.9 %collective-permute-done.25 = f32[80,256]{1,0:T(8,128)S(1)} collective-permute-done((f32[80,256]{1,0:T(8,128)S(1)}, f32[80,256]{1,0:T(8,128)S(1)}, u32[]{:S(2)}, u32[]{:S(2)}) %collective-permute-start.25) | collective-permute-done | bytes 81952 | tf_op jit(solution)/shard_map/ppermute | solution.py:379
  260.7 2.3 collective-permute-start.41
  263.3 5.1 %collective-permute-done.27 = bf16[80,256]{1,0:T(8,128)(2,1)S(1)} collective-permute-done((bf16[80,256]{1,0:T(8,128)(2,1)S(1)}, bf16[80,256]{1,0:T(8,128)(2,1)S(1)}, u32[]{:S(2)}, u32[]{:S(2)}) %collective-permute-start.27) | collective-permute-done | bytes 40992 | tf_op jit(solution)/shard_map/ppermute | solution.py:379
  268.5 5.5 %collective-permute-done.28 = bf16[80,256]{1,0:T(8,128)(2,1)S(1)} collective-permute-done((bf16[80,256]{1,0:T(8,128)(2,1)S(1)}, bf16[80,256]{1,0:T(8,128)(2,1)S(1)}, u32[]{:S(2)}, u32[]{:S(2)}) %collective-permute-start.28) | collective-permute-done | bytes 40992 | tf_op jit(solution)/shard_map/ppermute | solution.py:379
  274.3 5.5 %collective-permute-done.29 = bf16[80,256]{1,0:T(8,128)(2,1)S(1)} collective-permute-done((bf16[80,256]{1,0:T(8,128)(2,1)S(1)}, bf16[80,256]{1,0:T(8,128)(2,1)S(1)}, u32[]{:S(2)}, u32[]{:S(2)}) %collective-permute-start.29) | collective-permute-done | bytes 40992 | tf_op jit(solution)/shard_map/ppermute | solution.py:379
  285.4 2.6 collective-permute-done.31
  293.9 4.7 %layer_output.1 = bf16[864,1024]{1,0:T(8,128)(2,1)} custom-call(s32[6,3]{1,0:T(8,128)S(1)} %copy.76.cnt_ref, bf16[864,1024]{1,0:T(8,128)(2,1)} %collective-permute-done.18.recv_ref, bf16[864,1024]{1,0:T(8,128)(2,1)S(1)} %bitcast.113, bf16[1728,1024]{1,0:T(8,128)(2,1)} %attention.2.refs_0_.pack_ref, bf16[1728,1024]{1,0:T(8,128)(2,1)} %attention.3.refs_1_.pack_ref, ...), custom_call_target="tpu_custom_call" | custom-call | flops 1000000000 | bytes 10000000 | tf_op jit(solution)/shard_map/layer_output/pallas_call | solution.py:364
  (229 shorter events, 110.2 us)
Async XLA Ops:
  12.7 22.0 %collective-permute-start.10 = (bf16[128,1024]{1,0:T(8,128)(2,1)}, bf16[128,1024]{1,0:T(8,128)(2,1)}, u32[]{:S(2)}, u32[]{:S(2)}) collective-permute-start(bf16[128,1024]{1,0:T(8,128)(2,1)} %get-tuple-element.48), channel_id=1, source_target_pairs={{0,2},{1,3},{2,0},{3,1},{4,6},{5,7},{6,4},{7,5},{8,10},{9,11},{10,... | collective-permute-start | bytes 786440 | tf_op jit(solution)/shard_map/ppermute | solution.py:379
  15.6 21.9 %collective-permute-start.3 = (bf16[128,1024]{1,0:T(8,128)(2,1)}, bf16[128,1024]{1,0:T(8,128)(2,1)}, u32[]{:S(2)}, u32[]{:S(2)}) collective-permute-start(bf16[128,1024]{1,0:T(8,128)(2,1)} %get-tuple-element.48), channel_id=1, source_target_pairs={{0,8},{8,16},{16,24},{24,28},{28,20},{20,12},{12,4},{4,0},{1,9},{9... | collective-permute-start | bytes 786440 | tf_op jit(solution)/shard_map/ppermute | solution.py:403
  17.2 21.8 %collective-permute-start.4 = (bf16[128,1024]{1,0:T(8,128)(2,1)}, bf16[128,1024]{1,0:T(8,128)(2,1)}, u32[]{:S(2)}, u32[]{:S(2)}) collective-permute-start(bf16[128,1024]{1,0:T(8,128)(2,1)} %get-tuple-element.48), channel_id=1, source_target_pairs={{8,0},{16,8},{24,16},{28,24},{20,28},{12,20},{4,12},{0,4},{9,1},{1... | collective-permute-start | bytes 786440 | tf_op jit(solution)/shard_map/ppermute | solution.py:406
  17.6 16.8 %collective-permute-start = (s32[6,3]{0,1:T(4,128)S(1)}, s32[6,3]{0,1:T(4,128)S(1)}, u32[]{:S(2)}, u32[]{:S(2)}) collective-permute-start(s32[6,3]{0,1:T(4,128)S(1)} %copy-done.28), channel_id=1, source_target_pairs={{0,1},{1,0},{2,3},{3,2},{4,5},{5,4},{6,7},{7,6},{8,9},{9,8},{10,11... | collective-permute-start | bytes 224 | tf_op jit(solution)/shard_map/ppermute | solution.py:379
  29.6 47.7 %collective-permute-start.2 = (bf16[864,1024]{1,0:T(8,128)(2,1)}, bf16[864,1024]{1,0:T(8,128)(2,1)}, u32[]{:S(2)}, u32[]{:S(2)}) collective-permute-start(bf16[864,1024]{1,0:T(8,128)(2,1)} %bitcast.106), channel_id=1, source_target_pairs={{0,1},{1,0},{2,3},{3,2},{4,5},{5,4},{6,7},{7,6},{8,9},{9,8},{10,11... | collective-permute-start | bytes 5308424 | tf_op jit(solution)/shard_map/ppermute | solution.py:379
  34.5 42.9 %collective-permute-start.1 = (bf16[864,1024]{1,0:T(8,128)(2,1)}, bf16[864,1024]{1,0:T(8,128)(2,1)}, u32[]{:S(2)}, u32[]{:S(2)}) collective-permute-start(bf16[864,1024]{1,0:T(8,128)(2,1)} %bitcast.114), channel_id=1, source_target_pairs={{0,1},{1,0},{2,3},{3,2},{4,5},{5,4},{6,7},{7,6},{8,9},{9,8},{10,11... | collective-permute-start | bytes 5308424 | tf_op jit(solution)/shard_map/ppermute | solution.py:379
  34.6 9.4 %collective-permute-start.11 = (bf16[128,1024]{1,0:T(8,128)(2,1)}, bf16[128,1024]{1,0:T(8,128)(2,1)S(1)}, u32[]{:S(2)}, u32[]{:S(2)}) collective-permute-start(bf16[128,1024]{1,0:T(8,128)(2,1)} %collective-permute-done.10), channel_id=1, source_target_pairs={{0,8},{8,16},{16,24},{24,28},{28,20},{20,12},{12,4},{4,0},{1,9},{9... | collective-permute-start | bytes 786440 | tf_op jit(solution)/shard_map/ppermute | solution.py:403
  39.0 10.6 %collective-permute-start.5 = (bf16[128,1024]{1,0:T(8,128)(2,1)}, bf16[128,1024]{1,0:T(8,128)(2,1)S(1)}, u32[]{:S(2)}, u32[]{:S(2)}) collective-permute-start(bf16[128,1024]{1,0:T(8,128)(2,1)} %collective-permute-done.3), channel_id=1, source_target_pairs={{0,8},{8,16},{16,24},{24,28},{28,20},{20,12},{12,4},{4,0},{1,9},{9... | collective-permute-start | bytes 786440 | tf_op jit(solution)/shard_map/ppermute | solution.py:403
  46.2 9.2 %collective-permute-start.13 = (bf16[128,1024]{1,0:T(8,128)(2,1)S(1)}, bf16[128,1024]{1,0:T(8,128)(2,1)S(1)}, u32[]{:S(2)}, u32[]{:S(2)}) collective-permute-start(bf16[128,1024]{1,0:T(8,128)(2,1)S(1)} %collective-permute-done.11), channel_id=1, source_target_pairs={{0,8},{8,16},{16,24},{24,28},{28,20},{20,12},{12,4},{4,0},{1,9},{9... | collective-permute-start | bytes 786440 | tf_op jit(solution)/shard_map/ppermute | solution.py:403
  67.1 10.2 %collective-permute-start.17 = (bf16[128,1024]{1,0:T(8,128)(2,1)S(1)}, bf16[128,1024]{1,0:T(8,128)(2,1)S(1)}, u32[]{:S(2)}, u32[]{:S(2)}) collective-permute-start(bf16[128,1024]{1,0:T(8,128)(2,1)S(1)} %collective-permute-done.15), channel_id=1, source_target_pairs={{0,8},{8,16},{16,24},{24,28},{28,20},{20,12},{12,4},{4,0},{1,9},{9... | collective-permute-start | bytes 786440 | tf_op jit(solution)/shard_map/ppermute | solution.py:403
  131.4 62.7 %collective-permute-start.19 = (f32[864,1024]{1,0:T(8,128)}, f32[864,1024]{1,0:T(8,128)}, u32[]{:S(2)}, u32[]{:S(2)}) collective-permute-start(f32[864,1024]{1,0:T(8,128)} %back_qkv.1), channel_id=1, source_target_pairs={{0,1},{1,0},{2,3},{3,2},{4,5},{5,4},{6,7},{7,6},{8,9},{9,8},{10,11... | collective-permute-start | bytes 10616840 | tf_op jit(solution)/shard_map/ppermute | solution.py:379
  148.3 59.2 %collective-permute-start.42 = (bf16[4,128,512]{1,2,0:T(8,128)(2,1)}, bf16[4,128,512]{1,2,0:T(8,128)(2,1)}, u32[]{:S(2)}, u32[]{:S(2)}) collective-permute-start(bf16[4,128,512]{1,2,0:T(8,128)(2,1)} %bitcast.134), channel_id=1, source_target_pairs={{0,4},{4,0},{8,12},{12,8},{16,20},{20,16},{24,28},{28,24},{1,5},{5... | collective-permute-start | bytes 1572872 | tf_op jit(solution)/shard_map/ppermute | solution.py:379
  156.8 52.4 %collective-permute-start.46 = (bf16[4,128,512]{1,2,0:T(8,128)(2,1)}, bf16[4,128,512]{1,2,0:T(8,128)(2,1)}, u32[]{:S(2)}, u32[]{:S(2)}) collective-permute-start(bf16[4,128,512]{1,2,0:T(8,128)(2,1)} %bitcast.133), channel_id=1, source_target_pairs={{0,4},{4,0},{8,12},{12,8},{16,20},{20,16},{24,28},{28,24},{1,5},{5... | collective-permute-start | bytes 1572872 | tf_op jit(solution)/shard_map/ppermute | solution.py:379
  177.7 15.1 %collective-permute-start.34 = (bf16[4,128,512]{1,2,0:T(8,128)(2,1)}, bf16[4,128,512]{1,2,0:T(8,128)(2,1)}, u32[]{:S(2)}, u32[]{:S(2)}) collective-permute-start(bf16[4,128,512]{1,2,0:T(8,128)(2,1)} %bitcast.105), channel_id=1, source_target_pairs={{0,4},{4,0},{8,12},{12,8},{16,20},{20,16},{24,28},{28,24},{1,5},{5... | collective-permute-start | bytes 1572872 | tf_op jit(solution)/shard_map/ppermute | solution.py:379
  182.7 30.3 %collective-permute-start.38 = (bf16[4,128,512]{1,2,0:T(8,128)(2,1)}, bf16[4,128,512]{1,2,0:T(8,128)(2,1)}, u32[]{:S(2)}, u32[]{:S(2)}) collective-permute-start(bf16[4,128,512]{1,2,0:T(8,128)(2,1)} %bitcast.104), channel_id=1, source_target_pairs={{0,4},{4,0},{8,12},{12,8},{16,20},{20,16},{24,28},{28,24},{1,5},{5... | collective-permute-start | bytes 1572872 | tf_op jit(solution)/shard_map/ppermute | solution.py:379
  192.9 99.5 %collective-permute-start.18 = (bf16[864,1024]{1,0:T(8,128)(2,1)}, bf16[864,1024]{1,0:T(8,128)(2,1)}, u32[]{:S(2)}, u32[]{:S(2)}) collective-permute-start(bf16[864,1024]{1,0:T(8,128)(2,1)} %back_context.1), channel_id=1, source_target_pairs={{0,1},{1,0},{2,3},{3,2},{4,5},{5,4},{6,7},{7,6},{8,9},{9,8},{10,11... | collective-permute-start | bytes 5308424 | tf_op jit(solution)/shard_map/ppermute | solution.py:379
  194.1 20.6 %collective-permute-start.35 = (bf16[128,512]{0,1:T(8,128)(2,1)S(1)}, bf16[128,512]{0,1:T(8,128)(2,1)S(1)}, u32[]{:S(2)}, u32[]{:S(2)}) collective-permute-start(bf16[128,512]{0,1:T(8,128)(2,1)S(1)} %get-tuple-element.39), channel_id=1, source_target_pairs={{0,8},{4,12},{8,0},{12,4},{16,24},{20,28},{24,16},{28,20},{1,9},{5... | collective-permute-start | bytes 393224 | tf_op jit(solution)/shard_map/ppermute | solution.py:379
  207.6 17.1 %collective-permute-start.20 = (f32[320,1024]{1,0:T(8,128)S(1)}, f32[320,1024]{1,0:T(8,128)S(1)}, u32[]{:S(2)}, u32[]{:S(2)}) collective-permute-start(f32[320,1024]{1,0:T(8,128)S(1)} %constant_dynamic-slice_fusion.3), channel_id=1, source_target_pairs={{0,1},{1,0},{2,3},{3,2},{4,5},{5,4},{6,7},{7,6},{8,9},{9,8},{10,11... | collective-permute-start | bytes 3932168 | tf_op jit(solution)/shard_map/ppermute | solution.py:379
  209.1 12.2 %collective-permute-start.36 = (bf16[128,512]{0,1:T(8,128)(2,1)S(1)}, bf16[128,512]{0,1:T(8,128)(2,1)S(1)}, u32[]{:S(2)}, u32[]{:S(2)}) collective-permute-start(bf16[128,512]{0,1:T(8,128)(2,1)S(1)} %get-tuple-element.41), channel_id=1, source_target_pairs={{0,16},{4,20},{8,24},{12,28},{16,0},{20,4},{24,8},{28,12},{1,17},{... | collective-permute-start | bytes 393224 | tf_op jit(solution)/shard_map/ppermute | solution.py:379
  214.7 18.3 %collective-permute-start.43 = (bf16[128,512]{0,1:T(8,128)(2,1)S(1)}, bf16[128,512]{0,1:T(8,128)(2,1)S(1)}, u32[]{:S(2)}, u32[]{:S(2)}) collective-permute-start(bf16[128,512]{0,1:T(8,128)(2,1)S(1)} %get-tuple-element.33), channel_id=1, source_target_pairs={{0,8},{4,12},{8,0},{12,4},{16,24},{20,28},{24,16},{28,20},{1,9},{5... | collective-permute-start | bytes 393224 | tf_op jit(solution)/shard_map/ppermute | solution.py:379
  221.4 13.3 %collective-permute-start.44 = (bf16[128,512]{0,1:T(8,128)(2,1)S(1)}, bf16[128,512]{0,1:T(8,128)(2,1)S(1)}, u32[]{:S(2)}, u32[]{:S(2)}) collective-permute-start(bf16[128,512]{0,1:T(8,128)(2,1)S(1)} %get-tuple-element.35), channel_id=1, source_target_pairs={{0,16},{4,20},{8,24},{12,28},{16,0},{20,4},{24,8},{28,12},{1,17},{... | collective-permute-start | bytes 393224 | tf_op jit(solution)/shard_map/ppermute | solution.py:379
  221.4 13.7 %collective-permute-start.45 = (bf16[128,512]{0,1:T(8,128)(2,1)S(1)}, bf16[128,512]{0,1:T(8,128)(2,1)S(1)}, u32[]{:S(2)}, u32[]{:S(2)}) collective-permute-start(bf16[128,512]{0,1:T(8,128)(2,1)S(1)} %get-tuple-element.34), channel_id=1, source_target_pairs={{0,24},{4,28},{8,16},{12,20},{16,8},{20,12},{24,0},{28,4},{1,25},{... | collective-permute-start | bytes 393224 | tf_op jit(solution)/shard_map/ppermute | solution.py:379
  224.6 18.8 %collective-permute-start.47 = (bf16[128,512]{0,1:T(8,128)(2,1)S(1)}, bf16[128,512]{0,1:T(8,128)(2,1)S(1)}, u32[]{:S(2)}, u32[]{:S(2)}) collective-permute-start(bf16[128,512]{0,1:T(8,128)(2,1)S(1)} %get-tuple-element.36), channel_id=1, source_target_pairs={{0,8},{4,12},{8,0},{12,4},{16,24},{20,28},{24,16},{28,20},{1,9},{5... | collective-permute-start | bytes 393224 | tf_op jit(solution)/shard_map/ppermute | solution.py:379
  239.2 10.6 %collective-permute-start.48 = (bf16[128,512]{0,1:T(8,128)(2,1)S(1)}, bf16[128,512]{0,1:T(8,128)(2,1)S(1)}, u32[]{:S(2)}, u32[]{:S(2)}) collective-permute-start(bf16[128,512]{0,1:T(8,128)(2,1)S(1)} %get-tuple-element.38), channel_id=1, source_target_pairs={{0,16},{4,20},{8,24},{12,28},{16,0},{20,4},{24,8},{28,12},{1,17},{... | collective-permute-start | bytes 393224 | tf_op jit(solution)/shard_map/ppermute | solution.py:379
  240.5 9.3 %collective-permute-start.49 = (bf16[128,512]{0,1:T(8,128)(2,1)S(1)}, bf16[128,512]{0,1:T(8,128)(2,1)S(1)}, u32[]{:S(2)}, u32[]{:S(2)}) collective-permute-start(bf16[128,512]{0,1:T(8,128)(2,1)S(1)} %get-tuple-element.37), channel_id=1, source_target_pairs={{0,24},{4,28},{8,16},{12,20},{16,8},{20,12},{24,0},{28,4},{1,25},{... | collective-permute-start | bytes 393224 | tf_op jit(solution)/shard_map/ppermute | solution.py:379
  243.3 36.7 %collective-permute-start.39 = (bf16[128,512]{0,1:T(8,128)(2,1)S(1)}, bf16[128,512]{0,1:T(8,128)(2,1)S(1)}, u32[]{:S(2)}, u32[]{:S(2)}) collective-permute-start(bf16[128,512]{0,1:T(8,128)(2,1)S(1)} %get-tuple-element.42), channel_id=1, source_target_pairs={{0,8},{4,12},{8,0},{12,4},{16,24},{20,28},{24,16},{28,20},{1,9},{5... | collective-permute-start | bytes 393224 | tf_op jit(solution)/shard_map/ppermute | solution.py:379
  243.5 9.6 %collective-permute-start.24 = (f32[80,256]{1,0:T(8,128)S(1)}, f32[80,256]{1,0:T(8,128)S(1)}, u32[]{:S(2)}, u32[]{:S(2)}) collective-permute-start(f32[80,256]{1,0:T(8,128)S(1)} %get-tuple-element.45), channel_id=1, source_target_pairs={{0,8},{4,12},{8,0},{12,4},{16,24},{20,28},{24,16},{28,20},{1,9},{5... | collective-permute-start | bytes 245768 | tf_op jit(solution)/shard_map/ppermute | solution.py:379
  249.8 10.9 %collective-permute-start.25 = (f32[80,256]{1,0:T(8,128)S(1)}, f32[80,256]{1,0:T(8,128)S(1)}, u32[]{:S(2)}, u32[]{:S(2)}) collective-permute-start(f32[80,256]{1,0:T(8,128)S(1)} %get-tuple-element.47), channel_id=1, source_target_pairs={{0,16},{4,20},{8,24},{12,28},{16,0},{20,4},{24,8},{28,12},{1,17},{... | collective-permute-start | bytes 245768 | tf_op jit(solution)/shard_map/ppermute | solution.py:379
  249.8 13.2 %collective-permute-start.26 = (f32[80,256]{1,0:T(8,128)S(1)}, f32[80,256]{1,0:T(8,128)S(1)}, u32[]{:S(2)}, u32[]{:S(2)}) collective-permute-start(f32[80,256]{1,0:T(8,128)S(1)} %get-tuple-element.46), channel_id=1, source_target_pairs={{0,24},{4,28},{8,16},{12,20},{16,8},{20,12},{24,0},{28,4},{1,25},{... | collective-permute-start | bytes 245768 | tf_op jit(solution)/shard_map/ppermute | solution.py:379
  253.1 27.0 %collective-permute-start.40 = (bf16[128,512]{0,1:T(8,128)(2,1)S(1)}, bf16[128,512]{0,1:T(8,128)(2,1)S(1)}, u32[]{:S(2)}, u32[]{:S(2)}) collective-permute-start(bf16[128,512]{0,1:T(8,128)(2,1)S(1)} %get-tuple-element.44), channel_id=1, source_target_pairs={{0,16},{4,20},{8,24},{12,28},{16,0},{20,4},{24,8},{28,12},{1,17},{... | collective-permute-start | bytes 393224 | tf_op jit(solution)/shard_map/ppermute | solution.py:379
  260.7 19.3 %collective-permute-start.41 = (bf16[128,512]{0,1:T(8,128)(2,1)S(1)}, bf16[128,512]{0,1:T(8,128)(2,1)S(1)}, u32[]{:S(2)}, u32[]{:S(2)}) collective-permute-start(bf16[128,512]{0,1:T(8,128)(2,1)S(1)} %get-tuple-element.43), channel_id=1, source_target_pairs={{0,24},{4,28},{8,16},{12,20},{16,8},{20,12},{24,0},{28,4},{1,25},{... | collective-permute-start | bytes 393224 | tf_op jit(solution)/shard_map/ppermute | solution.py:379
  288.9 9.9 %collective-permute-start.33 = (bf16[320,1024]{1,0:T(8,128)(2,1)S(1)}, bf16[320,1024]{1,0:T(8,128)(2,1)}, u32[]{:S(2)}, u32[]{:S(2)}) collective-permute-start(bf16[320,1024]{1,0:T(8,128)(2,1)S(1)} %constant_dynamic-update-slice_fusion.9), channel_id=1, source_target_pairs={{0,1},{1,0},{2,3},{3,2},{4,5},{5,4},{6,7},{7,6},{8,9},{9,8},{10,11... | collective-permute-start | bytes 1966088 | tf_op jit(solution)/shard_map/ppermute | solution.py:379
  (48 other events, 350.8 us)

commit v2 on v1

v2 whole, which is shorter than its diff:
```python
import functools

import jax
import jax.numpy as jnp
from jax import lax
from jax.experimental import pallas as pl
from jax.experimental.pallas import tpu as pltpu
from jax.sharding import PartitionSpec as P

D = 1024
HD = 64
GROUPS = 3
CAP = 48
GRID = 12
PIX = 64
TOK = GROUPS * CAP
PAIR = 128
GROUP_BANDS = ((0, 4), (4, 8), (8, 10))
NORM_EPS = 1e-06
F32 = jnp.float32
BF16 = jnp.bfloat16
VMEM_LIMIT = 48 * 1024 * 1024


def dot_nn(a, b):
    return lax.dot_general(a, b, (((1,), (0,)), ((), ())), preferred_element_type=F32)


def dot_nt(a, b):
    return lax.dot_general(a, b, (((1,), (1,)), ((), ())), preferred_element_type=F32)


def dot_tn(a, b):
    return lax.dot_general(a, b, (((0,), (0,)), ((), ())), preferred_element_type=F32)


def live_column(c0, c1, c2):
    row = lax.broadcasted_iota(jnp.int32, (TOK, 1), 0)
    return (
        (row < c0)
        | ((row >= CAP) & (row < CAP + c1))
        | ((row >= 2 * CAP) & (row < 2 * CAP + c2))
    )


def params():
    return pltpu.CompilerParams(vmem_limit_bytes=VMEM_LIMIT)


def cost(flops, nbytes):
    return pl.CostEstimate(flops=int(flops), bytes_accessed=int(nbytes), transcendentals=0)


def stem_kernel(
    cnt_ref, idx_ref, patch_ref, w_ref, gain_ref, table_ref, genc_ref, og_ref,
    emb_ref, normed_ref, gl_ref, cols_ref, parts,
):
    step = pl.program_id(0)
    scenes = patch_ref.shape[0]

    @pl.when(step == 0)
    def _():
        whole = table_ref[...]
        high = whole.astype(BF16)
        rest = whole - high.astype(F32)
        mid = rest.astype(BF16)
        low = (rest - mid.astype(F32)).astype(BF16)
        parts[0] = high
        parts[1] = mid
        parts[2] = low

    patch_iota = lax.broadcasted_iota(jnp.int32, (TOK, table_ref.shape[0]), 1)
    picked, placed = [], []
    for s in range(scenes):
        onehot = (idx_ref[s] == patch_iota).astype(F32).astype(BF16)
        picked.append(dot_nn(onehot, patch_ref[s]).astype(BF16))
        placed.append(
            (dot_nn(onehot, parts[0]) + dot_nn(onehot, parts[1])) + dot_nn(onehot, parts[2])
        )
        live = live_column(
            cnt_ref[step * scenes + s, 0], cnt_ref[step * scenes + s, 1], cnt_ref[step * scenes + s, 2]
        )
        gl_ref[s] = jnp.where(live, og_ref[s].astype(F32), 0.0).astype(BF16)
    for g, (start, end) in enumerate(GROUP_BANDS):
        rows = slice(g * CAP, (g + 1) * CAP)
        columns = jnp.concatenate([p[rows, start * PIX : end * PIX] for p in picked], axis=0)
        summed = dot_nn(columns, w_ref[start * PIX : end * PIX, :])
        width = (end - start) * PIX
        for s in range(scenes):
            values = summed[s * CAP : (s + 1) * CAP] + (placed[s][rows] + genc_ref[g : g + 1, :])
            emb = values.astype(BF16)
            emb_ref[s, rows, :] = emb
            x = emb.astype(F32)
            centre = jnp.mean(x, axis=-1, keepdims=True)
            dev = x - centre
            spread = jnp.mean(dev * dev, axis=-1, keepdims=True)
            centred = dev * lax.rsqrt(spread + NORM_EPS)
            normed_ref[s, rows, :] = (centred * gain_ref[...]).astype(BF16)
            cols_ref[s, rows, :width] = columns[s * CAP : (s + 1) * CAP]
            if width < cols_ref.shape[2]:
                cols_ref[s, rows, width:] = jnp.zeros((CAP, cols_ref.shape[2] - width), BF16)


def stem_call(counts, index_col, patches, w_stem, gain, table, genc, out_grad):
    scenes, patch_count, width = patches.shape
    block = 3 if scenes % 3 == 0 else 1
    col_width = max(e - s for s, e in GROUP_BANDS) * PIX
    per = lambda shape: pl.BlockSpec((block,) + shape, lambda i: (i, 0, 0))
    whole = lambda a: pl.BlockSpec(a.shape, lambda i: (0,) * a.ndim)
    rows = jax.ShapeDtypeStruct((scenes, TOK, D), BF16)
    return pl.pallas_call(
        stem_kernel,
        grid=(scenes // block,),
        in_specs=[
            pl.BlockSpec(memory_space=pltpu.SMEM),
            per((TOK, 1)),
            per((patch_count, width)),
            whole(w_stem),
            whole(gain),
            whole(table),
            whole(genc),
            per((TOK, D)),
        ],
        out_specs=[per((TOK, D)), per((TOK, D)), per((TOK, D)), per((TOK, col_width))],
        out_shape=[rows, rows, rows, jax.ShapeDtypeStruct((scenes, TOK, col_width), BF16)],
        scratch_shapes=[pltpu.VMEM((3,) + table.shape, BF16)],
        compiler_params=params(),
        cost_estimate=cost(8e9, 12e6),
        name="stem_norm",
    )(counts, index_col, patches, w_stem, gain, table, genc, out_grad)


def attention_kernel(
    deps, cnt_ref, na_ref, nb_ref, ga_ref, gb_ref, wq_ref, wk_ref, wv_ref, wo_ref, *refs
):
    out_ref, n_s, g_s, qkv = refs[deps:]
    half, step = pl.program_id(0), pl.program_id(1)
    rows = n_s.shape[0]
    scenes = rows // TOK
    width = wq_ref.shape[1]

    @pl.when(half == 0)
    def _():
        n_s[...] = na_ref[...]
        g_s[...] = ga_ref[...]

    @pl.when(half != 0)
    def _():
        n_s[...] = nb_ref[...]
        g_s[...] = gb_ref[...]

    into = jnp.concatenate([wq_ref[...], wk_ref[...], wv_ref[...]], axis=1)
    qkv[:, : 3 * width] = dot_nn(n_s[...], into).astype(BF16)
    qkv[:, 3 * width :] = dot_nn(g_s[...], wo_ref[...]).astype(BF16)
    lane = lax.broadcasted_iota(jnp.int32, (1, PAIR), 1)
    masks = [(lane // HD == h).astype(F32).astype(BF16) for h in range(PAIR // HD)]

    def scene_body(s, _):
        base = pl.multiple_of(s * TOK, 16)
        at = pl.ds(base, TOK)
        scene = step * scenes + s
        live = live_column(cnt_ref[half, scene, 0], cnt_ref[half, scene, 1], cnt_ref[half, scene, 2])
        bias = jnp.where(live, 0.0, -1e30)
        for pair in range(width // PAIR):
            cols = [slice(part * width + pair * PAIR, part * width + (pair + 1) * PAIR) for part in range(4)]
            q, k, v, dc = [qkv[at, c] for c in cols]
            gq = gk = gv = ctx = None
            for mask in masks:
                qm = q * (mask * jnp.asarray(HD ** (-0.5), BF16))
                km, vm, dcm = k * mask, v * mask, dc * mask
                scores = dot_nt(k, qm) + bias
                lifted = jnp.exp(scores - jnp.max(scores, axis=0, keepdims=True))
                probs = lifted * (1.0 / jnp.sum(lifted, axis=0, keepdims=True))
                half_probs = probs.astype(BF16)
                grad_probs = dot_nt(v, dcm)
                inner = jnp.sum(probs * grad_probs, axis=0, keepdims=True)
                grad_score = (probs * (grad_probs - inner)).astype(BF16)
                new = (
                    dot_tn(grad_score, km),
                    dot_nn(grad_score, qm),
                    dot_nn(half_probs, dcm),
                    dot_tn(half_probs, vm),
                )
                if gq is None:
                    gq, gk, gv, ctx = new
                else:
                    gq, gk, gv, ctx = gq + new[0], gk + new[1], gv + new[2], ctx + new[3]
            out_ref[at, cols[0]] = (gq * HD ** (-0.5)).astype(BF16)
            out_ref[at, cols[1]] = gk.astype(BF16)
            out_ref[at, cols[2]] = gv.astype(BF16)
            out_ref[at, cols[3]] = ctx.astype(BF16)
        return 0

    lax.fori_loop(0, scenes, scene_body, 0)


def block_rows(tokens):
    return 3 * TOK if tokens % (3 * TOK) == 0 else TOK


def two_halves(rows, steps):
    first = pl.BlockSpec((rows, D), lambda h, i: (jnp.where(h == 0, i, steps - 1), 0))
    second = pl.BlockSpec((rows, D), lambda h, i: (jnp.where(h == 0, 0, i), 0))
    return [first, second, first, second]


ANYWHERE = pl.BlockSpec(memory_space=pl.ANY)
SCALARS = pl.BlockSpec(memory_space=pltpu.SMEM)


def attention_call(counts, na, nb, ga, gb, packed, part, parts, deps=()):
    tokens = na.shape[0]
    rows = block_rows(tokens)
    steps = tokens // rows
    first, second = packed
    width = first.shape[1] // 2 // parts
    weight = lambda c: pl.BlockSpec((D, width), lambda h, i: (0, (c % 2) * parts + part))
    return pl.pallas_call(
        functools.partial(attention_kernel, len(deps)),
        grid=(2, steps),
        in_specs=[SCALARS] + two_halves(rows, steps) + [weight(c) for c in range(4)] + [ANYWHERE] * len(deps),
        out_specs=pl.BlockSpec((rows, 4 * width), lambda h, i: (h * steps + i, 0)),
        out_shape=jax.ShapeDtypeStruct((2 * tokens, 4 * width), BF16),
        scratch_shapes=[
            pltpu.VMEM((rows, D), BF16),
            pltpu.VMEM((rows, D), BF16),
            pltpu.VMEM((rows, 4 * width), BF16),
        ],
        compiler_params=params(),
        cost_estimate=cost(24e9 / parts, 14e6),
        name="attention",
    )(counts, na, nb, ga, gb, first, first, second, second, *deps)


def weight_grad_kernel(
    deps, blocks, low_ref, na_ref, nb_ref, ga_ref, gb_ref, pack_ref, *refs
):
    send_ref, keep_ref, total = refs[deps:]
    half, step = pl.program_id(0), pl.program_id(1)
    width = pack_ref.shape[1] // 4

    @pl.when((half == 0) & (step == 0))
    def _():
        total[...] = jnp.zeros_like(total)

    def add(n_ref, g_ref):
        total[:, : 3 * width] += dot_tn(n_ref[...], pack_ref[:, : 3 * width])
        total[:, 3 * width :] += dot_tn(g_ref[...], pack_ref[:, 3 * width :])

    pl.when(half == 0)(lambda: add(na_ref, ga_ref))
    pl.when(half != 0)(lambda: add(nb_ref, gb_ref))

    @pl.when((half == pl.num_programs(0) - 1) & (step == pl.num_programs(1) - 1))
    def _():
        rows = total.shape[0] // blocks
        low = low_ref[0]
        for b in range(blocks // 2):
            at = slice(b * rows, (b + 1) * rows)
            mine = pl.multiple_of((2 * b + low) * rows, rows)
            other = pl.multiple_of((2 * b + 1 - low) * rows, rows)
            keep_ref[at, :] = total[pl.ds(mine, rows), :]
            send_ref[at, :] = total[pl.ds(other, rows), :].astype(BF16)


def weight_grad_call(low, na, nb, ga, gb, pack, blocks, deps=()):
    tokens = na.shape[0]
    rows = block_rows(tokens)
    steps = tokens // rows
    cols = pack.shape[1]
    whole = pl.BlockSpec((D // 2, cols), lambda h, i: (0, 0))
    return pl.pallas_call(
        functools.partial(weight_grad_kernel, len(deps), blocks),
        grid=(2, steps),
        in_specs=[SCALARS]
        + two_halves(rows, steps)
        + [pl.BlockSpec((rows, cols), lambda h, i: (h * steps + i, 0))]
        + [ANYWHERE] * len(deps),
        out_specs=[whole, whole],
        out_shape=[jax.ShapeDtypeStruct((D // 2, cols), BF16), jax.ShapeDtypeStruct((D // 2, cols), F32)],
        scratch_shapes=[pltpu.VMEM((D, cols), F32)],
        compiler_params=params(),
        cost_estimate=cost(10e9 * cols / D, 12e6),
        name="weight_grad",
    )(low, na, nb, ga, gb, pack, *deps)


def combine_kernel(deps, place_ref, keep_ref, recv_ref, *refs):
    refs = refs[deps:]
    rows = refs[0].shape[0]
    place = place_ref[0]
    for j, ref in enumerate(refs):
        at = pl.ds(pl.multiple_of((place ^ j) * rows, rows), rows)
        ref[...] = (keep_ref[at, :] + recv_ref[at, :].astype(F32)).astype(ref.dtype)


def combine_call(place, keep, recv, blocks, dtype, deps=()):
    rows, cols = keep.shape[0] // blocks, keep.shape[1]
    whole = lambda a: pl.BlockSpec(a.shape, lambda: (0, 0))
    shapes = [jax.ShapeDtypeStruct((rows, cols), F32 if j == 0 else dtype) for j in range(blocks)]
    return pl.pallas_call(
        functools.partial(combine_kernel, len(deps)),
        in_specs=[SCALARS, whole(keep), whole(recv)] + [ANYWHERE] * len(deps),
        out_specs=[pl.BlockSpec((rows, cols), lambda: (0, 0))] * blocks,
        out_shape=shapes,
        compiler_params=params(),
        cost_estimate=cost(1e6, 5e6),
        name="combine",
    )(place, keep, recv, *deps)


def add_kernel(count, *refs):
    total = refs[0][...]
    for ref in refs[1:count]:
        total = total + ref[...].astype(F32)
    refs[-1][...] = total


def add_call(parts, deps=()):
    spec = pl.BlockSpec(parts[0].shape, lambda: (0, 0))
    return pl.pallas_call(
        functools.partial(add_kernel, len(parts)),
        in_specs=[spec] * len(parts) + [ANYWHERE] * len(deps),
        out_specs=spec,
        out_shape=jax.ShapeDtypeStruct(parts[0].shape, F32),
        compiler_params=params(),
        cost_estimate=cost(1e6, 2e6),
        name="add_parts",
    )(*parts, *deps)


def weight_columns(w_refs, first, count, part, parts):
    width = w_refs[0].shape[1] // 2
    size = width // parts
    pieces = []
    for c in range(first, first + count):
        start = (c % 2) * width + part * size
        pieces.append(w_refs[c // 2][:, start : start + size])
    return pieces[0] if count == 1 else jnp.concatenate(pieces, axis=1)


def back_product(layout, pack_refs, weight_refs, first, count):
    total = None
    for pack_ref, (block, part, parts) in zip(pack_refs, layout):
        columns = weight_columns(weight_refs[2 * block : 2 * block + 2], first, count, part, parts)
        new = dot_nt(pack_ref[...], columns)
        total = new if total is None else total + new
    return total


def back_kernel(layout, deps, first, count, *refs):
    packs, refs = refs[: len(layout)], refs[len(layout) :]
    out_ref = refs[-1]
    out_ref[...] = back_product(layout, packs, refs, first, count).astype(out_ref.dtype)


def back_call(layout, packs, weights, half, context, out_dtype, deps=()):
    tokens = packs[0].shape[0] // 2
    rows = block_rows(tokens)
    steps = tokens // rows

    def pack_spec(pack):
        width = pack.shape[1] // 4
        if context:
            return pl.BlockSpec((rows, width), lambda i: (half * steps + i, 3))
        return pl.BlockSpec((rows, 3 * width), lambda i: (half * steps + i, 0))

    return pl.pallas_call(
        functools.partial(back_kernel, layout, len(deps), 3 if context else 0, 1 if context else 3),
        grid=(steps,),
        in_specs=[pack_spec(p) for p in packs]
        + [pl.BlockSpec(w.shape, lambda i: (0, 0)) for w in weights]
        + [ANYWHERE] * len(deps),
        out_specs=pl.BlockSpec((rows, D), lambda i: (i, 0)),
        out_shape=jax.ShapeDtypeStruct((tokens, D), out_dtype),
        compiler_params=params(),
        cost_estimate=cost(3.5e9 if context else 6e9, 8e6),
        name="back_context" if context else "back_qkv",
    )(*packs, *weights, *deps)


def tail_kernel(layout, blocks, deps, core_ref, recv_ref, emb_ref, gl_ref, cols_ref, gain_ref, *refs):
    packs, refs = refs[: len(layout)], refs[len(layout) :]
    weights = refs[:blocks]
    send_ref, keep_ref, acc = refs[blocks + deps :]
    step = pl.program_id(0)
    rows = emb_ref.shape[0]
    scenes = rows // TOK

    @pl.when(step == 0)
    def _():
        acc[...] = jnp.zeros_like(acc)

    grad_normed = recv_ref[...] + back_product(layout, packs, weights, 0, 3)
    x = emb_ref[...].astype(F32)
    dev = x - jnp.mean(x, axis=-1, keepdims=True)
    inv_std = lax.rsqrt(jnp.mean(dev * dev, axis=-1, keepdims=True) + NORM_EPS)
    centred = dev * inv_std
    scaled = grad_normed * gain_ref[...]
    first_mean = jnp.mean(scaled, axis=-1, keepdims=True)
    second_mean = jnp.mean(scaled * centred, axis=-1, keepdims=True)
    back = inv_std * (scaled - first_mean - centred * second_mean)
    grad_in = (gl_ref[...].astype(F32) + back).astype(BF16)
    for g, (start, end) in enumerate(GROUP_BANDS):
        at = [slice(s * TOK + g * CAP, s * TOK + (g + 1) * CAP) for s in range(scenes)]
        columns = jnp.concatenate([cols_ref[a, : (end - start) * PIX] for a in at], axis=0)
        grads = jnp.concatenate([grad_in[a] for a in at], axis=0)
        acc[start * PIX : end * PIX, :] += dot_tn(columns, grads)

    @pl.when(step == pl.num_programs(0) - 1)
    def _():
        size = keep_ref.shape[0]
        core = core_ref[0]
        keep_ref[...] = acc[pl.ds(pl.multiple_of(core * size, size), size), :]
        send_ref[...] = acc[pl.ds(pl.multiple_of((1 - core) * size, size), size), :]


def tail_call(layout, core, recv, emb, gl, cols, gain, packs, weights, deps=()):
    tokens = emb.shape[0]
    rows = block_rows(tokens)
    per = lambda a: pl.BlockSpec((rows, a.shape[1]), lambda i: (i, 0))
    stem_rows = GROUP_BANDS[-1][1] * PIX
    half = jax.ShapeDtypeStruct((stem_rows // 2, D), F32)
    return pl.pallas_call(
        functools.partial(tail_kernel, layout, len(weights), len(deps)),
        grid=(tokens // rows,),
        in_specs=[SCALARS, per(recv), per(emb), per(gl), per(cols)]
        + [pl.BlockSpec(gain.shape, lambda i: (0, 0))]
        + [pl.BlockSpec((rows, 3 * (p.shape[1] // 4)), lambda i: (i, 0)) for p in packs]
        + [pl.BlockSpec(w.shape, lambda i: (0, 0)) for w in weights]
        + [ANYWHERE] * len(deps),
        out_specs=[pl.BlockSpec(half.shape, lambda i: (0, 0))] * 2,
        out_shape=[half, half],
        scratch_shapes=[pltpu.VMEM((stem_rows, D), F32)],
        compiler_params=params(),
        cost_estimate=cost(10e9, 12e6),
        name="tail",
    )(core, recv, emb, gl, cols, gain, *packs, *weights, *deps)


def output_kernel(layout, blocks, cnt_ref, recv_ref, emb_ref, *refs):
    packs, weights, out_ref = refs[: len(layout)], refs[len(layout) : len(layout) + blocks], refs[-1]
    step = pl.program_id(0)
    scenes = emb_ref.shape[0] // TOK
    mixed = recv_ref[...].astype(F32) + back_product(layout, packs, weights, 3, 1)
    total = emb_ref[...].astype(F32) + mixed
    for s in range(scenes):
        scene = step * scenes + s
        live = live_column(cnt_ref[scene, 0], cnt_ref[scene, 1], cnt_ref[scene, 2])
        at = slice(s * TOK, (s + 1) * TOK)
        out_ref[at, :] = jnp.where(live, total[at], 0.0).astype(BF16)


def output_call(layout, counts, recv, emb, packs, weights, deps=()):
    tokens = emb.shape[0]
    rows = block_rows(tokens)
    per = lambda a: pl.BlockSpec((rows, a.shape[1]), lambda i: (i, 0))
    return pl.pallas_call(
        functools.partial(output_kernel, layout, len(weights)),
        grid=(tokens // rows,),
        in_specs=[SCALARS, per(recv), per(emb)]
        + [pl.BlockSpec((rows, p.shape[1] // 4), lambda i: (i, 3)) for p in packs]
        + [pl.BlockSpec(w.shape, lambda i: (0, 0)) for w in weights]
        + [ANYWHERE] * len(deps),
        out_specs=per(emb),
        out_shape=jax.ShapeDtypeStruct(emb.shape, BF16),
        compiler_params=params(),
        cost_estimate=cost(5e9, 10e6),
        name="layer_output",
    )(counts, recv, emb, *packs, *weights, *deps)


def swap(x, axis, size, bit):
    return lax.ppermute(x, axis, [(i, i ^ bit) for i in range(size)])


def ring_gather(pieces, axis, size):
    order = list(range(0, size, 2)) + list(range(size - 1, 0, -2))
    forward = [(order[i], order[(i + 1) % size]) for i in range(size)]
    backward = [(order[(i + 1) % size], order[i]) for i in range(size)]
    me = lax.axis_index(axis)
    here = jnp.where(me % 2 == 0, me // 2, size - 1 - me // 2)
    rows = pieces[0].shape[0]

    def put(full, block, distance):
        at = (here + distance + size) % size
        owner = jnp.where(at < size // 2, 2 * at, 2 * (size - 1 - at) + 1)
        return lax.dynamic_update_slice_in_dim(full, block, owner * rows, 0)

    fulls = [put(jnp.zeros((size * rows,) + x.shape[1:], x.dtype), x, 0) for x in pieces]
    ahead, behind = list(pieces), list(pieces)
    for s in range(1, size // 2 + 1):
        for i in range(len(pieces)):
            ahead[i] = lax.ppermute(ahead[i], axis, forward)
            fulls[i] = put(fulls[i], ahead[i], -s)
            if s <= (size - 1) // 2:
                behind[i] = lax.ppermute(behind[i], axis, backward)
                fulls[i] = put(fulls[i], behind[i], s)
    return fulls


def halve_stem(send, keep, group, after):
    recv = swap(send, "group", group, 1)
    mine = lax.axis_index("group") // 2 * 2 + lax.axis_index("dp") % 2
    return combine_call(mine.reshape(1), keep, recv, group // 2 * 2, F32, (after,))


def sum_stem(parts, dp, group):
    core = lax.axis_index("group") % 2
    far = lax.axis_index("group") // 2
    low = lax.axis_index("dp") % 2
    high = lax.axis_index("dp") // 2
    fars, highs = group // 2, dp // 2
    mine = far * 2 + low
    small, width = parts[0].shape
    rows = 2 * fars * small

    def hop(block, f, b):
        if f:
            pairs = [
                (d * group + g, (d ^ b) * group + (g ^ (2 * f))) for d in range(dp) for g in range(group)
            ]
            return lax.ppermute(block, ("dp", "group"), pairs)
        return swap(block, "dp", dp, b)

    hops = [(k // 2, k % 2) for k in range(1, 2 * fars)]
    total = add_call([parts[0]] + [hop(part, f, b) for part, (f, b) in zip(parts[1:], hops)])
    cols = width // highs
    part = lax.dynamic_slice_in_dim(total, high * cols, cols, 1)
    for j in range(1, highs):
        away = lax.dynamic_slice_in_dim(total, (high ^ j) * cols, cols, 1)
        part = part + swap(away, "dp", dp, 2 * j)
    part = part.astype(BF16)
    line = jnp.zeros((small, width), BF16)
    line = lax.dynamic_update_slice_in_dim(line, part, high * cols, 1)
    for j in range(1, highs):
        line = lax.dynamic_update_slice_in_dim(
            line, swap(part, "dp", dp, 2 * j), (high ^ j) * cols, 1
        )
    block = jnp.zeros((rows, width), BF16)
    block = lax.dynamic_update_slice_in_dim(block, line, mine * small, 0)
    for f, b in hops:
        target = (far ^ f) * 2 + (low ^ b)
        block = lax.dynamic_update_slice_in_dim(block, hop(line, f, b), target * small, 0)
    partner = swap(block, "group", group, 1)
    first = jnp.where(core == 0, block, partner)
    second = jnp.where(core == 0, partner, block)
    return jnp.concatenate([first, second], axis=0).astype(F32), total


def spatial_table(patch_count):
    quarter = D // 4
    half_width = D // 2
    row_freq = jnp.power(10000.0, -jnp.arange(quarter, dtype=F32) / quarter)
    group_freq = jnp.power(10000.0, -jnp.arange(half_width, dtype=F32) / half_width)
    at = jnp.arange(GRID).astype(F32)[:, None] * row_freq
    both = jnp.concatenate([jnp.sin(at), jnp.cos(at)], axis=-1)
    rows = patch_count // GRID
    by_row = jnp.broadcast_to(both[:rows, None], (rows, GRID, 2 * quarter))
    by_col = jnp.broadcast_to(both[None], (rows, GRID, 2 * quarter))
    table = jnp.concatenate([by_row, by_col], axis=-1).reshape(patch_count, D)
    group_at = jnp.arange(GROUPS).astype(F32)[:, None] * group_freq
    return table, jnp.concatenate([jnp.sin(group_at), jnp.cos(group_at)], axis=-1)


def on_device(dp, group, patches, vis_index, vis_count, w_stem, ln_gain, w_qkv, w_out, out_grad):
    scenes = patches.shape[0]
    tokens = scenes * TOK
    width = w_qkv.shape[2]
    fars = group // 2
    low = (lax.axis_index("dp") % 2).astype(jnp.int32).reshape(1)
    high = (lax.axis_index("dp") // 2).astype(jnp.int32).reshape(1)
    core = (lax.axis_index("group") % 2).astype(jnp.int32).reshape(1)

    pieces = [
        w_qkv[:, :2].reshape(w_qkv.shape[0], 2 * width),
        jnp.concatenate([w_qkv[:, 2], w_out.T], axis=1),
    ]
    own = ring_gather(pieces, "dp", dp)
    weights = [own] + [[swap(w, "group", group, 2 * f) for w in own] for f in range(1, fars)]
    flat = [w for pair in weights for w in pair]

    counts = vis_count.astype(jnp.int32)
    both_counts = jnp.stack([counts, swap(counts, "group", group, 1)])
    table, genc = spatial_table(patches.shape[1])
    gain = ln_gain.reshape(1, D)
    emb, normed, gl, cols = stem_call(
        counts,
        vis_index.reshape(scenes, TOK, 1),
        patches,
        w_stem,
        gain,
        table,
        genc,
        out_grad.reshape(scenes, TOK, D),
    )
    emb, normed, gl = [a.reshape(tokens, D) for a in (emb, normed, gl)]
    cols = cols.reshape(tokens, cols.shape[2])
    both = (normed, swap(normed, "group", group, 1), gl, swap(gl, "group", group, 1))

    layout = [(0, 0, 1)] + [(f, part, 2) for f in range(1, fars) for part in range(2)]
    packs, kept, coming, landing = [], [], [], []

    def first_leg(deps=()):
        send, keep = weight_grad_call(low, *both, packs[-1], dp, deps)
        kept.append(keep)
        coming.append(swap(send, "dp", dp, 1))
        return send

    def second_leg(n, deps):
        blocks = combine_call(high, kept[n], coming[n], dp // 2, BF16, deps)
        landing.append([blocks[0]] + [swap(blocks[j], "dp", dp, 2 * j) for j in range(1, dp // 2)])
        return blocks[-1]

    deps = ()
    for n, (f, part, parts) in enumerate(layout):
        packs.append(attention_call(both_counts, *both, weights[f], part, parts, deps))
        if n + 1 < len(layout):
            send = first_leg()
            deps = (send,) if n == 0 else (second_leg(n - 1, (send,)),)

    near = dp // 2 * 3 // 4
    back = back_call(layout, packs, flat, 1, False, F32, (coming[-1], *landing[-1][1:near]))
    back_far = swap(back, "group", group, 1)
    last = second_leg(len(layout) - 2, (back,))
    send = first_leg((last,))
    mixed = back_call(layout, packs, flat, 1, True, BF16, (send, *landing[-2][near:], *landing[-1][1:near]))
    mixed_far = swap(mixed, "group", group, 1)
    stem_send, stem_keep = tail_call(
        layout, core, back_far, emb, gl, cols, gain, packs, flat, (mixed, *landing[-1][near:])
    )
    output = output_call(layout, counts, mixed_far, emb, packs, flat, (stem_send, coming[-1]))
    stem_parts = halve_stem(stem_send, stem_keep, group, output)
    second_leg(len(layout) - 1, (stem_parts[-1],))
    grad_w_stem, stem_total = sum_stem(stem_parts, dp, group)
    shares = [add_call(parts) for parts in landing[:-1]] + [add_call(landing[-1], (stem_total,))]

    total = shares[0]
    for f in range(1, fars):
        parts = [swap(s, "group", group, 2 * f) for s, where in zip(shares, layout) if where[0] == f]
        size = width // len(parts)
        pieces = [p[:, c * size : (c + 1) * size] for c in range(4) for p in parts]
        total = total + jnp.concatenate(pieces, axis=1)
    grad_w_qkv = total[:, : 3 * width].reshape(total.shape[0], 3, width)
    grad_w_out = total[:, 3 * width :].T
    return (output.reshape(scenes, GROUPS, CAP, D), grad_w_stem, grad_w_qkv, grad_w_out)


def solution(mesh):
    sizes = dict(mesh.shape)
    return jax.shard_map(
        functools.partial(on_device, sizes["dp"], sizes["group"]),
        mesh=mesh,
        in_specs=(
            P(("dp", "group"), None, None),
            P(("dp", "group"), None, None),
            P(("dp", "group"), None),
            P(),
            P(),
            P("dp", None, "group"),
            P("group", "dp"),
            P(("dp", "group"), None, None, None),
        ),
        out_specs=(
            P(("dp", "group"), None, None, None),
            P(),
            P("dp", None, "group"),
            P("group", "dp"),
        ),
        check_vma=False,
    )
```

time: 303 us -> 269 us (0.89)
  local copies, waits for them, and re-layouts: 57.7 us -> 29.3 us
  Pallas kernels: 95.4 us -> 110 us
  between operations: 11.6 us -> 1.67 us
  waiting for transfers between devices: 67.1 us -> 59.9 us
    dynamic_slice x13 -> x0, local copies, waits for them, and re-layouts: 20.2 us -> none  [the longest x8 13.8 us: reduce_rows(): keep = lax.dynamic_index_in_dim(part, low, 1, keepdims=False)]
    ppermute x14, waiting for transfers between devices: 21.5 us -> 5.34 us  [the longest x8 4.54 us: ring_gather(): ahead[i] = lax.ppermute(ahead[i], axis, forward)]
    pallas_call x8 -> x18, Pallas kernels: 89 us -> 104 us  [the longest x3 51.3 us: attention_call(): pl.pallas_call(functools.partial(attention_kernel, len(deps)), grid=(2, s...]
    slice x2 -> x0, local copies, waits for them, and re-layouts: 5.32 us -> none  [reduce_rows(): part = x[:, c * cols:(c + 1) * cols].reshape(count, 2, rows, cols)]
    add x9 -> x1, other arithmetic: 5.25 us -> 0.06 us  [on_device(): total = total + jnp.concatenate(pieces, axis=1)]
    ppermute x4, waiting for transfers between devices: 5.5 us -> 10.5 us  [hop(): return lax.ppermute(block, ('dp', 'group'), pairs)]
    ppermute x33 -> x31, waiting for transfers between devices: 40.1 us -> 44.1 us  [swap(): return lax.ppermute(x, axis, [(i, i ^ bit) for i in range(size)])]
    ppermute x33 -> x31, starting transfers between devices: 36.6 us -> 33.2 us  [swap(): return lax.ppermute(x, axis, [(i, i ^ bit) for i in range(size)])]
  transfers between devices with their start and end apart: 51 -> 49, of which waited for: 25 -> 18; matrix products, arithmetic and copies ran while one was open for 15% -> 3% of each run, Pallas kernels for 15% -> 38%
where the time goes in v2:
time: 269 us; the launch traced here: 268 us
  Pallas kernels  110 us (41%)
  starting transfers between devices  61 us (23%)
  waiting for transfers between devices  59.9 us (22%)
  local copies, waits for them, and re-layouts  29.3 us (11%)
  other arithmetic  6 us (2%)
    pallas_call x3, Pallas kernels, attention_call(): pl.pallas_call(functools.partial(attention_kernel, len(deps)), grid=(2, s...  51.3 us
    ppermute x31, waiting for transfers between devices, swap(): return lax.ppermute(x, axis, [(i, i ^ bit) for i in range(size)])  44.1 us
    ppermute x31, starting transfers between devices, swap(): return lax.ppermute(x, axis, [(i, i ^ bit) for i in range(size)])  33.2 us
    pallas_call x3, Pallas kernels, weight_grad_call(): pl.pallas_call(functools.partial(weight_grad_kernel, len(deps), blocks),...  24.5 us
    unnamed x106, local copies, waits for them, and re-layouts  24.4 us
    ppermute x8, starting transfers between devices, ring_gather(): ahead[i] = lax.ppermute(ahead[i], axis, forward)  14.9 us
    ppermute x4, waiting for transfers between devices, hop(): return lax.ppermute(block, ('dp', 'group'), pairs)  10.5 us
    pallas_call x1, Pallas kernels, tail_call(): pl.pallas_call(functools.partial(tail_kernel, layout, len(weights), len(d...  10.5 us
  transfers between devices with their start and end apart: 49, of which 18 were waited for; matrix products, arithmetic and copies ran while one was open for 3% of the time, Pallas kernels for 38%

profile of v2, /device:TPU:0, one launch (start us, length us, event | category | flops | bytes accessed | tf_op | source)
XLA Modules:
  0.0 267.9 jit_solution(3644104275668818070)
XLA Ops:
  3.2 3.0 %collective-permute-start.10 = (bf16[128,512]{1,0:T(8,128)(2,1)}, bf16[128,512]{1,0:T(8,128)(2,1)}, u32[]{:S(2)}, u32[]{:S(2)}) collective-permute-start(bf16[128,512]{1,0:T(8,128)(2,1)} %get-tuple-element.83), channel_id=1, source_target_pairs={{0,8},{8,16},{16,24},{24,28},{28,20},{20,12},{12,4},{4,0},{1,9},{9... | collective-permute-start | bytes 393224 | tf_op jit(solution)/shard_map/ppermute | solution.py:493
  11.7 6.4 %stem_norm.1 = (bf16[6,144,1024]{2,1,0:T(8,128)(2,1)S(1)}, bf16[6,144,1024]{2,1,0:T(8,128)(2,1)}, bf16[6,144,1024]{2,1,0:T(8,128)(2,1)}, bf16[6,144,256]{2,1,0:T(8,128)(2,1)S(1)}) custom-call(s32[6,3]{1,0:T(8,128)S(1)} %copy.49.cnt_ref, s32[6,144,1]{2,1,0:T(8,128)S(1)} %reshape.90.idx_ref, bf16[6,144,640]{2,1,0:T(8,128)(2,1)S(1)} %copy-done.39, ...), custom_call_target="tpu_custom_call" | custom-call | flops 8000000000 | bytes 12000000 | tf_op jit(solution)/shard_map/stem_norm/pallas_call | solution.py:111
  20.6 2.0 collective-permute-start.3
  23.7 2.1 collective-permute-start.12
  38.2 2.3 collective-permute-start.8
  43.6 2.1 collective-permute-done.16
  48.7 22.2 %attention.3.pack_ref.refs_0_ = bf16[1728,1024]{1,0:T(8,128)(2,1)} custom-call(s32[2,6,3]{2,1,0:T(8,128)S(1)} %pad_add_fusion.cnt_ref, bf16[864,1024]{1,0:T(8,128)(2,1)S(1)} %bitcast.25, bf16[864,1024]{1,0:T(8,128)(2,1)} %collective-permute-done.1.nb_ref, bf16[864,1024]{1,0:T(8,128)(2,1)} %bitcast.44, bf16[864,1024]{1,0:T(8,128)(2,1)} %collective-permute-done.2.gb_ref, ...), custom_call_target="tpu_custom_call" | custom-call | flops 24000000000 | bytes 14000000 | tf_op jit(solution)/shard_map/attention/pallas_call | solution.py:218
  70.9 9.9 %weight_grad.3 = (bf16[512,1024]{1,0:T(8,128)(2,1)}, f32[512,1024]{1,0:T(8,128)}) custom-call(s32[1]{0:T(128)} %bitcast.8.low_ref, bf16[864,1024]{1,0:T(8,128)(2,1)S(1)} %bitcast.26, bf16[864,1024]{1,0:T(8,128)(2,1)} %collective-permute-done.1.nb_ref, bf16[864,1024]{1,0:T(8,128)(2,1)} %bitcast.45, bf16[864,1024]{1,0:T(8,128)(2,1)} %collective-permute-done.2.gb_ref, ...), custom_call_target="tpu_custom_call" | custom-call | flops 10000000000 | bytes 12000000 | tf_op jit(solution)/shard_map/weight_grad/pallas_call | solution.py:271
  82.5 8.1 %collective-permute-done.17.wq_ref.wk_ref.refs_5_ = bf16[1024,512]{1,0:T(8,128)(2,1)S(1)} collective-permute-done((bf16[1024,512]{1,0:T(8,128)(2,1)S(1)}, bf16[1024,512]{1,0:T(8,128)(2,1)S(1)}, u32[]{:S(2)}, u32[]{:S(2)}) %collective-permute-start.17) | collective-permute-done | bytes 1048608 | tf_op jit(solution)/shard_map/ppermute | solution.py:473
  90.6 14.9 %attention.4.pack_ref.refs_1_ = bf16[1728,512]{1,0:T(8,128)(2,1)S(1)} custom-call(s32[2,6,3]{2,1,0:T(8,128)S(1)} %pad_add_fusion.cnt_ref, bf16[864,1024]{1,0:T(8,128)(2,1)} %bitcast.24, bf16[864,1024]{1,0:T(8,128)(2,1)} %collective-permute-done.1.nb_ref, bf16[864,1024]{1,0:T(8,128)(2,1)} %bitcast.46, bf16[864,1024]{1,0:T(8,128)(2,1)} %collective-permute-done.2.gb_ref, ...), custom_call_target="tpu_custom_call" | custom-call | flops 12000000000 | bytes 14000000 | tf_op jit(solution)/shard_map/attention/pallas_call | solution.py:218
  106.7 7.0 %weight_grad.4 = (bf16[512,512]{1,0:T(8,128)(2,1)S(1)}, f32[512,512]{1,0:T(8,128)S(1)}) custom-call(s32[1]{0:T(128)} %bitcast.8.low_ref, bf16[864,1024]{1,0:T(8,128)(2,1)S(1)} %bitcast.27, bf16[864,1024]{1,0:T(8,128)(2,1)} %collective-permute-done.1.nb_ref, bf16[864,1024]{1,0:T(8,128)(2,1)} %bitcast.47, bf16[864,1024]{1,0:T(8,128)(2,1)} %collective-permute-done.2.gb_ref, ...), custom_call_target="tpu_custom_call" | custom-call | flops 5000000000 | bytes 12000000 | tf_op jit(solution)/shard_map/weight_grad/pallas_call | solution.py:271
  118.3 2.0 collective-permute-start.22
  120.3 14.2 %attention.5.refs_2_.pack_ref = bf16[1728,512]{1,0:T(8,128)(2,1)S(1)} custom-call(s32[2,6,3]{2,1,0:T(8,128)S(1)} %pad_add_fusion.cnt_ref, bf16[864,1024]{1,0:T(8,128)(2,1)S(1)} %bitcast.28, bf16[864,1024]{1,0:T(8,128)(2,1)} %collective-permute-done.1.nb_ref, bf16[864,1024]{1,0:T(8,128)(2,1)} %bitcast.48, bf16[864,1024]{1,0:T(8,128)(2,1)} %collective-permute-done.2.gb_ref, ...), custom_call_target="tpu_custom_call" | custom-call | flops 12000000000 | bytes 14000000 | tf_op jit(solution)/shard_map/attention/pallas_call | solution.py:218
  135.8 6.4 %back_qkv.1.refs_0_ = f32[864,1024]{1,0:T(8,128)} custom-call(bf16[1728,1024]{1,0:T(8,128)(2,1)} %attention.3.pack_ref.refs_0_, bf16[1728,512]{1,0:T(8,128)(2,1)} %copy-done.3, bf16[1728,512]{1,0:T(8,128)(2,1)} %copy-done.4, bf16[1024,512]{1,0:T(8,128)(2,1)S(1)} %constant_dynamic-update-slice_fusion.16.wq_ref.wk_ref.refs_3_, ...), custom_call_target="tpu_custom_call" | custom-call | flops 6000000000 | bytes 8000000 | tf_op jit(solution)/shard_map/back_qkv/pallas_call | solution.py:367
  143.2 2.0 copy-done
  149.0 2.8 %collective-permute-start.25 = (bf16[128,512]{1,0:T(8,128)(2,1)S(1)}, bf16[128,512]{1,0:T(8,128)(2,1)S(1)}, u32[]{:S(2)}, u32[]{:S(2)}) collective-permute-start(bf16[128,512]{1,0:T(8,128)(2,1)S(1)} %get-tuple-element.44), channel_id=1, source_target_pairs={{0,16},{4,20},{8,24},{12,28},{16,0},{20,4},{24,8},{28,12},{1,17},{... | collective-permute-start | bytes 393224 | tf_op jit(solution)/shard_map/ppermute | solution.py:473
  152.6 7.6 %weight_grad.5 = (bf16[512,512]{1,0:T(8,128)(2,1)}, f32[512,512]{1,0:T(8,128)S(1)}) custom-call(s32[1]{0:T(128)} %bitcast.8.low_ref, bf16[864,1024]{1,0:T(8,128)(2,1)S(1)} %bitcast.29, bf16[864,1024]{1,0:T(8,128)(2,1)} %collective-permute-done.1.nb_ref, bf16[864,1024]{1,0:T(8,128)(2,1)} %bitcast.49, bf16[864,1024]{1,0:T(8,128)(2,1)} %collective-permute-done.2.gb_ref, ...), custom_call_target="tpu_custom_call" | custom-call | flops 5000000000 | bytes 12000000 | tf_op jit(solution)/shard_map/weight_grad/pallas_call | solution.py:271
  160.2 5.8 %collective-permute-done.25.refs_10_.refs_2_ = bf16[128,512]{1,0:T(8,128)(2,1)S(1)} collective-permute-done((bf16[128,512]{1,0:T(8,128)(2,1)S(1)}, bf16[128,512]{1,0:T(8,128)(2,1)S(1)}, u32[]{:S(2)}, u32[]{:S(2)}) %collective-permute-start.25) | collective-permute-done | bytes 131104 | tf_op jit(solution)/shard_map/ppermute | solution.py:473
  166.0 3.8 %back_context.1.refs_7_ = bf16[864,1024]{1,0:T(8,128)(2,1)} custom-call(bf16[1728,1024]{1,0:T(8,128)(2,1)} %attention.3.pack_ref.refs_0_, bf16[1728,512]{1,0:T(8,128)(2,1)} %copy-done.3, bf16[1728,512]{1,0:T(8,128)(2,1)} %copy-done.4, bf16[1024,512]{1,0:T(8,128)(2,1)S(1)} %constant_dynamic-update-slice_fusion.16.wq_ref.wk_ref.refs_3_, ...), custom_call_target="tpu_custom_call" | custom-call | flops 3500000000 | bytes 8000000 | tf_op jit(solution)/shard_map/back_context/pallas_call | solution.py:367
  169.9 10.5 %tail.1 = (f32[320,1024]{1,0:T(8,128)}, f32[320,1024]{1,0:T(8,128)}) custom-call(s32[1]{0:T(128)} %bitcast.11.core_ref, f32[864,1024]{1,0:T(8,128)} %collective-permute-done.27.recv_ref, bf16[864,1024]{1,0:T(8,128)(2,1)} %bitcast.32, bf16[864,1024]{1,0:T(8,128)(2,1)} %bitcast.50, bf16[864,256]{1,0:T(8,128)(2,1)S(1)} %bitcast.34, f32[1,1024]{1,0:T(1,128)S(1)} %bitcast.31, ...), custom_call_target="tpu_custom_call" | custom-call | flops 10000000000 | bytes 12000000 | tf_op jit(solution)/shard_map/tail/pallas_call | solution.py:423
  181.3 13.8 %collective-permute-done.29.refs_8_.recv_ref = bf16[512,512]{1,0:T(8,128)(2,1)} collective-permute-done((bf16[512,512]{1,0:T(8,128)(2,1)}, bf16[512,512]{1,0:T(8,128)(2,1)}, u32[]{:S(2)}, u32[]{:S(2)}) %collective-permute-start.29) | collective-permute-done | bytes 524320 | tf_op jit(solution)/shard_map/ppermute | solution.py:473
  197.6 4.5 %layer_output.1.refs_0_ = bf16[864,1024]{1,0:T(8,128)(2,1)} custom-call(s32[6,3]{1,0:T(8,128)S(1)} %copy.49.cnt_ref, bf16[864,1024]{1,0:T(8,128)(2,1)} %collective-permute-done.26.recv_ref, bf16[864,1024]{1,0:T(8,128)(2,1)} %bitcast.33, bf16[1728,1024]{1,0:T(8,128)(2,1)} %attention.3.pack_ref.refs_0_, bf16[1728,512]{1,0:T(8,128)(2,1)} %copy-done.3, ...), custom_call_target="tpu_custom_call" | custom-call | flops 5000000000 | bytes 10000000 | tf_op jit(solution)/shard_map/layer_output/pallas_call | solution.py:457
  208.8 6.5 %collective-permute-done.31.refs_1_ = f32[80,1024]{1,0:T(8,128)S(1)} collective-permute-done((f32[80,1024]{1,0:T(8,128)}, f32[80,1024]{1,0:T(8,128)S(1)}, u32[]{:S(2)}, u32[]{:S(2)}) %collective-permute-start.31) | collective-permute-done | bytes 327712 | tf_op jit(solution)/shard_map/ppermute | solution.py:473
  216.6 6.0 %collective-permute-done.33.refs_3_ = f32[80,1024]{1,0:T(8,128)S(1)} collective-permute-done((f32[80,1024]{1,0:T(8,128)}, f32[80,1024]{1,0:T(8,128)S(1)}, u32[]{:S(2)}, u32[]{:S(2)}) %collective-permute-start.33) | collective-permute-done | bytes 327712 | tf_op jit(solution)/shard_map/ppermute | solution.py:522
  224.4 2.0 collective-permute-start.35
  226.4 2.4 collective-permute-start.36
  236.5 2.0 collective-permute-start.46
  238.5 2.4 collective-permute-start.47
  243.6 3.3 %collective-permute-done.46.refs_2_ = bf16[128,512]{1,0:T(8,128)(2,1)S(1)} collective-permute-done((bf16[128,512]{1,0:T(8,128)(2,1)S(1)}, bf16[128,512]{1,0:T(8,128)(2,1)S(1)}, u32[]{:S(2)}, u32[]{:S(2)}) %collective-permute-start.46) | collective-permute-done | bytes 131104 | tf_op jit(solution)/shard_map/ppermute | solution.py:473
  249.5 2.6 collective-permute-start.39
  252.5 2.7 %collective-permute-done.39 = bf16[80,256]{1,0:T(8,128)(2,1)S(1)} collective-permute-done((bf16[80,256]{1,0:T(8,128)(2,1)S(1)}, bf16[80,256]{1,0:T(8,128)(2,1)S(1)}, u32[]{:S(2)}, u32[]{:S(2)}) %collective-permute-start.39) | collective-permute-done | bytes 40992 | tf_op jit(solution)/shard_map/ppermute | solution.py:473
  261.0 2.8 %collective-permute-done.42 = bf16[80,1024]{1,0:T(8,128)(2,1)S(1)} collective-permute-done((bf16[80,1024]{1,0:T(8,128)(2,1)S(1)}, bf16[80,1024]{1,0:T(8,128)(2,1)S(1)}, u32[]{:S(2)}, u32[]{:S(2)}) %collective-permute-start.42) | collective-permute-done | bytes 163872 | tf_op jit(solution)/shard_map/ppermute | solution.py:522
  (245 shorter events, 80.3 us)
Async XLA Ops:
  3.2 19.4 %collective-permute-start.10 = (bf16[128,512]{1,0:T(8,128)(2,1)}, bf16[128,512]{1,0:T(8,128)(2,1)}, u32[]{:S(2)}, u32[]{:S(2)}) collective-permute-start(bf16[128,512]{1,0:T(8,128)(2,1)} %get-tuple-element.83), channel_id=1, source_target_pairs={{0,8},{8,16},{16,24},{24,28},{28,20},{20,12},{12,4},{4,0},{1,9},{9... | collective-permute-start | bytes 393224 | tf_op jit(solution)/shard_map/ppermute | solution.py:493
  6.3 17.4 %collective-permute-start.11 = (bf16[128,512]{1,0:T(8,128)(2,1)}, bf16[128,512]{1,0:T(8,128)(2,1)S(1)}, u32[]{:S(2)}, u32[]{:S(2)}) collective-permute-start(bf16[128,512]{1,0:T(8,128)(2,1)} %get-tuple-element.83), channel_id=1, source_target_pairs={{8,0},{16,8},{24,16},{28,24},{20,28},{12,20},{4,12},{0,4},{9,1},{1... | collective-permute-start | bytes 393224 | tf_op jit(solution)/shard_map/ppermute | solution.py:496
  6.3 14.3 %collective-permute-start = (s32[6,3]{0,1:T(4,128)S(1)}, s32[6,3]{0,1:T(4,128)S(1)}, u32[]{:S(2)}, u32[]{:S(2)}) collective-permute-start(s32[6,3]{0,1:T(4,128)S(1)} %copy-done.46), channel_id=1, source_target_pairs={{0,1},{1,0},{2,3},{3,2},{4,5},{5,4},{6,7},{7,6},{8,9},{9,8},{10,11... | collective-permute-start | bytes 224 | tf_op jit(solution)/shard_map/ppermute | solution.py:473
  19.4 29.3 %collective-permute-start.2 = (bf16[864,1024]{1,0:T(8,128)(2,1)}, bf16[864,1024]{1,0:T(8,128)(2,1)}, u32[]{:S(2)}, u32[]{:S(2)}) collective-permute-start(bf16[864,1024]{1,0:T(8,128)(2,1)} %bitcast.43), channel_id=1, source_target_pairs={{0,1},{1,0},{2,3},{3,2},{4,5},{5,4},{6,7},{7,6},{8,9},{9,8},{10,11... | collective-permute-start | bytes 5308424 | tf_op jit(solution)/shard_map/ppermute | solution.py:473
  19.9 28.8 %collective-permute-start.1 = (bf16[864,1024]{1,0:T(8,128)(2,1)}, bf16[864,1024]{1,0:T(8,128)(2,1)}, u32[]{:S(2)}, u32[]{:S(2)}) collective-permute-start(bf16[864,1024]{1,0:T(8,128)(2,1)} %bitcast.23), channel_id=1, source_target_pairs={{0,1},{1,0},{2,3},{3,2},{4,5},{5,4},{6,7},{7,6},{8,9},{9,8},{10,11... | collective-permute-start | bytes 5308424 | tf_op jit(solution)/shard_map/ppermute | solution.py:473
  33.9 7.8 %collective-permute-start.15 = (bf16[128,512]{1,0:T(8,128)(2,1)S(1)}, bf16[128,512]{1,0:T(8,128)(2,1)S(1)}, u32[]{:S(2)}, u32[]{:S(2)}) collective-permute-start(bf16[128,512]{1,0:T(8,128)(2,1)S(1)} %collective-permute-done.13), channel_id=1, source_target_pairs={{8,0},{16,8},{24,16},{28,24},{20,28},{12,20},{4,12},{0,4},{9,1},{1... | collective-permute-start | bytes 393224 | tf_op jit(solution)/shard_map/ppermute | solution.py:496
  45.7 36.8 %collective-permute-start.18 = (bf16[1024,512]{1,0:T(8,128)(2,1)S(1)}, bf16[1024,512]{1,0:T(8,128)(2,1)S(1)}, u32[]{:S(2)}, u32[]{:S(2)}) collective-permute-start(bf16[1024,512]{1,0:T(8,128)(2,1)S(1)} %constant_dynamic-update-slice_fusion.8.wv_ref.wo_ref.refs_4_), channel_id=1, source_target_pairs={{0,2},{1,3},{2,0},{3,1},{4,6},{5,7},{6,4},{7,5},{8,10},{9,11},{10,... | collective-permute-start | bytes 3145736 | tf_op jit(solution)/shard_map/ppermute | solution.py:473
  47.3 43.3 %collective-permute-start.17 = (bf16[1024,512]{1,0:T(8,128)(2,1)S(1)}, bf16[1024,512]{1,0:T(8,128)(2,1)S(1)}, u32[]{:S(2)}, u32[]{:S(2)}) collective-permute-start(bf16[1024,512]{1,0:T(8,128)(2,1)S(1)} %constant_dynamic-update-slice_fusion.16.wq_ref.wk_ref.refs_3_), channel_id=1, source_target_pairs={{0,2},{1,3},{2,0},{3,1},{4,6},{5,7},{6,4},{7,5},{8,10},{9,11},{10,... | collective-permute-start | bytes 3145736 | tf_op jit(solution)/shard_map/ppermute | solution.py:473
  80.8 35.7 %collective-permute-start.19 = (bf16[512,1024]{1,0:T(8,128)(2,1)}, bf16[512,1024]{1,0:T(8,128)(2,1)S(1)}, u32[]{:S(2)}, u32[]{:S(2)}) collective-permute-start(bf16[512,1024]{1,0:T(8,128)(2,1)} %get-tuple-element.34.refs_0_), channel_id=1, source_target_pairs={{0,4},{4,0},{8,12},{12,8},{16,20},{20,16},{24,28},{28,24},{1,5},{5... | collective-permute-start | bytes 3145736 | tf_op jit(solution)/shard_map/ppermute | solution.py:473
  114.7 21.1 %collective-permute-start.20 = (bf16[512,512]{1,0:T(8,128)(2,1)S(1)}, bf16[512,512]{1,0:T(8,128)(2,1)S(1)}, u32[]{:S(2)}, u32[]{:S(2)}) collective-permute-start(bf16[512,512]{1,0:T(8,128)(2,1)S(1)} %get-tuple-element.36.refs_0_), channel_id=1, source_target_pairs={{0,4},{4,0},{8,12},{12,8},{16,20},{20,16},{24,28},{28,24},{1,5},{5... | collective-permute-start | bytes 1572872 | tf_op jit(solution)/shard_map/ppermute | solution.py:473
  116.6 19.1 %collective-permute-start.21 = (bf16[128,1024]{1,0:T(8,128)(2,1)S(1)}, bf16[128,1024]{1,0:T(8,128)(2,1)S(1)}, u32[]{:S(2)}, u32[]{:S(2)}) collective-permute-start(bf16[128,1024]{1,0:T(8,128)(2,1)S(1)} %get-tuple-element.39), channel_id=1, source_target_pairs={{0,8},{4,12},{8,0},{12,4},{16,24},{20,28},{24,16},{28,20},{1,9},{5... | collective-permute-start | bytes 786440 | tf_op jit(solution)/shard_map/ppermute | solution.py:473
  118.3 17.4 %collective-permute-start.22 = (bf16[128,1024]{1,0:T(8,128)(2,1)S(1)}, bf16[128,1024]{1,0:T(8,128)(2,1)S(1)}, u32[]{:S(2)}, u32[]{:S(2)}) collective-permute-start(bf16[128,1024]{1,0:T(8,128)(2,1)S(1)} %get-tuple-element.40), channel_id=1, source_target_pairs={{0,16},{4,20},{8,24},{12,28},{16,0},{20,4},{24,8},{28,12},{1,17},{... | collective-permute-start | bytes 786440 | tf_op jit(solution)/shard_map/ppermute | solution.py:473
  142.2 27.7 %collective-permute-start.27 = (f32[864,1024]{1,0:T(8,128)}, f32[864,1024]{1,0:T(8,128)}, u32[]{:S(2)}, u32[]{:S(2)}) collective-permute-start(f32[864,1024]{1,0:T(8,128)} %back_qkv.1.refs_0_), channel_id=1, source_target_pairs={{0,1},{1,0},{2,3},{3,2},{4,5},{5,4},{6,7},{7,6},{8,9},{9,8},{10,11... | collective-permute-start | bytes 10616840 | tf_op jit(solution)/shard_map/ppermute | solution.py:473
  142.3 17.9 %collective-permute-start.23 = (bf16[128,1024]{1,0:T(8,128)(2,1)S(1)}, bf16[128,1024]{1,0:T(8,128)(2,1)S(1)}, u32[]{:S(2)}, u32[]{:S(2)}) collective-permute-start(bf16[128,1024]{1,0:T(8,128)(2,1)S(1)} %get-tuple-element.37.refs_0_), channel_id=1, source_target_pairs={{0,24},{4,28},{8,16},{12,20},{16,8},{20,12},{24,0},{28,4},{1,25},{... | collective-permute-start | bytes 786440 | tf_op jit(solution)/shard_map/ppermute | solution.py:473
  148.2 12.0 %collective-permute-start.24 = (bf16[128,512]{1,0:T(8,128)(2,1)S(1)}, bf16[128,512]{1,0:T(8,128)(2,1)S(1)}, u32[]{:S(2)}, u32[]{:S(2)}) collective-permute-start(bf16[128,512]{1,0:T(8,128)(2,1)S(1)} %get-tuple-element.43), channel_id=1, source_target_pairs={{0,8},{4,12},{8,0},{12,4},{16,24},{20,28},{24,16},{28,20},{1,9},{5... | collective-permute-start | bytes 393224 | tf_op jit(solution)/shard_map/ppermute | solution.py:473
  149.0 17.0 %collective-permute-start.25 = (bf16[128,512]{1,0:T(8,128)(2,1)S(1)}, bf16[128,512]{1,0:T(8,128)(2,1)S(1)}, u32[]{:S(2)}, u32[]{:S(2)}) collective-permute-start(bf16[128,512]{1,0:T(8,128)(2,1)S(1)} %get-tuple-element.44), channel_id=1, source_target_pairs={{0,16},{4,20},{8,24},{12,28},{16,0},{20,4},{24,8},{28,12},{1,17},{... | collective-permute-start | bytes 393224 | tf_op jit(solution)/shard_map/ppermute | solution.py:473
  151.8 18.1 %collective-permute-start.28 = (bf16[128,512]{1,0:T(8,128)(2,1)S(1)}, bf16[128,512]{1,0:T(8,128)(2,1)S(1)}, u32[]{:S(2)}, u32[]{:S(2)}) collective-permute-start(bf16[128,512]{1,0:T(8,128)(2,1)S(1)} %get-tuple-element.41.refs_0_), channel_id=1, source_target_pairs={{0,24},{4,28},{8,16},{12,20},{16,8},{20,12},{24,0},{28,4},{1,25},{... | collective-permute-start | bytes 393224 | tf_op jit(solution)/shard_map/ppermute | solution.py:473
  169.8 25.3 %collective-permute-start.26 = (bf16[864,1024]{1,0:T(8,128)(2,1)}, bf16[864,1024]{1,0:T(8,128)(2,1)}, u32[]{:S(2)}, u32[]{:S(2)}) collective-permute-start(bf16[864,1024]{1,0:T(8,128)(2,1)} %back_context.1.refs_7_), channel_id=1, source_target_pairs={{0,1},{1,0},{2,3},{3,2},{4,5},{5,4},{6,7},{7,6},{8,9},{9,8},{10,11... | collective-permute-start | bytes 5308424 | tf_op jit(solution)/shard_map/ppermute | solution.py:473
  180.4 21.6 %collective-permute-start.30 = (f32[320,1024]{1,0:T(8,128)}, f32[320,1024]{1,0:T(8,128)S(1)}, u32[]{:S(2)}, u32[]{:S(2)}) collective-permute-start(f32[320,1024]{1,0:T(8,128)} %get-tuple-element.47.refs_7_), channel_id=1, source_target_pairs={{0,1},{1,0},{2,3},{3,2},{4,5},{5,4},{6,7},{7,6},{8,9},{9,8},{10,11... | collective-permute-start | bytes 3932168 | tf_op jit(solution)/shard_map/ppermute | solution.py:473
  180.9 14.2 %collective-permute-start.29 = (bf16[512,512]{1,0:T(8,128)(2,1)}, bf16[512,512]{1,0:T(8,128)(2,1)}, u32[]{:S(2)}, u32[]{:S(2)}) collective-permute-start(bf16[512,512]{1,0:T(8,128)(2,1)} %get-tuple-element.42.refs_7_), channel_id=1, source_target_pairs={{0,4},{4,0},{8,12},{12,8},{16,20},{20,16},{24,28},{28,24},{1,5},{5... | collective-permute-start | bytes 1572872 | tf_op jit(solution)/shard_map/ppermute | solution.py:473
  205.3 10.0 %collective-permute-start.31 = (f32[80,1024]{1,0:T(8,128)}, f32[80,1024]{1,0:T(8,128)S(1)}, u32[]{:S(2)}, u32[]{:S(2)}) collective-permute-start(f32[80,1024]{1,0:T(8,128)} %get-tuple-element.50), channel_id=1, source_target_pairs={{0,4},{4,0},{8,12},{12,8},{16,20},{20,16},{24,28},{28,24},{1,5},{5... | collective-permute-start | bytes 983048 | tf_op jit(solution)/shard_map/ppermute | solution.py:473
  205.7 10.9 %collective-permute-start.32 = (f32[80,1024]{1,0:T(8,128)}, f32[80,1024]{1,0:T(8,128)S(1)}, u32[]{:S(2)}, u32[]{:S(2)}) collective-permute-start(f32[80,1024]{1,0:T(8,128)} %get-tuple-element.51), channel_id=1, source_target_pairs={{0,2},{1,3},{2,0},{3,1},{4,6},{5,7},{6,4},{7,5},{8,10},{9,11},{10,... | collective-permute-start | bytes 983048 | tf_op jit(solution)/shard_map/ppermute | solution.py:522
  207.2 15.4 %collective-permute-start.33 = (f32[80,1024]{1,0:T(8,128)}, f32[80,1024]{1,0:T(8,128)S(1)}, u32[]{:S(2)}, u32[]{:S(2)}) collective-permute-start(f32[80,1024]{1,0:T(8,128)} %get-tuple-element.52.refs_0_), channel_id=1, source_target_pairs={{0,6},{1,7},{2,4},{3,5},{4,2},{5,3},{6,0},{7,1},{8,14},{9,15},{10,... | collective-permute-start | bytes 983048 | tf_op jit(solution)/shard_map/ppermute | solution.py:522
  224.4 12.1 %collective-permute-start.34 = (f32[80,256]{1,0:T(8,128)}, f32[80,256]{1,0:T(8,128)S(1)}, u32[]{:S(2)}, u32[]{:S(2)}) collective-permute-start(f32[80,256]{1,0:T(8,128)} %get-tuple-element.80), channel_id=1, source_target_pairs={{0,8},{4,12},{8,0},{12,4},{16,24},{20,28},{24,16},{28,20},{1,9},{5... | collective-permute-start | bytes 245768 | tf_op jit(solution)/shard_map/ppermute | solution.py:473
  224.4 14.1 %collective-permute-start.35 = (f32[80,256]{1,0:T(8,128)}, f32[80,256]{1,0:T(8,128)S(1)}, u32[]{:S(2)}, u32[]{:S(2)}) collective-permute-start(f32[80,256]{1,0:T(8,128)} %get-tuple-element.82), channel_id=1, source_target_pairs={{0,16},{4,20},{8,24},{12,28},{16,0},{20,4},{24,8},{28,12},{1,17},{... | collective-permute-start | bytes 245768 | tf_op jit(solution)/shard_map/ppermute | solution.py:473
  226.4 14.5 %collective-permute-start.36 = (f32[80,256]{1,0:T(8,128)S(1)}, f32[80,256]{1,0:T(8,128)}, u32[]{:S(2)}, u32[]{:S(2)}) collective-permute-start(f32[80,256]{1,0:T(8,128)S(1)} %get-tuple-element.81), channel_id=1, source_target_pairs={{0,24},{4,28},{8,16},{12,20},{16,8},{20,12},{24,0},{28,4},{1,25},{... | collective-permute-start | bytes 245768 | tf_op jit(solution)/shard_map/ppermute | solution.py:473
  230.7 11.2 %collective-permute-start.44 = (f32[128,512]{1,0:T(8,128)S(1)}, f32[128,512]{1,0:T(8,128)S(1)}, u32[]{:S(2)}, u32[]{:S(2)}) collective-permute-start(f32[128,512]{1,0:T(8,128)S(1)} %add_parts.6), channel_id=1, source_target_pairs={{0,2},{1,3},{2,0},{3,1},{4,6},{5,7},{6,4},{7,5},{8,10},{9,11},{10,... | collective-permute-start | bytes 786440 | tf_op jit(solution)/shard_map/ppermute | solution.py:473
  236.4 7.2 %collective-permute-start.45 = (bf16[128,512]{1,0:T(8,128)(2,1)S(1)}, bf16[128,512]{1,0:T(8,128)(2,1)S(1)}, u32[]{:S(2)}, u32[]{:S(2)}) collective-permute-start(bf16[128,512]{1,0:T(8,128)(2,1)S(1)} %get-tuple-element.57), channel_id=1, source_target_pairs={{0,8},{4,12},{8,0},{12,4},{16,24},{20,28},{24,16},{28,20},{1,9},{5... | collective-permute-start | bytes 393224 | tf_op jit(solution)/shard_map/ppermute | solution.py:473
  236.5 10.4 %collective-permute-start.46 = (bf16[128,512]{1,0:T(8,128)(2,1)S(1)}, bf16[128,512]{1,0:T(8,128)(2,1)S(1)}, u32[]{:S(2)}, u32[]{:S(2)}) collective-permute-start(bf16[128,512]{1,0:T(8,128)(2,1)S(1)} %get-tuple-element.58), channel_id=1, source_target_pairs={{0,16},{4,20},{8,24},{12,28},{16,0},{20,4},{24,8},{28,12},{1,17},{... | collective-permute-start | bytes 393224 | tf_op jit(solution)/shard_map/ppermute | solution.py:473
  238.5 8.4 %collective-permute-start.47 = (bf16[128,512]{1,0:T(8,128)(2,1)S(1)}, bf16[128,512]{1,0:T(8,128)(2,1)S(1)}, u32[]{:S(2)}, u32[]{:S(2)}) collective-permute-start(bf16[128,512]{1,0:T(8,128)(2,1)S(1)} %get-tuple-element.59), channel_id=1, source_target_pairs={{0,24},{4,28},{8,16},{12,20},{16,8},{20,12},{24,0},{28,4},{1,25},{... | collective-permute-start | bytes 393224 | tf_op jit(solution)/shard_map/ppermute | solution.py:473
  241.8 10.2 %collective-permute-start.37 = (bf16[80,256]{1,0:T(8,128)(2,1)S(1)}, bf16[80,256]{1,0:T(8,128)(2,1)S(1)}, u32[]{:S(2)}, u32[]{:S(2)}) collective-permute-start(bf16[80,256]{1,0:T(8,128)(2,1)S(1)} %get-tuple-element.77), channel_id=1, source_target_pairs={{0,8},{4,12},{8,0},{12,4},{16,24},{20,28},{24,16},{28,20},{1,9},{5... | collective-permute-start | bytes 122888 | tf_op jit(solution)/shard_map/ppermute | solution.py:473
  247.0 11.9 %collective-permute-start.48 = (f32[128,512]{1,0:T(8,128)S(1)}, f32[128,512]{1,0:T(8,128)S(1)}, u32[]{:S(2)}, u32[]{:S(2)}) collective-permute-start(f32[128,512]{1,0:T(8,128)S(1)} %add_parts.7), channel_id=1, source_target_pairs={{0,2},{1,3},{2,0},{3,1},{4,6},{5,7},{6,4},{7,5},{8,10},{9,11},{10,... | collective-permute-start | bytes 786440 | tf_op jit(solution)/shard_map/ppermute | solution.py:473
  (64 other events, 539.6 us)

commit v3 on v2

v3 whole, which is shorter than its diff:
```python
import functools

import jax
import jax.numpy as jnp
import ml_dtypes
import numpy as np
from jax import lax
from jax.experimental import pallas as pl
from jax.experimental.pallas import tpu as pltpu
from jax.sharding import PartitionSpec as P

D = 1024
HD = 64
GROUPS = 3
CAP = 48
GRID = 12
PIX = 64
TOK = GROUPS * CAP
PAIR = 128
GROUP_BANDS = ((0, 4), (4, 8), (8, 10))
NORM_EPS = 1e-06
F32 = jnp.float32
BF16 = jnp.bfloat16
VMEM_LIMIT = 48 * 1024 * 1024


def dot_nn(a, b):
    return lax.dot_general(a, b, (((1,), (0,)), ((), ())), preferred_element_type=F32)


def dot_nt(a, b):
    return lax.dot_general(a, b, (((1,), (1,)), ((), ())), preferred_element_type=F32)


def dot_tn(a, b):
    return lax.dot_general(a, b, (((0,), (0,)), ((), ())), preferred_element_type=F32)


def live_column(c0, c1, c2):
    row = lax.broadcasted_iota(jnp.int32, (TOK, 1), 0)
    return (
        (row < c0)
        | ((row >= CAP) & (row < CAP + c1))
        | ((row >= 2 * CAP) & (row < 2 * CAP + c2))
    )


def params():
    return pltpu.CompilerParams(vmem_limit_bytes=VMEM_LIMIT)


def cost(flops, nbytes):
    return pl.CostEstimate(flops=int(flops / 1000), bytes_accessed=int(nbytes / 1000), transcendentals=0)


def stem_kernel(
    cnt_ref, idx_ref, patch_ref, w_ref, gain_ref, parts, genc_ref, og_ref,
    emb_ref, normed_ref, gl_ref, cols_ref,
):
    step = pl.program_id(0)
    scenes = patch_ref.shape[0]
    patch_iota = lax.broadcasted_iota(jnp.int32, (TOK, parts.shape[1]), 1)
    picked, placed = [], []
    for s in range(scenes):
        onehot = (idx_ref[s] == patch_iota).astype(F32).astype(BF16)
        picked.append(dot_nn(onehot, patch_ref[s]).astype(BF16))
        placed.append(
            (dot_nn(onehot, parts[0]) + dot_nn(onehot, parts[1])) + dot_nn(onehot, parts[2])
        )
        live = live_column(
            cnt_ref[step * scenes + s, 0], cnt_ref[step * scenes + s, 1], cnt_ref[step * scenes + s, 2]
        )
        gl_ref[s] = jnp.where(live, og_ref[s].astype(F32), 0.0).astype(BF16)
    for g, (start, end) in enumerate(GROUP_BANDS):
        rows = slice(g * CAP, (g + 1) * CAP)
        columns = jnp.concatenate([p[rows, start * PIX : end * PIX] for p in picked], axis=0)
        summed = dot_nn(columns, w_ref[start * PIX : end * PIX, :])
        width = (end - start) * PIX
        for s in range(scenes):
            values = summed[s * CAP : (s + 1) * CAP] + (placed[s][rows] + genc_ref[g : g + 1, :])
            emb = values.astype(BF16)
            emb_ref[s, rows, :] = emb
            x = emb.astype(F32)
            centre = jnp.mean(x, axis=-1, keepdims=True)
            dev = x - centre
            spread = jnp.mean(dev * dev, axis=-1, keepdims=True)
            centred = dev * lax.rsqrt(spread + NORM_EPS)
            normed_ref[s, rows, :] = (centred * gain_ref[...]).astype(BF16)
            cols_ref[s, rows, :width] = columns[s * CAP : (s + 1) * CAP]
            if width < cols_ref.shape[2]:
                cols_ref[s, rows, width:] = jnp.zeros((CAP, cols_ref.shape[2] - width), BF16)


def stem_call(counts, index_col, patches, w_stem, gain, table, genc, out_grad):
    scenes, patch_count, width = patches.shape
    block = 3 if scenes % 3 == 0 else 1
    col_width = max(e - s for s, e in GROUP_BANDS) * PIX
    per = lambda shape: pl.BlockSpec((block,) + shape, lambda i: (i, 0, 0))
    whole = lambda a: pl.BlockSpec(a.shape, lambda i: (0,) * a.ndim)
    rows = jax.ShapeDtypeStruct((scenes, TOK, D), BF16)
    return pl.pallas_call(
        stem_kernel,
        grid=(scenes // block,),
        in_specs=[
            pl.BlockSpec(memory_space=pltpu.SMEM),
            per((TOK, 1)),
            per((patch_count, width)),
            whole(w_stem),
            whole(gain),
            whole(table),
            whole(genc),
            per((TOK, D)),
        ],
        out_specs=[per((TOK, D)), per((TOK, D)), per((TOK, D)), per((TOK, col_width))],
        out_shape=[rows, rows, rows, jax.ShapeDtypeStruct((scenes, TOK, col_width), BF16)],
        compiler_params=params(),
        cost_estimate=cost(8e9, 12e6),
        name="stem_norm",
    )(counts, index_col, patches, w_stem, gain, table, genc, out_grad)


def attention_kernel(
    deps, cnt_ref, na_ref, nb_ref, ga_ref, gb_ref, wq_ref, wk_ref, wv_ref, wo_ref, *refs
):
    out_ref, n_s, g_s, qkv = refs[deps:]
    half, step = pl.program_id(0), pl.program_id(1)
    rows = n_s.shape[0]
    scenes = rows // TOK
    width = wq_ref.shape[1]

    @pl.when(half == 0)
    def _():
        n_s[...] = na_ref[...]
        g_s[...] = ga_ref[...]

    @pl.when(half != 0)
    def _():
        n_s[...] = nb_ref[...]
        g_s[...] = gb_ref[...]

    into = jnp.concatenate([wq_ref[...], wk_ref[...], wv_ref[...]], axis=1)
    qkv[:, : 3 * width] = dot_nn(n_s[...], into).astype(BF16)
    qkv[:, 3 * width :] = dot_nn(g_s[...], wo_ref[...]).astype(BF16)
    heads = width // HD
    lane = lax.broadcasted_iota(jnp.int32, (1, width), 1)
    masks = [(lane // HD == h).astype(F32).astype(BF16) for h in range(heads)]
    scale = jnp.asarray(HD ** (-0.5), BF16)
    first_of_pair = lax.broadcasted_iota(jnp.int32, (1, PAIR), 1) < HD

    def own_lanes(tall):
        tiles = []
        for t in range(width // PAIR):
            at = slice(t * PAIR, (t + 1) * PAIR)
            one = tall[2 * t * TOK : (2 * t + 1) * TOK, at]
            two = tall[(2 * t + 1) * TOK : (2 * t + 2) * TOK, at]
            tiles.append(jnp.where(first_of_pair, one, two))
        return jnp.concatenate(tiles, axis=1)

    def scene_body(s, _):
        base = pl.multiple_of(s * TOK, 16)
        at = pl.ds(base, TOK)
        scene = step * scenes + s
        live = live_column(cnt_ref[half, scene, 0], cnt_ref[half, scene, 1], cnt_ref[half, scene, 2])
        bias = jnp.where(live, 0.0, -1e30)
        q, k, v, dc = [qkv[at, c * width : (c + 1) * width] for c in range(4)]
        tall_q = jnp.concatenate([q * (m * scale) for m in masks], axis=0)
        tall_dc = jnp.concatenate([dc * m for m in masks], axis=0)
        scores = dot_nt(k, tall_q)
        grad_probs = dot_nt(v, tall_dc)
        probs_parts, score_parts = [], []
        for start in range(0, heads * TOK, PAIR):
            cols = slice(start, min(start + PAIR, heads * TOK))
            part = scores[:, cols] + bias
            lifted = jnp.exp(part - jnp.max(part, axis=0, keepdims=True))
            probs = lifted * (1.0 / jnp.sum(lifted, axis=0, keepdims=True))
            weighted = probs * grad_probs[:, cols]
            inner = jnp.sum(weighted, axis=0, keepdims=True)
            probs_parts.append(probs.astype(BF16))
            score_parts.append((weighted - probs * inner).astype(BF16))
        half_probs = jnp.concatenate(probs_parts, axis=1)
        grad_score = jnp.concatenate(score_parts, axis=1)
        out_ref[at, :width] = (own_lanes(dot_tn(grad_score, k)) * HD ** (-0.5)).astype(BF16)
        out_ref[at, width : 2 * width] = dot_nn(grad_score, tall_q).astype(BF16)
        out_ref[at, 2 * width : 3 * width] = dot_nn(half_probs, tall_dc).astype(BF16)
        out_ref[at, 3 * width :] = own_lanes(dot_tn(half_probs, v)).astype(BF16)
        return 0

    lax.fori_loop(0, scenes, scene_body, 0)


def block_rows(tokens):
    return 3 * TOK if tokens % (3 * TOK) == 0 else TOK


def two_halves(rows, steps):
    first = pl.BlockSpec((rows, D), lambda h, i: (jnp.where(h == 0, i, steps - 1), 0))
    second = pl.BlockSpec((rows, D), lambda h, i: (jnp.where(h == 0, 0, i), 0))
    return [first, second, first, second]


ANYWHERE = pl.BlockSpec(memory_space=pl.ANY)
SCALARS = pl.BlockSpec(memory_space=pltpu.SMEM)


def section(weights, c):
    each = 4 // len(weights)
    return weights[c // each], c % each


def attention_call(counts, na, nb, ga, gb, weights, deps=()):
    tokens = na.shape[0]
    rows = block_rows(tokens)
    steps = tokens // rows
    sections = [section(weights, c) for c in range(4)]
    width = weights[0].shape[1] * len(weights) // 4
    weight = lambda at: pl.BlockSpec((D, width), lambda h, i: (0, at))
    return pl.pallas_call(
        functools.partial(attention_kernel, len(deps)),
        grid=(2, steps),
        in_specs=[SCALARS] + two_halves(rows, steps) + [weight(at) for _, at in sections] + [ANYWHERE] * len(deps),
        out_specs=pl.BlockSpec((rows, 4 * width), lambda h, i: (h * steps + i, 0)),
        out_shape=jax.ShapeDtypeStruct((2 * tokens, 4 * width), BF16),
        scratch_shapes=[
            pltpu.VMEM((rows, D), BF16),
            pltpu.VMEM((rows, D), BF16),
            pltpu.VMEM((rows, 4 * width), BF16),
        ],
        compiler_params=params(),
        cost_estimate=cost(20e9, 14e6),
        name="attention",
    )(counts, na, nb, ga, gb, *[a for a, _ in sections], *deps)


def transpose_kernel(*refs):
    count = len(refs) // 2
    for ref, out_ref in zip(refs[:count], refs[count:]):
        out_ref[...] = ref[...].T


def transpose_call(arrays):
    shapes = [jax.ShapeDtypeStruct(a.shape[::-1], a.dtype) for a in arrays]
    return pl.pallas_call(
        transpose_kernel,
        out_shape=shapes,
        compiler_params=params(),
        cost_estimate=cost(4e9, 8e6),
        name="transpose_rows",
    )(*arrays)


def weight_grad_kernel(deps, blocks, low_ref, na_ref, nb_ref, ga_ref, gb_ref, pack_ref, *refs):
    send_ref, keep_ref, total = refs[deps:]
    section_at = pl.program_id(0)
    tokens = na_ref.shape[1]

    def product(a_ref, b_ref):
        total[...] = dot_nn(a_ref[...], pack_ref[:tokens, :]) + dot_nn(b_ref[...], pack_ref[tokens:, :])

    pl.when(section_at < 3)(lambda: product(na_ref, nb_ref))
    pl.when(section_at == 3)(lambda: product(ga_ref, gb_ref))
    rows = total.shape[0] // blocks
    low = low_ref[0]
    for b in range(blocks // 2):
        at = slice(b * rows, (b + 1) * rows)
        mine = pl.multiple_of((2 * b + low) * rows, rows)
        other = pl.multiple_of((2 * b + 1 - low) * rows, rows)
        keep_ref[at, :] = total[pl.ds(mine, rows), :]
        send_ref[at, :] = total[pl.ds(other, rows), :].astype(BF16)


def weight_grad_call(low, na, nb, ga, gb, pack, blocks, deps=()):
    width = pack.shape[1] // 4
    whole = pl.BlockSpec(na.shape, lambda c: (0, 0))
    out = pl.BlockSpec((D // 2, width), lambda c: (0, c))
    return pl.pallas_call(
        functools.partial(weight_grad_kernel, len(deps), blocks),
        grid=(4,),
        in_specs=[SCALARS]
        + [whole] * 4
        + [pl.BlockSpec((pack.shape[0], width), lambda c: (0, c))]
        + [ANYWHERE] * len(deps),
        out_specs=[out, out],
        out_shape=[
            jax.ShapeDtypeStruct((D // 2, 4 * width), BF16),
            jax.ShapeDtypeStruct((D // 2, 4 * width), F32),
        ],
        scratch_shapes=[pltpu.VMEM((D, width), F32)],
        compiler_params=params(),
        cost_estimate=cost(6e9, 12e6),
        name="weight_grad",
    )(low, na, nb, ga, gb, pack, *deps)


def combine_kernel(deps, place_ref, keep_ref, recv_ref, *refs):
    refs = refs[deps:]
    rows = refs[0].shape[0]
    place = place_ref[0]
    for j, ref in enumerate(refs):
        at = pl.ds(pl.multiple_of((place ^ j) * rows, rows), rows)
        ref[...] = (keep_ref[at, :] + recv_ref[at, :].astype(F32)).astype(ref.dtype)


def combine_call(place, keep, recv, blocks, dtype, deps=()):
    rows, cols = keep.shape[0] // blocks, keep.shape[1]
    whole = lambda a: pl.BlockSpec(a.shape, lambda: (0, 0))
    shapes = [jax.ShapeDtypeStruct((rows, cols), F32 if j == 0 else dtype) for j in range(blocks)]
    return pl.pallas_call(
        functools.partial(combine_kernel, len(deps)),
        in_specs=[SCALARS, whole(keep), whole(recv)] + [ANYWHERE] * len(deps),
        out_specs=[pl.BlockSpec((rows, cols), lambda: (0, 0))] * blocks,
        out_shape=shapes,
        compiler_params=params(),
        cost_estimate=cost(1e6, 5e6),
        name="combine",
    )(place, keep, recv, *deps)


def add_kernel(count, *refs):
    total = refs[0][...]
    for ref in refs[1:count]:
        total = total + ref[...].astype(F32)
    refs[-1][...] = total


def add_call(parts, deps=()):
    spec = pl.BlockSpec(parts[0].shape, lambda: (0, 0))
    return pl.pallas_call(
        functools.partial(add_kernel, len(parts)),
        in_specs=[spec] * len(parts) + [ANYWHERE] * len(deps),
        out_specs=spec,
        out_shape=jax.ShapeDtypeStruct(parts[0].shape, F32),
        compiler_params=params(),
        cost_estimate=cost(1e6, 2e6),
        name="add_parts",
    )(*parts, *deps)


def split_weights(counts, refs):
    out = []
    for count in counts:
        out.append(refs[:count])
        refs = refs[count:]
    return out, refs


def back_product(pack_refs, weight_refs, start, first, count):
    total = None
    for pack_ref, refs in zip(pack_refs, weight_refs):
        width = refs[0].shape[1] * len(refs) // 4
        for c in range(first, first + count):
            ref, at = section(refs, c)
            columns = pack_ref[:, (c - start) * width : (c - start + 1) * width]
            new = dot_nt(columns, ref[:, at * width : (at + 1) * width])
            total = new if total is None else total + new
    return total


def weight_specs(weights):
    return [pl.BlockSpec(w.shape, lambda i: (0, 0)) for block in weights for w in block]


def back_kernel(counts, *refs):
    packs = refs[: len(counts)]
    weights, refs = split_weights(counts, refs[len(counts) :])
    grad_ref, mixed_ref = refs[-2:]
    grad_ref[...] = back_product(packs, weights, 0, 0, 3)
    mixed_ref[...] = back_product(packs, weights, 0, 3, 1).astype(BF16)


def back_call(packs, weights, half, deps=()):
    tokens = packs[0].shape[0] // 2
    rows = block_rows(tokens)
    steps = tokens // rows
    out = pl.BlockSpec((rows, D), lambda i: (i, 0))
    return pl.pallas_call(
        functools.partial(back_kernel, [len(w) for w in weights]),
        grid=(steps,),
        in_specs=[pl.BlockSpec((rows, p.shape[1]), lambda i: (half * steps + i, 0)) for p in packs]
        + weight_specs(weights)
        + [ANYWHERE] * len(deps),
        out_specs=[out, out],
        out_shape=[jax.ShapeDtypeStruct((tokens, D), F32), jax.ShapeDtypeStruct((tokens, D), BF16)],
        compiler_params=params(),
        cost_estimate=cost(10e9, 12e6),
        name="back",
    )(*packs, *[w for block in weights for w in block], *deps)


def tail_kernel(counts, core_ref, recv_ref, emb_ref, gl_ref, cols_ref, gain_ref, *refs):
    packs = refs[: len(counts)]
    weights, refs = split_weights(counts, refs[len(counts) :])
    send_ref, keep_ref, acc = refs[-3:]
    step = pl.program_id(0)
    rows = emb_ref.shape[0]
    scenes = rows // TOK

    @pl.when(step == 0)
    def _():
        acc[...] = jnp.zeros_like(acc)

    grad_normed = recv_ref[...] + back_product(packs, weights, 0, 0, 3)
    x = emb_ref[...].astype(F32)
    dev = x - jnp.mean(x, axis=-1, keepdims=True)
    inv_std = lax.rsqrt(jnp.mean(dev * dev, axis=-1, keepdims=True) + NORM_EPS)
    centred = dev * inv_std
    scaled = grad_normed * gain_ref[...]
    first_mean = jnp.mean(scaled, axis=-1, keepdims=True)
    second_mean = jnp.mean(scaled * centred, axis=-1, keepdims=True)
    back = inv_std * (scaled - first_mean - centred * second_mean)
    grad_in = (gl_ref[...].astype(F32) + back).astype(BF16)
    for g, (start, end) in enumerate(GROUP_BANDS):
        at = [slice(s * TOK + g * CAP, s * TOK + (g + 1) * CAP) for s in range(scenes)]
        columns = jnp.concatenate([cols_ref[a, : (end - start) * PIX] for a in at], axis=0)
        grads = jnp.concatenate([grad_in[a] for a in at], axis=0)
        acc[start * PIX : end * PIX, :] += dot_tn(columns, grads)

    @pl.when(step == pl.num_programs(0) - 1)
    def _():
        size = keep_ref.shape[0]
        core = core_ref[0]
        keep_ref[...] = acc[pl.ds(pl.multiple_of(core * size, size), size), :]
        send_ref[...] = acc[pl.ds(pl.multiple_of((1 - core) * size, size), size), :]


def tail_call(core, recv, emb, gl, cols, gain, packs, weights, deps=()):
    tokens = emb.shape[0]
    rows = block_rows(tokens)
    per = lambda a: pl.BlockSpec((rows, a.shape[1]), lambda i: (i, 0))
    stem_rows = GROUP_BANDS[-1][1] * PIX
    half = jax.ShapeDtypeStruct((stem_rows // 2, D), F32)
    return pl.pallas_call(
        functools.partial(tail_kernel, [len(w) for w in weights]),
        grid=(tokens // rows,),
        in_specs=[SCALARS, per(recv), per(emb), per(gl), per(cols)]
        + [pl.BlockSpec(gain.shape, lambda i: (0, 0))]
        + [pl.BlockSpec((rows, 3 * (p.shape[1] // 4)), lambda i: (i, 0)) for p in packs]
        + weight_specs(weights)
        + [ANYWHERE] * len(deps),
        out_specs=[pl.BlockSpec(half.shape, lambda i: (0, 0))] * 2,
        out_shape=[half, half],
        scratch_shapes=[pltpu.VMEM((stem_rows, D), F32)],
        compiler_params=params(),
        cost_estimate=cost(10e9, 12e6),
        name="tail",
    )(core, recv, emb, gl, cols, gain, *packs, *[w for block in weights for w in block], *deps)


def output_kernel(counts, cnt_ref, recv_ref, emb_ref, *refs):
    packs, out_ref = refs[: len(counts)], refs[-1]
    weights, _ = split_weights(counts, refs[len(counts) :])
    step = pl.program_id(0)
    scenes = emb_ref.shape[0] // TOK
    mixed = recv_ref[...].astype(F32) + back_product(packs, weights, 3, 3, 1)
    total = emb_ref[...].astype(F32) + mixed
    for s in range(scenes):
        scene = step * scenes + s
        live = live_column(cnt_ref[scene, 0], cnt_ref[scene, 1], cnt_ref[scene, 2])
        at = slice(s * TOK, (s + 1) * TOK)
        out_ref[at, :] = jnp.where(live, total[at], 0.0).astype(BF16)


def output_call(counts, recv, emb, packs, weights, deps=()):
    tokens = emb.shape[0]
    rows = block_rows(tokens)
    per = lambda a: pl.BlockSpec((rows, a.shape[1]), lambda i: (i, 0))
    return pl.pallas_call(
        functools.partial(output_kernel, [len(w) for w in weights]),
        grid=(tokens // rows,),
        in_specs=[SCALARS, per(recv), per(emb)]
        + [pl.BlockSpec((rows, p.shape[1] // 4), lambda i: (i, 3)) for p in packs]
        + weight_specs(weights)
        + [ANYWHERE] * len(deps),
        out_specs=per(emb),
        out_shape=jax.ShapeDtypeStruct(emb.shape, BF16),
        compiler_params=params(),
        cost_estimate=cost(5e9, 10e6),
        name="layer_output",
    )(counts, recv, emb, *packs, *[w for block in weights for w in block], *deps)


def swap(x, axis, size, bit):
    return lax.ppermute(x, axis, [(i, i ^ bit) for i in range(size)])


def together(*values):
    return lax.optimization_barrier(values)


class Ring:
    def __init__(self, x, axis, size):
        self.axis, self.size, self.rows = axis, size, x.shape[0]
        order = list(range(0, size, 2)) + list(range(size - 1, 0, -2))
        self.forward = [(order[i], order[(i + 1) % size]) for i in range(size)]
        self.backward = [(order[(i + 1) % size], order[i]) for i in range(size)]
        me = lax.axis_index(axis)
        self.here = jnp.where(me % 2 == 0, me // 2, size - 1 - me // 2)
        self.moving = [x, x]
        self.full = jnp.zeros((size * self.rows,) + x.shape[1:], x.dtype)
        self.steps = 0
        self.put(x, 0)

    def put(self, block, distance):
        size = self.size
        at = (self.here + distance + size) % size
        owner = jnp.where(at < size // 2, 2 * at, 2 * (size - 1 - at) + 1)
        self.full = lax.dynamic_update_slice_in_dim(self.full, block, owner * self.rows, 0)

    def step(self, *beside):
        self.steps += 1
        moved = [lax.ppermute(self.moving[0], self.axis, self.forward)]
        if self.steps <= (self.size - 1) // 2:
            moved.append(lax.ppermute(self.moving[1], self.axis, self.backward))
        moved, beside = together(moved, beside)
        self.moving = moved
        self.put(moved[0], -self.steps)
        if len(moved) > 1:
            self.put(moved[1], self.steps)
        return beside


def line_up(pair, arrived, high):
    rows = pair.shape[0]
    full = jnp.zeros(((len(arrived) + 1) * rows,) + pair.shape[1:], pair.dtype)
    for j, block in enumerate([pair] + list(arrived)):
        full = lax.dynamic_update_slice_in_dim(full, block, (high ^ j) * rows, 0)
    return full


def halve_stem(recv, keep, group):
    mine = lax.axis_index("group") // 2 * 2 + lax.axis_index("dp") % 2
    return combine_call(mine.reshape(1), keep, recv, group // 2 * 2, F32)


def sum_stem(parts, beside, dp, group):
    core = lax.axis_index("group") % 2
    far = lax.axis_index("group") // 2
    low = lax.axis_index("dp") % 2
    high = lax.axis_index("dp") // 2
    fars, highs = group // 2, dp // 2
    mine = far * 2 + low
    small, width = parts[0].shape
    rows = 2 * fars * small

    def hop(block, f, b):
        if f:
            pairs = [
                (d * group + g, (d ^ b) * group + (g ^ (2 * f))) for d in range(dp) for g in range(group)
            ]
            return lax.ppermute(block, ("dp", "group"), pairs)
        return swap(block, "dp", dp, b)

    hops = [(k // 2, k % 2) for k in range(1, 2 * fars)]
    arrived, beside = together([hop(part, f, b) for part, (f, b) in zip(parts[1:], hops)], beside)
    total = parts[0]
    for part in arrived:
        total = total + part
    cols = width // highs
    part = lax.dynamic_slice_in_dim(total, high * cols, cols, 1)
    for j in range(1, highs):
        away = lax.dynamic_slice_in_dim(total, (high ^ j) * cols, cols, 1)
        part = part + swap(away, "dp", dp, 2 * j)
    part = part.astype(BF16)
    line = jnp.zeros((small, width), BF16)
    line = lax.dynamic_update_slice_in_dim(line, part, high * cols, 1)
    for j in range(1, highs):
        line = lax.dynamic_update_slice_in_dim(
            line, swap(part, "dp", dp, 2 * j), (high ^ j) * cols, 1
        )
    block = jnp.zeros((rows, width), BF16)
    block = lax.dynamic_update_slice_in_dim(block, line, mine * small, 0)
    for f, b in hops:
        target = (far ^ f) * 2 + (low ^ b)
        block = lax.dynamic_update_slice_in_dim(block, hop(line, f, b), target * small, 0)
    partner = swap(block, "group", group, 1)
    first = jnp.where(core == 0, block, partner)
    second = jnp.where(core == 0, partner, block)
    return jnp.concatenate([first, second], axis=0).astype(F32), beside


def encoding_tables(patch_count):
    quarter = D // 4
    half_width = D // 2
    power = lambda n: np.power(np.float32(10000.0), -np.arange(n, dtype=np.float32) / np.float32(n))
    at = np.arange(GRID).astype(np.float32)[:, None] * power(quarter)
    both = np.concatenate([np.sin(at), np.cos(at)], axis=-1)
    patch = np.arange(patch_count)
    rest = np.concatenate([both[patch // GRID], both[patch % GRID]], axis=-1).astype(np.float32)
    parts = []
    for _ in range(3):
        parts.append(rest.astype(ml_dtypes.bfloat16))
        rest = rest - parts[-1].astype(np.float32)
    group_at = np.arange(GROUPS).astype(np.float32)[:, None] * power(half_width)
    return np.stack(parts), np.concatenate([np.sin(group_at), np.cos(group_at)], axis=-1).astype(np.float32)


def on_device(dp, group, patches, vis_index, vis_count, w_stem, ln_gain, w_qkv, w_out, out_grad):
    scenes = patches.shape[0]
    tokens = scenes * TOK
    width = w_qkv.shape[2]
    fars = range(1, group // 2)
    rests = range(1, dp // 2)
    dp_low, dp_high = lax.axis_index("dp") % 2, lax.axis_index("dp") // 2
    low, high = dp_low.reshape(1), dp_high.reshape(1)
    core = (lax.axis_index("group") % 2).reshape(1)

    shard = jnp.concatenate([w_qkv.reshape(w_qkv.shape[0], 3 * width), w_out.T], axis=1)
    ring = Ring(shard, "dp", dp)
    far_shards = [swap(shard[:, 2 * width :], "group", group, 2 * f) for f in fars]
    counts = vis_count.astype(jnp.int32)
    counts_far = swap(counts, "group", group, 1)
    table, genc = encoding_tables(patches.shape[1])
    gain = ln_gain.reshape(1, D)
    stem = stem_call(
        counts,
        vis_index.reshape(scenes, TOK, 1),
        patches,
        w_stem,
        gain,
        jnp.asarray(table),
        jnp.asarray(genc),
        out_grad.reshape(scenes, TOK, D),
    )
    stem, far_shards, counts_far = ring.step(stem, far_shards, counts_far)
    emb, normed, gl = [a.reshape(tokens, D) for a in stem[:3]]
    cols = stem[3].reshape(tokens, stem[3].shape[2])
    both_counts = jnp.stack([counts, counts_far])
    both = [normed, swap(normed, "group", group, 1), gl, swap(gl, "group", group, 1)]
    partners = [swap(x, "dp", dp, 1) for x in far_shards]
    both, partners = ring.step(both, partners)
    (turned,) = ring.step(transpose_call(both))
    while ring.steps < dp // 2:
        ring.step()
    own = ring.full
    pairs = [
        jnp.concatenate([jnp.where(dp_low == 0, x, y), jnp.where(dp_low == 0, y, x)], axis=0)
        for x, y in zip(far_shards, partners)
    ]
    own, pairs = together(own, pairs)
    weights = [[own]]
    far_own = [swap(own[:, : 2 * width], "group", group, 2 * f) for f in fars]
    far_rest = [[swap(pair, "dp", dp, 2 * j) for j in rests] for pair in pairs]

    packs, kept, coming, landing = [], [], [], []

    def first_to_rest(n):
        return combine_call(high, kept[n], coming[n], dp // 2, BF16)

    def rest_swaps(blocks):
        return [blocks[0]] + [swap(blocks[j], "dp", dp, 2 * j) for j in rests]

    packs.extend(together(attention_call(both_counts, *both, weights[0])))
    for n in fars:
        send, keep = weight_grad_call(low, *turned, packs[-1], dp)
        if n == 1:
            send, keep, far_own, far_rest = together(send, keep, far_own, far_rest)
            for f in fars:
                weights.append([far_own[f - 1], line_up(pairs[f - 1], far_rest[f - 1], dp_high)])
        else:
            send, keep = together(send, keep)
        kept.append(keep)
        coming.append(swap(send, "dp", dp, 1))
        pack, coming[-1] = together(attention_call(both_counts, *both, weights[n]), coming[-1])
        packs.append(pack)
        blocks, packs = together(first_to_rest(n - 1), packs)
        landing.append(rest_swaps(blocks))
    back, mixed = together(*back_call(packs, weights, 1))
    back = swap(back, "group", group, 1)
    mixed = swap(mixed, "group", group, 1)
    send, keep = weight_grad_call(low, *turned, packs[-1], dp)
    send, keep, landing[-1][1] = together(send, keep, landing[-1][1])
    kept.append(keep)
    coming.append(swap(send, "dp", dp, 1))
    back, landing = together(back, landing)
    stem_send, stem_keep, mixed, coming[-1] = together(
        *tail_call(core, back, emb, gl, cols, gain, packs, weights), mixed, coming[-1]
    )
    stem_recv = swap(stem_send, "group", group, 1)
    last = rest_swaps(first_to_rest(-1))
    near = dp // 2 * 3 // 4
    output, stem_recv, last[:near] = together(
        output_call(counts, mixed, emb, packs, weights), stem_recv, last[:near]
    )
    stem_parts = halve_stem(stem_recv, stem_keep, group)
    grad_w_stem, last[near:] = sum_stem(stem_parts, last[near:], dp, group)
    shares = [add_call(parts) for parts in landing + [last]]

    total = shares[0]
    for f in fars:
        total = total + swap(shares[f], "group", group, 2 * f)
    grad_w_qkv = total[:, : 3 * width].reshape(total.shape[0], 3, width)
    grad_w_out = total[:, 3 * width :].T
    return (output.reshape(scenes, GROUPS, CAP, D), grad_w_stem, grad_w_qkv, grad_w_out)


def solution(mesh):
    sizes = dict(mesh.shape)
    return jax.shard_map(
        functools.partial(on_device, sizes["dp"], sizes["group"]),
        mesh=mesh,
        in_specs=(
            P(("dp", "group"), None, None),
            P(("dp", "group"), None, None),
            P(("dp", "group"), None),
            P(),
            P(),
            P("dp", None, "group"),
            P("group", "dp"),
            P(("dp", "group"), None, None, None),
        ),
        out_specs=(
            P(("dp", "group"), None, None, None),
            P(),
            P("dp", None, "group"),
            P("group", "dp"),
        ),
        check_vma=False,
    )
```

time: 269 us -> 254 us (0.944)
  Pallas kernels: 110 us -> 95.2 us
  waiting for transfers between devices: 59.9 us -> 67.2 us
  starting transfers between devices: 61 us -> 54.7 us
    ppermute x14 -> x7, starting transfers between devices: 21.5 us -> 7.37 us  [the longest x4 5.11 us: step(): moved = [lax.ppermute(self.moving[0], self.axis, self.forward)]]
    pallas_call x3 -> x2, Pallas kernels: 51.3 us -> 37.4 us  [attention_call(): pl.pallas_call(functools.partial(attention_kernel, len(deps)), grid=(2, s...]
    ppermute x31 -> x30, starting transfers between devices: 33.2 us -> 42.9 us  [swap(): return lax.ppermute(x, axis, [(i, i ^ bit) for i in range(size)])]
    pallas_call x3 -> x2, Pallas kernels: 24.5 us -> 17.5 us  [weight_grad_call(): pl.pallas_call(functools.partial(weight_grad_kernel, len(deps), blocks),...]
    ppermute x4, waiting for transfers between devices: 10.5 us -> 16.7 us  [hop(): return lax.ppermute(block, ('dp', 'group'), pairs)]
    dynamic_update_slice x15 -> x11, local copies, waits for them, and re-layouts: 1.1 us -> 5.01 us  [the longest x4 2.95 us: line_up(): full = lax.dynamic_update_slice_in_dim(full, block, (high ^ j) * rows, 0)]
    pallas_call x4, Pallas kernels: 25.2 us -> 28.2 us  [the longest x1 10.9 us: tail_call(): pl.pallas_call(functools.partial(tail_kernel, [len(w) for w in weights]),...]
    ppermute x14 -> x7, waiting for transfers between devices: 5.34 us -> 7.22 us  [the longest x4 7.21 us: step(): moved = [lax.ppermute(self.moving[0], self.axis, self.forward)]]
  transfers between devices with their start and end apart: 49 -> 41, of which waited for: 18 -> 13; matrix products, arithmetic and copies ran while one was open for 3% -> 4% of each run, Pallas kernels for 38% -> 33%
where the time goes in v3:
time: 254 us; the launch traced here: 253 us
  Pallas kernels  95.2 us (37%)
  waiting for transfers between devices  67.2 us (26%)
  starting transfers between devices  54.7 us (22%)
  local copies, waits for them, and re-layouts  30.4 us (12%)
  other arithmetic  4.46 us (2%)
    ppermute x30, waiting for transfers between devices, swap(): return lax.ppermute(x, axis, [(i, i ^ bit) for i in range(size)])  43.3 us
    ppermute x30, starting transfers between devices, swap(): return lax.ppermute(x, axis, [(i, i ^ bit) for i in range(size)])  42.9 us
    pallas_call x2, Pallas kernels, attention_call(): pl.pallas_call(functools.partial(attention_kernel, len(deps)), grid=(2, s...  37.4 us
    unnamed x77, local copies, waits for them, and re-layouts  22.9 us
    pallas_call x2, Pallas kernels, weight_grad_call(): pl.pallas_call(functools.partial(weight_grad_kernel, len(deps), blocks),...  17.5 us
    ppermute x4, waiting for transfers between devices, hop(): return lax.ppermute(block, ('dp', 'group'), pairs)  16.7 us
    pallas_call x1, Pallas kernels, tail_call(): pl.pallas_call(functools.partial(tail_kernel, [len(w) for w in weights]),...  10.9 us
    ppermute x4, waiting for transfers between devices, step(): moved = [lax.ppermute(self.moving[0], self.axis, self.forward)]  7.21 us
  transfers between devices with their start and end apart: 41, of which 13 were waited for; matrix products, arithmetic and copies ran while one was open for 4% of the time, Pallas kernels for 33%

profile of v3, /device:TPU:0, one launch (start us, length us, event | category | flops | bytes accessed | tf_op | source)
XLA Modules:
  0.0 253.2 jit_solution(597970724067616347)
XLA Ops:
  4.1 3.0 %collective-permute-start = (bf16[128,1024]{1,0:T(8,128)(2,1)}, bf16[128,1024]{1,0:T(8,128)(2,1)}, u32[]{:S(2)}, u32[]{:S(2)}) collective-permute-start(bf16[128,1024]{1,0:T(8,128)(2,1)} %get-tuple-element.202), channel_id=1, source_target_pairs={{0,8},{8,16},{16,24},{24,28},{28,20},{20,12},{12,4},{4,0},{1,9},{9... | collective-permute-start | bytes 786440 | tf_op jit(solution)/shard_map/ppermute | solution.py:510
  7.8 1.9 collective-permute-start.2
  12.7 6.2 %stem_norm.1 = (bf16[6,144,1024]{2,1,0:T(8,128)(2,1)S(1)}, bf16[6,144,1024]{2,1,0:T(8,128)(2,1)}, bf16[6,144,1024]{2,1,0:T(8,128)(2,1)}, bf16[6,144,256]{2,1,0:T(8,128)(2,1)S(1)}) custom-call(s32[6,3]{1,0:T(8,128)S(1)} %copy.53.cnt_ref, s32[6,144,1]{2,1,0:T(8,128)S(1)} %reshape.64.idx_ref, bf16[6,144,640]{2,1,0:T(8,128)(2,1)S(1)} %copy-done.22, ...), custom_call_target="tpu_custom_call" | custom-call | flops 8000000 | bytes 12000 | tf_op jit(solution)/shard_map/stem_norm/pallas_call | solution.py:101
  27.0 6.2 %collective-permute-done.8 = bf16[128,512]{1,0:T(8,128)(2,1)S(1)} collective-permute-done((bf16[128,512]{1,0:T(8,128)(2,1)}, bf16[128,512]{1,0:T(8,128)(2,1)S(1)}, u32[]{:S(2)}, u32[]{:S(2)}) %collective-permute-start.8) | collective-permute-done | bytes 131104 | tf_op jit(solution)/shard_map/ppermute | solution.py:482
  39.2 5.7 %transpose_rows.1 = (bf16[1024,864]{1,0:T(8,128)(2,1)}, bf16[1024,864]{1,0:T(8,128)(2,1)}, bf16[1024,864]{1,0:T(8,128)(2,1)}, bf16[1024,864]{1,0:T(8,128)(2,1)}) custom-call(bf16[864,1024]{1,0:T(8,128)(2,1)S(1)} %bitcast.24, bf16[864,1024]{1,0:T(8,128)(2,1)} %collective-permute-done.6.refs_1_.nb_ref, bf16[864,1024]{1,0:T(8,128)(2,1)S(1)} %bitcast.21, ...), custom_call_target="tpu_custom_call" | custom-call | flops 4000000 | bytes 8000 | tf_op jit(solution)/shard_map/transpose_rows/pallas_call | solution.py:242
  45.3 7.2 %collective-permute-done.11 = bf16[128,1024]{1,0:T(8,128)(2,1)S(1)} collective-permute-done((bf16[128,1024]{1,0:T(8,128)(2,1)S(1)}, bf16[128,1024]{1,0:T(8,128)(2,1)S(1)}, u32[]{:S(2)}, u32[]{:S(2)}) %collective-permute-start.11) | collective-permute-done | bytes 262176 | tf_op jit(solution)/shard_map/ppermute | solution.py:510
  55.8 3.6 %collective-permute-start.14 = (bf16[256,512]{1,0:T(8,128)(2,1)S(1)}, bf16[256,512]{1,0:T(8,128)(2,1)}, u32[]{:S(2)}, u32[]{:S(2)}) collective-permute-start(bf16[256,512]{1,0:T(8,128)(2,1)S(1)} %pad_maximum_fusion.1), channel_id=1, source_target_pairs={{0,16},{4,20},{8,24},{12,28},{16,0},{20,4},{24,8},{28,12},{1,17},{... | collective-permute-start | bytes 786440 | tf_op jit(solution)/shard_map/ppermute | solution.py:482
  62.5 18.9 %attention.2.pack_ref.refs_0_ = bf16[1728,1024]{1,0:T(8,128)(2,1)} custom-call(s32[2,6,3]{2,1,0:T(8,128)S(1)} %pad_add_fusion.cnt_ref, bf16[864,1024]{1,0:T(8,128)(2,1)S(1)} %bitcast.25, bf16[864,1024]{1,0:T(8,128)(2,1)} %collective-permute-done.6.refs_1_.nb_ref, bf16[864,1024]{1,0:T(8,128)(2,1)S(1)} %bitcast.22, ...), custom_call_target="tpu_custom_call" | custom-call | flops 20000000 | bytes 14000 | tf_op jit(solution)/shard_map/attention/pallas_call | solution.py:217
  81.4 8.7 %weight_grad.2 = (bf16[512,1024]{1,0:T(8,128)(2,1)}, f32[512,1024]{1,0:T(8,128)}) custom-call(s32[1]{0:T(128)} %bitcast.2.low_ref, bf16[1024,864]{1,0:T(8,128)(2,1)S(1)} %copy-done.11, bf16[1024,864]{1,0:T(8,128)(2,1)S(1)} %copy-done.13, bf16[1024,864]{1,0:T(8,128)(2,1)} %get-tuple-element.111.ga_ref, bf16[1024,864]{1,0:T(8,128)(2,1)} %get-tuple-element.112.gb_ref, ...), custom_call_target="tpu_custom_call" | custom-call | flops 6000000 | bytes 12000 | tf_op jit(solution)/shard_map/weight_grad/pallas_call | solution.py:275
  96.6 18.6 %attention.3.refs_1_.pack_ref = bf16[1728,1024]{1,0:T(8,128)(2,1)} custom-call(s32[2,6,3]{2,1,0:T(8,128)S(1)} %pad_add_fusion.cnt_ref, bf16[864,1024]{1,0:T(8,128)(2,1)S(1)} %bitcast.26, bf16[864,1024]{1,0:T(8,128)(2,1)} %collective-permute-done.6.refs_1_.nb_ref, bf16[864,1024]{1,0:T(8,128)(2,1)} %bitcast.19, ...), custom_call_target="tpu_custom_call" | custom-call | flops 20000000 | bytes 14000 | tf_op jit(solution)/shard_map/attention/pallas_call | solution.py:217
  115.2 2.3 combine.3
  118.3 6.7 %back.1 = (f32[864,1024]{1,0:T(8,128)}, bf16[864,1024]{1,0:T(8,128)(2,1)}) custom-call(bf16[1728,1024]{1,0:T(8,128)(2,1)} %attention.2.pack_ref.refs_0_, bf16[1728,1024]{1,0:T(8,128)(2,1)} %attention.3.refs_1_.pack_ref, bf16[1024,1024]{1,0:T(8,128)(2,1)S(1)} %copy-done.1, bf16[1024,512]{1,0:T(8,128)(2,1)S(1)} %copy-done.6, ...), custom_call_target="tpu_custom_call" | custom-call | flops 10000000 | bytes 12000 | tf_op jit(solution)/shard_map/back/pallas_call | solution.py:375
  125.9 8.7 %weight_grad.3 = (bf16[512,1024]{1,0:T(8,128)(2,1)}, f32[512,1024]{1,0:T(8,128)}) custom-call(s32[1]{0:T(128)} %bitcast.2.low_ref, bf16[1024,864]{1,0:T(8,128)(2,1)S(1)} %copy-done.12, bf16[1024,864]{1,0:T(8,128)(2,1)S(1)} %copy-done.14, bf16[1024,864]{1,0:T(8,128)(2,1)} %get-tuple-element.111.ga_ref, bf16[1024,864]{1,0:T(8,128)(2,1)} %get-tuple-element.112.gb_ref, ...), custom_call_target="tpu_custom_call" | custom-call | flops 6000000 | bytes 12000 | tf_op jit(solution)/shard_map/weight_grad/pallas_call | solution.py:275
  136.1 3.8 %collective-permute-start.19 = (bf16[128,1024]{1,0:T(8,128)(2,1)}, bf16[128,1024]{1,0:T(8,128)(2,1)}, u32[]{:S(2)}, u32[]{:S(2)}) collective-permute-start(bf16[128,1024]{1,0:T(8,128)(2,1)} %get-tuple-element.141), channel_id=1, source_target_pairs={{0,16},{4,20},{8,24},{12,28},{16,0},{20,4},{24,8},{28,12},{1,17},{... | collective-permute-start | bytes 786440 | tf_op jit(solution)/shard_map/ppermute | solution.py:482
  139.9 17.4 %collective-permute-done.19.refs_2_ = bf16[128,1024]{1,0:T(8,128)(2,1)} collective-permute-done((bf16[128,1024]{1,0:T(8,128)(2,1)}, bf16[128,1024]{1,0:T(8,128)(2,1)}, u32[]{:S(2)}, u32[]{:S(2)}) %collective-permute-start.19) | collective-permute-done | bytes 262176 | tf_op jit(solution)/shard_map/ppermute | solution.py:482
  158.3 10.9 %tail.1 = (f32[320,1024]{1,0:T(8,128)}, f32[320,1024]{1,0:T(8,128)S(1)}) custom-call(s32[1]{0:T(128)} %bitcast.core_ref, f32[864,1024]{1,0:T(8,128)} %collective-permute-done.17.recv_ref, bf16[864,1024]{1,0:T(8,128)(2,1)} %bitcast.27, bf16[864,1024]{1,0:T(8,128)(2,1)} %bitcast.20, bf16[864,256]{1,0:T(8,128)(2,1)S(1)} %bitcast.29, f32[1,1024]{1,0:T(1,128)S(1)} %bitcast.31, ...), custom_call_target="tpu_custom_call" | custom-call | flops 10000000 | bytes 12000 | tf_op jit(solution)/shard_map/tail/pallas_call | solution.py:431
  172.9 6.1 %collective-permute-start.24 = (bf16[128,1024]{1,0:T(8,128)(2,1)}, bf16[128,1024]{1,0:T(8,128)(2,1)S(1)}, u32[]{:S(2)}, u32[]{:S(2)}) collective-permute-start(bf16[128,1024]{1,0:T(8,128)(2,1)} %get-tuple-element.155), channel_id=1, source_target_pairs={{0,8},{4,12},{8,0},{12,4},{16,24},{20,28},{24,16},{28,20},{1,9},{5... | collective-permute-start | bytes 786440 | tf_op jit(solution)/shard_map/ppermute | solution.py:482
  181.6 4.8 %layer_output.1 = bf16[864,1024]{1,0:T(8,128)(2,1)} custom-call(s32[6,3]{1,0:T(8,128)S(1)} %copy.53.cnt_ref, bf16[864,1024]{1,0:T(8,128)(2,1)} %collective-permute-done.21.recv_ref, bf16[864,1024]{1,0:T(8,128)(2,1)S(1)} %bitcast.28, bf16[1728,1024]{1,0:T(8,128)(2,1)} %attention.2.pack_ref.refs_0_, bf16[1728,1024]{1,0:T(8,128)(2,1)} %attention.3.refs_1_.pack_ref, ...), custom_call_target="tpu_custom_call" | custom-call | flops 5000000 | bytes 10000 | tf_op jit(solution)/shard_map/layer_output/pallas_call | solution.py:466
  186.4 5.3 %collective-permute-done.24.refs_1_ = bf16[128,1024]{1,0:T(8,128)(2,1)S(1)} collective-permute-done((bf16[128,1024]{1,0:T(8,128)(2,1)}, bf16[128,1024]{1,0:T(8,128)(2,1)S(1)}, u32[]{:S(2)}, u32[]{:S(2)}) %collective-permute-start.24) | collective-permute-done | bytes 262176 | tf_op jit(solution)/shard_map/ppermute | solution.py:482
  193.2 3.3 %collective-permute-start.26 = (f32[80,1024]{1,0:T(8,128)S(1)}, f32[80,1024]{1,0:T(8,128)S(1)}, u32[]{:S(2)}, u32[]{:S(2)}) collective-permute-start(f32[80,1024]{1,0:T(8,128)S(1)} %get-tuple-element.161), channel_id=1, source_target_pairs={{0,4},{4,0},{8,12},{12,8},{16,20},{20,16},{24,28},{28,24},{1,5},{5... | collective-permute-start | bytes 983048 | tf_op jit(solution)/shard_map/ppermute | solution.py:482
  198.1 3.7 %collective-permute-start.29 = (bf16[128,1024]{1,0:T(8,128)(2,1)S(1)}, bf16[128,1024]{1,0:T(8,128)(2,1)S(1)}, u32[]{:S(2)}, u32[]{:S(2)}) collective-permute-start(bf16[128,1024]{1,0:T(8,128)(2,1)S(1)} %copy-done.33), channel_id=1, source_target_pairs={{0,24},{4,28},{8,16},{12,20},{16,8},{20,12},{24,0},{28,4},{1,25},{... | collective-permute-start | bytes 786440 | tf_op jit(solution)/shard_map/ppermute | solution.py:482
  201.8 5.1 %collective-permute-done.29.refs_3_ = bf16[128,1024]{1,0:T(8,128)(2,1)S(1)} collective-permute-done((bf16[128,1024]{1,0:T(8,128)(2,1)S(1)}, bf16[128,1024]{1,0:T(8,128)(2,1)S(1)}, u32[]{:S(2)}, u32[]{:S(2)}) %collective-permute-start.29) | collective-permute-done | bytes 262176 | tf_op jit(solution)/shard_map/ppermute | solution.py:482
  206.9 4.1 %collective-permute-done.28 = f32[80,1024]{1,0:T(8,128)S(1)} collective-permute-done((f32[80,1024]{1,0:T(8,128)S(1)}, f32[80,1024]{1,0:T(8,128)S(1)}, u32[]{:S(2)}, u32[]{:S(2)}) %collective-permute-start.28) | collective-permute-done | bytes 327712 | tf_op jit(solution)/shard_map/ppermute | solution.py:549
  211.2 2.8 %collective-permute-start.30 = (f32[80,256]{1,0:T(8,128)S(1)}, f32[80,256]{1,0:T(8,128)S(1)}, u32[]{:S(2)}, u32[]{:S(2)}) collective-permute-start(f32[80,256]{1,0:T(8,128)S(1)} %get-tuple-element.196), channel_id=1, source_target_pairs={{0,8},{4,12},{8,0},{12,4},{16,24},{20,28},{24,16},{28,20},{1,9},{5... | collective-permute-start | bytes 245768 | tf_op jit(solution)/shard_map/ppermute | solution.py:482
  213.9 2.3 collective-permute-start.31
  216.7 4.1 %collective-permute-done.31 = f32[80,256]{1,0:T(8,128)S(1)} collective-permute-done((f32[80,256]{1,0:T(8,128)S(1)}, f32[80,256]{1,0:T(8,128)S(1)}, u32[]{:S(2)}, u32[]{:S(2)}) %collective-permute-start.31) | collective-permute-done | bytes 81952 | tf_op jit(solution)/shard_map/ppermute | solution.py:482
  220.9 2.2 collective-permute-done.32
  224.3 3.3 %collective-permute-start.35 = (bf16[80,256]{1,0:T(8,128)(2,1)S(1)}, bf16[80,256]{1,0:T(8,128)(2,1)S(1)}, u32[]{:S(2)}, u32[]{:S(2)}) collective-permute-start(bf16[80,256]{1,0:T(8,128)(2,1)S(1)} %get-tuple-element.193), channel_id=1, source_target_pairs={{0,24},{4,28},{8,16},{12,20},{16,8},{20,12},{24,0},{28,4},{1,25},{... | collective-permute-start | bytes 122888 | tf_op jit(solution)/shard_map/ppermute | solution.py:482
  228.2 1.9 collective-permute-done.35
  233.0 2.3 collective-permute-start.38
  235.5 10.1 %collective-permute-done.37 = bf16[80,1024]{1,0:T(8,128)(2,1)S(1)} collective-permute-done((bf16[80,1024]{1,0:T(8,128)(2,1)S(1)}, bf16[80,1024]{1,0:T(8,128)(2,1)S(1)}, u32[]{:S(2)}, u32[]{:S(2)}) %collective-permute-start.37) | collective-permute-done | bytes 163872 | tf_op jit(solution)/shard_map/ppermute | solution.py:549
  245.5 2.5 %collective-permute-done.38 = bf16[80,1024]{1,0:T(8,128)(2,1)S(1)} collective-permute-done((bf16[80,1024]{1,0:T(8,128)(2,1)S(1)}, bf16[80,1024]{1,0:T(8,128)(2,1)S(1)}, u32[]{:S(2)}, u32[]{:S(2)}) %collective-permute-start.38) | collective-permute-done | bytes 163872 | tf_op jit(solution)/shard_map/ppermute | solution.py:549
  (182 shorter events, 58.0 us)
Async XLA Ops:
  4.1 16.8 %collective-permute-start = (bf16[128,1024]{1,0:T(8,128)(2,1)}, bf16[128,1024]{1,0:T(8,128)(2,1)}, u32[]{:S(2)}, u32[]{:S(2)}) collective-permute-start(bf16[128,1024]{1,0:T(8,128)(2,1)} %get-tuple-element.202), channel_id=1, source_target_pairs={{0,8},{8,16},{16,24},{24,28},{28,20},{20,12},{12,4},{4,0},{1,9},{9... | collective-permute-start | bytes 786440 | tf_op jit(solution)/shard_map/ppermute | solution.py:510
  7.1 13.7 %collective-permute-start.1 = (bf16[128,1024]{1,0:T(8,128)(2,1)}, bf16[128,1024]{1,0:T(8,128)(2,1)}, u32[]{:S(2)}, u32[]{:S(2)}) collective-permute-start(bf16[128,1024]{1,0:T(8,128)(2,1)} %get-tuple-element.202), channel_id=1, source_target_pairs={{8,0},{16,8},{24,16},{28,24},{20,28},{12,20},{4,12},{0,4},{9,1},{1... | collective-permute-start | bytes 786440 | tf_op jit(solution)/shard_map/ppermute | solution.py:512
  7.8 13.1 %collective-permute-start.2 = (bf16[128,512]{1,0:T(8,128)(2,1)}, bf16[128,512]{1,0:T(8,128)(2,1)}, u32[]{:S(2)}, u32[]{:S(2)}) collective-permute-start(bf16[128,512]{1,0:T(8,128)(2,1)} %fusion), channel_id=1, source_target_pairs={{0,2},{1,3},{2,0},{3,1},{4,6},{5,7},{6,4},{7,5},{8,10},{9,11},{10,... | collective-permute-start | bytes 393224 | tf_op jit(solution)/shard_map/ppermute | solution.py:482
  9.7 11.1 %collective-permute-start.3 = (s32[6,3]{0,1:T(4,128)S(1)}, s32[6,3]{0,1:T(4,128)S(1)}, u32[]{:S(2)}, u32[]{:S(2)}) collective-permute-start(s32[6,3]{0,1:T(4,128)S(1)} %copy-done.35), channel_id=1, source_target_pairs={{0,1},{1,0},{2,3},{3,2},{4,5},{5,4},{6,7},{7,6},{8,9},{9,8},{10,11... | collective-permute-start | bytes 224 | tf_op jit(solution)/shard_map/ppermute | solution.py:482
  20.9 12.3 %collective-permute-start.6 = (bf16[864,1024]{1,0:T(8,128)(2,1)}, bf16[864,1024]{1,0:T(8,128)(2,1)}, u32[]{:S(2)}, u32[]{:S(2)}) collective-permute-start(bf16[864,1024]{1,0:T(8,128)(2,1)} %bitcast.23), channel_id=1, source_target_pairs={{0,1},{1,0},{2,3},{3,2},{4,5},{5,4},{6,7},{7,6},{8,9},{9,8},{10,11... | collective-permute-start | bytes 5308424 | tf_op jit(solution)/shard_map/ppermute | solution.py:482
  21.4 11.8 %collective-permute-start.7 = (bf16[864,1024]{1,0:T(8,128)(2,1)}, bf16[864,1024]{1,0:T(8,128)(2,1)}, u32[]{:S(2)}, u32[]{:S(2)}) collective-permute-start(bf16[864,1024]{1,0:T(8,128)(2,1)} %bitcast.18), channel_id=1, source_target_pairs={{0,1},{1,0},{2,3},{3,2},{4,5},{5,4},{6,7},{7,6},{8,9},{9,8},{10,11... | collective-permute-start | bytes 5308424 | tf_op jit(solution)/shard_map/ppermute | solution.py:482
  21.5 11.7 %collective-permute-start.4 = (bf16[128,1024]{1,0:T(8,128)(2,1)}, bf16[128,1024]{1,0:T(8,128)(2,1)S(1)}, u32[]{:S(2)}, u32[]{:S(2)}) collective-permute-start(bf16[128,1024]{1,0:T(8,128)(2,1)} %collective-permute-done), channel_id=1, source_target_pairs={{0,8},{8,16},{16,24},{24,28},{28,20},{20,12},{12,4},{4,0},{1,9},{9... | collective-permute-start | bytes 786440 | tf_op jit(solution)/shard_map/ppermute | solution.py:510
  23.1 10.1 %collective-permute-start.5 = (bf16[128,1024]{1,0:T(8,128)(2,1)}, bf16[128,1024]{1,0:T(8,128)(2,1)S(1)}, u32[]{:S(2)}, u32[]{:S(2)}) collective-permute-start(bf16[128,1024]{1,0:T(8,128)(2,1)} %collective-permute-done.1), channel_id=1, source_target_pairs={{8,0},{16,8},{24,16},{28,24},{20,28},{12,20},{4,12},{0,4},{9,1},{1... | collective-permute-start | bytes 786440 | tf_op jit(solution)/shard_map/ppermute | solution.py:512
  23.5 9.6 %collective-permute-start.8 = (bf16[128,512]{1,0:T(8,128)(2,1)}, bf16[128,512]{1,0:T(8,128)(2,1)S(1)}, u32[]{:S(2)}, u32[]{:S(2)}) collective-permute-start(bf16[128,512]{1,0:T(8,128)(2,1)} %collective-permute-done.2), channel_id=1, source_target_pairs={{0,4},{4,0},{8,12},{12,8},{16,20},{20,16},{24,28},{28,24},{1,5},{5... | collective-permute-start | bytes 393224 | tf_op jit(solution)/shard_map/ppermute | solution.py:482
  33.2 11.8 %collective-permute-start.10 = (bf16[128,1024]{1,0:T(8,128)(2,1)S(1)}, bf16[128,1024]{1,0:T(8,128)(2,1)S(1)}, u32[]{:S(2)}, u32[]{:S(2)}) collective-permute-start(bf16[128,1024]{1,0:T(8,128)(2,1)S(1)} %collective-permute-done.5), channel_id=1, source_target_pairs={{8,0},{16,8},{24,16},{28,24},{20,28},{12,20},{4,12},{0,4},{9,1},{1... | collective-permute-start | bytes 786440 | tf_op jit(solution)/shard_map/ppermute | solution.py:512
  35.0 10.0 %collective-permute-start.9 = (bf16[128,1024]{1,0:T(8,128)(2,1)S(1)}, bf16[128,1024]{1,0:T(8,128)(2,1)S(1)}, u32[]{:S(2)}, u32[]{:S(2)}) collective-permute-start(bf16[128,1024]{1,0:T(8,128)(2,1)S(1)} %collective-permute-done.4), channel_id=1, source_target_pairs={{0,8},{8,16},{16,24},{24,28},{28,20},{20,12},{12,4},{4,0},{1,9},{9... | collective-permute-start | bytes 786440 | tf_op jit(solution)/shard_map/ppermute | solution.py:510
  53.8 36.4 %collective-permute-start.12 = (bf16[1024,512]{1,0:T(8,128)(2,1)}, bf16[1024,512]{1,0:T(8,128)(2,1)S(1)}, u32[]{:S(2)}, u32[]{:S(2)}) collective-permute-start(bf16[1024,512]{1,0:T(8,128)(2,1)} %slice.13), channel_id=1, source_target_pairs={{0,2},{1,3},{2,0},{3,1},{4,6},{5,7},{6,4},{7,5},{8,10},{9,11},{10,... | collective-permute-start | bytes 3145736 | tf_op jit(solution)/shard_map/ppermute | solution.py:482
  54.2 35.9 %collective-permute-start.13 = (bf16[256,512]{1,0:T(8,128)(2,1)S(1)}, bf16[256,512]{1,0:T(8,128)(2,1)}, u32[]{:S(2)}, u32[]{:S(2)}) collective-permute-start(bf16[256,512]{1,0:T(8,128)(2,1)S(1)} %pad_maximum_fusion.1), channel_id=1, source_target_pairs={{0,8},{4,12},{8,0},{12,4},{16,24},{20,28},{24,16},{28,20},{1,9},{5... | collective-permute-start | bytes 786440 | tf_op jit(solution)/shard_map/ppermute | solution.py:482
  55.8 34.4 %collective-permute-start.14 = (bf16[256,512]{1,0:T(8,128)(2,1)S(1)}, bf16[256,512]{1,0:T(8,128)(2,1)}, u32[]{:S(2)}, u32[]{:S(2)}) collective-permute-start(bf16[256,512]{1,0:T(8,128)(2,1)S(1)} %pad_maximum_fusion.1), channel_id=1, source_target_pairs={{0,16},{4,20},{8,24},{12,28},{16,0},{20,4},{24,8},{28,12},{1,17},{... | collective-permute-start | bytes 786440 | tf_op jit(solution)/shard_map/ppermute | solution.py:482
  59.4 30.8 %collective-permute-start.15 = (bf16[256,512]{1,0:T(8,128)(2,1)S(1)}, bf16[256,512]{1,0:T(8,128)(2,1)}, u32[]{:S(2)}, u32[]{:S(2)}) collective-permute-start(bf16[256,512]{1,0:T(8,128)(2,1)S(1)} %pad_maximum_fusion.1), channel_id=1, source_target_pairs={{0,24},{4,28},{8,16},{12,20},{16,8},{20,12},{24,0},{28,4},{1,25},{... | collective-permute-start | bytes 786440 | tf_op jit(solution)/shard_map/ppermute | solution.py:482
  91.2 24.0 %collective-permute-start.16 = (bf16[512,1024]{1,0:T(8,128)(2,1)}, bf16[512,1024]{1,0:T(8,128)(2,1)}, u32[]{:S(2)}, u32[]{:S(2)}) collective-permute-start(bf16[512,1024]{1,0:T(8,128)(2,1)} %get-tuple-element.126), channel_id=1, source_target_pairs={{0,4},{4,0},{8,12},{12,8},{16,20},{20,16},{24,28},{28,24},{1,5},{5... | collective-permute-start | bytes 3145736 | tf_op jit(solution)/shard_map/ppermute | solution.py:482
  125.1 32.2 %collective-permute-start.17 = (f32[864,1024]{1,0:T(8,128)}, f32[864,1024]{1,0:T(8,128)}, u32[]{:S(2)}, u32[]{:S(2)}) collective-permute-start(f32[864,1024]{1,0:T(8,128)} %get-tuple-element.135), channel_id=1, source_target_pairs={{0,1},{1,0},{2,3},{3,2},{4,5},{5,4},{6,7},{7,6},{8,9},{9,8},{10,11... | collective-permute-start | bytes 10616840 | tf_op jit(solution)/shard_map/ppermute | solution.py:482
  125.1 45.3 %collective-permute-start.21 = (bf16[864,1024]{1,0:T(8,128)(2,1)}, bf16[864,1024]{1,0:T(8,128)(2,1)}, u32[]{:S(2)}, u32[]{:S(2)}) collective-permute-start(bf16[864,1024]{1,0:T(8,128)(2,1)} %get-tuple-element.148), channel_id=1, source_target_pairs={{0,1},{1,0},{2,3},{3,2},{4,5},{5,4},{6,7},{7,6},{8,9},{9,8},{10,11... | collective-permute-start | bytes 5308424 | tf_op jit(solution)/shard_map/ppermute | solution.py:482
  125.6 9.1 %collective-permute-start.18 = (bf16[128,1024]{1,0:T(8,128)(2,1)S(1)}, bf16[128,1024]{1,0:T(8,128)(2,1)S(1)}, u32[]{:S(2)}, u32[]{:S(2)}) collective-permute-start(bf16[128,1024]{1,0:T(8,128)(2,1)S(1)} %get-tuple-element.139), channel_id=1, source_target_pairs={{0,8},{4,12},{8,0},{12,4},{16,24},{20,28},{24,16},{28,20},{1,9},{5... | collective-permute-start | bytes 786440 | tf_op jit(solution)/shard_map/ppermute | solution.py:482
  134.6 35.8 %collective-permute-start.22 = (bf16[512,1024]{1,0:T(8,128)(2,1)}, bf16[512,1024]{1,0:T(8,128)(2,1)S(1)}, u32[]{:S(2)}, u32[]{:S(2)}) collective-permute-start(bf16[512,1024]{1,0:T(8,128)(2,1)} %get-tuple-element.149), channel_id=1, source_target_pairs={{0,4},{4,0},{8,12},{12,8},{16,20},{20,16},{24,28},{28,24},{1,5},{5... | collective-permute-start | bytes 3145736 | tf_op jit(solution)/shard_map/ppermute | solution.py:482
  136.1 21.2 %collective-permute-start.19 = (bf16[128,1024]{1,0:T(8,128)(2,1)}, bf16[128,1024]{1,0:T(8,128)(2,1)}, u32[]{:S(2)}, u32[]{:S(2)}) collective-permute-start(bf16[128,1024]{1,0:T(8,128)(2,1)} %get-tuple-element.141), channel_id=1, source_target_pairs={{0,16},{4,20},{8,24},{12,28},{16,0},{20,4},{24,8},{28,12},{1,17},{... | collective-permute-start | bytes 786440 | tf_op jit(solution)/shard_map/ppermute | solution.py:482
  139.9 17.4 %collective-permute-start.20 = (bf16[128,1024]{1,0:T(8,128)(2,1)}, bf16[128,1024]{1,0:T(8,128)(2,1)}, u32[]{:S(2)}, u32[]{:S(2)}) collective-permute-start(bf16[128,1024]{1,0:T(8,128)(2,1)} %get-tuple-element.142), channel_id=1, source_target_pairs={{0,24},{4,28},{8,16},{12,20},{16,8},{20,12},{24,0},{28,4},{1,25},{... | collective-permute-start | bytes 786440 | tf_op jit(solution)/shard_map/ppermute | solution.py:482
  170.4 21.4 %collective-permute-start.23 = (f32[320,1024]{1,0:T(8,128)}, f32[320,1024]{1,0:T(8,128)}, u32[]{:S(2)}, u32[]{:S(2)}) collective-permute-start(f32[320,1024]{1,0:T(8,128)} %get-tuple-element.151), channel_id=1, source_target_pairs={{0,1},{1,0},{2,3},{3,2},{4,5},{5,4},{6,7},{7,6},{8,9},{9,8},{10,11... | collective-permute-start | bytes 3932168 | tf_op jit(solution)/shard_map/ppermute | solution.py:482
  172.9 18.9 %collective-permute-start.24 = (bf16[128,1024]{1,0:T(8,128)(2,1)}, bf16[128,1024]{1,0:T(8,128)(2,1)S(1)}, u32[]{:S(2)}, u32[]{:S(2)}) collective-permute-start(bf16[128,1024]{1,0:T(8,128)(2,1)} %get-tuple-element.155), channel_id=1, source_target_pairs={{0,8},{4,12},{8,0},{12,4},{16,24},{20,28},{24,16},{28,20},{1,9},{5... | collective-permute-start | bytes 786440 | tf_op jit(solution)/shard_map/ppermute | solution.py:482
  179.0 12.8 %collective-permute-start.25 = (bf16[128,1024]{1,0:T(8,128)(2,1)}, bf16[128,1024]{1,0:T(8,128)(2,1)S(1)}, u32[]{:S(2)}, u32[]{:S(2)}) collective-permute-start(bf16[128,1024]{1,0:T(8,128)(2,1)} %get-tuple-element.156), channel_id=1, source_target_pairs={{0,16},{4,20},{8,24},{12,28},{16,0},{20,4},{24,8},{28,12},{1,17},{... | collective-permute-start | bytes 786440 | tf_op jit(solution)/shard_map/ppermute | solution.py:482
  193.2 13.7 %collective-permute-start.26 = (f32[80,1024]{1,0:T(8,128)S(1)}, f32[80,1024]{1,0:T(8,128)S(1)}, u32[]{:S(2)}, u32[]{:S(2)}) collective-permute-start(f32[80,1024]{1,0:T(8,128)S(1)} %get-tuple-element.161), channel_id=1, source_target_pairs={{0,4},{4,0},{8,12},{12,8},{16,20},{20,16},{24,28},{28,24},{1,5},{5... | collective-permute-start | bytes 983048 | tf_op jit(solution)/shard_map/ppermute | solution.py:482
  196.5 10.4 %collective-permute-start.27 = (f32[80,1024]{1,0:T(8,128)S(1)}, f32[80,1024]{1,0:T(8,128)S(1)}, u32[]{:S(2)}, u32[]{:S(2)}) collective-permute-start(f32[80,1024]{1,0:T(8,128)S(1)} %get-tuple-element.162), channel_id=1, source_target_pairs={{0,2},{1,3},{2,0},{3,1},{4,6},{5,7},{6,4},{7,5},{8,10},{9,11},{10,... | collective-permute-start | bytes 983048 | tf_op jit(solution)/shard_map/ppermute | solution.py:549
  197.9 13.1 %collective-permute-start.28 = (f32[80,1024]{1,0:T(8,128)S(1)}, f32[80,1024]{1,0:T(8,128)S(1)}, u32[]{:S(2)}, u32[]{:S(2)}) collective-permute-start(f32[80,1024]{1,0:T(8,128)S(1)} %get-tuple-element.163), channel_id=1, source_target_pairs={{0,6},{1,7},{2,4},{3,5},{4,2},{5,3},{6,0},{7,1},{8,14},{9,15},{10,... | collective-permute-start | bytes 983048 | tf_op jit(solution)/shard_map/ppermute | solution.py:549
  198.1 8.8 %collective-permute-start.29 = (bf16[128,1024]{1,0:T(8,128)(2,1)S(1)}, bf16[128,1024]{1,0:T(8,128)(2,1)S(1)}, u32[]{:S(2)}, u32[]{:S(2)}) collective-permute-start(bf16[128,1024]{1,0:T(8,128)(2,1)S(1)} %copy-done.33), channel_id=1, source_target_pairs={{0,24},{4,28},{8,16},{12,20},{16,8},{20,12},{24,0},{28,4},{1,25},{... | collective-permute-start | bytes 786440 | tf_op jit(solution)/shard_map/ppermute | solution.py:482
  230.9 18.5 %collective-permute-start.40 = (f32[128,1024]{1,0:T(8,128)S(1)}, f32[128,1024]{1,0:T(8,128)S(1)}, u32[]{:S(2)}, u32[]{:S(2)}) collective-permute-start(f32[128,1024]{1,0:T(8,128)S(1)} %add_parts.3), channel_id=1, source_target_pairs={{0,2},{1,3},{2,0},{3,1},{4,6},{5,7},{6,4},{7,5},{8,10},{9,11},{10,... | collective-permute-start | bytes 1572872 | tf_op jit(solution)/shard_map/ppermute | solution.py:482
  232.4 13.1 %collective-permute-start.37 = (bf16[80,1024]{1,0:T(8,128)(2,1)S(1)}, bf16[80,1024]{1,0:T(8,128)(2,1)S(1)}, u32[]{:S(2)}, u32[]{:S(2)}) collective-permute-start(bf16[80,1024]{1,0:T(8,128)(2,1)S(1)} %constant_dynamic-update-slice_fusion.4), channel_id=1, source_target_pairs={{0,2},{1,3},{2,0},{3,1},{4,6},{5,7},{6,4},{7,5},{8,10},{9,11},{10,... | collective-permute-start | bytes 491528 | tf_op jit(solution)/shard_map/ppermute | solution.py:549
  233.0 15.1 %collective-permute-start.38 = (bf16[80,1024]{1,0:T(8,128)(2,1)S(1)}, bf16[80,1024]{1,0:T(8,128)(2,1)S(1)}, u32[]{:S(2)}, u32[]{:S(2)}) collective-permute-start(bf16[80,1024]{1,0:T(8,128)(2,1)S(1)} %constant_dynamic-update-slice_fusion.4), channel_id=1, source_target_pairs={{0,6},{1,7},{2,4},{3,5},{4,2},{5,3},{6,0},{7,1},{8,14},{9,15},{10,... | collective-permute-start | bytes 491528 | tf_op jit(solution)/shard_map/ppermute | solution.py:549
  (45 other events, 329.9 us)

commit v4 on v3

--- a/solution.py
+++ b/solution.py
@@ -21,7 +21,7 @@
 NORM_EPS = 1e-06
 F32 = jnp.float32
 BF16 = jnp.bfloat16
-VMEM_LIMIT = 48 * 1024 * 1024
+VMEM_LIMIT = 60 * 1024 * 1024
 
 
 def dot_nn(a, b):
@@ -120,13 +120,19 @@
 
 
 def attention_kernel(
-    deps, cnt_ref, na_ref, nb_ref, ga_ref, gb_ref, wq_ref, wk_ref, wv_ref, wo_ref, *refs
+    cnt_ref, owner_ref, na_ref, nb_ref, ga_ref, gb_ref, *refs
 ):
-    out_ref, n_s, g_s, qkv = refs[deps:]
+    blocks, (out_ref, w_ref, n_s, g_s, qkv) = refs[:-5], refs[-5:]
     half, step = pl.program_id(0), pl.program_id(1)
     rows = n_s.shape[0]
     scenes = rows // TOK
-    width = wq_ref.shape[1]
+    width = w_ref.shape[1] // 4
+
+    @pl.when((half == 0) & (step == 0))
+    def _():
+        size = blocks[0].shape[0]
+        for b, block in enumerate(blocks):
+            w_ref[pl.ds(pl.multiple_of(owner_ref[b] * size, size), size), :] = block[...]
 
     @pl.when(half == 0)
     def _():
@@ -138,9 +144,8 @@
         n_s[...] = nb_ref[...]
         g_s[...] = gb_ref[...]
 
-    into = jnp.concatenate([wq_ref[...], wk_ref[...], wv_ref[...]], axis=1)
-    qkv[:, : 3 * width] = dot_nn(n_s[...], into).astype(BF16)
-    qkv[:, 3 * width :] = dot_nn(g_s[...], wo_ref[...]).astype(BF16)
+    qkv[:, : 3 * width] = dot_nn(n_s[...], w_ref[:, : 3 * width]).astype(BF16)
+    qkv[:, 3 * width :] = dot_nn(g_s[...], w_ref[:, 3 * width :]).astype(BF16)
     heads = width // HD
     lane = lax.broadcasted_iota(jnp.int32, (1, width), 1)
     masks = [(lane // HD == h).astype(F32).astype(BF16) for h in range(heads)]
@@ -185,7 +190,7 @@
         out_ref[at, 3 * width :] = own_lanes(dot_tn(half_probs, v)).astype(BF16)
         return 0
 
-    lax.fori_loop(0, scenes, scene_body, 0)
+    lax.fori_loop(0, scenes, scene_body, 0, unroll=True)
 
 
 def block_rows(tokens):
@@ -202,33 +207,33 @@
 SCALARS = pl.BlockSpec(memory_space=pltpu.SMEM)
 
 
-def section(weights, c):
-    each = 4 // len(weights)
-    return weights[c // each], c % each
-
-
-def attention_call(counts, na, nb, ga, gb, weights, deps=()):
+def attention_call(counts, owners, na, nb, ga, gb, blocks):
     tokens = na.shape[0]
     rows = block_rows(tokens)
     steps = tokens // rows
-    sections = [section(weights, c) for c in range(4)]
-    width = weights[0].shape[1] * len(weights) // 4
-    weight = lambda at: pl.BlockSpec((D, width), lambda h, i: (0, at))
-    return pl.pallas_call(
-        functools.partial(attention_kernel, len(deps)),
+    cols = blocks[0].shape[1]
+    whole = lambda a: pl.BlockSpec(a.shape, lambda h, i: (0, 0))
+    return pl.pallas_call(
+        attention_kernel,
         grid=(2, steps),
-        in_specs=[SCALARS] + two_halves(rows, steps) + [weight(at) for _, at in sections] + [ANYWHERE] * len(deps),
-        out_specs=pl.BlockSpec((rows, 4 * width), lambda h, i: (h * steps + i, 0)),
-        out_shape=jax.ShapeDtypeStruct((2 * tokens, 4 * width), BF16),
+        in_specs=[SCALARS, SCALARS] + two_halves(rows, steps) + [whole(b) for b in blocks],
+        out_specs=[
+            pl.BlockSpec((rows, cols), lambda h, i: (h * steps + i, 0)),
+            pl.BlockSpec((D, cols), lambda h, i: (0, 0)),
+        ],
+        out_shape=[
+            jax.ShapeDtypeStruct((2 * tokens, cols), BF16),
+            jax.ShapeDtypeStruct((D, cols), BF16),
+        ],
         scratch_shapes=[
             pltpu.VMEM((rows, D), BF16),
             pltpu.VMEM((rows, D), BF16),
-            pltpu.VMEM((rows, 4 * width), BF16),
+            pltpu.VMEM((rows, cols), BF16),
         ],
         compiler_params=params(),
         cost_estimate=cost(20e9, 14e6),
         name="attention",
-    )(counts, na, nb, ga, gb, *[a for a, _ in sections], *deps)
+    )(counts, owners, na, nb, ga, gb, *blocks)
 
 
 def transpose_kernel(*refs):
@@ -335,33 +340,22 @@
     )(*parts, *deps)
 
 
-def split_weights(counts, refs):
-    out = []
-    for count in counts:
-        out.append(refs[:count])
-        refs = refs[count:]
-    return out, refs
-
-
 def back_product(pack_refs, weight_refs, start, first, count):
     total = None
-    for pack_ref, refs in zip(pack_refs, weight_refs):
-        width = refs[0].shape[1] * len(refs) // 4
-        for c in range(first, first + count):
-            ref, at = section(refs, c)
-            columns = pack_ref[:, (c - start) * width : (c - start + 1) * width]
-            new = dot_nt(columns, ref[:, at * width : (at + 1) * width])
-            total = new if total is None else total + new
+    for pack_ref, w_ref in zip(pack_refs, weight_refs):
+        width = w_ref.shape[1] // 4
+        columns = pack_ref[:, (first - start) * width : (first - start + count) * width]
+        new = dot_nt(columns, w_ref[:, first * width : (first + count) * width])
+        total = new if total is None else total + new
     return total
 
 
 def weight_specs(weights):
-    return [pl.BlockSpec(w.shape, lambda i: (0, 0)) for block in weights for w in block]
-
-
-def back_kernel(counts, *refs):
-    packs = refs[: len(counts)]
-    weights, refs = split_weights(counts, refs[len(counts) :])
+    return [pl.BlockSpec(w.shape, lambda i: (0, 0)) for w in weights]
+
+
+def back_kernel(count, *refs):
+    packs, weights = refs[:count], refs[count : 2 * count]
     grad_ref, mixed_ref = refs[-2:]
     grad_ref[...] = back_product(packs, weights, 0, 0, 3)
     mixed_ref[...] = back_product(packs, weights, 0, 3, 1).astype(BF16)
@@ -373,7 +367,7 @@
     steps = tokens // rows
     out = pl.BlockSpec((rows, D), lambda i: (i, 0))
     return pl.pallas_call(
-        functools.partial(back_kernel, [len(w) for w in weights]),
+        functools.partial(back_kernel, len(packs)),
         grid=(steps,),
         in_specs=[pl.BlockSpec((rows, p.shape[1]), lambda i: (half * steps + i, 0)) for p in packs]
         + weight_specs(weights)
@@ -383,12 +377,11 @@
         compiler_params=params(),
         cost_estimate=cost(10e9, 12e6),
         name="back",
-    )(*packs, *[w for block in weights for w in block], *deps)
-
-
-def tail_kernel(counts, core_ref, recv_ref, emb_ref, gl_ref, cols_ref, gain_ref, *refs):
-    packs = refs[: len(counts)]
-    weights, refs = split_weights(counts, refs[len(counts) :])
+    )(*packs, *weights, *deps)
+
+
+def tail_kernel(count, core_ref, recv_ref, emb_ref, gl_ref, cols_ref, gain_ref, *refs):
+    packs, weights = refs[:count], refs[count : 2 * count]
     send_ref, keep_ref, acc = refs[-3:]
     step = pl.program_id(0)
     rows = emb_ref.shape[0]
@@ -429,7 +422,7 @@
     stem_rows = GROUP_BANDS[-1][1] * PIX
     half = jax.ShapeDtypeStruct((stem_rows // 2, D), F32)
     return pl.pallas_call(
-        functools.partial(tail_kernel, [len(w) for w in weights]),
+        functools.partial(tail_kernel, len(packs)),
         grid=(tokens // rows,),
         in_specs=[SCALARS, per(recv), per(emb), per(gl), per(cols)]
         + [pl.BlockSpec(gain.shape, lambda i: (0, 0))]
@@ -442,12 +435,11 @@
         compiler_params=params(),
         cost_estimate=cost(10e9, 12e6),
         name="tail",
-    )(core, recv, emb, gl, cols, gain, *packs, *[w for block in weights for w in block], *deps)
-
-
-def output_kernel(counts, cnt_ref, recv_ref, emb_ref, *refs):
-    packs, out_ref = refs[: len(counts)], refs[-1]
-    weights, _ = split_weights(counts, refs[len(counts) :])
+    )(core, recv, emb, gl, cols, gain, *packs, *weights, *deps)
+
+
+def output_kernel(count, cnt_ref, recv_ref, emb_ref, *refs):
+    packs, weights, out_ref = refs[:count], refs[count : 2 * count], refs[-1]
     step = pl.program_id(0)
     scenes = emb_ref.shape[0] // TOK
     mixed = recv_ref[...].astype(F32) + back_product(packs, weights, 3, 3, 1)
@@ -464,7 +456,7 @@
     rows = block_rows(tokens)
     per = lambda a: pl.BlockSpec((rows, a.shape[1]), lambda i: (i, 0))
     return pl.pallas_call(
-        functools.partial(output_kernel, [len(w) for w in weights]),
+        functools.partial(output_kernel, len(packs)),
         grid=(tokens // rows,),
         in_specs=[SCALARS, per(recv), per(emb)]
         + [pl.BlockSpec((rows, p.shape[1] // 4), lambda i: (i, 3)) for p in packs]
@@ -475,7 +467,7 @@
         compiler_params=params(),
         cost_estimate=cost(5e9, 10e6),
         name="layer_output",
-    )(counts, recv, emb, *packs, *[w for block in weights for w in block], *deps)
+    )(counts, recv, emb, *packs, *weights, *deps)
 
 
 def swap(x, axis, size, bit):
@@ -488,42 +480,30 @@
 
 class Ring:
     def __init__(self, x, axis, size):
-        self.axis, self.size, self.rows = axis, size, x.shape[0]
+        self.axis, self.size = axis, size
         order = list(range(0, size, 2)) + list(range(size - 1, 0, -2))
         self.forward = [(order[i], order[(i + 1) % size]) for i in range(size)]
         self.backward = [(order[(i + 1) % size], order[i]) for i in range(size)]
-        me = lax.axis_index(axis)
-        self.here = jnp.where(me % 2 == 0, me // 2, size - 1 - me // 2)
-        self.moving = [x, x]
-        self.full = jnp.zeros((size * self.rows,) + x.shape[1:], x.dtype)
-        self.steps = 0
-        self.put(x, 0)
-
-    def put(self, block, distance):
+        self.ahead, self.behind = [x], [x]
+
+    def step(self, *beside):
+        ahead = lax.ppermute(self.ahead[-1], self.axis, self.forward)
+        if len(self.behind) <= (self.size - 1) // 2:
+            behind = lax.ppermute(self.behind[-1], self.axis, self.backward)
+            ahead, behind, beside = together(ahead, behind, beside)
+            self.behind.append(behind)
+        else:
+            ahead, beside = together(ahead, beside)
+        self.ahead.append(ahead)
+        return beside
+
+    def owners(self):
         size = self.size
-        at = (self.here + distance + size) % size
-        owner = jnp.where(at < size // 2, 2 * at, 2 * (size - 1 - at) + 1)
-        self.full = lax.dynamic_update_slice_in_dim(self.full, block, owner * self.rows, 0)
-
-    def step(self, *beside):
-        self.steps += 1
-        moved = [lax.ppermute(self.moving[0], self.axis, self.forward)]
-        if self.steps <= (self.size - 1) // 2:
-            moved.append(lax.ppermute(self.moving[1], self.axis, self.backward))
-        moved, beside = together(moved, beside)
-        self.moving = moved
-        self.put(moved[0], -self.steps)
-        if len(moved) > 1:
-            self.put(moved[1], self.steps)
-        return beside
-
-
-def line_up(pair, arrived, high):
-    rows = pair.shape[0]
-    full = jnp.zeros(((len(arrived) + 1) * rows,) + pair.shape[1:], pair.dtype)
-    for j, block in enumerate([pair] + list(arrived)):
-        full = lax.dynamic_update_slice_in_dim(full, block, (high ^ j) * rows, 0)
-    return full
+        me = lax.axis_index(self.axis)
+        here = jnp.where(me % 2 == 0, me // 2, size - 1 - me // 2)
+        distances = [-s for s in range(len(self.ahead))] + list(range(1, len(self.behind)))
+        at = (here + size + jnp.array(distances, jnp.int32)) % size
+        return jnp.where(at < size // 2, 2 * at, 2 * (size - 1 - at) + 1)
 
 
 def halve_stem(recv, keep, group):
@@ -550,22 +530,27 @@
         return swap(block, "dp", dp, b)
 
     hops = [(k // 2, k % 2) for k in range(1, 2 * fars)]
-    arrived, beside = together([hop(part, f, b) for part, (f, b) in zip(parts[1:], hops)], beside)
+    arrived = [hop(part, f, b) for part, (f, b) in zip(parts[1:], hops)]
+    beside = beside()
+    arrived, beside[:2] = together(arrived, beside[:2])
+    near = (len(beside) + 2) // 2
     total = parts[0]
     for part in arrived:
         total = total + part
     cols = width // highs
     part = lax.dynamic_slice_in_dim(total, high * cols, cols, 1)
-    for j in range(1, highs):
-        away = lax.dynamic_slice_in_dim(total, (high ^ j) * cols, cols, 1)
-        part = part + swap(away, "dp", dp, 2 * j)
+    away = [lax.dynamic_slice_in_dim(total, (high ^ j) * cols, cols, 1) for j in range(1, highs)]
+    arrived = [swap(a, "dp", dp, 2 * (j + 1)) for j, a in enumerate(away)]
+    arrived, beside[:near] = together(arrived, beside[:near])
+    for block in arrived:
+        part = part + block
     part = part.astype(BF16)
     line = jnp.zeros((small, width), BF16)
     line = lax.dynamic_update_slice_in_dim(line, part, high * cols, 1)
-    for j in range(1, highs):
-        line = lax.dynamic_update_slice_in_dim(
-            line, swap(part, "dp", dp, 2 * j), (high ^ j) * cols, 1
-        )
+    arrived = [swap(part, "dp", dp, 2 * j) for j in range(1, highs)]
+    arrived, beside = together(arrived, beside)
+    for j, block in enumerate(arrived):
+        line = lax.dynamic_update_slice_in_dim(line, block, (high ^ (j + 1)) * cols, 1)
     block = jnp.zeros((rows, width), BF16)
     block = lax.dynamic_update_slice_in_dim(block, line, mine * small, 0)
     for f, b in hops:
@@ -605,7 +590,8 @@
 
     shard = jnp.concatenate([w_qkv.reshape(w_qkv.shape[0], 3 * width), w_out.T], axis=1)
     ring = Ring(shard, "dp", dp)
-    far_shards = [swap(shard[:, 2 * width :], "group", group, 2 * f) for f in fars]
+    cross = lambda x: [swap(x, "group", group, 2 * f) for f in fars]
+    far = [cross(shard)]
     counts = vis_count.astype(jnp.int32)
     counts_far = swap(counts, "group", group, 1)
     table, genc = encoding_tables(patches.shape[1])
@@ -620,25 +606,22 @@
         jnp.asarray(genc),
         out_grad.reshape(scenes, TOK, D),
     )
-    stem, far_shards, counts_far = ring.step(stem, far_shards, counts_far)
+    stem, counts_far = ring.step(stem, counts_far)
     emb, normed, gl = [a.reshape(tokens, D) for a in stem[:3]]
     cols = stem[3].reshape(tokens, stem[3].shape[2])
     both_counts = jnp.stack([counts, counts_far])
     both = [normed, swap(normed, "group", group, 1), gl, swap(gl, "group", group, 1)]
-    partners = [swap(x, "dp", dp, 1) for x in far_shards]
-    both, partners = ring.step(both, partners)
-    (turned,) = ring.step(transpose_call(both))
-    while ring.steps < dp // 2:
-        ring.step()
-    own = ring.full
-    pairs = [
-        jnp.concatenate([jnp.where(dp_low == 0, x, y), jnp.where(dp_low == 0, y, x)], axis=0)
-        for x, y in zip(far_shards, partners)
-    ]
-    own, pairs = together(own, pairs)
-    weights = [[own]]
-    far_own = [swap(own[:, : 2 * width], "group", group, 2 * f) for f in fars]
-    far_rest = [[swap(pair, "dp", dp, 2 * j) for j in rests] for pair in pairs]
+    far.append(cross(ring.ahead[-1]))
+    both, far[0] = ring.step(both, far[0])
+    while len(ring.ahead) < dp // 2:
+        far.append(cross(ring.ahead[-1]))
+        (far[-2],) = ring.step(far[-2])
+    far.append(cross(ring.ahead[-1]))
+    turned, far[-2:] = ring.step(transpose_call(both), far[-2:])
+    far.append(cross(ring.ahead[-1]))
+    behind = ring.behind[1:]
+    far.append(cross(jnp.concatenate(behind, axis=0)))
+    owners = ring.owners()
 
     packs, kept, coming, landing = [], [], [], []
 
@@ -648,40 +631,50 @@
     def rest_swaps(blocks):
         return [blocks[0]] + [swap(blocks[j], "dp", dp, 2 * j) for j in rests]
 
-    packs.extend(together(attention_call(both_counts, *both, weights[0])))
-    for n in fars:
-        send, keep = weight_grad_call(low, *turned, packs[-1], dp)
-        if n == 1:
-            send, keep, far_own, far_rest = together(send, keep, far_own, far_rest)
-            for f in fars:
-                weights.append([far_own[f - 1], line_up(pairs[f - 1], far_rest[f - 1], dp_high)])
+    weights = []
+    for n in range(group // 2):
+        if n == 0:
+            blocks = ring.ahead + behind
+        else:
+            rows = shard.shape[0]
+            last = [far[-1][n - 1][b * rows : (b + 1) * rows] for b in range(len(behind))]
+            blocks = [f[n - 1] for f in far[:-1]] + last
+        made = attention_call(both_counts, owners, *both, blocks)
+        if n == 0:
+            pack, weight = together(*made)
+        else:
+            pack, weight, coming[-1] = together(*made, coming[-1])
+        packs.append(pack)
+        weights.append(weight)
+        if n == len(fars):
+            break
+        send, keep = weight_grad_call(low, *turned, pack, dp)
+        if n == 0:
+            send, keep, far[-2:] = together(send, keep, far[-2:])
         else:
             send, keep = together(send, keep)
         kept.append(keep)
         coming.append(swap(send, "dp", dp, 1))
-        pack, coming[-1] = together(attention_call(both_counts, *both, weights[n]), coming[-1])
-        packs.append(pack)
-        blocks, packs = together(first_to_rest(n - 1), packs)
-        landing.append(rest_swaps(blocks))
     back, mixed = together(*back_call(packs, weights, 1))
     back = swap(back, "group", group, 1)
     mixed = swap(mixed, "group", group, 1)
+    near = dp // 2 * 3 // 4
+    for n in range(len(fars)):
+        landing.append(rest_swaps(first_to_rest(n)))
     send, keep = weight_grad_call(low, *turned, packs[-1], dp)
-    send, keep, landing[-1][1] = together(send, keep, landing[-1][1])
+    send, keep, back, landing[-1][:near] = together(send, keep, back, landing[-1][:near])
     kept.append(keep)
     coming.append(swap(send, "dp", dp, 1))
-    back, landing = together(back, landing)
-    stem_send, stem_keep, mixed, coming[-1] = together(
-        *tail_call(core, back, emb, gl, cols, gain, packs, weights), mixed, coming[-1]
+    stem_send, stem_keep, mixed, landing = together(
+        *tail_call(core, back, emb, gl, cols, gain, packs, weights), mixed, landing
     )
-    stem_recv = swap(stem_send, "group", group, 1)
-    last = rest_swaps(first_to_rest(-1))
-    near = dp // 2 * 3 // 4
-    output, stem_recv, last[:near] = together(
-        output_call(counts, mixed, emb, packs, weights), stem_recv, last[:near]
+    cols = stem_send.shape[1] // 2
+    stem_recv = [swap(stem_send[:, c * cols : (c + 1) * cols], "group", group, 1) for c in range(2)]
+    output, stem_recv, coming[-1] = together(
+        output_call(counts, mixed, emb, packs, weights), stem_recv, coming[-1]
     )
-    stem_parts = halve_stem(stem_recv, stem_keep, group)
-    grad_w_stem, last[near:] = sum_stem(stem_parts, last[near:], dp, group)
+    stem_parts = halve_stem(jnp.concatenate(stem_recv, axis=1), stem_keep, group)
+    grad_w_stem, last = sum_stem(stem_parts, lambda: rest_swaps(first_to_rest(-1)), dp, group)
     shares = [add_call(parts) for parts in landing + [last]]
 
     total = shares[0]

time: 254 us -> 251 us (0.988)
  local copies, waits for them, and re-layouts: 30.4 us -> 12.5 us
  Pallas kernels: 95.2 us -> 106 us
  waiting for transfers between devices: 67.2 us -> 74 us
  starting transfers between devices: 54.7 us -> 48.7 us
  other arithmetic: 4.46 us -> 7.47 us
    ppermute x30 -> x31, waiting for transfers between devices: 43.3 us -> 66.2 us  [swap(): return lax.ppermute(x, axis, [(i, i ^ bit) for i in range(size)])]
    unnamed x77 -> x47, local copies, waits for them, and re-layouts: 22.9 us -> 6.61 us
    ppermute x4, waiting for transfers between devices: 16.7 us -> 3.71 us  [hop(): return lax.ppermute(block, ('dp', 'group'), pairs)]
    ppermute x30 -> x31, starting transfers between devices: 42.9 us -> 35.5 us  [swap(): return lax.ppermute(x, axis, [(i, i ^ bit) for i in range(size)])]
    dynamic_update_slice x14 -> x3, local copies, waits for them, and re-layouts: 5.03 us -> 0.03 us  [sum_stem(): lax.dynamic_update_slice_in_dim(line, block, (high ^ j + 1) * cols, 1)]
    pallas_call x3, Pallas kernels: 4.73 us -> 8.97 us  [combine_call(): pl.pallas_call(functools.partial(combine_kernel, len(deps)), in_specs=[SC...]
    concatenate x1 -> x2, other arithmetic: 0.02 us -> 3.21 us  [the longest x1 2.05 us: on_device(): far.append(cross(jnp.concatenate(behind, axis=0)))]
    pallas_call x2, Pallas kernels: 1.24 us -> 4.37 us  [add_call(): pl.pallas_call(functools.partial(add_kernel, len(parts)), in_specs=[spec]...]
  transfers between devices with their start and end apart: 41 -> 42, of which waited for: 13 -> 15; matrix products, arithmetic and copies ran while one was open for 4% -> 4% of each run, Pallas kernels for 33% -> 38%
where the time goes in v4:
time: 251 us; the launch traced here: 250 us
  Pallas kernels  106 us (42%)
  waiting for transfers between devices  74 us (29%)
  starting transfers between devices  48.7 us (19%)
  local copies, waits for them, and re-layouts  12.5 us (5%)
  other arithmetic  7.47 us (3%)
    ppermute x31, waiting for transfers between devices, swap(): return lax.ppermute(x, axis, [(i, i ^ bit) for i in range(size)])  66.2 us
    ppermute x31, starting transfers between devices, swap(): return lax.ppermute(x, axis, [(i, i ^ bit) for i in range(size)])  35.5 us
    pallas_call x2, Pallas kernels, attention_call(): pl.pallas_call(attention_kernel, grid=(2, steps), in_specs=[SCALARS, SCAL...  33 us
    pallas_call x2, Pallas kernels, weight_grad_call(): pl.pallas_call(functools.partial(weight_grad_kernel, len(deps), blocks),...  19.8 us
    pallas_call x1, Pallas kernels, tail_call(): pl.pallas_call(functools.partial(tail_kernel, len(packs)), grid=(tokens /...  11.7 us
    pallas_call x3, Pallas kernels, combine_call(): pl.pallas_call(functools.partial(combine_kernel, len(deps)), in_specs=[SC...  8.97 us
    pallas_call x1, Pallas kernels, back_call(): pl.pallas_call(functools.partial(back_kernel, len(packs)), grid=(steps,),...  8.27 us
    ppermute x4, starting transfers between devices, step(): ahead = lax.ppermute(self.ahead[-1], self.axis, self.forward)  7.87 us
  transfers between devices with their start and end apart: 42, of which 15 were waited for; matrix products, arithmetic and copies ran while one was open for 4% of the time, Pallas kernels for 38%

profile of v4, /device:TPU:0, one launch (start us, length us, event | category | flops | bytes accessed | tf_op | source)
XLA Modules:
  0.0 250.0 jit_solution(2094084294274748978)
XLA Ops:
  2.9 3.1 %collective-permute-start = (bf16[128,1024]{1,0:T(8,128)(2,1)S(1)}, bf16[128,1024]{1,0:T(8,128)(2,1)S(1)}, u32[]{:S(2)}, u32[]{:S(2)}) collective-permute-start(bf16[128,1024]{1,0:T(8,128)(2,1)S(1)} %pad_maximum_fusion.2.refs_0_), channel_id=1, source_target_pairs={{0,8},{8,16},{16,24},{24,28},{28,20},{20,12},{12,4},{4,0},{1,9},{9... | collective-permute-start | bytes 786440 | tf_op jit(solution)/shard_map/ppermute | solution.py:490
  9.0 7.6 %stem_norm.1 = (bf16[6,144,1024]{2,1,0:T(8,128)(2,1)}, bf16[6,144,1024]{2,1,0:T(8,128)(2,1)}, bf16[6,144,1024]{2,1,0:T(8,128)(2,1)}, bf16[6,144,256]{2,1,0:T(8,128)(2,1)}) custom-call(s32[6,3]{1,0:T(8,128)} %copy.54.cnt_ref, s32[6,144,1]{2,1,0:T(8,128)} %reshape.64.idx_ref, bf16[6,144,640]{2,1,0:T(8,128)(2,1)} %patch_ref.1, bf16[640,1024]{1,0:T(8,128)(2,1)} %w_ref.1, ...), custom_call_target="tpu_custom_call" | custom-call | flops 8000000 | bytes 12000 | tf_op jit(solution)/shard_map/stem_norm/pallas_call | solution.py:101
  22.0 5.2 %collective-permute-done.7.refs_0_ = bf16[128,1024]{1,0:T(8,128)(2,1)S(1)} collective-permute-done((bf16[128,1024]{1,0:T(8,128)(2,1)}, bf16[128,1024]{1,0:T(8,128)(2,1)S(1)}, u32[]{:S(2)}, u32[]{:S(2)}) %collective-permute-start.7) | collective-permute-done | bytes 262176 | tf_op jit(solution)/shard_map/ppermute | solution.py:474
  32.0 3.5 %collective-permute-done.10.refs_1_ = bf16[128,1024]{1,0:T(8,128)(2,1)S(1)} collective-permute-done((bf16[128,1024]{1,0:T(8,128)(2,1)}, bf16[128,1024]{1,0:T(8,128)(2,1)S(1)}, u32[]{:S(2)}, u32[]{:S(2)}) %collective-permute-start.10) | collective-permute-done | bytes 262176 | tf_op jit(solution)/shard_map/ppermute | solution.py:474
  35.5 2.1 collective-permute-done.8.refs_3_
  44.8 6.6 %transpose_rows.1 = (bf16[1024,864]{1,0:T(8,128)(2,1)}, bf16[1024,864]{1,0:T(8,128)(2,1)}, bf16[1024,864]{1,0:T(8,128)(2,1)}, bf16[1024,864]{1,0:T(8,128)(2,1)}) custom-call(bf16[864,1024]{1,0:T(8,128)(2,1)} %bitcast.24, bf16[864,1024]{1,0:T(8,128)(2,1)} %copy-done.1, bf16[864,1024]{1,0:T(8,128)(2,1)} %bitcast.19, bf16[864,1024]{1,0:T(8,128)(2,1)} %copy-done), custom_call_target="tpu_custom_call" | custom-call | flops 4000000 | bytes 8000 | tf_op jit(solution)/shard_map/transpose_rows/pallas_call | solution.py:247
  51.4 15.4 %collective-permute-done.12.refs_2_ = bf16[128,1024]{1,0:T(8,128)(2,1)} collective-permute-done((bf16[128,1024]{1,0:T(8,128)(2,1)}, bf16[128,1024]{1,0:T(8,128)(2,1)}, u32[]{:S(2)}, u32[]{:S(2)}) %collective-permute-start.12) | collective-permute-done | bytes 262176 | tf_op jit(solution)/shard_map/ppermute | solution.py:474
  66.8 2.8 %collective-permute-done.13.refs_3_ = bf16[128,1024]{1,0:T(8,128)(2,1)} collective-permute-done((bf16[128,1024]{1,0:T(8,128)(2,1)}, bf16[128,1024]{1,0:T(8,128)(2,1)}, u32[]{:S(2)}, u32[]{:S(2)}) %collective-permute-start.13) | collective-permute-done | bytes 262176 | tf_op jit(solution)/shard_map/ppermute | solution.py:474
  71.4 16.6 %attention.2 = (bf16[1728,1024]{1,0:T(8,128)(2,1)}, bf16[1024,1024]{1,0:T(8,128)(2,1)}) custom-call(s32[2,6,3]{2,1,0:T(8,128)} %pad_add_fusion.cnt_ref, s32[8]{0:T(128)} %compare_select_fusion.2.owner_ref, bf16[864,1024]{1,0:T(8,128)(2,1)} %bitcast.25, bf16[864,1024]{1,0:T(8,128)(2,1)} %copy-done.1, bf16[864,1024]{1,0:T(8,128)(2,1)} %bitcast.20, ...), custom_call_target="tpu_custom_call" | custom-call | flops 20000000 | bytes 14000 | tf_op jit(solution)/shard_map/attention/pallas_call | solution.py:216
  88.0 9.8 %weight_grad.2 = (bf16[512,1024]{1,0:T(8,128)(2,1)}, f32[512,1024]{1,0:T(8,128)}) custom-call(s32[1]{0:T(128)} %bitcast.1.low_ref, bf16[1024,864]{1,0:T(8,128)(2,1)} %get-tuple-element.121.na_ref, bf16[1024,864]{1,0:T(8,128)(2,1)} %get-tuple-element.122.nb_ref, bf16[1024,864]{1,0:T(8,128)(2,1)} %get-tuple-element.123.ga_ref, ...), custom_call_target="tpu_custom_call" | custom-call | flops 6000000 | bytes 12000 | tf_op jit(solution)/shard_map/weight_grad/pallas_call | solution.py:280
  101.3 16.4 %attention.3 = (bf16[1728,1024]{1,0:T(8,128)(2,1)}, bf16[1024,1024]{1,0:T(8,128)(2,1)}) custom-call(s32[2,6,3]{2,1,0:T(8,128)} %pad_add_fusion.cnt_ref, s32[8]{0:T(128)} %compare_select_fusion.2.owner_ref, bf16[864,1024]{1,0:T(8,128)(2,1)} %bitcast.26, bf16[864,1024]{1,0:T(8,128)(2,1)} %copy-done.1, bf16[864,1024]{1,0:T(8,128)(2,1)} %bitcast.21, ...), custom_call_target="tpu_custom_call" | custom-call | flops 20000000 | bytes 14000 | tf_op jit(solution)/shard_map/attention/pallas_call | solution.py:216
  117.7 2.8 %collective-permute-done.16.recv_ref = bf16[512,1024]{1,0:T(8,128)(2,1)S(1)} collective-permute-done((bf16[512,1024]{1,0:T(8,128)(2,1)}, bf16[512,1024]{1,0:T(8,128)(2,1)S(1)}, u32[]{:S(2)}, u32[]{:S(2)}) %collective-permute-start.16) | collective-permute-done | bytes 1048608 | tf_op jit(solution)/shard_map/ppermute | solution.py:474
  120.4 8.3 %back.1 = (f32[864,1024]{1,0:T(8,128)}, bf16[864,1024]{1,0:T(8,128)(2,1)}) custom-call(bf16[1728,1024]{1,0:T(8,128)(2,1)} %get-tuple-element.132.pack_ref.refs_0_, bf16[1728,1024]{1,0:T(8,128)(2,1)} %get-tuple-element.140.pack_ref.refs_1_, bf16[1024,1024]{1,0:T(8,128)(2,1)} %get-tuple-element.143.refs_2_, bf16[1024,1024]{1,0:T(8,128)(2,1)} %get-tuple-element.144.refs_3_), custom_call_target="tpu_custom_call" | custom-call | flops 10000000 | bytes 12000 | tf_op jit(solution)/shard_map/back/pallas_call | solution.py:369
  129.2 3.0 %combine.3 = (f32[128,1024]{1,0:T(8,128)}, bf16[128,1024]{1,0:T(8,128)(2,1)}, bf16[128,1024]{1,0:T(8,128)(2,1)}, bf16[128,1024]{1,0:T(8,128)(2,1)}) custom-call(s32[1]{0:T(128)} %bitcast.10.place_ref, f32[512,1024]{1,0:T(8,128)} %get-tuple-element.146.keep_ref, bf16[512,1024]{1,0:T(8,128)(2,1)} %copy-done.4), custom_call_target="tpu_custom_call" | custom-call | flops 1000 | bytes 5000 | tf_op jit(solution)/shard_map/combine/pallas_call | solution.py:312
  134.0 2.6 %collective-permute-start.19 = (bf16[128,1024]{1,0:T(8,128)(2,1)}, bf16[128,1024]{1,0:T(8,128)(2,1)S(1)}, u32[]{:S(2)}, u32[]{:S(2)}) collective-permute-start(bf16[128,1024]{1,0:T(8,128)(2,1)} %get-tuple-element.150), channel_id=1, source_target_pairs={{0,16},{4,20},{8,24},{12,28},{16,0},{20,4},{24,8},{28,12},{1,17},{... | collective-permute-start | bytes 786440 | tf_op jit(solution)/shard_map/ppermute | solution.py:474
  136.6 10.0 %weight_grad.3 = (bf16[512,1024]{1,0:T(8,128)(2,1)}, f32[512,1024]{1,0:T(8,128)}) custom-call(s32[1]{0:T(128)} %bitcast.1.low_ref, bf16[1024,864]{1,0:T(8,128)(2,1)} %get-tuple-element.121.na_ref, bf16[1024,864]{1,0:T(8,128)(2,1)} %get-tuple-element.122.nb_ref, bf16[1024,864]{1,0:T(8,128)(2,1)} %get-tuple-element.123.ga_ref, ...), custom_call_target="tpu_custom_call" | custom-call | flops 6000000 | bytes 12000 | tf_op jit(solution)/shard_map/weight_grad/pallas_call | solution.py:280
  146.7 8.9 %collective-permute-done.19.refs_2_ = bf16[128,1024]{1,0:T(8,128)(2,1)S(1)} collective-permute-done((bf16[128,1024]{1,0:T(8,128)(2,1)}, bf16[128,1024]{1,0:T(8,128)(2,1)S(1)}, u32[]{:S(2)}, u32[]{:S(2)}) %collective-permute-start.19) | collective-permute-done | bytes 262176 | tf_op jit(solution)/shard_map/ppermute | solution.py:474
  158.0 11.7 %tail.1 = (f32[320,1024]{1,0:T(8,128)}, f32[320,1024]{1,0:T(8,128)}) custom-call(s32[1]{0:T(128)} %bitcast.core_ref, f32[864,1024]{1,0:T(8,128)} %copy-done.2, bf16[864,1024]{1,0:T(8,128)(2,1)} %bitcast.27, bf16[864,1024]{1,0:T(8,128)(2,1)} %bitcast.22, bf16[864,256]{1,0:T(8,128)(2,1)} %bitcast.33, f32[1,1024]{1,0:T(1,128)} %bitcast.36, ...), custom_call_target="tpu_custom_call" | custom-call | flops 10000000 | bytes 12000 | tf_op jit(solution)/shard_map/tail/pallas_call | solution.py:424
  171.7 6.0 %layer_output.1 = bf16[864,1024]{1,0:T(8,128)(2,1)} custom-call(s32[6,3]{1,0:T(8,128)} %copy.54.cnt_ref, bf16[864,1024]{1,0:T(8,128)(2,1)} %collective-permute-done.20.recv_ref, bf16[864,1024]{1,0:T(8,128)(2,1)} %bitcast.28, bf16[1728,1024]{1,0:T(8,128)(2,1)} %get-tuple-element.132.pack_ref.refs_0_, bf16[1728,1024]{1,0:T(8,128)(2,1)} %get-tuple-element.140.pack_ref.refs_1_, ...), custom_call_target="tpu_custom_call" | custom-call | flops 5000000 | bytes 10000 | tf_op jit(solution)/shard_map/layer_output/pallas_call | solution.py:458
  178.9 2.9 %combine.4 = (f32[80,1024]{1,0:T(8,128)}, f32[80,1024]{1,0:T(8,128)}, f32[80,1024]{1,0:T(8,128)}, f32[80,1024]{1,0:T(8,128)}) custom-call(s32[1]{0:T(128)} %bitcast.14.place_ref, f32[320,1024]{1,0:T(8,128)} %get-tuple-element.165.keep_ref, f32[320,1024]{1,0:T(8,128)} %pad_maximum_fusion.recv_ref), custom_call_target="tpu_custom_call" | custom-call | flops 1000 | bytes 5000 | tf_op jit(solution)/shard_map/combine/pallas_call | solution.py:312
  185.3 3.0 %combine.5 = (f32[128,1024]{1,0:T(8,128)}, bf16[128,1024]{1,0:T(8,128)(2,1)}, bf16[128,1024]{1,0:T(8,128)(2,1)}, bf16[128,1024]{1,0:T(8,128)(2,1)}) custom-call(s32[1]{0:T(128)} %bitcast.10.place_ref, f32[512,1024]{1,0:T(8,128)} %get-tuple-element.172.keep_ref, bf16[512,1024]{1,0:T(8,128)(2,1)} %collective-permute-done.24.recv_ref), custom_call_target="tpu_custom_call" | custom-call | flops 1000 | bytes 5000 | tf_op jit(solution)/shard_map/combine/pallas_call | solution.py:312
  188.9 4.2 %collective-permute-start.32 = (bf16[128,1024]{1,0:T(8,128)(2,1)}, bf16[128,1024]{1,0:T(8,128)(2,1)S(1)}, u32[]{:S(2)}, u32[]{:S(2)}) collective-permute-start(bf16[128,1024]{1,0:T(8,128)(2,1)} %get-tuple-element.181), channel_id=1, source_target_pairs={{0,16},{4,20},{8,24},{12,28},{16,0},{20,4},{24,8},{28,12},{1,17},{... | collective-permute-start | bytes 786440 | tf_op jit(solution)/shard_map/ppermute | solution.py:474
  193.1 8.2 %collective-permute-done.28.refs_1_ = bf16[128,1024]{1,0:T(8,128)(2,1)S(1)} collective-permute-done((bf16[128,1024]{1,0:T(8,128)(2,1)}, bf16[128,1024]{1,0:T(8,128)(2,1)S(1)}, u32[]{:S(2)}, u32[]{:S(2)}) %collective-permute-start.28) | collective-permute-done | bytes 262176 | tf_op jit(solution)/shard_map/ppermute | solution.py:474
  203.6 2.3 collective-permute-start.31
  207.4 9.0 %collective-permute-done.30 = f32[80,256]{1,0:T(8,128)S(1)} collective-permute-done((f32[80,256]{1,0:T(8,128)S(1)}, f32[80,256]{1,0:T(8,128)S(1)}, u32[]{:S(2)}, u32[]{:S(2)}) %collective-permute-start.30) | collective-permute-done | bytes 81952 | tf_op jit(solution)/shard_map/ppermute | solution.py:474
  216.4 2.4 collective-permute-start.33
  218.8 2.4 collective-permute-start.35
  221.3 4.0 %collective-permute-done.34 = bf16[80,256]{1,0:T(8,128)(2,1)S(1)} collective-permute-done((bf16[80,256]{1,0:T(8,128)(2,1)S(1)}, bf16[80,256]{1,0:T(8,128)(2,1)S(1)}, u32[]{:S(2)}, u32[]{:S(2)}) %collective-permute-start.34) | collective-permute-done | bytes 40992 | tf_op jit(solution)/shard_map/ppermute | solution.py:474
  228.9 2.2 add_parts.3
  233.7 2.6 %collective-permute-done.39 = bf16[80,1024]{1,0:T(8,128)(2,1)S(1)} collective-permute-done((bf16[80,1024]{1,0:T(8,128)(2,1)S(1)}, bf16[80,1024]{1,0:T(8,128)(2,1)S(1)}, u32[]{:S(2)}, u32[]{:S(2)}) %collective-permute-start.39) | collective-permute-done | bytes 163872 | tf_op jit(solution)/shard_map/ppermute | solution.py:529
  236.5 2.2 add_parts.2
  238.6 6.5 %collective-permute-done.41 = f32[128,1024]{1,0:T(8,128)S(1)} collective-permute-done((f32[128,1024]{1,0:T(8,128)}, f32[128,1024]{1,0:T(8,128)S(1)}, u32[]{:S(2)}, u32[]{:S(2)}) %collective-permute-start.41) | collective-permute-done | bytes 524320 | tf_op jit(solution)/shard_map/ppermute | solution.py:474
  (142 shorter events, 54.8 us)
Async XLA Ops:
  2.9 13.8 %collective-permute-start = (bf16[128,1024]{1,0:T(8,128)(2,1)S(1)}, bf16[128,1024]{1,0:T(8,128)(2,1)S(1)}, u32[]{:S(2)}, u32[]{:S(2)}) collective-permute-start(bf16[128,1024]{1,0:T(8,128)(2,1)S(1)} %pad_maximum_fusion.2.refs_0_), channel_id=1, source_target_pairs={{0,8},{8,16},{16,24},{24,28},{28,20},{20,12},{12,4},{4,0},{1,9},{9... | collective-permute-start | bytes 786440 | tf_op jit(solution)/shard_map/ppermute | solution.py:490
  5.9 10.7 %collective-permute-start.1 = (bf16[128,1024]{1,0:T(8,128)(2,1)S(1)}, bf16[128,1024]{1,0:T(8,128)(2,1)S(1)}, u32[]{:S(2)}, u32[]{:S(2)}) collective-permute-start(bf16[128,1024]{1,0:T(8,128)(2,1)S(1)} %pad_maximum_fusion.2.refs_0_), channel_id=1, source_target_pairs={{8,0},{16,8},{24,16},{28,24},{20,28},{12,20},{4,12},{0,4},{9,1},{1... | collective-permute-start | bytes 786440 | tf_op jit(solution)/shard_map/ppermute | solution.py:492
  5.9 10.7 %collective-permute-start.2 = (s32[6,3]{0,1:T(4,128)}, s32[6,3]{0,1:T(4,128)S(1)}, u32[]{:S(2)}, u32[]{:S(2)}) collective-permute-start(s32[6,3]{0,1:T(4,128)} %param.13), channel_id=1, source_target_pairs={{0,1},{1,0},{2,3},{3,2},{4,5},{5,4},{6,7},{7,6},{8,9},{9,8},{10,11... | collective-permute-start | bytes 224 | tf_op jit(solution)/shard_map/ppermute | solution.py:474
  17.5 12.4 %collective-permute-start.6 = (bf16[864,1024]{1,0:T(8,128)(2,1)}, bf16[864,1024]{1,0:T(8,128)(2,1)S(1)}, u32[]{:S(2)}, u32[]{:S(2)}) collective-permute-start(bf16[864,1024]{1,0:T(8,128)(2,1)} %bitcast.18), channel_id=1, source_target_pairs={{0,1},{1,0},{2,3},{3,2},{4,5},{5,4},{6,7},{7,6},{8,9},{9,8},{10,11... | collective-permute-start | bytes 5308424 | tf_op jit(solution)/shard_map/ppermute | solution.py:474
  18.0 11.9 %collective-permute-start.5 = (bf16[864,1024]{1,0:T(8,128)(2,1)}, bf16[864,1024]{1,0:T(8,128)(2,1)S(1)}, u32[]{:S(2)}, u32[]{:S(2)}) collective-permute-start(bf16[864,1024]{1,0:T(8,128)(2,1)} %bitcast.23), channel_id=1, source_target_pairs={{0,1},{1,0},{2,3},{3,2},{4,5},{5,4},{6,7},{7,6},{8,9},{9,8},{10,11... | collective-permute-start | bytes 5308424 | tf_op jit(solution)/shard_map/ppermute | solution.py:474
  18.0 9.1 %collective-permute-start.7 = (bf16[128,1024]{1,0:T(8,128)(2,1)}, bf16[128,1024]{1,0:T(8,128)(2,1)S(1)}, u32[]{:S(2)}, u32[]{:S(2)}) collective-permute-start(bf16[128,1024]{1,0:T(8,128)(2,1)} %copy-done.3), channel_id=1, source_target_pairs={{0,2},{1,3},{2,0},{3,1},{4,6},{5,7},{6,4},{7,5},{8,10},{9,11},{10,... | collective-permute-start | bytes 786440 | tf_op jit(solution)/shard_map/ppermute | solution.py:474
  19.9 8.9 %collective-permute-start.3 = (bf16[128,1024]{1,0:T(8,128)(2,1)}, bf16[128,1024]{1,0:T(8,128)(2,1)}, u32[]{:S(2)}, u32[]{:S(2)}) collective-permute-start(bf16[128,1024]{1,0:T(8,128)(2,1)} %copy-done.12), channel_id=1, source_target_pairs={{0,8},{8,16},{16,24},{24,28},{28,20},{20,12},{12,4},{4,0},{1,9},{9... | collective-permute-start | bytes 786440 | tf_op jit(solution)/shard_map/ppermute | solution.py:490
  21.5 8.4 %collective-permute-start.4 = (bf16[128,1024]{1,0:T(8,128)(2,1)}, bf16[128,1024]{1,0:T(8,128)(2,1)S(1)}, u32[]{:S(2)}, u32[]{:S(2)}) collective-permute-start(bf16[128,1024]{1,0:T(8,128)(2,1)} %copy-done.5), channel_id=1, source_target_pairs={{8,0},{16,8},{24,16},{28,24},{20,28},{12,20},{4,12},{0,4},{9,1},{1... | collective-permute-start | bytes 786440 | tf_op jit(solution)/shard_map/ppermute | solution.py:492
  27.1 8.4 %collective-permute-start.10 = (bf16[128,1024]{1,0:T(8,128)(2,1)}, bf16[128,1024]{1,0:T(8,128)(2,1)S(1)}, u32[]{:S(2)}, u32[]{:S(2)}) collective-permute-start(bf16[128,1024]{1,0:T(8,128)(2,1)} %copy-done.12), channel_id=1, source_target_pairs={{0,2},{1,3},{2,0},{3,1},{4,6},{5,7},{6,4},{7,5},{8,10},{9,11},{10,... | collective-permute-start | bytes 786440 | tf_op jit(solution)/shard_map/ppermute | solution.py:474
  40.6 57.2 %collective-permute-start.15 = (bf16[384,1024]{1,0:T(8,128)(2,1)}, bf16[384,1024]{1,0:T(8,128)(2,1)}, u32[]{:S(2)}, u32[]{:S(2)}) collective-permute-start(bf16[384,1024]{1,0:T(8,128)(2,1)} %pad_maximum_fusion.1), channel_id=1, source_target_pairs={{0,2},{1,3},{2,0},{3,1},{4,6},{5,7},{6,4},{7,5},{8,10},{9,11},{10,... | collective-permute-start | bytes 2359304 | tf_op jit(solution)/shard_map/ppermute | solution.py:474
  41.1 25.6 %collective-permute-start.12 = (bf16[128,1024]{1,0:T(8,128)(2,1)}, bf16[128,1024]{1,0:T(8,128)(2,1)}, u32[]{:S(2)}, u32[]{:S(2)}) collective-permute-start(bf16[128,1024]{1,0:T(8,128)(2,1)} %collective-permute-done.3.refs_2_), channel_id=1, source_target_pairs={{0,2},{1,3},{2,0},{3,1},{4,6},{5,7},{6,4},{7,5},{8,10},{9,11},{10,... | collective-permute-start | bytes 786440 | tf_op jit(solution)/shard_map/ppermute | solution.py:474
  42.6 24.2 %collective-permute-start.11 = (bf16[128,1024]{1,0:T(8,128)(2,1)}, bf16[128,1024]{1,0:T(8,128)(2,1)}, u32[]{:S(2)}, u32[]{:S(2)}) collective-permute-start(bf16[128,1024]{1,0:T(8,128)(2,1)} %collective-permute-done.8.refs_3_), channel_id=1, source_target_pairs={{0,8},{8,16},{16,24},{24,28},{28,20},{20,12},{12,4},{4,0},{1,9},{9... | collective-permute-start | bytes 786440 | tf_op jit(solution)/shard_map/ppermute | solution.py:490
  44.2 25.4 %collective-permute-start.13 = (bf16[128,1024]{1,0:T(8,128)(2,1)}, bf16[128,1024]{1,0:T(8,128)(2,1)}, u32[]{:S(2)}, u32[]{:S(2)}) collective-permute-start(bf16[128,1024]{1,0:T(8,128)(2,1)} %collective-permute-done.8.refs_3_), channel_id=1, source_target_pairs={{0,2},{1,3},{2,0},{3,1},{4,6},{5,7},{6,4},{7,5},{8,10},{9,11},{10,... | collective-permute-start | bytes 786440 | tf_op jit(solution)/shard_map/ppermute | solution.py:474
  69.6 28.2 %collective-permute-start.14 = (bf16[128,1024]{1,0:T(8,128)(2,1)}, bf16[128,1024]{1,0:T(8,128)(2,1)S(1)}, u32[]{:S(2)}, u32[]{:S(2)}) collective-permute-start(bf16[128,1024]{1,0:T(8,128)(2,1)} %collective-permute-done.11.refs_4_), channel_id=1, source_target_pairs={{0,2},{1,3},{2,0},{3,1},{4,6},{5,7},{6,4},{7,5},{8,10},{9,11},{10,... | collective-permute-start | bytes 786440 | tf_op jit(solution)/shard_map/ppermute | solution.py:474
  97.9 22.6 %collective-permute-start.16 = (bf16[512,1024]{1,0:T(8,128)(2,1)}, bf16[512,1024]{1,0:T(8,128)(2,1)S(1)}, u32[]{:S(2)}, u32[]{:S(2)}) collective-permute-start(bf16[512,1024]{1,0:T(8,128)(2,1)} %get-tuple-element.139), channel_id=1, source_target_pairs={{0,4},{4,0},{8,12},{12,8},{16,20},{20,16},{24,28},{28,24},{1,5},{5... | collective-permute-start | bytes 3145736 | tf_op jit(solution)/shard_map/ppermute | solution.py:474
  128.7 26.9 %collective-permute-start.17 = (f32[864,1024]{1,0:T(8,128)}, f32[864,1024]{1,0:T(8,128)S(1)}, u32[]{:S(2)}, u32[]{:S(2)}) collective-permute-start(f32[864,1024]{1,0:T(8,128)} %get-tuple-element.145), channel_id=1, source_target_pairs={{0,1},{1,0},{2,3},{3,2},{4,5},{5,4},{6,7},{7,6},{8,9},{9,8},{10,11... | collective-permute-start | bytes 10616840 | tf_op jit(solution)/shard_map/ppermute | solution.py:474
  128.7 41.0 %collective-permute-start.20 = (bf16[864,1024]{1,0:T(8,128)(2,1)}, bf16[864,1024]{1,0:T(8,128)(2,1)}, u32[]{:S(2)}, u32[]{:S(2)}) collective-permute-start(bf16[864,1024]{1,0:T(8,128)(2,1)} %get-tuple-element.156), channel_id=1, source_target_pairs={{0,1},{1,0},{2,3},{3,2},{4,5},{5,4},{6,7},{7,6},{8,9},{9,8},{10,11... | collective-permute-start | bytes 5308424 | tf_op jit(solution)/shard_map/ppermute | solution.py:474
  132.2 14.4 %collective-permute-start.18 = (bf16[128,1024]{1,0:T(8,128)(2,1)}, bf16[128,1024]{1,0:T(8,128)(2,1)S(1)}, u32[]{:S(2)}, u32[]{:S(2)}) collective-permute-start(bf16[128,1024]{1,0:T(8,128)(2,1)} %get-tuple-element.149), channel_id=1, source_target_pairs={{0,8},{4,12},{8,0},{12,4},{16,24},{20,28},{24,16},{28,20},{1,9},{5... | collective-permute-start | bytes 786440 | tf_op jit(solution)/shard_map/ppermute | solution.py:474
  134.0 21.5 %collective-permute-start.19 = (bf16[128,1024]{1,0:T(8,128)(2,1)}, bf16[128,1024]{1,0:T(8,128)(2,1)S(1)}, u32[]{:S(2)}, u32[]{:S(2)}) collective-permute-start(bf16[128,1024]{1,0:T(8,128)(2,1)} %get-tuple-element.150), channel_id=1, source_target_pairs={{0,16},{4,20},{8,24},{12,28},{16,0},{20,4},{24,8},{28,12},{1,17},{... | collective-permute-start | bytes 786440 | tf_op jit(solution)/shard_map/ppermute | solution.py:474
  136.6 33.1 %collective-permute-start.21 = (bf16[128,1024]{1,0:T(8,128)(2,1)}, bf16[128,1024]{1,0:T(8,128)(2,1)}, u32[]{:S(2)}, u32[]{:S(2)}) collective-permute-start(bf16[128,1024]{1,0:T(8,128)(2,1)} %get-tuple-element.160), channel_id=1, source_target_pairs={{0,24},{4,28},{8,16},{12,20},{16,8},{20,12},{24,0},{28,4},{1,25},{... | collective-permute-start | bytes 786440 | tf_op jit(solution)/shard_map/ppermute | solution.py:474
  156.3 21.4 %collective-permute-start.24 = (bf16[512,1024]{1,0:T(8,128)(2,1)}, bf16[512,1024]{1,0:T(8,128)(2,1)}, u32[]{:S(2)}, u32[]{:S(2)}) collective-permute-start(bf16[512,1024]{1,0:T(8,128)(2,1)} %get-tuple-element.163), channel_id=1, source_target_pairs={{0,4},{4,0},{8,12},{12,8},{16,20},{20,16},{24,28},{28,24},{1,5},{5... | collective-permute-start | bytes 3145736 | tf_op jit(solution)/shard_map/ppermute | solution.py:474
  181.8 19.5 %collective-permute-start.25 = (f32[80,1024]{1,0:T(8,128)}, f32[80,1024]{1,0:T(8,128)S(1)}, u32[]{:S(2)}, u32[]{:S(2)}) collective-permute-start(f32[80,1024]{1,0:T(8,128)} %get-tuple-element.169), channel_id=1, source_target_pairs={{0,4},{4,0},{8,12},{12,8},{16,20},{20,16},{24,28},{28,24},{1,5},{5... | collective-permute-start | bytes 983048 | tf_op jit(solution)/shard_map/ppermute | solution.py:474
  183.0 18.3 %collective-permute-start.26 = (f32[80,1024]{1,0:T(8,128)}, f32[80,1024]{1,0:T(8,128)S(1)}, u32[]{:S(2)}, u32[]{:S(2)}) collective-permute-start(f32[80,1024]{1,0:T(8,128)} %get-tuple-element.170), channel_id=1, source_target_pairs={{0,2},{1,3},{2,0},{3,1},{4,6},{5,7},{6,4},{7,5},{8,10},{9,11},{10,... | collective-permute-start | bytes 983048 | tf_op jit(solution)/shard_map/ppermute | solution.py:529
  183.4 17.8 %collective-permute-start.27 = (f32[80,1024]{1,0:T(8,128)}, f32[80,1024]{1,0:T(8,128)S(1)}, u32[]{:S(2)}, u32[]{:S(2)}) collective-permute-start(f32[80,1024]{1,0:T(8,128)} %get-tuple-element.171), channel_id=1, source_target_pairs={{0,6},{1,7},{2,4},{3,5},{4,2},{5,3},{6,0},{7,1},{8,14},{9,15},{10,... | collective-permute-start | bytes 983048 | tf_op jit(solution)/shard_map/ppermute | solution.py:529
  188.3 12.9 %collective-permute-start.28 = (bf16[128,1024]{1,0:T(8,128)(2,1)}, bf16[128,1024]{1,0:T(8,128)(2,1)S(1)}, u32[]{:S(2)}, u32[]{:S(2)}) collective-permute-start(bf16[128,1024]{1,0:T(8,128)(2,1)} %get-tuple-element.175), channel_id=1, source_target_pairs={{0,8},{4,12},{8,0},{12,4},{16,24},{20,28},{24,16},{28,20},{1,9},{5... | collective-permute-start | bytes 786440 | tf_op jit(solution)/shard_map/ppermute | solution.py:474
  188.9 18.5 %collective-permute-start.32 = (bf16[128,1024]{1,0:T(8,128)(2,1)}, bf16[128,1024]{1,0:T(8,128)(2,1)S(1)}, u32[]{:S(2)}, u32[]{:S(2)}) collective-permute-start(bf16[128,1024]{1,0:T(8,128)(2,1)} %get-tuple-element.181), channel_id=1, source_target_pairs={{0,16},{4,20},{8,24},{12,28},{16,0},{20,4},{24,8},{28,12},{1,17},{... | collective-permute-start | bytes 786440 | tf_op jit(solution)/shard_map/ppermute | solution.py:474
  201.5 14.9 %collective-permute-start.30 = (f32[80,256]{1,0:T(8,128)S(1)}, f32[80,256]{1,0:T(8,128)S(1)}, u32[]{:S(2)}, u32[]{:S(2)}) collective-permute-start(f32[80,256]{1,0:T(8,128)S(1)} %get-tuple-element.226), channel_id=1, source_target_pairs={{0,16},{4,20},{8,24},{12,28},{16,0},{20,4},{24,8},{28,12},{1,17},{... | collective-permute-start | bytes 245768 | tf_op jit(solution)/shard_map/ppermute | solution.py:474
  203.6 12.8 %collective-permute-start.31 = (f32[80,256]{1,0:T(8,128)S(1)}, f32[80,256]{1,0:T(8,128)S(1)}, u32[]{:S(2)}, u32[]{:S(2)}) collective-permute-start(f32[80,256]{1,0:T(8,128)S(1)} %get-tuple-element.225), channel_id=1, source_target_pairs={{0,24},{4,28},{8,16},{12,20},{16,8},{20,12},{24,0},{28,4},{1,25},{... | collective-permute-start | bytes 245768 | tf_op jit(solution)/shard_map/ppermute | solution.py:474
  205.9 15.4 %collective-permute-start.36 = (bf16[128,1024]{1,0:T(8,128)(2,1)S(1)}, bf16[128,1024]{1,0:T(8,128)(2,1)S(1)}, u32[]{:S(2)}, u32[]{:S(2)}) collective-permute-start(bf16[128,1024]{1,0:T(8,128)(2,1)S(1)} %copy-done.19), channel_id=1, source_target_pairs={{0,24},{4,28},{8,16},{12,20},{16,8},{20,12},{24,0},{28,4},{1,25},{... | collective-permute-start | bytes 786440 | tf_op jit(solution)/shard_map/ppermute | solution.py:474
  227.2 9.2 %collective-permute-start.39 = (bf16[80,1024]{1,0:T(8,128)(2,1)S(1)}, bf16[80,1024]{1,0:T(8,128)(2,1)S(1)}, u32[]{:S(2)}, u32[]{:S(2)}) collective-permute-start(bf16[80,1024]{1,0:T(8,128)(2,1)S(1)} %constant_dynamic-update-slice_fusion.4), channel_id=1, source_target_pairs={{0,6},{1,7},{2,4},{3,5},{4,2},{5,3},{6,0},{7,1},{8,14},{9,15},{10,... | collective-permute-start | bytes 491528 | tf_op jit(solution)/shard_map/ppermute | solution.py:529
  231.1 14.0 %collective-permute-start.41 = (f32[128,1024]{1,0:T(8,128)}, f32[128,1024]{1,0:T(8,128)S(1)}, u32[]{:S(2)}, u32[]{:S(2)}) collective-permute-start(f32[128,1024]{1,0:T(8,128)} %add_parts.3), channel_id=1, source_target_pairs={{0,2},{1,3},{2,0},{3,1},{4,6},{5,7},{6,4},{7,5},{8,10},{9,11},{10,... | collective-permute-start | bytes 1572872 | tf_op jit(solution)/shard_map/ppermute | solution.py:474
  236.4 11.7 %collective-permute-start.40 = (bf16[320,1024]{1,0:T(8,128)(2,1)S(1)}, bf16[320,1024]{1,0:T(8,128)(2,1)S(1)}, u32[]{:S(2)}, u32[]{:S(2)}) collective-permute-start(bf16[320,1024]{1,0:T(8,128)(2,1)S(1)} %constant_dynamic-update-slice_fusion), channel_id=1, source_target_pairs={{0,1},{1,0},{2,3},{3,2},{4,5},{5,4},{6,7},{7,6},{8,9},{9,8},{10,11... | collective-permute-start | bytes 1966088 | tf_op jit(solution)/shard_map/ppermute | solution.py:474
  (31 other events, 310.8 us)

commit v5 on v4

--- a/solution.py
+++ b/solution.py
@@ -21,7 +21,7 @@
 NORM_EPS = 1e-06
 F32 = jnp.float32
 BF16 = jnp.bfloat16
-VMEM_LIMIT = 60 * 1024 * 1024
+VMEM_LIMIT = 36 * 1024 * 1024
 
 
 def dot_nn(a, b):
@@ -59,25 +59,23 @@
 ):
     step = pl.program_id(0)
     scenes = patch_ref.shape[0]
-    patch_iota = lax.broadcasted_iota(jnp.int32, (TOK, parts.shape[1]), 1)
-    picked, placed = [], []
-    for s in range(scenes):
-        onehot = (idx_ref[s] == patch_iota).astype(F32).astype(BF16)
-        picked.append(dot_nn(onehot, patch_ref[s]).astype(BF16))
-        placed.append(
-            (dot_nn(onehot, parts[0]) + dot_nn(onehot, parts[1])) + dot_nn(onehot, parts[2])
-        )
-        live = live_column(
-            cnt_ref[step * scenes + s, 0], cnt_ref[step * scenes + s, 1], cnt_ref[step * scenes + s, 2]
-        )
-        gl_ref[s] = jnp.where(live, og_ref[s].astype(F32), 0.0).astype(BF16)
+    patch_iota = lax.broadcasted_iota(jnp.int32, (parts.shape[1], CAP), 0)
+    slot = lax.broadcasted_iota(jnp.int32, (CAP, 1), 0)
     for g, (start, end) in enumerate(GROUP_BANDS):
         rows = slice(g * CAP, (g + 1) * CAP)
-        columns = jnp.concatenate([p[rows, start * PIX : end * PIX] for p in picked], axis=0)
-        summed = dot_nn(columns, w_ref[start * PIX : end * PIX, :])
         width = (end - start) * PIX
+        picked, placed = [], []
         for s in range(scenes):
-            values = summed[s * CAP : (s + 1) * CAP] + (placed[s][rows] + genc_ref[g : g + 1, :])
+            onehot = (idx_ref[s, g : g + 1, :] == patch_iota).astype(F32).astype(BF16).T
+            picked.append(dot_nn(onehot, patch_ref[s, :, start * PIX : end * PIX]).astype(BF16))
+            placed.append(
+                (dot_nn(onehot, parts[0]) + dot_nn(onehot, parts[1])) + dot_nn(onehot, parts[2])
+            )
+            live = slot < cnt_ref[step * scenes + s, g]
+            gl_ref[s, rows, :] = jnp.where(live, og_ref[s, rows, :].astype(F32), 0.0).astype(BF16)
+        summed = dot_nn(jnp.concatenate(picked, axis=0), w_ref[start * PIX : end * PIX, :])
+        for s in range(scenes):
+            values = summed[s * CAP : (s + 1) * CAP] + (placed[s] + genc_ref[g : g + 1, :])
             emb = values.astype(BF16)
             emb_ref[s, rows, :] = emb
             x = emb.astype(F32)
@@ -86,12 +84,12 @@
             spread = jnp.mean(dev * dev, axis=-1, keepdims=True)
             centred = dev * lax.rsqrt(spread + NORM_EPS)
             normed_ref[s, rows, :] = (centred * gain_ref[...]).astype(BF16)
-            cols_ref[s, rows, :width] = columns[s * CAP : (s + 1) * CAP]
+            cols_ref[s, rows, :width] = picked[s]
             if width < cols_ref.shape[2]:
                 cols_ref[s, rows, width:] = jnp.zeros((CAP, cols_ref.shape[2] - width), BF16)
 
 
-def stem_call(counts, index_col, patches, w_stem, gain, table, genc, out_grad):
+def stem_call(counts, index, patches, w_stem, gain, table, genc, out_grad):
     scenes, patch_count, width = patches.shape
     block = 3 if scenes % 3 == 0 else 1
     col_width = max(e - s for s, e in GROUP_BANDS) * PIX
@@ -103,7 +101,7 @@
         grid=(scenes // block,),
         in_specs=[
             pl.BlockSpec(memory_space=pltpu.SMEM),
-            per((TOK, 1)),
+            per((GROUPS, CAP)),
             per((patch_count, width)),
             whole(w_stem),
             whole(gain),
@@ -116,13 +114,12 @@
         compiler_params=params(),
         cost_estimate=cost(8e9, 12e6),
         name="stem_norm",
-    )(counts, index_col, patches, w_stem, gain, table, genc, out_grad)
-
-
-def attention_kernel(
-    cnt_ref, owner_ref, na_ref, nb_ref, ga_ref, gb_ref, *refs
-):
-    blocks, (out_ref, w_ref, n_s, g_s, qkv) = refs[:-5], refs[-5:]
+    )(counts, index, patches, w_stem, gain, table, genc, out_grad)
+
+
+def attention_kernel(first, cnt_ref, owner_ref, na_ref, nb_ref, ga_ref, gb_ref, *refs):
+    before, refs = refs[: 0 if first else 2], refs[0 if first else 2 :]
+    blocks, (out_ref, w_ref, back_own_ref, back_far_ref, n_s, g_s, qkv) = refs[:-7], refs[-7:]
     half, step = pl.program_id(0), pl.program_id(1)
     rows = n_s.shape[0]
     scenes = rows // TOK
@@ -191,6 +188,15 @@
         return 0
 
     lax.fori_loop(0, scenes, scene_body, 0, unroll=True)
+    back = dot_nt(out_ref[:, : 3 * width], w_ref[:, : 3 * width])
+
+    @pl.when(half == 0)
+    def _():
+        back_own_ref[...] = back if first else before[0][...] + back
+
+    @pl.when(half != 0)
+    def _():
+        back_far_ref[...] = back if first else before[1][...] + back
 
 
 def block_rows(tokens):
@@ -203,27 +209,30 @@
     return [first, second, first, second]
 
 
-ANYWHERE = pl.BlockSpec(memory_space=pl.ANY)
 SCALARS = pl.BlockSpec(memory_space=pltpu.SMEM)
 
 
-def attention_call(counts, owners, na, nb, ga, gb, blocks):
+def attention_call(counts, owners, na, nb, ga, gb, before, blocks):
     tokens = na.shape[0]
     rows = block_rows(tokens)
     steps = tokens // rows
     cols = blocks[0].shape[1]
     whole = lambda a: pl.BlockSpec(a.shape, lambda h, i: (0, 0))
-    return pl.pallas_call(
-        attention_kernel,
+    halves = two_halves(rows, steps)
+    return pl.pallas_call(
+        functools.partial(attention_kernel, not before),
         grid=(2, steps),
-        in_specs=[SCALARS, SCALARS] + two_halves(rows, steps) + [whole(b) for b in blocks],
+        in_specs=[SCALARS, SCALARS] + halves + halves[: len(before)] + [whole(b) for b in blocks],
         out_specs=[
             pl.BlockSpec((rows, cols), lambda h, i: (h * steps + i, 0)),
             pl.BlockSpec((D, cols), lambda h, i: (0, 0)),
-        ],
+        ]
+        + halves[:2],
         out_shape=[
             jax.ShapeDtypeStruct((2 * tokens, cols), BF16),
             jax.ShapeDtypeStruct((D, cols), BF16),
+            jax.ShapeDtypeStruct((tokens, D), F32),
+            jax.ShapeDtypeStruct((tokens, D), F32),
         ],
         scratch_shapes=[
             pltpu.VMEM((rows, D), BF16),
@@ -233,91 +242,105 @@
         compiler_params=params(),
         cost_estimate=cost(20e9, 14e6),
         name="attention",
-    )(counts, owners, na, nb, ga, gb, *blocks)
+    )(counts, owners, na, nb, ga, gb, *before, *blocks)
 
 
 def transpose_kernel(*refs):
-    count = len(refs) // 2
-    for ref, out_ref in zip(refs[:count], refs[count:]):
-        out_ref[...] = ref[...].T
+    out_ref = refs[-1]
+    for k, ref in enumerate(refs[:-1]):
+
+        @pl.when(pl.program_id(0) == k)
+        def _():
+            out_ref[0] = ref[...].T
 
 
 def transpose_call(arrays):
-    shapes = [jax.ShapeDtypeStruct(a.shape[::-1], a.dtype) for a in arrays]
+    rows, cols = arrays[0].shape
     return pl.pallas_call(
         transpose_kernel,
-        out_shape=shapes,
+        grid=(len(arrays),),
+        in_specs=[pl.BlockSpec((rows, cols), lambda i: (0, 0))] * len(arrays),
+        out_specs=pl.BlockSpec((1, cols, rows), lambda i: (i, 0, 0)),
+        out_shape=jax.ShapeDtypeStruct((len(arrays), cols, rows), BF16),
         compiler_params=params(),
         cost_estimate=cost(4e9, 8e6),
         name="transpose_rows",
     )(*arrays)
 
 
-def weight_grad_kernel(deps, blocks, low_ref, na_ref, nb_ref, ga_ref, gb_ref, pack_ref, *refs):
-    send_ref, keep_ref, total = refs[deps:]
-    section_at = pl.program_id(0)
-    tokens = na_ref.shape[1]
-
-    def product(a_ref, b_ref):
-        total[...] = dot_nn(a_ref[...], pack_ref[:tokens, :]) + dot_nn(b_ref[...], pack_ref[tokens:, :])
-
-    pl.when(section_at < 3)(lambda: product(na_ref, nb_ref))
-    pl.when(section_at == 3)(lambda: product(ga_ref, gb_ref))
-    rows = total.shape[0] // blocks
-    low = low_ref[0]
-    for b in range(blocks // 2):
-        at = slice(b * rows, (b + 1) * rows)
-        mine = pl.multiple_of((2 * b + low) * rows, rows)
-        other = pl.multiple_of((2 * b + 1 - low) * rows, rows)
-        keep_ref[at, :] = total[pl.ds(mine, rows), :]
-        send_ref[at, :] = total[pl.ds(other, rows), :].astype(BF16)
-
-
-def weight_grad_call(low, na, nb, ga, gb, pack, blocks, deps=()):
-    width = pack.shape[1] // 4
-    whole = pl.BlockSpec(na.shape, lambda c: (0, 0))
-    out = pl.BlockSpec((D // 2, width), lambda c: (0, c))
-    return pl.pallas_call(
-        functools.partial(weight_grad_kernel, len(deps), blocks),
+def weight_grad_kernel(blocks, low_ref, turned_ref, pack_ref, keep_ref, *refs):
+    sends, total = refs[:-1], refs[-1]
+    step = pl.program_id(0)
+    width = pack_ref.shape[1] // 4
+    parts = [slice(0, 3 * width), slice(3 * width, 4 * width)]
+    for k in range(4):
+
+        @pl.when(step == k)
+        def _():
+            new = dot_nn(turned_ref[0], pack_ref[:, parts[k % 2]])
+            total[:, parts[k % 2]] = new if k < 2 else total[:, parts[k % 2]] + new
+
+    @pl.when(step == 3)
+    def _():
+        rows = total.shape[0] // blocks
+        low = low_ref[0]
+        for b in range(blocks // 2):
+            at = slice(b * rows, (b + 1) * rows)
+            mine = pl.multiple_of((2 * b + low) * rows, rows)
+            other = pl.multiple_of((2 * b + 1 - low) * rows, rows)
+            keep_ref[at, :] = total[pl.ds(mine, rows), :]
+            for c, send_ref in enumerate(sends):
+                cols = send_ref.shape[1]
+                send_ref[at, :] = total[pl.ds(other, rows), c * cols : (c + 1) * cols].astype(BF16)
+
+
+def weight_grad_call(low, turned, pack, blocks):
+    tokens, cols = pack.shape
+    out = lambda cols: pl.BlockSpec((D // 2, cols), lambda i: (0, 0))
+    send = jax.ShapeDtypeStruct((D // 2, cols // 2), BF16)
+    return pl.pallas_call(
+        functools.partial(weight_grad_kernel, blocks),
         grid=(4,),
-        in_specs=[SCALARS]
-        + [whole] * 4
-        + [pl.BlockSpec((pack.shape[0], width), lambda c: (0, c))]
-        + [ANYWHERE] * len(deps),
-        out_specs=[out, out],
-        out_shape=[
-            jax.ShapeDtypeStruct((D // 2, 4 * width), BF16),
-            jax.ShapeDtypeStruct((D // 2, 4 * width), F32),
+        in_specs=[
+            SCALARS,
+            pl.BlockSpec((1,) + turned.shape[1:], lambda i: (i, 0, 0)),
+            pl.BlockSpec((tokens // 2, cols), lambda i: (i // 2, 0)),
         ],
-        scratch_shapes=[pltpu.VMEM((D, width), F32)],
+        out_specs=[out(cols), out(cols // 2), out(cols // 2)],
+        out_shape=[jax.ShapeDtypeStruct((D // 2, cols), F32), send, send],
+        scratch_shapes=[pltpu.VMEM((D, cols), F32)],
         compiler_params=params(),
         cost_estimate=cost(6e9, 12e6),
         name="weight_grad",
-    )(low, na, nb, ga, gb, pack, *deps)
-
-
-def combine_kernel(deps, place_ref, keep_ref, recv_ref, *refs):
-    refs = refs[deps:]
+    )(low, turned, pack)
+
+
+def combine_kernel(pieces, place_ref, keep_ref, *refs):
+    recvs, refs = refs[:pieces], refs[pieces:]
     rows = refs[0].shape[0]
     place = place_ref[0]
     for j, ref in enumerate(refs):
         at = pl.ds(pl.multiple_of((place ^ j) * rows, rows), rows)
-        ref[...] = (keep_ref[at, :] + recv_ref[at, :].astype(F32)).astype(ref.dtype)
-
-
-def combine_call(place, keep, recv, blocks, dtype, deps=()):
+        start = 0
+        for recv_ref in recvs:
+            cols = slice(start, start + recv_ref.shape[1])
+            ref[:, cols] = (keep_ref[at, cols] + recv_ref[at, :].astype(F32)).astype(ref.dtype)
+            start = cols.stop
+
+
+def combine_call(place, keep, recvs, blocks, dtype):
     rows, cols = keep.shape[0] // blocks, keep.shape[1]
     whole = lambda a: pl.BlockSpec(a.shape, lambda: (0, 0))
     shapes = [jax.ShapeDtypeStruct((rows, cols), F32 if j == 0 else dtype) for j in range(blocks)]
     return pl.pallas_call(
-        functools.partial(combine_kernel, len(deps)),
-        in_specs=[SCALARS, whole(keep), whole(recv)] + [ANYWHERE] * len(deps),
+        functools.partial(combine_kernel, len(recvs)),
+        in_specs=[SCALARS, whole(keep)] + [whole(r) for r in recvs],
         out_specs=[pl.BlockSpec((rows, cols), lambda: (0, 0))] * blocks,
         out_shape=shapes,
         compiler_params=params(),
         cost_estimate=cost(1e6, 5e6),
         name="combine",
-    )(place, keep, recv, *deps)
+    )(place, keep, *recvs)
 
 
 def add_kernel(count, *refs):
@@ -327,62 +350,54 @@
     refs[-1][...] = total
 
 
-def add_call(parts, deps=()):
+def add_call(parts):
     spec = pl.BlockSpec(parts[0].shape, lambda: (0, 0))
     return pl.pallas_call(
         functools.partial(add_kernel, len(parts)),
-        in_specs=[spec] * len(parts) + [ANYWHERE] * len(deps),
+        in_specs=[spec] * len(parts),
         out_specs=spec,
         out_shape=jax.ShapeDtypeStruct(parts[0].shape, F32),
         compiler_params=params(),
         cost_estimate=cost(1e6, 2e6),
         name="add_parts",
-    )(*parts, *deps)
-
-
-def back_product(pack_refs, weight_refs, start, first, count):
+    )(*parts)
+
+
+def mixed_product(context_refs, weight_refs):
     total = None
-    for pack_ref, w_ref in zip(pack_refs, weight_refs):
-        width = w_ref.shape[1] // 4
-        columns = pack_ref[:, (first - start) * width : (first - start + count) * width]
-        new = dot_nt(columns, w_ref[:, first * width : (first + count) * width])
+    for context_ref, w_ref in zip(context_refs, weight_refs):
+        new = dot_nt(context_ref[...], w_ref[...])
         total = new if total is None else total + new
     return total
 
 
-def weight_specs(weights):
-    return [pl.BlockSpec(w.shape, lambda i: (0, 0)) for w in weights]
-
-
-def back_kernel(count, *refs):
-    packs, weights = refs[:count], refs[count : 2 * count]
-    grad_ref, mixed_ref = refs[-2:]
-    grad_ref[...] = back_product(packs, weights, 0, 0, 3)
-    mixed_ref[...] = back_product(packs, weights, 0, 3, 1).astype(BF16)
-
-
-def back_call(packs, weights, half, deps=()):
+def context_specs(rows, packs, weights, first):
+    width = packs[0].shape[1] // 4
+    return [pl.BlockSpec((rows, width), lambda i: (first + i, 3))] * len(packs) + [
+        pl.BlockSpec((D, width), lambda i: (0, 3))
+    ] * len(weights)
+
+
+def mixed_kernel(count, *refs):
+    refs[-1][...] = mixed_product(refs[:count], refs[count : 2 * count]).astype(BF16)
+
+
+def mixed_call(packs, weights):
     tokens = packs[0].shape[0] // 2
     rows = block_rows(tokens)
-    steps = tokens // rows
-    out = pl.BlockSpec((rows, D), lambda i: (i, 0))
-    return pl.pallas_call(
-        functools.partial(back_kernel, len(packs)),
-        grid=(steps,),
-        in_specs=[pl.BlockSpec((rows, p.shape[1]), lambda i: (half * steps + i, 0)) for p in packs]
-        + weight_specs(weights)
-        + [ANYWHERE] * len(deps),
-        out_specs=[out, out],
-        out_shape=[jax.ShapeDtypeStruct((tokens, D), F32), jax.ShapeDtypeStruct((tokens, D), BF16)],
-        compiler_params=params(),
-        cost_estimate=cost(10e9, 12e6),
-        name="back",
-    )(*packs, *weights, *deps)
-
-
-def tail_kernel(count, core_ref, recv_ref, emb_ref, gl_ref, cols_ref, gain_ref, *refs):
-    packs, weights = refs[:count], refs[count : 2 * count]
-    send_ref, keep_ref, acc = refs[-3:]
+    return pl.pallas_call(
+        functools.partial(mixed_kernel, len(packs)),
+        grid=(tokens // rows,),
+        in_specs=context_specs(rows, packs, weights, tokens // rows),
+        out_specs=pl.BlockSpec((rows, D), lambda i: (i, 0)),
+        out_shape=jax.ShapeDtypeStruct((tokens, D), BF16),
+        compiler_params=params(),
+        cost_estimate=cost(2e9, 5e6),
+        name="mixed",
+    )(*packs, *weights)
+
+
+def tail_kernel(core_ref, own_ref, recv_ref, emb_ref, gl_ref, cols_ref, gain_ref, send_ref, keep_ref, acc):
     step = pl.program_id(0)
     rows = emb_ref.shape[0]
     scenes = rows // TOK
@@ -391,7 +406,7 @@
     def _():
         acc[...] = jnp.zeros_like(acc)
 
-    grad_normed = recv_ref[...] + back_product(packs, weights, 0, 0, 3)
+    grad_normed = own_ref[...] + recv_ref[...]
     x = emb_ref[...].astype(F32)
     dev = x - jnp.mean(x, axis=-1, keepdims=True)
     inv_std = lax.rsqrt(jnp.mean(dev * dev, axis=-1, keepdims=True) + NORM_EPS)
@@ -415,34 +430,31 @@
         send_ref[...] = acc[pl.ds(pl.multiple_of((1 - core) * size, size), size), :]
 
 
-def tail_call(core, recv, emb, gl, cols, gain, packs, weights, deps=()):
+def tail_call(core, own, recv, emb, gl, cols, gain):
     tokens = emb.shape[0]
-    rows = block_rows(tokens)
+    rows = 2 * TOK if tokens % (2 * TOK) == 0 else TOK
     per = lambda a: pl.BlockSpec((rows, a.shape[1]), lambda i: (i, 0))
     stem_rows = GROUP_BANDS[-1][1] * PIX
     half = jax.ShapeDtypeStruct((stem_rows // 2, D), F32)
     return pl.pallas_call(
-        functools.partial(tail_kernel, len(packs)),
+        tail_kernel,
         grid=(tokens // rows,),
-        in_specs=[SCALARS, per(recv), per(emb), per(gl), per(cols)]
-        + [pl.BlockSpec(gain.shape, lambda i: (0, 0))]
-        + [pl.BlockSpec((rows, 3 * (p.shape[1] // 4)), lambda i: (i, 0)) for p in packs]
-        + weight_specs(weights)
-        + [ANYWHERE] * len(deps),
+        in_specs=[SCALARS, per(own), per(recv), per(emb), per(gl), per(cols)]
+        + [pl.BlockSpec(gain.shape, lambda i: (0, 0))],
         out_specs=[pl.BlockSpec(half.shape, lambda i: (0, 0))] * 2,
         out_shape=[half, half],
         scratch_shapes=[pltpu.VMEM((stem_rows, D), F32)],
         compiler_params=params(),
         cost_estimate=cost(10e9, 12e6),
         name="tail",
-    )(core, recv, emb, gl, cols, gain, *packs, *weights, *deps)
+    )(core, own, recv, emb, gl, cols, gain)
 
 
 def output_kernel(count, cnt_ref, recv_ref, emb_ref, *refs):
-    packs, weights, out_ref = refs[:count], refs[count : 2 * count], refs[-1]
+    out_ref = refs[-1]
     step = pl.program_id(0)
     scenes = emb_ref.shape[0] // TOK
-    mixed = recv_ref[...].astype(F32) + back_product(packs, weights, 3, 3, 1)
+    mixed = recv_ref[...].astype(F32) + mixed_product(refs[:count], refs[count : 2 * count])
     total = emb_ref[...].astype(F32) + mixed
     for s in range(scenes):
         scene = step * scenes + s
@@ -451,7 +463,7 @@
         out_ref[at, :] = jnp.where(live, total[at], 0.0).astype(BF16)
 
 
-def output_call(counts, recv, emb, packs, weights, deps=()):
+def output_call(counts, recv, emb, packs, weights):
     tokens = emb.shape[0]
     rows = block_rows(tokens)
     per = lambda a: pl.BlockSpec((rows, a.shape[1]), lambda i: (i, 0))
@@ -459,15 +471,13 @@
         functools.partial(output_kernel, len(packs)),
         grid=(tokens // rows,),
         in_specs=[SCALARS, per(recv), per(emb)]
-        + [pl.BlockSpec((rows, p.shape[1] // 4), lambda i: (i, 3)) for p in packs]
-        + weight_specs(weights)
-        + [ANYWHERE] * len(deps),
+        + context_specs(rows, packs, weights, 0),
         out_specs=per(emb),
         out_shape=jax.ShapeDtypeStruct(emb.shape, BF16),
         compiler_params=params(),
         cost_estimate=cost(5e9, 10e6),
         name="layer_output",
-    )(counts, recv, emb, *packs, *weights, *deps)
+    )(counts, recv, emb, *packs, *weights)
 
 
 def swap(x, axis, size, bit):
@@ -532,8 +542,8 @@
     hops = [(k // 2, k % 2) for k in range(1, 2 * fars)]
     arrived = [hop(part, f, b) for part, (f, b) in zip(parts[1:], hops)]
     beside = beside()
-    arrived, beside[:2] = together(arrived, beside[:2])
-    near = (len(beside) + 2) // 2
+    arrived, beside[:3] = together(arrived, beside[:3])
+    near = (len(beside) + 3) // 2
     total = parts[0]
     for part in arrived:
         total = total + part
@@ -598,7 +608,7 @@
     gain = ln_gain.reshape(1, D)
     stem = stem_call(
         counts,
-        vis_index.reshape(scenes, TOK, 1),
+        vis_index,
         patches,
         w_stem,
         gain,
@@ -617,7 +627,8 @@
         far.append(cross(ring.ahead[-1]))
         (far[-2],) = ring.step(far[-2])
     far.append(cross(ring.ahead[-1]))
-    turned, far[-2:] = ring.step(transpose_call(both), far[-2:])
+    turned, far[-2] = ring.step(transpose_call([both[0], both[2], both[1], both[3]]), far[-2])
+    ring.ahead, ring.behind = together(ring.ahead, ring.behind)
     far.append(cross(ring.ahead[-1]))
     behind = ring.behind[1:]
     far.append(cross(jnp.concatenate(behind, axis=0)))
@@ -631,7 +642,7 @@
     def rest_swaps(blocks):
         return [blocks[0]] + [swap(blocks[j], "dp", dp, 2 * j) for j in rests]
 
-    weights = []
+    weights, back = [], []
     for n in range(group // 2):
         if n == 0:
             blocks = ring.ahead + behind
@@ -639,42 +650,40 @@
             rows = shard.shape[0]
             last = [far[-1][n - 1][b * rows : (b + 1) * rows] for b in range(len(behind))]
             blocks = [f[n - 1] for f in far[:-1]] + last
-        made = attention_call(both_counts, owners, *both, blocks)
+        made = attention_call(both_counts, owners, *both, back, blocks)
         if n == 0:
-            pack, weight = together(*made)
+            pack, weight, *back = together(*made)
         else:
-            pack, weight, coming[-1] = together(*made, coming[-1])
+            pack, weight, *back, coming[-1] = together(*made, coming[-1])
         packs.append(pack)
         weights.append(weight)
         if n == len(fars):
-            break
-        send, keep = weight_grad_call(low, *turned, pack, dp)
+            back_far = swap(back[1], "group", group, 1)
+        keep, *send = weight_grad_call(low, turned, pack, dp)
         if n == 0:
-            send, keep, far[-2:] = together(send, keep, far[-2:])
-        else:
-            send, keep = together(send, keep)
+            send, keep, far[-3:] = together(send, keep, far[-3:])
+        if n == len(fars):
+            send, keep, back_far, kept, coming = together(send, keep, back_far, kept, coming)
         kept.append(keep)
-        coming.append(swap(send, "dp", dp, 1))
-    back, mixed = together(*back_call(packs, weights, 1))
-    back = swap(back, "group", group, 1)
+        coming.append([swap(x, "dp", dp, 1) for x in send])
+    blocks, back_far = together([first_to_rest(n) for n in range(len(fars))], back_far)
+    landing = [rest_swaps(b) for b in blocks]
+    near = dp // 2 * 3 // 4
+    stem_send, stem_keep, landing[-1][:near], coming[-1][0] = together(
+        *tail_call(core, back[0], back_far, emb, gl, cols, gain), landing[-1][:near], coming[-1][0]
+    )
+    half = stem_send.shape[1] // 2
+    stem_recv = [swap(stem_send[:, c * half : (c + 1) * half], "group", group, 1) for c in range(2)]
+    mixed, stem_recv, landing, coming = together(mixed_call(packs, weights), stem_recv, landing, coming)
     mixed = swap(mixed, "group", group, 1)
-    near = dp // 2 * 3 // 4
-    for n in range(len(fars)):
-        landing.append(rest_swaps(first_to_rest(n)))
-    send, keep = weight_grad_call(low, *turned, packs[-1], dp)
-    send, keep, back, landing[-1][:near] = together(send, keep, back, landing[-1][:near])
-    kept.append(keep)
-    coming.append(swap(send, "dp", dp, 1))
-    stem_send, stem_keep, mixed, landing = together(
-        *tail_call(core, back, emb, gl, cols, gain, packs, weights), mixed, landing
-    )
-    cols = stem_send.shape[1] // 2
-    stem_recv = [swap(stem_send[:, c * cols : (c + 1) * cols], "group", group, 1) for c in range(2)]
-    output, stem_recv, coming[-1] = together(
-        output_call(counts, mixed, emb, packs, weights), stem_recv, coming[-1]
-    )
-    stem_parts = halve_stem(jnp.concatenate(stem_recv, axis=1), stem_keep, group)
-    grad_w_stem, last = sum_stem(stem_parts, lambda: rest_swaps(first_to_rest(-1)), dp, group)
+    stem_parts = halve_stem(stem_recv, stem_keep, group)
+
+    def beside():
+        last = rest_swaps(first_to_rest(-1))
+        output = output_call(counts, mixed, emb, packs, weights)
+        return [output] + last
+
+    grad_w_stem, (output, *last) = sum_stem(stem_parts, beside, dp, group)
     shares = [add_call(parts) for parts in landing + [last]]
 
     total = shares[0]

time: 251 us -> 248 us (0.988)
  local copies, waits for them, and re-layouts: 12.5 us -> 70.5 us
  Pallas kernels: 106 us -> 76.2 us
  waiting for transfers between devices: 74 us -> 44.9 us
  other arithmetic: 7.47 us -> 4.31 us
    unnamed x47 -> x177, local copies, waits for them, and re-layouts: 6.61 us -> 68.5 us
    ppermute x31 -> x33, waiting for transfers between devices: 66.2 us -> 36.5 us  [swap(): return lax.ppermute(x, axis, [(i, i ^ bit) for i in range(size)])]
    pallas_call x10, Pallas kernels: 88.4 us -> 64.8 us  [the longest x2 38.1 us: attention_call(): pl.pallas_call(functools.partial(attention_kernel, not before), grid=(2,...]
    ppermute x31 -> x33, starting transfers between devices: 35.5 us -> 35.1 us  [swap(): return lax.ppermute(x, axis, [(i, i ^ bit) for i in range(size)])]
  transfers between devices with their start and end apart: 42 -> 44, of which waited for: 15 -> 14; matrix products, arithmetic and copies ran while one was open for 4% -> 2% of each run, Pallas kernels for 38% -> 31%
where the time goes in v5:
time: 248 us; the launch traced here: 247 us
  Pallas kernels  76.2 us (31%)
  local copies, waits for them, and re-layouts  70.5 us (28%)
  starting transfers between devices  49.4 us (20%)
  waiting for transfers between devices  44.9 us (18%)
  other arithmetic  4.31 us (2%)
    unnamed x177, local copies, waits for them, and re-layouts  68.5 us
    pallas_call x2, Pallas kernels, attention_call(): pl.pallas_call(functools.partial(attention_kernel, not before), grid=(2,...  38.1 us
    ppermute x33, waiting for transfers between devices, swap(): return lax.ppermute(x, axis, [(i, i ^ bit) for i in range(size)])  36.5 us
    ppermute x33, starting transfers between devices, swap(): return lax.ppermute(x, axis, [(i, i ^ bit) for i in range(size)])  35.1 us
    pallas_call x2, Pallas kernels, weight_grad_call(): pl.pallas_call(functools.partial(weight_grad_kernel, blocks), grid=(4,),...  12.6 us
    ppermute x4, starting transfers between devices, step(): ahead = lax.ppermute(self.ahead[-1], self.axis, self.forward)  7.86 us
    ppermute x4, starting transfers between devices, hop(): return lax.ppermute(block, ('dp', 'group'), pairs)  5.55 us
    pallas_call x1, Pallas kernels, stem_call(): pl.pallas_call(stem_kernel, grid=(scenes // block,), in_specs=[pl.BlockSp...  5.33 us
  transfers between devices with their start and end apart: 44, of which 14 were waited for; matrix products, arithmetic and copies ran while one was open for 2% of the time, Pallas kernels for 31%

profile of v5, /device:TPU:0, one launch (start us, length us, event | category | flops | bytes accessed | tf_op | source)
XLA Modules:
  0.0 246.5 jit_solution(8743813112300143469)
XLA Ops:
  3.0 3.1 %collective-permute-start = (bf16[128,1024]{1,0:T(8,128)(2,1)S(1)}, bf16[128,1024]{1,0:T(8,128)(2,1)S(1)}, u32[]{:S(2)}, u32[]{:S(2)}) collective-permute-start(bf16[128,1024]{1,0:T(8,128)(2,1)S(1)} %pad_maximum_fusion.1.refs_0_), channel_id=1, source_target_pairs={{0,8},{8,16},{16,24},{24,28},{28,20},{20,12},{12,4},{4,0},{1,9},{9... | collective-permute-start | bytes 786440 | tf_op jit(solution)/shard_map/ppermute | solution.py:500
  12.8 5.3 %stem_norm.1 = (bf16[6,144,1024]{2,1,0:T(8,128)(2,1)S(1)}, bf16[6,144,1024]{2,1,0:T(8,128)(2,1)S(1)}, bf16[6,144,1024]{2,1,0:T(8,128)(2,1)S(1)}, bf16[6,144,256]{2,1,0:T(8,128)(2,1)S(1)}) custom-call(s32[6,3]{1,0:T(8,128)S(1)} %copy.48.cnt_ref, s32[6,3,48]{2,1,0:T(4,128)S(1)} %copy-done.76, bf16[6,144,640]{2,1,0:T(8,128)(2,1)S(1)} %copy-done.37, ...), custom_call_target="tpu_custom_call" | custom-call | flops 8000000 | bytes 12000 | tf_op jit(solution)/shard_map/stem_norm/pallas_call | solution.py:99
  20.9 1.9 collective-permute-start.7
  24.8 4.9 %collective-permute-done.7.refs_2_ = bf16[128,1024]{1,0:T(8,128)(2,1)S(1)} collective-permute-done((bf16[128,1024]{1,0:T(8,128)(2,1)S(1)}, bf16[128,1024]{1,0:T(8,128)(2,1)S(1)}, u32[]{:S(2)}, u32[]{:S(2)}) %collective-permute-start.7) | collective-permute-done | bytes 262176 | tf_op jit(solution)/shard_map/ppermute | solution.py:484
  35.1 3.8 %collective-permute-done.10.refs_3_ = bf16[128,1024]{1,0:T(8,128)(2,1)S(1)} collective-permute-done((bf16[128,1024]{1,0:T(8,128)(2,1)S(1)}, bf16[128,1024]{1,0:T(8,128)(2,1)S(1)}, u32[]{:S(2)}, u32[]{:S(2)}) %collective-permute-start.10) | collective-permute-done | bytes 262176 | tf_op jit(solution)/shard_map/ppermute | solution.py:484
  42.6 2.2 transpose_rows.1.turned_ref
  44.9 2.9 %copy-done = bf16[4,1024,864]{2,1,0:T(8,128)(2,1)} copy-done((bf16[4,1024,864]{2,1,0:T(8,128)(2,1)}, bf16[4,1024,864]{2,1,0:T(8,128)(2,1)S(1)}, u32[]{:S(2)}) %copy-start) | copy-done | bytes 7077912
  63.2 18.3 %attention.2 = (bf16[1728,1024]{1,0:T(8,128)(2,1)S(1)}, bf16[1024,1024]{1,0:T(8,128)(2,1)S(1)}, f32[864,1024]{1,0:T(8,128)S(1)}, f32[864,1024]{1,0:T(8,128)}) custom-call(s32[2,6,3]{2,1,0:T(8,128)S(1)} %pad_add_fusion.cnt_ref, s32[8]{0:T(128)S(1)} %compare_select_fusion.2.owner_ref, bf16[864,1024]{1,0:T(8,128)(2,1)S(1)} %bitcast.25, ...), custom_call_target="tpu_custom_call" | custom-call | flops 20000000 | bytes 14000 | tf_op jit(solution)/shard_map/attention/pallas_call | solution.py:222
  84.6 6.4 %weight_grad.2 = (f32[512,1024]{1,0:T(8,128)S(1)}, bf16[512,512]{1,0:T(8,128)(2,1)}, bf16[512,512]{1,0:T(8,128)(2,1)}) custom-call(s32[1]{0:T(128)} %bitcast.10.low_ref, bf16[4,1024,864]{2,1,0:T(8,128)(2,1)S(1)} %copy-done.1, bf16[1728,1024]{1,0:T(8,128)(2,1)S(1)} %get-tuple-element.156.pack_ref.refs_0_), custom_call_target="tpu_custom_call" | custom-call | flops 6000000 | bytes 12000 | tf_op jit(solution)/shard_map/weight_grad/pallas_call | solution.py:301
  95.7 19.8 %attention.3 = (bf16[1728,1024]{1,0:T(8,128)(2,1)S(1)}, bf16[1024,1024]{1,0:T(8,128)(2,1)S(1)}, f32[864,1024]{1,0:T(8,128)S(1)}, f32[864,1024]{1,0:T(8,128)}) custom-call(s32[2,6,3]{2,1,0:T(8,128)S(1)} %pad_add_fusion.cnt_ref, s32[8]{0:T(128)S(1)} %compare_select_fusion.2.owner_ref, bf16[864,1024]{1,0:T(8,128)(2,1)S(1)} %bitcast.26, ...), custom_call_target="tpu_custom_call" | custom-call | flops 20000000 | bytes 14000 | tf_op jit(solution)/shard_map/attention/pallas_call | solution.py:222
  120.6 2.0 copy-done.3
  122.5 6.2 %weight_grad.3 = (f32[512,1024]{1,0:T(8,128)S(1)}, bf16[512,512]{1,0:T(8,128)(2,1)}, bf16[512,512]{1,0:T(8,128)(2,1)S(1)}) custom-call(s32[1]{0:T(128)} %bitcast.10.low_ref, bf16[4,1024,864]{2,1,0:T(8,128)(2,1)S(1)} %copy-done.1, bf16[1728,1024]{1,0:T(8,128)(2,1)S(1)} %copy-done.3), custom_call_target="tpu_custom_call" | custom-call | flops 6000000 | bytes 12000 | tf_op jit(solution)/shard_map/weight_grad/pallas_call | solution.py:301
  133.3 2.1 combine.3
  138.6 2.6 %collective-permute-start.20 = (bf16[128,1024]{1,0:T(8,128)(2,1)}, bf16[128,1024]{1,0:T(8,128)(2,1)}, u32[]{:S(2)}, u32[]{:S(2)}) collective-permute-start(bf16[128,1024]{1,0:T(8,128)(2,1)} %get-tuple-element.193), channel_id=1, source_target_pairs={{0,16},{4,20},{8,24},{12,28},{16,0},{20,4},{24,8},{28,12},{1,17},{... | collective-permute-start | bytes 786440 | tf_op jit(solution)/shard_map/ppermute | solution.py:484
  144.1 2.0 copy-done.26
  146.1 2.0 copy-done.28
  149.1 4.3 %tail.1 = (f32[320,1024]{1,0:T(8,128)S(1)}, f32[320,1024]{1,0:T(8,128)S(1)}) custom-call(s32[1]{0:T(128)} %bitcast.1.core_ref, f32[864,1024]{1,0:T(8,128)S(1)} %copy-done.26, f32[864,1024]{1,0:T(8,128)S(1)} %copy-done.28, bf16[864,1024]{1,0:T(8,128)(2,1)S(1)} %bitcast.27, bf16[864,1024]{1,0:T(8,128)(2,1)S(1)} %bitcast.22, bf16[864,256]{1,0:T(8,128)(2,1)S(1)} %bitcast.30, ...), custom_call_target="tpu_custom_call" | custom-call | flops 10000000 | bytes 12000 | tf_op jit(solution)/shard_map/tail/pallas_call | solution.py:439
  155.6 2.3 collective-permute-start.24
  157.9 2.5 %mixed.1 = bf16[864,1024]{1,0:T(8,128)(2,1)} custom-call(bf16[1728,1024]{1,0:T(8,128)(2,1)S(1)} %get-tuple-element.156.pack_ref.refs_0_, bf16[1728,1024]{1,0:T(8,128)(2,1)S(1)} %copy-done.4, bf16[1024,1024]{1,0:T(8,128)(2,1)S(1)} %copy-done.16, bf16[1024,1024]{1,0:T(8,128)(2,1)S(1)} %copy-done.19), custom_call_target="tpu_custom_call" | custom-call | flops 2000000 | bytes 5000 | tf_op jit(solution)/shard_map/mixed/pallas_call | solution.py:388
  160.4 5.0 %collective-permute-done.24.refs_3_ = bf16[128,1024]{1,0:T(8,128)(2,1)S(1)} collective-permute-done((bf16[128,1024]{1,0:T(8,128)(2,1)S(1)}, bf16[128,1024]{1,0:T(8,128)(2,1)S(1)}, u32[]{:S(2)}, u32[]{:S(2)}) %collective-permute-start.24) | collective-permute-done | bytes 262176 | tf_op jit(solution)/shard_map/ppermute | solution.py:484
  166.2 2.6 %collective-permute-done.25.refs_1_ = bf16[512,512]{1,0:T(8,128)(2,1)S(1)} collective-permute-done((bf16[512,512]{1,0:T(8,128)(2,1)S(1)}, bf16[512,512]{1,0:T(8,128)(2,1)S(1)}, u32[]{:S(2)}, u32[]{:S(2)}) %collective-permute-start.25) | collective-permute-done | bytes 524320 | tf_op jit(solution)/shard_map/ppermute | solution.py:484
  179.5 1.9 combine.5
  183.6 2.0 collective-permute-start.30
  186.1 2.0 copy-done.5
  192.8 3.8 %layer_output.1 = bf16[864,1024]{1,0:T(8,128)(2,1)} custom-call(s32[6,3]{1,0:T(8,128)S(1)} %copy.48.cnt_ref, bf16[864,1024]{1,0:T(8,128)(2,1)} %collective-permute-done.29.recv_ref, bf16[864,1024]{1,0:T(8,128)(2,1)S(1)} %bitcast.28, bf16[1728,1024]{1,0:T(8,128)(2,1)S(1)} %get-tuple-element.156.pack_ref.refs_0_, bf16[1728,1024]{1,0:T(8,128)(2,1)S(1)} %copy-done.5, ...), custom_call_target="tpu_custom_call" | custom-call | flops 5000000 | bytes 10000 | tf_op jit(solution)/shard_map/layer_output/pallas_call | solution.py:470
  202.5 2.4 collective-permute-start.38
  204.9 9.2 %collective-permute-done.32 = f32[80,256]{1,0:T(8,128)S(1)} collective-permute-done((f32[80,256]{1,0:T(8,128)S(1)}, f32[80,256]{1,0:T(8,128)S(1)}, u32[]{:S(2)}, u32[]{:S(2)}) %collective-permute-start.32) | collective-permute-done | bytes 81952 | tf_op jit(solution)/shard_map/ppermute | solution.py:484
  214.1 2.4 collective-permute-start.35
  217.0 1.9 collective-permute-start.37
  218.9 4.4 %collective-permute-done.36 = bf16[80,256]{1,0:T(8,128)(2,1)S(1)} collective-permute-done((bf16[80,256]{1,0:T(8,128)(2,1)S(1)}, bf16[80,256]{1,0:T(8,128)(2,1)S(1)}, u32[]{:S(2)}, u32[]{:S(2)}) %collective-permute-start.36) | collective-permute-done | bytes 40992 | tf_op jit(solution)/shard_map/ppermute | solution.py:484
  231.3 4.2 %collective-permute-done.41 = bf16[80,1024]{1,0:T(8,128)(2,1)S(1)} collective-permute-done((bf16[80,1024]{1,0:T(8,128)(2,1)S(1)}, bf16[80,1024]{1,0:T(8,128)(2,1)S(1)}, u32[]{:S(2)}, u32[]{:S(2)}) %collective-permute-start.41) | collective-permute-done | bytes 163872 | tf_op jit(solution)/shard_map/ppermute | solution.py:539
  236.8 5.8 %collective-permute-done.43 = f32[128,1024]{1,0:T(8,128)S(1)} collective-permute-done((f32[128,1024]{1,0:T(8,128)S(1)}, f32[128,1024]{1,0:T(8,128)S(1)}, u32[]{:S(2)}, u32[]{:S(2)}) %collective-permute-start.43) | collective-permute-done | bytes 524320 | tf_op jit(solution)/shard_map/ppermute | solution.py:484
  (274 shorter events, 103.0 us)
Async XLA Ops:
  3.0 17.2 %collective-permute-start = (bf16[128,1024]{1,0:T(8,128)(2,1)S(1)}, bf16[128,1024]{1,0:T(8,128)(2,1)S(1)}, u32[]{:S(2)}, u32[]{:S(2)}) collective-permute-start(bf16[128,1024]{1,0:T(8,128)(2,1)S(1)} %pad_maximum_fusion.1.refs_0_), channel_id=1, source_target_pairs={{0,8},{8,16},{16,24},{24,28},{28,20},{20,12},{12,4},{4,0},{1,9},{9... | collective-permute-start | bytes 786440 | tf_op jit(solution)/shard_map/ppermute | solution.py:500
  6.1 14.1 %collective-permute-start.1 = (bf16[128,1024]{1,0:T(8,128)(2,1)S(1)}, bf16[128,1024]{1,0:T(8,128)(2,1)S(1)}, u32[]{:S(2)}, u32[]{:S(2)}) collective-permute-start(bf16[128,1024]{1,0:T(8,128)(2,1)S(1)} %pad_maximum_fusion.1.refs_0_), channel_id=1, source_target_pairs={{8,0},{16,8},{24,16},{28,24},{20,28},{12,20},{4,12},{0,4},{9,1},{1... | collective-permute-start | bytes 786440 | tf_op jit(solution)/shard_map/ppermute | solution.py:502
  6.1 14.1 %collective-permute-start.2 = (s32[6,3]{0,1:T(4,128)}, s32[6,3]{0,1:T(4,128)S(1)}, u32[]{:S(2)}, u32[]{:S(2)}) collective-permute-start(s32[6,3]{0,1:T(4,128)} %param.13), channel_id=1, source_target_pairs={{0,1},{1,0},{2,3},{3,2},{4,5},{5,4},{6,7},{7,6},{8,9},{9,8},{10,11... | collective-permute-start | bytes 224 | tf_op jit(solution)/shard_map/ppermute | solution.py:484
  20.2 12.3 %collective-permute-start.6 = (bf16[864,1024]{1,0:T(8,128)(2,1)S(1)}, bf16[864,1024]{1,0:T(8,128)(2,1)S(1)}, u32[]{:S(2)}, u32[]{:S(2)}) collective-permute-start(bf16[864,1024]{1,0:T(8,128)(2,1)S(1)} %bitcast.18), channel_id=1, source_target_pairs={{0,1},{1,0},{2,3},{3,2},{4,5},{5,4},{6,7},{7,6},{8,9},{9,8},{10,11... | collective-permute-start | bytes 5308424 | tf_op jit(solution)/shard_map/ppermute | solution.py:484
  20.8 11.7 %collective-permute-start.5 = (bf16[864,1024]{1,0:T(8,128)(2,1)S(1)}, bf16[864,1024]{1,0:T(8,128)(2,1)S(1)}, u32[]{:S(2)}, u32[]{:S(2)}) collective-permute-start(bf16[864,1024]{1,0:T(8,128)(2,1)S(1)} %bitcast.23), channel_id=1, source_target_pairs={{0,1},{1,0},{2,3},{3,2},{4,5},{5,4},{6,7},{7,6},{8,9},{9,8},{10,11... | collective-permute-start | bytes 5308424 | tf_op jit(solution)/shard_map/ppermute | solution.py:484
  29.7 9.2 %collective-permute-start.10 = (bf16[128,1024]{1,0:T(8,128)(2,1)S(1)}, bf16[128,1024]{1,0:T(8,128)(2,1)S(1)}, u32[]{:S(2)}, u32[]{:S(2)}) collective-permute-start(bf16[128,1024]{1,0:T(8,128)(2,1)S(1)} %collective-permute-done.refs_1_), channel_id=1, source_target_pairs={{0,2},{1,3},{2,0},{3,1},{4,6},{5,7},{6,4},{7,5},{8,10},{9,11},{10,... | collective-permute-start | bytes 786440 | tf_op jit(solution)/shard_map/ppermute | solution.py:484
  34.6 13.3 %collective-permute-start.12 = (bf16[128,1024]{1,0:T(8,128)(2,1)S(1)}, bf16[128,1024]{1,0:T(8,128)(2,1)S(1)}, u32[]{:S(2)}, u32[]{:S(2)}) collective-permute-start(bf16[128,1024]{1,0:T(8,128)(2,1)S(1)} %collective-permute-done.3.refs_2_), channel_id=1, source_target_pairs={{0,2},{1,3},{2,0},{3,1},{4,6},{5,7},{6,4},{7,5},{8,10},{9,11},{10,... | collective-permute-start | bytes 786440 | tf_op jit(solution)/shard_map/ppermute | solution.py:484
  48.8 43.6 %collective-permute-start.15 = (bf16[384,1024]{1,0:T(8,128)(2,1)}, bf16[384,1024]{1,0:T(8,128)(2,1)}, u32[]{:S(2)}, u32[]{:S(2)}) collective-permute-start(bf16[384,1024]{1,0:T(8,128)(2,1)} %pad_maximum_fusion), channel_id=1, source_target_pairs={{0,2},{1,3},{2,0},{3,1},{4,6},{5,7},{6,4},{7,5},{8,10},{9,11},{10,... | collective-permute-start | bytes 2359304 | tf_op jit(solution)/shard_map/ppermute | solution.py:484
  49.5 42.9 %collective-permute-start.13 = (bf16[128,1024]{1,0:T(8,128)(2,1)}, bf16[128,1024]{1,0:T(8,128)(2,1)}, u32[]{:S(2)}, u32[]{:S(2)}) collective-permute-start(bf16[128,1024]{1,0:T(8,128)(2,1)} %collective-permute-done.8.refs_3_), channel_id=1, source_target_pairs={{0,2},{1,3},{2,0},{3,1},{4,6},{5,7},{6,4},{7,5},{8,10},{9,11},{10,... | collective-permute-start | bytes 786440 | tf_op jit(solution)/shard_map/ppermute | solution.py:484
  51.0 41.4 %collective-permute-start.14 = (bf16[128,1024]{1,0:T(8,128)(2,1)}, bf16[128,1024]{1,0:T(8,128)(2,1)}, u32[]{:S(2)}, u32[]{:S(2)}) collective-permute-start(bf16[128,1024]{1,0:T(8,128)(2,1)} %collective-permute-done.11.refs_4_), channel_id=1, source_target_pairs={{0,2},{1,3},{2,0},{3,1},{4,6},{5,7},{6,4},{7,5},{8,10},{9,11},{10,... | collective-permute-start | bytes 786440 | tf_op jit(solution)/shard_map/ppermute | solution.py:484
  92.4 28.1 %collective-permute-start.16 = (bf16[512,512]{1,0:T(8,128)(2,1)}, bf16[512,512]{1,0:T(8,128)(2,1)}, u32[]{:S(2)}, u32[]{:S(2)}) collective-permute-start(bf16[512,512]{1,0:T(8,128)(2,1)} %get-tuple-element.167), channel_id=1, source_target_pairs={{0,4},{4,0},{8,12},{12,8},{16,20},{20,16},{24,28},{28,24},{1,5},{5... | collective-permute-start | bytes 1572872 | tf_op jit(solution)/shard_map/ppermute | solution.py:484
  93.2 27.4 %collective-permute-start.17 = (bf16[512,512]{1,0:T(8,128)(2,1)}, bf16[512,512]{1,0:T(8,128)(2,1)}, u32[]{:S(2)}, u32[]{:S(2)}) collective-permute-start(bf16[512,512]{1,0:T(8,128)(2,1)} %get-tuple-element.168), channel_id=1, source_target_pairs={{0,4},{4,0},{8,12},{12,8},{16,20},{20,16},{24,28},{28,24},{1,5},{5... | collective-permute-start | bytes 1572872 | tf_op jit(solution)/shard_map/ppermute | solution.py:484
  120.5 10.3 %collective-permute-start.18 = (f32[864,1024]{1,0:T(8,128)}, f32[864,1024]{1,0:T(8,128)S(1)}, u32[]{:S(2)}, u32[]{:S(2)}) collective-permute-start(f32[864,1024]{1,0:T(8,128)} %get-tuple-element.174), channel_id=1, source_target_pairs={{0,1},{1,0},{2,3},{3,2},{4,5},{5,4},{6,7},{7,6},{8,9},{9,8},{10,11... | collective-permute-start | bytes 10616840 | tf_op jit(solution)/shard_map/ppermute | solution.py:484
  132.6 21.0 %collective-permute-start.21 = (bf16[512,512]{1,0:T(8,128)(2,1)}, bf16[512,512]{1,0:T(8,128)(2,1)}, u32[]{:S(2)}, u32[]{:S(2)}) collective-permute-start(bf16[512,512]{1,0:T(8,128)(2,1)} %get-tuple-element.194), channel_id=1, source_target_pairs={{0,4},{4,0},{8,12},{12,8},{16,20},{20,16},{24,28},{28,24},{1,5},{5... | collective-permute-start | bytes 1572872 | tf_op jit(solution)/shard_map/ppermute | solution.py:484
  137.0 16.5 %collective-permute-start.19 = (bf16[128,1024]{1,0:T(8,128)(2,1)}, bf16[128,1024]{1,0:T(8,128)(2,1)}, u32[]{:S(2)}, u32[]{:S(2)}) collective-permute-start(bf16[128,1024]{1,0:T(8,128)(2,1)} %get-tuple-element.192), channel_id=1, source_target_pairs={{0,8},{4,12},{8,0},{12,4},{16,24},{20,28},{24,16},{28,20},{1,9},{5... | collective-permute-start | bytes 786440 | tf_op jit(solution)/shard_map/ppermute | solution.py:484
  138.6 15.0 %collective-permute-start.20 = (bf16[128,1024]{1,0:T(8,128)(2,1)}, bf16[128,1024]{1,0:T(8,128)(2,1)}, u32[]{:S(2)}, u32[]{:S(2)}) collective-permute-start(bf16[128,1024]{1,0:T(8,128)(2,1)} %get-tuple-element.193), channel_id=1, source_target_pairs={{0,16},{4,20},{8,24},{12,28},{16,0},{20,4},{24,8},{28,12},{1,17},{... | collective-permute-start | bytes 786440 | tf_op jit(solution)/shard_map/ppermute | solution.py:484
  154.5 15.1 %collective-permute-start.22 = (f32[320,512]{1,0:T(8,128)S(1)}, f32[320,512]{1,0:T(8,128)S(1)}, u32[]{:S(2)}, u32[]{:S(2)}) collective-permute-start(f32[320,512]{1,0:T(8,128)S(1)} %get-tuple-element.265), channel_id=1, source_target_pairs={{0,1},{1,0},{2,3},{3,2},{4,5},{5,4},{6,7},{7,6},{8,9},{9,8},{10,11... | collective-permute-start | bytes 1966088 | tf_op jit(solution)/shard_map/ppermute | solution.py:484
  154.5 16.0 %collective-permute-start.23 = (f32[320,512]{1,0:T(8,128)S(1)}, f32[320,512]{1,0:T(8,128)S(1)}, u32[]{:S(2)}, u32[]{:S(2)}) collective-permute-start(f32[320,512]{1,0:T(8,128)S(1)} %get-tuple-element.264), channel_id=1, source_target_pairs={{0,1},{1,0},{2,3},{3,2},{4,5},{5,4},{6,7},{7,6},{8,9},{9,8},{10,11... | collective-permute-start | bytes 1966088 | tf_op jit(solution)/shard_map/ppermute | solution.py:484
  155.0 13.8 %collective-permute-start.25 = (bf16[512,512]{1,0:T(8,128)(2,1)S(1)}, bf16[512,512]{1,0:T(8,128)(2,1)S(1)}, u32[]{:S(2)}, u32[]{:S(2)}) collective-permute-start(bf16[512,512]{1,0:T(8,128)(2,1)S(1)} %copy-done.78), channel_id=1, source_target_pairs={{0,4},{4,0},{8,12},{12,8},{16,20},{20,16},{24,28},{28,24},{1,5},{5... | collective-permute-start | bytes 1572872 | tf_op jit(solution)/shard_map/ppermute | solution.py:484
  155.6 9.9 %collective-permute-start.24 = (bf16[128,1024]{1,0:T(8,128)(2,1)S(1)}, bf16[128,1024]{1,0:T(8,128)(2,1)S(1)}, u32[]{:S(2)}, u32[]{:S(2)}) collective-permute-start(bf16[128,1024]{1,0:T(8,128)(2,1)S(1)} %copy-done.83), channel_id=1, source_target_pairs={{0,24},{4,28},{8,16},{12,20},{16,8},{20,12},{24,0},{28,4},{1,25},{... | collective-permute-start | bytes 786440 | tf_op jit(solution)/shard_map/ppermute | solution.py:484
  171.3 14.3 %collective-permute-start.29 = (bf16[864,1024]{1,0:T(8,128)(2,1)}, bf16[864,1024]{1,0:T(8,128)(2,1)}, u32[]{:S(2)}, u32[]{:S(2)}) collective-permute-start(bf16[864,1024]{1,0:T(8,128)(2,1)} %mixed.1), channel_id=1, source_target_pairs={{0,1},{1,0},{2,3},{3,2},{4,5},{5,4},{6,7},{7,6},{8,9},{9,8},{10,11... | collective-permute-start | bytes 5308424 | tf_op jit(solution)/shard_map/ppermute | solution.py:484
  176.0 20.6 %collective-permute-start.26 = (f32[80,1024]{1,0:T(8,128)}, f32[80,1024]{1,0:T(8,128)}, u32[]{:S(2)}, u32[]{:S(2)}) collective-permute-start(f32[80,1024]{1,0:T(8,128)} %get-tuple-element.208), channel_id=1, source_target_pairs={{0,4},{4,0},{8,12},{12,8},{16,20},{20,16},{24,28},{28,24},{1,5},{5... | collective-permute-start | bytes 983048 | tf_op jit(solution)/shard_map/ppermute | solution.py:484
  176.7 19.9 %collective-permute-start.27 = (f32[80,1024]{1,0:T(8,128)}, f32[80,1024]{1,0:T(8,128)}, u32[]{:S(2)}, u32[]{:S(2)}) collective-permute-start(f32[80,1024]{1,0:T(8,128)} %get-tuple-element.209), channel_id=1, source_target_pairs={{0,2},{1,3},{2,0},{3,1},{4,6},{5,7},{6,4},{7,5},{8,10},{9,11},{10,... | collective-permute-start | bytes 983048 | tf_op jit(solution)/shard_map/ppermute | solution.py:539
  178.2 18.5 %collective-permute-start.28 = (f32[80,1024]{1,0:T(8,128)}, f32[80,1024]{1,0:T(8,128)}, u32[]{:S(2)}, u32[]{:S(2)}) collective-permute-start(f32[80,1024]{1,0:T(8,128)} %get-tuple-element.210), channel_id=1, source_target_pairs={{0,6},{1,7},{2,4},{3,5},{4,2},{5,3},{6,0},{7,1},{8,14},{9,15},{10,... | collective-permute-start | bytes 983048 | tf_op jit(solution)/shard_map/ppermute | solution.py:539
  183.6 13.0 %collective-permute-start.30 = (bf16[128,1024]{1,0:T(8,128)(2,1)}, bf16[128,1024]{1,0:T(8,128)(2,1)}, u32[]{:S(2)}, u32[]{:S(2)}) collective-permute-start(bf16[128,1024]{1,0:T(8,128)(2,1)} %get-tuple-element.216), channel_id=1, source_target_pairs={{0,8},{4,12},{8,0},{12,4},{16,24},{20,28},{24,16},{28,20},{1,9},{5... | collective-permute-start | bytes 786440 | tf_op jit(solution)/shard_map/ppermute | solution.py:484
  185.6 19.2 %collective-permute-start.34 = (bf16[128,1024]{1,0:T(8,128)(2,1)}, bf16[128,1024]{1,0:T(8,128)(2,1)}, u32[]{:S(2)}, u32[]{:S(2)}) collective-permute-start(bf16[128,1024]{1,0:T(8,128)(2,1)} %copy-done.81), channel_id=1, source_target_pairs={{0,16},{4,20},{8,24},{12,28},{16,0},{20,4},{24,8},{28,12},{1,17},{... | collective-permute-start | bytes 786440 | tf_op jit(solution)/shard_map/ppermute | solution.py:484
  199.7 14.4 %collective-permute-start.32 = (f32[80,256]{1,0:T(8,128)S(1)}, f32[80,256]{1,0:T(8,128)S(1)}, u32[]{:S(2)}, u32[]{:S(2)}) collective-permute-start(f32[80,256]{1,0:T(8,128)S(1)} %get-tuple-element.270), channel_id=1, source_target_pairs={{0,16},{4,20},{8,24},{12,28},{16,0},{20,4},{24,8},{28,12},{1,17},{... | collective-permute-start | bytes 245768 | tf_op jit(solution)/shard_map/ppermute | solution.py:484
  201.0 13.0 %collective-permute-start.33 = (f32[80,256]{1,0:T(8,128)S(1)}, f32[80,256]{1,0:T(8,128)S(1)}, u32[]{:S(2)}, u32[]{:S(2)}) collective-permute-start(f32[80,256]{1,0:T(8,128)S(1)} %get-tuple-element.269), channel_id=1, source_target_pairs={{0,24},{4,28},{8,16},{12,20},{16,8},{20,12},{24,0},{28,4},{1,25},{... | collective-permute-start | bytes 245768 | tf_op jit(solution)/shard_map/ppermute | solution.py:484
  202.5 16.5 %collective-permute-start.38 = (bf16[128,1024]{1,0:T(8,128)(2,1)S(1)}, bf16[128,1024]{1,0:T(8,128)(2,1)S(1)}, u32[]{:S(2)}, u32[]{:S(2)}) collective-permute-start(bf16[128,1024]{1,0:T(8,128)(2,1)S(1)} %copy-done.80), channel_id=1, source_target_pairs={{0,24},{4,28},{8,16},{12,20},{16,8},{20,12},{24,0},{28,4},{1,25},{... | collective-permute-start | bytes 786440 | tf_op jit(solution)/shard_map/ppermute | solution.py:484
  225.3 10.3 %collective-permute-start.41 = (bf16[80,1024]{1,0:T(8,128)(2,1)S(1)}, bf16[80,1024]{1,0:T(8,128)(2,1)S(1)}, u32[]{:S(2)}, u32[]{:S(2)}) collective-permute-start(bf16[80,1024]{1,0:T(8,128)(2,1)S(1)} %constant_dynamic-update-slice_fusion.4), channel_id=1, source_target_pairs={{0,6},{1,7},{2,4},{3,5},{4,2},{5,3},{6,0},{7,1},{8,14},{9,15},{10,... | collective-permute-start | bytes 491528 | tf_op jit(solution)/shard_map/ppermute | solution.py:539
  228.1 14.6 %collective-permute-start.43 = (f32[128,1024]{1,0:T(8,128)S(1)}, f32[128,1024]{1,0:T(8,128)S(1)}, u32[]{:S(2)}, u32[]{:S(2)}) collective-permute-start(f32[128,1024]{1,0:T(8,128)S(1)} %add_parts.3), channel_id=1, source_target_pairs={{0,2},{1,3},{2,0},{3,1},{4,6},{5,7},{6,4},{7,5},{8,10},{9,11},{10,... | collective-permute-start | bytes 1572872 | tf_op jit(solution)/shard_map/ppermute | solution.py:484
  235.6 9.1 %collective-permute-start.42 = (bf16[320,1024]{1,0:T(8,128)(2,1)S(1)}, bf16[320,1024]{1,0:T(8,128)(2,1)S(1)}, u32[]{:S(2)}, u32[]{:S(2)}) collective-permute-start(bf16[320,1024]{1,0:T(8,128)(2,1)S(1)} %constant_dynamic-update-slice_fusion), channel_id=1, source_target_pairs={{0,1},{1,0},{2,3},{3,2},{4,5},{5,4},{6,7},{7,6},{8,9},{9,8},{10,11... | collective-permute-start | bytes 1966088 | tf_op jit(solution)/shard_map/ppermute | solution.py:484
  (98 other events, 604.6 us)

commit v6 on v5

--- a/solution.py
+++ b/solution.py
@@ -21,7 +21,7 @@
 NORM_EPS = 1e-06
 F32 = jnp.float32
 BF16 = jnp.bfloat16
-VMEM_LIMIT = 36 * 1024 * 1024
+VMEM_LIMIT = 60 * 1024 * 1024
 
 
 def dot_nn(a, b):
@@ -91,7 +91,7 @@
 
 def stem_call(counts, index, patches, w_stem, gain, table, genc, out_grad):
     scenes, patch_count, width = patches.shape
-    block = 3 if scenes % 3 == 0 else 1
+    block = 2 if scenes % 2 == 0 else 1
     col_width = max(e - s for s, e in GROUP_BANDS) * PIX
     per = lambda shape: pl.BlockSpec((block,) + shape, lambda i: (i, 0, 0))
     whole = lambda a: pl.BlockSpec(a.shape, lambda i: (0,) * a.ndim)
@@ -246,21 +246,18 @@
 
 
 def transpose_kernel(*refs):
-    out_ref = refs[-1]
     for k, ref in enumerate(refs[:-1]):
-
-        @pl.when(pl.program_id(0) == k)
-        def _():
-            out_ref[0] = ref[...].T
+        refs[-1][k] = ref[...].T
 
 
 def transpose_call(arrays):
     rows, cols = arrays[0].shape
+    block = cols // 4
     return pl.pallas_call(
         transpose_kernel,
-        grid=(len(arrays),),
-        in_specs=[pl.BlockSpec((rows, cols), lambda i: (0, 0))] * len(arrays),
-        out_specs=pl.BlockSpec((1, cols, rows), lambda i: (i, 0, 0)),
+        grid=(4,),
+        in_specs=[pl.BlockSpec((rows, block), lambda i: (0, i))] * len(arrays),
+        out_specs=pl.BlockSpec((len(arrays), block, rows), lambda i: (0, i, 0)),
         out_shape=jax.ShapeDtypeStruct((len(arrays), cols, rows), BF16),
         compiler_params=params(),
         cost_estimate=cost(4e9, 8e6),
@@ -315,27 +312,29 @@
     )(low, turned, pack)
 
 
-def combine_kernel(pieces, place_ref, keep_ref, *refs):
-    recvs, refs = refs[:pieces], refs[pieces:]
+def combine_kernel(place_ref, keep_ref, first_ref, second_ref, *refs):
     rows = refs[0].shape[0]
     place = place_ref[0]
-    for j, ref in enumerate(refs):
-        at = pl.ds(pl.multiple_of((place ^ j) * rows, rows), rows)
-        start = 0
-        for recv_ref in recvs:
-            cols = slice(start, start + recv_ref.shape[1])
-            ref[:, cols] = (keep_ref[at, cols] + recv_ref[at, :].astype(F32)).astype(ref.dtype)
-            start = cols.stop
+
+    def add(recv_ref):
+        for j, ref in enumerate(refs):
+            at = pl.ds(pl.multiple_of((place ^ j) * rows, rows), rows)
+            ref[...] = (keep_ref[at, :] + recv_ref[at, :].astype(F32)).astype(ref.dtype)
+
+    pl.when(pl.program_id(0) < 2)(lambda: add(first_ref))
+    pl.when(pl.program_id(0) >= 2)(lambda: add(second_ref))
 
 
 def combine_call(place, keep, recvs, blocks, dtype):
     rows, cols = keep.shape[0] // blocks, keep.shape[1]
-    whole = lambda a: pl.BlockSpec(a.shape, lambda: (0, 0))
+    step = cols // 4
+    whole = lambda at: pl.BlockSpec((keep.shape[0], step), lambda c: (0, at(c)))
     shapes = [jax.ShapeDtypeStruct((rows, cols), F32 if j == 0 else dtype) for j in range(blocks)]
     return pl.pallas_call(
-        functools.partial(combine_kernel, len(recvs)),
-        in_specs=[SCALARS, whole(keep)] + [whole(r) for r in recvs],
-        out_specs=[pl.BlockSpec((rows, cols), lambda: (0, 0))] * blocks,
+        combine_kernel,
+        grid=(4,),
+        in_specs=[SCALARS, whole(lambda c: c), whole(lambda c: jnp.minimum(c, 1)), whole(lambda c: jnp.maximum(c - 2, 0))],
+        out_specs=[pl.BlockSpec((rows, step), lambda c: (0, c))] * blocks,
         out_shape=shapes,
         compiler_params=params(),
         cost_estimate=cost(1e6, 5e6),
@@ -343,17 +342,19 @@
     )(place, keep, *recvs)
 
 
-def add_kernel(count, *refs):
+def add_kernel(*refs):
     total = refs[0][...]
-    for ref in refs[1:count]:
+    for ref in refs[1:-1]:
         total = total + ref[...].astype(F32)
     refs[-1][...] = total
 
 
 def add_call(parts):
-    spec = pl.BlockSpec(parts[0].shape, lambda: (0, 0))
-    return pl.pallas_call(
-        functools.partial(add_kernel, len(parts)),
+    rows, cols = parts[0].shape
+    spec = pl.BlockSpec((rows, cols // 4), lambda c: (0, c))
+    return pl.pallas_call(
+        add_kernel,
+        grid=(4,),
         in_specs=[spec] * len(parts),
         out_specs=spec,
         out_shape=jax.ShapeDtypeStruct(parts[0].shape, F32),
@@ -465,7 +466,7 @@
 
 def output_call(counts, recv, emb, packs, weights):
     tokens = emb.shape[0]
-    rows = block_rows(tokens)
+    rows = 2 * TOK if tokens % (2 * TOK) == 0 else TOK
     per = lambda a: pl.BlockSpec((rows, a.shape[1]), lambda i: (i, 0))
     return pl.pallas_call(
         functools.partial(output_kernel, len(packs)),

time: 248 us -> 232 us (0.935)
  local copies, waits for them, and re-layouts: 70.5 us -> 10.9 us
  Pallas kernels: 76.2 us -> 118 us
    unnamed x177 -> x55, local copies, waits for them, and re-layouts: 68.5 us -> 7.84 us
    pallas_call x6, Pallas kernels: 9.58 us -> 26.3 us  [the longest x3 12.4 us: combine_call(): pl.pallas_call(combine_kernel, grid=(4,), in_specs=[SCALARS, whole(lambda...]
    pallas_call x2, Pallas kernels: 12.6 us -> 20.7 us  [weight_grad_call(): pl.pallas_call(functools.partial(weight_grad_kernel, blocks), grid=(4,),...]
    pallas_call x2, Pallas kernels: 38.1 us -> 44.4 us  [attention_call(): pl.pallas_call(functools.partial(attention_kernel, not before), grid=(2,...]
    pallas_call x1, Pallas kernels: 4.26 us -> 9.03 us  [tail_call(): pl.pallas_call(tail_kernel, grid=(tokens // rows,), in_specs=[SCALARS, pe...]
    pallas_call x1, Pallas kernels: 5.33 us -> 8.16 us  [stem_call(): pl.pallas_call(stem_kernel, grid=(scenes // block,), in_specs=[pl.BlockSp...]
    ppermute x33, waiting for transfers between devices: 36.5 us -> 39.1 us  [swap(): return lax.ppermute(x, axis, [(i, i ^ bit) for i in range(size)])]
  transfers between devices with their start and end apart: 44 -> 44, of which waited for: 14 -> 15; matrix products, arithmetic and copies ran while one was open for 2% -> 3% of each run, Pallas kernels for 31% -> 51%
where the time goes in v6:
time: 232 us; the launch traced here: 231 us
  Pallas kernels  118 us (51%)
  starting transfers between devices  50.2 us (22%)
  waiting for transfers between devices  45.7 us (20%)
  local copies, waits for them, and re-layouts  10.9 us (5%)
  other arithmetic  5.27 us (2%)
    pallas_call x2, Pallas kernels, attention_call(): pl.pallas_call(functools.partial(attention_kernel, not before), grid=(2,...  44.4 us
    ppermute x33, waiting for transfers between devices, swap(): return lax.ppermute(x, axis, [(i, i ^ bit) for i in range(size)])  39.1 us
    ppermute x33, starting transfers between devices, swap(): return lax.ppermute(x, axis, [(i, i ^ bit) for i in range(size)])  35.5 us
    pallas_call x2, Pallas kernels, weight_grad_call(): pl.pallas_call(functools.partial(weight_grad_kernel, blocks), grid=(4,),...  20.7 us
    pallas_call x3, Pallas kernels, combine_call(): pl.pallas_call(combine_kernel, grid=(4,), in_specs=[SCALARS, whole(lambda...  12.4 us
    pallas_call x1, Pallas kernels, tail_call(): pl.pallas_call(tail_kernel, grid=(tokens // rows,), in_specs=[SCALARS, pe...  9.03 us
    pallas_call x1, Pallas kernels, stem_call(): pl.pallas_call(stem_kernel, grid=(scenes // block,), in_specs=[pl.BlockSp...  8.16 us
    ppermute x4, starting transfers between devices, step(): ahead = lax.ppermute(self.ahead[-1], self.axis, self.forward)  7.86 us
  transfers between devices with their start and end apart: 44, of which 15 were waited for; matrix products, arithmetic and copies ran while one was open for 3% of the time, Pallas kernels for 51%

profile of v6, /device:TPU:0, one launch (start us, length us, event | category | flops | bytes accessed | tf_op | source)
XLA Modules:
  0.0 231.0 jit_solution(5063622796735352994)
XLA Ops:
  2.9 3.1 %collective-permute-start = (bf16[128,1024]{1,0:T(8,128)(2,1)S(1)}, bf16[128,1024]{1,0:T(8,128)(2,1)}, u32[]{:S(2)}, u32[]{:S(2)}) collective-permute-start(bf16[128,1024]{1,0:T(8,128)(2,1)S(1)} %pad_maximum_fusion.1.refs_0_), channel_id=1, source_target_pairs={{0,8},{8,16},{16,24},{24,28},{28,20},{20,12},{12,4},{4,0},{1,9},{9... | collective-permute-start | bytes 786440 | tf_op jit(solution)/shard_map/ppermute | solution.py:501
  7.3 8.2 %stem_norm.1 = (bf16[6,144,1024]{2,1,0:T(8,128)(2,1)}, bf16[6,144,1024]{2,1,0:T(8,128)(2,1)}, bf16[6,144,1024]{2,1,0:T(8,128)(2,1)}, bf16[6,144,256]{2,1,0:T(8,128)(2,1)}) custom-call(s32[6,3]{1,0:T(8,128)} %copy.48.cnt_ref, s32[6,3,48]{2,1,0:T(4,128)} %idx_ref.1, bf16[6,144,640]{2,1,0:T(8,128)(2,1)} %patch_ref.1, bf16[640,1024]{1,0:T(8,128)(2,1)} %w_ref.1, ...), custom_call_target="tpu_custom_call" | custom-call | flops 8000000 | bytes 12000 | tf_op jit(solution)/shard_map/stem_norm/pallas_call | solution.py:99
  20.1 4.9 %collective-permute-done.7.refs_2_ = bf16[128,1024]{1,0:T(8,128)(2,1)S(1)} collective-permute-done((bf16[128,1024]{1,0:T(8,128)(2,1)S(1)}, bf16[128,1024]{1,0:T(8,128)(2,1)S(1)}, u32[]{:S(2)}, u32[]{:S(2)}) %collective-permute-start.7) | collective-permute-done | bytes 262176 | tf_op jit(solution)/shard_map/ppermute | solution.py:485
  30.4 4.0 %collective-permute-done.10.refs_3_ = bf16[128,1024]{1,0:T(8,128)(2,1)S(1)} collective-permute-done((bf16[128,1024]{1,0:T(8,128)(2,1)}, bf16[128,1024]{1,0:T(8,128)(2,1)S(1)}, u32[]{:S(2)}, u32[]{:S(2)}) %collective-permute-start.10) | collective-permute-done | bytes 262176 | tf_op jit(solution)/shard_map/ppermute | solution.py:485
  38.2 7.2 %transpose_rows.1.turned_ref = bf16[4,1024,864]{2,1,0:T(8,128)(2,1)} custom-call(bf16[864,1024]{1,0:T(8,128)(2,1)} %bitcast.24, bf16[864,1024]{1,0:T(8,128)(2,1)} %bitcast.19, bf16[864,1024]{1,0:T(8,128)(2,1)} %copy-done.1, bf16[864,1024]{1,0:T(8,128)(2,1)} %copy-done), custom_call_target="tpu_custom_call" | custom-call | flops 4000000 | bytes 8000 | tf_op jit(solution)/shard_map/transpose_rows/pallas_call | solution.py:256
  50.4 21.5 %attention.2 = (bf16[1728,1024]{1,0:T(8,128)(2,1)}, bf16[1024,1024]{1,0:T(8,128)(2,1)}, f32[864,1024]{1,0:T(8,128)}, f32[864,1024]{1,0:T(8,128)}) custom-call(s32[2,6,3]{2,1,0:T(8,128)} %pad_add_fusion.cnt_ref, s32[8]{0:T(128)} %compare_select_fusion.2.owner_ref, bf16[864,1024]{1,0:T(8,128)(2,1)} %bitcast.25, bf16[864,1024]{1,0:T(8,128)(2,1)} %copy-done.1, ...), custom_call_target="tpu_custom_call" | custom-call | flops 20000000 | bytes 14000 | tf_op jit(solution)/shard_map/attention/pallas_call | solution.py:222
  71.9 10.3 %weight_grad.2 = (f32[512,1024]{1,0:T(8,128)}, bf16[512,512]{1,0:T(8,128)(2,1)}, bf16[512,512]{1,0:T(8,128)(2,1)}) custom-call(s32[1]{0:T(128)} %bitcast.10.low_ref, bf16[4,1024,864]{2,1,0:T(8,128)(2,1)} %transpose_rows.1.turned_ref, bf16[1728,1024]{1,0:T(8,128)(2,1)} %get-tuple-element.156.pack_ref.refs_0_), custom_call_target="tpu_custom_call" | custom-call | flops 6000000 | bytes 12000 | tf_op jit(solution)/shard_map/weight_grad/pallas_call | solution.py:298
  85.3 22.9 %attention.3 = (bf16[1728,1024]{1,0:T(8,128)(2,1)}, bf16[1024,1024]{1,0:T(8,128)(2,1)}, f32[864,1024]{1,0:T(8,128)}, f32[864,1024]{1,0:T(8,128)}) custom-call(s32[2,6,3]{2,1,0:T(8,128)} %pad_add_fusion.cnt_ref, s32[8]{0:T(128)} %compare_select_fusion.2.owner_ref, bf16[864,1024]{1,0:T(8,128)(2,1)} %bitcast.26, bf16[864,1024]{1,0:T(8,128)(2,1)} %copy-done.1, ...), custom_call_target="tpu_custom_call" | custom-call | flops 20000000 | bytes 14000 | tf_op jit(solution)/shard_map/attention/pallas_call | solution.py:222
  109.1 10.4 %weight_grad.3 = (f32[512,1024]{1,0:T(8,128)}, bf16[512,512]{1,0:T(8,128)(2,1)}, bf16[512,512]{1,0:T(8,128)(2,1)}) custom-call(s32[1]{0:T(128)} %bitcast.10.low_ref, bf16[4,1024,864]{2,1,0:T(8,128)(2,1)} %transpose_rows.1.turned_ref, bf16[1728,1024]{1,0:T(8,128)(2,1)} %get-tuple-element.170.pack_ref.refs_1_), custom_call_target="tpu_custom_call" | custom-call | flops 6000000 | bytes 12000 | tf_op jit(solution)/shard_map/weight_grad/pallas_call | solution.py:298
  120.0 4.6 %combine.3 = (f32[128,1024]{1,0:T(8,128)}, bf16[128,1024]{1,0:T(8,128)(2,1)}, bf16[128,1024]{1,0:T(8,128)(2,1)}, bf16[128,1024]{1,0:T(8,128)(2,1)}) custom-call(s32[1]{0:T(128)} %bitcast.11.place_ref, f32[512,1024]{1,0:T(8,128)} %get-tuple-element.178.keep_ref, bf16[512,512]{1,0:T(8,128)(2,1)} %copy-done.11, bf16[512,512]{1,0:T(8,128)(2,1)} %copy-done.12), custom_call_target="tpu_custom_call" | custom-call | flops 1000 | bytes 5000 | tf_op jit(solution)/shard_map/combine/pallas_call | solution.py:333
  126.0 2.5 %collective-permute-start.20 = (bf16[128,1024]{1,0:T(8,128)(2,1)}, bf16[128,1024]{1,0:T(8,128)(2,1)}, u32[]{:S(2)}, u32[]{:S(2)}) collective-permute-start(bf16[128,1024]{1,0:T(8,128)(2,1)} %get-tuple-element.193), channel_id=1, source_target_pairs={{0,16},{4,20},{8,24},{12,28},{16,0},{20,4},{24,8},{28,12},{1,17},{... | collective-permute-start | bytes 786440 | tf_op jit(solution)/shard_map/ppermute | solution.py:485
  128.5 9.0 %tail.1 = (f32[320,1024]{1,0:T(8,128)}, f32[320,1024]{1,0:T(8,128)}) custom-call(s32[1]{0:T(128)} %bitcast.1.core_ref, f32[864,1024]{1,0:T(8,128)} %get-tuple-element.169.own_ref, f32[864,1024]{1,0:T(8,128)} %copy-done.2, bf16[864,1024]{1,0:T(8,128)(2,1)} %bitcast.27, bf16[864,1024]{1,0:T(8,128)(2,1)} %bitcast.22, bf16[864,256]{1,0:T(8,128)(2,1)} %bitcast.33, ...), custom_call_target="tpu_custom_call" | custom-call | flops 10000000 | bytes 12000 | tf_op jit(solution)/shard_map/tail/pallas_call | solution.py:440
  138.8 2.4 %collective-permute-done.20.refs_2_ = bf16[128,1024]{1,0:T(8,128)(2,1)} collective-permute-done((bf16[128,1024]{1,0:T(8,128)(2,1)}, bf16[128,1024]{1,0:T(8,128)(2,1)}, u32[]{:S(2)}, u32[]{:S(2)}) %collective-permute-start.20) | collective-permute-done | bytes 262176 | tf_op jit(solution)/shard_map/ppermute | solution.py:485
  144.0 2.3 collective-permute-start.24
  146.3 3.7 %mixed.1 = bf16[864,1024]{1,0:T(8,128)(2,1)} custom-call(bf16[1728,1024]{1,0:T(8,128)(2,1)} %get-tuple-element.156.pack_ref.refs_0_, bf16[1728,1024]{1,0:T(8,128)(2,1)} %get-tuple-element.170.pack_ref.refs_1_, bf16[1024,1024]{1,0:T(8,128)(2,1)} %get-tuple-element.196.refs_2_, bf16[1024,1024]{1,0:T(8,128)(2,1)} %get-tuple-element.197.refs_3_), custom_call_target="tpu_custom_call" | custom-call | flops 2000000 | bytes 5000 | tf_op jit(solution)/shard_map/mixed/pallas_call | solution.py:389
  150.0 3.9 %collective-permute-done.24.refs_3_ = bf16[128,1024]{1,0:T(8,128)(2,1)S(1)} collective-permute-done((bf16[128,1024]{1,0:T(8,128)(2,1)S(1)}, bf16[128,1024]{1,0:T(8,128)(2,1)S(1)}, u32[]{:S(2)}, u32[]{:S(2)}) %collective-permute-start.24) | collective-permute-done | bytes 262176 | tf_op jit(solution)/shard_map/ppermute | solution.py:485
  153.9 3.3 %collective-permute-done.25.second_ref = bf16[512,512]{1,0:T(8,128)(2,1)S(1)} collective-permute-done((bf16[512,512]{1,0:T(8,128)(2,1)}, bf16[512,512]{1,0:T(8,128)(2,1)S(1)}, u32[]{:S(2)}, u32[]{:S(2)}) %collective-permute-start.25) | collective-permute-done | bytes 524320 | tf_op jit(solution)/shard_map/ppermute | solution.py:485
  159.1 3.8 %combine.4 = (f32[80,1024]{1,0:T(8,128)}, f32[80,1024]{1,0:T(8,128)}, f32[80,1024]{1,0:T(8,128)}, f32[80,1024]{1,0:T(8,128)}) custom-call(s32[1]{0:T(128)} %bitcast.place_ref, f32[320,1024]{1,0:T(8,128)} %get-tuple-element.195.keep_ref, f32[320,512]{1,0:T(8,128)} %copy-done.8, f32[320,512]{1,0:T(8,128)} %copy-done.9), custom_call_target="tpu_custom_call" | custom-call | flops 1000 | bytes 5000 | tf_op jit(solution)/shard_map/combine/pallas_call | solution.py:333
  166.4 4.0 %combine.5 = (f32[128,1024]{1,0:T(8,128)}, bf16[128,1024]{1,0:T(8,128)(2,1)}, bf16[128,1024]{1,0:T(8,128)(2,1)}, bf16[128,1024]{1,0:T(8,128)(2,1)}) custom-call(s32[1]{0:T(128)} %bitcast.11.place_ref, f32[512,1024]{1,0:T(8,128)} %get-tuple-element.212.keep_ref, bf16[512,512]{1,0:T(8,128)(2,1)} %collective-permute-done.21.first_ref, bf16[512,512]{1,0:T(8,128)(2,1)} %copy-done.10), custom_call_target="tpu_custom_call" | custom-call | flops 1000 | bytes 5000 | tf_op jit(solution)/shard_map/combine/pallas_call | solution.py:333
  171.1 2.2 collective-permute-start.34
  173.3 5.7 %layer_output.1 = bf16[864,1024]{1,0:T(8,128)(2,1)} custom-call(s32[6,3]{1,0:T(8,128)} %copy.48.cnt_ref, bf16[864,1024]{1,0:T(8,128)(2,1)} %copy-done.3, bf16[864,1024]{1,0:T(8,128)(2,1)} %bitcast.28, bf16[1728,1024]{1,0:T(8,128)(2,1)} %get-tuple-element.156.pack_ref.refs_0_, bf16[1728,1024]{1,0:T(8,128)(2,1)} %get-tuple-element.170.pack_ref.refs_1_, ...), custom_call_target="tpu_custom_call" | custom-call | flops 5000000 | bytes 10000 | tf_op jit(solution)/shard_map/layer_output/pallas_call | solution.py:471
  179.0 3.4 %collective-permute-done.30.refs_1_ = bf16[128,1024]{1,0:T(8,128)(2,1)S(1)} collective-permute-done((bf16[128,1024]{1,0:T(8,128)(2,1)}, bf16[128,1024]{1,0:T(8,128)(2,1)S(1)}, u32[]{:S(2)}, u32[]{:S(2)}) %collective-permute-start.30) | collective-permute-done | bytes 262176 | tf_op jit(solution)/shard_map/ppermute | solution.py:485
  182.6 2.8 %collective-permute-start.32 = (f32[80,256]{1,0:T(8,128)S(1)}, f32[80,256]{1,0:T(8,128)S(1)}, u32[]{:S(2)}, u32[]{:S(2)}) collective-permute-start(f32[80,256]{1,0:T(8,128)S(1)} %get-tuple-element.270), channel_id=1, source_target_pairs={{0,16},{4,20},{8,24},{12,28},{16,0},{20,4},{24,8},{28,12},{1,17},{... | collective-permute-start | bytes 245768 | tf_op jit(solution)/shard_map/ppermute | solution.py:485
  186.9 2.2 collective-permute-start.38
  189.2 8.1 %collective-permute-done.32 = f32[80,256]{1,0:T(8,128)S(1)} collective-permute-done((f32[80,256]{1,0:T(8,128)S(1)}, f32[80,256]{1,0:T(8,128)S(1)}, u32[]{:S(2)}, u32[]{:S(2)}) %collective-permute-start.32) | collective-permute-done | bytes 81952 | tf_op jit(solution)/shard_map/ppermute | solution.py:485
  197.3 2.8 %collective-permute-start.35 = (bf16[80,256]{1,0:T(8,128)(2,1)S(1)}, bf16[80,256]{1,0:T(8,128)(2,1)S(1)}, u32[]{:S(2)}, u32[]{:S(2)}) collective-permute-start(bf16[80,256]{1,0:T(8,128)(2,1)S(1)} %get-tuple-element.261), channel_id=1, source_target_pairs={{0,8},{4,12},{8,0},{12,4},{16,24},{20,28},{24,16},{28,20},{1,9},{5... | collective-permute-start | bytes 122888 | tf_op jit(solution)/shard_map/ppermute | solution.py:485
  203.1 2.9 %collective-permute-done.36 = bf16[80,256]{1,0:T(8,128)(2,1)S(1)} collective-permute-done((bf16[80,256]{1,0:T(8,128)(2,1)S(1)}, bf16[80,256]{1,0:T(8,128)(2,1)S(1)}, u32[]{:S(2)}, u32[]{:S(2)}) %collective-permute-start.36) | collective-permute-done | bytes 40992 | tf_op jit(solution)/shard_map/ppermute | solution.py:485
  208.9 2.2 collective-permute-start.41
  211.1 3.4 %add_parts.3 = f32[128,1024]{1,0:T(8,128)} custom-call(f32[128,1024]{1,0:T(8,128)} %get-tuple-element.240.refs_0_, bf16[128,1024]{1,0:T(8,128)(2,1)} %copy-done.19, bf16[128,1024]{1,0:T(8,128)(2,1)} %collective-permute-done.34.refs_2_, bf16[128,1024]{1,0:T(8,128)(2,1)} %copy-done.20), custom_call_target="tpu_custom_call" | custom-call | flops 1000 | bytes 2000 | tf_op jit(solution)/shard_map/add_parts/pallas_call | solution.py:355
  215.8 3.4 %collective-permute-done.41 = bf16[80,1024]{1,0:T(8,128)(2,1)S(1)} collective-permute-done((bf16[80,1024]{1,0:T(8,128)(2,1)S(1)}, bf16[80,1024]{1,0:T(8,128)(2,1)S(1)}, u32[]{:S(2)}, u32[]{:S(2)}) %collective-permute-start.41) | collective-permute-done | bytes 163872 | tf_op jit(solution)/shard_map/ppermute | solution.py:540
  219.3 3.3 %add_parts.2 = f32[128,1024]{1,0:T(8,128)} custom-call(f32[128,1024]{1,0:T(8,128)} %get-tuple-element.236.refs_0_, bf16[128,1024]{1,0:T(8,128)(2,1)} %collective-permute-done.19.refs_1_, bf16[128,1024]{1,0:T(8,128)(2,1)} %collective-permute-done.20.refs_2_, bf16[128,1024]{1,0:T(8,128)(2,1)} %copy-done.18), custom_call_target="tpu_custom_call" | custom-call | flops 1000 | bytes 2000 | tf_op jit(solution)/shard_map/add_parts/pallas_call | solution.py:355
  222.6 3.5 %collective-permute-done.43 = f32[128,1024]{1,0:T(8,128)S(1)} collective-permute-done((f32[128,1024]{1,0:T(8,128)}, f32[128,1024]{1,0:T(8,128)S(1)}, u32[]{:S(2)}, u32[]{:S(2)}) %collective-permute-start.43) | collective-permute-done | bytes 524320 | tf_op jit(solution)/shard_map/ppermute | solution.py:485
  (152 shorter events, 52.3 us)
Async XLA Ops:
  2.9 12.6 %collective-permute-start = (bf16[128,1024]{1,0:T(8,128)(2,1)S(1)}, bf16[128,1024]{1,0:T(8,128)(2,1)}, u32[]{:S(2)}, u32[]{:S(2)}) collective-permute-start(bf16[128,1024]{1,0:T(8,128)(2,1)S(1)} %pad_maximum_fusion.1.refs_0_), channel_id=1, source_target_pairs={{0,8},{8,16},{16,24},{24,28},{28,20},{20,12},{12,4},{4,0},{1,9},{9... | collective-permute-start | bytes 786440 | tf_op jit(solution)/shard_map/ppermute | solution.py:501
  5.9 9.5 %collective-permute-start.1 = (bf16[128,1024]{1,0:T(8,128)(2,1)S(1)}, bf16[128,1024]{1,0:T(8,128)(2,1)S(1)}, u32[]{:S(2)}, u32[]{:S(2)}) collective-permute-start(bf16[128,1024]{1,0:T(8,128)(2,1)S(1)} %pad_maximum_fusion.1.refs_0_), channel_id=1, source_target_pairs={{8,0},{16,8},{24,16},{28,24},{20,28},{12,20},{4,12},{0,4},{9,1},{1... | collective-permute-start | bytes 786440 | tf_op jit(solution)/shard_map/ppermute | solution.py:503
  5.9 9.5 %collective-permute-start.2 = (s32[6,3]{0,1:T(4,128)}, s32[6,3]{0,1:T(4,128)S(1)}, u32[]{:S(2)}, u32[]{:S(2)}) collective-permute-start(s32[6,3]{0,1:T(4,128)} %param.13), channel_id=1, source_target_pairs={{0,1},{1,0},{2,3},{3,2},{4,5},{5,4},{6,7},{7,6},{8,9},{9,8},{10,11... | collective-permute-start | bytes 224 | tf_op jit(solution)/shard_map/ppermute | solution.py:485
  15.5 12.3 %collective-permute-start.6 = (bf16[864,1024]{1,0:T(8,128)(2,1)}, bf16[864,1024]{1,0:T(8,128)(2,1)S(1)}, u32[]{:S(2)}, u32[]{:S(2)}) collective-permute-start(bf16[864,1024]{1,0:T(8,128)(2,1)} %bitcast.18), channel_id=1, source_target_pairs={{0,1},{1,0},{2,3},{3,2},{4,5},{5,4},{6,7},{7,6},{8,9},{9,8},{10,11... | collective-permute-start | bytes 5308424 | tf_op jit(solution)/shard_map/ppermute | solution.py:485
  16.1 11.7 %collective-permute-start.5 = (bf16[864,1024]{1,0:T(8,128)(2,1)}, bf16[864,1024]{1,0:T(8,128)(2,1)S(1)}, u32[]{:S(2)}, u32[]{:S(2)}) collective-permute-start(bf16[864,1024]{1,0:T(8,128)(2,1)} %bitcast.23), channel_id=1, source_target_pairs={{0,1},{1,0},{2,3},{3,2},{4,5},{5,4},{6,7},{7,6},{8,9},{9,8},{10,11... | collective-permute-start | bytes 5308424 | tf_op jit(solution)/shard_map/ppermute | solution.py:485
  25.0 9.4 %collective-permute-start.10 = (bf16[128,1024]{1,0:T(8,128)(2,1)}, bf16[128,1024]{1,0:T(8,128)(2,1)S(1)}, u32[]{:S(2)}, u32[]{:S(2)}) collective-permute-start(bf16[128,1024]{1,0:T(8,128)(2,1)} %collective-permute-done.refs_1_), channel_id=1, source_target_pairs={{0,2},{1,3},{2,0},{3,1},{4,6},{5,7},{6,4},{7,5},{8,10},{9,11},{10,... | collective-permute-start | bytes 786440 | tf_op jit(solution)/shard_map/ppermute | solution.py:485
  29.9 15.5 %collective-permute-start.12 = (bf16[128,1024]{1,0:T(8,128)(2,1)}, bf16[128,1024]{1,0:T(8,128)(2,1)}, u32[]{:S(2)}, u32[]{:S(2)}) collective-permute-start(bf16[128,1024]{1,0:T(8,128)(2,1)} %collective-permute-done.3.refs_2_), channel_id=1, source_target_pairs={{0,2},{1,3},{2,0},{3,1},{4,6},{5,7},{6,4},{7,5},{8,10},{9,11},{10,... | collective-permute-start | bytes 786440 | tf_op jit(solution)/shard_map/ppermute | solution.py:485
  46.4 35.8 %collective-permute-start.15 = (bf16[384,1024]{1,0:T(8,128)(2,1)S(1)}, bf16[384,1024]{1,0:T(8,128)(2,1)S(1)}, u32[]{:S(2)}, u32[]{:S(2)}) collective-permute-start(bf16[384,1024]{1,0:T(8,128)(2,1)S(1)} %pad_maximum_fusion), channel_id=1, source_target_pairs={{0,2},{1,3},{2,0},{3,1},{4,6},{5,7},{6,4},{7,5},{8,10},{9,11},{10,... | collective-permute-start | bytes 2359304 | tf_op jit(solution)/shard_map/ppermute | solution.py:485
  47.1 35.1 %collective-permute-start.13 = (bf16[128,1024]{1,0:T(8,128)(2,1)}, bf16[128,1024]{1,0:T(8,128)(2,1)S(1)}, u32[]{:S(2)}, u32[]{:S(2)}) collective-permute-start(bf16[128,1024]{1,0:T(8,128)(2,1)} %collective-permute-done.8.refs_3_), channel_id=1, source_target_pairs={{0,2},{1,3},{2,0},{3,1},{4,6},{5,7},{6,4},{7,5},{8,10},{9,11},{10,... | collective-permute-start | bytes 786440 | tf_op jit(solution)/shard_map/ppermute | solution.py:485
  48.6 33.6 %collective-permute-start.14 = (bf16[128,1024]{1,0:T(8,128)(2,1)}, bf16[128,1024]{1,0:T(8,128)(2,1)S(1)}, u32[]{:S(2)}, u32[]{:S(2)}) collective-permute-start(bf16[128,1024]{1,0:T(8,128)(2,1)} %collective-permute-done.11.refs_4_), channel_id=1, source_target_pairs={{0,2},{1,3},{2,0},{3,1},{4,6},{5,7},{6,4},{7,5},{8,10},{9,11},{10,... | collective-permute-start | bytes 786440 | tf_op jit(solution)/shard_map/ppermute | solution.py:485
  82.3 25.9 %collective-permute-start.16 = (bf16[512,512]{1,0:T(8,128)(2,1)}, bf16[512,512]{1,0:T(8,128)(2,1)S(1)}, u32[]{:S(2)}, u32[]{:S(2)}) collective-permute-start(bf16[512,512]{1,0:T(8,128)(2,1)} %get-tuple-element.167), channel_id=1, source_target_pairs={{0,4},{4,0},{8,12},{12,8},{16,20},{20,16},{24,28},{28,24},{1,5},{5... | collective-permute-start | bytes 1572872 | tf_op jit(solution)/shard_map/ppermute | solution.py:485
  82.8 25.4 %collective-permute-start.17 = (bf16[512,512]{1,0:T(8,128)(2,1)}, bf16[512,512]{1,0:T(8,128)(2,1)S(1)}, u32[]{:S(2)}, u32[]{:S(2)}) collective-permute-start(bf16[512,512]{1,0:T(8,128)(2,1)} %get-tuple-element.168), channel_id=1, source_target_pairs={{0,4},{4,0},{8,12},{12,8},{16,20},{20,16},{24,28},{28,24},{1,5},{5... | collective-permute-start | bytes 1572872 | tf_op jit(solution)/shard_map/ppermute | solution.py:485
  109.1 10.4 %collective-permute-start.18 = (f32[864,1024]{1,0:T(8,128)}, f32[864,1024]{1,0:T(8,128)S(1)}, u32[]{:S(2)}, u32[]{:S(2)}) collective-permute-start(f32[864,1024]{1,0:T(8,128)} %get-tuple-element.174), channel_id=1, source_target_pairs={{0,1},{1,0},{2,3},{3,2},{4,5},{5,4},{6,7},{7,6},{8,9},{9,8},{10,11... | collective-permute-start | bytes 10616840 | tf_op jit(solution)/shard_map/ppermute | solution.py:485
  119.5 21.7 %collective-permute-start.21 = (bf16[512,512]{1,0:T(8,128)(2,1)}, bf16[512,512]{1,0:T(8,128)(2,1)}, u32[]{:S(2)}, u32[]{:S(2)}) collective-permute-start(bf16[512,512]{1,0:T(8,128)(2,1)} %get-tuple-element.194), channel_id=1, source_target_pairs={{0,4},{4,0},{8,12},{12,8},{16,20},{20,16},{24,28},{28,24},{1,5},{5... | collective-permute-start | bytes 1572872 | tf_op jit(solution)/shard_map/ppermute | solution.py:485
  124.6 14.2 %collective-permute-start.19 = (bf16[128,1024]{1,0:T(8,128)(2,1)}, bf16[128,1024]{1,0:T(8,128)(2,1)}, u32[]{:S(2)}, u32[]{:S(2)}) collective-permute-start(bf16[128,1024]{1,0:T(8,128)(2,1)} %get-tuple-element.192), channel_id=1, source_target_pairs={{0,8},{4,12},{8,0},{12,4},{16,24},{20,28},{24,16},{28,20},{1,9},{5... | collective-permute-start | bytes 786440 | tf_op jit(solution)/shard_map/ppermute | solution.py:485
  126.0 15.2 %collective-permute-start.20 = (bf16[128,1024]{1,0:T(8,128)(2,1)}, bf16[128,1024]{1,0:T(8,128)(2,1)}, u32[]{:S(2)}, u32[]{:S(2)}) collective-permute-start(bf16[128,1024]{1,0:T(8,128)(2,1)} %get-tuple-element.193), channel_id=1, source_target_pairs={{0,16},{4,20},{8,24},{12,28},{16,0},{20,4},{24,8},{28,12},{1,17},{... | collective-permute-start | bytes 786440 | tf_op jit(solution)/shard_map/ppermute | solution.py:485
  142.5 14.7 %collective-permute-start.22 = (f32[320,512]{1,0:T(8,128)S(1)}, f32[320,512]{1,0:T(8,128)S(1)}, u32[]{:S(2)}, u32[]{:S(2)}) collective-permute-start(f32[320,512]{1,0:T(8,128)S(1)} %get-tuple-element.265), channel_id=1, source_target_pairs={{0,1},{1,0},{2,3},{3,2},{4,5},{5,4},{6,7},{7,6},{8,9},{9,8},{10,11... | collective-permute-start | bytes 1966088 | tf_op jit(solution)/shard_map/ppermute | solution.py:485
  142.6 15.4 %collective-permute-start.23 = (f32[320,512]{1,0:T(8,128)S(1)}, f32[320,512]{1,0:T(8,128)S(1)}, u32[]{:S(2)}, u32[]{:S(2)}) collective-permute-start(f32[320,512]{1,0:T(8,128)S(1)} %get-tuple-element.264), channel_id=1, source_target_pairs={{0,1},{1,0},{2,3},{3,2},{4,5},{5,4},{6,7},{7,6},{8,9},{9,8},{10,11... | collective-permute-start | bytes 1966088 | tf_op jit(solution)/shard_map/ppermute | solution.py:485
  143.1 14.1 %collective-permute-start.25 = (bf16[512,512]{1,0:T(8,128)(2,1)}, bf16[512,512]{1,0:T(8,128)(2,1)S(1)}, u32[]{:S(2)}, u32[]{:S(2)}) collective-permute-start(bf16[512,512]{1,0:T(8,128)(2,1)} %get-tuple-element.204), channel_id=1, source_target_pairs={{0,4},{4,0},{8,12},{12,8},{16,20},{20,16},{24,28},{28,24},{1,5},{5... | collective-permute-start | bytes 1572872 | tf_op jit(solution)/shard_map/ppermute | solution.py:485
  144.0 9.9 %collective-permute-start.24 = (bf16[128,1024]{1,0:T(8,128)(2,1)S(1)}, bf16[128,1024]{1,0:T(8,128)(2,1)S(1)}, u32[]{:S(2)}, u32[]{:S(2)}) collective-permute-start(bf16[128,1024]{1,0:T(8,128)(2,1)S(1)} %copy-done.23), channel_id=1, source_target_pairs={{0,24},{4,28},{8,16},{12,20},{16,8},{20,12},{24,0},{28,4},{1,25},{... | collective-permute-start | bytes 786440 | tf_op jit(solution)/shard_map/ppermute | solution.py:485
  158.1 13.0 %collective-permute-start.29 = (bf16[864,1024]{1,0:T(8,128)(2,1)}, bf16[864,1024]{1,0:T(8,128)(2,1)S(1)}, u32[]{:S(2)}, u32[]{:S(2)}) collective-permute-start(bf16[864,1024]{1,0:T(8,128)(2,1)} %mixed.1), channel_id=1, source_target_pairs={{0,1},{1,0},{2,3},{3,2},{4,5},{5,4},{6,7},{7,6},{8,9},{9,8},{10,11... | collective-permute-start | bytes 5308424 | tf_op jit(solution)/shard_map/ppermute | solution.py:485
  162.9 19.5 %collective-permute-start.26 = (f32[80,1024]{1,0:T(8,128)}, f32[80,1024]{1,0:T(8,128)S(1)}, u32[]{:S(2)}, u32[]{:S(2)}) collective-permute-start(f32[80,1024]{1,0:T(8,128)} %get-tuple-element.208), channel_id=1, source_target_pairs={{0,4},{4,0},{8,12},{12,8},{16,20},{20,16},{24,28},{28,24},{1,5},{5... | collective-permute-start | bytes 983048 | tf_op jit(solution)/shard_map/ppermute | solution.py:485
  163.8 18.6 %collective-permute-start.27 = (f32[80,1024]{1,0:T(8,128)}, f32[80,1024]{1,0:T(8,128)S(1)}, u32[]{:S(2)}, u32[]{:S(2)}) collective-permute-start(f32[80,1024]{1,0:T(8,128)} %get-tuple-element.209), channel_id=1, source_target_pairs={{0,2},{1,3},{2,0},{3,1},{4,6},{5,7},{6,4},{7,5},{8,10},{9,11},{10,... | collective-permute-start | bytes 983048 | tf_op jit(solution)/shard_map/ppermute | solution.py:540
  165.3 17.1 %collective-permute-start.28 = (f32[80,1024]{1,0:T(8,128)}, f32[80,1024]{1,0:T(8,128)S(1)}, u32[]{:S(2)}, u32[]{:S(2)}) collective-permute-start(f32[80,1024]{1,0:T(8,128)} %get-tuple-element.210), channel_id=1, source_target_pairs={{0,6},{1,7},{2,4},{3,5},{4,2},{5,3},{6,0},{7,1},{8,14},{9,15},{10,... | collective-permute-start | bytes 983048 | tf_op jit(solution)/shard_map/ppermute | solution.py:540
  170.4 12.0 %collective-permute-start.30 = (bf16[128,1024]{1,0:T(8,128)(2,1)}, bf16[128,1024]{1,0:T(8,128)(2,1)S(1)}, u32[]{:S(2)}, u32[]{:S(2)}) collective-permute-start(bf16[128,1024]{1,0:T(8,128)(2,1)} %get-tuple-element.216), channel_id=1, source_target_pairs={{0,8},{4,12},{8,0},{12,4},{16,24},{20,28},{24,16},{28,20},{1,9},{5... | collective-permute-start | bytes 786440 | tf_op jit(solution)/shard_map/ppermute | solution.py:485
  171.1 18.1 %collective-permute-start.34 = (bf16[128,1024]{1,0:T(8,128)(2,1)}, bf16[128,1024]{1,0:T(8,128)(2,1)}, u32[]{:S(2)}, u32[]{:S(2)}) collective-permute-start(bf16[128,1024]{1,0:T(8,128)(2,1)} %get-tuple-element.223), channel_id=1, source_target_pairs={{0,16},{4,20},{8,24},{12,28},{16,0},{20,4},{24,8},{28,12},{1,17},{... | collective-permute-start | bytes 786440 | tf_op jit(solution)/shard_map/ppermute | solution.py:485
  182.6 14.7 %collective-permute-start.32 = (f32[80,256]{1,0:T(8,128)S(1)}, f32[80,256]{1,0:T(8,128)S(1)}, u32[]{:S(2)}, u32[]{:S(2)}) collective-permute-start(f32[80,256]{1,0:T(8,128)S(1)} %get-tuple-element.270), channel_id=1, source_target_pairs={{0,16},{4,20},{8,24},{12,28},{16,0},{20,4},{24,8},{28,12},{1,17},{... | collective-permute-start | bytes 245768 | tf_op jit(solution)/shard_map/ppermute | solution.py:485
  185.4 11.9 %collective-permute-start.33 = (f32[80,256]{1,0:T(8,128)S(1)}, f32[80,256]{1,0:T(8,128)S(1)}, u32[]{:S(2)}, u32[]{:S(2)}) collective-permute-start(f32[80,256]{1,0:T(8,128)S(1)} %get-tuple-element.269), channel_id=1, source_target_pairs={{0,24},{4,28},{8,16},{12,20},{16,8},{20,12},{24,0},{28,4},{1,25},{... | collective-permute-start | bytes 245768 | tf_op jit(solution)/shard_map/ppermute | solution.py:485
  186.9 16.1 %collective-permute-start.38 = (bf16[128,1024]{1,0:T(8,128)(2,1)S(1)}, bf16[128,1024]{1,0:T(8,128)(2,1)S(1)}, u32[]{:S(2)}, u32[]{:S(2)}) collective-permute-start(bf16[128,1024]{1,0:T(8,128)(2,1)S(1)} %copy-done.22), channel_id=1, source_target_pairs={{0,24},{4,28},{8,16},{12,20},{16,8},{20,12},{24,0},{28,4},{1,25},{... | collective-permute-start | bytes 786440 | tf_op jit(solution)/shard_map/ppermute | solution.py:485
  208.9 10.3 %collective-permute-start.41 = (bf16[80,1024]{1,0:T(8,128)(2,1)S(1)}, bf16[80,1024]{1,0:T(8,128)(2,1)S(1)}, u32[]{:S(2)}, u32[]{:S(2)}) collective-permute-start(bf16[80,1024]{1,0:T(8,128)(2,1)S(1)} %constant_dynamic-update-slice_fusion.4), channel_id=1, source_target_pairs={{0,6},{1,7},{2,4},{3,5},{4,2},{5,3},{6,0},{7,1},{8,14},{9,15},{10,... | collective-permute-start | bytes 491528 | tf_op jit(solution)/shard_map/ppermute | solution.py:540
  214.5 11.6 %collective-permute-start.43 = (f32[128,1024]{1,0:T(8,128)}, f32[128,1024]{1,0:T(8,128)S(1)}, u32[]{:S(2)}, u32[]{:S(2)}) collective-permute-start(f32[128,1024]{1,0:T(8,128)} %add_parts.3), channel_id=1, source_target_pairs={{0,2},{1,3},{2,0},{3,1},{4,6},{5,7},{6,4},{7,5},{8,10},{9,11},{10,... | collective-permute-start | bytes 1572872 | tf_op jit(solution)/shard_map/ppermute | solution.py:485
  219.2 9.9 %collective-permute-start.42 = (bf16[320,1024]{1,0:T(8,128)(2,1)S(1)}, bf16[320,1024]{1,0:T(8,128)(2,1)S(1)}, u32[]{:S(2)}, u32[]{:S(2)}) collective-permute-start(bf16[320,1024]{1,0:T(8,128)(2,1)S(1)} %constant_dynamic-update-slice_fusion), channel_id=1, source_target_pairs={{0,1},{1,0},{2,3},{3,2},{4,5},{5,4},{6,7},{7,6},{8,9},{9,8},{10,11... | collective-permute-start | bytes 1966088 | tf_op jit(solution)/shard_map/ppermute | solution.py:485
  (37 other events, 368.2 us)

commit v7 on v6

--- a/solution.py
+++ b/solution.py
@@ -55,9 +55,8 @@
 
 def stem_kernel(
     cnt_ref, idx_ref, patch_ref, w_ref, gain_ref, parts, genc_ref, og_ref,
-    emb_ref, normed_ref, gl_ref, cols_ref,
+    emb_ref, rows_ref, cols_ref,
 ):
-    step = pl.program_id(0)
     scenes = patch_ref.shape[0]
     patch_iota = lax.broadcasted_iota(jnp.int32, (parts.shape[1], CAP), 0)
     slot = lax.broadcasted_iota(jnp.int32, (CAP, 1), 0)
@@ -71,8 +70,8 @@
             placed.append(
                 (dot_nn(onehot, parts[0]) + dot_nn(onehot, parts[1])) + dot_nn(onehot, parts[2])
             )
-            live = slot < cnt_ref[step * scenes + s, g]
-            gl_ref[s, rows, :] = jnp.where(live, og_ref[s, rows, :].astype(F32), 0.0).astype(BF16)
+            live = slot < cnt_ref[s, :, g : g + 1]
+            rows_ref[1, s, rows, :] = jnp.where(live, og_ref[s, rows, :].astype(F32), 0.0).astype(BF16)
         summed = dot_nn(jnp.concatenate(picked, axis=0), w_ref[start * PIX : end * PIX, :])
         for s in range(scenes):
             values = summed[s * CAP : (s + 1) * CAP] + (placed[s] + genc_ref[g : g + 1, :])
@@ -83,7 +82,7 @@
             dev = x - centre
             spread = jnp.mean(dev * dev, axis=-1, keepdims=True)
             centred = dev * lax.rsqrt(spread + NORM_EPS)
-            normed_ref[s, rows, :] = (centred * gain_ref[...]).astype(BF16)
+            rows_ref[0, s, rows, :] = (centred * gain_ref[...]).astype(BF16)
             cols_ref[s, rows, :width] = picked[s]
             if width < cols_ref.shape[2]:
                 cols_ref[s, rows, width:] = jnp.zeros((CAP, cols_ref.shape[2] - width), BF16)
@@ -91,16 +90,15 @@
 
 def stem_call(counts, index, patches, w_stem, gain, table, genc, out_grad):
     scenes, patch_count, width = patches.shape
-    block = 2 if scenes % 2 == 0 else 1
+    block = 3 if scenes % 3 == 0 else 1
     col_width = max(e - s for s, e in GROUP_BANDS) * PIX
     per = lambda shape: pl.BlockSpec((block,) + shape, lambda i: (i, 0, 0))
     whole = lambda a: pl.BlockSpec(a.shape, lambda i: (0,) * a.ndim)
-    rows = jax.ShapeDtypeStruct((scenes, TOK, D), BF16)
     return pl.pallas_call(
         stem_kernel,
         grid=(scenes // block,),
         in_specs=[
-            pl.BlockSpec(memory_space=pltpu.SMEM),
+            per((1, GROUPS)),
             per((GROUPS, CAP)),
             per((patch_count, width)),
             whole(w_stem),
@@ -109,17 +107,30 @@
             whole(genc),
             per((TOK, D)),
         ],
-        out_specs=[per((TOK, D)), per((TOK, D)), per((TOK, D)), per((TOK, col_width))],
-        out_shape=[rows, rows, rows, jax.ShapeDtypeStruct((scenes, TOK, col_width), BF16)],
+        out_specs=[
+            per((TOK, D)),
+            pl.BlockSpec((2, block, TOK, D), lambda i: (0, i, 0, 0)),
+            per((TOK, col_width)),
+        ],
+        out_shape=[
+            jax.ShapeDtypeStruct((scenes, TOK, D), BF16),
+            jax.ShapeDtypeStruct((2, scenes, TOK, D), BF16),
+            jax.ShapeDtypeStruct((scenes, TOK, col_width), BF16),
+        ],
         compiler_params=params(),
         cost_estimate=cost(8e9, 12e6),
         name="stem_norm",
-    )(counts, index, patches, w_stem, gain, table, genc, out_grad)
-
-
-def attention_kernel(first, cnt_ref, owner_ref, na_ref, nb_ref, ga_ref, gb_ref, *refs):
-    before, refs = refs[: 0 if first else 2], refs[0 if first else 2 :]
-    blocks, (out_ref, w_ref, back_own_ref, back_far_ref, n_s, g_s, qkv) = refs[:-7], refs[-7:]
+    )(counts.reshape(scenes, 1, GROUPS), index, patches, w_stem, gain, table, genc, out_grad)
+
+
+def attention_kernel(
+    packs, blocks, dp, cnt_ref, owner_ref, low_ref, na_ref, nb_ref, ga_ref, gb_ref, *refs
+):
+    earlier, refs = refs[: 2 * (packs or 0)], refs[2 * (packs or 0) :]
+    blocks, refs = refs[:blocks], refs[blocks:]
+    out_ref, w_ref, keep_ref, *refs = refs
+    sends, refs = refs[:2], refs[2:]
+    n_s, g_s, qkv, total = refs[-4:]
     half, step = pl.program_id(0), pl.program_id(1)
     rows = n_s.shape[0]
     scenes = rows // TOK
@@ -130,16 +141,17 @@
         size = blocks[0].shape[0]
         for b, block in enumerate(blocks):
             w_ref[pl.ds(pl.multiple_of(owner_ref[b] * size, size), size), :] = block[...]
+        total[...] = jnp.zeros_like(total)
 
     @pl.when(half == 0)
     def _():
-        n_s[...] = na_ref[...]
-        g_s[...] = ga_ref[...]
+        n_s[...] = na_ref[0]
+        g_s[...] = ga_ref[0]
 
     @pl.when(half != 0)
     def _():
-        n_s[...] = nb_ref[...]
-        g_s[...] = gb_ref[...]
+        n_s[...] = nb_ref[0]
+        g_s[...] = gb_ref[0]
 
     qkv[:, : 3 * width] = dot_nn(n_s[...], w_ref[:, : 3 * width]).astype(BF16)
     qkv[:, 3 * width :] = dot_nn(g_s[...], w_ref[:, 3 * width :]).astype(BF16)
@@ -188,153 +200,111 @@
         return 0
 
     lax.fori_loop(0, scenes, scene_body, 0, unroll=True)
-    back = dot_nt(out_ref[:, : 3 * width], w_ref[:, : 3 * width])
-
-    @pl.when(half == 0)
+    total[:, : 3 * width] += dot_tn(n_s[...], out_ref[:, : 3 * width])
+    total[:, 3 * width :] += dot_tn(g_s[...], out_ref[:, 3 * width :])
+
+    @pl.when((half == pl.num_programs(0) - 1) & (step == pl.num_programs(1) - 1))
     def _():
-        back_own_ref[...] = back if first else before[0][...] + back
-
-    @pl.when(half != 0)
-    def _():
-        back_far_ref[...] = back if first else before[1][...] + back
+        size = total.shape[0] // dp
+        low = low_ref[0]
+        for b in range(dp // 2):
+            at = slice(b * size, (b + 1) * size)
+            mine = pl.multiple_of((2 * b + low) * size, size)
+            other = pl.multiple_of((2 * b + 1 - low) * size, size)
+            keep_ref[at, :] = total[pl.ds(mine, size), :]
+            for c, send_ref in enumerate(sends):
+                cols = send_ref.shape[1]
+                send_ref[at, :] = total[pl.ds(other, size), c * cols : (c + 1) * cols].astype(BF16)
+
+    if packs is not None:
+        back = dot_nt(out_ref[:, : 3 * width], w_ref[:, : 3 * width])
+        for pack_ref, weight_ref in zip(earlier[:packs], earlier[packs:]):
+            back = back + dot_nt(pack_ref[...], weight_ref[...])
+
+        @pl.when(half == 0)
+        def _():
+            refs[0][...] = back
+
+        @pl.when(half != 0)
+        def _():
+            refs[1][...] = back
 
 
 def block_rows(tokens):
     return 3 * TOK if tokens % (3 * TOK) == 0 else TOK
 
 
-def two_halves(rows, steps):
-    first = pl.BlockSpec((rows, D), lambda h, i: (jnp.where(h == 0, i, steps - 1), 0))
-    second = pl.BlockSpec((rows, D), lambda h, i: (jnp.where(h == 0, 0, i), 0))
-    return [first, second, first, second]
+def two_halves(rows, steps, lead):
+    shape = (1,) * len(lead) + (rows, D)
+    first = pl.BlockSpec(shape, lambda h, i: lead + (jnp.where(h == 0, i, steps - 1), 0))
+    second = pl.BlockSpec(shape, lambda h, i: lead + (jnp.where(h == 0, 0, i), 0))
+    return [first, second]
 
 
 SCALARS = pl.BlockSpec(memory_space=pltpu.SMEM)
 
 
-def attention_call(counts, owners, na, nb, ga, gb, before, blocks):
-    tokens = na.shape[0]
+def attention_call(counts, owners, low, own, far, earlier, blocks, dp):
+    tokens = own.shape[1]
     rows = block_rows(tokens)
     steps = tokens // rows
     cols = blocks[0].shape[1]
-    whole = lambda a: pl.BlockSpec(a.shape, lambda h, i: (0, 0))
-    halves = two_halves(rows, steps)
+    whole = lambda shape: pl.BlockSpec(shape, lambda h, i: (0, 0))
+    at = lambda h, i: (h * steps + i, 0)
+    packs = None if earlier is None else len(earlier[0])
+    back = [] if earlier is None else two_halves(rows, steps, ())
+    send = jax.ShapeDtypeStruct((D // 2, cols // 2), BF16)
+    back_shape = jax.ShapeDtypeStruct((tokens, D), F32)
     return pl.pallas_call(
-        functools.partial(attention_kernel, not before),
+        functools.partial(attention_kernel, packs, len(blocks), dp),
         grid=(2, steps),
-        in_specs=[SCALARS, SCALARS] + halves + halves[: len(before)] + [whole(b) for b in blocks],
-        out_specs=[
-            pl.BlockSpec((rows, cols), lambda h, i: (h * steps + i, 0)),
-            pl.BlockSpec((D, cols), lambda h, i: (0, 0)),
-        ]
-        + halves[:2],
+        in_specs=[SCALARS] * 3
+        + two_halves(rows, steps, (0,))
+        + two_halves(rows, steps, (1,))
+        + [pl.BlockSpec((rows, cols // 4 * 3), at)] * (packs or 0)
+        + [whole((D, cols // 4 * 3))] * (packs or 0)
+        + [whole(b.shape) for b in blocks],
+        out_specs=[pl.BlockSpec((rows, cols), at), whole((D, cols)), whole((D // 2, cols))]
+        + [whole(send.shape)] * 2
+        + back,
         out_shape=[
             jax.ShapeDtypeStruct((2 * tokens, cols), BF16),
             jax.ShapeDtypeStruct((D, cols), BF16),
-            jax.ShapeDtypeStruct((tokens, D), F32),
-            jax.ShapeDtypeStruct((tokens, D), F32),
-        ],
+            jax.ShapeDtypeStruct((D // 2, cols), F32),
+            send,
+            send,
+        ]
+        + [back_shape] * len(back),
         scratch_shapes=[
             pltpu.VMEM((rows, D), BF16),
             pltpu.VMEM((rows, D), BF16),
             pltpu.VMEM((rows, cols), BF16),
+            pltpu.VMEM((D, cols), F32),
         ],
         compiler_params=params(),
         cost_estimate=cost(20e9, 14e6),
         name="attention",
-    )(counts, owners, na, nb, ga, gb, *before, *blocks)
-
-
-def transpose_kernel(*refs):
-    for k, ref in enumerate(refs[:-1]):
-        refs[-1][k] = ref[...].T
-
-
-def transpose_call(arrays):
-    rows, cols = arrays[0].shape
-    block = cols // 4
-    return pl.pallas_call(
-        transpose_kernel,
-        grid=(4,),
-        in_specs=[pl.BlockSpec((rows, block), lambda i: (0, i))] * len(arrays),
-        out_specs=pl.BlockSpec((len(arrays), block, rows), lambda i: (0, i, 0)),
-        out_shape=jax.ShapeDtypeStruct((len(arrays), cols, rows), BF16),
-        compiler_params=params(),
-        cost_estimate=cost(4e9, 8e6),
-        name="transpose_rows",
-    )(*arrays)
-
-
-def weight_grad_kernel(blocks, low_ref, turned_ref, pack_ref, keep_ref, *refs):
-    sends, total = refs[:-1], refs[-1]
-    step = pl.program_id(0)
-    width = pack_ref.shape[1] // 4
-    parts = [slice(0, 3 * width), slice(3 * width, 4 * width)]
-    for k in range(4):
-
-        @pl.when(step == k)
-        def _():
-            new = dot_nn(turned_ref[0], pack_ref[:, parts[k % 2]])
-            total[:, parts[k % 2]] = new if k < 2 else total[:, parts[k % 2]] + new
-
-    @pl.when(step == 3)
-    def _():
-        rows = total.shape[0] // blocks
-        low = low_ref[0]
-        for b in range(blocks // 2):
-            at = slice(b * rows, (b + 1) * rows)
-            mine = pl.multiple_of((2 * b + low) * rows, rows)
-            other = pl.multiple_of((2 * b + 1 - low) * rows, rows)
-            keep_ref[at, :] = total[pl.ds(mine, rows), :]
-            for c, send_ref in enumerate(sends):
-                cols = send_ref.shape[1]
-                send_ref[at, :] = total[pl.ds(other, rows), c * cols : (c + 1) * cols].astype(BF16)
-
-
-def weight_grad_call(low, turned, pack, blocks):
-    tokens, cols = pack.shape
-    out = lambda cols: pl.BlockSpec((D // 2, cols), lambda i: (0, 0))
-    send = jax.ShapeDtypeStruct((D // 2, cols // 2), BF16)
-    return pl.pallas_call(
-        functools.partial(weight_grad_kernel, blocks),
-        grid=(4,),
-        in_specs=[
-            SCALARS,
-            pl.BlockSpec((1,) + turned.shape[1:], lambda i: (i, 0, 0)),
-            pl.BlockSpec((tokens // 2, cols), lambda i: (i // 2, 0)),
-        ],
-        out_specs=[out(cols), out(cols // 2), out(cols // 2)],
-        out_shape=[jax.ShapeDtypeStruct((D // 2, cols), F32), send, send],
-        scratch_shapes=[pltpu.VMEM((D, cols), F32)],
-        compiler_params=params(),
-        cost_estimate=cost(6e9, 12e6),
-        name="weight_grad",
-    )(low, turned, pack)
+    )(counts, owners, low, own, far, own, far, *[x for group in earlier or () for x in group], *blocks)
 
 
 def combine_kernel(place_ref, keep_ref, first_ref, second_ref, *refs):
-    rows = refs[0].shape[0]
+    rows, cols = refs[0].shape
     place = place_ref[0]
-
-    def add(recv_ref):
+    for c, recv_ref in enumerate((first_ref, second_ref)):
+        half = slice(c * cols // 2, (c + 1) * cols // 2)
         for j, ref in enumerate(refs):
             at = pl.ds(pl.multiple_of((place ^ j) * rows, rows), rows)
-            ref[...] = (keep_ref[at, :] + recv_ref[at, :].astype(F32)).astype(ref.dtype)
-
-    pl.when(pl.program_id(0) < 2)(lambda: add(first_ref))
-    pl.when(pl.program_id(0) >= 2)(lambda: add(second_ref))
+            ref[:, half] = (keep_ref[at, half] + recv_ref[at, :].astype(F32)).astype(ref.dtype)
 
 
 def combine_call(place, keep, recvs, blocks, dtype):
     rows, cols = keep.shape[0] // blocks, keep.shape[1]
-    step = cols // 4
-    whole = lambda at: pl.BlockSpec((keep.shape[0], step), lambda c: (0, at(c)))
+    whole = lambda a: pl.BlockSpec(a.shape, lambda: (0, 0))
     shapes = [jax.ShapeDtypeStruct((rows, cols), F32 if j == 0 else dtype) for j in range(blocks)]
     return pl.pallas_call(
         combine_kernel,
-        grid=(4,),
-        in_specs=[SCALARS, whole(lambda c: c), whole(lambda c: jnp.minimum(c, 1)), whole(lambda c: jnp.maximum(c - 2, 0))],
-        out_specs=[pl.BlockSpec((rows, step), lambda c: (0, c))] * blocks,
+        in_specs=[SCALARS, whole(keep)] + [whole(r) for r in recvs],
+        out_specs=[pl.BlockSpec((rows, cols), lambda: (0, 0))] * blocks,
         out_shape=shapes,
         compiler_params=params(),
         cost_estimate=cost(1e6, 5e6),
@@ -350,11 +320,9 @@
 
 
 def add_call(parts):
-    rows, cols = parts[0].shape
-    spec = pl.BlockSpec((rows, cols // 4), lambda c: (0, c))
+    spec = pl.BlockSpec(parts[0].shape, lambda: (0, 0))
     return pl.pallas_call(
         add_kernel,
-        grid=(4,),
         in_specs=[spec] * len(parts),
         out_specs=spec,
         out_shape=jax.ShapeDtypeStruct(parts[0].shape, F32),
@@ -398,7 +366,7 @@
     )(*packs, *weights)
 
 
-def tail_kernel(core_ref, own_ref, recv_ref, emb_ref, gl_ref, cols_ref, gain_ref, send_ref, keep_ref, acc):
+def tail_kernel(core_ref, own_ref, recv_ref, emb_ref, gl_ref, cols_ref, gain_ref, keep_ref, first_ref, second_ref, acc):
     step = pl.program_id(0)
     rows = emb_ref.shape[0]
     scenes = rows // TOK
@@ -416,7 +384,7 @@
     first_mean = jnp.mean(scaled, axis=-1, keepdims=True)
     second_mean = jnp.mean(scaled * centred, axis=-1, keepdims=True)
     back = inv_std * (scaled - first_mean - centred * second_mean)
-    grad_in = (gl_ref[...].astype(F32) + back).astype(BF16)
+    grad_in = (gl_ref[0].astype(F32) + back).astype(BF16)
     for g, (start, end) in enumerate(GROUP_BANDS):
         at = [slice(s * TOK + g * CAP, s * TOK + (g + 1) * CAP) for s in range(scenes)]
         columns = jnp.concatenate([cols_ref[a, : (end - start) * PIX] for a in at], axis=0)
@@ -428,27 +396,30 @@
         size = keep_ref.shape[0]
         core = core_ref[0]
         keep_ref[...] = acc[pl.ds(pl.multiple_of(core * size, size), size), :]
-        send_ref[...] = acc[pl.ds(pl.multiple_of((1 - core) * size, size), size), :]
-
-
-def tail_call(core, own, recv, emb, gl, cols, gain):
+        other = pl.ds(pl.multiple_of((1 - core) * size, size), size)
+        first_ref[...] = acc[other, : D // 2]
+        second_ref[...] = acc[other, D // 2 :]
+
+
+def tail_call(core, own, recv, emb, rows_own, cols, gain):
     tokens = emb.shape[0]
     rows = 2 * TOK if tokens % (2 * TOK) == 0 else TOK
     per = lambda a: pl.BlockSpec((rows, a.shape[1]), lambda i: (i, 0))
     stem_rows = GROUP_BANDS[-1][1] * PIX
-    half = jax.ShapeDtypeStruct((stem_rows // 2, D), F32)
+    keep = jax.ShapeDtypeStruct((stem_rows // 2, D), F32)
+    send = jax.ShapeDtypeStruct((stem_rows // 2, D // 2), F32)
     return pl.pallas_call(
         tail_kernel,
         grid=(tokens // rows,),
-        in_specs=[SCALARS, per(own), per(recv), per(emb), per(gl), per(cols)]
+        in_specs=[SCALARS, per(own), per(recv), per(emb), pl.BlockSpec((1, rows, D), lambda i: (1, i, 0)), per(cols)]
         + [pl.BlockSpec(gain.shape, lambda i: (0, 0))],
-        out_specs=[pl.BlockSpec(half.shape, lambda i: (0, 0))] * 2,
-        out_shape=[half, half],
+        out_specs=[pl.BlockSpec(a.shape, lambda i: (0, 0)) for a in (keep, send, send)],
+        out_shape=[keep, send, send],
         scratch_shapes=[pltpu.VMEM((stem_rows, D), F32)],
         compiler_params=params(),
         cost_estimate=cost(10e9, 12e6),
         name="tail",
-    )(core, own, recv, emb, gl, cols, gain)
+    )(core, own, recv, emb, rows_own, cols, gain)
 
 
 def output_kernel(count, cnt_ref, recv_ref, emb_ref, *refs):
@@ -522,7 +493,7 @@
     return combine_call(mine.reshape(1), keep, recv, group // 2 * 2, F32)
 
 
-def sum_stem(parts, beside, dp, group):
+def sum_stem(parts, beside, after, dp, group):
     core = lax.axis_index("group") % 2
     far = lax.axis_index("group") // 2
     low = lax.axis_index("dp") % 2
@@ -542,9 +513,8 @@
 
     hops = [(k // 2, k % 2) for k in range(1, 2 * fars)]
     arrived = [hop(part, f, b) for part, (f, b) in zip(parts[1:], hops)]
-    beside = beside()
-    arrived, beside[:3] = together(arrived, beside[:3])
-    near = (len(beside) + 3) // 2
+    arrived, beside = together(arrived, beside)
+    beside = after(*beside)
     total = parts[0]
     for part in arrived:
         total = total + part
@@ -552,14 +522,13 @@
     part = lax.dynamic_slice_in_dim(total, high * cols, cols, 1)
     away = [lax.dynamic_slice_in_dim(total, (high ^ j) * cols, cols, 1) for j in range(1, highs)]
     arrived = [swap(a, "dp", dp, 2 * (j + 1)) for j, a in enumerate(away)]
-    arrived, beside[:near] = together(arrived, beside[:near])
+    arrived, beside = together(arrived, beside)
     for block in arrived:
         part = part + block
     part = part.astype(BF16)
     line = jnp.zeros((small, width), BF16)
     line = lax.dynamic_update_slice_in_dim(line, part, high * cols, 1)
     arrived = [swap(part, "dp", dp, 2 * j) for j in range(1, highs)]
-    arrived, beside = together(arrived, beside)
     for j, block in enumerate(arrived):
         line = lax.dynamic_update_slice_in_dim(line, block, (high ^ (j + 1)) * cols, 1)
     block = jnp.zeros((rows, width), BF16)
@@ -618,17 +587,18 @@
         out_grad.reshape(scenes, TOK, D),
     )
     stem, counts_far = ring.step(stem, counts_far)
-    emb, normed, gl = [a.reshape(tokens, D) for a in stem[:3]]
-    cols = stem[3].reshape(tokens, stem[3].shape[2])
+    emb = stem[0].reshape(tokens, D)
+    both = [stem[1].reshape(2, tokens, D)]
+    cols = stem[2].reshape(tokens, stem[2].shape[2])
     both_counts = jnp.stack([counts, counts_far])
-    both = [normed, swap(normed, "group", group, 1), gl, swap(gl, "group", group, 1)]
+    both.append(swap(both[0], "group", group, 1))
     far.append(cross(ring.ahead[-1]))
     both, far[0] = ring.step(both, far[0])
     while len(ring.ahead) < dp // 2:
         far.append(cross(ring.ahead[-1]))
         (far[-2],) = ring.step(far[-2])
     far.append(cross(ring.ahead[-1]))
-    turned, far[-2] = ring.step(transpose_call([both[0], both[2], both[1], both[3]]), far[-2])
+    (far[-2],) = ring.step(far[-2])
     ring.ahead, ring.behind = together(ring.ahead, ring.behind)
     far.append(cross(ring.ahead[-1]))
     behind = ring.behind[1:]
@@ -643,7 +613,7 @@
     def rest_swaps(blocks):
         return [blocks[0]] + [swap(blocks[j], "dp", dp, 2 * j) for j in rests]
 
-    weights, back = [], []
+    weights = []
     for n in range(group // 2):
         if n == 0:
             blocks = ring.ahead + behind
@@ -651,40 +621,37 @@
             rows = shard.shape[0]
             last = [far[-1][n - 1][b * rows : (b + 1) * rows] for b in range(len(behind))]
             blocks = [f[n - 1] for f in far[:-1]] + last
-        made = attention_call(both_counts, owners, *both, back, blocks)
+        earlier = (packs, weights) if n == len(fars) else None
+        made = attention_call(both_counts, owners, low, *both, earlier, blocks, dp)
         if n == 0:
-            pack, weight, *back = together(*made)
+            made, far[-3:] = together(made, far[-3:])
         else:
-            pack, weight, *back, coming[-1] = together(*made, coming[-1])
+            made, coming[-1] = together(made, coming[-1])
+        pack, weight, keep, first, second, *back = made
         packs.append(pack)
         weights.append(weight)
-        if n == len(fars):
-            back_far = swap(back[1], "group", group, 1)
-        keep, *send = weight_grad_call(low, turned, pack, dp)
-        if n == 0:
-            send, keep, far[-3:] = together(send, keep, far[-3:])
-        if n == len(fars):
-            send, keep, back_far, kept, coming = together(send, keep, back_far, kept, coming)
         kept.append(keep)
-        coming.append([swap(x, "dp", dp, 1) for x in send])
+        coming.append([swap(x, "dp", dp, 1) for x in (first, second)])
+    back_far = swap(back[1], "group", group, 1)
     blocks, back_far = together([first_to_rest(n) for n in range(len(fars))], back_far)
     landing = [rest_swaps(b) for b in blocks]
     near = dp // 2 * 3 // 4
-    stem_send, stem_keep, landing[-1][:near], coming[-1][0] = together(
-        *tail_call(core, back[0], back_far, emb, gl, cols, gain), landing[-1][:near], coming[-1][0]
+    stem_made, landing[-1][:near], coming[-1] = together(
+        tail_call(core, back[0], back_far, emb, both[0], cols, gain), landing[-1][:near], coming[-1]
     )
-    half = stem_send.shape[1] // 2
-    stem_recv = [swap(stem_send[:, c * half : (c + 1) * half], "group", group, 1) for c in range(2)]
-    mixed, stem_recv, landing, coming = together(mixed_call(packs, weights), stem_recv, landing, coming)
-    mixed = swap(mixed, "group", group, 1)
-    stem_parts = halve_stem(stem_recv, stem_keep, group)
-
-    def beside():
-        last = rest_swaps(first_to_rest(-1))
-        output = output_call(counts, mixed, emb, packs, weights)
-        return [output] + last
-
-    grad_w_stem, (output, *last) = sum_stem(stem_parts, beside, dp, group)
+    stem_keep, *stem_recv = stem_made
+    stem_recv = [swap(x, "group", group, 1) for x in stem_recv]
+    blocks = list(first_to_rest(-1))
+    stem_recv, blocks[0], landing = together(stem_recv, blocks[0], landing)
+    last = rest_swaps(blocks)
+
+    def after(mixed, *near_last):
+        mixed = swap(mixed, "group", group, 1)
+        return [output_call(counts, mixed, emb, packs, weights)] + list(near_last) + last[near:]
+
+    grad_w_stem, (output, *last) = sum_stem(
+        halve_stem(stem_recv, stem_keep, group), [mixed_call(packs, weights)] + last[:near], after, dp, group
+    )
     shares = [add_call(parts) for parts in landing + [last]]
 
     total = shares[0]

time: 232 us -> 231 us (level)
  Pallas kernels: 118 us -> 94.1 us
  waiting for transfers between devices: 45.7 us -> 62 us
  starting transfers between devices: 50.2 us -> 53.2 us
  local copies, waits for them, and re-layouts: 10.9 us -> 13.8 us
    pallas_call x11 -> x8, Pallas kernels: 99.5 us -> 76.3 us  [the longest x2 54.8 us: attention_call(): pl.pallas_call(functools.partial(attention_kernel, packs, len(blocks), dp...]
    ppermute x4, waiting for transfers between devices: 3.4 us -> 15.5 us  [hop(): return lax.ppermute(block, ('dp', 'group'), pairs)]
    ppermute x4, waiting for transfers between devices: 1.14 us -> 8.5 us  [step(): ahead = lax.ppermute(self.ahead[-1], self.axis, self.forward)]
    ppermute x33 -> x32, waiting for transfers between devices: 39.1 us -> 35.4 us  [swap(): return lax.ppermute(x, axis, [(i, i ^ bit) for i in range(size)])]
    ppermute x33 -> x32, starting transfers between devices: 35.5 us -> 38.2 us  [swap(): return lax.ppermute(x, axis, [(i, i ^ bit) for i in range(size)])]
    unnamed x55 -> x53, local copies, waits for them, and re-layouts: 7.84 us -> 9.71 us
  transfers between devices with their start and end apart: 44 -> 43, of which waited for: 15 -> 16; matrix products, arithmetic and copies ran while one was open for 3% -> 4% of each run, Pallas kernels for 51% -> 40%
where the time goes in v7:
time: 231 us; the launch traced here: 230 us
  Pallas kernels  94.1 us (41%)
  waiting for transfers between devices  62 us (27%)
  starting transfers between devices  53.2 us (23%)
  local copies, waits for them, and re-layouts  13.8 us (6%)
  other arithmetic  6.15 us (3%)
    pallas_call x2, Pallas kernels, attention_call(): pl.pallas_call(functools.partial(attention_kernel, packs, len(blocks), dp...  54.8 us
    ppermute x32, starting transfers between devices, swap(): return lax.ppermute(x, axis, [(i, i ^ bit) for i in range(size)])  38.2 us
    ppermute x32, waiting for transfers between devices, swap(): return lax.ppermute(x, axis, [(i, i ^ bit) for i in range(size)])  35.4 us
    ppermute x4, waiting for transfers between devices, hop(): return lax.ppermute(block, ('dp', 'group'), pairs)  15.5 us
    unnamed x53, local copies, waits for them, and re-layouts  9.71 us
    pallas_call x3, Pallas kernels, combine_call(): pl.pallas_call(combine_kernel, in_specs=[SCALARS, whole(keep)] + [whole(r...  8.88 us
    pallas_call x1, Pallas kernels, tail_call(): pl.pallas_call(tail_kernel, grid=(tokens // rows,), in_specs=[SCALARS, pe...  8.66 us
    ppermute x4, waiting for transfers between devices, step(): ahead = lax.ppermute(self.ahead[-1], self.axis, self.forward)  8.5 us
  transfers between devices with their start and end apart: 43, of which 16 were waited for; matrix products, arithmetic and copies ran while one was open for 4% of the time, Pallas kernels for 40%

profile of v7, /device:TPU:0, one launch (start us, length us, event | category | flops | bytes accessed | tf_op | source)
XLA Modules:
  0.0 230.2 jit_solution(17836124418949063465)
XLA Ops:
  2.9 3.1 %collective-permute-start = (bf16[128,1024]{1,0:T(8,128)(2,1)S(1)}, bf16[128,1024]{1,0:T(8,128)(2,1)S(1)}, u32[]{:S(2)}, u32[]{:S(2)}) collective-permute-start(bf16[128,1024]{1,0:T(8,128)(2,1)S(1)} %pad_maximum_fusion.1.refs_0_), channel_id=1, source_target_pairs={{0,8},{8,16},{16,24},{24,28},{28,20},{20,12},{12,4},{4,0},{1,9},{9... | collective-permute-start | bytes 786440 | tf_op jit(solution)/shard_map/ppermute | solution.py:472
  7.3 8.3 %stem_norm.1 = (bf16[6,144,1024]{2,1,0:T(8,128)(2,1)}, bf16[2,6,144,1024]{3,2,1,0:T(8,128)(2,1)}, bf16[6,144,256]{2,1,0:T(8,128)(2,1)}) custom-call(s32[6,1,3]{2,1,0:T(1,128)} %copy.48.cnt_ref, s32[6,3,48]{2,1,0:T(4,128)} %idx_ref.1, bf16[6,144,640]{2,1,0:T(8,128)(2,1)} %patch_ref.1, bf16[640,1024]{1,0:T(8,128)(2,1)} %w_ref.1, f32[1,1024]{1,0:T(1,128)} %bitcast.34, ...), custom_call_target="tpu_custom_call" | custom-call | flops 8000000 | bytes 12000 | tf_op jit(solution)/shard_map/stem_norm/pallas_call | solution.py:97
  16.9 1.9 collective-permute-start.6
  20.9 5.3 %collective-permute-done.6.refs_2_ = bf16[128,1024]{1,0:T(8,128)(2,1)S(1)} collective-permute-done((bf16[128,1024]{1,0:T(8,128)(2,1)}, bf16[128,1024]{1,0:T(8,128)(2,1)S(1)}, u32[]{:S(2)}, u32[]{:S(2)}) %collective-permute-start.6) | collective-permute-done | bytes 262176 | tf_op jit(solution)/shard_map/ppermute | solution.py:456
  31.4 3.6 %collective-permute-done.7.refs_3_ = bf16[128,1024]{1,0:T(8,128)(2,1)S(1)} collective-permute-done((bf16[128,1024]{1,0:T(8,128)(2,1)S(1)}, bf16[128,1024]{1,0:T(8,128)(2,1)S(1)}, u32[]{:S(2)}, u32[]{:S(2)}) %collective-permute-start.7) | collective-permute-done | bytes 262176 | tf_op jit(solution)/shard_map/ppermute | solution.py:472
  38.6 4.2 %collective-permute-done.10.refs_4_ = bf16[128,1024]{1,0:T(8,128)(2,1)} collective-permute-done((bf16[128,1024]{1,0:T(8,128)(2,1)S(1)}, bf16[128,1024]{1,0:T(8,128)(2,1)}, u32[]{:S(2)}, u32[]{:S(2)}) %collective-permute-start.10) | collective-permute-done | bytes 262176 | tf_op jit(solution)/shard_map/ppermute | solution.py:472
  42.8 1.9 pad_maximum_fusion
  48.6 23.2 %attention.2 = (bf16[1728,1024]{1,0:T(8,128)(2,1)}, bf16[1024,1024]{1,0:T(8,128)(2,1)}, f32[512,1024]{1,0:T(8,128)}, bf16[512,512]{1,0:T(8,128)(2,1)}, bf16[512,512]{1,0:T(8,128)(2,1)}) custom-call(s32[2,6,3]{2,1,0:T(8,128)} %pad_add_fusion.cnt_ref, s32[8]{0:T(128)} %compare_select_fusion.2.owner_ref, s32[1]{0:T(128)} %bitcast.9.low_ref, ...), custom_call_target="tpu_custom_call" | custom-call | flops 20000000 | bytes 14000 | tf_op jit(solution)/shard_map/attention/pallas_call | solution.py:258
  74.0 2.0 fusion.1
  76.0 31.6 %attention.3 = (bf16[1728,1024]{1,0:T(8,128)(2,1)}, bf16[1024,1024]{1,0:T(8,128)(2,1)}, f32[512,1024]{1,0:T(8,128)}, bf16[512,512]{1,0:T(8,128)(2,1)}, bf16[512,...) custom-call(s32[2,6,3]{2,1,0:T(8,128)} %pad_add_fusion.cnt_ref, s32[8]{0:T(128)} %compare_select_fusion.2.owner_ref, ...), custom_call_target="tpu_custom_call" | custom-call | flops 20000000 | bytes 14000 | tf_op jit(solution)/shard_map/attention/pallas_call | solution.py:258
  110.4 3.0 %combine.3 = (f32[128,1024]{1,0:T(8,128)}, bf16[128,1024]{1,0:T(8,128)(2,1)}, bf16[128,1024]{1,0:T(8,128)(2,1)}, bf16[128,1024]{1,0:T(8,128)(2,1)}) custom-call(s32[1]{0:T(128)} %bitcast.11.place_ref, f32[512,1024]{1,0:T(8,128)} %get-tuple-element.155.keep_ref, bf16[512,512]{1,0:T(8,128)(2,1)} %copy-done.9, bf16[512,512]{1,0:T(8,128)(2,1)} %copy-done.10), custom_call_target="tpu_custom_call" | custom-call | flops 1000 | bytes 5000 | tf_op jit(solution)/shard_map/combine/pallas_call | solution.py:304
  116.4 1.9 collective-permute-start.19
  118.3 8.7 %tail.1 = (f32[320,1024]{1,0:T(8,128)}, f32[320,512]{1,0:T(8,128)}, f32[320,512]{1,0:T(8,128)}) custom-call(s32[1]{0:T(128)} %bitcast.1.core_ref, f32[864,1024]{1,0:T(8,128)} %get-tuple-element.154.own_ref, f32[864,1024]{1,0:T(8,128)} %copy-done.1, bf16[864,1024]{1,0:T(8,128)(2,1)} %bitcast.24, bf16[2,864,1024]{2,1,0:T(8,128)(2,1)} %bitcast.23, ...), custom_call_target="tpu_custom_call" | custom-call | flops 10000000 | bytes 12000 | tf_op jit(solution)/shard_map/tail/pallas_call | solution.py:411
  127.0 7.3 %collective-permute-done.21.second_ref = bf16[512,512]{1,0:T(8,128)(2,1)} collective-permute-done((bf16[512,512]{1,0:T(8,128)(2,1)}, bf16[512,512]{1,0:T(8,128)(2,1)}, u32[]{:S(2)}, u32[]{:S(2)}) %collective-permute-start.21) | collective-permute-done | bytes 524320 | tf_op jit(solution)/shard_map/ppermute | solution.py:456
  134.8 2.9 %collective-permute-start.24 = (bf16[128,1024]{1,0:T(8,128)(2,1)}, bf16[128,1024]{1,0:T(8,128)(2,1)S(1)}, u32[]{:S(2)}, u32[]{:S(2)}) collective-permute-start(bf16[128,1024]{1,0:T(8,128)(2,1)} %get-tuple-element.184), channel_id=1, source_target_pairs={{0,24},{4,28},{8,16},{12,20},{16,8},{20,12},{24,0},{28,4},{1,25},{... | collective-permute-start | bytes 786440 | tf_op jit(solution)/shard_map/ppermute | solution.py:456
  137.7 3.0 %combine.4 = (f32[128,1024]{1,0:T(8,128)}, bf16[128,1024]{1,0:T(8,128)(2,1)}, bf16[128,1024]{1,0:T(8,128)(2,1)}, bf16[128,1024]{1,0:T(8,128)(2,1)}) custom-call(s32[1]{0:T(128)} %bitcast.11.place_ref, f32[512,1024]{1,0:T(8,128)} %get-tuple-element.177.keep_ref, bf16[512,512]{1,0:T(8,128)(2,1)} %collective-permute-done.20.first_ref, ...), custom_call_target="tpu_custom_call" | custom-call | flops 1000 | bytes 5000 | tf_op jit(solution)/shard_map/combine/pallas_call | solution.py:304
  140.7 4.5 %collective-permute-done.24.refs_3_ = bf16[128,1024]{1,0:T(8,128)(2,1)S(1)} collective-permute-done((bf16[128,1024]{1,0:T(8,128)(2,1)}, bf16[128,1024]{1,0:T(8,128)(2,1)S(1)}, u32[]{:S(2)}, u32[]{:S(2)}) %collective-permute-start.24) | collective-permute-done | bytes 262176 | tf_op jit(solution)/shard_map/ppermute | solution.py:456
  146.3 2.8 %combine.5 = (f32[80,1024]{1,0:T(8,128)}, f32[80,1024]{1,0:T(8,128)}, f32[80,1024]{1,0:T(8,128)}, f32[80,1024]{1,0:T(8,128)}) custom-call(s32[1]{0:T(128)} %bitcast.place_ref, f32[320,1024]{1,0:T(8,128)} %get-tuple-element.174.keep_ref, f32[320,512]{1,0:T(8,128)} %copy-done.7, f32[320,512]{1,0:T(8,128)} %copy-done.8), custom_call_target="tpu_custom_call" | custom-call | flops 1000 | bytes 5000 | tf_op jit(solution)/shard_map/combine/pallas_call | solution.py:304
  152.6 5.3 %collective-permute-start.28 = (bf16[128,1024]{1,0:T(8,128)(2,1)}, bf16[128,1024]{1,0:T(8,128)(2,1)S(1)}, u32[]{:S(2)}, u32[]{:S(2)}) collective-permute-start(bf16[128,1024]{1,0:T(8,128)(2,1)} %get-tuple-element.194), channel_id=1, source_target_pairs={{0,8},{4,12},{8,0},{12,4},{16,24},{20,28},{24,16},{28,20},{1,9},{5... | collective-permute-start | bytes 786440 | tf_op jit(solution)/shard_map/ppermute | solution.py:456
  159.0 3.7 %mixed.1 = bf16[864,1024]{1,0:T(8,128)(2,1)} custom-call(bf16[1728,1024]{1,0:T(8,128)(2,1)} %get-tuple-element.137.refs_0_, bf16[1728,1024]{1,0:T(8,128)(2,1)} %get-tuple-element.191.refs_1_, bf16[1024,1024]{1,0:T(8,128)(2,1)} %get-tuple-element.138.refs_1_.refs_2_, bf16[1024,1024]{1,0:T(8,128)(2,1)} %get-tuple-element.192.refs_3_), custom_call_target="tpu_custom_call" | custom-call | flops 2000000 | bytes 5000 | tf_op jit(solution)/shard_map/mixed/pallas_call | solution.py:357
  162.7 6.0 %collective-permute-done.28.refs_1_ = bf16[128,1024]{1,0:T(8,128)(2,1)S(1)} collective-permute-done((bf16[128,1024]{1,0:T(8,128)(2,1)}, bf16[128,1024]{1,0:T(8,128)(2,1)S(1)}, u32[]{:S(2)}, u32[]{:S(2)}) %collective-permute-start.28) | collective-permute-done | bytes 262176 | tf_op jit(solution)/shard_map/ppermute | solution.py:456
  169.4 4.1 %collective-permute-start.34 = (bf16[128,1024]{1,0:T(8,128)(2,1)}, bf16[128,1024]{1,0:T(8,128)(2,1)}, u32[]{:S(2)}, u32[]{:S(2)}) collective-permute-start(bf16[128,1024]{1,0:T(8,128)(2,1)} %get-tuple-element.203), channel_id=1, source_target_pairs={{0,24},{4,28},{8,16},{12,20},{16,8},{20,12},{24,0},{28,4},{1,25},{... | collective-permute-start | bytes 786440 | tf_op jit(solution)/shard_map/ppermute | solution.py:456
  174.7 3.3 %collective-permute-start.32 = (f32[80,256]{1,0:T(8,128)S(1)}, f32[80,256]{1,0:T(8,128)S(1)}, u32[]{:S(2)}, u32[]{:S(2)}) collective-permute-start(f32[80,256]{1,0:T(8,128)S(1)} %get-tuple-element.239), channel_id=1, source_target_pairs={{0,24},{4,28},{8,16},{12,20},{16,8},{20,12},{24,0},{28,4},{1,25},{... | collective-permute-start | bytes 245768 | tf_op jit(solution)/shard_map/ppermute | solution.py:456
  180.0 5.4 %layer_output.1 = bf16[864,1024]{1,0:T(8,128)(2,1)} custom-call(s32[6,3]{1,0:T(8,128)} %copy.51.cnt_ref, bf16[864,1024]{1,0:T(8,128)(2,1)} %copy-done.2, bf16[864,1024]{1,0:T(8,128)(2,1)} %bitcast.25, bf16[1728,1024]{1,0:T(8,128)(2,1)} %get-tuple-element.137.refs_0_, bf16[1728,1024]{1,0:T(8,128)(2,1)} %get-tuple-element.191.refs_1_, ...), custom_call_target="tpu_custom_call" | custom-call | flops 5000000 | bytes 10000 | tf_op jit(solution)/shard_map/layer_output/pallas_call | solution.py:442
  185.4 6.0 %collective-permute-done.31 = f32[80,256]{1,0:T(8,128)S(1)} collective-permute-done((f32[80,256]{1,0:T(8,128)S(1)}, f32[80,256]{1,0:T(8,128)S(1)}, u32[]{:S(2)}, u32[]{:S(2)}) %collective-permute-start.31) | collective-permute-done | bytes 81952 | tf_op jit(solution)/shard_map/ppermute | solution.py:456
  191.4 2.0 collective-permute-start.35
  195.9 3.4 %collective-permute-done.36 = bf16[80,256]{1,0:T(8,128)(2,1)S(1)} collective-permute-done((bf16[80,256]{1,0:T(8,128)(2,1)S(1)}, bf16[80,256]{1,0:T(8,128)(2,1)S(1)}, u32[]{:S(2)}, u32[]{:S(2)}) %collective-permute-start.36) | collective-permute-done | bytes 40992 | tf_op jit(solution)/shard_map/ppermute | solution.py:456
  200.6 2.2 add_parts.3
  204.8 2.7 %collective-permute-start.40 = (bf16[80,1024]{1,0:T(8,128)(2,1)S(1)}, bf16[80,1024]{1,0:T(8,128)(2,1)S(1)}, u32[]{:S(2)}, u32[]{:S(2)}) collective-permute-start(bf16[80,1024]{1,0:T(8,128)(2,1)S(1)} %constant_dynamic-update-slice_fusion.4), channel_id=1, source_target_pairs={{0,6},{1,7},{2,4},{3,5},{4,2},{5,3},{6,0},{7,1},{8,14},{9,15},{10,... | collective-permute-start | bytes 491528 | tf_op jit(solution)/shard_map/ppermute | solution.py:511
  207.6 12.6 %collective-permute-done.39 = bf16[80,1024]{1,0:T(8,128)(2,1)S(1)} collective-permute-done((bf16[80,1024]{1,0:T(8,128)(2,1)S(1)}, bf16[80,1024]{1,0:T(8,128)(2,1)S(1)}, u32[]{:S(2)}, u32[]{:S(2)}) %collective-permute-start.39) | collective-permute-done | bytes 163872 | tf_op jit(solution)/shard_map/ppermute | solution.py:511
  220.2 2.9 %collective-permute-done.40 = bf16[80,1024]{1,0:T(8,128)(2,1)S(1)} collective-permute-done((bf16[80,1024]{1,0:T(8,128)(2,1)S(1)}, bf16[80,1024]{1,0:T(8,128)(2,1)S(1)}, u32[]{:S(2)}, u32[]{:S(2)}) %collective-permute-start.40) | collective-permute-done | bytes 163872 | tf_op jit(solution)/shard_map/ppermute | solution.py:511
  223.2 2.2 add_parts.2
  (145 shorter events, 48.3 us)
Async XLA Ops:
  2.9 12.7 %collective-permute-start = (bf16[128,1024]{1,0:T(8,128)(2,1)S(1)}, bf16[128,1024]{1,0:T(8,128)(2,1)S(1)}, u32[]{:S(2)}, u32[]{:S(2)}) collective-permute-start(bf16[128,1024]{1,0:T(8,128)(2,1)S(1)} %pad_maximum_fusion.1.refs_0_), channel_id=1, source_target_pairs={{0,8},{8,16},{16,24},{24,28},{28,20},{20,12},{12,4},{4,0},{1,9},{9... | collective-permute-start | bytes 786440 | tf_op jit(solution)/shard_map/ppermute | solution.py:472
  5.9 9.7 %collective-permute-start.1 = (bf16[128,1024]{1,0:T(8,128)(2,1)S(1)}, bf16[128,1024]{1,0:T(8,128)(2,1)S(1)}, u32[]{:S(2)}, u32[]{:S(2)}) collective-permute-start(bf16[128,1024]{1,0:T(8,128)(2,1)S(1)} %pad_maximum_fusion.1.refs_0_), channel_id=1, source_target_pairs={{8,0},{16,8},{24,16},{28,24},{20,28},{12,20},{4,12},{0,4},{9,1},{1... | collective-permute-start | bytes 786440 | tf_op jit(solution)/shard_map/ppermute | solution.py:474
  5.9 9.6 %collective-permute-start.2 = (s32[6,3]{0,1:T(4,128)}, s32[6,3]{0,1:T(4,128)S(1)}, u32[]{:S(2)}, u32[]{:S(2)}) collective-permute-start(s32[6,3]{0,1:T(4,128)} %param.13), channel_id=1, source_target_pairs={{0,1},{1,0},{2,3},{3,2},{4,5},{5,4},{6,7},{7,6},{8,9},{9,8},{10,11... | collective-permute-start | bytes 224 | tf_op jit(solution)/shard_map/ppermute | solution.py:456
  16.4 11.9 %collective-permute-start.5 = (bf16[2,864,1024]{2,1,0:T(8,128)(2,1)}, bf16[2,864,1024]{2,1,0:T(8,128)(2,1)S(1)}, u32[]{:S(2)}, u32[]{:S(2)}) collective-permute-start(bf16[2,864,1024]{2,1,0:T(8,128)(2,1)} %bitcast.18), channel_id=1, source_target_pairs={{0,1},{1,0},{2,3},{3,2},{4,5},{5,4},{6,7},{7,6},{8,9},{9,8},{10,11... | collective-permute-start | bytes 10616840 | tf_op jit(solution)/shard_map/ppermute | solution.py:456
  16.9 9.4 %collective-permute-start.6 = (bf16[128,1024]{1,0:T(8,128)(2,1)}, bf16[128,1024]{1,0:T(8,128)(2,1)S(1)}, u32[]{:S(2)}, u32[]{:S(2)}) collective-permute-start(bf16[128,1024]{1,0:T(8,128)(2,1)} %copy-done.3), channel_id=1, source_target_pairs={{0,2},{1,3},{2,0},{3,1},{4,6},{5,7},{6,4},{7,5},{8,10},{9,11},{10,... | collective-permute-start | bytes 786440 | tf_op jit(solution)/shard_map/ppermute | solution.py:456
  18.8 8.1 %collective-permute-start.3 = (bf16[128,1024]{1,0:T(8,128)(2,1)}, bf16[128,1024]{1,0:T(8,128)(2,1)S(1)}, u32[]{:S(2)}, u32[]{:S(2)}) collective-permute-start(bf16[128,1024]{1,0:T(8,128)(2,1)} %copy-done.18), channel_id=1, source_target_pairs={{0,8},{8,16},{16,24},{24,28},{28,20},{20,12},{12,4},{4,0},{1,9},{9... | collective-permute-start | bytes 786440 | tf_op jit(solution)/shard_map/ppermute | solution.py:472
  20.8 10.6 %collective-permute-start.9 = (bf16[128,1024]{1,0:T(8,128)(2,1)}, bf16[128,1024]{1,0:T(8,128)(2,1)S(1)}, u32[]{:S(2)}, u32[]{:S(2)}) collective-permute-start(bf16[128,1024]{1,0:T(8,128)(2,1)} %copy-done.18), channel_id=1, source_target_pairs={{0,2},{1,3},{2,0},{3,1},{4,6},{5,7},{6,4},{7,5},{8,10},{9,11},{10,... | collective-permute-start | bytes 786440 | tf_op jit(solution)/shard_map/ppermute | solution.py:456
  44.7 27.2 %collective-permute-start.14 = (bf16[384,1024]{1,0:T(8,128)(2,1)}, bf16[384,1024]{1,0:T(8,128)(2,1)}, u32[]{:S(2)}, u32[]{:S(2)}) collective-permute-start(bf16[384,1024]{1,0:T(8,128)(2,1)} %pad_maximum_fusion), channel_id=1, source_target_pairs={{0,2},{1,3},{2,0},{3,1},{4,6},{5,7},{6,4},{7,5},{8,10},{9,11},{10,... | collective-permute-start | bytes 2359304 | tf_op jit(solution)/shard_map/ppermute | solution.py:456
  45.3 26.5 %collective-permute-start.12 = (bf16[128,1024]{1,0:T(8,128)(2,1)}, bf16[128,1024]{1,0:T(8,128)(2,1)}, u32[]{:S(2)}, u32[]{:S(2)}) collective-permute-start(bf16[128,1024]{1,0:T(8,128)(2,1)} %copy-done.20), channel_id=1, source_target_pairs={{0,2},{1,3},{2,0},{3,1},{4,6},{5,7},{6,4},{7,5},{8,10},{9,11},{10,... | collective-permute-start | bytes 786440 | tf_op jit(solution)/shard_map/ppermute | solution.py:456
  46.8 25.0 %collective-permute-start.13 = (bf16[128,1024]{1,0:T(8,128)(2,1)}, bf16[128,1024]{1,0:T(8,128)(2,1)}, u32[]{:S(2)}, u32[]{:S(2)}) collective-permute-start(bf16[128,1024]{1,0:T(8,128)(2,1)} %collective-permute-done.10.refs_4_), channel_id=1, source_target_pairs={{0,2},{1,3},{2,0},{3,1},{4,6},{5,7},{6,4},{7,5},{8,10},{9,11},{10,... | collective-permute-start | bytes 786440 | tf_op jit(solution)/shard_map/ppermute | solution.py:456
  71.9 35.7 %collective-permute-start.15 = (bf16[512,512]{1,0:T(8,128)(2,1)}, bf16[512,512]{1,0:T(8,128)(2,1)S(1)}, u32[]{:S(2)}, u32[]{:S(2)}) collective-permute-start(bf16[512,512]{1,0:T(8,128)(2,1)} %get-tuple-element.152), channel_id=1, source_target_pairs={{0,4},{4,0},{8,12},{12,8},{16,20},{20,16},{24,28},{28,24},{1,5},{5... | collective-permute-start | bytes 1572872 | tf_op jit(solution)/shard_map/ppermute | solution.py:456
  72.4 35.2 %collective-permute-start.16 = (bf16[512,512]{1,0:T(8,128)(2,1)}, bf16[512,512]{1,0:T(8,128)(2,1)S(1)}, u32[]{:S(2)}, u32[]{:S(2)}) collective-permute-start(bf16[512,512]{1,0:T(8,128)(2,1)} %get-tuple-element.153), channel_id=1, source_target_pairs={{0,4},{4,0},{8,12},{12,8},{16,20},{20,16},{24,28},{28,24},{1,5},{5... | collective-permute-start | bytes 1572872 | tf_op jit(solution)/shard_map/ppermute | solution.py:456
  108.4 18.6 %collective-permute-start.20 = (bf16[512,512]{1,0:T(8,128)(2,1)}, bf16[512,512]{1,0:T(8,128)(2,1)}, u32[]{:S(2)}, u32[]{:S(2)}) collective-permute-start(bf16[512,512]{1,0:T(8,128)(2,1)} %get-tuple-element.172), channel_id=1, source_target_pairs={{0,4},{4,0},{8,12},{12,8},{16,20},{20,16},{24,28},{28,24},{1,5},{5... | collective-permute-start | bytes 1572872 | tf_op jit(solution)/shard_map/ppermute | solution.py:456
  108.9 25.4 %collective-permute-start.21 = (bf16[512,512]{1,0:T(8,128)(2,1)}, bf16[512,512]{1,0:T(8,128)(2,1)}, u32[]{:S(2)}, u32[]{:S(2)}) collective-permute-start(bf16[512,512]{1,0:T(8,128)(2,1)} %get-tuple-element.173), channel_id=1, source_target_pairs={{0,4},{4,0},{8,12},{12,8},{16,20},{20,16},{24,28},{28,24},{1,5},{5... | collective-permute-start | bytes 1572872 | tf_op jit(solution)/shard_map/ppermute | solution.py:456
  114.8 19.5 %collective-permute-start.18 = (bf16[128,1024]{1,0:T(8,128)(2,1)}, bf16[128,1024]{1,0:T(8,128)(2,1)}, u32[]{:S(2)}, u32[]{:S(2)}) collective-permute-start(bf16[128,1024]{1,0:T(8,128)(2,1)} %get-tuple-element.170), channel_id=1, source_target_pairs={{0,8},{4,12},{8,0},{12,4},{16,24},{20,28},{24,16},{28,20},{1,9},{5... | collective-permute-start | bytes 786440 | tf_op jit(solution)/shard_map/ppermute | solution.py:456
  116.4 17.9 %collective-permute-start.19 = (bf16[128,1024]{1,0:T(8,128)(2,1)}, bf16[128,1024]{1,0:T(8,128)(2,1)}, u32[]{:S(2)}, u32[]{:S(2)}) collective-permute-start(bf16[128,1024]{1,0:T(8,128)(2,1)} %get-tuple-element.171), channel_id=1, source_target_pairs={{0,16},{4,20},{8,24},{12,28},{16,0},{20,4},{24,8},{28,12},{1,17},{... | collective-permute-start | bytes 786440 | tf_op jit(solution)/shard_map/ppermute | solution.py:456
  134.3 10.9 %collective-permute-start.22 = (f32[320,512]{1,0:T(8,128)}, f32[320,512]{1,0:T(8,128)S(1)}, u32[]{:S(2)}, u32[]{:S(2)}) collective-permute-start(f32[320,512]{1,0:T(8,128)} %get-tuple-element.175), channel_id=1, source_target_pairs={{0,1},{1,0},{2,3},{3,2},{4,5},{5,4},{6,7},{7,6},{8,9},{9,8},{10,11... | collective-permute-start | bytes 1966088 | tf_op jit(solution)/shard_map/ppermute | solution.py:456
  134.3 10.9 %collective-permute-start.23 = (f32[320,512]{1,0:T(8,128)}, f32[320,512]{1,0:T(8,128)S(1)}, u32[]{:S(2)}, u32[]{:S(2)}) collective-permute-start(f32[320,512]{1,0:T(8,128)} %get-tuple-element.176), channel_id=1, source_target_pairs={{0,1},{1,0},{2,3},{3,2},{4,5},{5,4},{6,7},{7,6},{8,9},{9,8},{10,11... | collective-permute-start | bytes 1966088 | tf_op jit(solution)/shard_map/ppermute | solution.py:456
  134.8 10.4 %collective-permute-start.24 = (bf16[128,1024]{1,0:T(8,128)(2,1)}, bf16[128,1024]{1,0:T(8,128)(2,1)S(1)}, u32[]{:S(2)}, u32[]{:S(2)}) collective-permute-start(bf16[128,1024]{1,0:T(8,128)(2,1)} %get-tuple-element.184), channel_id=1, source_target_pairs={{0,24},{4,28},{8,16},{12,20},{16,8},{20,12},{24,0},{28,4},{1,25},{... | collective-permute-start | bytes 786440 | tf_op jit(solution)/shard_map/ppermute | solution.py:456
  149.2 19.5 %collective-permute-start.25 = (f32[80,1024]{1,0:T(8,128)}, f32[80,1024]{1,0:T(8,128)S(1)}, u32[]{:S(2)}, u32[]{:S(2)}) collective-permute-start(f32[80,1024]{1,0:T(8,128)} %get-tuple-element.188), channel_id=1, source_target_pairs={{0,4},{4,0},{8,12},{12,8},{16,20},{20,16},{24,28},{28,24},{1,5},{5... | collective-permute-start | bytes 983048 | tf_op jit(solution)/shard_map/ppermute | solution.py:456
  149.6 19.1 %collective-permute-start.26 = (f32[80,1024]{1,0:T(8,128)}, f32[80,1024]{1,0:T(8,128)S(1)}, u32[]{:S(2)}, u32[]{:S(2)}) collective-permute-start(f32[80,1024]{1,0:T(8,128)} %get-tuple-element.189), channel_id=1, source_target_pairs={{0,2},{1,3},{2,0},{3,1},{4,6},{5,7},{6,4},{7,5},{8,10},{9,11},{10,... | collective-permute-start | bytes 983048 | tf_op jit(solution)/shard_map/ppermute | solution.py:511
  151.1 18.3 %collective-permute-start.27 = (f32[80,1024]{1,0:T(8,128)}, f32[80,1024]{1,0:T(8,128)S(1)}, u32[]{:S(2)}, u32[]{:S(2)}) collective-permute-start(f32[80,1024]{1,0:T(8,128)} %get-tuple-element.190), channel_id=1, source_target_pairs={{0,6},{1,7},{2,4},{3,5},{4,2},{5,3},{6,0},{7,1},{8,14},{9,15},{10,... | collective-permute-start | bytes 983048 | tf_op jit(solution)/shard_map/ppermute | solution.py:511
  152.6 16.0 %collective-permute-start.28 = (bf16[128,1024]{1,0:T(8,128)(2,1)}, bf16[128,1024]{1,0:T(8,128)(2,1)S(1)}, u32[]{:S(2)}, u32[]{:S(2)}) collective-permute-start(bf16[128,1024]{1,0:T(8,128)(2,1)} %get-tuple-element.194), channel_id=1, source_target_pairs={{0,8},{4,12},{8,0},{12,4},{16,24},{20,28},{24,16},{28,20},{1,9},{5... | collective-permute-start | bytes 786440 | tf_op jit(solution)/shard_map/ppermute | solution.py:456
  158.0 10.7 %collective-permute-start.29 = (bf16[128,1024]{1,0:T(8,128)(2,1)S(1)}, bf16[128,1024]{1,0:T(8,128)(2,1)S(1)}, u32[]{:S(2)}, u32[]{:S(2)}) collective-permute-start(bf16[128,1024]{1,0:T(8,128)(2,1)S(1)} %copy-done.22), channel_id=1, source_target_pairs={{0,16},{4,20},{8,24},{12,28},{16,0},{20,4},{24,8},{28,12},{1,17},{... | collective-permute-start | bytes 786440 | tf_op jit(solution)/shard_map/ppermute | solution.py:456
  169.4 9.3 %collective-permute-start.33 = (bf16[864,1024]{1,0:T(8,128)(2,1)}, bf16[864,1024]{1,0:T(8,128)(2,1)S(1)}, u32[]{:S(2)}, u32[]{:S(2)}) collective-permute-start(bf16[864,1024]{1,0:T(8,128)(2,1)} %mixed.1), channel_id=1, source_target_pairs={{0,1},{1,0},{2,3},{3,2},{4,5},{5,4},{6,7},{7,6},{8,9},{9,8},{10,11... | collective-permute-start | bytes 5308424 | tf_op jit(solution)/shard_map/ppermute | solution.py:456
  169.4 16.0 %collective-permute-start.34 = (bf16[128,1024]{1,0:T(8,128)(2,1)}, bf16[128,1024]{1,0:T(8,128)(2,1)}, u32[]{:S(2)}, u32[]{:S(2)}) collective-permute-start(bf16[128,1024]{1,0:T(8,128)(2,1)} %get-tuple-element.203), channel_id=1, source_target_pairs={{0,24},{4,28},{8,16},{12,20},{16,8},{20,12},{24,0},{28,4},{1,25},{... | collective-permute-start | bytes 786440 | tf_op jit(solution)/shard_map/ppermute | solution.py:456
  173.6 11.8 %collective-permute-start.30 = (f32[80,256]{1,0:T(8,128)S(1)}, f32[80,256]{1,0:T(8,128)S(1)}, u32[]{:S(2)}, u32[]{:S(2)}) collective-permute-start(f32[80,256]{1,0:T(8,128)S(1)} %get-tuple-element.241), channel_id=1, source_target_pairs={{0,8},{4,12},{8,0},{12,4},{16,24},{20,28},{24,16},{28,20},{1,9},{5... | collective-permute-start | bytes 245768 | tf_op jit(solution)/shard_map/ppermute | solution.py:456
  173.7 17.7 %collective-permute-start.31 = (f32[80,256]{1,0:T(8,128)S(1)}, f32[80,256]{1,0:T(8,128)S(1)}, u32[]{:S(2)}, u32[]{:S(2)}) collective-permute-start(f32[80,256]{1,0:T(8,128)S(1)} %get-tuple-element.240), channel_id=1, source_target_pairs={{0,16},{4,20},{8,24},{12,28},{16,0},{20,4},{24,8},{28,12},{1,17},{... | collective-permute-start | bytes 245768 | tf_op jit(solution)/shard_map/ppermute | solution.py:456
  174.7 16.7 %collective-permute-start.32 = (f32[80,256]{1,0:T(8,128)S(1)}, f32[80,256]{1,0:T(8,128)S(1)}, u32[]{:S(2)}, u32[]{:S(2)}) collective-permute-start(f32[80,256]{1,0:T(8,128)S(1)} %get-tuple-element.239), channel_id=1, source_target_pairs={{0,24},{4,28},{8,16},{12,20},{16,8},{20,12},{24,0},{28,4},{1,25},{... | collective-permute-start | bytes 245768 | tf_op jit(solution)/shard_map/ppermute | solution.py:456
  202.8 22.6 %collective-permute-start.42 = (f32[128,1024]{1,0:T(8,128)}, f32[128,1024]{1,0:T(8,128)S(1)}, u32[]{:S(2)}, u32[]{:S(2)}) collective-permute-start(f32[128,1024]{1,0:T(8,128)} %add_parts.3), channel_id=1, source_target_pairs={{0,2},{1,3},{2,0},{3,1},{4,6},{5,7},{6,4},{7,5},{8,10},{9,11},{10,... | collective-permute-start | bytes 1572872 | tf_op jit(solution)/shard_map/ppermute | solution.py:456
  204.2 15.9 %collective-permute-start.39 = (bf16[80,1024]{1,0:T(8,128)(2,1)S(1)}, bf16[80,1024]{1,0:T(8,128)(2,1)S(1)}, u32[]{:S(2)}, u32[]{:S(2)}) collective-permute-start(bf16[80,1024]{1,0:T(8,128)(2,1)S(1)} %constant_dynamic-update-slice_fusion.4), channel_id=1, source_target_pairs={{0,2},{1,3},{2,0},{3,1},{4,6},{5,7},{6,4},{7,5},{8,10},{9,11},{10,... | collective-permute-start | bytes 491528 | tf_op jit(solution)/shard_map/ppermute | solution.py:511
  204.8 18.3 %collective-permute-start.40 = (bf16[80,1024]{1,0:T(8,128)(2,1)S(1)}, bf16[80,1024]{1,0:T(8,128)(2,1)S(1)}, u32[]{:S(2)}, u32[]{:S(2)}) collective-permute-start(bf16[80,1024]{1,0:T(8,128)(2,1)S(1)} %constant_dynamic-update-slice_fusion.4), channel_id=1, source_target_pairs={{0,6},{1,7},{2,4},{3,5},{4,2},{5,3},{6,0},{7,1},{8,14},{9,15},{10,... | collective-permute-start | bytes 491528 | tf_op jit(solution)/shard_map/ppermute | solution.py:511
  (35 other events, 303.0 us)

commit v8 on v7

--- a/solution.py
+++ b/solution.py
@@ -128,8 +128,7 @@
 ):
     earlier, refs = refs[: 2 * (packs or 0)], refs[2 * (packs or 0) :]
     blocks, refs = refs[:blocks], refs[blocks:]
-    out_ref, w_ref, keep_ref, *refs = refs
-    sends, refs = refs[:2], refs[2:]
+    out_ref, w_ref, keep_ref, other_ref, *refs = refs
     n_s, g_s, qkv, total = refs[-4:]
     half, step = pl.program_id(0), pl.program_id(1)
     rows = n_s.shape[0]
@@ -211,10 +210,8 @@
             at = slice(b * size, (b + 1) * size)
             mine = pl.multiple_of((2 * b + low) * size, size)
             other = pl.multiple_of((2 * b + 1 - low) * size, size)
-            keep_ref[at, :] = total[pl.ds(mine, size), :]
-            for c, send_ref in enumerate(sends):
-                cols = send_ref.shape[1]
-                send_ref[at, :] = total[pl.ds(other, size), c * cols : (c + 1) * cols].astype(BF16)
+            keep_ref[at, :] = total[pl.ds(mine, size), :].astype(keep_ref.dtype)
+            other_ref[at, :] = total[pl.ds(other, size), :].astype(other_ref.dtype)
 
     if packs is not None:
         back = dot_nt(out_ref[:, : 3 * width], w_ref[:, : 3 * width])
@@ -253,7 +250,7 @@
     at = lambda h, i: (h * steps + i, 0)
     packs = None if earlier is None else len(earlier[0])
     back = [] if earlier is None else two_halves(rows, steps, ())
-    send = jax.ShapeDtypeStruct((D // 2, cols // 2), BF16)
+    grads = jax.ShapeDtypeStruct((D // 2, cols), BF16 if earlier is None else F32)
     back_shape = jax.ShapeDtypeStruct((tokens, D), F32)
     return pl.pallas_call(
         functools.partial(attention_kernel, packs, len(blocks), dp),
@@ -264,15 +261,12 @@
         + [pl.BlockSpec((rows, cols // 4 * 3), at)] * (packs or 0)
         + [whole((D, cols // 4 * 3))] * (packs or 0)
         + [whole(b.shape) for b in blocks],
-        out_specs=[pl.BlockSpec((rows, cols), at), whole((D, cols)), whole((D // 2, cols))]
-        + [whole(send.shape)] * 2
-        + back,
+        out_specs=[pl.BlockSpec((rows, cols), at), whole((D, cols))] + [whole(grads.shape)] * 2 + back,
         out_shape=[
             jax.ShapeDtypeStruct((2 * tokens, cols), BF16),
             jax.ShapeDtypeStruct((D, cols), BF16),
-            jax.ShapeDtypeStruct((D // 2, cols), F32),
-            send,
-            send,
+            grads,
+            grads,
         ]
         + [back_shape] * len(back),
         scratch_shapes=[
@@ -287,25 +281,30 @@
     )(counts, owners, low, own, far, own, far, *[x for group in earlier or () for x in group], *blocks)
 
 
-def combine_kernel(place_ref, keep_ref, first_ref, second_ref, *refs):
-    rows, cols = refs[0].shape
+def combine_kernel(counts, place_ref, keep_ref, *refs):
+    recvs, refs = refs[: sum(counts)], refs[sum(counts) :]
+    rows = refs[0].shape[0]
     place = place_ref[0]
-    for c, recv_ref in enumerate((first_ref, second_ref)):
-        half = slice(c * cols // 2, (c + 1) * cols // 2)
-        for j, ref in enumerate(refs):
-            at = pl.ds(pl.multiple_of((place ^ j) * rows, rows), rows)
-            ref[:, half] = (keep_ref[at, half] + recv_ref[at, :].astype(F32)).astype(ref.dtype)
-
-
-def combine_call(place, keep, recvs, blocks, dtype):
-    rows, cols = keep.shape[0] // blocks, keep.shape[1]
+    for j, ref in enumerate(refs):
+        at = pl.ds(pl.multiple_of((place ^ j) * rows, rows), rows)
+        total = keep_ref[at, :]
+        first = 0
+        for count in counts:
+            pieces = [r[at, :].astype(F32) for r in recvs[first : first + count]]
+            total = total + (pieces[0] if count == 1 else jnp.concatenate(pieces, axis=1))
+            first += count
+        ref[...] = total.astype(ref.dtype)
+
+
+def combine_call(place, keep, arrived, dtypes):
+    rows, cols = keep.shape[0] // len(dtypes), keep.shape[1]
+    recvs = [r for pieces in arrived for r in pieces]
     whole = lambda a: pl.BlockSpec(a.shape, lambda: (0, 0))
-    shapes = [jax.ShapeDtypeStruct((rows, cols), F32 if j == 0 else dtype) for j in range(blocks)]
     return pl.pallas_call(
-        combine_kernel,
+        functools.partial(combine_kernel, [len(pieces) for pieces in arrived]),
         in_specs=[SCALARS, whole(keep)] + [whole(r) for r in recvs],
-        out_specs=[pl.BlockSpec((rows, cols), lambda: (0, 0))] * blocks,
-        out_shape=shapes,
+        out_specs=[pl.BlockSpec((rows, cols), lambda: (0, 0))] * len(dtypes),
+        out_shape=[jax.ShapeDtypeStruct((rows, cols), d) for d in dtypes],
         compiler_params=params(),
         cost_estimate=cost(1e6, 5e6),
         name="combine",
@@ -468,16 +467,19 @@
         self.backward = [(order[(i + 1) % size], order[i]) for i in range(size)]
         self.ahead, self.behind = [x], [x]
 
-    def step(self, *beside):
-        ahead = lax.ppermute(self.ahead[-1], self.axis, self.forward)
+    def send(self):
+        moved = [lax.ppermute(self.ahead[-1], self.axis, self.forward)]
         if len(self.behind) <= (self.size - 1) // 2:
-            behind = lax.ppermute(self.behind[-1], self.axis, self.backward)
-            ahead, behind, beside = together(ahead, behind, beside)
-            self.behind.append(behind)
-        else:
-            ahead, beside = together(ahead, beside)
-        self.ahead.append(ahead)
-        return beside
+            moved.append(lax.ppermute(self.behind[-1], self.axis, self.backward))
+        return moved
+
+    def receive(self, moved):
+        self.ahead.append(moved[0])
+        self.behind.extend(moved[1:])
+
+    @property
+    def steps(self):
+        return len(self.ahead) - 1
 
     def owners(self):
         size = self.size
@@ -488,9 +490,16 @@
         return jnp.where(at < size // 2, 2 * at, 2 * (size - 1 - at) + 1)
 
 
+def step_all(rings, *beside):
+    moved, beside = together([ring.send() for ring in rings], beside)
+    for ring, blocks in zip(rings, moved):
+        ring.receive(blocks)
+    return beside
+
+
 def halve_stem(recv, keep, group):
     mine = lax.axis_index("group") // 2 * 2 + lax.axis_index("dp") % 2
-    return combine_call(mine.reshape(1), keep, recv, group // 2 * 2, F32)
+    return combine_call(mine.reshape(1), keep, [recv], [F32] * (group // 2 * 2))
 
 
 def sum_stem(parts, beside, after, dp, group):
@@ -569,9 +578,8 @@
     core = (lax.axis_index("group") % 2).reshape(1)
 
     shard = jnp.concatenate([w_qkv.reshape(w_qkv.shape[0], 3 * width), w_out.T], axis=1)
-    ring = Ring(shard, "dp", dp)
-    cross = lambda x: [swap(x, "group", group, 2 * f) for f in fars]
-    far = [cross(shard)]
+    cross = lambda x, f: swap(x, "group", group, 2 * f)
+    far_shards = [cross(shard, f) for f in fars]
     counts = vis_count.astype(jnp.int32)
     counts_far = swap(counts, "group", group, 1)
     table, genc = encoding_tables(patches.shape[1])
@@ -586,77 +594,71 @@
         jnp.asarray(genc),
         out_grad.reshape(scenes, TOK, D),
     )
-    stem, counts_far = ring.step(stem, counts_far)
+    stem, counts_far, far_shards = together(stem, counts_far, far_shards)
     emb = stem[0].reshape(tokens, D)
     both = [stem[1].reshape(2, tokens, D)]
     cols = stem[2].reshape(tokens, stem[2].shape[2])
     both_counts = jnp.stack([counts, counts_far])
     both.append(swap(both[0], "group", group, 1))
-    far.append(cross(ring.ahead[-1]))
-    both, far[0] = ring.step(both, far[0])
-    while len(ring.ahead) < dp // 2:
-        far.append(cross(ring.ahead[-1]))
-        (far[-2],) = ring.step(far[-2])
-    far.append(cross(ring.ahead[-1]))
-    (far[-2],) = ring.step(far[-2])
+    rings = [Ring(x, "dp", dp) for x in far_shards]
+    passed = []
+    (both,) = step_all(rings, both)
+    while rings[0].steps < dp // 2:
+        passed.append(cross(rings[0].ahead[-1], 1))
+        if len(passed) > 1:
+            (passed[-2],) = step_all(rings, passed[-2])
+        else:
+            step_all(rings)
+    ring = rings[0]
     ring.ahead, ring.behind = together(ring.ahead, ring.behind)
-    far.append(cross(ring.ahead[-1]))
+    passed.append(cross(ring.ahead[-1], 1))
     behind = ring.behind[1:]
-    far.append(cross(jnp.concatenate(behind, axis=0)))
+    passed.append(cross(jnp.concatenate(behind, axis=0), 1))
     owners = ring.owners()
 
-    packs, kept, coming, landing = [], [], [], []
-
-    def first_to_rest(n):
-        return combine_call(high, kept[n], coming[n], dp // 2, BF16)
-
-    def rest_swaps(blocks):
-        return [blocks[0]] + [swap(blocks[j], "dp", dp, 2 * j) for j in rests]
-
-    weights = []
-    for n in range(group // 2):
-        if n == 0:
-            blocks = ring.ahead + behind
+    packs, weights, crossing = [], [], []
+    for f in list(fars) + [0]:
+        if f:
+            blocks = rings[f - 1].ahead + rings[f - 1].behind[1:]
         else:
             rows = shard.shape[0]
-            last = [far[-1][n - 1][b * rows : (b + 1) * rows] for b in range(len(behind))]
-            blocks = [f[n - 1] for f in far[:-1]] + last
-        earlier = (packs, weights) if n == len(fars) else None
-        made = attention_call(both_counts, owners, low, *both, earlier, blocks, dp)
-        if n == 0:
-            made, far[-3:] = together(made, far[-3:])
+            blocks = [shard] + passed[:-1] + [passed[-1][b * rows : (b + 1) * rows] for b in range(len(behind))]
+        made = attention_call(both_counts, owners, low, *both, None if f else (packs, weights), blocks, dp)
+        if f == 1:
+            made, passed[-3:] = together(made, passed[-3:])
+        elif f:
+            made = together(*made)
         else:
-            made, coming[-1] = together(made, coming[-1])
-        pack, weight, keep, first, second, *back = made
+            made, others = together(made, [c[1] for c in crossing])
+        pack, weight, keep, other, *back = made
         packs.append(pack)
         weights.append(weight)
-        kept.append(keep)
-        coming.append([swap(x, "dp", dp, 1) for x in (first, second)])
+        if f:
+            crossing.append([cross(keep, f), cross(other, f)])
     back_far = swap(back[1], "group", group, 1)
-    blocks, back_far = together([first_to_rest(n) for n in range(len(fars))], back_far)
-    landing = [rest_swaps(b) for b in blocks]
-    near = dp // 2 * 3 // 4
-    stem_made, landing[-1][:near], coming[-1] = together(
-        tail_call(core, back[0], back_far, emb, both[0], cols, gain), landing[-1][:near], coming[-1]
+    for x in others:
+        other = other + x.astype(F32)
+    coming = swap(other.astype(BF16), "dp", dp, 1)
+    stem_made, keeps = together(
+        tail_call(core, back[0], back_far, emb, both[0], cols, gain), [c[0] for c in crossing]
     )
     stem_keep, *stem_recv = stem_made
     stem_recv = [swap(x, "group", group, 1) for x in stem_recv]
-    blocks = list(first_to_rest(-1))
-    stem_recv, blocks[0], landing = together(stem_recv, blocks[0], landing)
-    last = rest_swaps(blocks)
-
-    def after(mixed, *near_last):
+    stem_recv, coming = together(stem_recv, coming)
+    stem_parts = halve_stem(stem_recv, stem_keep, group)
+    kinds = [F32 if j < 2 else BF16 for j in range(dp // 2)]
+    blocks = combine_call(high, keep, [[k] for k in keeps] + [[coming]], kinds)
+    landing = [blocks[0]] + [swap(blocks[j], "dp", dp, 2 * j) for j in rests]
+    near = dp // 2 * 3 // 4
+
+    def after(mixed, *arrived):
         mixed = swap(mixed, "group", group, 1)
-        return [output_call(counts, mixed, emb, packs, weights)] + list(near_last) + last[near:]
-
-    grad_w_stem, (output, *last) = sum_stem(
-        halve_stem(stem_recv, stem_keep, group), [mixed_call(packs, weights)] + last[:near], after, dp, group
+        return [output_call(counts, mixed, emb, packs, weights)] + list(arrived) + landing[near:]
+
+    grad_w_stem, (output, *landing) = sum_stem(
+        stem_parts, [mixed_call(packs, weights)] + landing[:near], after, dp, group
     )
-    shares = [add_call(parts) for parts in landing + [last]]
-
-    total = shares[0]
-    for f in fars:
-        total = total + swap(shares[f], "group", group, 2 * f)
+    total = add_call(landing)
     grad_w_qkv = total[:, : 3 * width].reshape(total.shape[0], 3, width)
     grad_w_out = total[:, 3 * width :].T
     return (output.reshape(scenes, GROUPS, CAP, D), grad_w_stem, grad_w_qkv, grad_w_out)

time: 231 us -> 217 us (0.939)
  starting transfers between devices: 53.2 us -> 38.1 us
  Pallas kernels: 94.1 us -> 89.9 us
    ppermute x32 -> x27, starting transfers between devices: 38.2 us -> 24.2 us  [swap(): return lax.ppermute(x, axis, [(i, i ^ bit) for i in range(size)])]
    ppermute x4, waiting for transfers between devices: 15.5 us -> 2.74 us  [hop(): return lax.ppermute(block, ('dp', 'group'), pairs)]
    ppermute x7, waiting for transfers between devices: 11.1 us -> 23.8 us  [the longest x4 19.6 us: send(): moved = [lax.ppermute(self.ahead[-1], self.axis, self.forward)]]
    convert_element_type x0 -> x1, other arithmetic: none -> 3.18 us  [on_device(): coming = swap(other.astype(BF16), 'dp', dp, 1)]
    pallas_call x3 -> x2, Pallas kernels: 8.88 us -> 6.87 us  [combine_call(): pl.pallas_call(functools.partial(combine_kernel, [len(pieces) for pieces...]
    ppermute x32 -> x27, waiting for transfers between devices: 35.4 us -> 37.2 us  [swap(): return lax.ppermute(x, axis, [(i, i ^ bit) for i in range(size)])]
    unnamed x53 -> x51, local copies, waits for them, and re-layouts: 9.71 us -> 9.92 us
  transfers between devices with their start and end apart: 43 -> 38, of which waited for: 16 -> 18; matrix products, arithmetic and copies ran while one was open for 4% -> 6% of each run, Pallas kernels for 40% -> 40%
where the time goes in v8:
time: 217 us
  Pallas kernels  89.9 us (41%)
  waiting for transfers between devices  63.7 us (29%)
  starting transfers between devices  38.1 us (18%)
  local copies, waits for them, and re-layouts  15.9 us (7%)
  other arithmetic  8.36 us (4%)
    pallas_call x2, Pallas kernels, attention_call(): pl.pallas_call(functools.partial(attention_kernel, packs, len(blocks), dp...  54.6 us
    ppermute x27, waiting for transfers between devices, swap(): return lax.ppermute(x, axis, [(i, i ^ bit) for i in range(size)])  37.2 us
    ppermute x27, starting transfers between devices, swap(): return lax.ppermute(x, axis, [(i, i ^ bit) for i in range(size)])  24.2 us
    ppermute x4, waiting for transfers between devices, send(): moved = [lax.ppermute(self.ahead[-1], self.axis, self.forward)]  19.6 us
    unnamed x51, local copies, waits for them, and re-layouts  9.92 us
    pallas_call x1, Pallas kernels, tail_call(): pl.pallas_call(tail_kernel, grid=(tokens // rows,), in_specs=[SCALARS, pe...  8.68 us
    pallas_call x1, Pallas kernels, stem_call(): pl.pallas_call(stem_kernel, grid=(scenes // block,), in_specs=[per((1, GR...  8.35 us
    pallas_call x2, Pallas kernels, combine_call(): pl.pallas_call(functools.partial(combine_kernel, [len(pieces) for pieces...  6.87 us
  transfers between devices with their start and end apart: 38, of which 18 were waited for; matrix products, arithmetic and copies ran while one was open for 6% of the time, Pallas kernels for 40%

profile of v8, /device:TPU:0, one launch (start us, length us, event | category | flops | bytes accessed | tf_op | source)
XLA Modules:
  0.0 216.8 jit_solution(1405113423348329798)
XLA Ops:
  2.9 3.0 %collective-permute-start.1 = (bf16[128,1024]{1,0:T(8,128)(2,1)S(1)}, bf16[128,1024]{1,0:T(8,128)(2,1)S(1)}, u32[]{:S(2)}, u32[]{:S(2)}) collective-permute-start(bf16[128,1024]{1,0:T(8,128)(2,1)S(1)} %pad_maximum_fusion.1.refs_2_), channel_id=1, source_target_pairs={{0,2},{1,3},{2,0},{3,1},{4,6},{5,7},{6,4},{7,5},{8,10},{9,11},{10,... | collective-permute-start | bytes 786440 | tf_op jit(solution)/shard_map/ppermute | solution.py:455
  7.2 8.4 %stem_norm.1 = (bf16[6,144,1024]{2,1,0:T(8,128)(2,1)}, bf16[2,6,144,1024]{3,2,1,0:T(8,128)(2,1)}, bf16[6,144,256]{2,1,0:T(8,128)(2,1)}) custom-call(s32[6,1,3]{2,1,0:T(1,128)} %copy.45.cnt_ref, s32[6,3,48]{2,1,0:T(4,128)} %idx_ref.1, bf16[6,144,640]{2,1,0:T(8,128)(2,1)} %patch_ref.1, bf16[640,1024]{1,0:T(8,128)(2,1)} %w_ref.1, f32[1,1024]{1,0:T(1,128)} %bitcast.34, ...), custom_call_target="tpu_custom_call" | custom-call | flops 8000000 | bytes 12000 | tf_op jit(solution)/shard_map/stem_norm/pallas_call | solution.py:97
  18.8 6.4 %collective-permute-done.2.refs_1_ = bf16[128,1024]{1,0:T(8,128)(2,1)S(1)} collective-permute-done((bf16[128,1024]{1,0:T(8,128)(2,1)}, bf16[128,1024]{1,0:T(8,128)(2,1)S(1)}, u32[]{:S(2)}, u32[]{:S(2)}) %collective-permute-start.2) | collective-permute-done | bytes 262176 | tf_op jit(solution)/shard_map/ppermute | solution.py:471
  29.1 4.5 %collective-permute-done.5.refs_2_ = bf16[128,1024]{1,0:T(8,128)(2,1)S(1)} collective-permute-done((bf16[128,1024]{1,0:T(8,128)(2,1)S(1)}, bf16[128,1024]{1,0:T(8,128)(2,1)S(1)}, u32[]{:S(2)}, u32[]{:S(2)}) %collective-permute-start.5) | collective-permute-done | bytes 262176 | tf_op jit(solution)/shard_map/ppermute | solution.py:471
  37.5 3.8 %collective-permute-done.7.refs_3_ = bf16[128,1024]{1,0:T(8,128)(2,1)S(1)} collective-permute-done((bf16[128,1024]{1,0:T(8,128)(2,1)S(1)}, bf16[128,1024]{1,0:T(8,128)(2,1)S(1)}, u32[]{:S(2)}, u32[]{:S(2)}) %collective-permute-start.7) | collective-permute-done | bytes 262176 | tf_op jit(solution)/shard_map/ppermute | solution.py:471
  44.4 4.9 %collective-permute-done.10.refs_4_ = bf16[128,1024]{1,0:T(8,128)(2,1)} collective-permute-done((bf16[128,1024]{1,0:T(8,128)(2,1)S(1)}, bf16[128,1024]{1,0:T(8,128)(2,1)}, u32[]{:S(2)}, u32[]{:S(2)}) %collective-permute-start.10) | collective-permute-done | bytes 262176 | tf_op jit(solution)/shard_map/ppermute | solution.py:471
  54.2 22.7 %attention.2 = (bf16[1728,1024]{1,0:T(8,128)(2,1)}, bf16[1024,1024]{1,0:T(8,128)(2,1)}, bf16[512,1024]{1,0:T(8,128)(2,1)}, bf16[512,1024]{1,0:T(8,128)(2,1)}) custom-call(s32[2,6,3]{2,1,0:T(8,128)} %pad_add_fusion.cnt_ref, s32[8]{0:T(128)} %compare_select_fusion.2.owner_ref, s32[1]{0:T(128)} %bitcast.9.low_ref, bf16[2,864,1024]{2,1,0:T(8,128)(2,1)} %bitcast.19, ...), custom_call_target="tpu_custom_call" | custom-call | flops 20000000 | bytes 14000 | tf_op jit(solution)/shard_map/attention/pallas_call | solution.py:255
  76.9 1.9 collective-permute-done.13.refs_6_
  78.8 2.0 fusion.1
  80.8 31.9 %attention.3 = (bf16[1728,1024]{1,0:T(8,128)(2,1)}, bf16[1024,1024]{1,0:T(8,128)(2,1)}, f32[512,1024]{1,0:T(8,128)}, f32[512,1024]{1,0:T(8,128)}, f32[864,1024]{1,0:T(8,128)}, /*index=5*/f32[864,1024]{1,0:T(8,128)}) custom-call(s32[2,6,3]{2,1,0:T(8,128)} %pad_add_fusion.cnt_ref, s32[8]{0:T(128)} %compare_select_fusion.2.owner_ref, s32[1]{0:T(128)} %bitcast.9.low_ref, ...), custom_call_target="tpu_custom_call" | custom-call | flops 20000000 | bytes 14000 | tf_op jit(solution)/shard_map/attention/pallas_call | solution.py:255
  113.7 2.0 collective-permute-start.17
  115.8 3.2 %add_convert_fusion = bf16[512,1024]{1,0:T(8,128)(2,1)} fusion(f32[512,1024]{1,0:T(8,128)} %get-tuple-element.140, bf16[512,1024]{1,0:T(8,128)(2,1)} %copy-done.4), kind=kLoop, calls=%fused_computation | loop fusion | flops 1572864 | bytes 4194304 | tf_op jit(solution)/shard_map/convert_element_type | solution.py:641
  120.2 1.9 copy-done.1
  122.1 8.7 %tail.1 = (f32[320,1024]{1,0:T(8,128)}, f32[320,512]{1,0:T(8,128)}, f32[320,512]{1,0:T(8,128)}) custom-call(s32[1]{0:T(128)} %bitcast.1.core_ref, f32[864,1024]{1,0:T(8,128)} %get-tuple-element.129.own_ref, f32[864,1024]{1,0:T(8,128)} %copy-done.1, bf16[864,1024]{1,0:T(8,128)(2,1)} %bitcast.24, bf16[2,864,1024]{2,1,0:T(8,128)(2,1)} %bitcast.23, ...), custom_call_target="tpu_custom_call" | custom-call | flops 10000000 | bytes 12000 | tf_op jit(solution)/shard_map/tail/pallas_call | solution.py:410
  130.7 9.2 %collective-permute-done.17.refs_0_ = bf16[512,1024]{1,0:T(8,128)(2,1)} collective-permute-done((bf16[512,1024]{1,0:T(8,128)(2,1)}, bf16[512,1024]{1,0:T(8,128)(2,1)}, u32[]{:S(2)}, u32[]{:S(2)}) %collective-permute-start.17) | collective-permute-done | bytes 1048608 | tf_op jit(solution)/shard_map/ppermute | solution.py:455
  140.4 4.1 %collective-permute-done.20.refs_1_ = bf16[512,1024]{1,0:T(8,128)(2,1)} collective-permute-done((bf16[512,1024]{1,0:T(8,128)(2,1)}, bf16[512,1024]{1,0:T(8,128)(2,1)}, u32[]{:S(2)}, u32[]{:S(2)}) %collective-permute-start.20) | collective-permute-done | bytes 1048608 | tf_op jit(solution)/shard_map/ppermute | solution.py:455
  144.6 4.0 %combine.3 = (f32[128,1024]{1,0:T(8,128)}, f32[128,1024]{1,0:T(8,128)}, bf16[128,1024]{1,0:T(8,128)(2,1)}, bf16[128,1024]{1,0:T(8,128)(2,1)}) custom-call(s32[1]{0:T(128)} %bitcast.13.place_ref, f32[512,1024]{1,0:T(8,128)} %get-tuple-element.150.keep_ref, bf16[512,1024]{1,0:T(8,128)(2,1)} %collective-permute-done.17.refs_0_, ...), custom_call_target="tpu_custom_call" | custom-call | flops 1000 | bytes 5000 | tf_op jit(solution)/shard_map/combine/pallas_call | solution.py:303
  150.2 2.9 %combine.2 = (f32[80,1024]{1,0:T(8,128)}, f32[80,1024]{1,0:T(8,128)}, f32[80,1024]{1,0:T(8,128)}, f32[80,1024]{1,0:T(8,128)}) custom-call(s32[1]{0:T(128)} %bitcast.place_ref, f32[320,1024]{1,0:T(8,128)} %get-tuple-element.137.keep_ref, f32[320,512]{1,0:T(8,128)} %copy-done.8, f32[320,512]{1,0:T(8,128)} %copy-done.9), custom_call_target="tpu_custom_call" | custom-call | flops 1000 | bytes 5000 | tf_op jit(solution)/shard_map/combine/pallas_call | solution.py:303
  153.6 2.9 %collective-permute-start.23 = (f32[80,1024]{1,0:T(8,128)}, f32[80,1024]{1,0:T(8,128)S(1)}, u32[]{:S(2)}, u32[]{:S(2)}) collective-permute-start(f32[80,1024]{1,0:T(8,128)} %get-tuple-element.147), channel_id=1, source_target_pairs={{0,6},{1,7},{2,4},{3,5},{4,2},{5,3},{6,0},{7,1},{8,14},{9,15},{10,... | collective-permute-start | bytes 983048 | tf_op jit(solution)/shard_map/ppermute | solution.py:520
  157.5 3.7 %mixed.1 = bf16[864,1024]{1,0:T(8,128)(2,1)} custom-call(bf16[1728,1024]{1,0:T(8,128)(2,1)} %get-tuple-element.115.refs_0_, bf16[1728,1024]{1,0:T(8,128)(2,1)} %get-tuple-element.148.refs_1_, bf16[1024,1024]{1,0:T(8,128)(2,1)} %get-tuple-element.116.refs_1_.refs_2_, bf16[1024,1024]{1,0:T(8,128)(2,1)} %get-tuple-element.149.refs_3_), custom_call_target="tpu_custom_call" | custom-call | flops 2000000 | bytes 5000 | tf_op jit(solution)/shard_map/mixed/pallas_call | solution.py:356
  161.2 8.4 %collective-permute-done.25.refs_2_ = bf16[128,1024]{1,0:T(8,128)(2,1)S(1)} collective-permute-done((bf16[128,1024]{1,0:T(8,128)(2,1)S(1)}, bf16[128,1024]{1,0:T(8,128)(2,1)S(1)}, u32[]{:S(2)}, u32[]{:S(2)}) %collective-permute-start.25) | collective-permute-done | bytes 262176 | tf_op jit(solution)/shard_map/ppermute | solution.py:455
  174.0 2.6 %collective-permute-start.27 = (f32[80,256]{1,0:T(8,128)S(1)}, f32[80,256]{1,0:T(8,128)S(1)}, u32[]{:S(2)}, u32[]{:S(2)}) collective-permute-start(f32[80,256]{1,0:T(8,128)S(1)} %get-tuple-element.196), channel_id=1, source_target_pairs={{0,16},{4,20},{8,24},{12,28},{16,0},{20,4},{24,8},{28,12},{1,17},{... | collective-permute-start | bytes 245768 | tf_op jit(solution)/shard_map/ppermute | solution.py:455
  180.3 5.4 %layer_output.1 = bf16[864,1024]{1,0:T(8,128)(2,1)} custom-call(s32[6,3]{1,0:T(8,128)} %copy.51.cnt_ref, bf16[864,1024]{1,0:T(8,128)(2,1)} %copy-done.2, bf16[864,1024]{1,0:T(8,128)(2,1)} %bitcast.25, bf16[1728,1024]{1,0:T(8,128)(2,1)} %get-tuple-element.115.refs_0_, bf16[1728,1024]{1,0:T(8,128)(2,1)} %get-tuple-element.148.refs_1_, ...), custom_call_target="tpu_custom_call" | custom-call | flops 5000000 | bytes 10000 | tf_op jit(solution)/shard_map/layer_output/pallas_call | solution.py:441
  185.7 5.3 %collective-permute-done.27 = f32[80,256]{1,0:T(8,128)S(1)} collective-permute-done((f32[80,256]{1,0:T(8,128)S(1)}, f32[80,256]{1,0:T(8,128)S(1)}, u32[]{:S(2)}, u32[]{:S(2)}) %collective-permute-start.27) | collective-permute-done | bytes 81952 | tf_op jit(solution)/shard_map/ppermute | solution.py:455
  191.1 2.0 collective-permute-start.31
  193.7 1.9 collective-permute-start.33
  195.6 3.0 %collective-permute-done.32 = bf16[80,256]{1,0:T(8,128)(2,1)S(1)} collective-permute-done((bf16[80,256]{1,0:T(8,128)(2,1)S(1)}, bf16[80,256]{1,0:T(8,128)(2,1)S(1)}, u32[]{:S(2)}, u32[]{:S(2)}) %collective-permute-start.32) | collective-permute-done | bytes 40992 | tf_op jit(solution)/shard_map/ppermute | solution.py:455
  200.8 2.2 %collective-permute-start.36 = (bf16[80,1024]{1,0:T(8,128)(2,1)S(1)}, bf16[80,1024]{1,0:T(8,128)(2,1)S(1)}, u32[]{:S(2)}, u32[]{:S(2)}) collective-permute-start(bf16[80,1024]{1,0:T(8,128)(2,1)S(1)} %constant_dynamic-update-slice_fusion.4), channel_id=1, source_target_pairs={{0,6},{1,7},{2,4},{3,5},{4,2},{5,3},{6,0},{7,1},{8,14},{9,15},{10,... | collective-permute-start | bytes 491528 | tf_op jit(solution)/shard_map/ppermute | solution.py:520
  203.1 3.5 %collective-permute-done.34 = bf16[80,1024]{1,0:T(8,128)(2,1)S(1)} collective-permute-done((bf16[80,1024]{1,0:T(8,128)(2,1)S(1)}, bf16[80,1024]{1,0:T(8,128)(2,1)S(1)}, u32[]{:S(2)}, u32[]{:S(2)}) %collective-permute-start.34) | collective-permute-done | bytes 163872 | tf_op jit(solution)/shard_map/ppermute | solution.py:455
  206.6 2.1 collective-permute-done.36
  208.9 2.2 %add_parts.1 = f32[128,1024]{1,0:T(8,128)} custom-call(f32[128,1024]{1,0:T(8,128)} %get-tuple-element.168.refs_0_, f32[128,1024]{1,0:T(8,128)} %copy-done.10, bf16[128,1024]{1,0:T(8,128)(2,1)} %copy-done.15, bf16[128,1024]{1,0:T(8,128)(2,1)} %collective-permute-done.30.refs_3_), custom_call_target="tpu_custom_call" | custom-call | flops 1000 | bytes 2000 | tf_op jit(solution)/shard_map/add_parts/pallas_call | solution.py:323
  215.0 1.8 maximum_convert_fusion
  (131 shorter events, 43.3 us)
Async XLA Ops:
  2.9 12.7 %collective-permute-start.1 = (bf16[128,1024]{1,0:T(8,128)(2,1)S(1)}, bf16[128,1024]{1,0:T(8,128)(2,1)S(1)}, u32[]{:S(2)}, u32[]{:S(2)}) collective-permute-start(bf16[128,1024]{1,0:T(8,128)(2,1)S(1)} %pad_maximum_fusion.1.refs_2_), channel_id=1, source_target_pairs={{0,2},{1,3},{2,0},{3,1},{4,6},{5,7},{6,4},{7,5},{8,10},{9,11},{10,... | collective-permute-start | bytes 786440 | tf_op jit(solution)/shard_map/ppermute | solution.py:455
  5.9 9.7 %collective-permute-start = (s32[6,3]{0,1:T(4,128)}, s32[6,3]{0,1:T(4,128)S(1)}, u32[]{:S(2)}, u32[]{:S(2)}) collective-permute-start(s32[6,3]{0,1:T(4,128)} %param.13), channel_id=1, source_target_pairs={{0,1},{1,0},{2,3},{3,2},{4,5},{5,4},{6,7},{7,6},{8,9},{9,8},{10,11... | collective-permute-start | bytes 224 | tf_op jit(solution)/shard_map/ppermute | solution.py:455
  16.3 10.2 %collective-permute-start.4 = (bf16[2,864,1024]{2,1,0:T(8,128)(2,1)}, bf16[2,864,1024]{2,1,0:T(8,128)(2,1)S(1)}, u32[]{:S(2)}, u32[]{:S(2)}) collective-permute-start(bf16[2,864,1024]{2,1,0:T(8,128)(2,1)} %bitcast.18), channel_id=1, source_target_pairs={{0,1},{1,0},{2,3},{3,2},{4,5},{5,4},{6,7},{7,6},{8,9},{9,8},{10,11... | collective-permute-start | bytes 10616840 | tf_op jit(solution)/shard_map/ppermute | solution.py:455
  16.8 8.4 %collective-permute-start.2 = (bf16[128,1024]{1,0:T(8,128)(2,1)}, bf16[128,1024]{1,0:T(8,128)(2,1)S(1)}, u32[]{:S(2)}, u32[]{:S(2)}) collective-permute-start(bf16[128,1024]{1,0:T(8,128)(2,1)} %copy-done.16), channel_id=1, source_target_pairs={{0,8},{8,16},{16,24},{24,28},{28,20},{20,12},{12,4},{4,0},{1,9},{9... | collective-permute-start | bytes 786440 | tf_op jit(solution)/shard_map/ppermute | solution.py:471
  18.4 8.1 %collective-permute-start.3 = (bf16[128,1024]{1,0:T(8,128)(2,1)}, bf16[128,1024]{1,0:T(8,128)(2,1)S(1)}, u32[]{:S(2)}, u32[]{:S(2)}) collective-permute-start(bf16[128,1024]{1,0:T(8,128)(2,1)} %copy-done.16), channel_id=1, source_target_pairs={{8,0},{16,8},{24,16},{28,24},{20,28},{12,20},{4,12},{0,4},{9,1},{1... | collective-permute-start | bytes 786440 | tf_op jit(solution)/shard_map/ppermute | solution.py:473
  26.5 7.1 %collective-permute-start.5 = (bf16[128,1024]{1,0:T(8,128)(2,1)S(1)}, bf16[128,1024]{1,0:T(8,128)(2,1)S(1)}, u32[]{:S(2)}, u32[]{:S(2)}) collective-permute-start(bf16[128,1024]{1,0:T(8,128)(2,1)S(1)} %collective-permute-done.2.refs_1_), channel_id=1, source_target_pairs={{0,8},{8,16},{16,24},{24,28},{28,20},{20,12},{12,4},{4,0},{1,9},{9... | collective-permute-start | bytes 786440 | tf_op jit(solution)/shard_map/ppermute | solution.py:471
  28.2 6.8 %collective-permute-start.6 = (bf16[128,1024]{1,0:T(8,128)(2,1)S(1)}, bf16[128,1024]{1,0:T(8,128)(2,1)S(1)}, u32[]{:S(2)}, u32[]{:S(2)}) collective-permute-start(bf16[128,1024]{1,0:T(8,128)(2,1)S(1)} %collective-permute-done.3.refs_5_), channel_id=1, source_target_pairs={{8,0},{16,8},{24,16},{28,24},{20,28},{12,20},{4,12},{0,4},{9,1},{1... | collective-permute-start | bytes 786440 | tf_op jit(solution)/shard_map/ppermute | solution.py:473
  28.6 8.9 %collective-permute-start.9 = (bf16[128,1024]{1,0:T(8,128)(2,1)S(1)}, bf16[128,1024]{1,0:T(8,128)(2,1)S(1)}, u32[]{:S(2)}, u32[]{:S(2)}) collective-permute-start(bf16[128,1024]{1,0:T(8,128)(2,1)S(1)} %collective-permute-done.2.refs_1_), channel_id=1, source_target_pairs={{0,2},{1,3},{2,0},{3,1},{4,6},{5,7},{6,4},{7,5},{8,10},{9,11},{10,... | collective-permute-start | bytes 786440 | tf_op jit(solution)/shard_map/ppermute | solution.py:455
  34.9 6.4 %collective-permute-start.7 = (bf16[128,1024]{1,0:T(8,128)(2,1)S(1)}, bf16[128,1024]{1,0:T(8,128)(2,1)S(1)}, u32[]{:S(2)}, u32[]{:S(2)}) collective-permute-start(bf16[128,1024]{1,0:T(8,128)(2,1)S(1)} %collective-permute-done.5.refs_2_), channel_id=1, source_target_pairs={{0,8},{8,16},{16,24},{24,28},{28,20},{20,12},{12,4},{4,0},{1,9},{9... | collective-permute-start | bytes 786440 | tf_op jit(solution)/shard_map/ppermute | solution.py:471
  36.5 6.4 %collective-permute-start.8 = (bf16[128,1024]{1,0:T(8,128)(2,1)S(1)}, bf16[128,1024]{1,0:T(8,128)(2,1)S(1)}, u32[]{:S(2)}, u32[]{:S(2)}) collective-permute-start(bf16[128,1024]{1,0:T(8,128)(2,1)S(1)} %collective-permute-done.6.refs_6_), channel_id=1, source_target_pairs={{8,0},{16,8},{24,16},{28,24},{20,28},{12,20},{4,12},{0,4},{9,1},{1... | collective-permute-start | bytes 786440 | tf_op jit(solution)/shard_map/ppermute | solution.py:473
  36.9 7.5 %collective-permute-start.11 = (bf16[128,1024]{1,0:T(8,128)(2,1)S(1)}, bf16[128,1024]{1,0:T(8,128)(2,1)}, u32[]{:S(2)}, u32[]{:S(2)}) collective-permute-start(bf16[128,1024]{1,0:T(8,128)(2,1)S(1)} %collective-permute-done.5.refs_2_), channel_id=1, source_target_pairs={{0,2},{1,3},{2,0},{3,1},{4,6},{5,7},{6,4},{7,5},{8,10},{9,11},{10,... | collective-permute-start | bytes 786440 | tf_op jit(solution)/shard_map/ppermute | solution.py:455
  42.9 6.5 %collective-permute-start.10 = (bf16[128,1024]{1,0:T(8,128)(2,1)S(1)}, bf16[128,1024]{1,0:T(8,128)(2,1)}, u32[]{:S(2)}, u32[]{:S(2)}) collective-permute-start(bf16[128,1024]{1,0:T(8,128)(2,1)S(1)} %collective-permute-done.7.refs_3_), channel_id=1, source_target_pairs={{0,8},{8,16},{16,24},{24,28},{28,20},{20,12},{12,4},{4,0},{1,9},{9... | collective-permute-start | bytes 786440 | tf_op jit(solution)/shard_map/ppermute | solution.py:471
  50.3 28.5 %collective-permute-start.14 = (bf16[384,1024]{1,0:T(8,128)(2,1)}, bf16[384,1024]{1,0:T(8,128)(2,1)}, u32[]{:S(2)}, u32[]{:S(2)}) collective-permute-start(bf16[384,1024]{1,0:T(8,128)(2,1)} %pad_maximum_fusion), channel_id=1, source_target_pairs={{0,2},{1,3},{2,0},{3,1},{4,6},{5,7},{6,4},{7,5},{8,10},{9,11},{10,... | collective-permute-start | bytes 2359304 | tf_op jit(solution)/shard_map/ppermute | solution.py:455
  50.9 25.9 %collective-permute-start.12 = (bf16[128,1024]{1,0:T(8,128)(2,1)}, bf16[128,1024]{1,0:T(8,128)(2,1)}, u32[]{:S(2)}, u32[]{:S(2)}) collective-permute-start(bf16[128,1024]{1,0:T(8,128)(2,1)} %copy-done.19), channel_id=1, source_target_pairs={{0,2},{1,3},{2,0},{3,1},{4,6},{5,7},{6,4},{7,5},{8,10},{9,11},{10,... | collective-permute-start | bytes 786440 | tf_op jit(solution)/shard_map/ppermute | solution.py:455
  52.4 26.4 %collective-permute-start.13 = (bf16[128,1024]{1,0:T(8,128)(2,1)}, bf16[128,1024]{1,0:T(8,128)(2,1)}, u32[]{:S(2)}, u32[]{:S(2)}) collective-permute-start(bf16[128,1024]{1,0:T(8,128)(2,1)} %collective-permute-done.10.refs_4_), channel_id=1, source_target_pairs={{0,2},{1,3},{2,0},{3,1},{4,6},{5,7},{6,4},{7,5},{8,10},{9,11},{10,... | collective-permute-start | bytes 786440 | tf_op jit(solution)/shard_map/ppermute | solution.py:455
  78.8 33.9 %collective-permute-start.15 = (bf16[512,1024]{1,0:T(8,128)(2,1)}, bf16[512,1024]{1,0:T(8,128)(2,1)S(1)}, u32[]{:S(2)}, u32[]{:S(2)}) collective-permute-start(bf16[512,1024]{1,0:T(8,128)(2,1)} %get-tuple-element.128), channel_id=1, source_target_pairs={{0,2},{1,3},{2,0},{3,1},{4,6},{5,7},{6,4},{7,5},{8,10},{9,11},{10,... | collective-permute-start | bytes 3145736 | tf_op jit(solution)/shard_map/ppermute | solution.py:455
  113.7 6.4 %collective-permute-start.16 = (f32[864,1024]{1,0:T(8,128)}, f32[864,1024]{1,0:T(8,128)S(1)}, u32[]{:S(2)}, u32[]{:S(2)}) collective-permute-start(f32[864,1024]{1,0:T(8,128)} %get-tuple-element.130), channel_id=1, source_target_pairs={{0,1},{1,0},{2,3},{3,2},{4,5},{5,4},{6,7},{7,6},{8,9},{9,8},{10,11... | collective-permute-start | bytes 10616840 | tf_op jit(solution)/shard_map/ppermute | solution.py:455
  113.7 26.2 %collective-permute-start.17 = (bf16[512,1024]{1,0:T(8,128)(2,1)}, bf16[512,1024]{1,0:T(8,128)(2,1)}, u32[]{:S(2)}, u32[]{:S(2)}) collective-permute-start(bf16[512,1024]{1,0:T(8,128)(2,1)} %get-tuple-element.136), channel_id=1, source_target_pairs={{0,2},{1,3},{2,0},{3,1},{4,6},{5,7},{6,4},{7,5},{8,10},{9,11},{10,... | collective-permute-start | bytes 3145736 | tf_op jit(solution)/shard_map/ppermute | solution.py:455
  119.0 25.6 %collective-permute-start.20 = (bf16[512,1024]{1,0:T(8,128)(2,1)}, bf16[512,1024]{1,0:T(8,128)(2,1)}, u32[]{:S(2)}, u32[]{:S(2)}) collective-permute-start(bf16[512,1024]{1,0:T(8,128)(2,1)} %add_convert_fusion), channel_id=1, source_target_pairs={{0,4},{4,0},{8,12},{12,8},{16,20},{20,16},{24,28},{28,24},{1,5},{5... | collective-permute-start | bytes 3145736 | tf_op jit(solution)/shard_map/ppermute | solution.py:455
  148.6 21.6 %collective-permute-start.24 = (f32[128,1024]{1,0:T(8,128)}, f32[128,1024]{1,0:T(8,128)S(1)}, u32[]{:S(2)}, u32[]{:S(2)}) collective-permute-start(f32[128,1024]{1,0:T(8,128)} %get-tuple-element.154), channel_id=1, source_target_pairs={{0,8},{4,12},{8,0},{12,4},{16,24},{20,28},{24,16},{28,20},{1,9},{5... | collective-permute-start | bytes 1572872 | tf_op jit(solution)/shard_map/ppermute | solution.py:455
  153.0 16.6 %collective-permute-start.21 = (f32[80,1024]{1,0:T(8,128)}, f32[80,1024]{1,0:T(8,128)S(1)}, u32[]{:S(2)}, u32[]{:S(2)}) collective-permute-start(f32[80,1024]{1,0:T(8,128)} %get-tuple-element.145), channel_id=1, source_target_pairs={{0,4},{4,0},{8,12},{12,8},{16,20},{20,16},{24,28},{28,24},{1,5},{5... | collective-permute-start | bytes 983048 | tf_op jit(solution)/shard_map/ppermute | solution.py:455
  153.3 16.3 %collective-permute-start.22 = (f32[80,1024]{1,0:T(8,128)}, f32[80,1024]{1,0:T(8,128)S(1)}, u32[]{:S(2)}, u32[]{:S(2)}) collective-permute-start(f32[80,1024]{1,0:T(8,128)} %get-tuple-element.146), channel_id=1, source_target_pairs={{0,2},{1,3},{2,0},{3,1},{4,6},{5,7},{6,4},{7,5},{8,10},{9,11},{10,... | collective-permute-start | bytes 983048 | tf_op jit(solution)/shard_map/ppermute | solution.py:520
  153.6 16.6 %collective-permute-start.23 = (f32[80,1024]{1,0:T(8,128)}, f32[80,1024]{1,0:T(8,128)S(1)}, u32[]{:S(2)}, u32[]{:S(2)}) collective-permute-start(f32[80,1024]{1,0:T(8,128)} %get-tuple-element.147), channel_id=1, source_target_pairs={{0,6},{1,7},{2,4},{3,5},{4,2},{5,3},{6,0},{7,1},{8,14},{9,15},{10,... | collective-permute-start | bytes 983048 | tf_op jit(solution)/shard_map/ppermute | solution.py:520
  156.5 13.1 %collective-permute-start.25 = (bf16[128,1024]{1,0:T(8,128)(2,1)S(1)}, bf16[128,1024]{1,0:T(8,128)(2,1)S(1)}, u32[]{:S(2)}, u32[]{:S(2)}) collective-permute-start(bf16[128,1024]{1,0:T(8,128)(2,1)S(1)} %copy-done.21), channel_id=1, source_target_pairs={{0,16},{4,20},{8,24},{12,28},{16,0},{20,4},{24,8},{28,12},{1,17},{... | collective-permute-start | bytes 786440 | tf_op jit(solution)/shard_map/ppermute | solution.py:455
  170.9 8.1 %collective-permute-start.29 = (bf16[864,1024]{1,0:T(8,128)(2,1)}, bf16[864,1024]{1,0:T(8,128)(2,1)S(1)}, u32[]{:S(2)}, u32[]{:S(2)}) collective-permute-start(bf16[864,1024]{1,0:T(8,128)(2,1)} %mixed.1), channel_id=1, source_target_pairs={{0,1},{1,0},{2,3},{3,2},{4,5},{5,4},{6,7},{7,6},{8,9},{9,8},{10,11... | collective-permute-start | bytes 5308424 | tf_op jit(solution)/shard_map/ppermute | solution.py:455
  170.9 14.8 %collective-permute-start.30 = (bf16[128,1024]{1,0:T(8,128)(2,1)}, bf16[128,1024]{1,0:T(8,128)(2,1)}, u32[]{:S(2)}, u32[]{:S(2)}) collective-permute-start(bf16[128,1024]{1,0:T(8,128)(2,1)} %get-tuple-element.163), channel_id=1, source_target_pairs={{0,24},{4,28},{8,16},{12,20},{16,8},{20,12},{24,0},{28,4},{1,25},{... | collective-permute-start | bytes 786440 | tf_op jit(solution)/shard_map/ppermute | solution.py:455
  173.9 11.8 %collective-permute-start.26 = (f32[80,256]{1,0:T(8,128)S(1)}, f32[80,256]{1,0:T(8,128)S(1)}, u32[]{:S(2)}, u32[]{:S(2)}) collective-permute-start(f32[80,256]{1,0:T(8,128)S(1)} %get-tuple-element.197), channel_id=1, source_target_pairs={{0,8},{4,12},{8,0},{12,4},{16,24},{20,28},{24,16},{28,20},{1,9},{5... | collective-permute-start | bytes 245768 | tf_op jit(solution)/shard_map/ppermute | solution.py:455
  174.0 17.1 %collective-permute-start.27 = (f32[80,256]{1,0:T(8,128)S(1)}, f32[80,256]{1,0:T(8,128)S(1)}, u32[]{:S(2)}, u32[]{:S(2)}) collective-permute-start(f32[80,256]{1,0:T(8,128)S(1)} %get-tuple-element.196), channel_id=1, source_target_pairs={{0,16},{4,20},{8,24},{12,28},{16,0},{20,4},{24,8},{28,12},{1,17},{... | collective-permute-start | bytes 245768 | tf_op jit(solution)/shard_map/ppermute | solution.py:455
  176.6 14.5 %collective-permute-start.28 = (f32[80,256]{1,0:T(8,128)S(1)}, f32[80,256]{1,0:T(8,128)S(1)}, u32[]{:S(2)}, u32[]{:S(2)}) collective-permute-start(f32[80,256]{1,0:T(8,128)S(1)} %get-tuple-element.195), channel_id=1, source_target_pairs={{0,24},{4,28},{8,16},{12,20},{16,8},{20,12},{24,0},{28,4},{1,25},{... | collective-permute-start | bytes 245768 | tf_op jit(solution)/shard_map/ppermute | solution.py:455
  199.5 7.1 %collective-permute-start.34 = (bf16[80,1024]{1,0:T(8,128)(2,1)S(1)}, bf16[80,1024]{1,0:T(8,128)(2,1)S(1)}, u32[]{:S(2)}, u32[]{:S(2)}) collective-permute-start(bf16[80,1024]{1,0:T(8,128)(2,1)S(1)} %constant_dynamic-update-slice_fusion.4), channel_id=1, source_target_pairs={{0,4},{4,0},{8,12},{12,8},{16,20},{20,16},{24,28},{28,24},{1,5},{5... | collective-permute-start | bytes 491528 | tf_op jit(solution)/shard_map/ppermute | solution.py:455
  200.0 6.6 %collective-permute-start.35 = (bf16[80,1024]{1,0:T(8,128)(2,1)S(1)}, bf16[80,1024]{1,0:T(8,128)(2,1)S(1)}, u32[]{:S(2)}, u32[]{:S(2)}) collective-permute-start(bf16[80,1024]{1,0:T(8,128)(2,1)S(1)} %constant_dynamic-update-slice_fusion.4), channel_id=1, source_target_pairs={{0,2},{1,3},{2,0},{3,1},{4,6},{5,7},{6,4},{7,5},{8,10},{9,11},{10,... | collective-permute-start | bytes 491528 | tf_op jit(solution)/shard_map/ppermute | solution.py:520
  200.8 8.0 %collective-permute-start.36 = (bf16[80,1024]{1,0:T(8,128)(2,1)S(1)}, bf16[80,1024]{1,0:T(8,128)(2,1)S(1)}, u32[]{:S(2)}, u32[]{:S(2)}) collective-permute-start(bf16[80,1024]{1,0:T(8,128)(2,1)S(1)} %constant_dynamic-update-slice_fusion.4), channel_id=1, source_target_pairs={{0,6},{1,7},{2,4},{3,5},{4,2},{5,3},{6,0},{7,1},{8,14},{9,15},{10,... | collective-permute-start | bytes 491528 | tf_op jit(solution)/shard_map/ppermute | solution.py:520
  (29 other events, 314.9 us)

commit v9 on v8

--- a/solution.py
+++ b/solution.py
@@ -57,6 +57,7 @@
     cnt_ref, idx_ref, patch_ref, w_ref, gain_ref, parts, genc_ref, og_ref,
     emb_ref, rows_ref, cols_ref,
 ):
+    step = pl.program_id(0)
     scenes = patch_ref.shape[0]
     patch_iota = lax.broadcasted_iota(jnp.int32, (parts.shape[1], CAP), 0)
     slot = lax.broadcasted_iota(jnp.int32, (CAP, 1), 0)
@@ -70,7 +71,7 @@
             placed.append(
                 (dot_nn(onehot, parts[0]) + dot_nn(onehot, parts[1])) + dot_nn(onehot, parts[2])
             )
-            live = slot < cnt_ref[s, :, g : g + 1]
+            live = slot < cnt_ref[pl.ds(step * scenes + s, 1), g : g + 1]
             rows_ref[1, s, rows, :] = jnp.where(live, og_ref[s, rows, :].astype(F32), 0.0).astype(BF16)
         summed = dot_nn(jnp.concatenate(picked, axis=0), w_ref[start * PIX : end * PIX, :])
         for s in range(scenes):
@@ -98,7 +99,7 @@
         stem_kernel,
         grid=(scenes // block,),
         in_specs=[
-            per((1, GROUPS)),
+            whole(counts),
             per((GROUPS, CAP)),
             per((patch_count, width)),
             whole(w_stem),
@@ -120,7 +121,7 @@
         compiler_params=params(),
         cost_estimate=cost(8e9, 12e6),
         name="stem_norm",
-    )(counts.reshape(scenes, 1, GROUPS), index, patches, w_stem, gain, table, genc, out_grad)
+    )(counts, index, patches, w_stem, gain, table, genc, out_grad)
 
 
 def attention_kernel(
@@ -128,7 +129,8 @@
 ):
     earlier, refs = refs[: 2 * (packs or 0)], refs[2 * (packs or 0) :]
     blocks, refs = refs[:blocks], refs[blocks:]
-    out_ref, w_ref, keep_ref, other_ref, *refs = refs
+    out_ref, w_ref, *refs = refs
+    keeps, other_ref, refs = refs[:2], refs[2], refs[3:]
     n_s, g_s, qkv, total = refs[-4:]
     half, step = pl.program_id(0), pl.program_id(1)
     rows = n_s.shape[0]
@@ -210,7 +212,9 @@
             at = slice(b * size, (b + 1) * size)
             mine = pl.multiple_of((2 * b + low) * size, size)
             other = pl.multiple_of((2 * b + 1 - low) * size, size)
-            keep_ref[at, :] = total[pl.ds(mine, size), :].astype(keep_ref.dtype)
+            for c in range(2):
+                cols = slice(c * 2 * width, (c + 1) * 2 * width)
+                keeps[c][at, :] = total[pl.ds(mine, size), cols].astype(keeps[c].dtype)
             other_ref[at, :] = total[pl.ds(other, size), :].astype(other_ref.dtype)
 
     if packs is not None:
@@ -250,7 +254,8 @@
     at = lambda h, i: (h * steps + i, 0)
     packs = None if earlier is None else len(earlier[0])
     back = [] if earlier is None else two_halves(rows, steps, ())
-    grads = jax.ShapeDtypeStruct((D // 2, cols), BF16 if earlier is None else F32)
+    kind = BF16 if earlier is None else F32
+    grads = [jax.ShapeDtypeStruct((D // 2, c), kind) for c in (cols // 2, cols // 2, cols)]
     back_shape = jax.ShapeDtypeStruct((tokens, D), F32)
     return pl.pallas_call(
         functools.partial(attention_kernel, packs, len(blocks), dp),
@@ -261,12 +266,11 @@
         + [pl.BlockSpec((rows, cols // 4 * 3), at)] * (packs or 0)
         + [whole((D, cols // 4 * 3))] * (packs or 0)
         + [whole(b.shape) for b in blocks],
-        out_specs=[pl.BlockSpec((rows, cols), at), whole((D, cols))] + [whole(grads.shape)] * 2 + back,
+        out_specs=[pl.BlockSpec((rows, cols), at), whole((D, cols))] + [whole(g.shape) for g in grads] + back,
         out_shape=[
             jax.ShapeDtypeStruct((2 * tokens, cols), BF16),
             jax.ShapeDtypeStruct((D, cols), BF16),
-            grads,
-            grads,
+            *grads,
         ]
         + [back_shape] * len(back),
         scratch_shapes=[
@@ -281,34 +285,35 @@
     )(counts, owners, low, own, far, own, far, *[x for group in earlier or () for x in group], *blocks)
 
 
-def combine_kernel(counts, place_ref, keep_ref, *refs):
-    recvs, refs = refs[: sum(counts)], refs[sum(counts) :]
+def combine_kernel(counts, place_ref, *refs):
+    ins, refs = refs[: sum(counts)], refs[sum(counts) :]
     rows = refs[0].shape[0]
     place = place_ref[0]
     for j, ref in enumerate(refs):
         at = pl.ds(pl.multiple_of((place ^ j) * rows, rows), rows)
-        total = keep_ref[at, :]
+        total = None
         first = 0
         for count in counts:
-            pieces = [r[at, :].astype(F32) for r in recvs[first : first + count]]
-            total = total + (pieces[0] if count == 1 else jnp.concatenate(pieces, axis=1))
+            pieces = [r[at, :].astype(F32) for r in ins[first : first + count]]
+            new = pieces[0] if count == 1 else jnp.concatenate(pieces, axis=1)
+            total = new if total is None else total + new
             first += count
         ref[...] = total.astype(ref.dtype)
 
 
-def combine_call(place, keep, arrived, dtypes):
-    rows, cols = keep.shape[0] // len(dtypes), keep.shape[1]
-    recvs = [r for pieces in arrived for r in pieces]
+def combine_call(place, parts, dtypes):
+    ins = [piece for part in parts for piece in part]
+    rows, cols = ins[0].shape[0] // len(dtypes), sum(piece.shape[1] for piece in parts[0])
     whole = lambda a: pl.BlockSpec(a.shape, lambda: (0, 0))
     return pl.pallas_call(
-        functools.partial(combine_kernel, [len(pieces) for pieces in arrived]),
-        in_specs=[SCALARS, whole(keep)] + [whole(r) for r in recvs],
+        functools.partial(combine_kernel, [len(part) for part in parts]),
+        in_specs=[SCALARS] + [whole(a) for a in ins],
         out_specs=[pl.BlockSpec((rows, cols), lambda: (0, 0))] * len(dtypes),
         out_shape=[jax.ShapeDtypeStruct((rows, cols), d) for d in dtypes],
         compiler_params=params(),
         cost_estimate=cost(1e6, 5e6),
         name="combine",
-    )(place, keep, *recvs)
+    )(place, *ins)
 
 
 def add_kernel(*refs):
@@ -481,11 +486,11 @@
     def steps(self):
         return len(self.ahead) - 1
 
-    def owners(self):
+    def owners(self, ahead, behind):
         size = self.size
         me = lax.axis_index(self.axis)
         here = jnp.where(me % 2 == 0, me // 2, size - 1 - me // 2)
-        distances = [-s for s in range(len(self.ahead))] + list(range(1, len(self.behind)))
+        distances = [-s for s in range(ahead)] + list(range(1, behind))
         at = (here + size + jnp.array(distances, jnp.int32)) % size
         return jnp.where(at < size // 2, 2 * at, 2 * (size - 1 - at) + 1)
 
@@ -499,10 +504,10 @@
 
 def halve_stem(recv, keep, group):
     mine = lax.axis_index("group") // 2 * 2 + lax.axis_index("dp") % 2
-    return combine_call(mine.reshape(1), keep, [recv], [F32] * (group // 2 * 2))
-
-
-def sum_stem(parts, beside, after, dp, group):
+    return combine_call(mine.reshape(1), [[keep], recv], [F32] * (group // 2 * 2))
+
+
+def sum_stem(parts, beside, after, last, dp, group):
     core = lax.axis_index("group") % 2
     far = lax.axis_index("group") // 2
     low = lax.axis_index("dp") % 2
@@ -542,9 +547,10 @@
         line = lax.dynamic_update_slice_in_dim(line, block, (high ^ (j + 1)) * cols, 1)
     block = jnp.zeros((rows, width), BF16)
     block = lax.dynamic_update_slice_in_dim(block, line, mine * small, 0)
-    for f, b in hops:
+    arrived, beside = together([hop(line, f, b) for f, b in hops], last(*beside))
+    for (f, b), piece in zip(hops, arrived):
         target = (far ^ f) * 2 + (low ^ b)
-        block = lax.dynamic_update_slice_in_dim(block, hop(line, f, b), target * small, 0)
+        block = lax.dynamic_update_slice_in_dim(block, piece, target * small, 0)
     partner = swap(block, "group", group, 1)
     first = jnp.where(core == 0, block, partner)
     second = jnp.where(core == 0, partner, block)
@@ -584,6 +590,8 @@
     counts_far = swap(counts, "group", group, 1)
     table, genc = encoding_tables(patches.shape[1])
     gain = ln_gain.reshape(1, D)
+    counts_far, far_shards = together(counts_far, far_shards)
+    far_shards, gain = together(far_shards, gain)
     stem = stem_call(
         counts,
         vis_index,
@@ -594,27 +602,22 @@
         jnp.asarray(genc),
         out_grad.reshape(scenes, TOK, D),
     )
-    stem, counts_far, far_shards = together(stem, counts_far, far_shards)
+    rings = [Ring(x, "dp", dp) for x in far_shards]
+    ring = rings[0]
+    stem, both_counts, owners = step_all(rings, stem, jnp.stack([counts, counts_far]), ring.owners(dp // 2 + 1, dp // 2))
     emb = stem[0].reshape(tokens, D)
     both = [stem[1].reshape(2, tokens, D)]
     cols = stem[2].reshape(tokens, stem[2].shape[2])
-    both_counts = jnp.stack([counts, counts_far])
     both.append(swap(both[0], "group", group, 1))
-    rings = [Ring(x, "dp", dp) for x in far_shards]
-    passed = []
+    passed = [cross(ring.ahead[-1], 1)]
     (both,) = step_all(rings, both)
-    while rings[0].steps < dp // 2:
-        passed.append(cross(rings[0].ahead[-1], 1))
-        if len(passed) > 1:
-            (passed[-2],) = step_all(rings, passed[-2])
-        else:
-            step_all(rings)
-    ring = rings[0]
+    while ring.steps < dp // 2:
+        passed.append(cross(ring.ahead[-1], 1))
+        (passed[-2],) = step_all(rings, passed[-2])
     ring.ahead, ring.behind = together(ring.ahead, ring.behind)
     passed.append(cross(ring.ahead[-1], 1))
     behind = ring.behind[1:]
     passed.append(cross(jnp.concatenate(behind, axis=0), 1))
-    owners = ring.owners()
 
     packs, weights, crossing = [], [], []
     for f in list(fars) + [0]:
@@ -629,38 +632,40 @@
         elif f:
             made = together(*made)
         else:
-            made, others = together(made, [c[1] for c in crossing])
-        pack, weight, keep, other, *back = made
+            made, arrived = together(made, [x[:2] for x in crossing])
+        pack, weight, keep, other, back = made[0], made[1], made[2:4], made[4], made[5:]
         packs.append(pack)
         weights.append(weight)
         if f:
-            crossing.append([cross(keep, f), cross(other, f)])
+            crossing.append([cross(x, f) for x in (other, *keep)])
     back_far = swap(back[1], "group", group, 1)
-    for x in others:
-        other = other + x.astype(F32)
+    for x in arrived:
+        other = other + x[0].astype(F32)
     coming = swap(other.astype(BF16), "dp", dp, 1)
-    stem_made, keeps = together(
-        tail_call(core, back[0], back_far, emb, both[0], cols, gain), [c[0] for c in crossing]
+    stem_made, last_keeps = together(
+        tail_call(core, back[0], back_far, emb, both[0], cols, gain), [x[2] for x in crossing]
     )
+    keeps = [list(keep)] + [[x[1], y] for x, y in zip(arrived, last_keeps)]
     stem_keep, *stem_recv = stem_made
     stem_recv = [swap(x, "group", group, 1) for x in stem_recv]
-    stem_recv, coming = together(stem_recv, coming)
     stem_parts = halve_stem(stem_recv, stem_keep, group)
+    _, coming, keeps = together(stem_parts, coming, keeps)
     kinds = [F32 if j < 2 else BF16 for j in range(dp // 2)]
-    blocks = combine_call(high, keep, [[k] for k in keeps] + [[coming]], kinds)
+    blocks = combine_call(high, keeps + [[coming]], kinds)
     landing = [blocks[0]] + [swap(blocks[j], "dp", dp, 2 * j) for j in rests]
     near = dp // 2 * 3 // 4
 
-    def after(mixed, *arrived):
+    def after(mixed, share):
         mixed = swap(mixed, "group", group, 1)
-        return [output_call(counts, mixed, emb, packs, weights)] + list(arrived) + landing[near:]
-
-    grad_w_stem, (output, *landing) = sum_stem(
-        stem_parts, [mixed_call(packs, weights)] + landing[:near], after, dp, group
+        return [output_call(counts, mixed, emb, packs, weights), share] + landing[1:near]
+
+    def last(output, *arrived):
+        total = add_call(list(arrived) + landing[near:])
+        return output, total[:, : 3 * width].reshape(total.shape[0], 3, width), total[:, 3 * width :].T
+
+    grad_w_stem, (output, grad_w_qkv, grad_w_out) = sum_stem(
+        stem_parts, [mixed_call(packs, weights), landing[0]], after, last, dp, group
     )
-    total = add_call(landing)
-    grad_w_qkv = total[:, : 3 * width].reshape(total.shape[0], 3, width)
-    grad_w_out = total[:, 3 * width :].T
     return (output.reshape(scenes, GROUPS, CAP, D), grad_w_stem, grad_w_qkv, grad_w_out)
 
 

time: 217 us -> 220 us (1.014)
  waiting for transfers between devices: 63.7 us -> 56.6 us
  starting transfers between devices: 38.1 us -> 44.2 us
    ppermute x27 -> x28, starting transfers between devices: 24.2 us -> 30.8 us  [swap(): return lax.ppermute(x, axis, [(i, i ^ bit) for i in range(size)])]
    ppermute x4, waiting for transfers between devices: 19.6 us -> 14.4 us  [send(): moved = [lax.ppermute(self.ahead[-1], self.axis, self.forward)]]
    ppermute x27 -> x28, waiting for transfers between devices: 37.2 us -> 35.1 us  [swap(): return lax.ppermute(x, axis, [(i, i ^ bit) for i in range(size)])]
    unnamed x51 -> x47, local copies, waits for them, and re-layouts: 9.92 us -> 11.2 us
  transfers between devices with their start and end apart: 38 -> 39, of which waited for: 18 -> 20; matrix products, arithmetic and copies ran while one was open for 6% -> 7% of each run, Pallas kernels for 40% -> 41%
where the time goes in v9:
time: 220 us; the launch traced here: 219 us
  Pallas kernels  89.8 us (41%)
  waiting for transfers between devices  56.6 us (26%)
  starting transfers between devices  44.2 us (20%)
  local copies, waits for them, and re-layouts  17.8 us (8%)
  other arithmetic  9.66 us (4%)
    pallas_call x2, Pallas kernels, attention_call(): pl.pallas_call(functools.partial(attention_kernel, packs, len(blocks), dp...  54.7 us
    ppermute x28, waiting for transfers between devices, swap(): return lax.ppermute(x, axis, [(i, i ^ bit) for i in range(size)])  35.1 us
    ppermute x28, starting transfers between devices, swap(): return lax.ppermute(x, axis, [(i, i ^ bit) for i in range(size)])  30.8 us
    ppermute x4, waiting for transfers between devices, send(): moved = [lax.ppermute(self.ahead[-1], self.axis, self.forward)]  14.4 us
    unnamed x47, local copies, waits for them, and re-layouts  11.2 us
    pallas_call x1, Pallas kernels, tail_call(): pl.pallas_call(tail_kernel, grid=(tokens // rows,), in_specs=[SCALARS, pe...  8.97 us
    pallas_call x1, Pallas kernels, stem_call(): pl.pallas_call(stem_kernel, grid=(scenes // block,), in_specs=[whole(coun...  8.25 us
    ppermute x4, starting transfers between devices, send(): moved = [lax.ppermute(self.ahead[-1], self.axis, self.forward)]  6.91 us
  transfers between devices with their start and end apart: 39, of which 20 were waited for; matrix products, arithmetic and copies ran while one was open for 7% of the time, Pallas kernels for 41%

profile of v9, /device:TPU:0, one launch (start us, length us, event | category | flops | bytes accessed | tf_op | source)
XLA Modules:
  0.0 219.0 jit_solution(9310288826429359112)
XLA Ops:
  2.9 3.0 %collective-permute-start.1 = (bf16[128,1024]{1,0:T(8,128)(2,1)S(1)}, bf16[128,1024]{1,0:T(8,128)(2,1)S(1)}, u32[]{:S(2)}, u32[]{:S(2)}) collective-permute-start(bf16[128,1024]{1,0:T(8,128)(2,1)S(1)} %pad_maximum_fusion.1.refs_2_), channel_id=1, source_target_pairs={{0,2},{1,3},{2,0},{3,1},{4,6},{5,7},{6,4},{7,5},{8,10},{9,11},{10,... | collective-permute-start | bytes 786440 | tf_op jit(solution)/shard_map/ppermute | solution.py:460
  7.9 4.3 %collective-permute-done.1.refs_0_ = bf16[128,1024]{1,0:T(8,128)(2,1)S(1)} collective-permute-done((bf16[128,1024]{1,0:T(8,128)(2,1)S(1)}, bf16[128,1024]{1,0:T(8,128)(2,1)S(1)}, u32[]{:S(2)}, u32[]{:S(2)}) %collective-permute-start.1) | collective-permute-done | bytes 262176 | tf_op jit(solution)/shard_map/ppermute | solution.py:460
  12.2 1.8 collective-permute-start.2
  15.4 8.2 %stem_norm.1 = (bf16[6,144,1024]{2,1,0:T(8,128)(2,1)}, bf16[2,6,144,1024]{3,2,1,0:T(8,128)(2,1)}, bf16[6,144,256]{2,1,0:T(8,128)(2,1)}) custom-call(s32[6,3]{1,0:T(8,128)} %copy.36.cnt_ref, s32[6,3,48]{2,1,0:T(4,128)} %idx_ref.1, bf16[6,144,640]{2,1,0:T(8,128)(2,1)} %patch_ref.1, bf16[640,1024]{1,0:T(8,128)(2,1)} %w_ref.1, f32[1,1024]{1,0:T(1,128)} %bitcast.31, ...), custom_call_target="tpu_custom_call" | custom-call | flops 8000000 | bytes 12000 | tf_op jit(solution)/shard_map/stem_norm/pallas_call | solution.py:98
  23.8 1.9 collective-permute-start.4
  27.6 5.1 %collective-permute-done.4.refs_2_ = bf16[128,1024]{1,0:T(8,128)(2,1)S(1)} collective-permute-done((bf16[128,1024]{1,0:T(8,128)(2,1)}, bf16[128,1024]{1,0:T(8,128)(2,1)S(1)}, u32[]{:S(2)}, u32[]{:S(2)}) %collective-permute-start.4) | collective-permute-done | bytes 262176 | tf_op jit(solution)/shard_map/ppermute | solution.py:476
  37.7 4.1 %collective-permute-done.7.refs_3_ = bf16[128,1024]{1,0:T(8,128)(2,1)} collective-permute-done((bf16[128,1024]{1,0:T(8,128)(2,1)S(1)}, bf16[128,1024]{1,0:T(8,128)(2,1)}, u32[]{:S(2)}, u32[]{:S(2)}) %collective-permute-start.7) | collective-permute-done | bytes 262176 | tf_op jit(solution)/shard_map/ppermute | solution.py:476
  44.6 5.2 %collective-permute-done.10.refs_4_ = bf16[128,1024]{1,0:T(8,128)(2,1)} collective-permute-done((bf16[128,1024]{1,0:T(8,128)(2,1)}, bf16[128,1024]{1,0:T(8,128)(2,1)}, u32[]{:S(2)}, u32[]{:S(2)}) %collective-permute-start.10) | collective-permute-done | bytes 262176 | tf_op jit(solution)/shard_map/ppermute | solution.py:476
  55.0 22.7 %attention.2 = (bf16[1728,1024]{1,0:T(8,128)(2,1)}, bf16[1024,1024]{1,0:T(8,128)(2,1)}, bf16[512,512]{1,0:T(8,128)(2,1)}, bf16[512,512]{1,0:T(8,128)(2,1)}, bf16[512,1024]{1,0:T(8,128)(2,1)}) custom-call(s32[2,6,3]{2,1,0:T(8,128)} %copy.40.cnt_ref, s32[8]{0:T(128)} %compare_select_fusion.2.owner_ref, s32[1]{0:T(128)} %bitcast.8.low_ref, ...), custom_call_target="tpu_custom_call" | custom-call | flops 20000000 | bytes 14000 | tf_op jit(solution)/shard_map/attention/pallas_call | solution.py:260
  77.7 2.0 collective-permute-done.13.refs_6_
  81.7 2.0 fusion.1
  83.7 32.1 %attention.3 = (bf16[1728,1024]{1,0:T(8,128)(2,1)}, bf16[1024,1024]{1,0:T(8,128)(2,1)}, f32[512,512]{1,0:T(8,128)}, f32[512,512]{1,0:T(8,128)}, f32[512,1024]{1,...) custom-call(s32[2,6,3]{2,1,0:T(8,128)} %copy.40.cnt_ref, s32[8]{0:T(128)} %compare_select_fusion.2.owner_ref, ...), custom_call_target="tpu_custom_call" | custom-call | flops 20000000 | bytes 14000 | tf_op jit(solution)/shard_map/attention/pallas_call | solution.py:260
  118.4 3.2 %add_convert_fusion = bf16[512,1024]{1,0:T(8,128)(2,1)} fusion(f32[512,1024]{1,0:T(8,128)} %get-tuple-element.167, bf16[512,1024]{1,0:T(8,128)(2,1)} %copy-done.6), kind=kLoop, calls=%fused_computation | loop fusion | flops 1572864 | bytes 4194304 | tf_op jit(solution)/shard_map/convert_element_type | solution.py:644
  123.4 1.8 copy-done.1
  125.2 9.0 %tail.1 = (f32[320,1024]{1,0:T(8,128)}, f32[320,512]{1,0:T(8,128)}, f32[320,512]{1,0:T(8,128)}) custom-call(s32[1]{0:T(128)} %bitcast.1.core_ref, f32[864,1024]{1,0:T(8,128)} %get-tuple-element.150.own_ref, f32[864,1024]{1,0:T(8,128)} %copy-done.1, bf16[864,1024]{1,0:T(8,128)(2,1)} %bitcast.23, bf16[2,864,1024]{2,1,0:T(8,128)(2,1)} %bitcast.22, ...), custom_call_target="tpu_custom_call" | custom-call | flops 10000000 | bytes 12000 | tf_op jit(solution)/shard_map/tail/pallas_call | solution.py:415
  138.3 2.9 %combine.2 = (f32[80,1024]{1,0:T(8,128)}, f32[80,1024]{1,0:T(8,128)}, f32[80,1024]{1,0:T(8,128)}, f32[80,1024]{1,0:T(8,128)}) custom-call(s32[1]{0:T(128)} %bitcast.place_ref, f32[320,1024]{1,0:T(8,128)} %get-tuple-element.158.refs_0_, f32[320,512]{1,0:T(8,128)} %copy-done.10, f32[320,512]{1,0:T(8,128)} %copy-done.11), custom_call_target="tpu_custom_call" | custom-call | flops 1000 | bytes 5000 | tf_op jit(solution)/shard_map/combine/pallas_call | solution.py:308
  144.7 3.7 %mixed.1 = bf16[864,1024]{1,0:T(8,128)(2,1)} custom-call(bf16[1728,1024]{1,0:T(8,128)(2,1)} %get-tuple-element.134.refs_0_, bf16[1728,1024]{1,0:T(8,128)(2,1)} %get-tuple-element.165.refs_1_, bf16[1024,1024]{1,0:T(8,128)(2,1)} %get-tuple-element.135.refs_1_.refs_2_, bf16[1024,1024]{1,0:T(8,128)(2,1)} %get-tuple-element.166.refs_3_), custom_call_target="tpu_custom_call" | custom-call | flops 2000000 | bytes 5000 | tf_op jit(solution)/shard_map/mixed/pallas_call | solution.py:361
  148.4 3.6 %combine.3 = (f32[128,1024]{1,0:T(8,128)}, f32[128,1024]{1,0:T(8,128)}, bf16[128,1024]{1,0:T(8,128)(2,1)}, bf16[128,1024]{1,0:T(8,128)(2,1)}) custom-call(s32[1]{0:T(128)} %bitcast.12.place_ref, f32[512,512]{1,0:T(8,128)} %get-tuple-element.173.refs_0_, f32[512,512]{1,0:T(8,128)} %get-tuple-element.174.refs_1_, bf16[512,512]{1,0:T(8,128)(2,1)} %copy-done.12, ...), custom_call_target="tpu_custom_call" | custom-call | flops 1000 | bytes 5000 | tf_op jit(solution)/shard_map/combine/pallas_call | solution.py:308
  152.0 9.1 %collective-permute-done.21 = f32[80,1024]{1,0:T(8,128)S(1)} collective-permute-done((f32[80,1024]{1,0:T(8,128)}, f32[80,1024]{1,0:T(8,128)S(1)}, u32[]{:S(2)}, u32[]{:S(2)}) %collective-permute-start.21) | collective-permute-done | bytes 327712 | tf_op jit(solution)/shard_map/ppermute | solution.py:460
  164.3 2.1 collective-permute-start.30
  169.8 3.2 %collective-permute-start.27 = (f32[80,256]{1,0:T(8,128)}, f32[80,256]{1,0:T(8,128)S(1)}, u32[]{:S(2)}, u32[]{:S(2)}) collective-permute-start(f32[80,256]{1,0:T(8,128)} %get-tuple-element.219), channel_id=1, source_target_pairs={{0,24},{4,28},{8,16},{12,20},{16,8},{20,12},{24,0},{28,4},{1,25},{... | collective-permute-start | bytes 245768 | tf_op jit(solution)/shard_map/ppermute | solution.py:460
  173.0 5.5 %layer_output.1 = bf16[864,1024]{1,0:T(8,128)(2,1)} custom-call(s32[6,3]{1,0:T(8,128)} %copy.36.cnt_ref, bf16[864,1024]{1,0:T(8,128)(2,1)} %copy-done.2, bf16[864,1024]{1,0:T(8,128)(2,1)} %bitcast.24, bf16[1728,1024]{1,0:T(8,128)(2,1)} %get-tuple-element.134.refs_0_, bf16[1728,1024]{1,0:T(8,128)(2,1)} %get-tuple-element.165.refs_1_, ...), custom_call_target="tpu_custom_call" | custom-call | flops 5000000 | bytes 10000 | tf_op jit(solution)/shard_map/layer_output/pallas_call | solution.py:446
  178.5 4.0 %collective-permute-done.30.refs_2_ = bf16[128,1024]{1,0:T(8,128)(2,1)} collective-permute-done((bf16[128,1024]{1,0:T(8,128)(2,1)}, bf16[128,1024]{1,0:T(8,128)(2,1)}, u32[]{:S(2)}, u32[]{:S(2)}) %collective-permute-start.30) | collective-permute-done | bytes 262176 | tf_op jit(solution)/shard_map/ppermute | solution.py:460
  182.5 2.4 %collective-permute-start.37 = (bf16[128,1024]{1,0:T(8,128)(2,1)S(1)}, bf16[128,1024]{1,0:T(8,128)(2,1)S(1)}, u32[]{:S(2)}, u32[]{:S(2)}) collective-permute-start(bf16[128,1024]{1,0:T(8,128)(2,1)S(1)} %copy-done.20), channel_id=1, source_target_pairs={{0,24},{4,28},{8,16},{12,20},{16,8},{20,12},{24,0},{28,4},{1,25},{... | collective-permute-start | bytes 786440 | tf_op jit(solution)/shard_map/ppermute | solution.py:460
  186.5 4.2 %collective-permute-done.27 = f32[80,256]{1,0:T(8,128)S(1)} collective-permute-done((f32[80,256]{1,0:T(8,128)}, f32[80,256]{1,0:T(8,128)S(1)}, u32[]{:S(2)}, u32[]{:S(2)}) %collective-permute-start.27) | collective-permute-done | bytes 81952 | tf_op jit(solution)/shard_map/ppermute | solution.py:460
  191.8 1.9 collective-permute-start.32
  193.7 2.4 %collective-permute-start.33 = (bf16[80,256]{1,0:T(8,128)(2,1)S(1)}, bf16[80,256]{1,0:T(8,128)(2,1)S(1)}, u32[]{:S(2)}, u32[]{:S(2)}) collective-permute-start(bf16[80,256]{1,0:T(8,128)(2,1)S(1)} %get-tuple-element.213), channel_id=1, source_target_pairs={{0,24},{4,28},{8,16},{12,20},{16,8},{20,12},{24,0},{28,4},{1,25},{... | collective-permute-start | bytes 122888 | tf_op jit(solution)/shard_map/ppermute | solution.py:460
  196.9 2.2 %add_parts.1 = f32[128,1024]{1,0:T(8,128)} custom-call(f32[128,1024]{1,0:T(8,128)} %get-tuple-element.190.refs_0_, f32[128,1024]{1,0:T(8,128)} %collective-permute-done.29.refs_1_, bf16[128,1024]{1,0:T(8,128)(2,1)} %collective-permute-done.30.refs_2_, bf16[128,1024]{1,0:T(8,128)(2,1)} %copy-done.17), custom_call_target="tpu_custom_call" | custom-call | flops 1000 | bytes 2000 | tf_op jit(solution)/shard_map/add_parts/pallas_call | solution.py:328
  199.1 4.9 %collective-permute-done.32 = bf16[80,256]{1,0:T(8,128)(2,1)S(1)} collective-permute-done((bf16[80,256]{1,0:T(8,128)(2,1)S(1)}, bf16[80,256]{1,0:T(8,128)(2,1)S(1)}, u32[]{:S(2)}, u32[]{:S(2)}) %collective-permute-start.32) | collective-permute-done | bytes 40992 | tf_op jit(solution)/shard_map/ppermute | solution.py:460
  205.6 2.1 collective-permute-start.36
  212.0 2.9 %collective-permute-done.36 = bf16[80,1024]{1,0:T(8,128)(2,1)S(1)} collective-permute-done((bf16[80,1024]{1,0:T(8,128)(2,1)S(1)}, bf16[80,1024]{1,0:T(8,128)(2,1)S(1)}, u32[]{:S(2)}, u32[]{:S(2)}) %collective-permute-start.36) | collective-permute-done | bytes 163872 | tf_op jit(solution)/shard_map/ppermute | solution.py:525
  217.2 1.8 maximum_convert_fusion
  (129 shorter events, 52.8 us)
Async XLA Ops:
  2.9 9.3 %collective-permute-start.1 = (bf16[128,1024]{1,0:T(8,128)(2,1)S(1)}, bf16[128,1024]{1,0:T(8,128)(2,1)S(1)}, u32[]{:S(2)}, u32[]{:S(2)}) collective-permute-start(bf16[128,1024]{1,0:T(8,128)(2,1)S(1)} %pad_maximum_fusion.1.refs_2_), channel_id=1, source_target_pairs={{0,2},{1,3},{2,0},{3,1},{4,6},{5,7},{6,4},{7,5},{8,10},{9,11},{10,... | collective-permute-start | bytes 786440 | tf_op jit(solution)/shard_map/ppermute | solution.py:460
  12.2 11.5 %collective-permute-start.2 = (bf16[128,1024]{1,0:T(8,128)(2,1)S(1)}, bf16[128,1024]{1,0:T(8,128)(2,1)}, u32[]{:S(2)}, u32[]{:S(2)}) collective-permute-start(bf16[128,1024]{1,0:T(8,128)(2,1)S(1)} %collective-permute-done.1.refs_0_), channel_id=1, source_target_pairs={{0,8},{8,16},{16,24},{24,28},{28,20},{20,12},{12,4},{4,0},{1,9},{9... | collective-permute-start | bytes 786440 | tf_op jit(solution)/shard_map/ppermute | solution.py:476
  14.0 9.7 %collective-permute-start.3 = (bf16[128,1024]{1,0:T(8,128)(2,1)S(1)}, bf16[128,1024]{1,0:T(8,128)(2,1)S(1)}, u32[]{:S(2)}, u32[]{:S(2)}) collective-permute-start(bf16[128,1024]{1,0:T(8,128)(2,1)S(1)} %collective-permute-done.1.refs_0_), channel_id=1, source_target_pairs={{8,0},{16,8},{24,16},{28,24},{20,28},{12,20},{4,12},{0,4},{9,1},{1... | collective-permute-start | bytes 786440 | tf_op jit(solution)/shard_map/ppermute | solution.py:478
  23.7 10.3 %collective-permute-start.6 = (bf16[2,864,1024]{2,1,0:T(8,128)(2,1)}, bf16[2,864,1024]{2,1,0:T(8,128)(2,1)S(1)}, u32[]{:S(2)}, u32[]{:S(2)}) collective-permute-start(bf16[2,864,1024]{2,1,0:T(8,128)(2,1)} %bitcast.17), channel_id=1, source_target_pairs={{0,1},{1,0},{2,3},{3,2},{4,5},{5,4},{6,7},{7,6},{8,9},{9,8},{10,11... | collective-permute-start | bytes 10616840 | tf_op jit(solution)/shard_map/ppermute | solution.py:460
  23.8 8.9 %collective-permute-start.4 = (bf16[128,1024]{1,0:T(8,128)(2,1)}, bf16[128,1024]{1,0:T(8,128)(2,1)S(1)}, u32[]{:S(2)}, u32[]{:S(2)}) collective-permute-start(bf16[128,1024]{1,0:T(8,128)(2,1)} %collective-permute-done.2.refs_1_), channel_id=1, source_target_pairs={{0,8},{8,16},{16,24},{24,28},{28,20},{20,12},{12,4},{4,0},{1,9},{9... | collective-permute-start | bytes 786440 | tf_op jit(solution)/shard_map/ppermute | solution.py:476
  25.7 8.4 %collective-permute-start.5 = (bf16[128,1024]{1,0:T(8,128)(2,1)S(1)}, bf16[128,1024]{1,0:T(8,128)(2,1)S(1)}, u32[]{:S(2)}, u32[]{:S(2)}) collective-permute-start(bf16[128,1024]{1,0:T(8,128)(2,1)S(1)} %collective-permute-done.3.refs_5_), channel_id=1, source_target_pairs={{8,0},{16,8},{24,16},{28,24},{20,28},{12,20},{4,12},{0,4},{9,1},{1... | collective-permute-start | bytes 786440 | tf_op jit(solution)/shard_map/ppermute | solution.py:478
  25.9 11.8 %collective-permute-start.9 = (bf16[128,1024]{1,0:T(8,128)(2,1)}, bf16[128,1024]{1,0:T(8,128)(2,1)S(1)}, u32[]{:S(2)}, u32[]{:S(2)}) collective-permute-start(bf16[128,1024]{1,0:T(8,128)(2,1)} %collective-permute-done.2.refs_1_), channel_id=1, source_target_pairs={{0,2},{1,3},{2,0},{3,1},{4,6},{5,7},{6,4},{7,5},{8,10},{9,11},{10,... | collective-permute-start | bytes 786440 | tf_op jit(solution)/shard_map/ppermute | solution.py:460
  34.1 7.7 %collective-permute-start.7 = (bf16[128,1024]{1,0:T(8,128)(2,1)S(1)}, bf16[128,1024]{1,0:T(8,128)(2,1)}, u32[]{:S(2)}, u32[]{:S(2)}) collective-permute-start(bf16[128,1024]{1,0:T(8,128)(2,1)S(1)} %collective-permute-done.4.refs_2_), channel_id=1, source_target_pairs={{0,8},{8,16},{16,24},{24,28},{28,20},{20,12},{12,4},{4,0},{1,9},{9... | collective-permute-start | bytes 786440 | tf_op jit(solution)/shard_map/ppermute | solution.py:476
  35.7 7.3 %collective-permute-start.8 = (bf16[128,1024]{1,0:T(8,128)(2,1)S(1)}, bf16[128,1024]{1,0:T(8,128)(2,1)S(1)}, u32[]{:S(2)}, u32[]{:S(2)}) collective-permute-start(bf16[128,1024]{1,0:T(8,128)(2,1)S(1)} %collective-permute-done.5.refs_6_), channel_id=1, source_target_pairs={{8,0},{16,8},{24,16},{28,24},{20,28},{12,20},{4,12},{0,4},{9,1},{1... | collective-permute-start | bytes 786440 | tf_op jit(solution)/shard_map/ppermute | solution.py:478
  36.2 8.4 %collective-permute-start.11 = (bf16[128,1024]{1,0:T(8,128)(2,1)S(1)}, bf16[128,1024]{1,0:T(8,128)(2,1)}, u32[]{:S(2)}, u32[]{:S(2)}) collective-permute-start(bf16[128,1024]{1,0:T(8,128)(2,1)S(1)} %collective-permute-done.4.refs_2_), channel_id=1, source_target_pairs={{0,2},{1,3},{2,0},{3,1},{4,6},{5,7},{6,4},{7,5},{8,10},{9,11},{10,... | collective-permute-start | bytes 786440 | tf_op jit(solution)/shard_map/ppermute | solution.py:460
  50.7 28.9 %collective-permute-start.14 = (bf16[384,1024]{1,0:T(8,128)(2,1)}, bf16[384,1024]{1,0:T(8,128)(2,1)}, u32[]{:S(2)}, u32[]{:S(2)}) collective-permute-start(bf16[384,1024]{1,0:T(8,128)(2,1)} %pad_maximum_fusion), channel_id=1, source_target_pairs={{0,2},{1,3},{2,0},{3,1},{4,6},{5,7},{6,4},{7,5},{8,10},{9,11},{10,... | collective-permute-start | bytes 2359304 | tf_op jit(solution)/shard_map/ppermute | solution.py:460
  52.2 25.4 %collective-permute-start.12 = (bf16[128,1024]{1,0:T(8,128)(2,1)}, bf16[128,1024]{1,0:T(8,128)(2,1)}, u32[]{:S(2)}, u32[]{:S(2)}) collective-permute-start(bf16[128,1024]{1,0:T(8,128)(2,1)} %collective-permute-done.7.refs_3_), channel_id=1, source_target_pairs={{0,2},{1,3},{2,0},{3,1},{4,6},{5,7},{6,4},{7,5},{8,10},{9,11},{10,... | collective-permute-start | bytes 786440 | tf_op jit(solution)/shard_map/ppermute | solution.py:460
  52.8 26.9 %collective-permute-start.13 = (bf16[128,1024]{1,0:T(8,128)(2,1)}, bf16[128,1024]{1,0:T(8,128)(2,1)}, u32[]{:S(2)}, u32[]{:S(2)}) collective-permute-start(bf16[128,1024]{1,0:T(8,128)(2,1)} %collective-permute-done.10.refs_4_), channel_id=1, source_target_pairs={{0,2},{1,3},{2,0},{3,1},{4,6},{5,7},{6,4},{7,5},{8,10},{9,11},{10,... | collective-permute-start | bytes 786440 | tf_op jit(solution)/shard_map/ppermute | solution.py:460
  79.7 36.1 %collective-permute-start.15 = (bf16[512,1024]{1,0:T(8,128)(2,1)}, bf16[512,1024]{1,0:T(8,128)(2,1)S(1)}, u32[]{:S(2)}, u32[]{:S(2)}) collective-permute-start(bf16[512,1024]{1,0:T(8,128)(2,1)} %get-tuple-element.148), channel_id=1, source_target_pairs={{0,2},{1,3},{2,0},{3,1},{4,6},{5,7},{6,4},{7,5},{8,10},{9,11},{10,... | collective-permute-start | bytes 3145736 | tf_op jit(solution)/shard_map/ppermute | solution.py:460
  81.2 34.6 %collective-permute-start.16 = (bf16[512,512]{1,0:T(8,128)(2,1)}, bf16[512,512]{1,0:T(8,128)(2,1)S(1)}, u32[]{:S(2)}, u32[]{:S(2)}) collective-permute-start(bf16[512,512]{1,0:T(8,128)(2,1)} %get-tuple-element.149), channel_id=1, source_target_pairs={{0,2},{1,3},{2,0},{3,1},{4,6},{5,7},{6,4},{7,5},{8,10},{9,11},{10,... | collective-permute-start | bytes 1572872 | tf_op jit(solution)/shard_map/ppermute | solution.py:460
  116.9 17.3 %collective-permute-start.18 = (bf16[512,512]{1,0:T(8,128)(2,1)}, bf16[512,512]{1,0:T(8,128)(2,1)}, u32[]{:S(2)}, u32[]{:S(2)}) collective-permute-start(bf16[512,512]{1,0:T(8,128)(2,1)} %get-tuple-element.157), channel_id=1, source_target_pairs={{0,2},{1,3},{2,0},{3,1},{4,6},{5,7},{6,4},{7,5},{8,10},{9,11},{10,... | collective-permute-start | bytes 1572872 | tf_op jit(solution)/shard_map/ppermute | solution.py:460
  121.6 26.8 %collective-permute-start.24 = (bf16[512,1024]{1,0:T(8,128)(2,1)}, bf16[512,1024]{1,0:T(8,128)(2,1)}, u32[]{:S(2)}, u32[]{:S(2)}) collective-permute-start(bf16[512,1024]{1,0:T(8,128)(2,1)} %add_convert_fusion), channel_id=1, source_target_pairs={{0,4},{4,0},{8,12},{12,8},{16,20},{20,16},{24,28},{28,24},{1,5},{5... | collective-permute-start | bytes 3145736 | tf_op jit(solution)/shard_map/ppermute | solution.py:460
  141.2 19.9 %collective-permute-start.21 = (f32[80,1024]{1,0:T(8,128)}, f32[80,1024]{1,0:T(8,128)S(1)}, u32[]{:S(2)}, u32[]{:S(2)}) collective-permute-start(f32[80,1024]{1,0:T(8,128)} %get-tuple-element.162), channel_id=1, source_target_pairs={{0,4},{4,0},{8,12},{12,8},{16,20},{20,16},{24,28},{28,24},{1,5},{5... | collective-permute-start | bytes 983048 | tf_op jit(solution)/shard_map/ppermute | solution.py:460
  141.7 19.5 %collective-permute-start.22 = (f32[80,1024]{1,0:T(8,128)}, f32[80,1024]{1,0:T(8,128)S(1)}, u32[]{:S(2)}, u32[]{:S(2)}) collective-permute-start(f32[80,1024]{1,0:T(8,128)} %get-tuple-element.163), channel_id=1, source_target_pairs={{0,2},{1,3},{2,0},{3,1},{4,6},{5,7},{6,4},{7,5},{8,10},{9,11},{10,... | collective-permute-start | bytes 983048 | tf_op jit(solution)/shard_map/ppermute | solution.py:525
  143.2 18.0 %collective-permute-start.23 = (f32[80,1024]{1,0:T(8,128)}, f32[80,1024]{1,0:T(8,128)S(1)}, u32[]{:S(2)}, u32[]{:S(2)}) collective-permute-start(f32[80,1024]{1,0:T(8,128)} %get-tuple-element.164), channel_id=1, source_target_pairs={{0,6},{1,7},{2,4},{3,5},{4,2},{5,3},{6,0},{7,1},{8,14},{9,15},{10,... | collective-permute-start | bytes 983048 | tf_op jit(solution)/shard_map/ppermute | solution.py:525
  162.7 7.2 %collective-permute-start.28 = (bf16[864,1024]{1,0:T(8,128)(2,1)S(1)}, bf16[864,1024]{1,0:T(8,128)(2,1)S(1)}, u32[]{:S(2)}, u32[]{:S(2)}) collective-permute-start(bf16[864,1024]{1,0:T(8,128)(2,1)S(1)} %copy-done.3), channel_id=1, source_target_pairs={{0,1},{1,0},{2,3},{3,2},{4,5},{5,4},{6,7},{7,6},{8,9},{9,8},{10,11... | collective-permute-start | bytes 5308424 | tf_op jit(solution)/shard_map/ppermute | solution.py:460
  162.7 28.0 %collective-permute-start.29 = (f32[128,1024]{1,0:T(8,128)}, f32[128,1024]{1,0:T(8,128)}, u32[]{:S(2)}, u32[]{:S(2)}) collective-permute-start(f32[128,1024]{1,0:T(8,128)} %get-tuple-element.184), channel_id=1, source_target_pairs={{0,8},{4,12},{8,0},{12,4},{16,24},{20,28},{24,16},{28,20},{1,9},{5... | collective-permute-start | bytes 1572872 | tf_op jit(solution)/shard_map/ppermute | solution.py:460
  164.3 18.2 %collective-permute-start.30 = (bf16[128,1024]{1,0:T(8,128)(2,1)}, bf16[128,1024]{1,0:T(8,128)(2,1)}, u32[]{:S(2)}, u32[]{:S(2)}) collective-permute-start(bf16[128,1024]{1,0:T(8,128)(2,1)} %get-tuple-element.185), channel_id=1, source_target_pairs={{0,16},{4,20},{8,24},{12,28},{16,0},{20,4},{24,8},{28,12},{1,17},{... | collective-permute-start | bytes 786440 | tf_op jit(solution)/shard_map/ppermute | solution.py:460
  168.6 17.9 %collective-permute-start.25 = (f32[80,256]{1,0:T(8,128)}, f32[80,256]{1,0:T(8,128)}, u32[]{:S(2)}, u32[]{:S(2)}) collective-permute-start(f32[80,256]{1,0:T(8,128)} %get-tuple-element.221), channel_id=1, source_target_pairs={{0,8},{4,12},{8,0},{12,4},{16,24},{20,28},{24,16},{28,20},{1,9},{5... | collective-permute-start | bytes 245768 | tf_op jit(solution)/shard_map/ppermute | solution.py:460
  169.4 17.0 %collective-permute-start.26 = (f32[80,256]{1,0:T(8,128)}, f32[80,256]{1,0:T(8,128)}, u32[]{:S(2)}, u32[]{:S(2)}) collective-permute-start(f32[80,256]{1,0:T(8,128)} %get-tuple-element.220), channel_id=1, source_target_pairs={{0,16},{4,20},{8,24},{12,28},{16,0},{20,4},{24,8},{28,12},{1,17},{... | collective-permute-start | bytes 245768 | tf_op jit(solution)/shard_map/ppermute | solution.py:460
  169.8 20.8 %collective-permute-start.27 = (f32[80,256]{1,0:T(8,128)}, f32[80,256]{1,0:T(8,128)S(1)}, u32[]{:S(2)}, u32[]{:S(2)}) collective-permute-start(f32[80,256]{1,0:T(8,128)} %get-tuple-element.219), channel_id=1, source_target_pairs={{0,24},{4,28},{8,16},{12,20},{16,8},{20,12},{24,0},{28,4},{1,25},{... | collective-permute-start | bytes 245768 | tf_op jit(solution)/shard_map/ppermute | solution.py:460
  182.5 13.7 %collective-permute-start.37 = (bf16[128,1024]{1,0:T(8,128)(2,1)S(1)}, bf16[128,1024]{1,0:T(8,128)(2,1)S(1)}, u32[]{:S(2)}, u32[]{:S(2)}) collective-permute-start(bf16[128,1024]{1,0:T(8,128)(2,1)S(1)} %copy-done.20), channel_id=1, source_target_pairs={{0,24},{4,28},{8,16},{12,20},{16,8},{20,12},{24,0},{28,4},{1,25},{... | collective-permute-start | bytes 786440 | tf_op jit(solution)/shard_map/ppermute | solution.py:460
  191.6 7.5 %collective-permute-start.31 = (bf16[80,256]{1,0:T(8,128)(2,1)S(1)}, bf16[80,256]{1,0:T(8,128)(2,1)S(1)}, u32[]{:S(2)}, u32[]{:S(2)}) collective-permute-start(bf16[80,256]{1,0:T(8,128)(2,1)S(1)} %get-tuple-element.213), channel_id=1, source_target_pairs={{0,8},{4,12},{8,0},{12,4},{16,24},{20,28},{24,16},{28,20},{1,9},{5... | collective-permute-start | bytes 122888 | tf_op jit(solution)/shard_map/ppermute | solution.py:460
  191.8 12.3 %collective-permute-start.32 = (bf16[80,256]{1,0:T(8,128)(2,1)S(1)}, bf16[80,256]{1,0:T(8,128)(2,1)S(1)}, u32[]{:S(2)}, u32[]{:S(2)}) collective-permute-start(bf16[80,256]{1,0:T(8,128)(2,1)S(1)} %get-tuple-element.213), channel_id=1, source_target_pairs={{0,16},{4,20},{8,24},{12,28},{16,0},{20,4},{24,8},{28,12},{1,17},{... | collective-permute-start | bytes 122888 | tf_op jit(solution)/shard_map/ppermute | solution.py:460
  193.7 10.4 %collective-permute-start.33 = (bf16[80,256]{1,0:T(8,128)(2,1)S(1)}, bf16[80,256]{1,0:T(8,128)(2,1)S(1)}, u32[]{:S(2)}, u32[]{:S(2)}) collective-permute-start(bf16[80,256]{1,0:T(8,128)(2,1)S(1)} %get-tuple-element.213), channel_id=1, source_target_pairs={{0,24},{4,28},{8,16},{12,20},{16,8},{20,12},{24,0},{28,4},{1,25},{... | collective-permute-start | bytes 122888 | tf_op jit(solution)/shard_map/ppermute | solution.py:460
  205.0 7.0 %collective-permute-start.35 = (bf16[80,1024]{1,0:T(8,128)(2,1)S(1)}, bf16[80,1024]{1,0:T(8,128)(2,1)S(1)}, u32[]{:S(2)}, u32[]{:S(2)}) collective-permute-start(bf16[80,1024]{1,0:T(8,128)(2,1)S(1)} %constant_dynamic-update-slice_fusion.4), channel_id=1, source_target_pairs={{0,2},{1,3},{2,0},{3,1},{4,6},{5,7},{6,4},{7,5},{8,10},{9,11},{10,... | collective-permute-start | bytes 491528 | tf_op jit(solution)/shard_map/ppermute | solution.py:525
  205.6 9.3 %collective-permute-start.36 = (bf16[80,1024]{1,0:T(8,128)(2,1)S(1)}, bf16[80,1024]{1,0:T(8,128)(2,1)S(1)}, u32[]{:S(2)}, u32[]{:S(2)}) collective-permute-start(bf16[80,1024]{1,0:T(8,128)(2,1)S(1)} %constant_dynamic-update-slice_fusion.4), channel_id=1, source_target_pairs={{0,6},{1,7},{2,4},{3,5},{4,2},{5,3},{6,0},{7,1},{8,14},{9,15},{10,... | collective-permute-start | bytes 491528 | tf_op jit(solution)/shard_map/ppermute | solution.py:525
  (28 other events, 189.8 us)

commit v10 on v9

--- a/solution.py
+++ b/solution.py
@@ -228,7 +228,7 @@
 
         @pl.when(half != 0)
         def _():
-            refs[1][...] = back
+            refs[1][...] = back.astype(BF16)
 
 
 def block_rows(tokens):
@@ -256,7 +256,6 @@
     back = [] if earlier is None else two_halves(rows, steps, ())
     kind = BF16 if earlier is None else F32
     grads = [jax.ShapeDtypeStruct((D // 2, c), kind) for c in (cols // 2, cols // 2, cols)]
-    back_shape = jax.ShapeDtypeStruct((tokens, D), F32)
     return pl.pallas_call(
         functools.partial(attention_kernel, packs, len(blocks), dp),
         grid=(2, steps),
@@ -272,7 +271,7 @@
             jax.ShapeDtypeStruct((D, cols), BF16),
             *grads,
         ]
-        + [back_shape] * len(back),
+        + [jax.ShapeDtypeStruct((tokens, D), kind) for kind in (F32, BF16)[: len(back)]],
         scratch_shapes=[
             pltpu.VMEM((rows, D), BF16),
             pltpu.VMEM((rows, D), BF16),
@@ -379,7 +378,7 @@
     def _():
         acc[...] = jnp.zeros_like(acc)
 
-    grad_normed = own_ref[...] + recv_ref[...]
+    grad_normed = own_ref[...] + recv_ref[...].astype(F32)
     x = emb_ref[...].astype(F32)
     dev = x - jnp.mean(x, axis=-1, keepdims=True)
     inv_std = lax.rsqrt(jnp.mean(dev * dev, axis=-1, keepdims=True) + NORM_EPS)
@@ -471,6 +470,14 @@
         self.forward = [(order[i], order[(i + 1) % size]) for i in range(size)]
         self.backward = [(order[(i + 1) % size], order[i]) for i in range(size)]
         self.ahead, self.behind = [x], [x]
+
+    @classmethod
+    def across(cls, x, axis, size, other, other_size, bit):
+        ring = cls(swap(x, other, other_size, bit), axis, size)
+        for pairs, blocks in ((ring.forward, ring.ahead), (ring.backward, ring.behind)):
+            both = [(s * other_size + g, t * other_size + (g ^ bit)) for s, t in pairs for g in range(other_size)]
+            blocks.append(lax.ppermute(x, (axis, other), both))
+        return ring
 
     def send(self):
         moved = [lax.ppermute(self.ahead[-1], self.axis, self.forward)]
@@ -585,13 +592,12 @@
 
     shard = jnp.concatenate([w_qkv.reshape(w_qkv.shape[0], 3 * width), w_out.T], axis=1)
     cross = lambda x, f: swap(x, "group", group, 2 * f)
-    far_shards = [cross(shard, f) for f in fars]
+    rings = [Ring.across(shard, "dp", dp, "group", group, 2 * f) for f in fars]
+    ring = rings[0]
     counts = vis_count.astype(jnp.int32)
     counts_far = swap(counts, "group", group, 1)
     table, genc = encoding_tables(patches.shape[1])
     gain = ln_gain.reshape(1, D)
-    counts_far, far_shards = together(counts_far, far_shards)
-    far_shards, gain = together(far_shards, gain)
     stem = stem_call(
         counts,
         vis_index,
@@ -602,9 +608,11 @@
         jnp.asarray(genc),
         out_grad.reshape(scenes, TOK, D),
     )
-    rings = [Ring(x, "dp", dp) for x in far_shards]
-    ring = rings[0]
-    stem, both_counts, owners = step_all(rings, stem, jnp.stack([counts, counts_far]), ring.owners(dp // 2 + 1, dp // 2))
+    moved = [(r.ahead, r.behind) for r in rings]
+    owners = ring.owners(dp // 2 + 1, dp // 2)
+    stem, both_counts, owners, moved = together(stem, jnp.stack([counts, counts_far]), owners, moved)
+    for r, (ahead, behind) in zip(rings, moved):
+        r.ahead, r.behind = list(ahead), list(behind)
     emb = stem[0].reshape(tokens, D)
     both = [stem[1].reshape(2, tokens, D)]
     cols = stem[2].reshape(tokens, stem[2].shape[2])
@@ -613,11 +621,14 @@
     (both,) = step_all(rings, both)
     while ring.steps < dp // 2:
         passed.append(cross(ring.ahead[-1], 1))
-        (passed[-2],) = step_all(rings, passed[-2])
-    ring.ahead, ring.behind = together(ring.ahead, ring.behind)
+        if ring.steps == dp // 2 - 1:
+            behind = jnp.concatenate(ring.behind[1:], axis=0)
+            passed[-2], behind = step_all(rings, passed[-2], behind)
+        else:
+            (passed[-2],) = step_all(rings, passed[-2])
+    ring.ahead, behind = together(ring.ahead, behind)
     passed.append(cross(ring.ahead[-1], 1))
-    behind = ring.behind[1:]
-    passed.append(cross(jnp.concatenate(behind, axis=0), 1))
+    passed.append(cross(behind, 1))
 
     packs, weights, crossing = [], [], []
     for f in list(fars) + [0]:
@@ -625,7 +636,7 @@
             blocks = rings[f - 1].ahead + rings[f - 1].behind[1:]
         else:
             rows = shard.shape[0]
-            blocks = [shard] + passed[:-1] + [passed[-1][b * rows : (b + 1) * rows] for b in range(len(behind))]
+            blocks = [shard] + passed[:-1] + [passed[-1][b * rows : (b + 1) * rows] for b in range(dp // 2 - 1)]
         made = attention_call(both_counts, owners, low, *both, None if f else (packs, weights), blocks, dp)
         if f == 1:
             made, passed[-3:] = together(made, passed[-3:])
@@ -655,16 +666,16 @@
     landing = [blocks[0]] + [swap(blocks[j], "dp", dp, 2 * j) for j in rests]
     near = dp // 2 * 3 // 4
 
-    def after(mixed, share):
-        mixed = swap(mixed, "group", group, 1)
-        return [output_call(counts, mixed, emb, packs, weights), share] + landing[1:near]
-
-    def last(output, *arrived):
-        total = add_call(list(arrived) + landing[near:])
+    def after(mixed, *arrived):
+        return [mixed] + list(arrived) + [landing[1]] + landing[near:]
+
+    def last(mixed, *arrived):
+        output = output_call(counts, swap(mixed, "group", group, 1), emb, packs, weights)
+        total = add_call(list(arrived))
         return output, total[:, : 3 * width].reshape(total.shape[0], 3, width), total[:, 3 * width :].T
 
     grad_w_stem, (output, grad_w_qkv, grad_w_out) = sum_stem(
-        stem_parts, [mixed_call(packs, weights), landing[0]], after, last, dp, group
+        stem_parts, [mixed_call(packs, weights), landing[0]] + landing[2:near], after, last, dp, group
     )
     return (output.reshape(scenes, GROUPS, CAP, D), grad_w_stem, grad_w_qkv, grad_w_out)
 

time: 220 us -> 210 us (0.955)
  waiting for transfers between devices: 56.6 us -> 52.1 us
    ppermute x0 -> x2, waiting for transfers between devices: none -> 5.69 us  [across(): blocks.append(lax.ppermute(x, (axis, other), both))]
    ppermute x4, waiting for transfers between devices: 4.52 us -> 0.01 us  [hop(): return lax.ppermute(block, ('dp', 'group'), pairs)]
    ppermute x28, waiting for transfers between devices: 35.1 us -> 31.5 us  [swap(): return lax.ppermute(x, axis, [(i, i ^ bit) for i in range(size)])]
    ppermute x0 -> x2, starting transfers between devices: none -> 2.92 us  [across(): blocks.append(lax.ppermute(x, (axis, other), both))]
    ppermute x4 -> x3, starting transfers between devices: 6.91 us -> 4.34 us  [send(): moved = [lax.ppermute(self.ahead[-1], self.axis, self.forward)]]
    ppermute x4 -> x3, waiting for transfers between devices: 14.4 us -> 12.5 us  [send(): moved = [lax.ppermute(self.ahead[-1], self.axis, self.forward)]]
    unnamed x47 -> x51, local copies, waits for them, and re-layouts: 11.2 us -> 10.9 us
  transfers between devices with their start and end apart: 39 -> 39, of which waited for: 20 -> 17; matrix products, arithmetic and copies ran while one was open for 7% -> 7% of each run, Pallas kernels for 41% -> 42%
where the time goes in v10:
time: 210 us
  Pallas kernels  89.1 us (42%)
  waiting for transfers between devices  52.1 us (25%)
  starting transfers between devices  42.6 us (20%)
  local copies, waits for them, and re-layouts  16.9 us (8%)
  other arithmetic  8.04 us (4%)
    pallas_call x2, Pallas kernels, attention_call(): pl.pallas_call(functools.partial(attention_kernel, packs, len(blocks), dp...  54.4 us
    ppermute x28, waiting for transfers between devices, swap(): return lax.ppermute(x, axis, [(i, i ^ bit) for i in range(size)])  31.5 us
    ppermute x28, starting transfers between devices, swap(): return lax.ppermute(x, axis, [(i, i ^ bit) for i in range(size)])  29.2 us
    ppermute x3, waiting for transfers between devices, send(): moved = [lax.ppermute(self.ahead[-1], self.axis, self.forward)]  12.5 us
    unnamed x51, local copies, waits for them, and re-layouts  10.9 us
    pallas_call x1, Pallas kernels, tail_call(): pl.pallas_call(tail_kernel, grid=(tokens // rows,), in_specs=[SCALARS, pe...  8.77 us
    pallas_call x1, Pallas kernels, stem_call(): pl.pallas_call(stem_kernel, grid=(scenes // block,), in_specs=[whole(coun...  8.16 us
    pallas_call x2, Pallas kernels, combine_call(): pl.pallas_call(functools.partial(combine_kernel, [len(part) for part in p...  6.38 us
  transfers between devices with their start and end apart: 39, of which 17 were waited for; matrix products, arithmetic and copies ran while one was open for 7% of the time, Pallas kernels for 42%

profile of v10, /device:TPU:0, one launch (start us, length us, event | category | flops | bytes accessed | tf_op | source)
XLA Modules:
  0.0 209.8 jit_solution(14897379769280489163)
XLA Ops:
  2.9 3.0 %collective-permute-start.1 = (bf16[128,1024]{1,0:T(8,128)(2,1)S(1)}, bf16[128,1024]{1,0:T(8,128)(2,1)S(1)}, u32[]{:S(2)}, u32[]{:S(2)}) collective-permute-start(bf16[128,1024]{1,0:T(8,128)(2,1)S(1)} %pad_maximum_fusion.1.refs_2_), channel_id=1, source_target_pairs={{0,2},{1,3},{2,0},{3,1},{4,6},{5,7},{6,4},{7,5},{8,10},{9,11},{10,... | collective-permute-start | bytes 786440 | tf_op jit(solution)/shard_map/ppermute | solution.py:459
  5.9 1.5 collective-permute-start.2
  10.2 8.2 %stem_norm.1 = (bf16[6,144,1024]{2,1,0:T(8,128)(2,1)}, bf16[2,6,144,1024]{3,2,1,0:T(8,128)(2,1)}, bf16[6,144,256]{2,1,0:T(8,128)(2,1)}) custom-call(s32[6,3]{1,0:T(8,128)} %copy.33.cnt_ref, s32[6,3,48]{2,1,0:T(4,128)} %idx_ref.1, bf16[6,144,640]{2,1,0:T(8,128)(2,1)} %patch_ref.1, bf16[640,1024]{1,0:T(8,128)(2,1)} %w_ref.1, f32[1,1024]{1,0:T(1,128)} %bitcast.31, ...), custom_call_target="tpu_custom_call" | custom-call | flops 8000000 | bytes 12000 | tf_op jit(solution)/shard_map/stem_norm/pallas_call | solution.py:98
  18.9 5.7 %collective-permute-done.2.refs_1_ = bf16[128,1024]{1,0:T(8,128)(2,1)S(1)} collective-permute-done((bf16[128,1024]{1,0:T(8,128)(2,1)S(1)}, bf16[128,1024]{1,0:T(8,128)(2,1)S(1)}, u32[]{:S(2)}, u32[]{:S(2)}) %collective-permute-start.2) | collective-permute-done | bytes 262176 | tf_op jit(solution)/shard_map/ppermute | solution.py:479
  28.9 5.4 %collective-permute-done.4.refs_2_ = bf16[128,1024]{1,0:T(8,128)(2,1)S(1)} collective-permute-done((bf16[128,1024]{1,0:T(8,128)(2,1)}, bf16[128,1024]{1,0:T(8,128)(2,1)S(1)}, u32[]{:S(2)}, u32[]{:S(2)}) %collective-permute-start.4) | collective-permute-done | bytes 262176 | tf_op jit(solution)/shard_map/ppermute | solution.py:483
  34.8 2.2 %collective-permute-start.7 = (bf16[128,1024]{1,0:T(8,128)(2,1)S(1)}, bf16[128,1024]{1,0:T(8,128)(2,1)}, u32[]{:S(2)}, u32[]{:S(2)}) collective-permute-start(bf16[128,1024]{1,0:T(8,128)(2,1)S(1)} %collective-permute-done.4.refs_2_), channel_id=1, source_target_pairs={{0,8},{8,16},{16,24},{24,28},{28,20},{20,12},{12,4},{4,0},{1,9},{9... | collective-permute-start | bytes 786440 | tf_op jit(solution)/shard_map/ppermute | solution.py:483
  38.5 4.0 %collective-permute-done.7.refs_3_ = bf16[128,1024]{1,0:T(8,128)(2,1)} collective-permute-done((bf16[128,1024]{1,0:T(8,128)(2,1)S(1)}, bf16[128,1024]{1,0:T(8,128)(2,1)}, u32[]{:S(2)}, u32[]{:S(2)}) %collective-permute-start.7) | collective-permute-done | bytes 262176 | tf_op jit(solution)/shard_map/ppermute | solution.py:483
  42.5 2.1 %collective-permute-done.8.refs_7_ = bf16[128,1024]{1,0:T(8,128)(2,1)S(1)} collective-permute-done((bf16[128,1024]{1,0:T(8,128)(2,1)S(1)}, bf16[128,1024]{1,0:T(8,128)(2,1)S(1)}, u32[]{:S(2)}, u32[]{:S(2)}) %collective-permute-start.8) | collective-permute-done | bytes 262176 | tf_op jit(solution)/shard_map/ppermute | solution.py:485
  46.1 1.9 pad_maximum_fusion
  48.7 3.0 %collective-permute-done.10.refs_4_ = bf16[128,1024]{1,0:T(8,128)(2,1)} collective-permute-done((bf16[128,1024]{1,0:T(8,128)(2,1)}, bf16[128,1024]{1,0:T(8,128)(2,1)}, u32[]{:S(2)}, u32[]{:S(2)}) %collective-permute-start.10) | collective-permute-done | bytes 262176 | tf_op jit(solution)/shard_map/ppermute | solution.py:483
  55.9 22.7 %attention.2 = (bf16[1728,1024]{1,0:T(8,128)(2,1)}, bf16[1024,1024]{1,0:T(8,128)(2,1)}, bf16[512,512]{1,0:T(8,128)(2,1)}, bf16[512,512]{1,0:T(8,128)(2,1)}, bf16[512,1024]{1,0:T(8,128)(2,1)}) custom-call(s32[2,6,3]{2,1,0:T(8,128)} %copy.40.cnt_ref, s32[8]{0:T(128)} %compare_select_fusion.2.owner_ref, s32[1]{0:T(128)} %bitcast.8.low_ref, ...), custom_call_target="tpu_custom_call" | custom-call | flops 20000000 | bytes 14000 | tf_op jit(solution)/shard_map/attention/pallas_call | solution.py:259
  78.6 2.0 collective-permute-done.13.refs_6_
  82.7 2.0 fusion.1
  84.7 31.7 %attention.3 = (bf16[1728,1024]{1,0:T(8,128)(2,1)}, bf16[1024,1024]{1,0:T(8,128)(2,1)}, f32[512,512]{1,0:T(8,128)}, f32[512,512]{1,0:T(8,128)}, f32[512,1024]{1,...) custom-call(s32[2,6,3]{2,1,0:T(8,128)} %copy.40.cnt_ref, s32[8]{0:T(128)} %compare_select_fusion.2.owner_ref, ...), custom_call_target="tpu_custom_call" | custom-call | flops 20000000 | bytes 14000 | tf_op jit(solution)/shard_map/attention/pallas_call | solution.py:259
  116.5 1.6 collective-permute-start.18
  118.0 2.9 %add_convert_fusion = bf16[512,1024]{1,0:T(8,128)(2,1)} fusion(f32[512,1024]{1,0:T(8,128)} %get-tuple-element.161, bf16[512,1024]{1,0:T(8,128)(2,1)S(1)} %collective-permute-done.15), kind=kLoop, calls=%fused_computation | loop fusion | flops 1572864 | bytes 4194304 | tf_op jit(solution)/shard_map/convert_element_type | solution.py:655
  123.0 8.8 %tail.1 = (f32[320,1024]{1,0:T(8,128)}, f32[320,512]{1,0:T(8,128)}, f32[320,512]{1,0:T(8,128)}) custom-call(s32[1]{0:T(128)} %bitcast.1.core_ref, f32[864,1024]{1,0:T(8,128)} %get-tuple-element.144.own_ref, bf16[864,1024]{1,0:T(8,128)(2,1)} %copy-done.2, bf16[864,1024]{1,0:T(8,128)(2,1)} %bitcast.23, bf16[2,864,1024]{2,1,0:T(8,128)(2,1)} %bitcast.22, ...), custom_call_target="tpu_custom_call" | custom-call | flops 10000000 | bytes 12000 | tf_op jit(solution)/shard_map/tail/pallas_call | solution.py:414
  132.2 1.8 collective-permute-done.19.refs_1_
  135.8 2.9 %combine.2 = (f32[80,1024]{1,0:T(8,128)}, f32[80,1024]{1,0:T(8,128)}, f32[80,1024]{1,0:T(8,128)}, f32[80,1024]{1,0:T(8,128)}) custom-call(s32[1]{0:T(128)} %bitcast.place_ref, f32[320,1024]{1,0:T(8,128)} %get-tuple-element.152.refs_0_, f32[320,512]{1,0:T(8,128)} %copy-done.8, f32[320,512]{1,0:T(8,128)} %copy-done.9), custom_call_target="tpu_custom_call" | custom-call | flops 1000 | bytes 5000 | tf_op jit(solution)/shard_map/combine/pallas_call | solution.py:307
  140.5 1.7 collective-permute-start.23
  142.2 4.9 %collective-permute-done.24.refs_4_ = bf16[512,1024]{1,0:T(8,128)(2,1)S(1)} collective-permute-done((bf16[512,1024]{1,0:T(8,128)(2,1)}, bf16[512,1024]{1,0:T(8,128)(2,1)S(1)}, u32[]{:S(2)}, u32[]{:S(2)}) %collective-permute-start.24) | collective-permute-done | bytes 1048608 | tf_op jit(solution)/shard_map/ppermute | solution.py:459
  148.1 3.5 %combine.3 = (f32[128,1024]{1,0:T(8,128)}, f32[128,1024]{1,0:T(8,128)}, bf16[128,1024]{1,0:T(8,128)(2,1)}, bf16[128,1024]{1,0:T(8,128)(2,1)}) custom-call(s32[1]{0:T(128)} %bitcast.12.place_ref, f32[512,512]{1,0:T(8,128)} %get-tuple-element.167.refs_0_, f32[512,512]{1,0:T(8,128)} %get-tuple-element.168.refs_1_, bf16[512,512]{1,0:T(8,128)(2,1)} %copy-done.10, ...), custom_call_target="tpu_custom_call" | custom-call | flops 1000 | bytes 5000 | tf_op jit(solution)/shard_map/combine/pallas_call | solution.py:307
  153.7 3.8 %mixed.1 = bf16[864,1024]{1,0:T(8,128)(2,1)} custom-call(bf16[1728,1024]{1,0:T(8,128)(2,1)} %get-tuple-element.128.refs_0_, bf16[1728,1024]{1,0:T(8,128)(2,1)} %get-tuple-element.159.refs_1_, bf16[1024,1024]{1,0:T(8,128)(2,1)} %get-tuple-element.129.refs_1_.refs_2_, bf16[1024,1024]{1,0:T(8,128)(2,1)} %get-tuple-element.160.refs_3_), custom_call_target="tpu_custom_call" | custom-call | flops 2000000 | bytes 5000 | tf_op jit(solution)/shard_map/mixed/pallas_call | solution.py:360
  157.4 7.8 %collective-permute-done.25.refs_1_ = bf16[128,1024]{1,0:T(8,128)(2,1)S(1)} collective-permute-done((bf16[128,1024]{1,0:T(8,128)(2,1)}, bf16[128,1024]{1,0:T(8,128)(2,1)S(1)}, u32[]{:S(2)}, u32[]{:S(2)}) %collective-permute-start.25) | collective-permute-done | bytes 262176 | tf_op jit(solution)/shard_map/ppermute | solution.py:459
  166.9 2.9 %collective-permute-start.27 = (f32[80,256]{1,0:T(8,128)S(1)}, f32[80,256]{1,0:T(8,128)S(1)}, u32[]{:S(2)}, u32[]{:S(2)}) collective-permute-start(f32[80,256]{1,0:T(8,128)S(1)} %get-tuple-element.216), channel_id=1, source_target_pairs={{0,16},{4,20},{8,24},{12,28},{16,0},{20,4},{24,8},{28,12},{1,17},{... | collective-permute-start | bytes 245768 | tf_op jit(solution)/shard_map/ppermute | solution.py:459
  171.3 8.2 %collective-permute-done.30.refs_3_ = bf16[128,1024]{1,0:T(8,128)(2,1)S(1)} collective-permute-done((bf16[128,1024]{1,0:T(8,128)(2,1)S(1)}, bf16[128,1024]{1,0:T(8,128)(2,1)S(1)}, u32[]{:S(2)}, u32[]{:S(2)}) %collective-permute-start.30) | collective-permute-done | bytes 262176 | tf_op jit(solution)/shard_map/ppermute | solution.py:459
  180.0 2.5 %collective-permute-done.27 = f32[80,256]{1,0:T(8,128)S(1)} collective-permute-done((f32[80,256]{1,0:T(8,128)S(1)}, f32[80,256]{1,0:T(8,128)S(1)}, u32[]{:S(2)}, u32[]{:S(2)}) %collective-permute-start.27) | collective-permute-done | bytes 81952 | tf_op jit(solution)/shard_map/ppermute | solution.py:459
  187.7 2.2 %add_parts.1 = f32[128,1024]{1,0:T(8,128)} custom-call(f32[128,1024]{1,0:T(8,128)} %get-tuple-element.186.refs_0_, bf16[128,1024]{1,0:T(8,128)(2,1)} %copy-done.15, f32[128,1024]{1,0:T(8,128)} %copy-done.11, bf16[128,1024]{1,0:T(8,128)(2,1)} %copy-done.16), custom_call_target="tpu_custom_call" | custom-call | flops 1000 | bytes 2000 | tf_op jit(solution)/shard_map/add_parts/pallas_call | solution.py:327
  190.7 1.7 collective-permute-done.33
  193.9 2.0 collective-permute-start.36
  199.3 5.4 %layer_output.1 = bf16[864,1024]{1,0:T(8,128)(2,1)} custom-call(s32[6,3]{1,0:T(8,128)} %copy.33.cnt_ref, bf16[864,1024]{1,0:T(8,128)(2,1)} %copy-done.1, bf16[864,1024]{1,0:T(8,128)(2,1)} %bitcast.24, bf16[1728,1024]{1,0:T(8,128)(2,1)} %get-tuple-element.128.refs_0_, bf16[1728,1024]{1,0:T(8,128)(2,1)} %get-tuple-element.159.refs_1_, ...), custom_call_target="tpu_custom_call" | custom-call | flops 5000000 | bytes 10000 | tf_op jit(solution)/shard_map/layer_output/pallas_call | solution.py:445
  208.0 1.8 maximum_convert_fusion
  (133 shorter events, 47.1 us)
Async XLA Ops:
  2.9 16.0 %collective-permute-start.1 = (bf16[128,1024]{1,0:T(8,128)(2,1)S(1)}, bf16[128,1024]{1,0:T(8,128)(2,1)S(1)}, u32[]{:S(2)}, u32[]{:S(2)}) collective-permute-start(bf16[128,1024]{1,0:T(8,128)(2,1)S(1)} %pad_maximum_fusion.1.refs_2_), channel_id=1, source_target_pairs={{0,2},{1,3},{2,0},{3,1},{4,6},{5,7},{6,4},{7,5},{8,10},{9,11},{10,... | collective-permute-start | bytes 786440 | tf_op jit(solution)/shard_map/ppermute | solution.py:459
  5.9 18.7 %collective-permute-start.2 = (bf16[128,1024]{1,0:T(8,128)(2,1)S(1)}, bf16[128,1024]{1,0:T(8,128)(2,1)S(1)}, u32[]{:S(2)}, u32[]{:S(2)}) collective-permute-start(bf16[128,1024]{1,0:T(8,128)(2,1)S(1)} %pad_maximum_fusion.1.refs_2_), channel_id=1, source_target_pairs={{0,10},{1,11},{2,8},{3,9},{8,18},{9,19},{10,16},{11,17},{16,26},{1... | collective-permute-start | bytes 786440 | tf_op jit(solution)/shard_map/ppermute | solution.py:479
  7.4 17.2 %collective-permute-start.3 = (bf16[128,1024]{1,0:T(8,128)(2,1)S(1)}, bf16[128,1024]{1,0:T(8,128)(2,1)S(1)}, u32[]{:S(2)}, u32[]{:S(2)}) collective-permute-start(bf16[128,1024]{1,0:T(8,128)(2,1)S(1)} %pad_maximum_fusion.1.refs_2_), channel_id=1, source_target_pairs={{8,2},{9,3},{10,0},{11,1},{16,10},{17,11},{18,8},{19,9},{24,18},{2... | collective-permute-start | bytes 786440 | tf_op jit(solution)/shard_map/ppermute | solution.py:479
  8.8 10.1 %collective-permute-start = (s32[6,3]{0,1:T(4,128)}, s32[6,3]{0,1:T(4,128)S(1)}, u32[]{:S(2)}, u32[]{:S(2)}) collective-permute-start(s32[6,3]{0,1:T(4,128)} %param.13), channel_id=1, source_target_pairs={{0,1},{1,0},{2,3},{3,2},{4,5},{5,4},{6,7},{7,6},{8,9},{9,8},{10,11... | collective-permute-start | bytes 224 | tf_op jit(solution)/shard_map/ppermute | solution.py:459
  25.4 9.3 %collective-permute-start.6 = (bf16[2,864,1024]{2,1,0:T(8,128)(2,1)}, bf16[2,864,1024]{2,1,0:T(8,128)(2,1)S(1)}, u32[]{:S(2)}, u32[]{:S(2)}) collective-permute-start(bf16[2,864,1024]{2,1,0:T(8,128)(2,1)} %bitcast.17), channel_id=1, source_target_pairs={{0,1},{1,0},{2,3},{3,2},{4,5},{5,4},{6,7},{7,6},{8,9},{9,8},{10,11... | collective-permute-start | bytes 10616840 | tf_op jit(solution)/shard_map/ppermute | solution.py:459
  25.4 8.9 %collective-permute-start.4 = (bf16[128,1024]{1,0:T(8,128)(2,1)}, bf16[128,1024]{1,0:T(8,128)(2,1)S(1)}, u32[]{:S(2)}, u32[]{:S(2)}) collective-permute-start(bf16[128,1024]{1,0:T(8,128)(2,1)} %copy-done.18), channel_id=1, source_target_pairs={{0,8},{8,16},{16,24},{24,28},{28,20},{20,12},{12,4},{4,0},{1,9},{9... | collective-permute-start | bytes 786440 | tf_op jit(solution)/shard_map/ppermute | solution.py:483
  26.1 8.6 %collective-permute-start.5 = (bf16[128,1024]{1,0:T(8,128)(2,1)}, bf16[128,1024]{1,0:T(8,128)(2,1)S(1)}, u32[]{:S(2)}, u32[]{:S(2)}) collective-permute-start(bf16[128,1024]{1,0:T(8,128)(2,1)} %copy-done.5), channel_id=1, source_target_pairs={{8,0},{16,8},{24,16},{28,24},{20,28},{12,20},{4,12},{0,4},{9,1},{1... | collective-permute-start | bytes 786440 | tf_op jit(solution)/shard_map/ppermute | solution.py:485
  27.5 11.0 %collective-permute-start.9 = (bf16[128,1024]{1,0:T(8,128)(2,1)}, bf16[128,1024]{1,0:T(8,128)(2,1)S(1)}, u32[]{:S(2)}, u32[]{:S(2)}) collective-permute-start(bf16[128,1024]{1,0:T(8,128)(2,1)} %copy-done.18), channel_id=1, source_target_pairs={{0,2},{1,3},{2,0},{3,1},{4,6},{5,7},{6,4},{7,5},{8,10},{9,11},{10,... | collective-permute-start | bytes 786440 | tf_op jit(solution)/shard_map/ppermute | solution.py:459
  34.8 7.8 %collective-permute-start.7 = (bf16[128,1024]{1,0:T(8,128)(2,1)S(1)}, bf16[128,1024]{1,0:T(8,128)(2,1)}, u32[]{:S(2)}, u32[]{:S(2)}) collective-permute-start(bf16[128,1024]{1,0:T(8,128)(2,1)S(1)} %collective-permute-done.4.refs_2_), channel_id=1, source_target_pairs={{0,8},{8,16},{16,24},{24,28},{28,20},{20,12},{12,4},{4,0},{1,9},{9... | collective-permute-start | bytes 786440 | tf_op jit(solution)/shard_map/ppermute | solution.py:483
  37.0 7.7 %collective-permute-start.8 = (bf16[128,1024]{1,0:T(8,128)(2,1)S(1)}, bf16[128,1024]{1,0:T(8,128)(2,1)S(1)}, u32[]{:S(2)}, u32[]{:S(2)}) collective-permute-start(bf16[128,1024]{1,0:T(8,128)(2,1)S(1)} %collective-permute-done.5.refs_6_), channel_id=1, source_target_pairs={{8,0},{16,8},{24,16},{28,24},{20,28},{12,20},{4,12},{0,4},{9,1},{1... | collective-permute-start | bytes 786440 | tf_op jit(solution)/shard_map/ppermute | solution.py:485
  37.0 11.0 %collective-permute-start.11 = (bf16[128,1024]{1,0:T(8,128)(2,1)S(1)}, bf16[128,1024]{1,0:T(8,128)(2,1)S(1)}, u32[]{:S(2)}, u32[]{:S(2)}) collective-permute-start(bf16[128,1024]{1,0:T(8,128)(2,1)S(1)} %collective-permute-done.4.refs_2_), channel_id=1, source_target_pairs={{0,2},{1,3},{2,0},{3,1},{4,6},{5,7},{6,4},{7,5},{8,10},{9,11},{10,... | collective-permute-start | bytes 786440 | tf_op jit(solution)/shard_map/ppermute | solution.py:459
  44.7 7.1 %collective-permute-start.10 = (bf16[128,1024]{1,0:T(8,128)(2,1)}, bf16[128,1024]{1,0:T(8,128)(2,1)}, u32[]{:S(2)}, u32[]{:S(2)}) collective-permute-start(bf16[128,1024]{1,0:T(8,128)(2,1)} %collective-permute-done.7.refs_3_), channel_id=1, source_target_pairs={{0,8},{8,16},{16,24},{24,28},{28,20},{20,12},{12,4},{4,0},{1,9},{9... | collective-permute-start | bytes 786440 | tf_op jit(solution)/shard_map/ppermute | solution.py:483
  51.7 28.9 %collective-permute-start.14 = (bf16[384,1024]{1,0:T(8,128)(2,1)}, bf16[384,1024]{1,0:T(8,128)(2,1)}, u32[]{:S(2)}, u32[]{:S(2)}) collective-permute-start(bf16[384,1024]{1,0:T(8,128)(2,1)} %pad_maximum_fusion), channel_id=1, source_target_pairs={{0,2},{1,3},{2,0},{3,1},{4,6},{5,7},{6,4},{7,5},{8,10},{9,11},{10,... | collective-permute-start | bytes 2359304 | tf_op jit(solution)/shard_map/ppermute | solution.py:459
  53.2 25.4 %collective-permute-start.12 = (bf16[128,1024]{1,0:T(8,128)(2,1)}, bf16[128,1024]{1,0:T(8,128)(2,1)}, u32[]{:S(2)}, u32[]{:S(2)}) collective-permute-start(bf16[128,1024]{1,0:T(8,128)(2,1)} %collective-permute-done.7.refs_3_), channel_id=1, source_target_pairs={{0,2},{1,3},{2,0},{3,1},{4,6},{5,7},{6,4},{7,5},{8,10},{9,11},{10,... | collective-permute-start | bytes 786440 | tf_op jit(solution)/shard_map/ppermute | solution.py:459
  53.7 26.9 %collective-permute-start.13 = (bf16[128,1024]{1,0:T(8,128)(2,1)}, bf16[128,1024]{1,0:T(8,128)(2,1)}, u32[]{:S(2)}, u32[]{:S(2)}) collective-permute-start(bf16[128,1024]{1,0:T(8,128)(2,1)} %collective-permute-done.10.refs_4_), channel_id=1, source_target_pairs={{0,2},{1,3},{2,0},{3,1},{4,6},{5,7},{6,4},{7,5},{8,10},{9,11},{10,... | collective-permute-start | bytes 786440 | tf_op jit(solution)/shard_map/ppermute | solution.py:459
  80.7 35.7 %collective-permute-start.15 = (bf16[512,1024]{1,0:T(8,128)(2,1)}, bf16[512,1024]{1,0:T(8,128)(2,1)S(1)}, u32[]{:S(2)}, u32[]{:S(2)}) collective-permute-start(bf16[512,1024]{1,0:T(8,128)(2,1)} %get-tuple-element.142), channel_id=1, source_target_pairs={{0,2},{1,3},{2,0},{3,1},{4,6},{5,7},{6,4},{7,5},{8,10},{9,11},{10,... | collective-permute-start | bytes 3145736 | tf_op jit(solution)/shard_map/ppermute | solution.py:459
  82.1 34.2 %collective-permute-start.16 = (bf16[512,512]{1,0:T(8,128)(2,1)}, bf16[512,512]{1,0:T(8,128)(2,1)S(1)}, u32[]{:S(2)}, u32[]{:S(2)}) collective-permute-start(bf16[512,512]{1,0:T(8,128)(2,1)} %get-tuple-element.143), channel_id=1, source_target_pairs={{0,2},{1,3},{2,0},{3,1},{4,6},{5,7},{6,4},{7,5},{8,10},{9,11},{10,... | collective-permute-start | bytes 1572872 | tf_op jit(solution)/shard_map/ppermute | solution.py:459
  116.5 15.3 %collective-permute-start.18 = (bf16[512,512]{1,0:T(8,128)(2,1)}, bf16[512,512]{1,0:T(8,128)(2,1)}, u32[]{:S(2)}, u32[]{:S(2)}) collective-permute-start(bf16[512,512]{1,0:T(8,128)(2,1)} %get-tuple-element.151), channel_id=1, source_target_pairs={{0,2},{1,3},{2,0},{3,1},{4,6},{5,7},{6,4},{7,5},{8,10},{9,11},{10,... | collective-permute-start | bytes 1572872 | tf_op jit(solution)/shard_map/ppermute | solution.py:459
  121.0 26.2 %collective-permute-start.24 = (bf16[512,1024]{1,0:T(8,128)(2,1)}, bf16[512,1024]{1,0:T(8,128)(2,1)S(1)}, u32[]{:S(2)}, u32[]{:S(2)}) collective-permute-start(bf16[512,1024]{1,0:T(8,128)(2,1)} %add_convert_fusion), channel_id=1, source_target_pairs={{0,4},{4,0},{8,12},{12,8},{16,20},{20,16},{24,28},{28,24},{1,5},{5... | collective-permute-start | bytes 3145736 | tf_op jit(solution)/shard_map/ppermute | solution.py:459
  138.8 28.0 %collective-permute-start.21 = (f32[80,1024]{1,0:T(8,128)}, f32[80,1024]{1,0:T(8,128)S(1)}, u32[]{:S(2)}, u32[]{:S(2)}) collective-permute-start(f32[80,1024]{1,0:T(8,128)} %get-tuple-element.156), channel_id=1, source_target_pairs={{0,4},{4,0},{8,12},{12,8},{16,20},{20,16},{24,28},{28,24},{1,5},{5... | collective-permute-start | bytes 983048 | tf_op jit(solution)/shard_map/ppermute | solution.py:459
  140.0 26.7 %collective-permute-start.22 = (f32[80,1024]{1,0:T(8,128)}, f32[80,1024]{1,0:T(8,128)S(1)}, u32[]{:S(2)}, u32[]{:S(2)}) collective-permute-start(f32[80,1024]{1,0:T(8,128)} %get-tuple-element.157), channel_id=1, source_target_pairs={{0,2},{1,3},{2,0},{3,1},{4,6},{5,7},{6,4},{7,5},{8,10},{9,11},{10,... | collective-permute-start | bytes 983048 | tf_op jit(solution)/shard_map/ppermute | solution.py:532
  140.5 26.2 %collective-permute-start.23 = (f32[80,1024]{1,0:T(8,128)}, f32[80,1024]{1,0:T(8,128)S(1)}, u32[]{:S(2)}, u32[]{:S(2)}) collective-permute-start(f32[80,1024]{1,0:T(8,128)} %get-tuple-element.158), channel_id=1, source_target_pairs={{0,6},{1,7},{2,4},{3,5},{4,2},{5,3},{6,0},{7,1},{8,14},{9,15},{10,... | collective-permute-start | bytes 983048 | tf_op jit(solution)/shard_map/ppermute | solution.py:532
  151.6 13.6 %collective-permute-start.25 = (bf16[128,1024]{1,0:T(8,128)(2,1)}, bf16[128,1024]{1,0:T(8,128)(2,1)S(1)}, u32[]{:S(2)}, u32[]{:S(2)}) collective-permute-start(bf16[128,1024]{1,0:T(8,128)(2,1)} %get-tuple-element.173), channel_id=1, source_target_pairs={{0,16},{4,20},{8,24},{12,28},{16,0},{20,4},{24,8},{28,12},{1,17},{... | collective-permute-start | bytes 786440 | tf_op jit(solution)/shard_map/ppermute | solution.py:459
  153.1 29.5 %collective-permute-start.29 = (f32[128,1024]{1,0:T(8,128)}, f32[128,1024]{1,0:T(8,128)S(1)}, u32[]{:S(2)}, u32[]{:S(2)}) collective-permute-start(f32[128,1024]{1,0:T(8,128)} %get-tuple-element.180), channel_id=1, source_target_pairs={{0,8},{4,12},{8,0},{12,4},{16,24},{20,28},{24,16},{28,20},{1,9},{5... | collective-permute-start | bytes 1572872 | tf_op jit(solution)/shard_map/ppermute | solution.py:459
  165.2 14.3 %collective-permute-start.30 = (bf16[128,1024]{1,0:T(8,128)(2,1)S(1)}, bf16[128,1024]{1,0:T(8,128)(2,1)S(1)}, u32[]{:S(2)}, u32[]{:S(2)}) collective-permute-start(bf16[128,1024]{1,0:T(8,128)(2,1)S(1)} %copy-done.21), channel_id=1, source_target_pairs={{0,24},{4,28},{8,16},{12,20},{16,8},{20,12},{24,0},{28,4},{1,25},{... | collective-permute-start | bytes 786440 | tf_op jit(solution)/shard_map/ppermute | solution.py:459
  166.9 13.2 %collective-permute-start.26 = (f32[80,256]{1,0:T(8,128)S(1)}, f32[80,256]{1,0:T(8,128)S(1)}, u32[]{:S(2)}, u32[]{:S(2)}) collective-permute-start(f32[80,256]{1,0:T(8,128)S(1)} %get-tuple-element.217), channel_id=1, source_target_pairs={{0,8},{4,12},{8,0},{12,4},{16,24},{20,28},{24,16},{28,20},{1,9},{5... | collective-permute-start | bytes 245768 | tf_op jit(solution)/shard_map/ppermute | solution.py:459
  166.9 15.6 %collective-permute-start.27 = (f32[80,256]{1,0:T(8,128)S(1)}, f32[80,256]{1,0:T(8,128)S(1)}, u32[]{:S(2)}, u32[]{:S(2)}) collective-permute-start(f32[80,256]{1,0:T(8,128)S(1)} %get-tuple-element.216), channel_id=1, source_target_pairs={{0,16},{4,20},{8,24},{12,28},{16,0},{20,4},{24,8},{28,12},{1,17},{... | collective-permute-start | bytes 245768 | tf_op jit(solution)/shard_map/ppermute | solution.py:459
  169.8 12.7 %collective-permute-start.28 = (f32[80,256]{1,0:T(8,128)S(1)}, f32[80,256]{1,0:T(8,128)S(1)}, u32[]{:S(2)}, u32[]{:S(2)}) collective-permute-start(f32[80,256]{1,0:T(8,128)S(1)} %get-tuple-element.215), channel_id=1, source_target_pairs={{0,24},{4,28},{8,16},{12,20},{16,8},{20,12},{24,0},{28,4},{1,25},{... | collective-permute-start | bytes 245768 | tf_op jit(solution)/shard_map/ppermute | solution.py:459
  182.5 15.5 %collective-permute-start.37 = (bf16[864,1024]{1,0:T(8,128)(2,1)}, bf16[864,1024]{1,0:T(8,128)(2,1)S(1)}, u32[]{:S(2)}, u32[]{:S(2)}) collective-permute-start(bf16[864,1024]{1,0:T(8,128)(2,1)} %mixed.1), channel_id=1, source_target_pairs={{0,1},{1,0},{2,3},{3,2},{4,5},{5,4},{6,7},{7,6},{8,9},{9,8},{10,11... | collective-permute-start | bytes 5308424 | tf_op jit(solution)/shard_map/ppermute | solution.py:459
  192.4 12.4 %collective-permute-start.34 = (bf16[80,1024]{1,0:T(8,128)(2,1)S(1)}, bf16[80,1024]{1,0:T(8,128)(2,1)S(1)}, u32[]{:S(2)}, u32[]{:S(2)}) collective-permute-start(bf16[80,1024]{1,0:T(8,128)(2,1)S(1)} %constant_dynamic-update-slice_fusion.4), channel_id=1, source_target_pairs={{0,4},{4,0},{8,12},{12,8},{16,20},{20,16},{24,28},{28,24},{1,5},{5... | collective-permute-start | bytes 491528 | tf_op jit(solution)/shard_map/ppermute | solution.py:459
  193.3 11.4 %collective-permute-start.35 = (bf16[80,1024]{1,0:T(8,128)(2,1)S(1)}, bf16[80,1024]{1,0:T(8,128)(2,1)S(1)}, u32[]{:S(2)}, u32[]{:S(2)}) collective-permute-start(bf16[80,1024]{1,0:T(8,128)(2,1)S(1)} %constant_dynamic-update-slice_fusion.4), channel_id=1, source_target_pairs={{0,2},{1,3},{2,0},{3,1},{4,6},{5,7},{6,4},{7,5},{8,10},{9,11},{10,... | collective-permute-start | bytes 491528 | tf_op jit(solution)/shard_map/ppermute | solution.py:532
  193.9 10.9 %collective-permute-start.36 = (bf16[80,1024]{1,0:T(8,128)(2,1)S(1)}, bf16[80,1024]{1,0:T(8,128)(2,1)}, u32[]{:S(2)}, u32[]{:S(2)}) collective-permute-start(bf16[80,1024]{1,0:T(8,128)(2,1)S(1)} %constant_dynamic-update-slice_fusion.4), channel_id=1, source_target_pairs={{0,6},{1,7},{2,4},{3,5},{4,2},{5,3},{6,0},{7,1},{8,14},{9,15},{10,... | collective-permute-start | bytes 491528 | tf_op jit(solution)/shard_map/ppermute | solution.py:532
  (30 other events, 201.6 us)

commit v11 on v10

--- a/solution.py
+++ b/solution.py
@@ -249,7 +249,7 @@
     tokens = own.shape[1]
     rows = block_rows(tokens)
     steps = tokens // rows
-    cols = blocks[0].shape[1]
+    cols = blocks[0][0].shape[1]
     whole = lambda shape: pl.BlockSpec(shape, lambda h, i: (0, 0))
     at = lambda h, i: (h * steps + i, 0)
     packs = None if earlier is None else len(earlier[0])
@@ -264,7 +264,7 @@
         + two_halves(rows, steps, (1,))
         + [pl.BlockSpec((rows, cols // 4 * 3), at)] * (packs or 0)
         + [whole((D, cols // 4 * 3))] * (packs or 0)
-        + [whole(b.shape) for b in blocks],
+        + [pl.BlockSpec((D // dp, cols), functools.partial(lambda at, h, i: (at, 0), at)) for _, at in blocks],
         out_specs=[pl.BlockSpec((rows, cols), at), whole((D, cols))] + [whole(g.shape) for g in grads] + back,
         out_shape=[
             jax.ShapeDtypeStruct((2 * tokens, cols), BF16),
@@ -281,7 +281,7 @@
         compiler_params=params(),
         cost_estimate=cost(20e9, 14e6),
         name="attention",
-    )(counts, owners, low, own, far, own, far, *[x for group in earlier or () for x in group], *blocks)
+    )(counts, owners, low, own, far, own, far, *[x for group in earlier or () for x in group], *[b for b, _ in blocks])
 
 
 def combine_kernel(counts, place_ref, *refs):
@@ -474,9 +474,8 @@
     @classmethod
     def across(cls, x, axis, size, other, other_size, bit):
         ring = cls(swap(x, other, other_size, bit), axis, size)
-        for pairs, blocks in ((ring.forward, ring.ahead), (ring.backward, ring.behind)):
-            both = [(s * other_size + g, t * other_size + (g ^ bit)) for s, t in pairs for g in range(other_size)]
-            blocks.append(lax.ppermute(x, (axis, other), both))
+        both = [(s * other_size + g, t * other_size + (g ^ bit)) for s, t in ring.forward for g in range(other_size)]
+        ring.ahead.append(lax.ppermute(x, (axis, other), both))
         return ring
 
     def send(self):
@@ -621,22 +620,17 @@
     (both,) = step_all(rings, both)
     while ring.steps < dp // 2:
         passed.append(cross(ring.ahead[-1], 1))
-        if ring.steps == dp // 2 - 1:
-            behind = jnp.concatenate(ring.behind[1:], axis=0)
-            passed[-2], behind = step_all(rings, passed[-2], behind)
-        else:
-            (passed[-2],) = step_all(rings, passed[-2])
-    ring.ahead, behind = together(ring.ahead, behind)
+        (passed[-2],) = step_all(rings, passed[-2])
+    ring.ahead, ring.behind = together(ring.ahead, ring.behind)
     passed.append(cross(ring.ahead[-1], 1))
-    passed.append(cross(behind, 1))
+    passed.append(cross(jnp.concatenate(ring.behind[1:], axis=0), 1))
 
     packs, weights, crossing = [], [], []
     for f in list(fars) + [0]:
         if f:
-            blocks = rings[f - 1].ahead + rings[f - 1].behind[1:]
+            blocks = [(x, 0) for x in rings[f - 1].ahead + rings[f - 1].behind[1:]]
         else:
-            rows = shard.shape[0]
-            blocks = [shard] + passed[:-1] + [passed[-1][b * rows : (b + 1) * rows] for b in range(dp // 2 - 1)]
+            blocks = [(x, 0) for x in [shard] + passed[:-1]] + [(passed[-1], b) for b in range(dp // 2 - 1)]
         made = attention_call(both_counts, owners, low, *both, None if f else (packs, weights), blocks, dp)
         if f == 1:
             made, passed[-3:] = together(made, passed[-3:])
@@ -666,16 +660,16 @@
     landing = [blocks[0]] + [swap(blocks[j], "dp", dp, 2 * j) for j in rests]
     near = dp // 2 * 3 // 4
 
-    def after(mixed, *arrived):
-        return [mixed] + list(arrived) + [landing[1]] + landing[near:]
+    def after(mixed, share):
+        return [swap(mixed, "group", group, 1), share] + landing[2:near]
 
     def last(mixed, *arrived):
-        output = output_call(counts, swap(mixed, "group", group, 1), emb, packs, weights)
-        total = add_call(list(arrived))
+        output = output_call(counts, mixed, emb, packs, weights)
+        total = add_call(list(arrived) + [landing[1]] + landing[near:])
         return output, total[:, : 3 * width].reshape(total.shape[0], 3, width), total[:, 3 * width :].T
 
     grad_w_stem, (output, grad_w_qkv, grad_w_out) = sum_stem(
-        stem_parts, [mixed_call(packs, weights), landing[0]] + landing[2:near], after, last, dp, group
+        stem_parts, [mixed_call(packs, weights), landing[0]], after, last, dp, group
     )
     return (output.reshape(scenes, GROUPS, CAP, D), grad_w_stem, grad_w_qkv, grad_w_out)
 

time: 210 us -> 217 us (1.033)
  waiting for transfers between devices: 52.1 us -> 58.2 us
  local copies, waits for them, and re-layouts: 16.9 us -> 14.1 us
  starting transfers between devices: 42.6 us -> 45.1 us
    ppermute x2 -> x3, waiting for transfers between devices: 2.52 us -> 6.19 us  [send(): moved.append(lax.ppermute(self.behind[-1], self.axis, self.backward))]
    ppermute x28, waiting for transfers between devices: 31.5 us -> 34.8 us  [swap(): return lax.ppermute(x, axis, [(i, i ^ bit) for i in range(size)])]
    ppermute x28, starting transfers between devices: 29.2 us -> 32 us  [swap(): return lax.ppermute(x, axis, [(i, i ^ bit) for i in range(size)])]
    ppermute x2 -> x3, starting transfers between devices: 1.36 us -> 3.89 us  [send(): moved.append(lax.ppermute(self.behind[-1], self.axis, self.backward))]
    ppermute x3, waiting for transfers between devices: 12.5 us -> 10.2 us  [send(): moved = [lax.ppermute(self.ahead[-1], self.axis, self.forward)]]
    ppermute x2 -> x1, waiting for transfers between devices: 5.69 us -> 6.99 us  [across(): ring.ahead.append(lax.ppermute(x, (axis, other), both))]
    unnamed x51 -> x49, local copies, waits for them, and re-layouts: 10.9 us -> 10.3 us
  transfers between devices with their start and end apart: 39 -> 39, of which waited for: 17 -> 17; matrix products, arithmetic and copies ran while one was open for 7% -> 6% of each run, Pallas kernels for 42% -> 41%
where the time goes in v11:
time: 217 us
  Pallas kernels  89.2 us (41%)
  waiting for transfers between devices  58.2 us (27%)
  starting transfers between devices  45.1 us (21%)
  local copies, waits for them, and re-layouts  14.1 us (6%)
  other arithmetic  9.17 us (4%)
    pallas_call x2, Pallas kernels, attention_call(): pl.pallas_call(functools.partial(attention_kernel, packs, len(blocks), dp...  54.4 us
    ppermute x28, waiting for transfers between devices, swap(): return lax.ppermute(x, axis, [(i, i ^ bit) for i in range(size)])  34.8 us
    ppermute x28, starting transfers between devices, swap(): return lax.ppermute(x, axis, [(i, i ^ bit) for i in range(size)])  32 us
    unnamed x49, local copies, waits for them, and re-layouts  10.3 us
    ppermute x3, waiting for transfers between devices, send(): moved = [lax.ppermute(self.ahead[-1], self.axis, self.forward)]  10.2 us
    pallas_call x1, Pallas kernels, tail_call(): pl.pallas_call(tail_kernel, grid=(tokens // rows,), in_specs=[SCALARS, pe...  8.74 us
    pallas_call x1, Pallas kernels, stem_call(): pl.pallas_call(stem_kernel, grid=(scenes // block,), in_specs=[whole(coun...  8.18 us
    ppermute x1, waiting for transfers between devices, across(): ring.ahead.append(lax.ppermute(x, (axis, other), both))  6.99 us
  transfers between devices with their start and end apart: 39, of which 17 were waited for; matrix products, arithmetic and copies ran while one was open for 6% of the time, Pallas kernels for 41%

profile of v11, /device:TPU:0, one launch (start us, length us, event | category | flops | bytes accessed | tf_op | source)
XLA Modules:
  0.0 216.8 jit_solution(9405877428909434965)
XLA Ops:
  2.9 3.0 %collective-permute-start.1 = (bf16[128,1024]{1,0:T(8,128)(2,1)S(1)}, bf16[128,1024]{1,0:T(8,128)(2,1)S(1)}, u32[]{:S(2)}, u32[]{:S(2)}) collective-permute-start(bf16[128,1024]{1,0:T(8,128)(2,1)S(1)} %pad_maximum_fusion.1.refs_2_), channel_id=1, source_target_pairs={{0,2},{1,3},{2,0},{3,1},{4,6},{5,7},{6,4},{7,5},{8,10},{9,11},{10,... | collective-permute-start | bytes 786440 | tf_op jit(solution)/shard_map/ppermute | solution.py:459
  8.8 8.2 %stem_norm.1 = (bf16[6,144,1024]{2,1,0:T(8,128)(2,1)}, bf16[2,6,144,1024]{3,2,1,0:T(8,128)(2,1)}, bf16[6,144,256]{2,1,0:T(8,128)(2,1)}) custom-call(s32[6,3]{1,0:T(8,128)} %copy.33.cnt_ref, s32[6,3,48]{2,1,0:T(4,128)} %idx_ref.1, bf16[6,144,640]{2,1,0:T(8,128)(2,1)} %patch_ref.1, bf16[640,1024]{1,0:T(8,128)(2,1)} %w_ref.1, f32[1,1024]{1,0:T(1,128)} %bitcast.31, ...), custom_call_target="tpu_custom_call" | custom-call | flops 8000000 | bytes 12000 | tf_op jit(solution)/shard_map/stem_norm/pallas_call | solution.py:98
  17.6 7.0 %collective-permute-done.2.refs_1_ = bf16[128,1024]{1,0:T(8,128)(2,1)S(1)} collective-permute-done((bf16[128,1024]{1,0:T(8,128)(2,1)S(1)}, bf16[128,1024]{1,0:T(8,128)(2,1)S(1)}, u32[]{:S(2)}, u32[]{:S(2)}) %collective-permute-start.2) | collective-permute-done | bytes 262176 | tf_op jit(solution)/shard_map/ppermute | solution.py:478
  25.4 2.0 collective-permute-start.4
  28.9 5.4 %collective-permute-done.3.refs_2_ = bf16[128,1024]{1,0:T(8,128)(2,1)S(1)} collective-permute-done((bf16[128,1024]{1,0:T(8,128)(2,1)}, bf16[128,1024]{1,0:T(8,128)(2,1)S(1)}, u32[]{:S(2)}, u32[]{:S(2)}) %collective-permute-start.3) | collective-permute-done | bytes 262176 | tf_op jit(solution)/shard_map/ppermute | solution.py:482
  37.9 4.5 %collective-permute-done.6.refs_3_ = bf16[128,1024]{1,0:T(8,128)(2,1)} collective-permute-done((bf16[128,1024]{1,0:T(8,128)(2,1)S(1)}, bf16[128,1024]{1,0:T(8,128)(2,1)}, u32[]{:S(2)}, u32[]{:S(2)}) %collective-permute-start.6) | collective-permute-done | bytes 262176 | tf_op jit(solution)/shard_map/ppermute | solution.py:482
  45.5 5.1 %collective-permute-done.10.refs_7_ = bf16[128,1024]{1,0:T(8,128)(2,1)S(1)} collective-permute-done((bf16[128,1024]{1,0:T(8,128)(2,1)S(1)}, bf16[128,1024]{1,0:T(8,128)(2,1)S(1)}, u32[]{:S(2)}, u32[]{:S(2)}) %collective-permute-start.10) | collective-permute-done | bytes 262176 | tf_op jit(solution)/shard_map/ppermute | solution.py:484
  56.1 22.7 %attention.2 = (bf16[1728,1024]{1,0:T(8,128)(2,1)}, bf16[1024,1024]{1,0:T(8,128)(2,1)}, bf16[512,512]{1,0:T(8,128)(2,1)}, bf16[512,512]{1,0:T(8,128)(2,1)}, bf16[512,1024]{1,0:T(8,128)(2,1)}) custom-call(s32[2,6,3]{2,1,0:T(8,128)} %copy.40.cnt_ref, s32[8]{0:T(128)} %compare_select_fusion.2.owner_ref, s32[1]{0:T(128)} %bitcast.8.low_ref, ...), custom_call_target="tpu_custom_call" | custom-call | flops 20000000 | bytes 14000 | tf_op jit(solution)/shard_map/attention/pallas_call | solution.py:259
  78.8 2.0 collective-permute-done.13.refs_6_
  82.8 31.7 %attention.3 = (bf16[1728,1024]{1,0:T(8,128)(2,1)}, bf16[1024,1024]{1,0:T(8,128)(2,1)}, f32[512,512]{1,0:T(8,128)}, f32[512,512]{1,0:T(8,128)}, f32[512,1024]{1,...) custom-call(s32[2,6,3]{2,1,0:T(8,128)} %copy.40.cnt_ref, s32[8]{0:T(128)} %compare_select_fusion.2.owner_ref, ...), custom_call_target="tpu_custom_call" | custom-call | flops 20000000 | bytes 14000 | tf_op jit(solution)/shard_map/attention/pallas_call | solution.py:259
  114.6 1.6 collective-permute-start.18
  116.2 3.0 %add_convert_fusion = bf16[512,1024]{1,0:T(8,128)(2,1)} fusion(f32[512,1024]{1,0:T(8,128)} %get-tuple-element.162, bf16[512,1024]{1,0:T(8,128)(2,1)S(1)} %collective-permute-done.15), kind=kLoop, calls=%fused_computation | loop fusion | flops 1572864 | bytes 4194304 | tf_op jit(solution)/shard_map/convert_element_type | solution.py:649
  121.6 8.7 %tail.1 = (f32[320,1024]{1,0:T(8,128)}, f32[320,512]{1,0:T(8,128)}, f32[320,512]{1,0:T(8,128)}) custom-call(s32[1]{0:T(128)} %bitcast.1.core_ref, f32[864,1024]{1,0:T(8,128)} %get-tuple-element.145.own_ref, bf16[864,1024]{1,0:T(8,128)(2,1)} %copy-done.3, bf16[864,1024]{1,0:T(8,128)(2,1)} %bitcast.23, bf16[2,864,1024]{2,1,0:T(8,128)(2,1)} %bitcast.22, ...), custom_call_target="tpu_custom_call" | custom-call | flops 10000000 | bytes 12000 | tf_op jit(solution)/shard_map/tail/pallas_call | solution.py:414
  130.9 1.8 collective-permute-done.19.refs_1_
  134.5 2.9 %combine.2 = (f32[80,1024]{1,0:T(8,128)}, f32[80,1024]{1,0:T(8,128)}, f32[80,1024]{1,0:T(8,128)}, f32[80,1024]{1,0:T(8,128)}) custom-call(s32[1]{0:T(128)} %bitcast.place_ref, f32[320,1024]{1,0:T(8,128)} %get-tuple-element.153.refs_0_, f32[320,512]{1,0:T(8,128)} %copy-done.10, f32[320,512]{1,0:T(8,128)} %copy-done.11), custom_call_target="tpu_custom_call" | custom-call | flops 1000 | bytes 5000 | tf_op jit(solution)/shard_map/combine/pallas_call | solution.py:307
  138.9 2.0 collective-permute-start.23
  140.9 3.7 %mixed.1 = bf16[864,1024]{1,0:T(8,128)(2,1)} custom-call(bf16[1728,1024]{1,0:T(8,128)(2,1)} %get-tuple-element.129.refs_0_, bf16[1728,1024]{1,0:T(8,128)(2,1)} %get-tuple-element.160.refs_1_, bf16[1024,1024]{1,0:T(8,128)(2,1)} %get-tuple-element.130.refs_1_.refs_2_, bf16[1024,1024]{1,0:T(8,128)(2,1)} %get-tuple-element.161.refs_3_), custom_call_target="tpu_custom_call" | custom-call | flops 2000000 | bytes 5000 | tf_op jit(solution)/shard_map/mixed/pallas_call | solution.py:360
  146.3 3.6 %combine.3 = (f32[128,1024]{1,0:T(8,128)}, f32[128,1024]{1,0:T(8,128)}, bf16[128,1024]{1,0:T(8,128)(2,1)}, bf16[128,1024]{1,0:T(8,128)(2,1)}) custom-call(s32[1]{0:T(128)} %bitcast.12.place_ref, f32[512,512]{1,0:T(8,128)} %get-tuple-element.168.refs_0_, f32[512,512]{1,0:T(8,128)} %get-tuple-element.169.refs_1_, bf16[512,512]{1,0:T(8,128)(2,1)} %copy-done.12, ...), custom_call_target="tpu_custom_call" | custom-call | flops 1000 | bytes 5000 | tf_op jit(solution)/shard_map/combine/pallas_call | solution.py:307
  149.9 8.8 %collective-permute-done.21 = f32[80,1024]{1,0:T(8,128)} collective-permute-done((f32[80,1024]{1,0:T(8,128)}, f32[80,1024]{1,0:T(8,128)}, u32[]{:S(2)}, u32[]{:S(2)}) %collective-permute-start.21) | collective-permute-done | bytes 327712 | tf_op jit(solution)/shard_map/ppermute | solution.py:459
  159.5 2.5 %collective-permute-start.29 = (bf16[128,1024]{1,0:T(8,128)(2,1)}, bf16[128,1024]{1,0:T(8,128)(2,1)}, u32[]{:S(2)}, u32[]{:S(2)}) collective-permute-start(bf16[128,1024]{1,0:T(8,128)(2,1)} %get-tuple-element.179), channel_id=1, source_target_pairs={{0,16},{4,20},{8,24},{12,28},{16,0},{20,4},{24,8},{28,12},{1,17},{... | collective-permute-start | bytes 786440 | tf_op jit(solution)/shard_map/ppermute | solution.py:459
  167.2 8.3 %collective-permute-done.29.refs_1_ = bf16[128,1024]{1,0:T(8,128)(2,1)} collective-permute-done((bf16[128,1024]{1,0:T(8,128)(2,1)}, bf16[128,1024]{1,0:T(8,128)(2,1)}, u32[]{:S(2)}, u32[]{:S(2)}) %collective-permute-start.29) | collective-permute-done | bytes 262176 | tf_op jit(solution)/shard_map/ppermute | solution.py:459
  175.5 3.1 %collective-permute-start.27 = (f32[80,256]{1,0:T(8,128)}, f32[80,256]{1,0:T(8,128)}, u32[]{:S(2)}, u32[]{:S(2)}) collective-permute-start(f32[80,256]{1,0:T(8,128)} %get-tuple-element.210), channel_id=1, source_target_pairs={{0,24},{4,28},{8,16},{12,20},{16,8},{20,12},{24,0},{28,4},{1,25},{... | collective-permute-start | bytes 245768 | tf_op jit(solution)/shard_map/ppermute | solution.py:459
  178.6 5.6 %collective-permute-done.25 = f32[80,256]{1,0:T(8,128)} collective-permute-done((f32[80,256]{1,0:T(8,128)}, f32[80,256]{1,0:T(8,128)}, u32[]{:S(2)}, u32[]{:S(2)}) %collective-permute-start.25) | collective-permute-done | bytes 81952 | tf_op jit(solution)/shard_map/ppermute | solution.py:459
  184.2 2.9 %collective-permute-start.37 = (bf16[128,1024]{1,0:T(8,128)(2,1)}, bf16[128,1024]{1,0:T(8,128)(2,1)}, u32[]{:S(2)}, u32[]{:S(2)}) collective-permute-start(bf16[128,1024]{1,0:T(8,128)(2,1)} %get-tuple-element.187), channel_id=1, source_target_pairs={{0,24},{4,28},{8,16},{12,20},{16,8},{20,12},{24,0},{28,4},{1,25},{... | collective-permute-start | bytes 786440 | tf_op jit(solution)/shard_map/ppermute | solution.py:459
  188.8 2.7 %collective-permute-start.31 = (bf16[80,256]{1,0:T(8,128)(2,1)S(1)}, bf16[80,256]{1,0:T(8,128)(2,1)S(1)}, u32[]{:S(2)}, u32[]{:S(2)}) collective-permute-start(bf16[80,256]{1,0:T(8,128)(2,1)S(1)} %get-tuple-element.207), channel_id=1, source_target_pairs={{0,16},{4,20},{8,24},{12,28},{16,0},{20,4},{24,8},{28,12},{1,17},{... | collective-permute-start | bytes 122888 | tf_op jit(solution)/shard_map/ppermute | solution.py:459
  191.5 1.6 collective-permute-start.32
  193.1 1.8 collective-permute-done.37.refs_3_
  194.9 2.2 %add_parts.1 = f32[128,1024]{1,0:T(8,128)} custom-call(f32[128,1024]{1,0:T(8,128)} %get-tuple-element.184.refs_0_, bf16[128,1024]{1,0:T(8,128)(2,1)} %collective-permute-done.29.refs_1_, f32[128,1024]{1,0:T(8,128)} %collective-permute-done.36.refs_2_, bf16[128,1024]{1,0:T(8,128)(2,1)} %collective-permute-done.37.refs_3_), custom_call_target="tpu_custom_call" | custom-call | flops 1000 | bytes 2000 | tf_op jit(solution)/shard_map/add_parts/pallas_call | solution.py:327
  197.1 4.2 %collective-permute-done.31 = bf16[80,256]{1,0:T(8,128)(2,1)S(1)} collective-permute-done((bf16[80,256]{1,0:T(8,128)(2,1)S(1)}, bf16[80,256]{1,0:T(8,128)(2,1)S(1)}, u32[]{:S(2)}, u32[]{:S(2)}) %collective-permute-start.31) | collective-permute-done | bytes 40992 | tf_op jit(solution)/shard_map/ppermute | solution.py:459
  202.7 2.2 %collective-permute-start.35 = (bf16[80,1024]{1,0:T(8,128)(2,1)S(1)}, bf16[80,1024]{1,0:T(8,128)(2,1)S(1)}, u32[]{:S(2)}, u32[]{:S(2)}) collective-permute-start(bf16[80,1024]{1,0:T(8,128)(2,1)S(1)} %constant_dynamic-update-slice_fusion.4), channel_id=1, source_target_pairs={{0,6},{1,7},{2,4},{3,5},{4,2},{5,3},{6,0},{7,1},{8,14},{9,15},{10,... | collective-permute-start | bytes 491528 | tf_op jit(solution)/shard_map/ppermute | solution.py:531
  207.0 5.5 %layer_output.1 = bf16[864,1024]{1,0:T(8,128)(2,1)} custom-call(s32[6,3]{1,0:T(8,128)} %copy.33.cnt_ref, bf16[864,1024]{1,0:T(8,128)(2,1)} %copy-done.1, bf16[864,1024]{1,0:T(8,128)(2,1)} %bitcast.24, bf16[1728,1024]{1,0:T(8,128)(2,1)} %get-tuple-element.129.refs_0_, bf16[1728,1024]{1,0:T(8,128)(2,1)} %get-tuple-element.160.refs_1_, ...), custom_call_target="tpu_custom_call" | custom-call | flops 5000000 | bytes 10000 | tf_op jit(solution)/shard_map/layer_output/pallas_call | solution.py:445
  215.0 1.8 maximum_convert_fusion
  (130 shorter events, 43.7 us)
Async XLA Ops:
  2.9 14.7 %collective-permute-start.1 = (bf16[128,1024]{1,0:T(8,128)(2,1)S(1)}, bf16[128,1024]{1,0:T(8,128)(2,1)S(1)}, u32[]{:S(2)}, u32[]{:S(2)}) collective-permute-start(bf16[128,1024]{1,0:T(8,128)(2,1)S(1)} %pad_maximum_fusion.1.refs_2_), channel_id=1, source_target_pairs={{0,2},{1,3},{2,0},{3,1},{4,6},{5,7},{6,4},{7,5},{8,10},{9,11},{10,... | collective-permute-start | bytes 786440 | tf_op jit(solution)/shard_map/ppermute | solution.py:459
  5.9 18.7 %collective-permute-start.2 = (bf16[128,1024]{1,0:T(8,128)(2,1)S(1)}, bf16[128,1024]{1,0:T(8,128)(2,1)S(1)}, u32[]{:S(2)}, u32[]{:S(2)}) collective-permute-start(bf16[128,1024]{1,0:T(8,128)(2,1)S(1)} %pad_maximum_fusion.1.refs_2_), channel_id=1, source_target_pairs={{0,10},{1,11},{2,8},{3,9},{8,18},{9,19},{10,16},{11,17},{16,26},{1... | collective-permute-start | bytes 786440 | tf_op jit(solution)/shard_map/ppermute | solution.py:478
  7.4 10.1 %collective-permute-start = (s32[6,3]{0,1:T(4,128)}, s32[6,3]{0,1:T(4,128)S(1)}, u32[]{:S(2)}, u32[]{:S(2)}) collective-permute-start(s32[6,3]{0,1:T(4,128)} %param.13), channel_id=1, source_target_pairs={{0,1},{1,0},{2,3},{3,2},{4,5},{5,4},{6,7},{7,6},{8,9},{9,8},{10,11... | collective-permute-start | bytes 224 | tf_op jit(solution)/shard_map/ppermute | solution.py:459
  25.3 8.9 %collective-permute-start.5 = (bf16[2,864,1024]{2,1,0:T(8,128)(2,1)}, bf16[2,864,1024]{2,1,0:T(8,128)(2,1)S(1)}, u32[]{:S(2)}, u32[]{:S(2)}) collective-permute-start(bf16[2,864,1024]{2,1,0:T(8,128)(2,1)} %bitcast.17), channel_id=1, source_target_pairs={{0,1},{1,0},{2,3},{3,2},{4,5},{5,4},{6,7},{7,6},{8,9},{9,8},{10,11... | collective-permute-start | bytes 10616840 | tf_op jit(solution)/shard_map/ppermute | solution.py:459
  25.4 8.9 %collective-permute-start.3 = (bf16[128,1024]{1,0:T(8,128)(2,1)}, bf16[128,1024]{1,0:T(8,128)(2,1)S(1)}, u32[]{:S(2)}, u32[]{:S(2)}) collective-permute-start(bf16[128,1024]{1,0:T(8,128)(2,1)} %copy-done.18), channel_id=1, source_target_pairs={{0,8},{8,16},{16,24},{24,28},{28,20},{20,12},{12,4},{4,0},{1,9},{9... | collective-permute-start | bytes 786440 | tf_op jit(solution)/shard_map/ppermute | solution.py:482
  25.4 8.9 %collective-permute-start.4 = (bf16[128,1024]{1,0:T(8,128)(2,1)}, bf16[128,1024]{1,0:T(8,128)(2,1)S(1)}, u32[]{:S(2)}, u32[]{:S(2)}) collective-permute-start(bf16[128,1024]{1,0:T(8,128)(2,1)} %copy-done.17), channel_id=1, source_target_pairs={{8,0},{16,8},{24,16},{28,24},{20,28},{12,20},{4,12},{0,4},{9,1},{1... | collective-permute-start | bytes 786440 | tf_op jit(solution)/shard_map/ppermute | solution.py:484
  27.4 10.5 %collective-permute-start.8 = (bf16[128,1024]{1,0:T(8,128)(2,1)}, bf16[128,1024]{1,0:T(8,128)(2,1)S(1)}, u32[]{:S(2)}, u32[]{:S(2)}) collective-permute-start(bf16[128,1024]{1,0:T(8,128)(2,1)} %copy-done.18), channel_id=1, source_target_pairs={{0,2},{1,3},{2,0},{3,1},{4,6},{5,7},{6,4},{7,5},{8,10},{9,11},{10,... | collective-permute-start | bytes 786440 | tf_op jit(solution)/shard_map/ppermute | solution.py:459
  35.1 8.4 %collective-permute-start.7 = (bf16[128,1024]{1,0:T(8,128)(2,1)S(1)}, bf16[128,1024]{1,0:T(8,128)(2,1)S(1)}, u32[]{:S(2)}, u32[]{:S(2)}) collective-permute-start(bf16[128,1024]{1,0:T(8,128)(2,1)S(1)} %collective-permute-done.4.refs_5_), channel_id=1, source_target_pairs={{8,0},{16,8},{24,16},{28,24},{20,28},{12,20},{4,12},{0,4},{9,1},{1... | collective-permute-start | bytes 786440 | tf_op jit(solution)/shard_map/ppermute | solution.py:484
  36.4 9.1 %collective-permute-start.11 = (bf16[128,1024]{1,0:T(8,128)(2,1)S(1)}, bf16[128,1024]{1,0:T(8,128)(2,1)S(1)}, u32[]{:S(2)}, u32[]{:S(2)}) collective-permute-start(bf16[128,1024]{1,0:T(8,128)(2,1)S(1)} %collective-permute-done.3.refs_2_), channel_id=1, source_target_pairs={{0,2},{1,3},{2,0},{3,1},{4,6},{5,7},{6,4},{7,5},{8,10},{9,11},{10,... | collective-permute-start | bytes 786440 | tf_op jit(solution)/shard_map/ppermute | solution.py:459
  51.9 28.9 %collective-permute-start.14 = (bf16[384,1024]{1,0:T(8,128)(2,1)}, bf16[384,1024]{1,0:T(8,128)(2,1)}, u32[]{:S(2)}, u32[]{:S(2)}) collective-permute-start(bf16[384,1024]{1,0:T(8,128)(2,1)} %pad_maximum_fusion), channel_id=1, source_target_pairs={{0,2},{1,3},{2,0},{3,1},{4,6},{5,7},{6,4},{7,5},{8,10},{9,11},{10,... | collective-permute-start | bytes 2359304 | tf_op jit(solution)/shard_map/ppermute | solution.py:459
  53.4 25.4 %collective-permute-start.12 = (bf16[128,1024]{1,0:T(8,128)(2,1)}, bf16[128,1024]{1,0:T(8,128)(2,1)}, u32[]{:S(2)}, u32[]{:S(2)}) collective-permute-start(bf16[128,1024]{1,0:T(8,128)(2,1)} %collective-permute-done.6.refs_3_), channel_id=1, source_target_pairs={{0,2},{1,3},{2,0},{3,1},{4,6},{5,7},{6,4},{7,5},{8,10},{9,11},{10,... | collective-permute-start | bytes 786440 | tf_op jit(solution)/shard_map/ppermute | solution.py:459
  53.9 26.9 %collective-permute-start.13 = (bf16[128,1024]{1,0:T(8,128)(2,1)}, bf16[128,1024]{1,0:T(8,128)(2,1)}, u32[]{:S(2)}, u32[]{:S(2)}) collective-permute-start(bf16[128,1024]{1,0:T(8,128)(2,1)} %collective-permute-done.9.refs_4_), channel_id=1, source_target_pairs={{0,2},{1,3},{2,0},{3,1},{4,6},{5,7},{6,4},{7,5},{8,10},{9,11},{10,... | collective-permute-start | bytes 786440 | tf_op jit(solution)/shard_map/ppermute | solution.py:459
  80.8 33.7 %collective-permute-start.15 = (bf16[512,1024]{1,0:T(8,128)(2,1)}, bf16[512,1024]{1,0:T(8,128)(2,1)S(1)}, u32[]{:S(2)}, u32[]{:S(2)}) collective-permute-start(bf16[512,1024]{1,0:T(8,128)(2,1)} %get-tuple-element.143), channel_id=1, source_target_pairs={{0,2},{1,3},{2,0},{3,1},{4,6},{5,7},{6,4},{7,5},{8,10},{9,11},{10,... | collective-permute-start | bytes 3145736 | tf_op jit(solution)/shard_map/ppermute | solution.py:459
  82.3 32.2 %collective-permute-start.16 = (bf16[512,512]{1,0:T(8,128)(2,1)}, bf16[512,512]{1,0:T(8,128)(2,1)S(1)}, u32[]{:S(2)}, u32[]{:S(2)}) collective-permute-start(bf16[512,512]{1,0:T(8,128)(2,1)} %get-tuple-element.144), channel_id=1, source_target_pairs={{0,2},{1,3},{2,0},{3,1},{4,6},{5,7},{6,4},{7,5},{8,10},{9,11},{10,... | collective-permute-start | bytes 1572872 | tf_op jit(solution)/shard_map/ppermute | solution.py:459
  114.6 15.7 %collective-permute-start.18 = (bf16[512,512]{1,0:T(8,128)(2,1)}, bf16[512,512]{1,0:T(8,128)(2,1)S(1)}, u32[]{:S(2)}, u32[]{:S(2)}) collective-permute-start(bf16[512,512]{1,0:T(8,128)(2,1)} %get-tuple-element.152), channel_id=1, source_target_pairs={{0,2},{1,3},{2,0},{3,1},{4,6},{5,7},{6,4},{7,5},{8,10},{9,11},{10,... | collective-permute-start | bytes 1572872 | tf_op jit(solution)/shard_map/ppermute | solution.py:459
  119.1 26.2 %collective-permute-start.24 = (bf16[512,1024]{1,0:T(8,128)(2,1)}, bf16[512,1024]{1,0:T(8,128)(2,1)S(1)}, u32[]{:S(2)}, u32[]{:S(2)}) collective-permute-start(bf16[512,1024]{1,0:T(8,128)(2,1)} %add_convert_fusion), channel_id=1, source_target_pairs={{0,4},{4,0},{8,12},{12,8},{16,20},{20,16},{24,28},{28,24},{1,5},{5... | collective-permute-start | bytes 3145736 | tf_op jit(solution)/shard_map/ppermute | solution.py:459
  137.4 21.4 %collective-permute-start.21 = (f32[80,1024]{1,0:T(8,128)}, f32[80,1024]{1,0:T(8,128)}, u32[]{:S(2)}, u32[]{:S(2)}) collective-permute-start(f32[80,1024]{1,0:T(8,128)} %get-tuple-element.157), channel_id=1, source_target_pairs={{0,4},{4,0},{8,12},{12,8},{16,20},{20,16},{24,28},{28,24},{1,5},{5... | collective-permute-start | bytes 983048 | tf_op jit(solution)/shard_map/ppermute | solution.py:459
  138.2 20.5 %collective-permute-start.22 = (f32[80,1024]{1,0:T(8,128)}, f32[80,1024]{1,0:T(8,128)}, u32[]{:S(2)}, u32[]{:S(2)}) collective-permute-start(f32[80,1024]{1,0:T(8,128)} %get-tuple-element.158), channel_id=1, source_target_pairs={{0,2},{1,3},{2,0},{3,1},{4,6},{5,7},{6,4},{7,5},{8,10},{9,11},{10,... | collective-permute-start | bytes 983048 | tf_op jit(solution)/shard_map/ppermute | solution.py:531
  138.9 19.9 %collective-permute-start.23 = (f32[80,1024]{1,0:T(8,128)}, f32[80,1024]{1,0:T(8,128)S(1)}, u32[]{:S(2)}, u32[]{:S(2)}) collective-permute-start(f32[80,1024]{1,0:T(8,128)} %get-tuple-element.159), channel_id=1, source_target_pairs={{0,6},{1,7},{2,4},{3,5},{4,2},{5,3},{6,0},{7,1},{8,14},{9,15},{10,... | collective-permute-start | bytes 983048 | tf_op jit(solution)/shard_map/ppermute | solution.py:531
  159.5 27.8 %collective-permute-start.28 = (bf16[864,1024]{1,0:T(8,128)(2,1)S(1)}, bf16[864,1024]{1,0:T(8,128)(2,1)S(1)}, u32[]{:S(2)}, u32[]{:S(2)}) collective-permute-start(bf16[864,1024]{1,0:T(8,128)(2,1)S(1)} %copy-done.2), channel_id=1, source_target_pairs={{0,1},{1,0},{2,3},{3,2},{4,5},{5,4},{6,7},{7,6},{8,9},{9,8},{10,11... | collective-permute-start | bytes 5308424 | tf_op jit(solution)/shard_map/ppermute | solution.py:459
  159.5 16.0 %collective-permute-start.29 = (bf16[128,1024]{1,0:T(8,128)(2,1)}, bf16[128,1024]{1,0:T(8,128)(2,1)}, u32[]{:S(2)}, u32[]{:S(2)}) collective-permute-start(bf16[128,1024]{1,0:T(8,128)(2,1)} %get-tuple-element.179), channel_id=1, source_target_pairs={{0,16},{4,20},{8,24},{12,28},{16,0},{20,4},{24,8},{28,12},{1,17},{... | collective-permute-start | bytes 786440 | tf_op jit(solution)/shard_map/ppermute | solution.py:459
  162.0 32.9 %collective-permute-start.36 = (f32[128,1024]{1,0:T(8,128)}, f32[128,1024]{1,0:T(8,128)}, u32[]{:S(2)}, u32[]{:S(2)}) collective-permute-start(f32[128,1024]{1,0:T(8,128)} %get-tuple-element.186), channel_id=1, source_target_pairs={{0,8},{4,12},{8,0},{12,4},{16,24},{20,28},{24,16},{28,20},{1,9},{5... | collective-permute-start | bytes 1572872 | tf_op jit(solution)/shard_map/ppermute | solution.py:459
  166.1 18.1 %collective-permute-start.25 = (f32[80,256]{1,0:T(8,128)}, f32[80,256]{1,0:T(8,128)}, u32[]{:S(2)}, u32[]{:S(2)}) collective-permute-start(f32[80,256]{1,0:T(8,128)} %get-tuple-element.212), channel_id=1, source_target_pairs={{0,8},{4,12},{8,0},{12,4},{16,24},{20,28},{24,16},{28,20},{1,9},{5... | collective-permute-start | bytes 245768 | tf_op jit(solution)/shard_map/ppermute | solution.py:459
  166.8 20.3 %collective-permute-start.26 = (f32[80,256]{1,0:T(8,128)}, f32[80,256]{1,0:T(8,128)}, u32[]{:S(2)}, u32[]{:S(2)}) collective-permute-start(f32[80,256]{1,0:T(8,128)} %get-tuple-element.211), channel_id=1, source_target_pairs={{0,16},{4,20},{8,24},{12,28},{16,0},{20,4},{24,8},{28,12},{1,17},{... | collective-permute-start | bytes 245768 | tf_op jit(solution)/shard_map/ppermute | solution.py:459
  175.5 11.7 %collective-permute-start.27 = (f32[80,256]{1,0:T(8,128)}, f32[80,256]{1,0:T(8,128)}, u32[]{:S(2)}, u32[]{:S(2)}) collective-permute-start(f32[80,256]{1,0:T(8,128)} %get-tuple-element.210), channel_id=1, source_target_pairs={{0,24},{4,28},{8,16},{12,20},{16,8},{20,12},{24,0},{28,4},{1,25},{... | collective-permute-start | bytes 245768 | tf_op jit(solution)/shard_map/ppermute | solution.py:459
  184.2 10.7 %collective-permute-start.37 = (bf16[128,1024]{1,0:T(8,128)(2,1)}, bf16[128,1024]{1,0:T(8,128)(2,1)}, u32[]{:S(2)}, u32[]{:S(2)}) collective-permute-start(bf16[128,1024]{1,0:T(8,128)(2,1)} %get-tuple-element.187), channel_id=1, source_target_pairs={{0,24},{4,28},{8,16},{12,20},{16,8},{20,12},{24,0},{28,4},{1,25},{... | collective-permute-start | bytes 786440 | tf_op jit(solution)/shard_map/ppermute | solution.py:459
  188.7 8.5 %collective-permute-start.30 = (bf16[80,256]{1,0:T(8,128)(2,1)S(1)}, bf16[80,256]{1,0:T(8,128)(2,1)S(1)}, u32[]{:S(2)}, u32[]{:S(2)}) collective-permute-start(bf16[80,256]{1,0:T(8,128)(2,1)S(1)} %get-tuple-element.207), channel_id=1, source_target_pairs={{0,8},{4,12},{8,0},{12,4},{16,24},{20,28},{24,16},{28,20},{1,9},{5... | collective-permute-start | bytes 122888 | tf_op jit(solution)/shard_map/ppermute | solution.py:459
  188.8 12.5 %collective-permute-start.31 = (bf16[80,256]{1,0:T(8,128)(2,1)S(1)}, bf16[80,256]{1,0:T(8,128)(2,1)S(1)}, u32[]{:S(2)}, u32[]{:S(2)}) collective-permute-start(bf16[80,256]{1,0:T(8,128)(2,1)S(1)} %get-tuple-element.207), channel_id=1, source_target_pairs={{0,16},{4,20},{8,24},{12,28},{16,0},{20,4},{24,8},{28,12},{1,17},{... | collective-permute-start | bytes 122888 | tf_op jit(solution)/shard_map/ppermute | solution.py:459
  191.5 9.8 %collective-permute-start.32 = (bf16[80,256]{1,0:T(8,128)(2,1)S(1)}, bf16[80,256]{1,0:T(8,128)(2,1)S(1)}, u32[]{:S(2)}, u32[]{:S(2)}) collective-permute-start(bf16[80,256]{1,0:T(8,128)(2,1)S(1)} %get-tuple-element.207), channel_id=1, source_target_pairs={{0,24},{4,28},{8,16},{12,20},{16,8},{20,12},{24,0},{28,4},{1,25},{... | collective-permute-start | bytes 122888 | tf_op jit(solution)/shard_map/ppermute | solution.py:459
  201.4 11.2 %collective-permute-start.33 = (bf16[80,1024]{1,0:T(8,128)(2,1)S(1)}, bf16[80,1024]{1,0:T(8,128)(2,1)S(1)}, u32[]{:S(2)}, u32[]{:S(2)}) collective-permute-start(bf16[80,1024]{1,0:T(8,128)(2,1)S(1)} %constant_dynamic-update-slice_fusion.4), channel_id=1, source_target_pairs={{0,4},{4,0},{8,12},{12,8},{16,20},{20,16},{24,28},{28,24},{1,5},{5... | collective-permute-start | bytes 491528 | tf_op jit(solution)/shard_map/ppermute | solution.py:459
  202.2 10.5 %collective-permute-start.34 = (bf16[80,1024]{1,0:T(8,128)(2,1)S(1)}, bf16[80,1024]{1,0:T(8,128)(2,1)S(1)}, u32[]{:S(2)}, u32[]{:S(2)}) collective-permute-start(bf16[80,1024]{1,0:T(8,128)(2,1)S(1)} %constant_dynamic-update-slice_fusion.4), channel_id=1, source_target_pairs={{0,2},{1,3},{2,0},{3,1},{4,6},{5,7},{6,4},{7,5},{8,10},{9,11},{10,... | collective-permute-start | bytes 491528 | tf_op jit(solution)/shard_map/ppermute | solution.py:531
  202.7 9.9 %collective-permute-start.35 = (bf16[80,1024]{1,0:T(8,128)(2,1)S(1)}, bf16[80,1024]{1,0:T(8,128)(2,1)S(1)}, u32[]{:S(2)}, u32[]{:S(2)}) collective-permute-start(bf16[80,1024]{1,0:T(8,128)(2,1)S(1)} %constant_dynamic-update-slice_fusion.4), channel_id=1, source_target_pairs={{0,6},{1,7},{2,4},{3,5},{4,2},{5,3},{6,0},{7,1},{8,14},{9,15},{10,... | collective-permute-start | bytes 491528 | tf_op jit(solution)/shard_map/ppermute | solution.py:531
  (29 other events, 215.4 us)

commit v12 on v11

--- a/solution.py
+++ b/solution.py
@@ -130,7 +130,7 @@
     earlier, refs = refs[: 2 * (packs or 0)], refs[2 * (packs or 0) :]
     blocks, refs = refs[:blocks], refs[blocks:]
     out_ref, w_ref, *refs = refs
-    keeps, other_ref, refs = refs[:2], refs[2], refs[3:]
+    keeps, others, refs = refs[:2], refs[2:4], refs[4:]
     n_s, g_s, qkv, total = refs[-4:]
     half, step = pl.program_id(0), pl.program_id(1)
     rows = n_s.shape[0]
@@ -215,7 +215,7 @@
             for c in range(2):
                 cols = slice(c * 2 * width, (c + 1) * 2 * width)
                 keeps[c][at, :] = total[pl.ds(mine, size), cols].astype(keeps[c].dtype)
-            other_ref[at, :] = total[pl.ds(other, size), :].astype(other_ref.dtype)
+                others[c][at, :] = total[pl.ds(other, size), cols].astype(others[c].dtype)
 
     if packs is not None:
         back = dot_nt(out_ref[:, : 3 * width], w_ref[:, : 3 * width])
@@ -255,7 +255,7 @@
     packs = None if earlier is None else len(earlier[0])
     back = [] if earlier is None else two_halves(rows, steps, ())
     kind = BF16 if earlier is None else F32
-    grads = [jax.ShapeDtypeStruct((D // 2, c), kind) for c in (cols // 2, cols // 2, cols)]
+    grads = [jax.ShapeDtypeStruct((D // 2, c), kind) for c in [cols // 2] * 4]
     return pl.pallas_call(
         functools.partial(attention_kernel, packs, len(blocks), dp),
         grid=(2, steps),
@@ -470,13 +470,6 @@
         self.forward = [(order[i], order[(i + 1) % size]) for i in range(size)]
         self.backward = [(order[(i + 1) % size], order[i]) for i in range(size)]
         self.ahead, self.behind = [x], [x]
-
-    @classmethod
-    def across(cls, x, axis, size, other, other_size, bit):
-        ring = cls(swap(x, other, other_size, bit), axis, size)
-        both = [(s * other_size + g, t * other_size + (g ^ bit)) for s, t in ring.forward for g in range(other_size)]
-        ring.ahead.append(lax.ppermute(x, (axis, other), both))
-        return ring
 
     def send(self):
         moved = [lax.ppermute(self.ahead[-1], self.axis, self.forward)]
@@ -591,8 +584,7 @@
 
     shard = jnp.concatenate([w_qkv.reshape(w_qkv.shape[0], 3 * width), w_out.T], axis=1)
     cross = lambda x, f: swap(x, "group", group, 2 * f)
-    rings = [Ring.across(shard, "dp", dp, "group", group, 2 * f) for f in fars]
-    ring = rings[0]
+    far_shards = [cross(shard, f) for f in fars]
     counts = vis_count.astype(jnp.int32)
     counts_far = swap(counts, "group", group, 1)
     table, genc = encoding_tables(patches.shape[1])
@@ -607,20 +599,22 @@
         jnp.asarray(genc),
         out_grad.reshape(scenes, TOK, D),
     )
-    moved = [(r.ahead, r.behind) for r in rings]
+    stem, both_counts, far_shards = together(stem, jnp.stack([counts, counts_far]), far_shards)
+    rings = [Ring(x, "dp", dp) for x in far_shards]
+    ring = rings[0]
     owners = ring.owners(dp // 2 + 1, dp // 2)
-    stem, both_counts, owners, moved = together(stem, jnp.stack([counts, counts_far]), owners, moved)
-    for r, (ahead, behind) in zip(rings, moved):
-        r.ahead, r.behind = list(ahead), list(behind)
     emb = stem[0].reshape(tokens, D)
     both = [stem[1].reshape(2, tokens, D)]
     cols = stem[2].reshape(tokens, stem[2].shape[2])
     both.append(swap(both[0], "group", group, 1))
-    passed = [cross(ring.ahead[-1], 1)]
-    (both,) = step_all(rings, both)
+    passed = []
+    both, owners = step_all(rings, both, owners)
     while ring.steps < dp // 2:
         passed.append(cross(ring.ahead[-1], 1))
-        (passed[-2],) = step_all(rings, passed[-2])
+        if len(passed) > 1:
+            (passed[-2],) = step_all(rings, passed[-2])
+        else:
+            step_all(rings)
     ring.ahead, ring.behind = together(ring.ahead, ring.behind)
     passed.append(cross(ring.ahead[-1], 1))
     passed.append(cross(jnp.concatenate(ring.behind[1:], axis=0), 1))
@@ -637,39 +631,53 @@
         elif f:
             made = together(*made)
         else:
-            made, arrived = together(made, [x[:2] for x in crossing])
-        pack, weight, keep, other, back = made[0], made[1], made[2:4], made[4], made[5:]
+            made, arrived = together(made, [x[:3] for x in crossing])
+        pack, weight, keep, other, back = made[0], made[1], made[2:4], made[4:6], made[6:]
         packs.append(pack)
         weights.append(weight)
         if f:
-            crossing.append([cross(x, f) for x in (other, *keep)])
+            crossing.append([cross(x, f) for x in (*other, *keep)])
     back_far = swap(back[1], "group", group, 1)
-    for x in arrived:
-        other = other + x[0].astype(F32)
-    coming = swap(other.astype(BF16), "dp", dp, 1)
-    stem_made, last_keeps = together(
-        tail_call(core, back[0], back_far, emb, both[0], cols, gain), [x[2] for x in crossing]
+    coming = []
+    for c in range(2):
+        send = other[c]
+        for x in arrived:
+            send = send + x[c].astype(F32)
+        coming.append(swap(send.astype(BF16), "dp", dp, 1))
+    stem_made, coming[0], last_keeps = together(
+        tail_call(core, back[0], back_far, emb, both[0], cols, gain), coming[0], [x[3] for x in crossing]
     )
-    keeps = [list(keep)] + [[x[1], y] for x, y in zip(arrived, last_keeps)]
+    keeps = [[keep[0]] + [x[2] for x in arrived], [keep[1]] + list(last_keeps)]
     stem_keep, *stem_recv = stem_made
     stem_recv = [swap(x, "group", group, 1) for x in stem_recv]
+    kinds = [F32 if j < 2 else BF16 for j in range(dp // 2)]
+    second_leg = lambda c: combine_call(high, [[x] for x in keeps[c] + [coming[c]]], kinds)
+    spread = lambda blocks, js: [swap(blocks[j], "dp", dp, 2 * j) for j in js]
+    first = second_leg(0)
+    stem_recv, share = together(stem_recv, first[0])
+    first_rest = spread(first, rests[1:])
     stem_parts = halve_stem(stem_recv, stem_keep, group)
-    _, coming, keeps = together(stem_parts, coming, keeps)
-    kinds = [F32 if j < 2 else BF16 for j in range(dp // 2)]
-    blocks = combine_call(high, keeps + [[coming]], kinds)
-    landing = [blocks[0]] + [swap(blocks[j], "dp", dp, 2 * j) for j in rests]
+    _, coming[1], keeps[1] = together(stem_parts, coming[1], keeps[1])
+    second = second_leg(1)
     near = dp // 2 * 3 // 4
-
-    def after(mixed, share):
-        return [swap(mixed, "group", group, 1), share] + landing[2:near]
-
-    def last(mixed, *arrived):
+    beside = [
+        mixed_call(packs, weights),
+        [share, *first_rest],
+        [second[0], *spread(second, range(2, near))],
+    ]
+
+    def after(mixed, first, second):
+        return [swap(mixed, "group", group, 1), first, [*second, *spread(blocks[1], range(near, dp // 2))]]
+
+    def last(mixed, first, second):
         output = output_call(counts, mixed, emb, packs, weights)
-        total = add_call(list(arrived) + [landing[1]] + landing[near:])
-        return output, total[:, : 3 * width].reshape(total.shape[0], 3, width), total[:, 3 * width :].T
-
+        first, second = [add_call([*x, *spread(b, [1])]) for x, b in zip((first, second), blocks)]
+        qkv = jnp.concatenate([first, second[:, :width]], axis=1)
+        return output, qkv.reshape(qkv.shape[0], 3, width), second[:, width:].T
+
+    blocks = (first, second)
     grad_w_stem, (output, grad_w_qkv, grad_w_out) = sum_stem(
-        stem_parts, [mixed_call(packs, weights), landing[0]], after, last, dp, group
+        stem_parts, beside, after, last, dp, group
     )
     return (output.reshape(scenes, GROUPS, CAP, D), grad_w_stem, grad_w_qkv, grad_w_out)
 

time: 217 us -> 209 us (0.963)
  waiting for transfers between devices: 58.2 us -> 51.6 us
  starting transfers between devices: 45.1 us -> 41.7 us
  Pallas kernels: 89.2 us -> 92.5 us
    ppermute x3 -> x4, waiting for transfers between devices: 10.2 us -> 19.7 us  [send(): moved = [lax.ppermute(self.ahead[-1], self.axis, self.forward)]]
    ppermute x28 -> x33, waiting for transfers between devices: 34.8 us -> 27.6 us  [swap(): return lax.ppermute(x, axis, [(i, i ^ bit) for i in range(size)])]
    ppermute x1 -> x0, waiting for transfers between devices: 6.99 us -> none  [across(): ring.ahead.append(lax.ppermute(x, (axis, other), both))]
    ppermute x3 -> x4, starting transfers between devices: 2.24 us -> 6.25 us  [send(): moved = [lax.ppermute(self.ahead[-1], self.axis, self.forward)]]
    ppermute x3, starting transfers between devices: 3.89 us -> 1.35 us  [send(): moved.append(lax.ppermute(self.behind[-1], self.axis, self.backward))]
    ppermute x28 -> x33, starting transfers between devices: 32 us -> 30.4 us  [swap(): return lax.ppermute(x, axis, [(i, i ^ bit) for i in range(size)])]
    pallas_call x2 -> x3, Pallas kernels: 6.48 us -> 7.83 us  [combine_call(): pl.pallas_call(functools.partial(combine_kernel, [len(part) for part in p...]
    unnamed x49 -> x61, local copies, waits for them, and re-layouts: 10.3 us -> 11.1 us
  transfers between devices with their start and end apart: 39 -> 44, of which waited for: 17 -> 20; matrix products, arithmetic and copies ran while one was open for 6% -> 5% of each run, Pallas kernels for 41% -> 44%
where the time goes in v12:
time: 209 us
  Pallas kernels  92.5 us (44%)
  waiting for transfers between devices  51.6 us (25%)
  starting transfers between devices  41.7 us (20%)
  local copies, waits for them, and re-layouts  13.3 us (6%)
  other arithmetic  8.63 us (4%)
    pallas_call x2, Pallas kernels, attention_call(): pl.pallas_call(functools.partial(attention_kernel, packs, len(blocks), dp...  54.4 us
    ppermute x33, starting transfers between devices, swap(): return lax.ppermute(x, axis, [(i, i ^ bit) for i in range(size)])  30.4 us
    ppermute x33, waiting for transfers between devices, swap(): return lax.ppermute(x, axis, [(i, i ^ bit) for i in range(size)])  27.6 us
    ppermute x4, waiting for transfers between devices, send(): moved = [lax.ppermute(self.ahead[-1], self.axis, self.forward)]  19.7 us
    unnamed x61, local copies, waits for them, and re-layouts  11.1 us
    pallas_call x1, Pallas kernels, tail_call(): pl.pallas_call(tail_kernel, grid=(tokens // rows,), in_specs=[SCALARS, pe...  9.05 us
    pallas_call x1, Pallas kernels, stem_call(): pl.pallas_call(stem_kernel, grid=(scenes // block,), in_specs=[whole(coun...  8.2 us
    pallas_call x3, Pallas kernels, combine_call(): pl.pallas_call(functools.partial(combine_kernel, [len(part) for part in p...  7.83 us
  transfers between devices with their start and end apart: 44, of which 20 were waited for; matrix products, arithmetic and copies ran while one was open for 5% of the time, Pallas kernels for 44%

profile of v12, /device:TPU:0, one launch (start us, length us, event | category | flops | bytes accessed | tf_op | source)
XLA Modules:
  0.0 208.8 jit_solution(3318155568634687357)
XLA Ops:
  2.9 3.0 %collective-permute-start.1 = (bf16[128,1024]{1,0:T(8,128)(2,1)S(1)}, bf16[128,1024]{1,0:T(8,128)(2,1)S(1)}, u32[]{:S(2)}, u32[]{:S(2)}) collective-permute-start(bf16[128,1024]{1,0:T(8,128)(2,1)S(1)} %pad_maximum_fusion.2.refs_2_), channel_id=1, source_target_pairs={{0,2},{1,3},{2,0},{3,1},{4,6},{5,7},{6,4},{7,5},{8,10},{9,11},{10,... | collective-permute-start | bytes 786440 | tf_op jit(solution)/shard_map/ppermute | solution.py:459
  7.2 8.2 %stem_norm.1 = (bf16[6,144,1024]{2,1,0:T(8,128)(2,1)}, bf16[2,6,144,1024]{3,2,1,0:T(8,128)(2,1)}, bf16[6,144,256]{2,1,0:T(8,128)(2,1)}) custom-call(s32[6,3]{1,0:T(8,128)} %copy.33.cnt_ref, s32[6,3,48]{2,1,0:T(4,128)} %idx_ref.1, bf16[6,144,640]{2,1,0:T(8,128)(2,1)} %patch_ref.1, bf16[640,1024]{1,0:T(8,128)(2,1)} %w_ref.1, f32[1,1024]{1,0:T(1,128)} %bitcast.31, ...), custom_call_target="tpu_custom_call" | custom-call | flops 8000000 | bytes 12000 | tf_op jit(solution)/shard_map/stem_norm/pallas_call | solution.py:98
  19.3 5.9 %collective-permute-done.2.refs_1_ = bf16[128,1024]{1,0:T(8,128)(2,1)} collective-permute-done((bf16[128,1024]{1,0:T(8,128)(2,1)}, bf16[128,1024]{1,0:T(8,128)(2,1)}, u32[]{:S(2)}, u32[]{:S(2)}) %collective-permute-start.2) | collective-permute-done | bytes 262176 | tf_op jit(solution)/shard_map/ppermute | solution.py:475
  29.1 4.7 %collective-permute-done.5.refs_2_ = bf16[128,1024]{1,0:T(8,128)(2,1)S(1)} collective-permute-done((bf16[128,1024]{1,0:T(8,128)(2,1)}, bf16[128,1024]{1,0:T(8,128)(2,1)S(1)}, u32[]{:S(2)}, u32[]{:S(2)}) %collective-permute-start.5) | collective-permute-done | bytes 262176 | tf_op jit(solution)/shard_map/ppermute | solution.py:475
  37.7 3.9 %collective-permute-done.7.refs_3_ = bf16[128,1024]{1,0:T(8,128)(2,1)} collective-permute-done((bf16[128,1024]{1,0:T(8,128)(2,1)S(1)}, bf16[128,1024]{1,0:T(8,128)(2,1)}, u32[]{:S(2)}, u32[]{:S(2)}) %collective-permute-start.7) | collective-permute-done | bytes 262176 | tf_op jit(solution)/shard_map/ppermute | solution.py:475
  44.6 5.2 %collective-permute-done.10.refs_4_ = bf16[128,1024]{1,0:T(8,128)(2,1)} collective-permute-done((bf16[128,1024]{1,0:T(8,128)(2,1)}, bf16[128,1024]{1,0:T(8,128)(2,1)}, u32[]{:S(2)}, u32[]{:S(2)}) %collective-permute-start.10) | collective-permute-done | bytes 262176 | tf_op jit(solution)/shard_map/ppermute | solution.py:475
  49.7 1.9 pad_maximum_fusion
  54.9 22.7 %attention.2 = (bf16[1728,1024]{1,0:T(8,128)(2,1)}, bf16[1024,1024]{1,0:T(8,128)(2,1)}, bf16[512,512]{1,0:T(8,128)(2,1)}, bf16[512,512]{1,0:T(8,128)(2,1)}, bf16...) custom-call(s32[2,6,3]{2,1,0:T(8,128)} %copy.40.cnt_ref, s32[8]{0:T(128)} %compare_select_fusion.2.owner_ref, ...), custom_call_target="tpu_custom_call" | custom-call | flops 20000000 | bytes 14000 | tf_op jit(solution)/shard_map/attention/pallas_call | solution.py:259
  77.6 3.0 %collective-permute-done.13.refs_6_ = bf16[128,1024]{1,0:T(8,128)(2,1)} collective-permute-done((bf16[128,1024]{1,0:T(8,128)(2,1)}, bf16[128,1024]{1,0:T(8,128)(2,1)}, u32[]{:S(2)}, u32[]{:S(2)}) %collective-permute-start.13) | collective-permute-done | bytes 262176 | tf_op jit(solution)/shard_map/ppermute | solution.py:459
  80.6 2.0 collective-permute-start.16
  82.6 31.7 %attention.3 = (bf16[1728,1024]{1,0:T(8,128)(2,1)}, bf16[1024,1024]{1,0:T(8,128)(2,1)}, f32[512,512]{1,0:T(8,128)}, f32[512,512]{1,0:T(8,128)}, f32[512,512]{1,0...) custom-call(s32[2,6,3]{2,1,0:T(8,128)} %copy.40.cnt_ref, ...), custom_call_target="tpu_custom_call" | custom-call | flops 20000000 | bytes 14000 | tf_op jit(solution)/shard_map/attention/pallas_call | solution.py:259
  115.3 2.0 collective-permute-start.20
  117.3 2.2 %add_convert_fusion.1 = bf16[512,512]{1,0:T(8,128)(2,1)} fusion(f32[512,512]{1,0:T(8,128)} %get-tuple-element.172, bf16[512,512]{1,0:T(8,128)(2,1)S(1)} %collective-permute-done.15), kind=kLoop, calls=%fused_computation.2 | loop fusion | flops 786432 | bytes 2097152 | tf_op jit(solution)/shard_map/convert_element_type | solution.py:646
  121.2 9.1 %tail.1 = (f32[320,1024]{1,0:T(8,128)}, f32[320,512]{1,0:T(8,128)}, f32[320,512]{1,0:T(8,128)}) custom-call(s32[1]{0:T(128)} %bitcast.1.core_ref, f32[864,1024]{1,0:T(8,128)} %get-tuple-element.165.own_ref, bf16[864,1024]{1,0:T(8,128)(2,1)} %copy-done.2, bf16[864,1024]{1,0:T(8,128)(2,1)} %bitcast.23, bf16[2,864,1024]{2,1,0:T(8,128)(2,1)} %bitcast.22, ...), custom_call_target="tpu_custom_call" | custom-call | flops 10000000 | bytes 12000 | tf_op jit(solution)/shard_map/tail/pallas_call | solution.py:414
  130.2 3.7 %collective-permute-done.19.refs_2_ = bf16[512,512]{1,0:T(8,128)(2,1)} collective-permute-done((bf16[512,512]{1,0:T(8,128)(2,1)}, bf16[512,512]{1,0:T(8,128)(2,1)}, u32[]{:S(2)}, u32[]{:S(2)}) %collective-permute-start.19) | collective-permute-done | bytes 524320 | tf_op jit(solution)/shard_map/ppermute | solution.py:459
  135.8 2.5 %combine.3 = (f32[128,512]{1,0:T(8,128)}, f32[128,512]{1,0:T(8,128)}, bf16[128,512]{1,0:T(8,128)(2,1)}, bf16[128,512]{1,0:T(8,128)(2,1)}) custom-call(s32[1]{0:T(128)} %bitcast.12.place_ref, f32[512,512]{1,0:T(8,128)} %get-tuple-element.178.refs_0_, bf16[512,512]{1,0:T(8,128)(2,1)} %copy-done.10, bf16[512,512]{1,0:T(8,128)(2,1)} %collective-permute-done.19.refs_2_), custom_call_target="tpu_custom_call" | custom-call | flops 1000 | bytes 5000 | tf_op jit(solution)/shard_map/combine/pallas_call | solution.py:307
  139.4 2.9 %combine.4 = (f32[80,1024]{1,0:T(8,128)}, f32[80,1024]{1,0:T(8,128)}, f32[80,1024]{1,0:T(8,128)}, f32[80,1024]{1,0:T(8,128)}) custom-call(s32[1]{0:T(128)} %bitcast.place_ref, f32[320,1024]{1,0:T(8,128)} %get-tuple-element.175.refs_0_, f32[320,512]{1,0:T(8,128)} %copy-done.7, f32[320,512]{1,0:T(8,128)} %copy-done.8), custom_call_target="tpu_custom_call" | custom-call | flops 1000 | bytes 5000 | tf_op jit(solution)/shard_map/combine/pallas_call | solution.py:307
  147.3 3.1 %collective-permute-done.28.refs_2_ = bf16[512,512]{1,0:T(8,128)(2,1)S(1)} collective-permute-done((bf16[512,512]{1,0:T(8,128)(2,1)}, bf16[512,512]{1,0:T(8,128)(2,1)S(1)}, u32[]{:S(2)}, u32[]{:S(2)}) %collective-permute-start.28) | collective-permute-done | bytes 524320 | tf_op jit(solution)/shard_map/ppermute | solution.py:459
  151.9 2.5 %combine.5 = (f32[128,512]{1,0:T(8,128)}, f32[128,512]{1,0:T(8,128)}, bf16[128,512]{1,0:T(8,128)(2,1)}, bf16[128,512]{1,0:T(8,128)(2,1)}) custom-call(s32[1]{0:T(128)} %bitcast.12.place_ref, f32[512,512]{1,0:T(8,128)} %get-tuple-element.197.refs_0_, bf16[512,512]{1,0:T(8,128)(2,1)} %copy-done.9, bf16[512,512]{1,0:T(8,128)(2,1)} %copy-done.11), custom_call_target="tpu_custom_call" | custom-call | flops 1000 | bytes 5000 | tf_op jit(solution)/shard_map/combine/pallas_call | solution.py:307
  154.4 4.6 %collective-permute-done.26.refs_1_ = bf16[128,512]{1,0:T(8,128)(2,1)S(1)} collective-permute-done((bf16[128,512]{1,0:T(8,128)(2,1)S(1)}, bf16[128,512]{1,0:T(8,128)(2,1)S(1)}, u32[]{:S(2)}, u32[]{:S(2)}) %collective-permute-start.26) | collective-permute-done | bytes 131104 | tf_op jit(solution)/shard_map/ppermute | solution.py:459
  159.0 3.8 %mixed.1 = bf16[864,1024]{1,0:T(8,128)(2,1)} custom-call(bf16[1728,1024]{1,0:T(8,128)(2,1)} %get-tuple-element.147.refs_0_, bf16[1728,1024]{1,0:T(8,128)(2,1)} %get-tuple-element.188.refs_1_, bf16[1024,1024]{1,0:T(8,128)(2,1)} %get-tuple-element.148.refs_1_.refs_2_, bf16[1024,1024]{1,0:T(8,128)(2,1)} %get-tuple-element.189.refs_3_), custom_call_target="tpu_custom_call" | custom-call | flops 2000000 | bytes 5000 | tf_op jit(solution)/shard_map/mixed/pallas_call | solution.py:360
  162.8 2.3 %collective-permute-done.29.refs_1_ = bf16[128,512]{1,0:T(8,128)(2,1)S(1)} collective-permute-done((bf16[128,512]{1,0:T(8,128)(2,1)}, bf16[128,512]{1,0:T(8,128)(2,1)S(1)}, u32[]{:S(2)}, u32[]{:S(2)}) %collective-permute-start.29) | collective-permute-done | bytes 131104 | tf_op jit(solution)/shard_map/ppermute | solution.py:459
  165.8 2.3 %collective-permute-start.34 = (bf16[128,512]{1,0:T(8,128)(2,1)}, bf16[128,512]{1,0:T(8,128)(2,1)S(1)}, u32[]{:S(2)}, u32[]{:S(2)}) collective-permute-start(bf16[128,512]{1,0:T(8,128)(2,1)} %get-tuple-element.211), channel_id=1, source_target_pairs={{0,24},{4,28},{8,16},{12,20},{16,8},{20,12},{24,0},{28,4},{1,25},{... | collective-permute-start | bytes 393224 | tf_op jit(solution)/shard_map/ppermute | solution.py:459
  168.2 2.1 %collective-permute-start.31 = (f32[80,256]{1,0:T(8,128)S(1)}, f32[80,256]{1,0:T(8,128)S(1)}, u32[]{:S(2)}, u32[]{:S(2)}) collective-permute-start(f32[80,256]{1,0:T(8,128)S(1)} %get-tuple-element.247), channel_id=1, source_target_pairs={{0,16},{4,20},{8,24},{12,28},{16,0},{20,4},{24,8},{28,12},{1,17},{... | collective-permute-start | bytes 245768 | tf_op jit(solution)/shard_map/ppermute | solution.py:459
  170.3 2.3 %collective-permute-start.32 = (f32[80,256]{1,0:T(8,128)S(1)}, f32[80,256]{1,0:T(8,128)S(1)}, u32[]{:S(2)}, u32[]{:S(2)}) collective-permute-start(f32[80,256]{1,0:T(8,128)S(1)} %get-tuple-element.246), channel_id=1, source_target_pairs={{0,24},{4,28},{8,16},{12,20},{16,8},{20,12},{24,0},{28,4},{1,25},{... | collective-permute-start | bytes 245768 | tf_op jit(solution)/shard_map/ppermute | solution.py:459
  174.3 3.4 %collective-permute-done.30 = f32[80,256]{1,0:T(8,128)S(1)} collective-permute-done((f32[80,256]{1,0:T(8,128)S(1)}, f32[80,256]{1,0:T(8,128)S(1)}, u32[]{:S(2)}, u32[]{:S(2)}) %collective-permute-start.30) | collective-permute-done | bytes 81952 | tf_op jit(solution)/shard_map/ppermute | solution.py:459
  179.5 2.2 %collective-permute-start.35 = (bf16[80,256]{1,0:T(8,128)(2,1)S(1)}, bf16[80,256]{1,0:T(8,128)(2,1)S(1)}, u32[]{:S(2)}, u32[]{:S(2)}) collective-permute-start(bf16[80,256]{1,0:T(8,128)(2,1)S(1)} %get-tuple-element.243), channel_id=1, source_target_pairs={{0,8},{4,12},{8,0},{12,4},{16,24},{20,28},{24,16},{28,20},{1,9},{5... | collective-permute-start | bytes 122888 | tf_op jit(solution)/shard_map/ppermute | solution.py:459
  185.6 1.9 add_parts.3
  188.5 2.9 %collective-permute-done.41.refs_3_ = f32[128,512]{1,0:T(8,128)S(1)} collective-permute-done((f32[128,512]{1,0:T(8,128)}, f32[128,512]{1,0:T(8,128)S(1)}, u32[]{:S(2)}, u32[]{:S(2)}) %collective-permute-start.41) | collective-permute-done | bytes 262176 | tf_op jit(solution)/shard_map/ppermute | solution.py:459
  192.1 1.9 add_parts.2
  198.8 5.5 %layer_output.1 = bf16[864,1024]{1,0:T(8,128)(2,1)} custom-call(s32[6,3]{1,0:T(8,128)} %copy.33.cnt_ref, bf16[864,1024]{1,0:T(8,128)(2,1)} %copy-done.1, bf16[864,1024]{1,0:T(8,128)(2,1)} %bitcast.24, bf16[1728,1024]{1,0:T(8,128)(2,1)} %get-tuple-element.147.refs_0_, bf16[1728,1024]{1,0:T(8,128)(2,1)} %get-tuple-element.188.refs_1_, ...), custom_call_target="tpu_custom_call" | custom-call | flops 5000000 | bytes 10000 | tf_op jit(solution)/shard_map/layer_output/pallas_call | solution.py:445
  207.0 1.8 maximum_convert_fusion
  (155 shorter events, 50.9 us)
Async XLA Ops:
  2.9 12.6 %collective-permute-start.1 = (bf16[128,1024]{1,0:T(8,128)(2,1)S(1)}, bf16[128,1024]{1,0:T(8,128)(2,1)S(1)}, u32[]{:S(2)}, u32[]{:S(2)}) collective-permute-start(bf16[128,1024]{1,0:T(8,128)(2,1)S(1)} %pad_maximum_fusion.2.refs_2_), channel_id=1, source_target_pairs={{0,2},{1,3},{2,0},{3,1},{4,6},{5,7},{6,4},{7,5},{8,10},{9,11},{10,... | collective-permute-start | bytes 786440 | tf_op jit(solution)/shard_map/ppermute | solution.py:459
  5.9 9.6 %collective-permute-start = (s32[6,3]{0,1:T(4,128)}, s32[6,3]{0,1:T(4,128)S(1)}, u32[]{:S(2)}, u32[]{:S(2)}) collective-permute-start(s32[6,3]{0,1:T(4,128)} %param.13), channel_id=1, source_target_pairs={{0,1},{1,0},{2,3},{3,2},{4,5},{5,4},{6,7},{7,6},{8,9},{9,8},{10,11... | collective-permute-start | bytes 224 | tf_op jit(solution)/shard_map/ppermute | solution.py:459
  16.2 10.3 %collective-permute-start.4 = (bf16[2,864,1024]{2,1,0:T(8,128)(2,1)}, bf16[2,864,1024]{2,1,0:T(8,128)(2,1)S(1)}, u32[]{:S(2)}, u32[]{:S(2)}) collective-permute-start(bf16[2,864,1024]{2,1,0:T(8,128)(2,1)} %bitcast.17), channel_id=1, source_target_pairs={{0,1},{1,0},{2,3},{3,2},{4,5},{5,4},{6,7},{7,6},{8,9},{9,8},{10,11... | collective-permute-start | bytes 10616840 | tf_op jit(solution)/shard_map/ppermute | solution.py:459
  16.7 8.5 %collective-permute-start.2 = (bf16[128,1024]{1,0:T(8,128)(2,1)}, bf16[128,1024]{1,0:T(8,128)(2,1)}, u32[]{:S(2)}, u32[]{:S(2)}) collective-permute-start(bf16[128,1024]{1,0:T(8,128)(2,1)} %copy-done.18), channel_id=1, source_target_pairs={{0,8},{8,16},{16,24},{24,28},{28,20},{20,12},{12,4},{4,0},{1,9},{9... | collective-permute-start | bytes 786440 | tf_op jit(solution)/shard_map/ppermute | solution.py:475
  28.6 9.1 %collective-permute-start.9 = (bf16[128,1024]{1,0:T(8,128)(2,1)}, bf16[128,1024]{1,0:T(8,128)(2,1)S(1)}, u32[]{:S(2)}, u32[]{:S(2)}) collective-permute-start(bf16[128,1024]{1,0:T(8,128)(2,1)} %collective-permute-done.2.refs_1_), channel_id=1, source_target_pairs={{0,2},{1,3},{2,0},{3,1},{4,6},{5,7},{6,4},{7,5},{8,10},{9,11},{10,... | collective-permute-start | bytes 786440 | tf_op jit(solution)/shard_map/ppermute | solution.py:459
  51.6 28.9 %collective-permute-start.14 = (bf16[384,1024]{1,0:T(8,128)(2,1)}, bf16[384,1024]{1,0:T(8,128)(2,1)}, u32[]{:S(2)}, u32[]{:S(2)}) collective-permute-start(bf16[384,1024]{1,0:T(8,128)(2,1)} %pad_maximum_fusion), channel_id=1, source_target_pairs={{0,2},{1,3},{2,0},{3,1},{4,6},{5,7},{6,4},{7,5},{8,10},{9,11},{10,... | collective-permute-start | bytes 2359304 | tf_op jit(solution)/shard_map/ppermute | solution.py:459
  52.2 25.4 %collective-permute-start.12 = (bf16[128,1024]{1,0:T(8,128)(2,1)}, bf16[128,1024]{1,0:T(8,128)(2,1)}, u32[]{:S(2)}, u32[]{:S(2)}) collective-permute-start(bf16[128,1024]{1,0:T(8,128)(2,1)} %collective-permute-done.7.refs_3_), channel_id=1, source_target_pairs={{0,2},{1,3},{2,0},{3,1},{4,6},{5,7},{6,4},{7,5},{8,10},{9,11},{10,... | collective-permute-start | bytes 786440 | tf_op jit(solution)/shard_map/ppermute | solution.py:459
  53.7 26.9 %collective-permute-start.13 = (bf16[128,1024]{1,0:T(8,128)(2,1)}, bf16[128,1024]{1,0:T(8,128)(2,1)}, u32[]{:S(2)}, u32[]{:S(2)}) collective-permute-start(bf16[128,1024]{1,0:T(8,128)(2,1)} %collective-permute-done.10.refs_4_), channel_id=1, source_target_pairs={{0,2},{1,3},{2,0},{3,1},{4,6},{5,7},{6,4},{7,5},{8,10},{9,11},{10,... | collective-permute-start | bytes 786440 | tf_op jit(solution)/shard_map/ppermute | solution.py:459
  80.6 33.7 %collective-permute-start.15 = (bf16[512,512]{1,0:T(8,128)(2,1)}, bf16[512,512]{1,0:T(8,128)(2,1)S(1)}, u32[]{:S(2)}, u32[]{:S(2)}) collective-permute-start(bf16[512,512]{1,0:T(8,128)(2,1)} %get-tuple-element.162), channel_id=1, source_target_pairs={{0,2},{1,3},{2,0},{3,1},{4,6},{5,7},{6,4},{7,5},{8,10},{9,11},{10,... | collective-permute-start | bytes 1572872 | tf_op jit(solution)/shard_map/ppermute | solution.py:459
  80.6 33.7 %collective-permute-start.16 = (bf16[512,512]{1,0:T(8,128)(2,1)}, bf16[512,512]{1,0:T(8,128)(2,1)S(1)}, u32[]{:S(2)}, u32[]{:S(2)}) collective-permute-start(bf16[512,512]{1,0:T(8,128)(2,1)} %get-tuple-element.163), channel_id=1, source_target_pairs={{0,2},{1,3},{2,0},{3,1},{4,6},{5,7},{6,4},{7,5},{8,10},{9,11},{10,... | collective-permute-start | bytes 1572872 | tf_op jit(solution)/shard_map/ppermute | solution.py:459
  82.6 31.7 %collective-permute-start.17 = (bf16[512,512]{1,0:T(8,128)(2,1)}, bf16[512,512]{1,0:T(8,128)(2,1)S(1)}, u32[]{:S(2)}, u32[]{:S(2)}) collective-permute-start(bf16[512,512]{1,0:T(8,128)(2,1)} %get-tuple-element.164), channel_id=1, source_target_pairs={{0,2},{1,3},{2,0},{3,1},{4,6},{5,7},{6,4},{7,5},{8,10},{9,11},{10,... | collective-permute-start | bytes 1572872 | tf_op jit(solution)/shard_map/ppermute | solution.py:459
  115.3 14.9 %collective-permute-start.20 = (bf16[512,512]{1,0:T(8,128)(2,1)}, bf16[512,512]{1,0:T(8,128)(2,1)S(1)}, u32[]{:S(2)}, u32[]{:S(2)}) collective-permute-start(bf16[512,512]{1,0:T(8,128)(2,1)} %get-tuple-element.174), channel_id=1, source_target_pairs={{0,2},{1,3},{2,0},{3,1},{4,6},{5,7},{6,4},{7,5},{8,10},{9,11},{10,... | collective-permute-start | bytes 1572872 | tf_op jit(solution)/shard_map/ppermute | solution.py:459
  119.5 14.4 %collective-permute-start.19 = (bf16[512,512]{1,0:T(8,128)(2,1)}, bf16[512,512]{1,0:T(8,128)(2,1)}, u32[]{:S(2)}, u32[]{:S(2)}) collective-permute-start(bf16[512,512]{1,0:T(8,128)(2,1)} %add_convert_fusion.1), channel_id=1, source_target_pairs={{0,4},{4,0},{8,12},{12,8},{16,20},{20,16},{24,28},{28,24},{1,5},{5... | collective-permute-start | bytes 1572872 | tf_op jit(solution)/shard_map/ppermute | solution.py:459
  135.4 15.0 %collective-permute-start.28 = (bf16[512,512]{1,0:T(8,128)(2,1)}, bf16[512,512]{1,0:T(8,128)(2,1)S(1)}, u32[]{:S(2)}, u32[]{:S(2)}) collective-permute-start(bf16[512,512]{1,0:T(8,128)(2,1)} %add_convert_fusion), channel_id=1, source_target_pairs={{0,4},{4,0},{8,12},{12,8},{16,20},{20,16},{24,28},{28,24},{1,5},{5... | collective-permute-start | bytes 1572872 | tf_op jit(solution)/shard_map/ppermute | solution.py:459
  142.3 22.8 %collective-permute-start.23 = (f32[80,1024]{1,0:T(8,128)}, f32[80,1024]{1,0:T(8,128)S(1)}, u32[]{:S(2)}, u32[]{:S(2)}) collective-permute-start(f32[80,1024]{1,0:T(8,128)} %get-tuple-element.185), channel_id=1, source_target_pairs={{0,4},{4,0},{8,12},{12,8},{16,20},{20,16},{24,28},{28,24},{1,5},{5... | collective-permute-start | bytes 983048 | tf_op jit(solution)/shard_map/ppermute | solution.py:459
  143.9 21.2 %collective-permute-start.24 = (f32[80,1024]{1,0:T(8,128)}, f32[80,1024]{1,0:T(8,128)S(1)}, u32[]{:S(2)}, u32[]{:S(2)}) collective-permute-start(f32[80,1024]{1,0:T(8,128)} %get-tuple-element.186), channel_id=1, source_target_pairs={{0,2},{1,3},{2,0},{3,1},{4,6},{5,7},{6,4},{7,5},{8,10},{9,11},{10,... | collective-permute-start | bytes 983048 | tf_op jit(solution)/shard_map/ppermute | solution.py:524
  144.2 20.9 %collective-permute-start.25 = (f32[80,1024]{1,0:T(8,128)}, f32[80,1024]{1,0:T(8,128)S(1)}, u32[]{:S(2)}, u32[]{:S(2)}) collective-permute-start(f32[80,1024]{1,0:T(8,128)} %get-tuple-element.187), channel_id=1, source_target_pairs={{0,6},{1,7},{2,4},{3,5},{4,2},{5,3},{6,0},{7,1},{8,14},{9,15},{10,... | collective-permute-start | bytes 983048 | tf_op jit(solution)/shard_map/ppermute | solution.py:524
  145.8 13.2 %collective-permute-start.26 = (bf16[128,512]{1,0:T(8,128)(2,1)S(1)}, bf16[128,512]{1,0:T(8,128)(2,1)S(1)}, u32[]{:S(2)}, u32[]{:S(2)}) collective-permute-start(bf16[128,512]{1,0:T(8,128)(2,1)S(1)} %copy-done.26), channel_id=1, source_target_pairs={{0,16},{4,20},{8,24},{12,28},{16,0},{20,4},{24,8},{28,12},{1,17},{... | collective-permute-start | bytes 393224 | tf_op jit(solution)/shard_map/ppermute | solution.py:459
  150.4 12.4 %collective-permute-start.27 = (bf16[128,512]{1,0:T(8,128)(2,1)S(1)}, bf16[128,512]{1,0:T(8,128)(2,1)S(1)}, u32[]{:S(2)}, u32[]{:S(2)}) collective-permute-start(bf16[128,512]{1,0:T(8,128)(2,1)S(1)} %copy-done.25), channel_id=1, source_target_pairs={{0,24},{4,28},{8,16},{12,20},{16,8},{20,12},{24,0},{28,4},{1,25},{... | collective-permute-start | bytes 393224 | tf_op jit(solution)/shard_map/ppermute | solution.py:459
  165.8 13.7 %collective-permute-start.33 = (bf16[864,1024]{1,0:T(8,128)(2,1)}, bf16[864,1024]{1,0:T(8,128)(2,1)S(1)}, u32[]{:S(2)}, u32[]{:S(2)}) collective-permute-start(bf16[864,1024]{1,0:T(8,128)(2,1)} %mixed.1), channel_id=1, source_target_pairs={{0,1},{1,0},{2,3},{3,2},{4,5},{5,4},{6,7},{7,6},{8,9},{9,8},{10,11... | collective-permute-start | bytes 5308424 | tf_op jit(solution)/shard_map/ppermute | solution.py:459
  165.8 8.4 %collective-permute-start.34 = (bf16[128,512]{1,0:T(8,128)(2,1)}, bf16[128,512]{1,0:T(8,128)(2,1)S(1)}, u32[]{:S(2)}, u32[]{:S(2)}) collective-permute-start(bf16[128,512]{1,0:T(8,128)(2,1)} %get-tuple-element.211), channel_id=1, source_target_pairs={{0,24},{4,28},{8,16},{12,20},{16,8},{20,12},{24,0},{28,4},{1,25},{... | collective-permute-start | bytes 393224 | tf_op jit(solution)/shard_map/ppermute | solution.py:459
  168.1 9.5 %collective-permute-start.30 = (f32[80,256]{1,0:T(8,128)S(1)}, f32[80,256]{1,0:T(8,128)S(1)}, u32[]{:S(2)}, u32[]{:S(2)}) collective-permute-start(f32[80,256]{1,0:T(8,128)S(1)} %get-tuple-element.248), channel_id=1, source_target_pairs={{0,8},{4,12},{8,0},{12,4},{16,24},{20,28},{24,16},{28,20},{1,9},{5... | collective-permute-start | bytes 245768 | tf_op jit(solution)/shard_map/ppermute | solution.py:459
  168.2 10.8 %collective-permute-start.31 = (f32[80,256]{1,0:T(8,128)S(1)}, f32[80,256]{1,0:T(8,128)S(1)}, u32[]{:S(2)}, u32[]{:S(2)}) collective-permute-start(f32[80,256]{1,0:T(8,128)S(1)} %get-tuple-element.247), channel_id=1, source_target_pairs={{0,16},{4,20},{8,24},{12,28},{16,0},{20,4},{24,8},{28,12},{1,17},{... | collective-permute-start | bytes 245768 | tf_op jit(solution)/shard_map/ppermute | solution.py:459
  170.3 9.1 %collective-permute-start.32 = (f32[80,256]{1,0:T(8,128)S(1)}, f32[80,256]{1,0:T(8,128)S(1)}, u32[]{:S(2)}, u32[]{:S(2)}) collective-permute-start(f32[80,256]{1,0:T(8,128)S(1)} %get-tuple-element.246), channel_id=1, source_target_pairs={{0,24},{4,28},{8,16},{12,20},{16,8},{20,12},{24,0},{28,4},{1,25},{... | collective-permute-start | bytes 245768 | tf_op jit(solution)/shard_map/ppermute | solution.py:459
  174.2 10.8 %collective-permute-start.42 = (f32[128,512]{1,0:T(8,128)}, f32[128,512]{1,0:T(8,128)S(1)}, u32[]{:S(2)}, u32[]{:S(2)}) collective-permute-start(f32[128,512]{1,0:T(8,128)} %get-tuple-element.223), channel_id=1, source_target_pairs={{0,8},{4,12},{8,0},{12,4},{16,24},{20,28},{24,16},{28,20},{1,9},{5... | collective-permute-start | bytes 786440 | tf_op jit(solution)/shard_map/ppermute | solution.py:459
  177.7 13.8 %collective-permute-start.41 = (f32[128,512]{1,0:T(8,128)}, f32[128,512]{1,0:T(8,128)S(1)}, u32[]{:S(2)}, u32[]{:S(2)}) collective-permute-start(f32[128,512]{1,0:T(8,128)} %get-tuple-element.219), channel_id=1, source_target_pairs={{0,8},{4,12},{8,0},{12,4},{16,24},{20,28},{24,16},{28,20},{1,9},{5... | collective-permute-start | bytes 786440 | tf_op jit(solution)/shard_map/ppermute | solution.py:459
  179.5 14.6 %collective-permute-start.35 = (bf16[80,256]{1,0:T(8,128)(2,1)S(1)}, bf16[80,256]{1,0:T(8,128)(2,1)S(1)}, u32[]{:S(2)}, u32[]{:S(2)}) collective-permute-start(bf16[80,256]{1,0:T(8,128)(2,1)S(1)} %get-tuple-element.243), channel_id=1, source_target_pairs={{0,8},{4,12},{8,0},{12,4},{16,24},{20,28},{24,16},{28,20},{1,9},{5... | collective-permute-start | bytes 122888 | tf_op jit(solution)/shard_map/ppermute | solution.py:459
  181.6 12.4 %collective-permute-start.36 = (bf16[80,256]{1,0:T(8,128)(2,1)S(1)}, bf16[80,256]{1,0:T(8,128)(2,1)S(1)}, u32[]{:S(2)}, u32[]{:S(2)}) collective-permute-start(bf16[80,256]{1,0:T(8,128)(2,1)S(1)} %get-tuple-element.243), channel_id=1, source_target_pairs={{0,16},{4,20},{8,24},{12,28},{16,0},{20,4},{24,8},{28,12},{1,17},{... | collective-permute-start | bytes 122888 | tf_op jit(solution)/shard_map/ppermute | solution.py:459
  182.5 11.6 %collective-permute-start.37 = (bf16[80,256]{1,0:T(8,128)(2,1)S(1)}, bf16[80,256]{1,0:T(8,128)(2,1)S(1)}, u32[]{:S(2)}, u32[]{:S(2)}) collective-permute-start(bf16[80,256]{1,0:T(8,128)(2,1)S(1)} %get-tuple-element.243), channel_id=1, source_target_pairs={{0,24},{4,28},{8,16},{12,20},{16,8},{20,12},{24,0},{28,4},{1,25},{... | collective-permute-start | bytes 122888 | tf_op jit(solution)/shard_map/ppermute | solution.py:459
  194.1 10.3 %collective-permute-start.38 = (bf16[80,1024]{1,0:T(8,128)(2,1)S(1)}, bf16[80,1024]{1,0:T(8,128)(2,1)S(1)}, u32[]{:S(2)}, u32[]{:S(2)}) collective-permute-start(bf16[80,1024]{1,0:T(8,128)(2,1)S(1)} %constant_dynamic-update-slice_fusion.4), channel_id=1, source_target_pairs={{0,4},{4,0},{8,12},{12,8},{16,20},{20,16},{24,28},{28,24},{1,5},{5... | collective-permute-start | bytes 491528 | tf_op jit(solution)/shard_map/ppermute | solution.py:459
  195.9 8.5 %collective-permute-start.39 = (bf16[80,1024]{1,0:T(8,128)(2,1)S(1)}, bf16[80,1024]{1,0:T(8,128)(2,1)S(1)}, u32[]{:S(2)}, u32[]{:S(2)}) collective-permute-start(bf16[80,1024]{1,0:T(8,128)(2,1)S(1)} %constant_dynamic-update-slice_fusion.4), channel_id=1, source_target_pairs={{0,2},{1,3},{2,0},{3,1},{4,6},{5,7},{6,4},{7,5},{8,10},{9,11},{10,... | collective-permute-start | bytes 491528 | tf_op jit(solution)/shard_map/ppermute | solution.py:524
  196.2 8.4 %collective-permute-start.40 = (bf16[80,1024]{1,0:T(8,128)(2,1)S(1)}, bf16[80,1024]{1,0:T(8,128)(2,1)S(1)}, u32[]{:S(2)}, u32[]{:S(2)}) collective-permute-start(bf16[80,1024]{1,0:T(8,128)(2,1)S(1)} %constant_dynamic-update-slice_fusion.4), channel_id=1, source_target_pairs={{0,6},{1,7},{2,4},{3,5},{4,2},{5,3},{6,0},{7,1},{8,14},{9,15},{10,... | collective-permute-start | bytes 491528 | tf_op jit(solution)/shard_map/ppermute | solution.py:524
  (40 other events, 279.9 us)

commit v13 on v12

--- a/solution.py
+++ b/solution.py
@@ -71,7 +71,7 @@
             placed.append(
                 (dot_nn(onehot, parts[0]) + dot_nn(onehot, parts[1])) + dot_nn(onehot, parts[2])
             )
-            live = slot < cnt_ref[pl.ds(step * scenes + s, 1), g : g + 1]
+            live = slot < cnt_ref[g, step * scenes + s]
             rows_ref[1, s, rows, :] = jnp.where(live, og_ref[s, rows, :].astype(F32), 0.0).astype(BF16)
         summed = dot_nn(jnp.concatenate(picked, axis=0), w_ref[start * PIX : end * PIX, :])
         for s in range(scenes):
@@ -99,7 +99,7 @@
         stem_kernel,
         grid=(scenes // block,),
         in_specs=[
-            whole(counts),
+            pl.BlockSpec(memory_space=pltpu.SMEM),
             per((GROUPS, CAP)),
             per((patch_count, width)),
             whole(w_stem),
@@ -124,6 +124,24 @@
     )(counts, index, patches, w_stem, gain, table, genc, out_grad)
 
 
+def pack_kernel(qkv_ref, out_w_ref, pack_ref):
+    count, _, width = qkv_ref.shape
+    for c in range(count):
+        pack_ref[:, c * width : (c + 1) * width] = qkv_ref[c]
+    pack_ref[:, count * width :] = out_w_ref[...].T
+
+
+def pack_call(w_qkv, w_out):
+    parts = jnp.transpose(w_qkv, (1, 0, 2))
+    return pl.pallas_call(
+        pack_kernel,
+        out_shape=jax.ShapeDtypeStruct((w_qkv.shape[0], 3 * w_qkv.shape[2] + w_out.shape[0]), BF16),
+        compiler_params=params(),
+        cost_estimate=cost(1e6, 5e5),
+        name="pack_weights",
+    )(parts, w_out)
+
+
 def attention_kernel(
     packs, blocks, dp, cnt_ref, owner_ref, low_ref, na_ref, nb_ref, ga_ref, gb_ref, *refs
 ):
@@ -175,7 +193,7 @@
         base = pl.multiple_of(s * TOK, 16)
         at = pl.ds(base, TOK)
         scene = step * scenes + s
-        live = live_column(cnt_ref[half, scene, 0], cnt_ref[half, scene, 1], cnt_ref[half, scene, 2])
+        live = live_column(*[cnt_ref[half, g, scene] for g in range(GROUPS)])
         bias = jnp.where(live, 0.0, -1e30)
         q, k, v, dc = [qkv[at, c * width : (c + 1) * width] for c in range(4)]
         tall_q = jnp.concatenate([q * (m * scale) for m in masks], axis=0)
@@ -315,24 +333,29 @@
     )(place, *ins)
 
 
-def add_kernel(*refs):
-    total = refs[0][...]
-    for ref in refs[1:-1]:
-        total = total + ref[...].astype(F32)
-    refs[-1][...] = total
-
-
-def add_call(parts):
-    spec = pl.BlockSpec(parts[0].shape, lambda: (0, 0))
-    return pl.pallas_call(
-        add_kernel,
-        in_specs=[spec] * len(parts),
-        out_specs=spec,
-        out_shape=jax.ShapeDtypeStruct(parts[0].shape, F32),
+def result_kernel(count, *refs):
+    halves, qkv_ref, out_ref = (refs[:count], refs[count:-2]), refs[-2], refs[-1]
+    first, second = [functools.reduce(lambda a, b: a + b, [r[...].astype(F32) for r in half]) for half in halves]
+    width = first.shape[1] // 2
+    qkv_ref[0] = first[:, :width]
+    qkv_ref[1] = first[:, width:]
+    qkv_ref[2] = second[:, :width]
+    out_ref[...] = second[:, width:].T
+
+
+def result_call(first, second):
+    rows, cols = first[0].shape
+    qkv, out = pl.pallas_call(
+        functools.partial(result_kernel, len(first)),
+        out_shape=[
+            jax.ShapeDtypeStruct((3, rows, cols // 2), F32),
+            jax.ShapeDtypeStruct((cols // 2, rows), F32),
+        ],
         compiler_params=params(),
         cost_estimate=cost(1e6, 2e6),
-        name="add_parts",
-    )(*parts)
+        name="weight_results",
+    )(*first, *second)
+    return jnp.transpose(qkv, (1, 0, 2)), out
 
 
 def mixed_product(context_refs, weight_refs):
@@ -433,7 +456,7 @@
     total = emb_ref[...].astype(F32) + mixed
     for s in range(scenes):
         scene = step * scenes + s
-        live = live_column(cnt_ref[scene, 0], cnt_ref[scene, 1], cnt_ref[scene, 2])
+        live = live_column(*[cnt_ref[g, scene] for g in range(GROUPS)])
         at = slice(s * TOK, (s + 1) * TOK)
         out_ref[at, :] = jnp.where(live, total[at], 0.0).astype(BF16)
 
@@ -527,7 +550,7 @@
     hops = [(k // 2, k % 2) for k in range(1, 2 * fars)]
     arrived = [hop(part, f, b) for part, (f, b) in zip(parts[1:], hops)]
     arrived, beside = together(arrived, beside)
-    beside = after(*beside)
+    beside = after[0](*beside)
     total = parts[0]
     for part in arrived:
         total = total + part
@@ -542,6 +565,7 @@
     line = jnp.zeros((small, width), BF16)
     line = lax.dynamic_update_slice_in_dim(line, part, high * cols, 1)
     arrived = [swap(part, "dp", dp, 2 * j) for j in range(1, highs)]
+    arrived, beside = together(arrived, after[1](*beside))
     for j, block in enumerate(arrived):
         line = lax.dynamic_update_slice_in_dim(line, block, (high ^ (j + 1)) * cols, 1)
     block = jnp.zeros((rows, width), BF16)
@@ -582,10 +606,10 @@
     low, high = dp_low.reshape(1), dp_high.reshape(1)
     core = (lax.axis_index("group") % 2).reshape(1)
 
-    shard = jnp.concatenate([w_qkv.reshape(w_qkv.shape[0], 3 * width), w_out.T], axis=1)
+    shard = pack_call(w_qkv, w_out)
     cross = lambda x, f: swap(x, "group", group, 2 * f)
     far_shards = [cross(shard, f) for f in fars]
-    counts = vis_count.astype(jnp.int32)
+    counts = vis_count.astype(jnp.int32).T
     counts_far = swap(counts, "group", group, 1)
     table, genc = encoding_tables(patches.shape[1])
     gain = ln_gain.reshape(1, D)
@@ -660,24 +684,21 @@
     _, coming[1], keeps[1] = together(stem_parts, coming[1], keeps[1])
     second = second_leg(1)
     near = dp // 2 * 3 // 4
-    beside = [
-        mixed_call(packs, weights),
-        [share, *first_rest],
-        [second[0], *spread(second, range(2, near))],
-    ]
-
-    def after(mixed, first, second):
-        return [swap(mixed, "group", group, 1), first, [*second, *spread(blocks[1], range(near, dp // 2))]]
-
-    def last(mixed, first, second):
+    beside = [mixed_call(packs, weights), share, *first_rest, second[0]]
+    def after_first(mixed, *arrived):
+        return [swap(mixed, "group", group, 1), *arrived[:-1], *spread(first, [1]), arrived[-1]]
+
+    def after_second(*arrived):
+        return [*arrived, *spread(second, [1, *range(2, near)])]
+
+    def last(mixed, *arrived):
         output = output_call(counts, mixed, emb, packs, weights)
-        first, second = [add_call([*x, *spread(b, [1])]) for x, b in zip((first, second), blocks)]
-        qkv = jnp.concatenate([first, second[:, :width]], axis=1)
-        return output, qkv.reshape(qkv.shape[0], 3, width), second[:, width:].T
-
-    blocks = (first, second)
+        arrived = [*arrived, *spread(second, range(near, dp // 2))]
+        half = len(arrived) // 2
+        return output, *result_call(arrived[:half], arrived[half:])
+
     grad_w_stem, (output, grad_w_qkv, grad_w_out) = sum_stem(
-        stem_parts, beside, after, last, dp, group
+        stem_parts, beside, (after_first, after_second), last, dp, group
     )
     return (output.reshape(scenes, GROUPS, CAP, D), grad_w_stem, grad_w_qkv, grad_w_out)
 

time: 209 us -> 208 us (level)
  local copies, waits for them, and re-layouts: 13.3 us -> 7.18 us
  other arithmetic: 8.63 us -> 10.8 us
    unnamed x61 -> x54, local copies, waits for them, and re-layouts: 11.1 us -> 6.3 us
  transfers between devices with their start and end apart: 44 -> 44, of which waited for: 20 -> 20; matrix products, arithmetic and copies ran while one was open for 5% -> 4% of each run, Pallas kernels for 44% -> 44%
where the time goes in v13:
time: 208 us; the launch traced here: 206 us
  Pallas kernels  92.9 us (45%)
  waiting for transfers between devices  51.5 us (25%)
  starting transfers between devices  42.6 us (20%)
  other arithmetic  10.8 us (5%)
  local copies, waits for them, and re-layouts  7.18 us (3%)
    pallas_call x2, Pallas kernels, attention_call(): pl.pallas_call(functools.partial(attention_kernel, packs, len(blocks), dp...  54.5 us
    ppermute x33, starting transfers between devices, swap(): return lax.ppermute(x, axis, [(i, i ^ bit) for i in range(size)])  29.9 us
    ppermute x33, waiting for transfers between devices, swap(): return lax.ppermute(x, axis, [(i, i ^ bit) for i in range(size)])  27.7 us
    ppermute x4, waiting for transfers between devices, send(): moved = [lax.ppermute(self.ahead[-1], self.axis, self.forward)]  19.7 us
    pallas_call x1, Pallas kernels, tail_call(): pl.pallas_call(tail_kernel, grid=(tokens // rows,), in_specs=[SCALARS, pe...  9.05 us
    pallas_call x1, Pallas kernels, stem_call(): pl.pallas_call(stem_kernel, grid=(scenes // block,), in_specs=[pl.BlockSp...  8.27 us
    pallas_call x3, Pallas kernels, combine_call(): pl.pallas_call(functools.partial(combine_kernel, [len(part) for part in p...  7.99 us
    unnamed x54, local copies, waits for them, and re-layouts  6.3 us
  transfers between devices with their start and end apart: 44, of which 20 were waited for; matrix products, arithmetic and copies ran while one was open for 4% of the time, Pallas kernels for 44%

profile of v13, /device:TPU:0, one launch (start us, length us, event | category | flops | bytes accessed | tf_op | source)
XLA Modules:
  0.0 206.0 jit_solution(5714530987074107050)
XLA Ops:
  0.6 1.7 pack_weights.1.refs_2_
  2.3 2.9 %collective-permute-start.1 = (bf16[128,1024]{1,0:T(8,128)(2,1)}, bf16[128,1024]{1,0:T(8,128)(2,1)}, u32[]{:S(2)}, u32[]{:S(2)}) collective-permute-start(bf16[128,1024]{1,0:T(8,128)(2,1)} %pack_weights.1.refs_2_), channel_id=1, source_target_pairs={{0,2},{1,3},{2,0},{3,1},{4,6},{5,7},{6,4},{7,5},{8,10},{9,11},{10,... | collective-permute-start | bytes 786440 | tf_op jit(solution)/shard_map/ppermute | solution.py:482
  5.3 8.3 %stem_norm.1 = (bf16[6,144,1024]{2,1,0:T(8,128)(2,1)}, bf16[2,6,144,1024]{3,2,1,0:T(8,128)(2,1)}, bf16[6,144,256]{2,1,0:T(8,128)(2,1)}) custom-call(s32[3,6]{1,0:T(4,128)} %bitcast.29, s32[6,3,48]{2,1,0:T(4,128)} %idx_ref.1, bf16[6,144,640]{2,1,0:T(8,128)(2,1)} %patch_ref.1, bf16[640,1024]{1,0:T(8,128)(2,1)} %w_ref.1, f32[1,1024]{1,0:T(1,128)} %bitcast.32, ...), custom_call_target="tpu_custom_call" | custom-call | flops 8000000 | bytes 12000 | tf_op jit(solution)/shard_map/stem_norm/pallas_call | solution.py:98
  17.2 6.0 %collective-permute-done.2.refs_1_ = bf16[128,1024]{1,0:T(8,128)(2,1)} collective-permute-done((bf16[128,1024]{1,0:T(8,128)(2,1)}, bf16[128,1024]{1,0:T(8,128)(2,1)}, u32[]{:S(2)}, u32[]{:S(2)}) %collective-permute-start.2) | collective-permute-done | bytes 262176 | tf_op jit(solution)/shard_map/ppermute | solution.py:498
  27.1 4.7 %collective-permute-done.5.refs_2_ = bf16[128,1024]{1,0:T(8,128)(2,1)S(1)} collective-permute-done((bf16[128,1024]{1,0:T(8,128)(2,1)}, bf16[128,1024]{1,0:T(8,128)(2,1)S(1)}, u32[]{:S(2)}, u32[]{:S(2)}) %collective-permute-start.5) | collective-permute-done | bytes 262176 | tf_op jit(solution)/shard_map/ppermute | solution.py:498
  35.7 3.9 %collective-permute-done.7.refs_3_ = bf16[128,1024]{1,0:T(8,128)(2,1)} collective-permute-done((bf16[128,1024]{1,0:T(8,128)(2,1)S(1)}, bf16[128,1024]{1,0:T(8,128)(2,1)}, u32[]{:S(2)}, u32[]{:S(2)}) %collective-permute-start.7) | collective-permute-done | bytes 262176 | tf_op jit(solution)/shard_map/ppermute | solution.py:498
  42.6 5.2 %collective-permute-done.10.refs_4_ = bf16[128,1024]{1,0:T(8,128)(2,1)} collective-permute-done((bf16[128,1024]{1,0:T(8,128)(2,1)}, bf16[128,1024]{1,0:T(8,128)(2,1)}, u32[]{:S(2)}, u32[]{:S(2)}) %collective-permute-start.10) | collective-permute-done | bytes 262176 | tf_op jit(solution)/shard_map/ppermute | solution.py:498
  47.7 1.9 pad_maximum_fusion
  52.2 22.8 %attention.2 = (bf16[1728,1024]{1,0:T(8,128)(2,1)}, bf16[1024,1024]{1,0:T(8,128)(2,1)}, bf16[512,512]{1,0:T(8,128)(2,1)}, bf16[512,512]{1,0:T(8,128)(2,1)}, bf16...) custom-call(s32[2,3,6]{2,1,0:T(4,128)} %pad_add_fusion.cnt_ref, s32[8]{0:T(128)} %compare_select_fusion.2.owner_ref, ...), custom_call_target="tpu_custom_call" | custom-call | flops 20000000 | bytes 14000 | tf_op jit(solution)/shard_map/attention/pallas_call | solution.py:277
  75.0 3.6 %collective-permute-done.13.refs_6_ = bf16[128,1024]{1,0:T(8,128)(2,1)} collective-permute-done((bf16[128,1024]{1,0:T(8,128)(2,1)}, bf16[128,1024]{1,0:T(8,128)(2,1)}, u32[]{:S(2)}, u32[]{:S(2)}) %collective-permute-start.13) | collective-permute-done | bytes 262176 | tf_op jit(solution)/shard_map/ppermute | solution.py:482
  81.1 31.7 %attention.3 = (bf16[1728,1024]{1,0:T(8,128)(2,1)}, bf16[1024,1024]{1,0:T(8,128)(2,1)}, f32[512,512]{1,0:T(8,128)}, f32[512,512]{1,0:T(8,128)}, f32[512,512]{1,0...) custom-call(s32[2,3,6]{2,1,0:T(4,128)} %pad_add_fusion.cnt_ref, ...), custom_call_target="tpu_custom_call" | custom-call | flops 20000000 | bytes 14000 | tf_op jit(solution)/shard_map/attention/pallas_call | solution.py:277
  115.3 2.2 %add_convert_fusion.1 = bf16[512,512]{1,0:T(8,128)(2,1)} fusion(f32[512,512]{1,0:T(8,128)} %get-tuple-element.183, bf16[512,512]{1,0:T(8,128)(2,1)S(1)} %collective-permute-done.15), kind=kLoop, calls=%fused_computation.2 | loop fusion | flops 786432 | bytes 2097152 | tf_op jit(solution)/shard_map/convert_element_type | solution.py:670
  119.2 9.0 %tail.1 = (f32[320,1024]{1,0:T(8,128)}, f32[320,512]{1,0:T(8,128)}, f32[320,512]{1,0:T(8,128)}) custom-call(s32[1]{0:T(128)} %bitcast.1.core_ref, f32[864,1024]{1,0:T(8,128)} %get-tuple-element.176.own_ref, bf16[864,1024]{1,0:T(8,128)(2,1)} %copy-done.3, bf16[864,1024]{1,0:T(8,128)(2,1)} %bitcast.22, bf16[2,864,1024]{2,1,0:T(8,128)(2,1)} %bitcast.21, ...), custom_call_target="tpu_custom_call" | custom-call | flops 10000000 | bytes 12000 | tf_op jit(solution)/shard_map/tail/pallas_call | solution.py:437
  128.4 3.5 %collective-permute-done.19.refs_2_ = bf16[512,512]{1,0:T(8,128)(2,1)} collective-permute-done((bf16[512,512]{1,0:T(8,128)(2,1)}, bf16[512,512]{1,0:T(8,128)(2,1)}, u32[]{:S(2)}, u32[]{:S(2)}) %collective-permute-start.19) | collective-permute-done | bytes 524320 | tf_op jit(solution)/shard_map/ppermute | solution.py:482
  133.8 2.5 %combine.3 = (f32[128,512]{1,0:T(8,128)}, f32[128,512]{1,0:T(8,128)}, bf16[128,512]{1,0:T(8,128)(2,1)}, bf16[128,512]{1,0:T(8,128)(2,1)}) custom-call(s32[1]{0:T(128)} %bitcast.12.place_ref, f32[512,512]{1,0:T(8,128)} %get-tuple-element.189.refs_0_, bf16[512,512]{1,0:T(8,128)(2,1)} %copy-done.11, bf16[512,512]{1,0:T(8,128)(2,1)} %collective-permute-done.19.refs_2_), custom_call_target="tpu_custom_call" | custom-call | flops 1000 | bytes 5000 | tf_op jit(solution)/shard_map/combine/pallas_call | solution.py:325
  137.4 2.9 %combine.4 = (f32[80,1024]{1,0:T(8,128)}, f32[80,1024]{1,0:T(8,128)}, f32[80,1024]{1,0:T(8,128)}, f32[80,1024]{1,0:T(8,128)}) custom-call(s32[1]{0:T(128)} %bitcast.place_ref, f32[320,1024]{1,0:T(8,128)} %get-tuple-element.186.refs_0_, f32[320,512]{1,0:T(8,128)} %copy-done.8, f32[320,512]{1,0:T(8,128)} %copy-done.9), custom_call_target="tpu_custom_call" | custom-call | flops 1000 | bytes 5000 | tf_op jit(solution)/shard_map/combine/pallas_call | solution.py:325
  145.2 3.2 %collective-permute-done.28.refs_2_ = bf16[512,512]{1,0:T(8,128)(2,1)S(1)} collective-permute-done((bf16[512,512]{1,0:T(8,128)(2,1)}, bf16[512,512]{1,0:T(8,128)(2,1)S(1)}, u32[]{:S(2)}, u32[]{:S(2)}) %collective-permute-start.28) | collective-permute-done | bytes 524320 | tf_op jit(solution)/shard_map/ppermute | solution.py:482
  149.9 3.7 %mixed.1 = bf16[864,1024]{1,0:T(8,128)(2,1)} custom-call(bf16[1728,1024]{1,0:T(8,128)(2,1)} %get-tuple-element.158.refs_0_, bf16[1728,1024]{1,0:T(8,128)(2,1)} %get-tuple-element.199.refs_1_, bf16[1024,1024]{1,0:T(8,128)(2,1)} %get-tuple-element.159.refs_1_.refs_2_, bf16[1024,1024]{1,0:T(8,128)(2,1)} %get-tuple-element.200.refs_3_), custom_call_target="tpu_custom_call" | custom-call | flops 2000000 | bytes 5000 | tf_op jit(solution)/shard_map/mixed/pallas_call | solution.py:383
  153.6 2.6 %combine.5 = (f32[128,512]{1,0:T(8,128)}, f32[128,512]{1,0:T(8,128)}, bf16[128,512]{1,0:T(8,128)(2,1)}, bf16[128,512]{1,0:T(8,128)(2,1)}) custom-call(s32[1]{0:T(128)} %bitcast.12.place_ref, f32[512,512]{1,0:T(8,128)} %get-tuple-element.208.refs_0_, bf16[512,512]{1,0:T(8,128)(2,1)} %copy-done.10, bf16[512,512]{1,0:T(8,128)(2,1)} %copy-done.12), custom_call_target="tpu_custom_call" | custom-call | flops 1000 | bytes 5000 | tf_op jit(solution)/shard_map/combine/pallas_call | solution.py:325
  156.3 5.2 %collective-permute-done.23 = f32[80,1024]{1,0:T(8,128)S(1)} collective-permute-done((f32[80,1024]{1,0:T(8,128)}, f32[80,1024]{1,0:T(8,128)S(1)}, u32[]{:S(2)}, u32[]{:S(2)}) %collective-permute-start.23) | collective-permute-done | bytes 327712 | tf_op jit(solution)/shard_map/ppermute | solution.py:482
  169.5 2.3 %collective-permute-start.31 = (f32[80,256]{1,0:T(8,128)}, f32[80,256]{1,0:T(8,128)}, u32[]{:S(2)}, u32[]{:S(2)}) collective-permute-start(f32[80,256]{1,0:T(8,128)} %get-tuple-element.256), channel_id=1, source_target_pairs={{0,24},{4,28},{8,16},{12,20},{16,8},{20,12},{24,0},{28,4},{1,25},{... | collective-permute-start | bytes 245768 | tf_op jit(solution)/shard_map/ppermute | solution.py:482
  171.8 2.3 %collective-permute-done.33.refs_3_ = f32[128,512]{1,0:T(8,128)} collective-permute-done((f32[128,512]{1,0:T(8,128)}, f32[128,512]{1,0:T(8,128)}, u32[]{:S(2)}, u32[]{:S(2)}) %collective-permute-start.33) | collective-permute-done | bytes 262176 | tf_op jit(solution)/shard_map/ppermute | solution.py:482
  174.1 1.9 collective-permute-done.29
  176.3 2.6 %collective-permute-done.31 = f32[80,256]{1,0:T(8,128)} collective-permute-done((f32[80,256]{1,0:T(8,128)}, f32[80,256]{1,0:T(8,128)}, u32[]{:S(2)}, u32[]{:S(2)}) %collective-permute-start.31) | collective-permute-done | bytes 81952 | tf_op jit(solution)/shard_map/ppermute | solution.py:482
  180.6 2.6 %collective-permute-start.35 = (bf16[80,256]{1,0:T(8,128)(2,1)S(1)}, bf16[80,256]{1,0:T(8,128)(2,1)S(1)}, u32[]{:S(2)}, u32[]{:S(2)}) collective-permute-start(bf16[80,256]{1,0:T(8,128)(2,1)S(1)} %get-tuple-element.253), channel_id=1, source_target_pairs={{0,16},{4,20},{8,24},{12,28},{16,0},{20,4},{24,8},{28,12},{1,17},{... | collective-permute-start | bytes 122888 | tf_op jit(solution)/shard_map/ppermute | solution.py:482
  185.3 1.8 collective-permute-start.42
  188.0 1.7 collective-permute-done.36
  190.7 2.6 %collective-permute-start.41 = (bf16[80,1024]{1,0:T(8,128)(2,1)S(1)}, bf16[80,1024]{1,0:T(8,128)(2,1)S(1)}, u32[]{:S(2)}, u32[]{:S(2)}) collective-permute-start(bf16[80,1024]{1,0:T(8,128)(2,1)S(1)} %constant_dynamic-update-slice_fusion.4), channel_id=1, source_target_pairs={{0,6},{1,7},{2,4},{3,5},{4,2},{5,3},{6,0},{7,1},{8,14},{9,15},{10,... | collective-permute-start | bytes 491528 | tf_op jit(solution)/shard_map/ppermute | solution.py:547
  193.9 2.3 %weight_results.1 = (f32[3,128,256]{2,1,0:T(8,128)}, f32[256,128]{1,0:T(8,128)}) custom-call(f32[128,512]{1,0:T(8,128)} %get-tuple-element.236.refs_0_, bf16[128,512]{1,0:T(8,128)(2,1)} %copy-done.21, bf16[128,512]{1,0:T(8,128)(2,1)} %copy-done.22, f32[128,512]{1,0:T(8,128)} %collective-permute-done.33.refs_3_, f32[128,512]{1,0:T(8,128)} %get-tuple-element.240.refs_4_, ...), custom_call_target="tpu_custom_call" | custom-call | flops 1000 | bytes 2000 | tf_op jit(solution)/shard_map/weight_results/pallas_call | solution.py:348
  196.2 5.5 %layer_output.1 = bf16[864,1024]{1,0:T(8,128)(2,1)} custom-call(s32[3,6]{1,0:T(4,128)} %bitcast.30, bf16[864,1024]{1,0:T(8,128)(2,1)} %copy-done.1, bf16[864,1024]{1,0:T(8,128)(2,1)} %bitcast.23, bf16[1728,1024]{1,0:T(8,128)(2,1)} %get-tuple-element.158.refs_0_, bf16[1728,1024]{1,0:T(8,128)(2,1)} %get-tuple-element.199.refs_1_, ...), custom_call_target="tpu_custom_call" | custom-call | flops 5000000 | bytes 10000 | tf_op jit(solution)/shard_map/layer_output/pallas_call | solution.py:468
  202.0 2.1 %collective-permute-done.43 = bf16[320,1024]{1,0:T(8,128)(2,1)S(1)} collective-permute-done((bf16[320,1024]{1,0:T(8,128)(2,1)S(1)}, bf16[320,1024]{1,0:T(8,128)(2,1)S(1)}, u32[]{:S(2)}, u32[]{:S(2)}) %collective-permute-start.43) | collective-permute-done | bytes 655392 | tf_op jit(solution)/shard_map/ppermute | solution.py:482
  204.2 1.8 maximum_convert_fusion
  (140 shorter events, 48.2 us)
Async XLA Ops:
  2.3 11.8 %collective-permute-start.1 = (bf16[128,1024]{1,0:T(8,128)(2,1)}, bf16[128,1024]{1,0:T(8,128)(2,1)}, u32[]{:S(2)}, u32[]{:S(2)}) collective-permute-start(bf16[128,1024]{1,0:T(8,128)(2,1)} %pack_weights.1.refs_2_), channel_id=1, source_target_pairs={{0,2},{1,3},{2,0},{3,1},{4,6},{5,7},{6,4},{7,5},{8,10},{9,11},{10,... | collective-permute-start | bytes 786440 | tf_op jit(solution)/shard_map/ppermute | solution.py:482
  5.3 8.3 %collective-permute-start = (s32[3,6]{1,0:T(4,128)}, s32[3,6]{1,0:T(4,128)S(1)}, u32[]{:S(2)}, u32[]{:S(2)}) collective-permute-start(s32[3,6]{1,0:T(4,128)} %bitcast.28), channel_id=1, source_target_pairs={{0,1},{1,0},{2,3},{3,2},{4,5},{5,4},{6,7},{7,6},{8,9},{9,8},{10,11... | collective-permute-start | bytes 224 | tf_op jit(solution)/shard_map/ppermute | solution.py:482
  14.2 10.3 %collective-permute-start.4 = (bf16[2,864,1024]{2,1,0:T(8,128)(2,1)}, bf16[2,864,1024]{2,1,0:T(8,128)(2,1)S(1)}, u32[]{:S(2)}, u32[]{:S(2)}) collective-permute-start(bf16[2,864,1024]{2,1,0:T(8,128)(2,1)} %bitcast.16), channel_id=1, source_target_pairs={{0,1},{1,0},{2,3},{3,2},{4,5},{5,4},{6,7},{7,6},{8,9},{9,8},{10,11... | collective-permute-start | bytes 10616840 | tf_op jit(solution)/shard_map/ppermute | solution.py:482
  14.7 8.5 %collective-permute-start.2 = (bf16[128,1024]{1,0:T(8,128)(2,1)}, bf16[128,1024]{1,0:T(8,128)(2,1)}, u32[]{:S(2)}, u32[]{:S(2)}) collective-permute-start(bf16[128,1024]{1,0:T(8,128)(2,1)} %collective-permute-done.1.refs_0_), channel_id=1, source_target_pairs={{0,8},{8,16},{16,24},{24,28},{28,20},{20,12},{12,4},{4,0},{1,9},{9... | collective-permute-start | bytes 786440 | tf_op jit(solution)/shard_map/ppermute | solution.py:498
  16.3 8.2 %collective-permute-start.3 = (bf16[128,1024]{1,0:T(8,128)(2,1)}, bf16[128,1024]{1,0:T(8,128)(2,1)}, u32[]{:S(2)}, u32[]{:S(2)}) collective-permute-start(bf16[128,1024]{1,0:T(8,128)(2,1)} %collective-permute-done.1.refs_0_), channel_id=1, source_target_pairs={{8,0},{16,8},{24,16},{28,24},{20,28},{12,20},{4,12},{0,4},{9,1},{1... | collective-permute-start | bytes 786440 | tf_op jit(solution)/shard_map/ppermute | solution.py:500
  26.6 9.1 %collective-permute-start.9 = (bf16[128,1024]{1,0:T(8,128)(2,1)}, bf16[128,1024]{1,0:T(8,128)(2,1)S(1)}, u32[]{:S(2)}, u32[]{:S(2)}) collective-permute-start(bf16[128,1024]{1,0:T(8,128)(2,1)} %collective-permute-done.2.refs_1_), channel_id=1, source_target_pairs={{0,2},{1,3},{2,0},{3,1},{4,6},{5,7},{6,4},{7,5},{8,10},{9,11},{10,... | collective-permute-start | bytes 786440 | tf_op jit(solution)/shard_map/ppermute | solution.py:482
  35.1 7.5 %collective-permute-start.11 = (bf16[128,1024]{1,0:T(8,128)(2,1)S(1)}, bf16[128,1024]{1,0:T(8,128)(2,1)}, u32[]{:S(2)}, u32[]{:S(2)}) collective-permute-start(bf16[128,1024]{1,0:T(8,128)(2,1)S(1)} %collective-permute-done.5.refs_2_), channel_id=1, source_target_pairs={{0,2},{1,3},{2,0},{3,1},{4,6},{5,7},{6,4},{7,5},{8,10},{9,11},{10,... | collective-permute-start | bytes 786440 | tf_op jit(solution)/shard_map/ppermute | solution.py:482
  49.6 28.9 %collective-permute-start.14 = (bf16[384,1024]{1,0:T(8,128)(2,1)}, bf16[384,1024]{1,0:T(8,128)(2,1)}, u32[]{:S(2)}, u32[]{:S(2)}) collective-permute-start(bf16[384,1024]{1,0:T(8,128)(2,1)} %pad_maximum_fusion), channel_id=1, source_target_pairs={{0,2},{1,3},{2,0},{3,1},{4,6},{5,7},{6,4},{7,5},{8,10},{9,11},{10,... | collective-permute-start | bytes 2359304 | tf_op jit(solution)/shard_map/ppermute | solution.py:482
  50.2 24.8 %collective-permute-start.12 = (bf16[128,1024]{1,0:T(8,128)(2,1)}, bf16[128,1024]{1,0:T(8,128)(2,1)}, u32[]{:S(2)}, u32[]{:S(2)}) collective-permute-start(bf16[128,1024]{1,0:T(8,128)(2,1)} %collective-permute-done.7.refs_3_), channel_id=1, source_target_pairs={{0,2},{1,3},{2,0},{3,1},{4,6},{5,7},{6,4},{7,5},{8,10},{9,11},{10,... | collective-permute-start | bytes 786440 | tf_op jit(solution)/shard_map/ppermute | solution.py:482
  51.6 26.9 %collective-permute-start.13 = (bf16[128,1024]{1,0:T(8,128)(2,1)}, bf16[128,1024]{1,0:T(8,128)(2,1)}, u32[]{:S(2)}, u32[]{:S(2)}) collective-permute-start(bf16[128,1024]{1,0:T(8,128)(2,1)} %collective-permute-done.10.refs_4_), channel_id=1, source_target_pairs={{0,2},{1,3},{2,0},{3,1},{4,6},{5,7},{6,4},{7,5},{8,10},{9,11},{10,... | collective-permute-start | bytes 786440 | tf_op jit(solution)/shard_map/ppermute | solution.py:482
  78.6 34.3 %collective-permute-start.15 = (bf16[512,512]{1,0:T(8,128)(2,1)}, bf16[512,512]{1,0:T(8,128)(2,1)S(1)}, u32[]{:S(2)}, u32[]{:S(2)}) collective-permute-start(bf16[512,512]{1,0:T(8,128)(2,1)} %get-tuple-element.173), channel_id=1, source_target_pairs={{0,2},{1,3},{2,0},{3,1},{4,6},{5,7},{6,4},{7,5},{8,10},{9,11},{10,... | collective-permute-start | bytes 1572872 | tf_op jit(solution)/shard_map/ppermute | solution.py:482
  79.1 33.7 %collective-permute-start.16 = (bf16[512,512]{1,0:T(8,128)(2,1)}, bf16[512,512]{1,0:T(8,128)(2,1)S(1)}, u32[]{:S(2)}, u32[]{:S(2)}) collective-permute-start(bf16[512,512]{1,0:T(8,128)(2,1)} %get-tuple-element.174), channel_id=1, source_target_pairs={{0,2},{1,3},{2,0},{3,1},{4,6},{5,7},{6,4},{7,5},{8,10},{9,11},{10,... | collective-permute-start | bytes 1572872 | tf_op jit(solution)/shard_map/ppermute | solution.py:482
  80.6 32.3 %collective-permute-start.17 = (bf16[512,512]{1,0:T(8,128)(2,1)}, bf16[512,512]{1,0:T(8,128)(2,1)S(1)}, u32[]{:S(2)}, u32[]{:S(2)}) collective-permute-start(bf16[512,512]{1,0:T(8,128)(2,1)} %get-tuple-element.175), channel_id=1, source_target_pairs={{0,2},{1,3},{2,0},{3,1},{4,6},{5,7},{6,4},{7,5},{8,10},{9,11},{10,... | collective-permute-start | bytes 1572872 | tf_op jit(solution)/shard_map/ppermute | solution.py:482
  113.9 14.5 %collective-permute-start.20 = (bf16[512,512]{1,0:T(8,128)(2,1)}, bf16[512,512]{1,0:T(8,128)(2,1)S(1)}, u32[]{:S(2)}, u32[]{:S(2)}) collective-permute-start(bf16[512,512]{1,0:T(8,128)(2,1)} %get-tuple-element.185), channel_id=1, source_target_pairs={{0,2},{1,3},{2,0},{3,1},{4,6},{5,7},{6,4},{7,5},{8,10},{9,11},{10,... | collective-permute-start | bytes 1572872 | tf_op jit(solution)/shard_map/ppermute | solution.py:482
  117.5 14.4 %collective-permute-start.19 = (bf16[512,512]{1,0:T(8,128)(2,1)}, bf16[512,512]{1,0:T(8,128)(2,1)}, u32[]{:S(2)}, u32[]{:S(2)}) collective-permute-start(bf16[512,512]{1,0:T(8,128)(2,1)} %add_convert_fusion.1), channel_id=1, source_target_pairs={{0,4},{4,0},{8,12},{12,8},{16,20},{20,16},{24,28},{28,24},{1,5},{5... | collective-permute-start | bytes 1572872 | tf_op jit(solution)/shard_map/ppermute | solution.py:482
  133.4 15.0 %collective-permute-start.28 = (bf16[512,512]{1,0:T(8,128)(2,1)}, bf16[512,512]{1,0:T(8,128)(2,1)S(1)}, u32[]{:S(2)}, u32[]{:S(2)}) collective-permute-start(bf16[512,512]{1,0:T(8,128)(2,1)} %add_convert_fusion), channel_id=1, source_target_pairs={{0,4},{4,0},{8,12},{12,8},{16,20},{20,16},{24,28},{28,24},{1,5},{5... | collective-permute-start | bytes 1572872 | tf_op jit(solution)/shard_map/ppermute | solution.py:482
  140.3 21.2 %collective-permute-start.23 = (f32[80,1024]{1,0:T(8,128)}, f32[80,1024]{1,0:T(8,128)S(1)}, u32[]{:S(2)}, u32[]{:S(2)}) collective-permute-start(f32[80,1024]{1,0:T(8,128)} %get-tuple-element.196), channel_id=1, source_target_pairs={{0,4},{4,0},{8,12},{12,8},{16,20},{20,16},{24,28},{28,24},{1,5},{5... | collective-permute-start | bytes 983048 | tf_op jit(solution)/shard_map/ppermute | solution.py:482
  141.9 19.6 %collective-permute-start.24 = (f32[80,1024]{1,0:T(8,128)}, f32[80,1024]{1,0:T(8,128)S(1)}, u32[]{:S(2)}, u32[]{:S(2)}) collective-permute-start(f32[80,1024]{1,0:T(8,128)} %get-tuple-element.197), channel_id=1, source_target_pairs={{0,2},{1,3},{2,0},{3,1},{4,6},{5,7},{6,4},{7,5},{8,10},{9,11},{10,... | collective-permute-start | bytes 983048 | tf_op jit(solution)/shard_map/ppermute | solution.py:547
  142.4 19.1 %collective-permute-start.25 = (f32[80,1024]{1,0:T(8,128)}, f32[80,1024]{1,0:T(8,128)S(1)}, u32[]{:S(2)}, u32[]{:S(2)}) collective-permute-start(f32[80,1024]{1,0:T(8,128)} %get-tuple-element.198), channel_id=1, source_target_pairs={{0,6},{1,7},{2,4},{3,5},{4,2},{5,3},{6,0},{7,1},{8,14},{9,15},{10,... | collective-permute-start | bytes 983048 | tf_op jit(solution)/shard_map/ppermute | solution.py:547
  143.8 12.4 %collective-permute-start.26 = (bf16[128,512]{1,0:T(8,128)(2,1)}, bf16[128,512]{1,0:T(8,128)(2,1)S(1)}, u32[]{:S(2)}, u32[]{:S(2)}) collective-permute-start(bf16[128,512]{1,0:T(8,128)(2,1)} %get-tuple-element.202), channel_id=1, source_target_pairs={{0,16},{4,20},{8,24},{12,28},{16,0},{20,4},{24,8},{28,12},{1,17},{... | collective-permute-start | bytes 393224 | tf_op jit(solution)/shard_map/ppermute | solution.py:482
  148.4 7.8 %collective-permute-start.27 = (bf16[128,512]{1,0:T(8,128)(2,1)}, bf16[128,512]{1,0:T(8,128)(2,1)S(1)}, u32[]{:S(2)}, u32[]{:S(2)}) collective-permute-start(bf16[128,512]{1,0:T(8,128)(2,1)} %get-tuple-element.203), channel_id=1, source_target_pairs={{0,24},{4,28},{8,16},{12,20},{16,8},{20,12},{24,0},{28,4},{1,25},{... | collective-permute-start | bytes 393224 | tf_op jit(solution)/shard_map/ppermute | solution.py:482
  163.1 15.8 %collective-permute-start.32 = (bf16[864,1024]{1,0:T(8,128)(2,1)S(1)}, bf16[864,1024]{1,0:T(8,128)(2,1)S(1)}, u32[]{:S(2)}, u32[]{:S(2)}) collective-permute-start(bf16[864,1024]{1,0:T(8,128)(2,1)S(1)} %copy-done.2), channel_id=1, source_target_pairs={{0,1},{1,0},{2,3},{3,2},{4,5},{5,4},{6,7},{7,6},{8,9},{9,8},{10,11... | collective-permute-start | bytes 5308424 | tf_op jit(solution)/shard_map/ppermute | solution.py:482
  163.1 11.0 %collective-permute-start.33 = (f32[128,512]{1,0:T(8,128)}, f32[128,512]{1,0:T(8,128)}, u32[]{:S(2)}, u32[]{:S(2)}) collective-permute-start(f32[128,512]{1,0:T(8,128)} %get-tuple-element.219), channel_id=1, source_target_pairs={{0,8},{4,12},{8,0},{12,4},{16,24},{20,28},{24,16},{28,20},{1,9},{5... | collective-permute-start | bytes 786440 | tf_op jit(solution)/shard_map/ppermute | solution.py:482
  167.4 8.6 %collective-permute-start.29 = (f32[80,256]{1,0:T(8,128)}, f32[80,256]{1,0:T(8,128)}, u32[]{:S(2)}, u32[]{:S(2)}) collective-permute-start(f32[80,256]{1,0:T(8,128)} %get-tuple-element.258), channel_id=1, source_target_pairs={{0,8},{4,12},{8,0},{12,4},{16,24},{20,28},{24,16},{28,20},{1,9},{5... | collective-permute-start | bytes 245768 | tf_op jit(solution)/shard_map/ppermute | solution.py:482
  167.9 8.4 %collective-permute-start.30 = (f32[80,256]{1,0:T(8,128)}, f32[80,256]{1,0:T(8,128)}, u32[]{:S(2)}, u32[]{:S(2)}) collective-permute-start(f32[80,256]{1,0:T(8,128)} %get-tuple-element.257), channel_id=1, source_target_pairs={{0,16},{4,20},{8,24},{12,28},{16,0},{20,4},{24,8},{28,12},{1,17},{... | collective-permute-start | bytes 245768 | tf_op jit(solution)/shard_map/ppermute | solution.py:482
  169.5 9.4 %collective-permute-start.31 = (f32[80,256]{1,0:T(8,128)}, f32[80,256]{1,0:T(8,128)}, u32[]{:S(2)}, u32[]{:S(2)}) collective-permute-start(f32[80,256]{1,0:T(8,128)} %get-tuple-element.256), channel_id=1, source_target_pairs={{0,24},{4,28},{8,16},{12,20},{16,8},{20,12},{24,0},{28,4},{1,25},{... | collective-permute-start | bytes 245768 | tf_op jit(solution)/shard_map/ppermute | solution.py:482
  174.1 12.9 %collective-permute-start.37 = (f32[128,512]{1,0:T(8,128)}, f32[128,512]{1,0:T(8,128)S(1)}, u32[]{:S(2)}, u32[]{:S(2)}) collective-permute-start(f32[128,512]{1,0:T(8,128)} %get-tuple-element.230), channel_id=1, source_target_pairs={{0,8},{4,12},{8,0},{12,4},{16,24},{20,28},{24,16},{28,20},{1,9},{5... | collective-permute-start | bytes 786440 | tf_op jit(solution)/shard_map/ppermute | solution.py:482
  176.0 9.3 %collective-permute-start.38 = (bf16[128,512]{1,0:T(8,128)(2,1)}, bf16[128,512]{1,0:T(8,128)(2,1)S(1)}, u32[]{:S(2)}, u32[]{:S(2)}) collective-permute-start(bf16[128,512]{1,0:T(8,128)(2,1)} %get-tuple-element.231), channel_id=1, source_target_pairs={{0,16},{4,20},{8,24},{12,28},{16,0},{20,4},{24,8},{28,12},{1,17},{... | collective-permute-start | bytes 393224 | tf_op jit(solution)/shard_map/ppermute | solution.py:482
  185.3 8.0 %collective-permute-start.42 = (bf16[128,512]{1,0:T(8,128)(2,1)}, bf16[128,512]{1,0:T(8,128)(2,1)S(1)}, u32[]{:S(2)}, u32[]{:S(2)}) collective-permute-start(bf16[128,512]{1,0:T(8,128)(2,1)} %get-tuple-element.243), channel_id=1, source_target_pairs={{0,24},{4,28},{8,16},{12,20},{16,8},{20,12},{24,0},{28,4},{1,25},{... | collective-permute-start | bytes 393224 | tf_op jit(solution)/shard_map/ppermute | solution.py:482
  189.7 12.1 %collective-permute-start.39 = (bf16[80,1024]{1,0:T(8,128)(2,1)S(1)}, bf16[80,1024]{1,0:T(8,128)(2,1)S(1)}, u32[]{:S(2)}, u32[]{:S(2)}) collective-permute-start(bf16[80,1024]{1,0:T(8,128)(2,1)S(1)} %constant_dynamic-update-slice_fusion.4), channel_id=1, source_target_pairs={{0,4},{4,0},{8,12},{12,8},{16,20},{20,16},{24,28},{28,24},{1,5},{5... | collective-permute-start | bytes 491528 | tf_op jit(solution)/shard_map/ppermute | solution.py:482
  190.1 11.7 %collective-permute-start.40 = (bf16[80,1024]{1,0:T(8,128)(2,1)S(1)}, bf16[80,1024]{1,0:T(8,128)(2,1)S(1)}, u32[]{:S(2)}, u32[]{:S(2)}) collective-permute-start(bf16[80,1024]{1,0:T(8,128)(2,1)S(1)} %constant_dynamic-update-slice_fusion.4), channel_id=1, source_target_pairs={{0,2},{1,3},{2,0},{3,1},{4,6},{5,7},{6,4},{7,5},{8,10},{9,11},{10,... | collective-permute-start | bytes 491528 | tf_op jit(solution)/shard_map/ppermute | solution.py:547
  190.7 11.2 %collective-permute-start.41 = (bf16[80,1024]{1,0:T(8,128)(2,1)S(1)}, bf16[80,1024]{1,0:T(8,128)(2,1)S(1)}, u32[]{:S(2)}, u32[]{:S(2)}) collective-permute-start(bf16[80,1024]{1,0:T(8,128)(2,1)S(1)} %constant_dynamic-update-slice_fusion.4), channel_id=1, source_target_pairs={{0,6},{1,7},{2,4},{3,5},{4,2},{5,3},{6,0},{7,1},{8,14},{9,15},{10,... | collective-permute-start | bytes 491528 | tf_op jit(solution)/shard_map/ppermute | solution.py:547
  (39 other events, 254.6 us)

commit v14 on v13

--- a/solution.py
+++ b/solution.py
@@ -333,6 +333,33 @@
     )(place, *ins)
 
 
+def split_kernel(count, place_ref, *refs):
+    total = refs[0][...]
+    for ref in refs[1:count]:
+        total = total + ref[...]
+    outs = refs[count:]
+    cols = outs[0].shape[1]
+    place = place_ref[0]
+    for j, out_ref in enumerate(outs):
+        block = total[:, :cols]
+        for b in range(1, len(outs)):
+            block = jnp.where((place ^ j) == b, total[:, b * cols : (b + 1) * cols], block)
+        out_ref[...] = block
+
+
+def split_call(place, parts, blocks):
+    rows, cols = parts[0].shape
+    return pl.pallas_call(
+        functools.partial(split_kernel, len(parts)),
+        in_specs=[SCALARS] + [pl.BlockSpec((rows, cols), lambda: (0, 0))] * len(parts),
+        out_specs=[pl.BlockSpec((rows, cols // blocks), lambda: (0, 0))] * blocks,
+        out_shape=[jax.ShapeDtypeStruct((rows, cols // blocks), F32)] * blocks,
+        compiler_params=params(),
+        cost_estimate=cost(1e6, 2e6),
+        name="split_sum",
+    )(place, *parts)
+
+
 def result_kernel(count, *refs):
     halves, qkv_ref, out_ref = (refs[:count], refs[count:-2]), refs[-2], refs[-1]
     first, second = [functools.reduce(lambda a, b: a + b, [r[...].astype(F32) for r in half]) for half in halves]
@@ -551,12 +578,8 @@
     arrived = [hop(part, f, b) for part, (f, b) in zip(parts[1:], hops)]
     arrived, beside = together(arrived, beside)
     beside = after[0](*beside)
-    total = parts[0]
-    for part in arrived:
-        total = total + part
     cols = width // highs
-    part = lax.dynamic_slice_in_dim(total, high * cols, cols, 1)
-    away = [lax.dynamic_slice_in_dim(total, (high ^ j) * cols, cols, 1) for j in range(1, highs)]
+    part, *away = split_call(high.reshape(1), [parts[0], *arrived], highs)
     arrived = [swap(a, "dp", dp, 2 * (j + 1)) for j, a in enumerate(away)]
     arrived, beside = together(arrived, beside)
     for block in arrived:
@@ -671,28 +694,28 @@
     stem_made, coming[0], last_keeps = together(
         tail_call(core, back[0], back_far, emb, both[0], cols, gain), coming[0], [x[3] for x in crossing]
     )
-    keeps = [[keep[0]] + [x[2] for x in arrived], [keep[1]] + list(last_keeps)]
     stem_keep, *stem_recv = stem_made
     stem_recv = [swap(x, "group", group, 1) for x in stem_recv]
     kinds = [F32 if j < 2 else BF16 for j in range(dp // 2)]
     second_leg = lambda c: combine_call(high, [[x] for x in keeps[c] + [coming[c]]], kinds)
     spread = lambda blocks, js: [swap(blocks[j], "dp", dp, 2 * j) for j in js]
+    stem_recv = together(*stem_recv)
+    keeps = [[keep[0]] + [x[2] for x in arrived], [keep[1]] + list(last_keeps)]
+    stem_parts = halve_stem(stem_recv, stem_keep, group)
+    _, coming[0], keeps = together(stem_parts, coming[0], keeps)
     first = second_leg(0)
-    stem_recv, share = together(stem_recv, first[0])
     first_rest = spread(first, rests[1:])
-    stem_parts = halve_stem(stem_recv, stem_keep, group)
-    _, coming[1], keeps[1] = together(stem_parts, coming[1], keeps[1])
     second = second_leg(1)
     near = dp // 2 * 3 // 4
-    beside = [mixed_call(packs, weights), share, *first_rest, second[0]]
+    beside = [mixed_call(packs, weights), first[0], *first_rest, second[0]]
     def after_first(mixed, *arrived):
-        return [swap(mixed, "group", group, 1), *arrived[:-1], *spread(first, [1]), arrived[-1]]
+        output = output_call(counts, swap(mixed, "group", group, 1), emb, packs, weights)
+        return [output, *arrived[:-1], *spread(first, [1]), arrived[-1]]
 
     def after_second(*arrived):
         return [*arrived, *spread(second, [1, *range(2, near)])]
 
-    def last(mixed, *arrived):
-        output = output_call(counts, mixed, emb, packs, weights)
+    def last(output, *arrived):
         arrived = [*arrived, *spread(second, range(near, dp // 2))]
         half = len(arrived) // 2
         return output, *result_call(arrived[:half], arrived[half:])

time: 208 us -> 203 us (0.976)
  other arithmetic: 10.8 us -> 8.22 us
  Pallas kernels: 92.9 us -> 95 us
    ppermute x33, waiting for transfers between devices: 27.7 us -> 24.6 us  [swap(): return lax.ppermute(x, axis, [(i, i ^ bit) for i in range(size)])]
  transfers between devices with their start and end apart: 44 -> 44, of which waited for: 20 -> 21; matrix products, arithmetic and copies ran while one was open for 4% -> 2% of each run, Pallas kernels for 44% -> 46%
where the time goes in v14:
time: 203 us; the launch traced here: 202 us
  Pallas kernels  95 us (47%)
  waiting for transfers between devices  50.4 us (25%)
  starting transfers between devices  42 us (21%)
  other arithmetic  8.22 us (4%)
  local copies, waits for them, and re-layouts  5.73 us (3%)
    pallas_call x2, Pallas kernels, attention_call(): pl.pallas_call(functools.partial(attention_kernel, packs, len(blocks), dp...  54.5 us
    ppermute x33, starting transfers between devices, swap(): return lax.ppermute(x, axis, [(i, i ^ bit) for i in range(size)])  28.2 us
    ppermute x33, waiting for transfers between devices, swap(): return lax.ppermute(x, axis, [(i, i ^ bit) for i in range(size)])  24.6 us
    ppermute x4, waiting for transfers between devices, send(): moved = [lax.ppermute(self.ahead[-1], self.axis, self.forward)]  19.7 us
    pallas_call x1, Pallas kernels, tail_call(): pl.pallas_call(tail_kernel, grid=(tokens // rows,), in_specs=[SCALARS, pe...  9.06 us
    pallas_call x1, Pallas kernels, stem_call(): pl.pallas_call(stem_kernel, grid=(scenes // block,), in_specs=[pl.BlockSp...  8.27 us
    pallas_call x3, Pallas kernels, combine_call(): pl.pallas_call(functools.partial(combine_kernel, [len(part) for part in p...  8 us
    ppermute x4, starting transfers between devices, send(): moved = [lax.ppermute(self.ahead[-1], self.axis, self.forward)]  6.25 us
  transfers between devices with their start and end apart: 44, of which 21 were waited for; matrix products, arithmetic and copies ran while one was open for 2% of the time, Pallas kernels for 46%

profile of v14, /device:TPU:0, one launch (start us, length us, event | category | flops | bytes accessed | tf_op | source)
XLA Modules:
  0.0 202.2 jit_solution(13825924221008347981)
XLA Ops:
  0.6 1.7 pack_weights.1.refs_2_
  2.3 2.9 %collective-permute-start.1 = (bf16[128,1024]{1,0:T(8,128)(2,1)}, bf16[128,1024]{1,0:T(8,128)(2,1)}, u32[]{:S(2)}, u32[]{:S(2)}) collective-permute-start(bf16[128,1024]{1,0:T(8,128)(2,1)} %pack_weights.1.refs_2_), channel_id=1, source_target_pairs={{0,2},{1,3},{2,0},{3,1},{4,6},{5,7},{6,4},{7,5},{8,10},{9,11},{10,... | collective-permute-start | bytes 786440 | tf_op jit(solution)/shard_map/ppermute | solution.py:509
  5.3 8.3 %stem_norm.1 = (bf16[6,144,1024]{2,1,0:T(8,128)(2,1)}, bf16[2,6,144,1024]{3,2,1,0:T(8,128)(2,1)}, bf16[6,144,256]{2,1,0:T(8,128)(2,1)}) custom-call(s32[3,6]{1,0:T(4,128)} %bitcast.29, s32[6,3,48]{2,1,0:T(4,128)} %idx_ref.1, bf16[6,144,640]{2,1,0:T(8,128)(2,1)} %patch_ref.1, bf16[640,1024]{1,0:T(8,128)(2,1)} %w_ref.1, f32[1,1024]{1,0:T(1,128)} %bitcast.32, ...), custom_call_target="tpu_custom_call" | custom-call | flops 8000000 | bytes 12000 | tf_op jit(solution)/shard_map/stem_norm/pallas_call | solution.py:98
  17.2 6.0 %collective-permute-done.2.refs_1_ = bf16[128,1024]{1,0:T(8,128)(2,1)} collective-permute-done((bf16[128,1024]{1,0:T(8,128)(2,1)}, bf16[128,1024]{1,0:T(8,128)(2,1)}, u32[]{:S(2)}, u32[]{:S(2)}) %collective-permute-start.2) | collective-permute-done | bytes 262176 | tf_op jit(solution)/shard_map/ppermute | solution.py:525
  27.1 4.7 %collective-permute-done.5.refs_2_ = bf16[128,1024]{1,0:T(8,128)(2,1)S(1)} collective-permute-done((bf16[128,1024]{1,0:T(8,128)(2,1)}, bf16[128,1024]{1,0:T(8,128)(2,1)S(1)}, u32[]{:S(2)}, u32[]{:S(2)}) %collective-permute-start.5) | collective-permute-done | bytes 262176 | tf_op jit(solution)/shard_map/ppermute | solution.py:525
  35.7 3.9 %collective-permute-done.7.refs_3_ = bf16[128,1024]{1,0:T(8,128)(2,1)} collective-permute-done((bf16[128,1024]{1,0:T(8,128)(2,1)S(1)}, bf16[128,1024]{1,0:T(8,128)(2,1)}, u32[]{:S(2)}, u32[]{:S(2)}) %collective-permute-start.7) | collective-permute-done | bytes 262176 | tf_op jit(solution)/shard_map/ppermute | solution.py:525
  42.6 5.2 %collective-permute-done.10.refs_4_ = bf16[128,1024]{1,0:T(8,128)(2,1)} collective-permute-done((bf16[128,1024]{1,0:T(8,128)(2,1)}, bf16[128,1024]{1,0:T(8,128)(2,1)}, u32[]{:S(2)}, u32[]{:S(2)}) %collective-permute-start.10) | collective-permute-done | bytes 262176 | tf_op jit(solution)/shard_map/ppermute | solution.py:525
  47.7 1.9 pad_maximum_fusion
  52.2 22.8 %attention.2 = (bf16[1728,1024]{1,0:T(8,128)(2,1)}, bf16[1024,1024]{1,0:T(8,128)(2,1)}, bf16[512,512]{1,0:T(8,128)(2,1)}, bf16[512,512]{1,0:T(8,128)(2,1)}, bf16...) custom-call(s32[2,3,6]{2,1,0:T(4,128)} %pad_add_fusion.cnt_ref, s32[8]{0:T(128)} %compare_select_fusion.2.owner_ref, ...), custom_call_target="tpu_custom_call" | custom-call | flops 20000000 | bytes 14000 | tf_op jit(solution)/shard_map/attention/pallas_call | solution.py:277
  75.0 3.6 %collective-permute-done.13.refs_6_ = bf16[128,1024]{1,0:T(8,128)(2,1)} collective-permute-done((bf16[128,1024]{1,0:T(8,128)(2,1)}, bf16[128,1024]{1,0:T(8,128)(2,1)}, u32[]{:S(2)}, u32[]{:S(2)}) %collective-permute-start.13) | collective-permute-done | bytes 262176 | tf_op jit(solution)/shard_map/ppermute | solution.py:509
  81.1 31.7 %attention.3 = (bf16[1728,1024]{1,0:T(8,128)(2,1)}, bf16[1024,1024]{1,0:T(8,128)(2,1)}, f32[512,512]{1,0:T(8,128)}, f32[512,512]{1,0:T(8,128)}, f32[512,512]{1,0...) custom-call(s32[2,3,6]{2,1,0:T(4,128)} %pad_add_fusion.cnt_ref, ...), custom_call_target="tpu_custom_call" | custom-call | flops 20000000 | bytes 14000 | tf_op jit(solution)/shard_map/attention/pallas_call | solution.py:277
  115.1 2.2 %add_convert_fusion.1 = bf16[512,512]{1,0:T(8,128)(2,1)} fusion(f32[512,512]{1,0:T(8,128)} %get-tuple-element.188, bf16[512,512]{1,0:T(8,128)(2,1)S(1)} %collective-permute-done.15), kind=kLoop, calls=%fused_computation.2 | loop fusion | flops 786432 | bytes 2097152 | tf_op jit(solution)/shard_map/convert_element_type | solution.py:693
  119.0 9.1 %tail.1 = (f32[320,1024]{1,0:T(8,128)}, f32[320,512]{1,0:T(8,128)}, f32[320,512]{1,0:T(8,128)}) custom-call(s32[1]{0:T(128)} %bitcast.2.core_ref, f32[864,1024]{1,0:T(8,128)} %get-tuple-element.181.own_ref, bf16[864,1024]{1,0:T(8,128)(2,1)} %copy-done.3, bf16[864,1024]{1,0:T(8,128)(2,1)} %bitcast.22, bf16[2,864,1024]{2,1,0:T(8,128)(2,1)} %bitcast.21, ...), custom_call_target="tpu_custom_call" | custom-call | flops 10000000 | bytes 12000 | tf_op jit(solution)/shard_map/tail/pallas_call | solution.py:464
  128.3 3.4 %collective-permute-done.19.refs_2_ = bf16[512,512]{1,0:T(8,128)(2,1)} collective-permute-done((bf16[512,512]{1,0:T(8,128)(2,1)}, bf16[512,512]{1,0:T(8,128)(2,1)}, u32[]{:S(2)}, u32[]{:S(2)}) %collective-permute-start.19) | collective-permute-done | bytes 524320 | tf_op jit(solution)/shard_map/ppermute | solution.py:509
  135.8 2.9 %combine.3 = (f32[80,1024]{1,0:T(8,128)}, f32[80,1024]{1,0:T(8,128)}, f32[80,1024]{1,0:T(8,128)}, f32[80,1024]{1,0:T(8,128)}) custom-call(s32[1]{0:T(128)} %bitcast.1.place_ref, f32[320,1024]{1,0:T(8,128)} %get-tuple-element.191.refs_0_, f32[320,512]{1,0:T(8,128)} %copy-done.7, f32[320,512]{1,0:T(8,128)} %copy-done.8), custom_call_target="tpu_custom_call" | custom-call | flops 1000 | bytes 5000 | tf_op jit(solution)/shard_map/combine/pallas_call | solution.py:325
  139.7 2.5 %collective-permute-start.25 = (f32[80,1024]{1,0:T(8,128)}, f32[80,1024]{1,0:T(8,128)}, u32[]{:S(2)}, u32[]{:S(2)}) collective-permute-start(f32[80,1024]{1,0:T(8,128)} %get-tuple-element.199), channel_id=1, source_target_pairs={{0,6},{1,7},{2,4},{3,5},{4,2},{5,3},{6,0},{7,1},{8,14},{9,15},{10,... | collective-permute-start | bytes 983048 | tf_op jit(solution)/shard_map/ppermute | solution.py:574
  142.2 2.5 %combine.4 = (f32[128,512]{1,0:T(8,128)}, f32[128,512]{1,0:T(8,128)}, bf16[128,512]{1,0:T(8,128)(2,1)}, bf16[128,512]{1,0:T(8,128)(2,1)}) custom-call(s32[1]{0:T(128)} %bitcast.place_ref, f32[512,512]{1,0:T(8,128)} %get-tuple-element.207.refs_0_, bf16[512,512]{1,0:T(8,128)(2,1)} %copy-done.9, bf16[512,512]{1,0:T(8,128)(2,1)} %collective-permute-done.19.refs_2_), custom_call_target="tpu_custom_call" | custom-call | flops 1000 | bytes 5000 | tf_op jit(solution)/shard_map/combine/pallas_call | solution.py:325
  148.7 3.7 %mixed.1 = bf16[864,1024]{1,0:T(8,128)(2,1)} custom-call(bf16[1728,1024]{1,0:T(8,128)(2,1)} %get-tuple-element.163.refs_0_, bf16[1728,1024]{1,0:T(8,128)(2,1)} %get-tuple-element.200.refs_1_, bf16[1024,1024]{1,0:T(8,128)(2,1)} %get-tuple-element.164.refs_1_.refs_2_, bf16[1024,1024]{1,0:T(8,128)(2,1)} %get-tuple-element.201.refs_3_), custom_call_target="tpu_custom_call" | custom-call | flops 2000000 | bytes 5000 | tf_op jit(solution)/shard_map/mixed/pallas_call | solution.py:410
  152.4 2.6 %combine.5 = (f32[128,512]{1,0:T(8,128)}, f32[128,512]{1,0:T(8,128)}, bf16[128,512]{1,0:T(8,128)(2,1)}, bf16[128,512]{1,0:T(8,128)(2,1)}) custom-call(s32[1]{0:T(128)} %bitcast.place_ref, f32[512,512]{1,0:T(8,128)} %get-tuple-element.213.refs_0_, bf16[512,512]{1,0:T(8,128)(2,1)} %collective-permute-done.20.refs_1_, bf16[512,512]{1,0:T(8,128)(2,1)} %copy-done.10), custom_call_target="tpu_custom_call" | custom-call | flops 1000 | bytes 5000 | tf_op jit(solution)/shard_map/combine/pallas_call | solution.py:325
  155.0 2.2 %collective-permute-done.26.refs_1_ = bf16[128,512]{1,0:T(8,128)(2,1)S(1)} collective-permute-done((bf16[128,512]{1,0:T(8,128)(2,1)}, bf16[128,512]{1,0:T(8,128)(2,1)S(1)}, u32[]{:S(2)}, u32[]{:S(2)}) %collective-permute-start.26) | collective-permute-done | bytes 131104 | tf_op jit(solution)/shard_map/ppermute | solution.py:509
  157.2 3.1 %collective-permute-done.23.refs_1_ = f32[80,1024]{1,0:T(8,128)S(1)} collective-permute-done((f32[80,1024]{1,0:T(8,128)}, f32[80,1024]{1,0:T(8,128)S(1)}, u32[]{:S(2)}, u32[]{:S(2)}) %collective-permute-start.23) | collective-permute-done | bytes 327712 | tf_op jit(solution)/shard_map/ppermute | solution.py:509
  162.6 2.1 %split_sum.1 = (f32[80,256]{1,0:T(8,128)}, f32[80,256]{1,0:T(8,128)}, f32[80,256]{1,0:T(8,128)}, f32[80,256]{1,0:T(8,128)}) custom-call(s32[1]{0:T(128)} %bitcast.place_ref, f32[80,1024]{1,0:T(8,128)} %get-tuple-element.196.refs_0_, f32[80,1024]{1,0:T(8,128)} %copy-done.13, f32[80,1024]{1,0:T(8,128)} %copy-done.14, f32[80,1024]{1,0:T(8,128)} %collective-permute-done.25.refs_3_), custom_call_target="tpu_custom_call" | custom-call | flops 1000 | bytes 2000 | tf_op jit(solution)/shard_map/split_sum/pallas_call | solution.py:352
  166.8 2.3 %collective-permute-start.31 = (f32[80,256]{1,0:T(8,128)}, f32[80,256]{1,0:T(8,128)}, u32[]{:S(2)}, u32[]{:S(2)}) collective-permute-start(f32[80,256]{1,0:T(8,128)} %get-tuple-element.224), channel_id=1, source_target_pairs={{0,24},{4,28},{8,16},{12,20},{16,8},{20,12},{24,0},{28,4},{1,25},{... | collective-permute-start | bytes 245768 | tf_op jit(solution)/shard_map/ppermute | solution.py:509
  170.3 5.5 %layer_output.1 = bf16[864,1024]{1,0:T(8,128)(2,1)} custom-call(s32[3,6]{1,0:T(4,128)} %bitcast.30, bf16[864,1024]{1,0:T(8,128)(2,1)} %copy-done.1, bf16[864,1024]{1,0:T(8,128)(2,1)} %bitcast.23, bf16[1728,1024]{1,0:T(8,128)(2,1)} %get-tuple-element.163.refs_0_, bf16[1728,1024]{1,0:T(8,128)(2,1)} %get-tuple-element.200.refs_1_, ...), custom_call_target="tpu_custom_call" | custom-call | flops 5000000 | bytes 10000 | tf_op jit(solution)/shard_map/layer_output/pallas_call | solution.py:495
  179.1 1.7 collective-permute-start.35
  182.3 2.3 %collective-permute-done.38.refs_6_ = bf16[128,512]{1,0:T(8,128)(2,1)S(1)} collective-permute-done((bf16[128,512]{1,0:T(8,128)(2,1)S(1)}, bf16[128,512]{1,0:T(8,128)(2,1)S(1)}, u32[]{:S(2)}, u32[]{:S(2)}) %collective-permute-start.38) | collective-permute-done | bytes 131104 | tf_op jit(solution)/shard_map/ppermute | solution.py:509
  185.2 3.7 %collective-permute-done.35 = bf16[80,256]{1,0:T(8,128)(2,1)S(1)} collective-permute-done((bf16[80,256]{1,0:T(8,128)(2,1)S(1)}, bf16[80,256]{1,0:T(8,128)(2,1)S(1)}, u32[]{:S(2)}, u32[]{:S(2)}) %collective-permute-start.35) | collective-permute-done | bytes 40992 | tf_op jit(solution)/shard_map/ppermute | solution.py:509
  189.4 1.7 collective-permute-start.40
  193.2 2.3 %weight_results.1 = (f32[3,128,256]{2,1,0:T(8,128)}, f32[256,128]{1,0:T(8,128)}) custom-call(f32[128,512]{1,0:T(8,128)} %get-tuple-element.246.refs_0_, bf16[128,512]{1,0:T(8,128)(2,1)} %copy-done.18, bf16[128,512]{1,0:T(8,128)(2,1)} %copy-done.19, f32[128,512]{1,0:T(8,128)} %collective-permute-done.33.refs_3_, f32[128,512]{1,0:T(8,128)} %get-tuple-element.250.refs_4_, ...), custom_call_target="tpu_custom_call" | custom-call | flops 1000 | bytes 2000 | tf_op jit(solution)/shard_map/weight_results/pallas_call | solution.py:375
  196.1 2.0 collective-permute-done.41
  198.3 2.1 %collective-permute-done.43 = bf16[320,1024]{1,0:T(8,128)(2,1)S(1)} collective-permute-done((bf16[320,1024]{1,0:T(8,128)(2,1)S(1)}, bf16[320,1024]{1,0:T(8,128)(2,1)S(1)}, u32[]{:S(2)}, u32[]{:S(2)}) %collective-permute-start.43) | collective-permute-done | bytes 655392 | tf_op jit(solution)/shard_map/ppermute | solution.py:509
  200.4 1.8 maximum_convert_fusion
  (139 shorter events, 47.4 us)
Async XLA Ops:
  2.3 11.8 %collective-permute-start.1 = (bf16[128,1024]{1,0:T(8,128)(2,1)}, bf16[128,1024]{1,0:T(8,128)(2,1)}, u32[]{:S(2)}, u32[]{:S(2)}) collective-permute-start(bf16[128,1024]{1,0:T(8,128)(2,1)} %pack_weights.1.refs_2_), channel_id=1, source_target_pairs={{0,2},{1,3},{2,0},{3,1},{4,6},{5,7},{6,4},{7,5},{8,10},{9,11},{10,... | collective-permute-start | bytes 786440 | tf_op jit(solution)/shard_map/ppermute | solution.py:509
  5.3 8.3 %collective-permute-start = (s32[3,6]{1,0:T(4,128)}, s32[3,6]{1,0:T(4,128)S(1)}, u32[]{:S(2)}, u32[]{:S(2)}) collective-permute-start(s32[3,6]{1,0:T(4,128)} %bitcast.28), channel_id=1, source_target_pairs={{0,1},{1,0},{2,3},{3,2},{4,5},{5,4},{6,7},{7,6},{8,9},{9,8},{10,11... | collective-permute-start | bytes 224 | tf_op jit(solution)/shard_map/ppermute | solution.py:509
  14.2 10.3 %collective-permute-start.4 = (bf16[2,864,1024]{2,1,0:T(8,128)(2,1)}, bf16[2,864,1024]{2,1,0:T(8,128)(2,1)S(1)}, u32[]{:S(2)}, u32[]{:S(2)}) collective-permute-start(bf16[2,864,1024]{2,1,0:T(8,128)(2,1)} %bitcast.16), channel_id=1, source_target_pairs={{0,1},{1,0},{2,3},{3,2},{4,5},{5,4},{6,7},{7,6},{8,9},{9,8},{10,11... | collective-permute-start | bytes 10616840 | tf_op jit(solution)/shard_map/ppermute | solution.py:509
  14.7 8.5 %collective-permute-start.2 = (bf16[128,1024]{1,0:T(8,128)(2,1)}, bf16[128,1024]{1,0:T(8,128)(2,1)}, u32[]{:S(2)}, u32[]{:S(2)}) collective-permute-start(bf16[128,1024]{1,0:T(8,128)(2,1)} %collective-permute-done.1.refs_0_), channel_id=1, source_target_pairs={{0,8},{8,16},{16,24},{24,28},{28,20},{20,12},{12,4},{4,0},{1,9},{9... | collective-permute-start | bytes 786440 | tf_op jit(solution)/shard_map/ppermute | solution.py:525
  16.3 8.2 %collective-permute-start.3 = (bf16[128,1024]{1,0:T(8,128)(2,1)}, bf16[128,1024]{1,0:T(8,128)(2,1)}, u32[]{:S(2)}, u32[]{:S(2)}) collective-permute-start(bf16[128,1024]{1,0:T(8,128)(2,1)} %collective-permute-done.1.refs_0_), channel_id=1, source_target_pairs={{8,0},{16,8},{24,16},{28,24},{20,28},{12,20},{4,12},{0,4},{9,1},{1... | collective-permute-start | bytes 786440 | tf_op jit(solution)/shard_map/ppermute | solution.py:527
  26.6 9.1 %collective-permute-start.9 = (bf16[128,1024]{1,0:T(8,128)(2,1)}, bf16[128,1024]{1,0:T(8,128)(2,1)S(1)}, u32[]{:S(2)}, u32[]{:S(2)}) collective-permute-start(bf16[128,1024]{1,0:T(8,128)(2,1)} %collective-permute-done.2.refs_1_), channel_id=1, source_target_pairs={{0,2},{1,3},{2,0},{3,1},{4,6},{5,7},{6,4},{7,5},{8,10},{9,11},{10,... | collective-permute-start | bytes 786440 | tf_op jit(solution)/shard_map/ppermute | solution.py:509
  35.1 7.5 %collective-permute-start.11 = (bf16[128,1024]{1,0:T(8,128)(2,1)S(1)}, bf16[128,1024]{1,0:T(8,128)(2,1)}, u32[]{:S(2)}, u32[]{:S(2)}) collective-permute-start(bf16[128,1024]{1,0:T(8,128)(2,1)S(1)} %collective-permute-done.5.refs_2_), channel_id=1, source_target_pairs={{0,2},{1,3},{2,0},{3,1},{4,6},{5,7},{6,4},{7,5},{8,10},{9,11},{10,... | collective-permute-start | bytes 786440 | tf_op jit(solution)/shard_map/ppermute | solution.py:509
  49.6 28.9 %collective-permute-start.14 = (bf16[384,1024]{1,0:T(8,128)(2,1)}, bf16[384,1024]{1,0:T(8,128)(2,1)}, u32[]{:S(2)}, u32[]{:S(2)}) collective-permute-start(bf16[384,1024]{1,0:T(8,128)(2,1)} %pad_maximum_fusion), channel_id=1, source_target_pairs={{0,2},{1,3},{2,0},{3,1},{4,6},{5,7},{6,4},{7,5},{8,10},{9,11},{10,... | collective-permute-start | bytes 2359304 | tf_op jit(solution)/shard_map/ppermute | solution.py:509
  50.2 24.8 %collective-permute-start.12 = (bf16[128,1024]{1,0:T(8,128)(2,1)}, bf16[128,1024]{1,0:T(8,128)(2,1)}, u32[]{:S(2)}, u32[]{:S(2)}) collective-permute-start(bf16[128,1024]{1,0:T(8,128)(2,1)} %collective-permute-done.7.refs_3_), channel_id=1, source_target_pairs={{0,2},{1,3},{2,0},{3,1},{4,6},{5,7},{6,4},{7,5},{8,10},{9,11},{10,... | collective-permute-start | bytes 786440 | tf_op jit(solution)/shard_map/ppermute | solution.py:509
  51.6 26.9 %collective-permute-start.13 = (bf16[128,1024]{1,0:T(8,128)(2,1)}, bf16[128,1024]{1,0:T(8,128)(2,1)}, u32[]{:S(2)}, u32[]{:S(2)}) collective-permute-start(bf16[128,1024]{1,0:T(8,128)(2,1)} %collective-permute-done.10.refs_4_), channel_id=1, source_target_pairs={{0,2},{1,3},{2,0},{3,1},{4,6},{5,7},{6,4},{7,5},{8,10},{9,11},{10,... | collective-permute-start | bytes 786440 | tf_op jit(solution)/shard_map/ppermute | solution.py:509
  78.6 34.3 %collective-permute-start.15 = (bf16[512,512]{1,0:T(8,128)(2,1)}, bf16[512,512]{1,0:T(8,128)(2,1)S(1)}, u32[]{:S(2)}, u32[]{:S(2)}) collective-permute-start(bf16[512,512]{1,0:T(8,128)(2,1)} %get-tuple-element.178), channel_id=1, source_target_pairs={{0,2},{1,3},{2,0},{3,1},{4,6},{5,7},{6,4},{7,5},{8,10},{9,11},{10,... | collective-permute-start | bytes 1572872 | tf_op jit(solution)/shard_map/ppermute | solution.py:509
  79.1 33.7 %collective-permute-start.16 = (bf16[512,512]{1,0:T(8,128)(2,1)}, bf16[512,512]{1,0:T(8,128)(2,1)S(1)}, u32[]{:S(2)}, u32[]{:S(2)}) collective-permute-start(bf16[512,512]{1,0:T(8,128)(2,1)} %get-tuple-element.179), channel_id=1, source_target_pairs={{0,2},{1,3},{2,0},{3,1},{4,6},{5,7},{6,4},{7,5},{8,10},{9,11},{10,... | collective-permute-start | bytes 1572872 | tf_op jit(solution)/shard_map/ppermute | solution.py:509
  80.6 32.3 %collective-permute-start.17 = (bf16[512,512]{1,0:T(8,128)(2,1)}, bf16[512,512]{1,0:T(8,128)(2,1)S(1)}, u32[]{:S(2)}, u32[]{:S(2)}) collective-permute-start(bf16[512,512]{1,0:T(8,128)(2,1)} %get-tuple-element.180), channel_id=1, source_target_pairs={{0,2},{1,3},{2,0},{3,1},{4,6},{5,7},{6,4},{7,5},{8,10},{9,11},{10,... | collective-permute-start | bytes 1572872 | tf_op jit(solution)/shard_map/ppermute | solution.py:509
  113.7 14.7 %collective-permute-start.20 = (bf16[512,512]{1,0:T(8,128)(2,1)}, bf16[512,512]{1,0:T(8,128)(2,1)}, u32[]{:S(2)}, u32[]{:S(2)}) collective-permute-start(bf16[512,512]{1,0:T(8,128)(2,1)} %get-tuple-element.190), channel_id=1, source_target_pairs={{0,2},{1,3},{2,0},{3,1},{4,6},{5,7},{6,4},{7,5},{8,10},{9,11},{10,... | collective-permute-start | bytes 1572872 | tf_op jit(solution)/shard_map/ppermute | solution.py:509
  117.3 14.4 %collective-permute-start.19 = (bf16[512,512]{1,0:T(8,128)(2,1)}, bf16[512,512]{1,0:T(8,128)(2,1)}, u32[]{:S(2)}, u32[]{:S(2)}) collective-permute-start(bf16[512,512]{1,0:T(8,128)(2,1)} %add_convert_fusion.1), channel_id=1, source_target_pairs={{0,4},{4,0},{8,12},{12,8},{16,20},{20,16},{24,28},{28,24},{1,5},{5... | collective-permute-start | bytes 1572872 | tf_op jit(solution)/shard_map/ppermute | solution.py:509
  132.4 14.9 %collective-permute-start.28 = (bf16[512,512]{1,0:T(8,128)(2,1)S(1)}, bf16[512,512]{1,0:T(8,128)(2,1)S(1)}, u32[]{:S(2)}, u32[]{:S(2)}) collective-permute-start(bf16[512,512]{1,0:T(8,128)(2,1)S(1)} %add_convert_fusion), channel_id=1, source_target_pairs={{0,4},{4,0},{8,12},{12,8},{16,20},{20,16},{24,28},{28,24},{1,5},{5... | collective-permute-start | bytes 1572872 | tf_op jit(solution)/shard_map/ppermute | solution.py:509
  138.7 21.6 %collective-permute-start.23 = (f32[80,1024]{1,0:T(8,128)}, f32[80,1024]{1,0:T(8,128)S(1)}, u32[]{:S(2)}, u32[]{:S(2)}) collective-permute-start(f32[80,1024]{1,0:T(8,128)} %get-tuple-element.197), channel_id=1, source_target_pairs={{0,4},{4,0},{8,12},{12,8},{16,20},{20,16},{24,28},{28,24},{1,5},{5... | collective-permute-start | bytes 983048 | tf_op jit(solution)/shard_map/ppermute | solution.py:509
  139.2 21.1 %collective-permute-start.24 = (f32[80,1024]{1,0:T(8,128)}, f32[80,1024]{1,0:T(8,128)S(1)}, u32[]{:S(2)}, u32[]{:S(2)}) collective-permute-start(f32[80,1024]{1,0:T(8,128)} %get-tuple-element.198), channel_id=1, source_target_pairs={{0,2},{1,3},{2,0},{3,1},{4,6},{5,7},{6,4},{7,5},{8,10},{9,11},{10,... | collective-permute-start | bytes 983048 | tf_op jit(solution)/shard_map/ppermute | solution.py:574
  139.7 20.6 %collective-permute-start.25 = (f32[80,1024]{1,0:T(8,128)}, f32[80,1024]{1,0:T(8,128)}, u32[]{:S(2)}, u32[]{:S(2)}) collective-permute-start(f32[80,1024]{1,0:T(8,128)} %get-tuple-element.199), channel_id=1, source_target_pairs={{0,6},{1,7},{2,4},{3,5},{4,2},{5,3},{6,0},{7,1},{8,14},{9,15},{10,... | collective-permute-start | bytes 983048 | tf_op jit(solution)/shard_map/ppermute | solution.py:574
  144.7 12.5 %collective-permute-start.26 = (bf16[128,512]{1,0:T(8,128)(2,1)}, bf16[128,512]{1,0:T(8,128)(2,1)S(1)}, u32[]{:S(2)}, u32[]{:S(2)}) collective-permute-start(bf16[128,512]{1,0:T(8,128)(2,1)} %get-tuple-element.211), channel_id=1, source_target_pairs={{0,16},{4,20},{8,24},{12,28},{16,0},{20,4},{24,8},{28,12},{1,17},{... | collective-permute-start | bytes 393224 | tf_op jit(solution)/shard_map/ppermute | solution.py:509
  147.2 10.0 %collective-permute-start.27 = (bf16[128,512]{1,0:T(8,128)(2,1)}, bf16[128,512]{1,0:T(8,128)(2,1)S(1)}, u32[]{:S(2)}, u32[]{:S(2)}) collective-permute-start(bf16[128,512]{1,0:T(8,128)(2,1)} %get-tuple-element.212), channel_id=1, source_target_pairs={{0,24},{4,28},{8,16},{12,20},{16,8},{20,12},{24,0},{28,4},{1,25},{... | collective-permute-start | bytes 393224 | tf_op jit(solution)/shard_map/ppermute | solution.py:509
  161.1 8.0 %collective-permute-start.32 = (bf16[864,1024]{1,0:T(8,128)(2,1)S(1)}, bf16[864,1024]{1,0:T(8,128)(2,1)S(1)}, u32[]{:S(2)}, u32[]{:S(2)}) collective-permute-start(bf16[864,1024]{1,0:T(8,128)(2,1)S(1)} %copy-done.2), channel_id=1, source_target_pairs={{0,1},{1,0},{2,3},{3,2},{4,5},{5,4},{6,7},{7,6},{8,9},{9,8},{10,11... | collective-permute-start | bytes 5308424 | tf_op jit(solution)/shard_map/ppermute | solution.py:509
  161.1 14.7 %collective-permute-start.33 = (f32[128,512]{1,0:T(8,128)}, f32[128,512]{1,0:T(8,128)}, u32[]{:S(2)}, u32[]{:S(2)}) collective-permute-start(f32[128,512]{1,0:T(8,128)} %get-tuple-element.229), channel_id=1, source_target_pairs={{0,8},{4,12},{8,0},{12,4},{16,24},{20,28},{24,16},{28,20},{1,9},{5... | collective-permute-start | bytes 786440 | tf_op jit(solution)/shard_map/ppermute | solution.py:509
  164.7 12.1 %collective-permute-start.29 = (f32[80,256]{1,0:T(8,128)}, f32[80,256]{1,0:T(8,128)}, u32[]{:S(2)}, u32[]{:S(2)}) collective-permute-start(f32[80,256]{1,0:T(8,128)} %get-tuple-element.222), channel_id=1, source_target_pairs={{0,8},{4,12},{8,0},{12,4},{16,24},{20,28},{24,16},{28,20},{1,9},{5... | collective-permute-start | bytes 245768 | tf_op jit(solution)/shard_map/ppermute | solution.py:509
  165.2 11.6 %collective-permute-start.30 = (f32[80,256]{1,0:T(8,128)}, f32[80,256]{1,0:T(8,128)}, u32[]{:S(2)}, u32[]{:S(2)}) collective-permute-start(f32[80,256]{1,0:T(8,128)} %get-tuple-element.223), channel_id=1, source_target_pairs={{0,16},{4,20},{8,24},{12,28},{16,0},{20,4},{24,8},{28,12},{1,17},{... | collective-permute-start | bytes 245768 | tf_op jit(solution)/shard_map/ppermute | solution.py:509
  166.8 10.0 %collective-permute-start.31 = (f32[80,256]{1,0:T(8,128)}, f32[80,256]{1,0:T(8,128)}, u32[]{:S(2)}, u32[]{:S(2)}) collective-permute-start(f32[80,256]{1,0:T(8,128)} %get-tuple-element.224), channel_id=1, source_target_pairs={{0,24},{4,28},{8,16},{12,20},{16,8},{20,12},{24,0},{28,4},{1,25},{... | collective-permute-start | bytes 245768 | tf_op jit(solution)/shard_map/ppermute | solution.py:509
  169.1 15.6 %collective-permute-start.37 = (f32[128,512]{1,0:T(8,128)}, f32[128,512]{1,0:T(8,128)S(1)}, u32[]{:S(2)}, u32[]{:S(2)}) collective-permute-start(f32[128,512]{1,0:T(8,128)} %get-tuple-element.240), channel_id=1, source_target_pairs={{0,8},{4,12},{8,0},{12,4},{16,24},{20,28},{24,16},{28,20},{1,9},{5... | collective-permute-start | bytes 786440 | tf_op jit(solution)/shard_map/ppermute | solution.py:509
  175.8 8.7 %collective-permute-start.38 = (bf16[128,512]{1,0:T(8,128)(2,1)S(1)}, bf16[128,512]{1,0:T(8,128)(2,1)S(1)}, u32[]{:S(2)}, u32[]{:S(2)}) collective-permute-start(bf16[128,512]{1,0:T(8,128)(2,1)S(1)} %copy-done.25), channel_id=1, source_target_pairs={{0,16},{4,20},{8,24},{12,28},{16,0},{20,4},{24,8},{28,12},{1,17},{... | collective-permute-start | bytes 393224 | tf_op jit(solution)/shard_map/ppermute | solution.py:509
  177.8 7.4 %collective-permute-start.34 = (bf16[80,256]{1,0:T(8,128)(2,1)S(1)}, bf16[80,256]{1,0:T(8,128)(2,1)S(1)}, u32[]{:S(2)}, u32[]{:S(2)}) collective-permute-start(bf16[80,256]{1,0:T(8,128)(2,1)S(1)} %get-tuple-element.263), channel_id=1, source_target_pairs={{0,8},{4,12},{8,0},{12,4},{16,24},{20,28},{24,16},{28,20},{1,9},{5... | collective-permute-start | bytes 122888 | tf_op jit(solution)/shard_map/ppermute | solution.py:509
  179.1 9.8 %collective-permute-start.35 = (bf16[80,256]{1,0:T(8,128)(2,1)S(1)}, bf16[80,256]{1,0:T(8,128)(2,1)S(1)}, u32[]{:S(2)}, u32[]{:S(2)}) collective-permute-start(bf16[80,256]{1,0:T(8,128)(2,1)S(1)} %get-tuple-element.263), channel_id=1, source_target_pairs={{0,16},{4,20},{8,24},{12,28},{16,0},{20,4},{24,8},{28,12},{1,17},{... | collective-permute-start | bytes 122888 | tf_op jit(solution)/shard_map/ppermute | solution.py:509
  180.8 8.2 %collective-permute-start.36 = (bf16[80,256]{1,0:T(8,128)(2,1)S(1)}, bf16[80,256]{1,0:T(8,128)(2,1)S(1)}, u32[]{:S(2)}, u32[]{:S(2)}) collective-permute-start(bf16[80,256]{1,0:T(8,128)(2,1)S(1)} %get-tuple-element.263), channel_id=1, source_target_pairs={{0,24},{4,28},{8,16},{12,20},{16,8},{20,12},{24,0},{28,4},{1,25},{... | collective-permute-start | bytes 122888 | tf_op jit(solution)/shard_map/ppermute | solution.py:509
  184.6 8.0 %collective-permute-start.42 = (bf16[128,512]{1,0:T(8,128)(2,1)S(1)}, bf16[128,512]{1,0:T(8,128)(2,1)S(1)}, u32[]{:S(2)}, u32[]{:S(2)}) collective-permute-start(bf16[128,512]{1,0:T(8,128)(2,1)S(1)} %copy-done.24), channel_id=1, source_target_pairs={{0,24},{4,28},{8,16},{12,20},{16,8},{20,12},{24,0},{28,4},{1,25},{... | collective-permute-start | bytes 393224 | tf_op jit(solution)/shard_map/ppermute | solution.py:509
  (39 other events, 281.0 us)

commit v15 on v14

--- a/solution.py
+++ b/solution.py
@@ -149,9 +149,10 @@
     blocks, refs = refs[:blocks], refs[blocks:]
     out_ref, w_ref, *refs = refs
     keeps, others, refs = refs[:2], refs[2:4], refs[4:]
-    n_s, g_s, qkv, total = refs[-4:]
+    n_all, g_all, pack_all, qkv, total = refs[-5:]
     half, step = pl.program_id(0), pl.program_id(1)
-    rows = n_s.shape[0]
+    rows = qkv.shape[0]
+    here = pl.ds(pl.multiple_of((half * pl.num_programs(1) + step) * rows, 16), rows)
     scenes = rows // TOK
     width = w_ref.shape[1] // 4
 
@@ -160,20 +161,19 @@
         size = blocks[0].shape[0]
         for b, block in enumerate(blocks):
             w_ref[pl.ds(pl.multiple_of(owner_ref[b] * size, size), size), :] = block[...]
-        total[...] = jnp.zeros_like(total)
 
     @pl.when(half == 0)
     def _():
-        n_s[...] = na_ref[0]
-        g_s[...] = ga_ref[0]
+        n_all[here, :] = na_ref[0]
+        g_all[here, :] = ga_ref[0]
 
     @pl.when(half != 0)
     def _():
-        n_s[...] = nb_ref[0]
-        g_s[...] = gb_ref[0]
-
-    qkv[:, : 3 * width] = dot_nn(n_s[...], w_ref[:, : 3 * width]).astype(BF16)
-    qkv[:, 3 * width :] = dot_nn(g_s[...], w_ref[:, 3 * width :]).astype(BF16)
+        n_all[here, :] = nb_ref[0]
+        g_all[here, :] = gb_ref[0]
+
+    qkv[:, : 3 * width] = dot_nn(n_all[here, :], w_ref[:, : 3 * width]).astype(BF16)
+    qkv[:, 3 * width :] = dot_nn(g_all[here, :], w_ref[:, 3 * width :]).astype(BF16)
     heads = width // HD
     lane = lax.broadcasted_iota(jnp.int32, (1, width), 1)
     masks = [(lane // HD == h).astype(F32).astype(BF16) for h in range(heads)]
@@ -219,11 +219,12 @@
         return 0
 
     lax.fori_loop(0, scenes, scene_body, 0, unroll=True)
-    total[:, : 3 * width] += dot_tn(n_s[...], out_ref[:, : 3 * width])
-    total[:, 3 * width :] += dot_tn(g_s[...], out_ref[:, 3 * width :])
+    pack_all[here, :] = out_ref[...]
 
     @pl.when((half == pl.num_programs(0) - 1) & (step == pl.num_programs(1) - 1))
     def _():
+        total[:, : 3 * width] = dot_tn(n_all[...], pack_all[:, : 3 * width])
+        total[:, 3 * width :] = dot_tn(g_all[...], pack_all[:, 3 * width :])
         size = total.shape[0] // dp
         low = low_ref[0]
         for b in range(dp // 2):
@@ -268,7 +269,7 @@
     rows = block_rows(tokens)
     steps = tokens // rows
     cols = blocks[0][0].shape[1]
-    whole = lambda shape: pl.BlockSpec(shape, lambda h, i: (0, 0))
+    whole = lambda shape: pl.BlockSpec(shape, lambda h, i: (0, 0), pipeline_mode=pl.Buffered(1))
     at = lambda h, i: (h * steps + i, 0)
     packs = None if earlier is None else len(earlier[0])
     back = [] if earlier is None else two_halves(rows, steps, ())
@@ -282,7 +283,10 @@
         + two_halves(rows, steps, (1,))
         + [pl.BlockSpec((rows, cols // 4 * 3), at)] * (packs or 0)
         + [whole((D, cols // 4 * 3))] * (packs or 0)
-        + [pl.BlockSpec((D // dp, cols), functools.partial(lambda at, h, i: (at, 0), at)) for _, at in blocks],
+        + [
+            pl.BlockSpec((D // dp, cols), functools.partial(lambda at, h, i: (at, 0), at), pipeline_mode=pl.Buffered(1))
+            for _, at in blocks
+        ],
         out_specs=[pl.BlockSpec((rows, cols), at), whole((D, cols))] + [whole(g.shape) for g in grads] + back,
         out_shape=[
             jax.ShapeDtypeStruct((2 * tokens, cols), BF16),
@@ -291,8 +295,9 @@
         ]
         + [jax.ShapeDtypeStruct((tokens, D), kind) for kind in (F32, BF16)[: len(back)]],
         scratch_shapes=[
-            pltpu.VMEM((rows, D), BF16),
-            pltpu.VMEM((rows, D), BF16),
+            pltpu.VMEM((2 * tokens, D), BF16),
+            pltpu.VMEM((2 * tokens, D), BF16),
+            pltpu.VMEM((2 * tokens, cols), BF16),
             pltpu.VMEM((rows, cols), BF16),
             pltpu.VMEM((D, cols), F32),
         ],

time: 203 us -> 203 us (level)
  no operation moved by 1% of the time
where the time goes in v15:
time: 203 us; the launch traced here: 202 us
  Pallas kernels  93.6 us (46%)
  waiting for transfers between devices  51.3 us (25%)
  starting transfers between devices  42 us (21%)
  other arithmetic  8.22 us (4%)
  local copies, waits for them, and re-layouts  5.73 us (3%)
    pallas_call x2, Pallas kernels, attention_call(): pl.pallas_call(functools.partial(attention_kernel, packs, len(blocks), dp...  53.2 us
    ppermute x33, starting transfers between devices, swap(): return lax.ppermute(x, axis, [(i, i ^ bit) for i in range(size)])  29.6 us
    ppermute x33, waiting for transfers between devices, swap(): return lax.ppermute(x, axis, [(i, i ^ bit) for i in range(size)])  25.5 us
    ppermute x4, waiting for transfers between devices, send(): moved = [lax.ppermute(self.ahead[-1], self.axis, self.forward)]  19.7 us
    pallas_call x1, Pallas kernels, tail_call(): pl.pallas_call(tail_kernel, grid=(tokens // rows,), in_specs=[SCALARS, pe...  8.84 us
    pallas_call x1, Pallas kernels, stem_call(): pl.pallas_call(stem_kernel, grid=(scenes // block,), in_specs=[pl.BlockSp...  8.27 us
    pallas_call x3, Pallas kernels, combine_call(): pl.pallas_call(functools.partial(combine_kernel, [len(part) for part in p...  8 us
    ppermute x4, starting transfers between devices, send(): moved = [lax.ppermute(self.ahead[-1], self.axis, self.forward)]  6.25 us
  transfers between devices with their start and end apart: 44, of which 21 were waited for; matrix products, arithmetic and copies ran while one was open for 2% of the time, Pallas kernels for 46%

profile of v15, /device:TPU:0, one launch (start us, length us, event | category | flops | bytes accessed | tf_op | source)
XLA Modules:
  0.0 201.7 jit_solution(18423810685330325724)
XLA Ops:
  0.6 1.7 pack_weights.1.refs_2_
  2.3 2.9 %collective-permute-start.1 = (bf16[128,1024]{1,0:T(8,128)(2,1)}, bf16[128,1024]{1,0:T(8,128)(2,1)}, u32[]{:S(2)}, u32[]{:S(2)}) collective-permute-start(bf16[128,1024]{1,0:T(8,128)(2,1)} %pack_weights.1.refs_2_), channel_id=1, source_target_pairs={{0,2},{1,3},{2,0},{3,1},{4,6},{5,7},{6,4},{7,5},{8,10},{9,11},{10,... | collective-permute-start | bytes 786440 | tf_op jit(solution)/shard_map/ppermute | solution.py:514
  5.3 8.3 %stem_norm.1 = (bf16[6,144,1024]{2,1,0:T(8,128)(2,1)}, bf16[2,6,144,1024]{3,2,1,0:T(8,128)(2,1)}, bf16[6,144,256]{2,1,0:T(8,128)(2,1)}) custom-call(s32[3,6]{1,0:T(4,128)} %bitcast.29, s32[6,3,48]{2,1,0:T(4,128)} %idx_ref.1, bf16[6,144,640]{2,1,0:T(8,128)(2,1)} %patch_ref.1, bf16[640,1024]{1,0:T(8,128)(2,1)} %w_ref.1, f32[1,1024]{1,0:T(1,128)} %bitcast.32, ...), custom_call_target="tpu_custom_call" | custom-call | flops 8000000 | bytes 12000 | tf_op jit(solution)/shard_map/stem_norm/pallas_call | solution.py:98
  17.2 6.0 %collective-permute-done.2.refs_1_ = bf16[128,1024]{1,0:T(8,128)(2,1)} collective-permute-done((bf16[128,1024]{1,0:T(8,128)(2,1)}, bf16[128,1024]{1,0:T(8,128)(2,1)}, u32[]{:S(2)}, u32[]{:S(2)}) %collective-permute-start.2) | collective-permute-done | bytes 262176 | tf_op jit(solution)/shard_map/ppermute | solution.py:530
  27.1 4.7 %collective-permute-done.5.refs_2_ = bf16[128,1024]{1,0:T(8,128)(2,1)S(1)} collective-permute-done((bf16[128,1024]{1,0:T(8,128)(2,1)}, bf16[128,1024]{1,0:T(8,128)(2,1)S(1)}, u32[]{:S(2)}, u32[]{:S(2)}) %collective-permute-start.5) | collective-permute-done | bytes 262176 | tf_op jit(solution)/shard_map/ppermute | solution.py:530
  35.7 3.9 %collective-permute-done.7.refs_3_ = bf16[128,1024]{1,0:T(8,128)(2,1)} collective-permute-done((bf16[128,1024]{1,0:T(8,128)(2,1)S(1)}, bf16[128,1024]{1,0:T(8,128)(2,1)}, u32[]{:S(2)}, u32[]{:S(2)}) %collective-permute-start.7) | collective-permute-done | bytes 262176 | tf_op jit(solution)/shard_map/ppermute | solution.py:530
  42.6 5.2 %collective-permute-done.10.refs_4_ = bf16[128,1024]{1,0:T(8,128)(2,1)} collective-permute-done((bf16[128,1024]{1,0:T(8,128)(2,1)}, bf16[128,1024]{1,0:T(8,128)(2,1)}, u32[]{:S(2)}, u32[]{:S(2)}) %collective-permute-start.10) | collective-permute-done | bytes 262176 | tf_op jit(solution)/shard_map/ppermute | solution.py:530
  47.7 1.9 pad_maximum_fusion
  52.2 22.0 %attention.2 = (bf16[1728,1024]{1,0:T(8,128)(2,1)}, bf16[1024,1024]{1,0:T(8,128)(2,1)}, bf16[512,512]{1,0:T(8,128)(2,1)}, bf16[512,512]{1,0:T(8,128)(2,1)}, bf16...) custom-call(s32[2,3,6]{2,1,0:T(4,128)} %pad_add_fusion.cnt_ref, s32[8]{0:T(128)} %compare_select_fusion.2.owner_ref, ...), custom_call_target="tpu_custom_call" | custom-call | flops 20000000 | bytes 14000 | tf_op jit(solution)/shard_map/attention/pallas_call | solution.py:278
  74.3 4.3 %collective-permute-done.13.refs_6_ = bf16[128,1024]{1,0:T(8,128)(2,1)} collective-permute-done((bf16[128,1024]{1,0:T(8,128)(2,1)}, bf16[128,1024]{1,0:T(8,128)(2,1)}, u32[]{:S(2)}, u32[]{:S(2)}) %collective-permute-start.13) | collective-permute-done | bytes 262176 | tf_op jit(solution)/shard_map/ppermute | solution.py:514
  81.1 31.2 %attention.3 = (bf16[1728,1024]{1,0:T(8,128)(2,1)}, bf16[1024,1024]{1,0:T(8,128)(2,1)}, f32[512,512]{1,0:T(8,128)}, f32[512,512]{1,0:T(8,128)}, f32[512,512]{1,0...) custom-call(s32[2,3,6]{2,1,0:T(4,128)} %pad_add_fusion.cnt_ref, ...), custom_call_target="tpu_custom_call" | custom-call | flops 20000000 | bytes 14000 | tf_op jit(solution)/shard_map/attention/pallas_call | solution.py:278
  114.6 2.2 %add_convert_fusion.1 = bf16[512,512]{1,0:T(8,128)(2,1)} fusion(f32[512,512]{1,0:T(8,128)} %get-tuple-element.188, bf16[512,512]{1,0:T(8,128)(2,1)S(1)} %collective-permute-done.15), kind=kLoop, calls=%fused_computation.2 | loop fusion | flops 786432 | bytes 2097152 | tf_op jit(solution)/shard_map/convert_element_type | solution.py:698
  118.4 8.8 %tail.1 = (f32[320,1024]{1,0:T(8,128)}, f32[320,512]{1,0:T(8,128)}, f32[320,512]{1,0:T(8,128)}) custom-call(s32[1]{0:T(128)} %bitcast.2.core_ref, f32[864,1024]{1,0:T(8,128)} %get-tuple-element.181.own_ref, bf16[864,1024]{1,0:T(8,128)(2,1)} %copy-done.3, bf16[864,1024]{1,0:T(8,128)(2,1)} %bitcast.22, bf16[2,864,1024]{2,1,0:T(8,128)(2,1)} %bitcast.21, ...), custom_call_target="tpu_custom_call" | custom-call | flops 10000000 | bytes 12000 | tf_op jit(solution)/shard_map/tail/pallas_call | solution.py:469
  127.8 3.4 %collective-permute-done.19.refs_2_ = bf16[512,512]{1,0:T(8,128)(2,1)} collective-permute-done((bf16[512,512]{1,0:T(8,128)(2,1)}, bf16[512,512]{1,0:T(8,128)(2,1)}, u32[]{:S(2)}, u32[]{:S(2)}) %collective-permute-start.19) | collective-permute-done | bytes 524320 | tf_op jit(solution)/shard_map/ppermute | solution.py:514
  135.3 2.9 %combine.3 = (f32[80,1024]{1,0:T(8,128)}, f32[80,1024]{1,0:T(8,128)}, f32[80,1024]{1,0:T(8,128)}, f32[80,1024]{1,0:T(8,128)}) custom-call(s32[1]{0:T(128)} %bitcast.1.place_ref, f32[320,1024]{1,0:T(8,128)} %get-tuple-element.191.refs_0_, f32[320,512]{1,0:T(8,128)} %copy-done.7, f32[320,512]{1,0:T(8,128)} %copy-done.8), custom_call_target="tpu_custom_call" | custom-call | flops 1000 | bytes 5000 | tf_op jit(solution)/shard_map/combine/pallas_call | solution.py:330
  139.2 2.5 %collective-permute-start.25 = (f32[80,1024]{1,0:T(8,128)}, f32[80,1024]{1,0:T(8,128)}, u32[]{:S(2)}, u32[]{:S(2)}) collective-permute-start(f32[80,1024]{1,0:T(8,128)} %get-tuple-element.199), channel_id=1, source_target_pairs={{0,6},{1,7},{2,4},{3,5},{4,2},{5,3},{6,0},{7,1},{8,14},{9,15},{10,... | collective-permute-start | bytes 983048 | tf_op jit(solution)/shard_map/ppermute | solution.py:579
  141.7 2.5 %combine.4 = (f32[128,512]{1,0:T(8,128)}, f32[128,512]{1,0:T(8,128)}, bf16[128,512]{1,0:T(8,128)(2,1)}, bf16[128,512]{1,0:T(8,128)(2,1)}) custom-call(s32[1]{0:T(128)} %bitcast.place_ref, f32[512,512]{1,0:T(8,128)} %get-tuple-element.207.refs_0_, bf16[512,512]{1,0:T(8,128)(2,1)} %copy-done.9, bf16[512,512]{1,0:T(8,128)(2,1)} %collective-permute-done.19.refs_2_), custom_call_target="tpu_custom_call" | custom-call | flops 1000 | bytes 5000 | tf_op jit(solution)/shard_map/combine/pallas_call | solution.py:330
  148.2 3.7 %mixed.1 = bf16[864,1024]{1,0:T(8,128)(2,1)} custom-call(bf16[1728,1024]{1,0:T(8,128)(2,1)} %get-tuple-element.163.refs_0_, bf16[1728,1024]{1,0:T(8,128)(2,1)} %get-tuple-element.200.refs_1_, bf16[1024,1024]{1,0:T(8,128)(2,1)} %get-tuple-element.164.refs_1_.refs_2_, bf16[1024,1024]{1,0:T(8,128)(2,1)} %get-tuple-element.201.refs_3_), custom_call_target="tpu_custom_call" | custom-call | flops 2000000 | bytes 5000 | tf_op jit(solution)/shard_map/mixed/pallas_call | solution.py:415
  151.9 2.6 %combine.5 = (f32[128,512]{1,0:T(8,128)}, f32[128,512]{1,0:T(8,128)}, bf16[128,512]{1,0:T(8,128)(2,1)}, bf16[128,512]{1,0:T(8,128)(2,1)}) custom-call(s32[1]{0:T(128)} %bitcast.place_ref, f32[512,512]{1,0:T(8,128)} %get-tuple-element.213.refs_0_, bf16[512,512]{1,0:T(8,128)(2,1)} %collective-permute-done.20.refs_1_, bf16[512,512]{1,0:T(8,128)(2,1)} %copy-done.10), custom_call_target="tpu_custom_call" | custom-call | flops 1000 | bytes 5000 | tf_op jit(solution)/shard_map/combine/pallas_call | solution.py:330
  154.5 2.2 %collective-permute-done.26.refs_1_ = bf16[128,512]{1,0:T(8,128)(2,1)S(1)} collective-permute-done((bf16[128,512]{1,0:T(8,128)(2,1)}, bf16[128,512]{1,0:T(8,128)(2,1)S(1)}, u32[]{:S(2)}, u32[]{:S(2)}) %collective-permute-start.26) | collective-permute-done | bytes 131104 | tf_op jit(solution)/shard_map/ppermute | solution.py:514
  156.7 3.1 %collective-permute-done.23.refs_1_ = f32[80,1024]{1,0:T(8,128)S(1)} collective-permute-done((f32[80,1024]{1,0:T(8,128)}, f32[80,1024]{1,0:T(8,128)S(1)}, u32[]{:S(2)}, u32[]{:S(2)}) %collective-permute-start.23) | collective-permute-done | bytes 327712 | tf_op jit(solution)/shard_map/ppermute | solution.py:514
  162.1 2.1 %split_sum.1 = (f32[80,256]{1,0:T(8,128)}, f32[80,256]{1,0:T(8,128)}, f32[80,256]{1,0:T(8,128)}, f32[80,256]{1,0:T(8,128)}) custom-call(s32[1]{0:T(128)} %bitcast.place_ref, f32[80,1024]{1,0:T(8,128)} %get-tuple-element.196.refs_0_, f32[80,1024]{1,0:T(8,128)} %copy-done.13, f32[80,1024]{1,0:T(8,128)} %copy-done.14, f32[80,1024]{1,0:T(8,128)} %collective-permute-done.25.refs_3_), custom_call_target="tpu_custom_call" | custom-call | flops 1000 | bytes 2000 | tf_op jit(solution)/shard_map/split_sum/pallas_call | solution.py:357
  166.3 2.3 %collective-permute-start.31 = (f32[80,256]{1,0:T(8,128)}, f32[80,256]{1,0:T(8,128)}, u32[]{:S(2)}, u32[]{:S(2)}) collective-permute-start(f32[80,256]{1,0:T(8,128)} %get-tuple-element.224), channel_id=1, source_target_pairs={{0,24},{4,28},{8,16},{12,20},{16,8},{20,12},{24,0},{28,4},{1,25},{... | collective-permute-start | bytes 245768 | tf_op jit(solution)/shard_map/ppermute | solution.py:514
  169.8 5.5 %layer_output.1 = bf16[864,1024]{1,0:T(8,128)(2,1)} custom-call(s32[3,6]{1,0:T(4,128)} %bitcast.30, bf16[864,1024]{1,0:T(8,128)(2,1)} %copy-done.1, bf16[864,1024]{1,0:T(8,128)(2,1)} %bitcast.23, bf16[1728,1024]{1,0:T(8,128)(2,1)} %get-tuple-element.163.refs_0_, bf16[1728,1024]{1,0:T(8,128)(2,1)} %get-tuple-element.200.refs_1_, ...), custom_call_target="tpu_custom_call" | custom-call | flops 5000000 | bytes 10000 | tf_op jit(solution)/shard_map/layer_output/pallas_call | solution.py:500
  178.6 1.7 collective-permute-start.35
  181.8 2.2 %collective-permute-done.38.refs_6_ = bf16[128,512]{1,0:T(8,128)(2,1)S(1)} collective-permute-done((bf16[128,512]{1,0:T(8,128)(2,1)S(1)}, bf16[128,512]{1,0:T(8,128)(2,1)S(1)}, u32[]{:S(2)}, u32[]{:S(2)}) %collective-permute-start.38) | collective-permute-done | bytes 131104 | tf_op jit(solution)/shard_map/ppermute | solution.py:514
  184.7 3.7 %collective-permute-done.35 = bf16[80,256]{1,0:T(8,128)(2,1)S(1)} collective-permute-done((bf16[80,256]{1,0:T(8,128)(2,1)S(1)}, bf16[80,256]{1,0:T(8,128)(2,1)S(1)}, u32[]{:S(2)}, u32[]{:S(2)}) %collective-permute-start.35) | collective-permute-done | bytes 40992 | tf_op jit(solution)/shard_map/ppermute | solution.py:514
  188.4 1.7 collective-permute-start.39
  192.7 2.3 %weight_results.1 = (f32[3,128,256]{2,1,0:T(8,128)}, f32[256,128]{1,0:T(8,128)}) custom-call(f32[128,512]{1,0:T(8,128)} %get-tuple-element.246.refs_0_, bf16[128,512]{1,0:T(8,128)(2,1)} %copy-done.18, bf16[128,512]{1,0:T(8,128)(2,1)} %copy-done.19, f32[128,512]{1,0:T(8,128)} %collective-permute-done.33.refs_3_, f32[128,512]{1,0:T(8,128)} %get-tuple-element.250.refs_4_, ...), custom_call_target="tpu_custom_call" | custom-call | flops 1000 | bytes 2000 | tf_op jit(solution)/shard_map/weight_results/pallas_call | solution.py:380
  195.6 2.0 collective-permute-done.41
  197.8 2.1 %collective-permute-done.43 = bf16[320,1024]{1,0:T(8,128)(2,1)S(1)} collective-permute-done((bf16[320,1024]{1,0:T(8,128)(2,1)S(1)}, bf16[320,1024]{1,0:T(8,128)(2,1)S(1)}, u32[]{:S(2)}, u32[]{:S(2)}) %collective-permute-start.43) | collective-permute-done | bytes 655392 | tf_op jit(solution)/shard_map/ppermute | solution.py:514
  199.9 1.8 maximum_convert_fusion
  (139 shorter events, 47.6 us)
Async XLA Ops:
  2.3 11.8 %collective-permute-start.1 = (bf16[128,1024]{1,0:T(8,128)(2,1)}, bf16[128,1024]{1,0:T(8,128)(2,1)}, u32[]{:S(2)}, u32[]{:S(2)}) collective-permute-start(bf16[128,1024]{1,0:T(8,128)(2,1)} %pack_weights.1.refs_2_), channel_id=1, source_target_pairs={{0,2},{1,3},{2,0},{3,1},{4,6},{5,7},{6,4},{7,5},{8,10},{9,11},{10,... | collective-permute-start | bytes 786440 | tf_op jit(solution)/shard_map/ppermute | solution.py:514
  5.3 8.3 %collective-permute-start = (s32[3,6]{1,0:T(4,128)}, s32[3,6]{1,0:T(4,128)S(1)}, u32[]{:S(2)}, u32[]{:S(2)}) collective-permute-start(s32[3,6]{1,0:T(4,128)} %bitcast.28), channel_id=1, source_target_pairs={{0,1},{1,0},{2,3},{3,2},{4,5},{5,4},{6,7},{7,6},{8,9},{9,8},{10,11... | collective-permute-start | bytes 224 | tf_op jit(solution)/shard_map/ppermute | solution.py:514
  14.2 10.3 %collective-permute-start.4 = (bf16[2,864,1024]{2,1,0:T(8,128)(2,1)}, bf16[2,864,1024]{2,1,0:T(8,128)(2,1)S(1)}, u32[]{:S(2)}, u32[]{:S(2)}) collective-permute-start(bf16[2,864,1024]{2,1,0:T(8,128)(2,1)} %bitcast.16), channel_id=1, source_target_pairs={{0,1},{1,0},{2,3},{3,2},{4,5},{5,4},{6,7},{7,6},{8,9},{9,8},{10,11... | collective-permute-start | bytes 10616840 | tf_op jit(solution)/shard_map/ppermute | solution.py:514
  14.7 8.5 %collective-permute-start.2 = (bf16[128,1024]{1,0:T(8,128)(2,1)}, bf16[128,1024]{1,0:T(8,128)(2,1)}, u32[]{:S(2)}, u32[]{:S(2)}) collective-permute-start(bf16[128,1024]{1,0:T(8,128)(2,1)} %collective-permute-done.1.refs_0_), channel_id=1, source_target_pairs={{0,8},{8,16},{16,24},{24,28},{28,20},{20,12},{12,4},{4,0},{1,9},{9... | collective-permute-start | bytes 786440 | tf_op jit(solution)/shard_map/ppermute | solution.py:530
  16.3 8.2 %collective-permute-start.3 = (bf16[128,1024]{1,0:T(8,128)(2,1)}, bf16[128,1024]{1,0:T(8,128)(2,1)}, u32[]{:S(2)}, u32[]{:S(2)}) collective-permute-start(bf16[128,1024]{1,0:T(8,128)(2,1)} %collective-permute-done.1.refs_0_), channel_id=1, source_target_pairs={{8,0},{16,8},{24,16},{28,24},{20,28},{12,20},{4,12},{0,4},{9,1},{1... | collective-permute-start | bytes 786440 | tf_op jit(solution)/shard_map/ppermute | solution.py:532
  26.6 9.1 %collective-permute-start.9 = (bf16[128,1024]{1,0:T(8,128)(2,1)}, bf16[128,1024]{1,0:T(8,128)(2,1)S(1)}, u32[]{:S(2)}, u32[]{:S(2)}) collective-permute-start(bf16[128,1024]{1,0:T(8,128)(2,1)} %collective-permute-done.2.refs_1_), channel_id=1, source_target_pairs={{0,2},{1,3},{2,0},{3,1},{4,6},{5,7},{6,4},{7,5},{8,10},{9,11},{10,... | collective-permute-start | bytes 786440 | tf_op jit(solution)/shard_map/ppermute | solution.py:514
  35.1 7.5 %collective-permute-start.11 = (bf16[128,1024]{1,0:T(8,128)(2,1)S(1)}, bf16[128,1024]{1,0:T(8,128)(2,1)}, u32[]{:S(2)}, u32[]{:S(2)}) collective-permute-start(bf16[128,1024]{1,0:T(8,128)(2,1)S(1)} %collective-permute-done.5.refs_2_), channel_id=1, source_target_pairs={{0,2},{1,3},{2,0},{3,1},{4,6},{5,7},{6,4},{7,5},{8,10},{9,11},{10,... | collective-permute-start | bytes 786440 | tf_op jit(solution)/shard_map/ppermute | solution.py:514
  49.6 28.9 %collective-permute-start.14 = (bf16[384,1024]{1,0:T(8,128)(2,1)}, bf16[384,1024]{1,0:T(8,128)(2,1)}, u32[]{:S(2)}, u32[]{:S(2)}) collective-permute-start(bf16[384,1024]{1,0:T(8,128)(2,1)} %pad_maximum_fusion), channel_id=1, source_target_pairs={{0,2},{1,3},{2,0},{3,1},{4,6},{5,7},{6,4},{7,5},{8,10},{9,11},{10,... | collective-permute-start | bytes 2359304 | tf_op jit(solution)/shard_map/ppermute | solution.py:514
  50.2 24.1 %collective-permute-start.12 = (bf16[128,1024]{1,0:T(8,128)(2,1)}, bf16[128,1024]{1,0:T(8,128)(2,1)}, u32[]{:S(2)}, u32[]{:S(2)}) collective-permute-start(bf16[128,1024]{1,0:T(8,128)(2,1)} %collective-permute-done.7.refs_3_), channel_id=1, source_target_pairs={{0,2},{1,3},{2,0},{3,1},{4,6},{5,7},{6,4},{7,5},{8,10},{9,11},{10,... | collective-permute-start | bytes 786440 | tf_op jit(solution)/shard_map/ppermute | solution.py:514
  51.6 26.9 %collective-permute-start.13 = (bf16[128,1024]{1,0:T(8,128)(2,1)}, bf16[128,1024]{1,0:T(8,128)(2,1)}, u32[]{:S(2)}, u32[]{:S(2)}) collective-permute-start(bf16[128,1024]{1,0:T(8,128)(2,1)} %collective-permute-done.10.refs_4_), channel_id=1, source_target_pairs={{0,2},{1,3},{2,0},{3,1},{4,6},{5,7},{6,4},{7,5},{8,10},{9,11},{10,... | collective-permute-start | bytes 786440 | tf_op jit(solution)/shard_map/ppermute | solution.py:514
  78.6 33.8 %collective-permute-start.15 = (bf16[512,512]{1,0:T(8,128)(2,1)}, bf16[512,512]{1,0:T(8,128)(2,1)S(1)}, u32[]{:S(2)}, u32[]{:S(2)}) collective-permute-start(bf16[512,512]{1,0:T(8,128)(2,1)} %get-tuple-element.178), channel_id=1, source_target_pairs={{0,2},{1,3},{2,0},{3,1},{4,6},{5,7},{6,4},{7,5},{8,10},{9,11},{10,... | collective-permute-start | bytes 1572872 | tf_op jit(solution)/shard_map/ppermute | solution.py:514
  79.1 33.2 %collective-permute-start.16 = (bf16[512,512]{1,0:T(8,128)(2,1)}, bf16[512,512]{1,0:T(8,128)(2,1)S(1)}, u32[]{:S(2)}, u32[]{:S(2)}) collective-permute-start(bf16[512,512]{1,0:T(8,128)(2,1)} %get-tuple-element.179), channel_id=1, source_target_pairs={{0,2},{1,3},{2,0},{3,1},{4,6},{5,7},{6,4},{7,5},{8,10},{9,11},{10,... | collective-permute-start | bytes 1572872 | tf_op jit(solution)/shard_map/ppermute | solution.py:514
  80.6 31.8 %collective-permute-start.17 = (bf16[512,512]{1,0:T(8,128)(2,1)}, bf16[512,512]{1,0:T(8,128)(2,1)S(1)}, u32[]{:S(2)}, u32[]{:S(2)}) collective-permute-start(bf16[512,512]{1,0:T(8,128)(2,1)} %get-tuple-element.180), channel_id=1, source_target_pairs={{0,2},{1,3},{2,0},{3,1},{4,6},{5,7},{6,4},{7,5},{8,10},{9,11},{10,... | collective-permute-start | bytes 1572872 | tf_op jit(solution)/shard_map/ppermute | solution.py:514
  113.1 14.7 %collective-permute-start.20 = (bf16[512,512]{1,0:T(8,128)(2,1)}, bf16[512,512]{1,0:T(8,128)(2,1)}, u32[]{:S(2)}, u32[]{:S(2)}) collective-permute-start(bf16[512,512]{1,0:T(8,128)(2,1)} %get-tuple-element.190), channel_id=1, source_target_pairs={{0,2},{1,3},{2,0},{3,1},{4,6},{5,7},{6,4},{7,5},{8,10},{9,11},{10,... | collective-permute-start | bytes 1572872 | tf_op jit(solution)/shard_map/ppermute | solution.py:514
  116.8 14.4 %collective-permute-start.19 = (bf16[512,512]{1,0:T(8,128)(2,1)}, bf16[512,512]{1,0:T(8,128)(2,1)}, u32[]{:S(2)}, u32[]{:S(2)}) collective-permute-start(bf16[512,512]{1,0:T(8,128)(2,1)} %add_convert_fusion.1), channel_id=1, source_target_pairs={{0,4},{4,0},{8,12},{12,8},{16,20},{20,16},{24,28},{28,24},{1,5},{5... | collective-permute-start | bytes 1572872 | tf_op jit(solution)/shard_map/ppermute | solution.py:514
  131.8 14.9 %collective-permute-start.28 = (bf16[512,512]{1,0:T(8,128)(2,1)S(1)}, bf16[512,512]{1,0:T(8,128)(2,1)S(1)}, u32[]{:S(2)}, u32[]{:S(2)}) collective-permute-start(bf16[512,512]{1,0:T(8,128)(2,1)S(1)} %add_convert_fusion), channel_id=1, source_target_pairs={{0,4},{4,0},{8,12},{12,8},{16,20},{20,16},{24,28},{28,24},{1,5},{5... | collective-permute-start | bytes 1572872 | tf_op jit(solution)/shard_map/ppermute | solution.py:514
  138.2 21.6 %collective-permute-start.23 = (f32[80,1024]{1,0:T(8,128)}, f32[80,1024]{1,0:T(8,128)S(1)}, u32[]{:S(2)}, u32[]{:S(2)}) collective-permute-start(f32[80,1024]{1,0:T(8,128)} %get-tuple-element.197), channel_id=1, source_target_pairs={{0,4},{4,0},{8,12},{12,8},{16,20},{20,16},{24,28},{28,24},{1,5},{5... | collective-permute-start | bytes 983048 | tf_op jit(solution)/shard_map/ppermute | solution.py:514
  138.7 21.1 %collective-permute-start.24 = (f32[80,1024]{1,0:T(8,128)}, f32[80,1024]{1,0:T(8,128)S(1)}, u32[]{:S(2)}, u32[]{:S(2)}) collective-permute-start(f32[80,1024]{1,0:T(8,128)} %get-tuple-element.198), channel_id=1, source_target_pairs={{0,2},{1,3},{2,0},{3,1},{4,6},{5,7},{6,4},{7,5},{8,10},{9,11},{10,... | collective-permute-start | bytes 983048 | tf_op jit(solution)/shard_map/ppermute | solution.py:579
  139.2 20.6 %collective-permute-start.25 = (f32[80,1024]{1,0:T(8,128)}, f32[80,1024]{1,0:T(8,128)}, u32[]{:S(2)}, u32[]{:S(2)}) collective-permute-start(f32[80,1024]{1,0:T(8,128)} %get-tuple-element.199), channel_id=1, source_target_pairs={{0,6},{1,7},{2,4},{3,5},{4,2},{5,3},{6,0},{7,1},{8,14},{9,15},{10,... | collective-permute-start | bytes 983048 | tf_op jit(solution)/shard_map/ppermute | solution.py:579
  144.2 12.5 %collective-permute-start.26 = (bf16[128,512]{1,0:T(8,128)(2,1)}, bf16[128,512]{1,0:T(8,128)(2,1)S(1)}, u32[]{:S(2)}, u32[]{:S(2)}) collective-permute-start(bf16[128,512]{1,0:T(8,128)(2,1)} %get-tuple-element.211), channel_id=1, source_target_pairs={{0,16},{4,20},{8,24},{12,28},{16,0},{20,4},{24,8},{28,12},{1,17},{... | collective-permute-start | bytes 393224 | tf_op jit(solution)/shard_map/ppermute | solution.py:514
  146.7 10.0 %collective-permute-start.27 = (bf16[128,512]{1,0:T(8,128)(2,1)}, bf16[128,512]{1,0:T(8,128)(2,1)S(1)}, u32[]{:S(2)}, u32[]{:S(2)}) collective-permute-start(bf16[128,512]{1,0:T(8,128)(2,1)} %get-tuple-element.212), channel_id=1, source_target_pairs={{0,24},{4,28},{8,16},{12,20},{16,8},{20,12},{24,0},{28,4},{1,25},{... | collective-permute-start | bytes 393224 | tf_op jit(solution)/shard_map/ppermute | solution.py:514
  160.6 8.0 %collective-permute-start.32 = (bf16[864,1024]{1,0:T(8,128)(2,1)S(1)}, bf16[864,1024]{1,0:T(8,128)(2,1)S(1)}, u32[]{:S(2)}, u32[]{:S(2)}) collective-permute-start(bf16[864,1024]{1,0:T(8,128)(2,1)S(1)} %copy-done.2), channel_id=1, source_target_pairs={{0,1},{1,0},{2,3},{3,2},{4,5},{5,4},{6,7},{7,6},{8,9},{9,8},{10,11... | collective-permute-start | bytes 5308424 | tf_op jit(solution)/shard_map/ppermute | solution.py:514
  160.6 14.7 %collective-permute-start.33 = (f32[128,512]{1,0:T(8,128)}, f32[128,512]{1,0:T(8,128)}, u32[]{:S(2)}, u32[]{:S(2)}) collective-permute-start(f32[128,512]{1,0:T(8,128)} %get-tuple-element.229), channel_id=1, source_target_pairs={{0,8},{4,12},{8,0},{12,4},{16,24},{20,28},{24,16},{28,20},{1,9},{5... | collective-permute-start | bytes 786440 | tf_op jit(solution)/shard_map/ppermute | solution.py:514
  164.2 12.1 %collective-permute-start.29 = (f32[80,256]{1,0:T(8,128)}, f32[80,256]{1,0:T(8,128)}, u32[]{:S(2)}, u32[]{:S(2)}) collective-permute-start(f32[80,256]{1,0:T(8,128)} %get-tuple-element.222), channel_id=1, source_target_pairs={{0,8},{4,12},{8,0},{12,4},{16,24},{20,28},{24,16},{28,20},{1,9},{5... | collective-permute-start | bytes 245768 | tf_op jit(solution)/shard_map/ppermute | solution.py:514
  164.7 11.6 %collective-permute-start.30 = (f32[80,256]{1,0:T(8,128)}, f32[80,256]{1,0:T(8,128)}, u32[]{:S(2)}, u32[]{:S(2)}) collective-permute-start(f32[80,256]{1,0:T(8,128)} %get-tuple-element.223), channel_id=1, source_target_pairs={{0,16},{4,20},{8,24},{12,28},{16,0},{20,4},{24,8},{28,12},{1,17},{... | collective-permute-start | bytes 245768 | tf_op jit(solution)/shard_map/ppermute | solution.py:514
  166.3 10.0 %collective-permute-start.31 = (f32[80,256]{1,0:T(8,128)}, f32[80,256]{1,0:T(8,128)}, u32[]{:S(2)}, u32[]{:S(2)}) collective-permute-start(f32[80,256]{1,0:T(8,128)} %get-tuple-element.224), channel_id=1, source_target_pairs={{0,24},{4,28},{8,16},{12,20},{16,8},{20,12},{24,0},{28,4},{1,25},{... | collective-permute-start | bytes 245768 | tf_op jit(solution)/shard_map/ppermute | solution.py:514
  168.6 15.7 %collective-permute-start.37 = (f32[128,512]{1,0:T(8,128)}, f32[128,512]{1,0:T(8,128)S(1)}, u32[]{:S(2)}, u32[]{:S(2)}) collective-permute-start(f32[128,512]{1,0:T(8,128)} %get-tuple-element.240), channel_id=1, source_target_pairs={{0,8},{4,12},{8,0},{12,4},{16,24},{20,28},{24,16},{28,20},{1,9},{5... | collective-permute-start | bytes 786440 | tf_op jit(solution)/shard_map/ppermute | solution.py:514
  175.3 8.7 %collective-permute-start.38 = (bf16[128,512]{1,0:T(8,128)(2,1)S(1)}, bf16[128,512]{1,0:T(8,128)(2,1)S(1)}, u32[]{:S(2)}, u32[]{:S(2)}) collective-permute-start(bf16[128,512]{1,0:T(8,128)(2,1)S(1)} %copy-done.25), channel_id=1, source_target_pairs={{0,16},{4,20},{8,24},{12,28},{16,0},{20,4},{24,8},{28,12},{1,17},{... | collective-permute-start | bytes 393224 | tf_op jit(solution)/shard_map/ppermute | solution.py:514
  177.3 7.4 %collective-permute-start.34 = (bf16[80,256]{1,0:T(8,128)(2,1)S(1)}, bf16[80,256]{1,0:T(8,128)(2,1)S(1)}, u32[]{:S(2)}, u32[]{:S(2)}) collective-permute-start(bf16[80,256]{1,0:T(8,128)(2,1)S(1)} %get-tuple-element.263), channel_id=1, source_target_pairs={{0,8},{4,12},{8,0},{12,4},{16,24},{20,28},{24,16},{28,20},{1,9},{5... | collective-permute-start | bytes 122888 | tf_op jit(solution)/shard_map/ppermute | solution.py:514
  178.6 9.8 %collective-permute-start.35 = (bf16[80,256]{1,0:T(8,128)(2,1)S(1)}, bf16[80,256]{1,0:T(8,128)(2,1)S(1)}, u32[]{:S(2)}, u32[]{:S(2)}) collective-permute-start(bf16[80,256]{1,0:T(8,128)(2,1)S(1)} %get-tuple-element.263), channel_id=1, source_target_pairs={{0,16},{4,20},{8,24},{12,28},{16,0},{20,4},{24,8},{28,12},{1,17},{... | collective-permute-start | bytes 122888 | tf_op jit(solution)/shard_map/ppermute | solution.py:514
  180.2 8.2 %collective-permute-start.36 = (bf16[80,256]{1,0:T(8,128)(2,1)S(1)}, bf16[80,256]{1,0:T(8,128)(2,1)S(1)}, u32[]{:S(2)}, u32[]{:S(2)}) collective-permute-start(bf16[80,256]{1,0:T(8,128)(2,1)S(1)} %get-tuple-element.263), channel_id=1, source_target_pairs={{0,24},{4,28},{8,16},{12,20},{16,8},{20,12},{24,0},{28,4},{1,25},{... | collective-permute-start | bytes 122888 | tf_op jit(solution)/shard_map/ppermute | solution.py:514
  184.0 8.0 %collective-permute-start.42 = (bf16[128,512]{1,0:T(8,128)(2,1)S(1)}, bf16[128,512]{1,0:T(8,128)(2,1)S(1)}, u32[]{:S(2)}, u32[]{:S(2)}) collective-permute-start(bf16[128,512]{1,0:T(8,128)(2,1)S(1)} %copy-done.24), channel_id=1, source_target_pairs={{0,24},{4,28},{8,16},{12,20},{16,8},{20,12},{24,0},{28,4},{1,25},{... | collective-permute-start | bytes 393224 | tf_op jit(solution)/shard_map/ppermute | solution.py:514
  (39 other events, 279.2 us)

commit v16 on v15

--- a/solution.py
+++ b/solution.py
@@ -268,7 +268,7 @@
     tokens = own.shape[1]
     rows = block_rows(tokens)
     steps = tokens // rows
-    cols = blocks[0][0].shape[1]
+    cols = blocks[0].shape[1]
     whole = lambda shape: pl.BlockSpec(shape, lambda h, i: (0, 0), pipeline_mode=pl.Buffered(1))
     at = lambda h, i: (h * steps + i, 0)
     packs = None if earlier is None else len(earlier[0])
@@ -283,10 +283,7 @@
         + two_halves(rows, steps, (1,))
         + [pl.BlockSpec((rows, cols // 4 * 3), at)] * (packs or 0)
         + [whole((D, cols // 4 * 3))] * (packs or 0)
-        + [
-            pl.BlockSpec((D // dp, cols), functools.partial(lambda at, h, i: (at, 0), at), pipeline_mode=pl.Buffered(1))
-            for _, at in blocks
-        ],
+        + [whole(b.shape) for b in blocks],
         out_specs=[pl.BlockSpec((rows, cols), at), whole((D, cols))] + [whole(g.shape) for g in grads] + back,
         out_shape=[
             jax.ShapeDtypeStruct((2 * tokens, cols), BF16),
@@ -304,7 +301,7 @@
         compiler_params=params(),
         cost_estimate=cost(20e9, 14e6),
         name="attention",
-    )(counts, owners, low, own, far, own, far, *[x for group in earlier or () for x in group], *[b for b, _ in blocks])
+    )(counts, owners, low, own, far, own, far, *[x for group in earlier or () for x in group], *blocks)
 
 
 def combine_kernel(counts, place_ref, *refs):
@@ -659,27 +656,30 @@
     both = [stem[1].reshape(2, tokens, D)]
     cols = stem[2].reshape(tokens, stem[2].shape[2])
     both.append(swap(both[0], "group", group, 1))
-    passed = []
+    own_ahead, own_behind = [], []
     both, owners = step_all(rings, both, owners)
     while ring.steps < dp // 2:
-        passed.append(cross(ring.ahead[-1], 1))
-        if len(passed) > 1:
-            (passed[-2],) = step_all(rings, passed[-2])
-        else:
-            step_all(rings)
+        a, b = len(own_ahead), len(own_behind)
+        own_ahead.append(cross(ring.ahead[-1], 1))
+        if a:
+            own_behind.append(cross(ring.behind[a], 1))
+        last_ahead, last_behind = max(a - 1, 0), max(b - 1, 0)
+        own_ahead[last_ahead:a], own_behind[last_behind:b] = step_all(
+            rings, own_ahead[last_ahead:a], own_behind[last_behind:b]
+        )
     ring.ahead, ring.behind = together(ring.ahead, ring.behind)
-    passed.append(cross(ring.ahead[-1], 1))
-    passed.append(cross(jnp.concatenate(ring.behind[1:], axis=0), 1))
+    own_ahead.append(cross(ring.ahead[-1], 1))
+    own_behind.extend(cross(x, 1) for x in ring.behind[len(own_behind) + 1 :])
 
     packs, weights, crossing = [], [], []
     for f in list(fars) + [0]:
         if f:
-            blocks = [(x, 0) for x in rings[f - 1].ahead + rings[f - 1].behind[1:]]
+            blocks = rings[f - 1].ahead + rings[f - 1].behind[1:]
         else:
-            blocks = [(x, 0) for x in [shard] + passed[:-1]] + [(passed[-1], b) for b in range(dp // 2 - 1)]
+            blocks = [shard] + own_ahead + own_behind
         made = attention_call(both_counts, owners, low, *both, None if f else (packs, weights), blocks, dp)
         if f == 1:
-            made, passed[-3:] = together(made, passed[-3:])
+            made, own_ahead[-2:], own_behind[-2:] = together(made, own_ahead[-2:], own_behind[-2:])
         elif f:
             made = together(*made)
         else:

time: 203 us -> 200 us (0.985)
  waiting for transfers between devices: 51.3 us -> 40.1 us
  starting transfers between devices: 42 us -> 52 us
    ppermute x33 -> x35, starting transfers between devices: 29.6 us -> 38.1 us  [swap(): return lax.ppermute(x, axis, [(i, i ^ bit) for i in range(size)])]
    ppermute x4, waiting for transfers between devices: 19.7 us -> 13.1 us  [send(): moved = [lax.ppermute(self.ahead[-1], self.axis, self.forward)]]
    ppermute x33 -> x35, waiting for transfers between devices: 25.5 us -> 18.9 us  [swap(): return lax.ppermute(x, axis, [(i, i ^ bit) for i in range(size)])]
    unnamed x54 -> x50, local copies, waits for them, and re-layouts: 5.55 us -> 6.16 us
  transfers between devices with their start and end apart: 44 -> 46, of which waited for: 21 -> 17; matrix products, arithmetic and copies ran while one was open for 2% -> 2% of each run, Pallas kernels for 46% -> 46%
where the time goes in v16:
time: 200 us; the launch traced here: 199 us
  Pallas kernels  93.5 us (47%)
  starting transfers between devices  52 us (26%)
  waiting for transfers between devices  40.1 us (20%)
  other arithmetic  6.34 us (3%)
  local copies, waits for them, and re-layouts  6.33 us (3%)
    pallas_call x2, Pallas kernels, attention_call(): pl.pallas_call(functools.partial(attention_kernel, packs, len(blocks), dp...  53.1 us
    ppermute x35, starting transfers between devices, swap(): return lax.ppermute(x, axis, [(i, i ^ bit) for i in range(size)])  38.1 us
    ppermute x35, waiting for transfers between devices, swap(): return lax.ppermute(x, axis, [(i, i ^ bit) for i in range(size)])  18.9 us
    ppermute x4, waiting for transfers between devices, send(): moved = [lax.ppermute(self.ahead[-1], self.axis, self.forward)]  13.1 us
    pallas_call x1, Pallas kernels, tail_call(): pl.pallas_call(tail_kernel, grid=(tokens // rows,), in_specs=[SCALARS, pe...  8.84 us
    pallas_call x1, Pallas kernels, stem_call(): pl.pallas_call(stem_kernel, grid=(scenes // block,), in_specs=[pl.BlockSp...  8.32 us
    pallas_call x3, Pallas kernels, combine_call(): pl.pallas_call(functools.partial(combine_kernel, [len(part) for part in p...  8.02 us
    ppermute x4, starting transfers between devices, send(): moved = [lax.ppermute(self.ahead[-1], self.axis, self.forward)]  6.25 us
  transfers between devices with their start and end apart: 46, of which 17 were waited for; matrix products, arithmetic and copies ran while one was open for 2% of the time, Pallas kernels for 46%

profile of v16, /device:TPU:0, one launch (start us, length us, event | category | flops | bytes accessed | tf_op | source)
XLA Modules:
  0.0 199.2 jit_solution(2811195423994537738)
XLA Ops:
  0.6 1.7 pack_weights.1.refs_2_
  2.3 2.9 %collective-permute-start.1 = (bf16[128,1024]{1,0:T(8,128)(2,1)}, bf16[128,1024]{1,0:T(8,128)(2,1)}, u32[]{:S(2)}, u32[]{:S(2)}) collective-permute-start(bf16[128,1024]{1,0:T(8,128)(2,1)} %pack_weights.1.refs_2_), channel_id=1, source_target_pairs={{0,2},{1,3},{2,0},{3,1},{4,6},{5,7},{6,4},{7,5},{8,10},{9,11},{10,... | collective-permute-start | bytes 786440 | tf_op jit(solution)/shard_map/ppermute | solution.py:511
  5.3 8.3 %stem_norm.1 = (bf16[6,144,1024]{2,1,0:T(8,128)(2,1)}, bf16[2,6,144,1024]{3,2,1,0:T(8,128)(2,1)}, bf16[6,144,256]{2,1,0:T(8,128)(2,1)}) custom-call(s32[3,6]{1,0:T(4,128)} %bitcast.29, s32[6,3,48]{2,1,0:T(4,128)} %idx_ref.1, bf16[6,144,640]{2,1,0:T(8,128)(2,1)} %patch_ref.1, bf16[640,1024]{1,0:T(8,128)(2,1)} %w_ref.1, f32[1,1024]{1,0:T(1,128)} %bitcast.32, ...), custom_call_target="tpu_custom_call" | custom-call | flops 8000000 | bytes 12000 | tf_op jit(solution)/shard_map/stem_norm/pallas_call | solution.py:98
  17.3 6.0 %collective-permute-done.2.refs_1_ = bf16[128,1024]{1,0:T(8,128)(2,1)} collective-permute-done((bf16[128,1024]{1,0:T(8,128)(2,1)}, bf16[128,1024]{1,0:T(8,128)(2,1)}, u32[]{:S(2)}, u32[]{:S(2)}) %collective-permute-start.2) | collective-permute-done | bytes 262176 | tf_op jit(solution)/shard_map/ppermute | solution.py:527
  27.1 4.7 %collective-permute-done.5.refs_2_ = bf16[128,1024]{1,0:T(8,128)(2,1)S(1)} collective-permute-done((bf16[128,1024]{1,0:T(8,128)(2,1)}, bf16[128,1024]{1,0:T(8,128)(2,1)S(1)}, u32[]{:S(2)}, u32[]{:S(2)}) %collective-permute-start.5) | collective-permute-done | bytes 262176 | tf_op jit(solution)/shard_map/ppermute | solution.py:527
  37.3 2.4 %collective-permute-done.7.refs_3_ = bf16[128,1024]{1,0:T(8,128)(2,1)} collective-permute-done((bf16[128,1024]{1,0:T(8,128)(2,1)S(1)}, bf16[128,1024]{1,0:T(8,128)(2,1)}, u32[]{:S(2)}, u32[]{:S(2)}) %collective-permute-start.7) | collective-permute-done | bytes 262176 | tf_op jit(solution)/shard_map/ppermute | solution.py:527
  39.7 1.8 collective-permute-done.8.refs_7_
  45.0 5.4 %collective-permute-done.11.refs_4_ = bf16[128,1024]{1,0:T(8,128)(2,1)} collective-permute-done((bf16[128,1024]{1,0:T(8,128)(2,1)S(1)}, bf16[128,1024]{1,0:T(8,128)(2,1)}, u32[]{:S(2)}, u32[]{:S(2)}) %collective-permute-start.11) | collective-permute-done | bytes 262176 | tf_op jit(solution)/shard_map/ppermute | solution.py:511
  52.5 22.0 %attention.2 = (bf16[1728,1024]{1,0:T(8,128)(2,1)}, bf16[1024,1024]{1,0:T(8,128)(2,1)}, bf16[512,512]{1,0:T(8,128)(2,1)}, bf16[512,512]{1,0:T(8,128)(2,1)}, bf16...) custom-call(s32[2,3,6]{2,1,0:T(4,128)} %pad_add_fusion.cnt_ref, s32[8]{0:T(128)} %compare_select_fusion.2.owner_ref, ...), custom_call_target="tpu_custom_call" | custom-call | flops 20000000 | bytes 14000 | tf_op jit(solution)/shard_map/attention/pallas_call | solution.py:278
  77.8 31.1 %attention.3 = (bf16[1728,1024]{1,0:T(8,128)(2,1)}, bf16[1024,1024]{1,0:T(8,128)(2,1)}, f32[512,512]{1,0:T(8,128)}, f32[512,512]{1,0:T(8,128)}, f32[512,512]{1,0...) custom-call(s32[2,3,6]{2,1,0:T(4,128)} %pad_add_fusion.cnt_ref, ...), custom_call_target="tpu_custom_call" | custom-call | flops 20000000 | bytes 14000 | tf_op jit(solution)/shard_map/attention/pallas_call | solution.py:278
  111.2 2.2 %add_convert_fusion.1 = bf16[512,512]{1,0:T(8,128)(2,1)} fusion(f32[512,512]{1,0:T(8,128)} %get-tuple-element.192, bf16[512,512]{1,0:T(8,128)(2,1)S(1)} %collective-permute-done.17), kind=kLoop, calls=%fused_computation.2 | loop fusion | flops 786432 | bytes 2097152 | tf_op jit(solution)/shard_map/convert_element_type | solution.py:698
  115.0 8.8 %tail.1 = (f32[320,1024]{1,0:T(8,128)}, f32[320,512]{1,0:T(8,128)}, f32[320,512]{1,0:T(8,128)}) custom-call(s32[1]{0:T(128)} %bitcast.2.core_ref, f32[864,1024]{1,0:T(8,128)} %get-tuple-element.185.own_ref, bf16[864,1024]{1,0:T(8,128)(2,1)} %copy-done.3, bf16[864,1024]{1,0:T(8,128)(2,1)} %bitcast.22, bf16[2,864,1024]{2,1,0:T(8,128)(2,1)} %bitcast.21, ...), custom_call_target="tpu_custom_call" | custom-call | flops 10000000 | bytes 12000 | tf_op jit(solution)/shard_map/tail/pallas_call | solution.py:466
  124.4 3.4 %collective-permute-done.21.refs_2_ = bf16[512,512]{1,0:T(8,128)(2,1)} collective-permute-done((bf16[512,512]{1,0:T(8,128)(2,1)}, bf16[512,512]{1,0:T(8,128)(2,1)}, u32[]{:S(2)}, u32[]{:S(2)}) %collective-permute-start.21) | collective-permute-done | bytes 524320 | tf_op jit(solution)/shard_map/ppermute | solution.py:511
  131.9 2.9 %combine.3 = (f32[80,1024]{1,0:T(8,128)}, f32[80,1024]{1,0:T(8,128)}, f32[80,1024]{1,0:T(8,128)}, f32[80,1024]{1,0:T(8,128)}) custom-call(s32[1]{0:T(128)} %bitcast.1.place_ref, f32[320,1024]{1,0:T(8,128)} %get-tuple-element.195.refs_0_, f32[320,512]{1,0:T(8,128)} %copy-done.5, f32[320,512]{1,0:T(8,128)} %copy-done.6), custom_call_target="tpu_custom_call" | custom-call | flops 1000 | bytes 5000 | tf_op jit(solution)/shard_map/combine/pallas_call | solution.py:327
  135.7 2.5 %collective-permute-start.27 = (f32[80,1024]{1,0:T(8,128)}, f32[80,1024]{1,0:T(8,128)}, u32[]{:S(2)}, u32[]{:S(2)}) collective-permute-start(f32[80,1024]{1,0:T(8,128)} %get-tuple-element.203), channel_id=1, source_target_pairs={{0,6},{1,7},{2,4},{3,5},{4,2},{5,3},{6,0},{7,1},{8,14},{9,15},{10,... | collective-permute-start | bytes 983048 | tf_op jit(solution)/shard_map/ppermute | solution.py:576
  138.3 2.5 %combine.4 = (f32[128,512]{1,0:T(8,128)}, f32[128,512]{1,0:T(8,128)}, bf16[128,512]{1,0:T(8,128)(2,1)}, bf16[128,512]{1,0:T(8,128)(2,1)}) custom-call(s32[1]{0:T(128)} %bitcast.place_ref, f32[512,512]{1,0:T(8,128)} %get-tuple-element.211.refs_0_, bf16[512,512]{1,0:T(8,128)(2,1)} %copy-done.7, bf16[512,512]{1,0:T(8,128)(2,1)} %collective-permute-done.21.refs_2_), custom_call_target="tpu_custom_call" | custom-call | flops 1000 | bytes 5000 | tf_op jit(solution)/shard_map/combine/pallas_call | solution.py:327
  140.7 2.5 %collective-permute-start.28 = (bf16[128,512]{1,0:T(8,128)(2,1)}, bf16[128,512]{1,0:T(8,128)(2,1)S(1)}, u32[]{:S(2)}, u32[]{:S(2)}) collective-permute-start(bf16[128,512]{1,0:T(8,128)(2,1)} %get-tuple-element.215), channel_id=1, source_target_pairs={{0,16},{4,20},{8,24},{12,28},{16,0},{20,4},{24,8},{28,12},{1,17},{... | collective-permute-start | bytes 393224 | tf_op jit(solution)/shard_map/ppermute | solution.py:511
  143.3 2.6 %collective-permute-start.29 = (bf16[128,512]{1,0:T(8,128)(2,1)}, bf16[128,512]{1,0:T(8,128)(2,1)S(1)}, u32[]{:S(2)}, u32[]{:S(2)}) collective-permute-start(bf16[128,512]{1,0:T(8,128)(2,1)} %get-tuple-element.216), channel_id=1, source_target_pairs={{0,24},{4,28},{8,16},{12,20},{16,8},{20,12},{24,0},{28,4},{1,25},{... | collective-permute-start | bytes 393224 | tf_op jit(solution)/shard_map/ppermute | solution.py:511
  145.9 3.7 %mixed.1 = bf16[864,1024]{1,0:T(8,128)(2,1)} custom-call(bf16[1728,1024]{1,0:T(8,128)(2,1)} %get-tuple-element.165.refs_0_, bf16[1728,1024]{1,0:T(8,128)(2,1)} %get-tuple-element.204.refs_1_, bf16[1024,1024]{1,0:T(8,128)(2,1)} %get-tuple-element.166.refs_1_.refs_2_, bf16[1024,1024]{1,0:T(8,128)(2,1)} %get-tuple-element.205.refs_3_), custom_call_target="tpu_custom_call" | custom-call | flops 2000000 | bytes 5000 | tf_op jit(solution)/shard_map/mixed/pallas_call | solution.py:412
  149.6 2.6 %combine.5 = (f32[128,512]{1,0:T(8,128)}, f32[128,512]{1,0:T(8,128)}, bf16[128,512]{1,0:T(8,128)(2,1)}, bf16[128,512]{1,0:T(8,128)(2,1)}) custom-call(s32[1]{0:T(128)} %bitcast.place_ref, f32[512,512]{1,0:T(8,128)} %get-tuple-element.217.refs_0_, bf16[512,512]{1,0:T(8,128)(2,1)} %collective-permute-done.22.refs_1_, bf16[512,512]{1,0:T(8,128)(2,1)} %copy-done.8), custom_call_target="tpu_custom_call" | custom-call | flops 1000 | bytes 5000 | tf_op jit(solution)/shard_map/combine/pallas_call | solution.py:327
  153.3 3.0 %collective-permute-done.25.refs_1_ = f32[80,1024]{1,0:T(8,128)S(1)} collective-permute-done((f32[80,1024]{1,0:T(8,128)}, f32[80,1024]{1,0:T(8,128)S(1)}, u32[]{:S(2)}, u32[]{:S(2)}) %collective-permute-start.25) | collective-permute-done | bytes 327712 | tf_op jit(solution)/shard_map/ppermute | solution.py:511
  158.7 2.0 %split_sum.1 = (f32[80,256]{1,0:T(8,128)}, f32[80,256]{1,0:T(8,128)}, f32[80,256]{1,0:T(8,128)}, f32[80,256]{1,0:T(8,128)}) custom-call(s32[1]{0:T(128)} %bitcast.place_ref, f32[80,1024]{1,0:T(8,128)} %get-tuple-element.200.refs_0_, f32[80,1024]{1,0:T(8,128)} %copy-done.11, f32[80,1024]{1,0:T(8,128)} %copy-done.12, f32[80,1024]{1,0:T(8,128)} %collective-permute-done.27.refs_3_), custom_call_target="tpu_custom_call" | custom-call | flops 1000 | bytes 2000 | tf_op jit(solution)/shard_map/split_sum/pallas_call | solution.py:354
  161.2 2.5 %collective-permute-start.32 = (f32[80,256]{1,0:T(8,128)}, f32[80,256]{1,0:T(8,128)}, u32[]{:S(2)}, u32[]{:S(2)}) collective-permute-start(f32[80,256]{1,0:T(8,128)} %get-tuple-element.227), channel_id=1, source_target_pairs={{0,16},{4,20},{8,24},{12,28},{16,0},{20,4},{24,8},{28,12},{1,17},{... | collective-permute-start | bytes 245768 | tf_op jit(solution)/shard_map/ppermute | solution.py:511
  166.4 5.5 %layer_output.1 = bf16[864,1024]{1,0:T(8,128)(2,1)} custom-call(s32[3,6]{1,0:T(4,128)} %bitcast.30, bf16[864,1024]{1,0:T(8,128)(2,1)} %copy-done.1, bf16[864,1024]{1,0:T(8,128)(2,1)} %bitcast.23, bf16[1728,1024]{1,0:T(8,128)(2,1)} %get-tuple-element.165.refs_0_, bf16[1728,1024]{1,0:T(8,128)(2,1)} %get-tuple-element.204.refs_1_, ...), custom_call_target="tpu_custom_call" | custom-call | flops 5000000 | bytes 10000 | tf_op jit(solution)/shard_map/layer_output/pallas_call | solution.py:497
  171.9 1.9 collective-permute-start.40
  176.8 2.4 %collective-permute-start.38 = (bf16[80,256]{1,0:T(8,128)(2,1)S(1)}, bf16[80,256]{1,0:T(8,128)(2,1)S(1)}, u32[]{:S(2)}, u32[]{:S(2)}) collective-permute-start(bf16[80,256]{1,0:T(8,128)(2,1)S(1)} %get-tuple-element.267), channel_id=1, source_target_pairs={{0,24},{4,28},{8,16},{12,20},{16,8},{20,12},{24,0},{28,4},{1,25},{... | collective-permute-start | bytes 122888 | tf_op jit(solution)/shard_map/ppermute | solution.py:511
  179.3 4.2 %collective-permute-start.44 = (bf16[128,512]{1,0:T(8,128)(2,1)S(1)}, bf16[128,512]{1,0:T(8,128)(2,1)S(1)}, u32[]{:S(2)}, u32[]{:S(2)}) collective-permute-start(bf16[128,512]{1,0:T(8,128)(2,1)S(1)} %copy-done.22), channel_id=1, source_target_pairs={{0,24},{4,28},{8,16},{12,20},{16,8},{20,12},{24,0},{28,4},{1,25},{... | collective-permute-start | bytes 393224 | tf_op jit(solution)/shard_map/ppermute | solution.py:511
  185.8 2.7 %collective-permute-start.43 = (bf16[80,1024]{1,0:T(8,128)(2,1)S(1)}, bf16[80,1024]{1,0:T(8,128)(2,1)S(1)}, u32[]{:S(2)}, u32[]{:S(2)}) collective-permute-start(bf16[80,1024]{1,0:T(8,128)(2,1)S(1)} %constant_dynamic-update-slice_fusion.4), channel_id=1, source_target_pairs={{0,6},{1,7},{2,4},{3,5},{4,2},{5,3},{6,0},{7,1},{8,14},{9,15},{10,... | collective-permute-start | bytes 491528 | tf_op jit(solution)/shard_map/ppermute | solution.py:576
  189.1 2.3 %weight_results.1 = (f32[3,128,256]{2,1,0:T(8,128)}, f32[256,128]{1,0:T(8,128)}) custom-call(f32[128,512]{1,0:T(8,128)} %get-tuple-element.250.refs_0_, bf16[128,512]{1,0:T(8,128)(2,1)} %copy-done.16, bf16[128,512]{1,0:T(8,128)(2,1)} %copy-done.17, f32[128,512]{1,0:T(8,128)} %collective-permute-done.35.refs_3_, f32[128,512]{1,0:T(8,128)} %get-tuple-element.254.refs_4_, ...), custom_call_target="tpu_custom_call" | custom-call | flops 1000 | bytes 2000 | tf_op jit(solution)/shard_map/weight_results/pallas_call | solution.py:377
  192.2 2.9 %collective-permute-done.43 = bf16[80,1024]{1,0:T(8,128)(2,1)S(1)} collective-permute-done((bf16[80,1024]{1,0:T(8,128)(2,1)S(1)}, bf16[80,1024]{1,0:T(8,128)(2,1)S(1)}, u32[]{:S(2)}, u32[]{:S(2)}) %collective-permute-start.43) | collective-permute-done | bytes 163872 | tf_op jit(solution)/shard_map/ppermute | solution.py:576
  195.2 2.1 %collective-permute-done.45 = bf16[320,1024]{1,0:T(8,128)(2,1)S(1)} collective-permute-done((bf16[320,1024]{1,0:T(8,128)(2,1)S(1)}, bf16[320,1024]{1,0:T(8,128)(2,1)S(1)}, u32[]{:S(2)}, u32[]{:S(2)}) %collective-permute-start.45) | collective-permute-done | bytes 655392 | tf_op jit(solution)/shard_map/ppermute | solution.py:511
  197.3 1.8 maximum_convert_fusion
  (138 shorter events, 44.9 us)
Async XLA Ops:
  2.3 11.9 %collective-permute-start.1 = (bf16[128,1024]{1,0:T(8,128)(2,1)}, bf16[128,1024]{1,0:T(8,128)(2,1)}, u32[]{:S(2)}, u32[]{:S(2)}) collective-permute-start(bf16[128,1024]{1,0:T(8,128)(2,1)} %pack_weights.1.refs_2_), channel_id=1, source_target_pairs={{0,2},{1,3},{2,0},{3,1},{4,6},{5,7},{6,4},{7,5},{8,10},{9,11},{10,... | collective-permute-start | bytes 786440 | tf_op jit(solution)/shard_map/ppermute | solution.py:511
  5.3 8.3 %collective-permute-start = (s32[3,6]{1,0:T(4,128)}, s32[3,6]{1,0:T(4,128)S(1)}, u32[]{:S(2)}, u32[]{:S(2)}) collective-permute-start(s32[3,6]{1,0:T(4,128)} %bitcast.28), channel_id=1, source_target_pairs={{0,1},{1,0},{2,3},{3,2},{4,5},{5,4},{6,7},{7,6},{8,9},{9,8},{10,11... | collective-permute-start | bytes 224 | tf_op jit(solution)/shard_map/ppermute | solution.py:511
  14.2 10.3 %collective-permute-start.4 = (bf16[2,864,1024]{2,1,0:T(8,128)(2,1)}, bf16[2,864,1024]{2,1,0:T(8,128)(2,1)S(1)}, u32[]{:S(2)}, u32[]{:S(2)}) collective-permute-start(bf16[2,864,1024]{2,1,0:T(8,128)(2,1)} %bitcast.16), channel_id=1, source_target_pairs={{0,1},{1,0},{2,3},{3,2},{4,5},{5,4},{6,7},{7,6},{8,9},{9,8},{10,11... | collective-permute-start | bytes 10616840 | tf_op jit(solution)/shard_map/ppermute | solution.py:511
  14.7 8.5 %collective-permute-start.2 = (bf16[128,1024]{1,0:T(8,128)(2,1)}, bf16[128,1024]{1,0:T(8,128)(2,1)}, u32[]{:S(2)}, u32[]{:S(2)}) collective-permute-start(bf16[128,1024]{1,0:T(8,128)(2,1)} %collective-permute-done.1.refs_0_), channel_id=1, source_target_pairs={{0,8},{8,16},{16,24},{24,28},{28,20},{20,12},{12,4},{4,0},{1,9},{9... | collective-permute-start | bytes 786440 | tf_op jit(solution)/shard_map/ppermute | solution.py:527
  16.3 8.2 %collective-permute-start.3 = (bf16[128,1024]{1,0:T(8,128)(2,1)}, bf16[128,1024]{1,0:T(8,128)(2,1)}, u32[]{:S(2)}, u32[]{:S(2)}) collective-permute-start(bf16[128,1024]{1,0:T(8,128)(2,1)} %collective-permute-done.1.refs_0_), channel_id=1, source_target_pairs={{8,0},{16,8},{24,16},{28,24},{20,28},{12,20},{4,12},{0,4},{9,1},{1... | collective-permute-start | bytes 786440 | tf_op jit(solution)/shard_map/ppermute | solution.py:529
  26.6 10.7 %collective-permute-start.9 = (bf16[128,1024]{1,0:T(8,128)(2,1)}, bf16[128,1024]{1,0:T(8,128)(2,1)}, u32[]{:S(2)}, u32[]{:S(2)}) collective-permute-start(bf16[128,1024]{1,0:T(8,128)(2,1)} %collective-permute-done.2.refs_1_), channel_id=1, source_target_pairs={{0,2},{1,3},{2,0},{3,1},{4,6},{5,7},{6,4},{7,5},{8,10},{9,11},{10,... | collective-permute-start | bytes 786440 | tf_op jit(solution)/shard_map/ppermute | solution.py:511
  35.3 9.8 %collective-permute-start.12 = (bf16[128,1024]{1,0:T(8,128)(2,1)}, bf16[128,1024]{1,0:T(8,128)(2,1)}, u32[]{:S(2)}, u32[]{:S(2)}) collective-permute-start(bf16[128,1024]{1,0:T(8,128)(2,1)} %collective-permute-done.3.refs_5_), channel_id=1, source_target_pairs={{0,2},{1,3},{2,0},{3,1},{4,6},{5,7},{6,4},{7,5},{8,10},{9,11},{10,... | collective-permute-start | bytes 786440 | tf_op jit(solution)/shard_map/ppermute | solution.py:511
  35.8 14.6 %collective-permute-start.11 = (bf16[128,1024]{1,0:T(8,128)(2,1)S(1)}, bf16[128,1024]{1,0:T(8,128)(2,1)}, u32[]{:S(2)}, u32[]{:S(2)}) collective-permute-start(bf16[128,1024]{1,0:T(8,128)(2,1)S(1)} %collective-permute-done.5.refs_2_), channel_id=1, source_target_pairs={{0,2},{1,3},{2,0},{3,1},{4,6},{5,7},{6,4},{7,5},{8,10},{9,11},{10,... | collective-permute-start | bytes 786440 | tf_op jit(solution)/shard_map/ppermute | solution.py:511
  41.5 8.9 %collective-permute-start.10 = (bf16[128,1024]{1,0:T(8,128)(2,1)}, bf16[128,1024]{1,0:T(8,128)(2,1)}, u32[]{:S(2)}, u32[]{:S(2)}) collective-permute-start(bf16[128,1024]{1,0:T(8,128)(2,1)} %collective-permute-done.7.refs_3_), channel_id=1, source_target_pairs={{0,8},{8,16},{16,24},{24,28},{28,20},{20,12},{12,4},{4,0},{1,9},{9... | collective-permute-start | bytes 786440 | tf_op jit(solution)/shard_map/ppermute | solution.py:527
  43.0 31.4 %collective-permute-start.15 = (bf16[128,1024]{1,0:T(8,128)(2,1)}, bf16[128,1024]{1,0:T(8,128)(2,1)S(1)}, u32[]{:S(2)}, u32[]{:S(2)}) collective-permute-start(bf16[128,1024]{1,0:T(8,128)(2,1)} %collective-permute-done.6.refs_6_), channel_id=1, source_target_pairs={{0,2},{1,3},{2,0},{3,1},{4,6},{5,7},{6,4},{7,5},{8,10},{9,11},{10,... | collective-permute-start | bytes 786440 | tf_op jit(solution)/shard_map/ppermute | solution.py:511
  43.6 30.9 %collective-permute-start.13 = (bf16[128,1024]{1,0:T(8,128)(2,1)}, bf16[128,1024]{1,0:T(8,128)(2,1)}, u32[]{:S(2)}, u32[]{:S(2)}) collective-permute-start(bf16[128,1024]{1,0:T(8,128)(2,1)} %collective-permute-done.7.refs_3_), channel_id=1, source_target_pairs={{0,2},{1,3},{2,0},{3,1},{4,6},{5,7},{6,4},{7,5},{8,10},{9,11},{10,... | collective-permute-start | bytes 786440 | tf_op jit(solution)/shard_map/ppermute | solution.py:511
  50.4 24.1 %collective-permute-start.14 = (bf16[128,1024]{1,0:T(8,128)(2,1)}, bf16[128,1024]{1,0:T(8,128)(2,1)}, u32[]{:S(2)}, u32[]{:S(2)}) collective-permute-start(bf16[128,1024]{1,0:T(8,128)(2,1)} %collective-permute-done.10.refs_4_), channel_id=1, source_target_pairs={{0,2},{1,3},{2,0},{3,1},{4,6},{5,7},{6,4},{7,5},{8,10},{9,11},{10,... | collective-permute-start | bytes 786440 | tf_op jit(solution)/shard_map/ppermute | solution.py:511
  51.0 23.5 %collective-permute-start.16 = (bf16[128,1024]{1,0:T(8,128)(2,1)}, bf16[128,1024]{1,0:T(8,128)(2,1)}, u32[]{:S(2)}, u32[]{:S(2)}) collective-permute-start(bf16[128,1024]{1,0:T(8,128)(2,1)} %collective-permute-done.8.refs_7_), channel_id=1, source_target_pairs={{0,2},{1,3},{2,0},{3,1},{4,6},{5,7},{6,4},{7,5},{8,10},{9,11},{10,... | collective-permute-start | bytes 786440 | tf_op jit(solution)/shard_map/ppermute | solution.py:511
  75.2 33.7 %collective-permute-start.17 = (bf16[512,512]{1,0:T(8,128)(2,1)}, bf16[512,512]{1,0:T(8,128)(2,1)S(1)}, u32[]{:S(2)}, u32[]{:S(2)}) collective-permute-start(bf16[512,512]{1,0:T(8,128)(2,1)} %get-tuple-element.182), channel_id=1, source_target_pairs={{0,2},{1,3},{2,0},{3,1},{4,6},{5,7},{6,4},{7,5},{8,10},{9,11},{10,... | collective-permute-start | bytes 1572872 | tf_op jit(solution)/shard_map/ppermute | solution.py:511
  75.7 33.2 %collective-permute-start.18 = (bf16[512,512]{1,0:T(8,128)(2,1)}, bf16[512,512]{1,0:T(8,128)(2,1)S(1)}, u32[]{:S(2)}, u32[]{:S(2)}) collective-permute-start(bf16[512,512]{1,0:T(8,128)(2,1)} %get-tuple-element.183), channel_id=1, source_target_pairs={{0,2},{1,3},{2,0},{3,1},{4,6},{5,7},{6,4},{7,5},{8,10},{9,11},{10,... | collective-permute-start | bytes 1572872 | tf_op jit(solution)/shard_map/ppermute | solution.py:511
  77.2 31.7 %collective-permute-start.19 = (bf16[512,512]{1,0:T(8,128)(2,1)}, bf16[512,512]{1,0:T(8,128)(2,1)S(1)}, u32[]{:S(2)}, u32[]{:S(2)}) collective-permute-start(bf16[512,512]{1,0:T(8,128)(2,1)} %get-tuple-element.184), channel_id=1, source_target_pairs={{0,2},{1,3},{2,0},{3,1},{4,6},{5,7},{6,4},{7,5},{8,10},{9,11},{10,... | collective-permute-start | bytes 1572872 | tf_op jit(solution)/shard_map/ppermute | solution.py:511
  109.7 14.7 %collective-permute-start.22 = (bf16[512,512]{1,0:T(8,128)(2,1)}, bf16[512,512]{1,0:T(8,128)(2,1)}, u32[]{:S(2)}, u32[]{:S(2)}) collective-permute-start(bf16[512,512]{1,0:T(8,128)(2,1)} %get-tuple-element.194), channel_id=1, source_target_pairs={{0,2},{1,3},{2,0},{3,1},{4,6},{5,7},{6,4},{7,5},{8,10},{9,11},{10,... | collective-permute-start | bytes 1572872 | tf_op jit(solution)/shard_map/ppermute | solution.py:511
  113.3 14.4 %collective-permute-start.21 = (bf16[512,512]{1,0:T(8,128)(2,1)}, bf16[512,512]{1,0:T(8,128)(2,1)}, u32[]{:S(2)}, u32[]{:S(2)}) collective-permute-start(bf16[512,512]{1,0:T(8,128)(2,1)} %add_convert_fusion.1), channel_id=1, source_target_pairs={{0,4},{4,0},{8,12},{12,8},{16,20},{20,16},{24,28},{28,24},{1,5},{5... | collective-permute-start | bytes 1572872 | tf_op jit(solution)/shard_map/ppermute | solution.py:511
  128.4 14.9 %collective-permute-start.30 = (bf16[512,512]{1,0:T(8,128)(2,1)S(1)}, bf16[512,512]{1,0:T(8,128)(2,1)S(1)}, u32[]{:S(2)}, u32[]{:S(2)}) collective-permute-start(bf16[512,512]{1,0:T(8,128)(2,1)S(1)} %add_convert_fusion), channel_id=1, source_target_pairs={{0,4},{4,0},{8,12},{12,8},{16,20},{20,16},{24,28},{28,24},{1,5},{5... | collective-permute-start | bytes 1572872 | tf_op jit(solution)/shard_map/ppermute | solution.py:511
  134.8 21.6 %collective-permute-start.25 = (f32[80,1024]{1,0:T(8,128)}, f32[80,1024]{1,0:T(8,128)S(1)}, u32[]{:S(2)}, u32[]{:S(2)}) collective-permute-start(f32[80,1024]{1,0:T(8,128)} %get-tuple-element.201), channel_id=1, source_target_pairs={{0,4},{4,0},{8,12},{12,8},{16,20},{20,16},{24,28},{28,24},{1,5},{5... | collective-permute-start | bytes 983048 | tf_op jit(solution)/shard_map/ppermute | solution.py:511
  135.2 21.1 %collective-permute-start.26 = (f32[80,1024]{1,0:T(8,128)}, f32[80,1024]{1,0:T(8,128)S(1)}, u32[]{:S(2)}, u32[]{:S(2)}) collective-permute-start(f32[80,1024]{1,0:T(8,128)} %get-tuple-element.202), channel_id=1, source_target_pairs={{0,2},{1,3},{2,0},{3,1},{4,6},{5,7},{6,4},{7,5},{8,10},{9,11},{10,... | collective-permute-start | bytes 983048 | tf_op jit(solution)/shard_map/ppermute | solution.py:576
  135.7 20.6 %collective-permute-start.27 = (f32[80,1024]{1,0:T(8,128)}, f32[80,1024]{1,0:T(8,128)}, u32[]{:S(2)}, u32[]{:S(2)}) collective-permute-start(f32[80,1024]{1,0:T(8,128)} %get-tuple-element.203), channel_id=1, source_target_pairs={{0,6},{1,7},{2,4},{3,5},{4,2},{5,3},{6,0},{7,1},{8,14},{9,15},{10,... | collective-permute-start | bytes 983048 | tf_op jit(solution)/shard_map/ppermute | solution.py:576
  140.7 12.6 %collective-permute-start.28 = (bf16[128,512]{1,0:T(8,128)(2,1)}, bf16[128,512]{1,0:T(8,128)(2,1)S(1)}, u32[]{:S(2)}, u32[]{:S(2)}) collective-permute-start(bf16[128,512]{1,0:T(8,128)(2,1)} %get-tuple-element.215), channel_id=1, source_target_pairs={{0,16},{4,20},{8,24},{12,28},{16,0},{20,4},{24,8},{28,12},{1,17},{... | collective-permute-start | bytes 393224 | tf_op jit(solution)/shard_map/ppermute | solution.py:511
  143.3 10.1 %collective-permute-start.29 = (bf16[128,512]{1,0:T(8,128)(2,1)}, bf16[128,512]{1,0:T(8,128)(2,1)S(1)}, u32[]{:S(2)}, u32[]{:S(2)}) collective-permute-start(bf16[128,512]{1,0:T(8,128)(2,1)} %get-tuple-element.216), channel_id=1, source_target_pairs={{0,24},{4,28},{8,16},{12,20},{16,8},{20,12},{24,0},{28,4},{1,25},{... | collective-permute-start | bytes 393224 | tf_op jit(solution)/shard_map/ppermute | solution.py:511
  157.1 14.8 %collective-permute-start.35 = (f32[128,512]{1,0:T(8,128)}, f32[128,512]{1,0:T(8,128)}, u32[]{:S(2)}, u32[]{:S(2)}) collective-permute-start(f32[128,512]{1,0:T(8,128)} %get-tuple-element.233), channel_id=1, source_target_pairs={{0,8},{4,12},{8,0},{12,4},{16,24},{20,28},{24,16},{28,20},{1,9},{5... | collective-permute-start | bytes 786440 | tf_op jit(solution)/shard_map/ppermute | solution.py:511
  160.8 13.0 %collective-permute-start.31 = (f32[80,256]{1,0:T(8,128)}, f32[80,256]{1,0:T(8,128)}, u32[]{:S(2)}, u32[]{:S(2)}) collective-permute-start(f32[80,256]{1,0:T(8,128)} %get-tuple-element.226), channel_id=1, source_target_pairs={{0,8},{4,12},{8,0},{12,4},{16,24},{20,28},{24,16},{28,20},{1,9},{5... | collective-permute-start | bytes 245768 | tf_op jit(solution)/shard_map/ppermute | solution.py:511
  161.2 12.6 %collective-permute-start.32 = (f32[80,256]{1,0:T(8,128)}, f32[80,256]{1,0:T(8,128)}, u32[]{:S(2)}, u32[]{:S(2)}) collective-permute-start(f32[80,256]{1,0:T(8,128)} %get-tuple-element.227), channel_id=1, source_target_pairs={{0,16},{4,20},{8,24},{12,28},{16,0},{20,4},{24,8},{28,12},{1,17},{... | collective-permute-start | bytes 245768 | tf_op jit(solution)/shard_map/ppermute | solution.py:511
  163.7 10.0 %collective-permute-start.33 = (f32[80,256]{1,0:T(8,128)}, f32[80,256]{1,0:T(8,128)}, u32[]{:S(2)}, u32[]{:S(2)}) collective-permute-start(f32[80,256]{1,0:T(8,128)} %get-tuple-element.228), channel_id=1, source_target_pairs={{0,24},{4,28},{8,16},{12,20},{16,8},{20,12},{24,0},{28,4},{1,25},{... | collective-permute-start | bytes 245768 | tf_op jit(solution)/shard_map/ppermute | solution.py:511
  165.2 18.3 %collective-permute-start.39 = (f32[128,512]{1,0:T(8,128)}, f32[128,512]{1,0:T(8,128)S(1)}, u32[]{:S(2)}, u32[]{:S(2)}) collective-permute-start(f32[128,512]{1,0:T(8,128)} %get-tuple-element.244), channel_id=1, source_target_pairs={{0,8},{4,12},{8,0},{12,4},{16,24},{20,28},{24,16},{28,20},{1,9},{5... | collective-permute-start | bytes 786440 | tf_op jit(solution)/shard_map/ppermute | solution.py:511
  174.8 8.7 %collective-permute-start.36 = (bf16[80,256]{1,0:T(8,128)(2,1)S(1)}, bf16[80,256]{1,0:T(8,128)(2,1)S(1)}, u32[]{:S(2)}, u32[]{:S(2)}) collective-permute-start(bf16[80,256]{1,0:T(8,128)(2,1)S(1)} %get-tuple-element.267), channel_id=1, source_target_pairs={{0,8},{4,12},{8,0},{12,4},{16,24},{20,28},{24,16},{28,20},{1,9},{5... | collective-permute-start | bytes 122888 | tf_op jit(solution)/shard_map/ppermute | solution.py:511
  179.3 9.1 %collective-permute-start.44 = (bf16[128,512]{1,0:T(8,128)(2,1)S(1)}, bf16[128,512]{1,0:T(8,128)(2,1)S(1)}, u32[]{:S(2)}, u32[]{:S(2)}) collective-permute-start(bf16[128,512]{1,0:T(8,128)(2,1)S(1)} %copy-done.22), channel_id=1, source_target_pairs={{0,24},{4,28},{8,16},{12,20},{16,8},{20,12},{24,0},{28,4},{1,25},{... | collective-permute-start | bytes 393224 | tf_op jit(solution)/shard_map/ppermute | solution.py:511
  185.8 9.3 %collective-permute-start.43 = (bf16[80,1024]{1,0:T(8,128)(2,1)S(1)}, bf16[80,1024]{1,0:T(8,128)(2,1)S(1)}, u32[]{:S(2)}, u32[]{:S(2)}) collective-permute-start(bf16[80,1024]{1,0:T(8,128)(2,1)S(1)} %constant_dynamic-update-slice_fusion.4), channel_id=1, source_target_pairs={{0,6},{1,7},{2,4},{3,5},{4,2},{5,3},{6,0},{7,1},{8,14},{9,15},{10,... | collective-permute-start | bytes 491528 | tf_op jit(solution)/shard_map/ppermute | solution.py:576
  (39 other events, 270.9 us)

commit v17 on v16

--- a/solution.py
+++ b/solution.py
@@ -600,9 +600,10 @@
         target = (far ^ f) * 2 + (low ^ b)
         block = lax.dynamic_update_slice_in_dim(block, piece, target * small, 0)
     partner = swap(block, "group", group, 1)
-    first = jnp.where(core == 0, block, partner)
-    second = jnp.where(core == 0, partner, block)
-    return jnp.concatenate([first, second], axis=0).astype(F32), beside
+    whole = jnp.zeros((2 * rows, width), F32)
+    whole = lax.dynamic_update_slice_in_dim(whole, block.astype(F32), core * rows, 0)
+    whole = lax.dynamic_update_slice_in_dim(whole, partner.astype(F32), (1 - core) * rows, 0)
+    return whole, beside
 
 
 def encoding_tables(patch_count):
@@ -663,10 +664,8 @@
         own_ahead.append(cross(ring.ahead[-1], 1))
         if a:
             own_behind.append(cross(ring.behind[a], 1))
-        last_ahead, last_behind = max(a - 1, 0), max(b - 1, 0)
-        own_ahead[last_ahead:a], own_behind[last_behind:b] = step_all(
-            rings, own_ahead[last_ahead:a], own_behind[last_behind:b]
-        )
+        ahead, behind = slice(max(a - 1, 0), a), slice(max(b - 2, 0), max(b - 1, 0))
+        own_ahead[ahead], own_behind[behind] = step_all(rings, own_ahead[ahead], own_behind[behind])
     ring.ahead, ring.behind = together(ring.ahead, ring.behind)
     own_ahead.append(cross(ring.ahead[-1], 1))
     own_behind.extend(cross(x, 1) for x in ring.behind[len(own_behind) + 1 :])
@@ -679,7 +678,7 @@
             blocks = [shard] + own_ahead + own_behind
         made = attention_call(both_counts, owners, low, *both, None if f else (packs, weights), blocks, dp)
         if f == 1:
-            made, own_ahead[-2:], own_behind[-2:] = together(made, own_ahead[-2:], own_behind[-2:])
+            made, own_ahead[-2:], own_behind[-3:] = together(made, own_ahead[-2:], own_behind[-3:])
         elif f:
             made = together(*made)
         else:
@@ -688,16 +687,20 @@
         packs.append(pack)
         weights.append(weight)
         if f:
-            crossing.append([cross(x, f) for x in (*other, *keep)])
+            crossing.append([cross(x, f) for x in (*other, keep[0])] + [keep[1]])
     back_far = swap(back[1], "group", group, 1)
     coming = []
     for c in range(2):
         send = other[c]
         for x in arrived:
             send = send + x[c].astype(F32)
-        coming.append(swap(send.astype(BF16), "dp", dp, 1))
+        send = send.astype(BF16)
+        if c == 0:
+            send, last_keeps = together(send, [x[3] for x in crossing])
+        coming.append(swap(send, "dp", dp, 1))
+    last_keeps = [cross(x, f) for f, x in zip(fars, last_keeps)]
     stem_made, coming[0], last_keeps = together(
-        tail_call(core, back[0], back_far, emb, both[0], cols, gain), coming[0], [x[3] for x in crossing]
+        tail_call(core, back[0], back_far, emb, both[0], cols, gain), coming[0], last_keeps
     )
     stem_keep, *stem_recv = stem_made
     stem_recv = [swap(x, "group", group, 1) for x in stem_recv]

time: 200 us -> 197 us (0.985)
  starting transfers between devices: 52 us -> 46.2 us
  waiting for transfers between devices: 40.1 us -> 42.6 us
    ppermute x4, waiting for transfers between devices: 13.1 us -> 17.1 us  [send(): moved = [lax.ppermute(self.ahead[-1], self.axis, self.forward)]]
    ppermute x35, starting transfers between devices: 38.1 us -> 35 us  [swap(): return lax.ppermute(x, axis, [(i, i ^ bit) for i in range(size)])]
    ppermute x4, starting transfers between devices: 6.24 us -> 3.65 us  [hop(): return lax.ppermute(block, ('dp', 'group'), pairs)]
    convert_element_type x3 -> x2, other arithmetic: 4.13 us -> 2.34 us  [on_device(): send = send.astype(BF16)]
    unnamed x50 -> x54, local copies, waits for them, and re-layouts: 6.16 us -> 7.74 us
  transfers between devices with their start and end apart: 46 -> 46, of which waited for: 17 -> 19; matrix products, arithmetic and copies ran while one was open for 2% -> 3% of each run, Pallas kernels for 46% -> 47%
where the time goes in v17:
time: 197 us; the launch traced here: 196 us
  Pallas kernels  93.5 us (47%)
  starting transfers between devices  46.2 us (23%)
  waiting for transfers between devices  42.6 us (22%)
  local copies, waits for them, and re-layouts  8.23 us (4%)
  other arithmetic  4.8 us (2%)
    pallas_call x2, Pallas kernels, attention_call(): pl.pallas_call(functools.partial(attention_kernel, packs, len(blocks), dp...  53.1 us
    ppermute x35, starting transfers between devices, swap(): return lax.ppermute(x, axis, [(i, i ^ bit) for i in range(size)])  35 us
    ppermute x35, waiting for transfers between devices, swap(): return lax.ppermute(x, axis, [(i, i ^ bit) for i in range(size)])  18.2 us
    ppermute x4, waiting for transfers between devices, send(): moved = [lax.ppermute(self.ahead[-1], self.axis, self.forward)]  17.1 us
    pallas_call x1, Pallas kernels, tail_call(): pl.pallas_call(tail_kernel, grid=(tokens // rows,), in_specs=[SCALARS, pe...  8.83 us
    pallas_call x1, Pallas kernels, stem_call(): pl.pallas_call(stem_kernel, grid=(scenes // block,), in_specs=[pl.BlockSp...  8.29 us
    pallas_call x3, Pallas kernels, combine_call(): pl.pallas_call(functools.partial(combine_kernel, [len(part) for part in p...  8.05 us
    unnamed x54, local copies, waits for them, and re-layouts  7.74 us
  transfers between devices with their start and end apart: 46, of which 19 were waited for; matrix products, arithmetic and copies ran while one was open for 3% of the time, Pallas kernels for 47%

profile of v17, /device:TPU:0, one launch (start us, length us, event | category | flops | bytes accessed | tf_op | source)
XLA Modules:
  0.0 196.4 jit_solution(11907934982413511942)
XLA Ops:
  0.6 1.7 pack_weights.1.refs_2_
  2.3 2.9 %collective-permute-start.1 = (bf16[128,1024]{1,0:T(8,128)(2,1)}, bf16[128,1024]{1,0:T(8,128)(2,1)}, u32[]{:S(2)}, u32[]{:S(2)}) collective-permute-start(bf16[128,1024]{1,0:T(8,128)(2,1)} %pack_weights.1.refs_2_), channel_id=1, source_target_pairs={{0,2},{1,3},{2,0},{3,1},{4,6},{5,7},{6,4},{7,5},{8,10},{9,11},{10,... | collective-permute-start | bytes 786440 | tf_op jit(solution)/shard_map/ppermute | solution.py:511
  5.3 8.3 %stem_norm.1 = (bf16[6,144,1024]{2,1,0:T(8,128)(2,1)}, bf16[2,6,144,1024]{3,2,1,0:T(8,128)(2,1)}, bf16[6,144,256]{2,1,0:T(8,128)(2,1)}) custom-call(s32[3,6]{1,0:T(4,128)} %bitcast.29, s32[6,3,48]{2,1,0:T(4,128)} %idx_ref.1, bf16[6,144,640]{2,1,0:T(8,128)(2,1)} %patch_ref.1, bf16[640,1024]{1,0:T(8,128)(2,1)} %w_ref.1, f32[1,1024]{1,0:T(1,128)} %bitcast.32, ...), custom_call_target="tpu_custom_call" | custom-call | flops 8000000 | bytes 12000 | tf_op jit(solution)/shard_map/stem_norm/pallas_call | solution.py:98
  17.3 5.9 %collective-permute-done.2.refs_1_ = bf16[128,1024]{1,0:T(8,128)(2,1)} collective-permute-done((bf16[128,1024]{1,0:T(8,128)(2,1)}, bf16[128,1024]{1,0:T(8,128)(2,1)}, u32[]{:S(2)}, u32[]{:S(2)}) %collective-permute-start.2) | collective-permute-done | bytes 262176 | tf_op jit(solution)/shard_map/ppermute | solution.py:527
  24.5 1.6 collective-permute-start.5
  27.1 4.7 %collective-permute-done.5.refs_2_ = bf16[128,1024]{1,0:T(8,128)(2,1)S(1)} collective-permute-done((bf16[128,1024]{1,0:T(8,128)(2,1)}, bf16[128,1024]{1,0:T(8,128)(2,1)S(1)}, u32[]{:S(2)}, u32[]{:S(2)}) %collective-permute-start.5) | collective-permute-done | bytes 262176 | tf_op jit(solution)/shard_map/ppermute | solution.py:527
  33.2 1.6 collective-permute-start.7
  35.8 3.9 %collective-permute-done.7.refs_3_ = bf16[128,1024]{1,0:T(8,128)(2,1)} collective-permute-done((bf16[128,1024]{1,0:T(8,128)(2,1)S(1)}, bf16[128,1024]{1,0:T(8,128)(2,1)}, u32[]{:S(2)}, u32[]{:S(2)}) %collective-permute-start.7) | collective-permute-done | bytes 262176 | tf_op jit(solution)/shard_map/ppermute | solution.py:527
  39.7 1.8 collective-permute-done.8.refs_7_
  45.6 2.6 %collective-permute-done.10.refs_4_ = bf16[128,1024]{1,0:T(8,128)(2,1)} collective-permute-done((bf16[128,1024]{1,0:T(8,128)(2,1)}, bf16[128,1024]{1,0:T(8,128)(2,1)}, u32[]{:S(2)}, u32[]{:S(2)}) %collective-permute-start.10) | collective-permute-done | bytes 262176 | tf_op jit(solution)/shard_map/ppermute | solution.py:527
  50.2 22.0 %attention.2 = (bf16[1728,1024]{1,0:T(8,128)(2,1)}, bf16[1024,1024]{1,0:T(8,128)(2,1)}, bf16[512,512]{1,0:T(8,128)(2,1)}, bf16[512,512]{1,0:T(8,128)(2,1)}, bf16...) custom-call(s32[2,3,6]{2,1,0:T(4,128)} %pad_add_fusion.cnt_ref, s32[8]{0:T(128)} %compare_select_fusion.2.owner_ref, ...), custom_call_target="tpu_custom_call" | custom-call | flops 20000000 | bytes 14000 | tf_op jit(solution)/shard_map/attention/pallas_call | solution.py:278
  75.6 31.1 %attention.3 = (bf16[1728,1024]{1,0:T(8,128)(2,1)}, bf16[1024,1024]{1,0:T(8,128)(2,1)}, f32[512,512]{1,0:T(8,128)}, f32[512,512]{1,0:T(8,128)}, f32[512,512]{1,0...) custom-call(s32[2,3,6]{2,1,0:T(4,128)} %pad_add_fusion.cnt_ref, ...), custom_call_target="tpu_custom_call" | custom-call | flops 20000000 | bytes 14000 | tf_op jit(solution)/shard_map/attention/pallas_call | solution.py:278
  107.5 2.2 %add_convert_fusion.1 = bf16[512,512]{1,0:T(8,128)(2,1)} fusion(f32[512,512]{1,0:T(8,128)} %get-tuple-element.194, bf16[512,512]{1,0:T(8,128)(2,1)S(1)} %collective-permute-done.17), kind=kLoop, calls=%fused_computation.3 | loop fusion | flops 786432 | bytes 2097152 | tf_op jit(solution)/shard_map/convert_element_type | solution.py:697
  112.8 8.8 %tail.1 = (f32[320,1024]{1,0:T(8,128)}, f32[320,512]{1,0:T(8,128)}, f32[320,512]{1,0:T(8,128)}) custom-call(s32[1]{0:T(128)} %bitcast.2.core_ref, f32[864,1024]{1,0:T(8,128)} %get-tuple-element.187.own_ref, bf16[864,1024]{1,0:T(8,128)(2,1)} %copy-done.4, bf16[864,1024]{1,0:T(8,128)(2,1)} %bitcast.22, bf16[2,864,1024]{2,1,0:T(8,128)(2,1)} %bitcast.21, ...), custom_call_target="tpu_custom_call" | custom-call | flops 10000000 | bytes 12000 | tf_op jit(solution)/shard_map/tail/pallas_call | solution.py:466
  121.7 2.7 %collective-permute-done.21.refs_2_ = bf16[512,512]{1,0:T(8,128)(2,1)} collective-permute-done((bf16[512,512]{1,0:T(8,128)(2,1)}, bf16[512,512]{1,0:T(8,128)(2,1)}, u32[]{:S(2)}, u32[]{:S(2)}) %collective-permute-start.21) | collective-permute-done | bytes 524320 | tf_op jit(solution)/shard_map/ppermute | solution.py:511
  125.2 1.7 collective-permute-start.30
  128.7 2.9 %combine.3 = (f32[80,1024]{1,0:T(8,128)}, f32[80,1024]{1,0:T(8,128)}, f32[80,1024]{1,0:T(8,128)}, f32[80,1024]{1,0:T(8,128)}) custom-call(s32[1]{0:T(128)} %bitcast.1.place_ref, f32[320,1024]{1,0:T(8,128)} %get-tuple-element.199.refs_0_, f32[320,512]{1,0:T(8,128)} %copy-done.6, f32[320,512]{1,0:T(8,128)} %copy-done.7), custom_call_target="tpu_custom_call" | custom-call | flops 1000 | bytes 5000 | tf_op jit(solution)/shard_map/combine/pallas_call | solution.py:327
  131.6 1.6 collective-permute-start.25
  135.1 2.5 %combine.4 = (f32[128,512]{1,0:T(8,128)}, f32[128,512]{1,0:T(8,128)}, bf16[128,512]{1,0:T(8,128)(2,1)}, bf16[128,512]{1,0:T(8,128)(2,1)}) custom-call(s32[1]{0:T(128)} %bitcast.place_ref, f32[512,512]{1,0:T(8,128)} %get-tuple-element.215.refs_0_, bf16[512,512]{1,0:T(8,128)(2,1)} %copy-done.8, bf16[512,512]{1,0:T(8,128)(2,1)} %collective-permute-done.21.refs_2_), custom_call_target="tpu_custom_call" | custom-call | flops 1000 | bytes 5000 | tf_op jit(solution)/shard_map/combine/pallas_call | solution.py:327
  141.6 3.7 %mixed.1 = bf16[864,1024]{1,0:T(8,128)(2,1)} custom-call(bf16[1728,1024]{1,0:T(8,128)(2,1)} %get-tuple-element.167.refs_0_, bf16[1728,1024]{1,0:T(8,128)(2,1)} %get-tuple-element.208.refs_1_, bf16[1024,1024]{1,0:T(8,128)(2,1)} %get-tuple-element.168.refs_1_.refs_2_, bf16[1024,1024]{1,0:T(8,128)(2,1)} %get-tuple-element.209.refs_3_), custom_call_target="tpu_custom_call" | custom-call | flops 2000000 | bytes 5000 | tf_op jit(solution)/shard_map/mixed/pallas_call | solution.py:412
  145.3 2.7 %combine.5 = (f32[128,512]{1,0:T(8,128)}, f32[128,512]{1,0:T(8,128)}, bf16[128,512]{1,0:T(8,128)(2,1)}, bf16[128,512]{1,0:T(8,128)(2,1)}) custom-call(s32[1]{0:T(128)} %bitcast.place_ref, f32[512,512]{1,0:T(8,128)} %get-tuple-element.221.refs_0_, bf16[512,512]{1,0:T(8,128)(2,1)} %collective-permute-done.22.refs_1_, bf16[512,512]{1,0:T(8,128)(2,1)} %copy-done.9), custom_call_target="tpu_custom_call" | custom-call | flops 1000 | bytes 5000 | tf_op jit(solution)/shard_map/combine/pallas_call | solution.py:327
  147.9 2.0 %collective-permute-done.28.refs_1_ = bf16[128,512]{1,0:T(8,128)(2,1)S(1)} collective-permute-done((bf16[128,512]{1,0:T(8,128)(2,1)}, bf16[128,512]{1,0:T(8,128)(2,1)S(1)}, u32[]{:S(2)}, u32[]{:S(2)}) %collective-permute-start.28) | collective-permute-done | bytes 131104 | tf_op jit(solution)/shard_map/ppermute | solution.py:511
  149.9 3.2 %collective-permute-done.25.refs_1_ = f32[80,1024]{1,0:T(8,128)S(1)} collective-permute-done((f32[80,1024]{1,0:T(8,128)}, f32[80,1024]{1,0:T(8,128)S(1)}, u32[]{:S(2)}, u32[]{:S(2)}) %collective-permute-start.25) | collective-permute-done | bytes 327712 | tf_op jit(solution)/shard_map/ppermute | solution.py:511
  155.3 2.0 %split_sum.1 = (f32[80,256]{1,0:T(8,128)}, f32[80,256]{1,0:T(8,128)}, f32[80,256]{1,0:T(8,128)}, f32[80,256]{1,0:T(8,128)}) custom-call(s32[1]{0:T(128)} %bitcast.place_ref, f32[80,1024]{1,0:T(8,128)} %get-tuple-element.204.refs_0_, f32[80,1024]{1,0:T(8,128)} %copy-done.12, f32[80,1024]{1,0:T(8,128)} %copy-done.13, f32[80,1024]{1,0:T(8,128)} %collective-permute-done.27.refs_3_), custom_call_target="tpu_custom_call" | custom-call | flops 1000 | bytes 2000 | tf_op jit(solution)/shard_map/split_sum/pallas_call | solution.py:354
  159.5 2.3 %collective-permute-start.33 = (f32[80,256]{1,0:T(8,128)}, f32[80,256]{1,0:T(8,128)}, u32[]{:S(2)}, u32[]{:S(2)}) collective-permute-start(f32[80,256]{1,0:T(8,128)} %get-tuple-element.232), channel_id=1, source_target_pairs={{0,24},{4,28},{8,16},{12,20},{16,8},{20,12},{24,0},{28,4},{1,25},{... | collective-permute-start | bytes 245768 | tf_op jit(solution)/shard_map/ppermute | solution.py:511
  163.0 5.4 %layer_output.1 = bf16[864,1024]{1,0:T(8,128)(2,1)} custom-call(s32[3,6]{1,0:T(4,128)} %bitcast.30, bf16[864,1024]{1,0:T(8,128)(2,1)} %copy-done.2, bf16[864,1024]{1,0:T(8,128)(2,1)} %bitcast.23, bf16[1728,1024]{1,0:T(8,128)(2,1)} %get-tuple-element.167.refs_0_, bf16[1728,1024]{1,0:T(8,128)(2,1)} %get-tuple-element.208.refs_1_, ...), custom_call_target="tpu_custom_call" | custom-call | flops 5000000 | bytes 10000 | tf_op jit(solution)/shard_map/layer_output/pallas_call | solution.py:497
  171.8 1.7 collective-permute-start.37
  178.1 4.8 %collective-permute-done.37 = bf16[80,256]{1,0:T(8,128)(2,1)S(1)} collective-permute-done((bf16[80,256]{1,0:T(8,128)(2,1)S(1)}, bf16[80,256]{1,0:T(8,128)(2,1)S(1)}, u32[]{:S(2)}, u32[]{:S(2)}) %collective-permute-start.37) | collective-permute-done | bytes 40992 | tf_op jit(solution)/shard_map/ppermute | solution.py:511
  183.0 1.8 collective-permute-start.41
  187.3 2.3 %weight_results.1 = (f32[3,128,256]{2,1,0:T(8,128)}, f32[256,128]{1,0:T(8,128)}) custom-call(f32[128,512]{1,0:T(8,128)} %get-tuple-element.254.refs_0_, bf16[128,512]{1,0:T(8,128)(2,1)} %copy-done.18, bf16[128,512]{1,0:T(8,128)(2,1)} %copy-done.19, f32[128,512]{1,0:T(8,128)} %collective-permute-done.35.refs_3_, f32[128,512]{1,0:T(8,128)} %get-tuple-element.258.refs_4_, ...), custom_call_target="tpu_custom_call" | custom-call | flops 1000 | bytes 2000 | tf_op jit(solution)/shard_map/weight_results/pallas_call | solution.py:377
  190.2 2.4 %collective-permute-done.43 = bf16[80,1024]{1,0:T(8,128)(2,1)S(1)} collective-permute-done((bf16[80,1024]{1,0:T(8,128)(2,1)S(1)}, bf16[80,1024]{1,0:T(8,128)(2,1)S(1)}, u32[]{:S(2)}, u32[]{:S(2)}) %collective-permute-start.43) | collective-permute-done | bytes 163872 | tf_op jit(solution)/shard_map/ppermute | solution.py:576
  193.2 1.6 collective-permute-done.45
  (143 shorter events, 49.0 us)
Async XLA Ops:
  2.3 11.9 %collective-permute-start.1 = (bf16[128,1024]{1,0:T(8,128)(2,1)}, bf16[128,1024]{1,0:T(8,128)(2,1)}, u32[]{:S(2)}, u32[]{:S(2)}) collective-permute-start(bf16[128,1024]{1,0:T(8,128)(2,1)} %pack_weights.1.refs_2_), channel_id=1, source_target_pairs={{0,2},{1,3},{2,0},{3,1},{4,6},{5,7},{6,4},{7,5},{8,10},{9,11},{10,... | collective-permute-start | bytes 786440 | tf_op jit(solution)/shard_map/ppermute | solution.py:511
  5.3 8.3 %collective-permute-start = (s32[3,6]{1,0:T(4,128)}, s32[3,6]{1,0:T(4,128)S(1)}, u32[]{:S(2)}, u32[]{:S(2)}) collective-permute-start(s32[3,6]{1,0:T(4,128)} %bitcast.28), channel_id=1, source_target_pairs={{0,1},{1,0},{2,3},{3,2},{4,5},{5,4},{6,7},{7,6},{8,9},{9,8},{10,11... | collective-permute-start | bytes 224 | tf_op jit(solution)/shard_map/ppermute | solution.py:511
  14.2 10.3 %collective-permute-start.4 = (bf16[2,864,1024]{2,1,0:T(8,128)(2,1)}, bf16[2,864,1024]{2,1,0:T(8,128)(2,1)S(1)}, u32[]{:S(2)}, u32[]{:S(2)}) collective-permute-start(bf16[2,864,1024]{2,1,0:T(8,128)(2,1)} %bitcast.16), channel_id=1, source_target_pairs={{0,1},{1,0},{2,3},{3,2},{4,5},{5,4},{6,7},{7,6},{8,9},{9,8},{10,11... | collective-permute-start | bytes 10616840 | tf_op jit(solution)/shard_map/ppermute | solution.py:511
  14.7 8.5 %collective-permute-start.2 = (bf16[128,1024]{1,0:T(8,128)(2,1)}, bf16[128,1024]{1,0:T(8,128)(2,1)}, u32[]{:S(2)}, u32[]{:S(2)}) collective-permute-start(bf16[128,1024]{1,0:T(8,128)(2,1)} %collective-permute-done.1.refs_0_), channel_id=1, source_target_pairs={{0,8},{8,16},{16,24},{24,28},{28,20},{20,12},{12,4},{4,0},{1,9},{9... | collective-permute-start | bytes 786440 | tf_op jit(solution)/shard_map/ppermute | solution.py:527
  16.3 8.2 %collective-permute-start.3 = (bf16[128,1024]{1,0:T(8,128)(2,1)}, bf16[128,1024]{1,0:T(8,128)(2,1)}, u32[]{:S(2)}, u32[]{:S(2)}) collective-permute-start(bf16[128,1024]{1,0:T(8,128)(2,1)} %collective-permute-done.1.refs_0_), channel_id=1, source_target_pairs={{8,0},{16,8},{24,16},{28,24},{20,28},{12,20},{4,12},{0,4},{9,1},{1... | collective-permute-start | bytes 786440 | tf_op jit(solution)/shard_map/ppermute | solution.py:529
  26.6 9.2 %collective-permute-start.9 = (bf16[128,1024]{1,0:T(8,128)(2,1)}, bf16[128,1024]{1,0:T(8,128)(2,1)}, u32[]{:S(2)}, u32[]{:S(2)}) collective-permute-start(bf16[128,1024]{1,0:T(8,128)(2,1)} %collective-permute-done.2.refs_1_), channel_id=1, source_target_pairs={{0,2},{1,3},{2,0},{3,1},{4,6},{5,7},{6,4},{7,5},{8,10},{9,11},{10,... | collective-permute-start | bytes 786440 | tf_op jit(solution)/shard_map/ppermute | solution.py:511
  35.2 10.3 %collective-permute-start.11 = (bf16[128,1024]{1,0:T(8,128)(2,1)S(1)}, bf16[128,1024]{1,0:T(8,128)(2,1)}, u32[]{:S(2)}, u32[]{:S(2)}) collective-permute-start(bf16[128,1024]{1,0:T(8,128)(2,1)S(1)} %collective-permute-done.5.refs_2_), channel_id=1, source_target_pairs={{0,2},{1,3},{2,0},{3,1},{4,6},{5,7},{6,4},{7,5},{8,10},{9,11},{10,... | collective-permute-start | bytes 786440 | tf_op jit(solution)/shard_map/ppermute | solution.py:511
  43.0 29.2 %collective-permute-start.14 = (bf16[128,1024]{1,0:T(8,128)(2,1)}, bf16[128,1024]{1,0:T(8,128)(2,1)S(1)}, u32[]{:S(2)}, u32[]{:S(2)}) collective-permute-start(bf16[128,1024]{1,0:T(8,128)(2,1)} %collective-permute-done.3.refs_5_), channel_id=1, source_target_pairs={{0,2},{1,3},{2,0},{3,1},{4,6},{5,7},{6,4},{7,5},{8,10},{9,11},{10,... | collective-permute-start | bytes 786440 | tf_op jit(solution)/shard_map/ppermute | solution.py:511
  43.5 28.7 %collective-permute-start.15 = (bf16[128,1024]{1,0:T(8,128)(2,1)}, bf16[128,1024]{1,0:T(8,128)(2,1)S(1)}, u32[]{:S(2)}, u32[]{:S(2)}) collective-permute-start(bf16[128,1024]{1,0:T(8,128)(2,1)} %collective-permute-done.6.refs_6_), channel_id=1, source_target_pairs={{0,2},{1,3},{2,0},{3,1},{4,6},{5,7},{6,4},{7,5},{8,10},{9,11},{10,... | collective-permute-start | bytes 786440 | tf_op jit(solution)/shard_map/ppermute | solution.py:511
  45.0 27.2 %collective-permute-start.12 = (bf16[128,1024]{1,0:T(8,128)(2,1)}, bf16[128,1024]{1,0:T(8,128)(2,1)}, u32[]{:S(2)}, u32[]{:S(2)}) collective-permute-start(bf16[128,1024]{1,0:T(8,128)(2,1)} %collective-permute-done.7.refs_3_), channel_id=1, source_target_pairs={{0,2},{1,3},{2,0},{3,1},{4,6},{5,7},{6,4},{7,5},{8,10},{9,11},{10,... | collective-permute-start | bytes 786440 | tf_op jit(solution)/shard_map/ppermute | solution.py:511
  48.2 24.1 %collective-permute-start.13 = (bf16[128,1024]{1,0:T(8,128)(2,1)}, bf16[128,1024]{1,0:T(8,128)(2,1)}, u32[]{:S(2)}, u32[]{:S(2)}) collective-permute-start(bf16[128,1024]{1,0:T(8,128)(2,1)} %collective-permute-done.10.refs_4_), channel_id=1, source_target_pairs={{0,2},{1,3},{2,0},{3,1},{4,6},{5,7},{6,4},{7,5},{8,10},{9,11},{10,... | collective-permute-start | bytes 786440 | tf_op jit(solution)/shard_map/ppermute | solution.py:511
  48.7 23.5 %collective-permute-start.16 = (bf16[128,1024]{1,0:T(8,128)(2,1)}, bf16[128,1024]{1,0:T(8,128)(2,1)}, u32[]{:S(2)}, u32[]{:S(2)}) collective-permute-start(bf16[128,1024]{1,0:T(8,128)(2,1)} %collective-permute-done.8.refs_7_), channel_id=1, source_target_pairs={{0,2},{1,3},{2,0},{3,1},{4,6},{5,7},{6,4},{7,5},{8,10},{9,11},{10,... | collective-permute-start | bytes 786440 | tf_op jit(solution)/shard_map/ppermute | solution.py:511
  73.0 33.7 %collective-permute-start.17 = (bf16[512,512]{1,0:T(8,128)(2,1)}, bf16[512,512]{1,0:T(8,128)(2,1)S(1)}, u32[]{:S(2)}, u32[]{:S(2)}) collective-permute-start(bf16[512,512]{1,0:T(8,128)(2,1)} %get-tuple-element.184), channel_id=1, source_target_pairs={{0,2},{1,3},{2,0},{3,1},{4,6},{5,7},{6,4},{7,5},{8,10},{9,11},{10,... | collective-permute-start | bytes 1572872 | tf_op jit(solution)/shard_map/ppermute | solution.py:511
  73.5 33.2 %collective-permute-start.18 = (bf16[512,512]{1,0:T(8,128)(2,1)}, bf16[512,512]{1,0:T(8,128)(2,1)S(1)}, u32[]{:S(2)}, u32[]{:S(2)}) collective-permute-start(bf16[512,512]{1,0:T(8,128)(2,1)} %get-tuple-element.185), channel_id=1, source_target_pairs={{0,2},{1,3},{2,0},{3,1},{4,6},{5,7},{6,4},{7,5},{8,10},{9,11},{10,... | collective-permute-start | bytes 1572872 | tf_op jit(solution)/shard_map/ppermute | solution.py:511
  75.0 31.7 %collective-permute-start.19 = (bf16[512,512]{1,0:T(8,128)(2,1)}, bf16[512,512]{1,0:T(8,128)(2,1)S(1)}, u32[]{:S(2)}, u32[]{:S(2)}) collective-permute-start(bf16[512,512]{1,0:T(8,128)(2,1)} %get-tuple-element.186), channel_id=1, source_target_pairs={{0,2},{1,3},{2,0},{3,1},{4,6},{5,7},{6,4},{7,5},{8,10},{9,11},{10,... | collective-permute-start | bytes 1572872 | tf_op jit(solution)/shard_map/ppermute | solution.py:511
  109.7 14.7 %collective-permute-start.21 = (bf16[512,512]{1,0:T(8,128)(2,1)}, bf16[512,512]{1,0:T(8,128)(2,1)}, u32[]{:S(2)}, u32[]{:S(2)}) collective-permute-start(bf16[512,512]{1,0:T(8,128)(2,1)} %add_convert_fusion.1), channel_id=1, source_target_pairs={{0,4},{4,0},{8,12},{12,8},{16,20},{20,16},{24,28},{28,24},{1,5},{5... | collective-permute-start | bytes 1572872 | tf_op jit(solution)/shard_map/ppermute | solution.py:511
  110.2 14.4 %collective-permute-start.22 = (bf16[512,512]{1,0:T(8,128)(2,1)}, bf16[512,512]{1,0:T(8,128)(2,1)}, u32[]{:S(2)}, u32[]{:S(2)}) collective-permute-start(bf16[512,512]{1,0:T(8,128)(2,1)} %get-tuple-element.198), channel_id=1, source_target_pairs={{0,2},{1,3},{2,0},{3,1},{4,6},{5,7},{6,4},{7,5},{8,10},{9,11},{10,... | collective-permute-start | bytes 1572872 | tf_op jit(solution)/shard_map/ppermute | solution.py:511
  125.2 14.9 %collective-permute-start.30 = (bf16[512,512]{1,0:T(8,128)(2,1)S(1)}, bf16[512,512]{1,0:T(8,128)(2,1)S(1)}, u32[]{:S(2)}, u32[]{:S(2)}) collective-permute-start(bf16[512,512]{1,0:T(8,128)(2,1)S(1)} %add_convert_fusion), channel_id=1, source_target_pairs={{0,4},{4,0},{8,12},{12,8},{16,20},{20,16},{24,28},{28,24},{1,5},{5... | collective-permute-start | bytes 1572872 | tf_op jit(solution)/shard_map/ppermute | solution.py:511
  131.6 21.6 %collective-permute-start.25 = (f32[80,1024]{1,0:T(8,128)}, f32[80,1024]{1,0:T(8,128)S(1)}, u32[]{:S(2)}, u32[]{:S(2)}) collective-permute-start(f32[80,1024]{1,0:T(8,128)} %get-tuple-element.205), channel_id=1, source_target_pairs={{0,4},{4,0},{8,12},{12,8},{16,20},{20,16},{24,28},{28,24},{1,5},{5... | collective-permute-start | bytes 983048 | tf_op jit(solution)/shard_map/ppermute | solution.py:511
  133.1 20.0 %collective-permute-start.26 = (f32[80,1024]{1,0:T(8,128)}, f32[80,1024]{1,0:T(8,128)S(1)}, u32[]{:S(2)}, u32[]{:S(2)}) collective-permute-start(f32[80,1024]{1,0:T(8,128)} %get-tuple-element.206), channel_id=1, source_target_pairs={{0,2},{1,3},{2,0},{3,1},{4,6},{5,7},{6,4},{7,5},{8,10},{9,11},{10,... | collective-permute-start | bytes 983048 | tf_op jit(solution)/shard_map/ppermute | solution.py:576
  134.6 18.5 %collective-permute-start.27 = (f32[80,1024]{1,0:T(8,128)}, f32[80,1024]{1,0:T(8,128)}, u32[]{:S(2)}, u32[]{:S(2)}) collective-permute-start(f32[80,1024]{1,0:T(8,128)} %get-tuple-element.207), channel_id=1, source_target_pairs={{0,6},{1,7},{2,4},{3,5},{4,2},{5,3},{6,0},{7,1},{8,14},{9,15},{10,... | collective-permute-start | bytes 983048 | tf_op jit(solution)/shard_map/ppermute | solution.py:576
  137.5 12.4 %collective-permute-start.28 = (bf16[128,512]{1,0:T(8,128)(2,1)}, bf16[128,512]{1,0:T(8,128)(2,1)S(1)}, u32[]{:S(2)}, u32[]{:S(2)}) collective-permute-start(bf16[128,512]{1,0:T(8,128)(2,1)} %get-tuple-element.219), channel_id=1, source_target_pairs={{0,16},{4,20},{8,24},{12,28},{16,0},{20,4},{24,8},{28,12},{1,17},{... | collective-permute-start | bytes 393224 | tf_op jit(solution)/shard_map/ppermute | solution.py:511
  140.1 9.9 %collective-permute-start.29 = (bf16[128,512]{1,0:T(8,128)(2,1)}, bf16[128,512]{1,0:T(8,128)(2,1)S(1)}, u32[]{:S(2)}, u32[]{:S(2)}) collective-permute-start(bf16[128,512]{1,0:T(8,128)(2,1)} %get-tuple-element.220), channel_id=1, source_target_pairs={{0,24},{4,28},{8,16},{12,20},{16,8},{20,12},{24,0},{28,4},{1,25},{... | collective-permute-start | bytes 393224 | tf_op jit(solution)/shard_map/ppermute | solution.py:511
  153.9 7.8 %collective-permute-start.34 = (bf16[864,1024]{1,0:T(8,128)(2,1)S(1)}, bf16[864,1024]{1,0:T(8,128)(2,1)S(1)}, u32[]{:S(2)}, u32[]{:S(2)}) collective-permute-start(bf16[864,1024]{1,0:T(8,128)(2,1)S(1)} %copy-done.3), channel_id=1, source_target_pairs={{0,1},{1,0},{2,3},{3,2},{4,5},{5,4},{6,7},{7,6},{8,9},{9,8},{10,11... | collective-permute-start | bytes 5308424 | tf_op jit(solution)/shard_map/ppermute | solution.py:511
  153.9 14.5 %collective-permute-start.35 = (f32[128,512]{1,0:T(8,128)}, f32[128,512]{1,0:T(8,128)}, u32[]{:S(2)}, u32[]{:S(2)}) collective-permute-start(f32[128,512]{1,0:T(8,128)} %get-tuple-element.237), channel_id=1, source_target_pairs={{0,8},{4,12},{8,0},{12,4},{16,24},{20,28},{24,16},{28,20},{1,9},{5... | collective-permute-start | bytes 786440 | tf_op jit(solution)/shard_map/ppermute | solution.py:511
  157.3 12.1 %collective-permute-start.31 = (f32[80,256]{1,0:T(8,128)}, f32[80,256]{1,0:T(8,128)}, u32[]{:S(2)}, u32[]{:S(2)}) collective-permute-start(f32[80,256]{1,0:T(8,128)} %get-tuple-element.230), channel_id=1, source_target_pairs={{0,8},{4,12},{8,0},{12,4},{16,24},{20,28},{24,16},{28,20},{1,9},{5... | collective-permute-start | bytes 245768 | tf_op jit(solution)/shard_map/ppermute | solution.py:511
  158.0 11.5 %collective-permute-start.32 = (f32[80,256]{1,0:T(8,128)}, f32[80,256]{1,0:T(8,128)}, u32[]{:S(2)}, u32[]{:S(2)}) collective-permute-start(f32[80,256]{1,0:T(8,128)} %get-tuple-element.231), channel_id=1, source_target_pairs={{0,16},{4,20},{8,24},{12,28},{16,0},{20,4},{24,8},{28,12},{1,17},{... | collective-permute-start | bytes 245768 | tf_op jit(solution)/shard_map/ppermute | solution.py:511
  159.5 10.0 %collective-permute-start.33 = (f32[80,256]{1,0:T(8,128)}, f32[80,256]{1,0:T(8,128)}, u32[]{:S(2)}, u32[]{:S(2)}) collective-permute-start(f32[80,256]{1,0:T(8,128)} %get-tuple-element.232), channel_id=1, source_target_pairs={{0,24},{4,28},{8,16},{12,20},{16,8},{20,12},{24,0},{28,4},{1,25},{... | collective-permute-start | bytes 245768 | tf_op jit(solution)/shard_map/ppermute | solution.py:511
  161.8 15.7 %collective-permute-start.39 = (f32[128,512]{1,0:T(8,128)}, f32[128,512]{1,0:T(8,128)S(1)}, u32[]{:S(2)}, u32[]{:S(2)}) collective-permute-start(f32[128,512]{1,0:T(8,128)} %get-tuple-element.248), channel_id=1, source_target_pairs={{0,8},{4,12},{8,0},{12,4},{16,24},{20,28},{24,16},{28,20},{1,9},{5... | collective-permute-start | bytes 786440 | tf_op jit(solution)/shard_map/ppermute | solution.py:511
  171.8 11.2 %collective-permute-start.37 = (bf16[80,256]{1,0:T(8,128)(2,1)S(1)}, bf16[80,256]{1,0:T(8,128)(2,1)S(1)}, u32[]{:S(2)}, u32[]{:S(2)}) collective-permute-start(bf16[80,256]{1,0:T(8,128)(2,1)S(1)} %get-tuple-element.271), channel_id=1, source_target_pairs={{0,16},{4,20},{8,24},{12,28},{16,0},{20,4},{24,8},{28,12},{1,17},{... | collective-permute-start | bytes 122888 | tf_op jit(solution)/shard_map/ppermute | solution.py:511
  173.4 9.6 %collective-permute-start.38 = (bf16[80,256]{1,0:T(8,128)(2,1)S(1)}, bf16[80,256]{1,0:T(8,128)(2,1)S(1)}, u32[]{:S(2)}, u32[]{:S(2)}) collective-permute-start(bf16[80,256]{1,0:T(8,128)(2,1)S(1)} %get-tuple-element.271), channel_id=1, source_target_pairs={{0,24},{4,28},{8,16},{12,20},{16,8},{20,12},{24,0},{28,4},{1,25},{... | collective-permute-start | bytes 122888 | tf_op jit(solution)/shard_map/ppermute | solution.py:511
  175.9 10.7 %collective-permute-start.44 = (bf16[128,512]{1,0:T(8,128)(2,1)S(1)}, bf16[128,512]{1,0:T(8,128)(2,1)S(1)}, u32[]{:S(2)}, u32[]{:S(2)}) collective-permute-start(bf16[128,512]{1,0:T(8,128)(2,1)S(1)} %copy-done.24), channel_id=1, source_target_pairs={{0,24},{4,28},{8,16},{12,20},{16,8},{20,12},{24,0},{28,4},{1,25},{... | collective-permute-start | bytes 393224 | tf_op jit(solution)/shard_map/ppermute | solution.py:511
  (41 other events, 259.8 us)

commit v18 on v17

--- a/solution.py
+++ b/solution.py
@@ -721,16 +721,17 @@
         return [output, *arrived[:-1], *spread(first, [1]), arrived[-1]]
 
     def after_second(*arrived):
-        return [*arrived, *spread(second, [1, *range(2, near)])]
-
-    def last(output, *arrived):
-        arrived = [*arrived, *spread(second, range(near, dp // 2))]
-        half = len(arrived) // 2
-        return output, *result_call(arrived[:half], arrived[half:])
-
-    grad_w_stem, (output, grad_w_qkv, grad_w_out) = sum_stem(
+        return [*arrived, *spread(second, [1, *range(2, near)]), second[near:]]
+
+    def last(*arrived):
+        blocks = dict(enumerate(arrived[-1], near))
+        return [*arrived[:-1], *spread(blocks, blocks)]
+
+    grad_w_stem, (output, *arrived) = sum_stem(
         stem_parts, beside, (after_first, after_second), last, dp, group
     )
+    half = len(arrived) // 2
+    grad_w_qkv, grad_w_out = result_call(arrived[:half], arrived[half:])
     return (output.reshape(scenes, GROUPS, CAP, D), grad_w_stem, grad_w_qkv, grad_w_out)
 
 

time: 197 us -> 196 us (level)
    ppermute x4, waiting for transfers between devices: 2.88 us -> 0.01 us  [hop(): return lax.ppermute(block, ('dp', 'group'), pairs)]
    unnamed x54 -> x52, local copies, waits for them, and re-layouts: 7.74 us -> 7.51 us
  transfers between devices with their start and end apart: 46 -> 46, of which waited for: 19 -> 18; matrix products, arithmetic and copies ran while one was open for 3% -> 3% of each run, Pallas kernels for 47% -> 47%
where the time goes in v18:
time: 196 us
  Pallas kernels  93.5 us (48%)
  starting transfers between devices  47 us (24%)
  waiting for transfers between devices  41.7 us (21%)
  local copies, waits for them, and re-layouts  8 us (4%)
  other arithmetic  4.73 us (2%)
    pallas_call x2, Pallas kernels, attention_call(): pl.pallas_call(functools.partial(attention_kernel, packs, len(blocks), dp...  53.1 us
    ppermute x35, starting transfers between devices, swap(): return lax.ppermute(x, axis, [(i, i ^ bit) for i in range(size)])  35.7 us
    ppermute x35, waiting for transfers between devices, swap(): return lax.ppermute(x, axis, [(i, i ^ bit) for i in range(size)])  20.1 us
    ppermute x4, waiting for transfers between devices, send(): moved = [lax.ppermute(self.ahead[-1], self.axis, self.forward)]  17.2 us
    pallas_call x1, Pallas kernels, tail_call(): pl.pallas_call(tail_kernel, grid=(tokens // rows,), in_specs=[SCALARS, pe...  8.84 us
    pallas_call x1, Pallas kernels, stem_call(): pl.pallas_call(stem_kernel, grid=(scenes // block,), in_specs=[pl.BlockSp...  8.32 us
    pallas_call x3, Pallas kernels, combine_call(): pl.pallas_call(functools.partial(combine_kernel, [len(part) for part in p...  8.02 us
    unnamed x52, local copies, waits for them, and re-layouts  7.51 us
  transfers between devices with their start and end apart: 46, of which 18 were waited for; matrix products, arithmetic and copies ran while one was open for 3% of the time, Pallas kernels for 47%

profile of v18, /device:TPU:0, one launch (start us, length us, event | category | flops | bytes accessed | tf_op | source)
XLA Modules:
  0.0 195.9 jit_solution(9580113999837861930)
XLA Ops:
  0.6 1.7 pack_weights.1.refs_2_
  2.3 2.9 %collective-permute-start.1 = (bf16[128,1024]{1,0:T(8,128)(2,1)}, bf16[128,1024]{1,0:T(8,128)(2,1)}, u32[]{:S(2)}, u32[]{:S(2)}) collective-permute-start(bf16[128,1024]{1,0:T(8,128)(2,1)} %pack_weights.1.refs_2_), channel_id=1, source_target_pairs={{0,2},{1,3},{2,0},{3,1},{4,6},{5,7},{6,4},{7,5},{8,10},{9,11},{10,... | collective-permute-start | bytes 786440 | tf_op jit(solution)/shard_map/ppermute | solution.py:511
  5.3 8.3 %stem_norm.1 = (bf16[6,144,1024]{2,1,0:T(8,128)(2,1)}, bf16[2,6,144,1024]{3,2,1,0:T(8,128)(2,1)}, bf16[6,144,256]{2,1,0:T(8,128)(2,1)}) custom-call(s32[3,6]{1,0:T(4,128)} %bitcast.29, s32[6,3,48]{2,1,0:T(4,128)} %idx_ref.1, bf16[6,144,640]{2,1,0:T(8,128)(2,1)} %patch_ref.1, bf16[640,1024]{1,0:T(8,128)(2,1)} %w_ref.1, f32[1,1024]{1,0:T(1,128)} %bitcast.32, ...), custom_call_target="tpu_custom_call" | custom-call | flops 8000000 | bytes 12000 | tf_op jit(solution)/shard_map/stem_norm/pallas_call | solution.py:98
  17.3 6.0 %collective-permute-done.2.refs_1_ = bf16[128,1024]{1,0:T(8,128)(2,1)} collective-permute-done((bf16[128,1024]{1,0:T(8,128)(2,1)}, bf16[128,1024]{1,0:T(8,128)(2,1)}, u32[]{:S(2)}, u32[]{:S(2)}) %collective-permute-start.2) | collective-permute-done | bytes 262176 | tf_op jit(solution)/shard_map/ppermute | solution.py:527
  24.6 1.6 collective-permute-start.5
  27.1 4.7 %collective-permute-done.5.refs_2_ = bf16[128,1024]{1,0:T(8,128)(2,1)S(1)} collective-permute-done((bf16[128,1024]{1,0:T(8,128)(2,1)}, bf16[128,1024]{1,0:T(8,128)(2,1)S(1)}, u32[]{:S(2)}, u32[]{:S(2)}) %collective-permute-start.5) | collective-permute-done | bytes 262176 | tf_op jit(solution)/shard_map/ppermute | solution.py:527
  33.2 1.6 collective-permute-start.7
  35.8 3.9 %collective-permute-done.7.refs_3_ = bf16[128,1024]{1,0:T(8,128)(2,1)} collective-permute-done((bf16[128,1024]{1,0:T(8,128)(2,1)S(1)}, bf16[128,1024]{1,0:T(8,128)(2,1)}, u32[]{:S(2)}, u32[]{:S(2)}) %collective-permute-start.7) | collective-permute-done | bytes 262176 | tf_op jit(solution)/shard_map/ppermute | solution.py:527
  39.7 1.8 collective-permute-done.8.refs_7_
  45.6 2.6 %collective-permute-done.10.refs_4_ = bf16[128,1024]{1,0:T(8,128)(2,1)} collective-permute-done((bf16[128,1024]{1,0:T(8,128)(2,1)}, bf16[128,1024]{1,0:T(8,128)(2,1)}, u32[]{:S(2)}, u32[]{:S(2)}) %collective-permute-start.10) | collective-permute-done | bytes 262176 | tf_op jit(solution)/shard_map/ppermute | solution.py:527
  50.2 22.0 %attention.2 = (bf16[1728,1024]{1,0:T(8,128)(2,1)}, bf16[1024,1024]{1,0:T(8,128)(2,1)}, bf16[512,512]{1,0:T(8,128)(2,1)}, bf16[512,512]{1,0:T(8,128)(2,1)}, bf16...) custom-call(s32[2,3,6]{2,1,0:T(4,128)} %pad_add_fusion.cnt_ref, s32[8]{0:T(128)} %compare_select_fusion.2.owner_ref, ...), custom_call_target="tpu_custom_call" | custom-call | flops 20000000 | bytes 14000 | tf_op jit(solution)/shard_map/attention/pallas_call | solution.py:278
  75.6 31.1 %attention.3 = (bf16[1728,1024]{1,0:T(8,128)(2,1)}, bf16[1024,1024]{1,0:T(8,128)(2,1)}, f32[512,512]{1,0:T(8,128)}, f32[512,512]{1,0:T(8,128)}, f32[512,512]{1,0...) custom-call(s32[2,3,6]{2,1,0:T(4,128)} %pad_add_fusion.cnt_ref, ...), custom_call_target="tpu_custom_call" | custom-call | flops 20000000 | bytes 14000 | tf_op jit(solution)/shard_map/attention/pallas_call | solution.py:278
  107.5 2.2 %add_convert_fusion.1 = bf16[512,512]{1,0:T(8,128)(2,1)} fusion(f32[512,512]{1,0:T(8,128)} %get-tuple-element.201, bf16[512,512]{1,0:T(8,128)(2,1)S(1)} %collective-permute-done.17), kind=kLoop, calls=%fused_computation.3 | loop fusion | flops 786432 | bytes 2097152 | tf_op jit(solution)/shard_map/convert_element_type | solution.py:697
  112.8 8.8 %tail.1 = (f32[320,1024]{1,0:T(8,128)}, f32[320,512]{1,0:T(8,128)}, f32[320,512]{1,0:T(8,128)}) custom-call(s32[1]{0:T(128)} %bitcast.2.core_ref, f32[864,1024]{1,0:T(8,128)} %get-tuple-element.194.own_ref, bf16[864,1024]{1,0:T(8,128)(2,1)} %copy-done.4, bf16[864,1024]{1,0:T(8,128)(2,1)} %bitcast.22, bf16[2,864,1024]{2,1,0:T(8,128)(2,1)} %bitcast.21, ...), custom_call_target="tpu_custom_call" | custom-call | flops 10000000 | bytes 12000 | tf_op jit(solution)/shard_map/tail/pallas_call | solution.py:466
  121.7 2.7 %collective-permute-done.21.refs_2_ = bf16[512,512]{1,0:T(8,128)(2,1)} collective-permute-done((bf16[512,512]{1,0:T(8,128)(2,1)}, bf16[512,512]{1,0:T(8,128)(2,1)}, u32[]{:S(2)}, u32[]{:S(2)}) %collective-permute-start.21) | collective-permute-done | bytes 524320 | tf_op jit(solution)/shard_map/ppermute | solution.py:511
  125.2 1.7 collective-permute-start.30
  128.7 2.9 %combine.3 = (f32[80,1024]{1,0:T(8,128)}, f32[80,1024]{1,0:T(8,128)}, f32[80,1024]{1,0:T(8,128)}, f32[80,1024]{1,0:T(8,128)}) custom-call(s32[1]{0:T(128)} %bitcast.1.place_ref, f32[320,1024]{1,0:T(8,128)} %get-tuple-element.206.refs_0_, f32[320,512]{1,0:T(8,128)} %copy-done.6, f32[320,512]{1,0:T(8,128)} %copy-done.7), custom_call_target="tpu_custom_call" | custom-call | flops 1000 | bytes 5000 | tf_op jit(solution)/shard_map/combine/pallas_call | solution.py:327
  131.6 1.6 collective-permute-start.25
  135.0 2.5 %combine.4 = (f32[128,512]{1,0:T(8,128)}, f32[128,512]{1,0:T(8,128)}, bf16[128,512]{1,0:T(8,128)(2,1)}, bf16[128,512]{1,0:T(8,128)(2,1)}) custom-call(s32[1]{0:T(128)} %bitcast.place_ref, f32[512,512]{1,0:T(8,128)} %get-tuple-element.222.refs_0_, bf16[512,512]{1,0:T(8,128)(2,1)} %copy-done.8, bf16[512,512]{1,0:T(8,128)(2,1)} %collective-permute-done.21.refs_2_), custom_call_target="tpu_custom_call" | custom-call | flops 1000 | bytes 5000 | tf_op jit(solution)/shard_map/combine/pallas_call | solution.py:327
  141.5 3.7 %mixed.1 = bf16[864,1024]{1,0:T(8,128)(2,1)} custom-call(bf16[1728,1024]{1,0:T(8,128)(2,1)} %get-tuple-element.174.refs_0_, bf16[1728,1024]{1,0:T(8,128)(2,1)} %get-tuple-element.215.refs_1_, bf16[1024,1024]{1,0:T(8,128)(2,1)} %get-tuple-element.175.refs_1_.refs_2_, bf16[1024,1024]{1,0:T(8,128)(2,1)} %get-tuple-element.216.refs_3_), custom_call_target="tpu_custom_call" | custom-call | flops 2000000 | bytes 5000 | tf_op jit(solution)/shard_map/mixed/pallas_call | solution.py:412
  145.2 2.6 %combine.5 = (f32[128,512]{1,0:T(8,128)}, f32[128,512]{1,0:T(8,128)}, bf16[128,512]{1,0:T(8,128)(2,1)}, bf16[128,512]{1,0:T(8,128)(2,1)}) custom-call(s32[1]{0:T(128)} %bitcast.place_ref, f32[512,512]{1,0:T(8,128)} %get-tuple-element.228.refs_0_, bf16[512,512]{1,0:T(8,128)(2,1)} %collective-permute-done.22.refs_1_, bf16[512,512]{1,0:T(8,128)(2,1)} %copy-done.9), custom_call_target="tpu_custom_call" | custom-call | flops 1000 | bytes 5000 | tf_op jit(solution)/shard_map/combine/pallas_call | solution.py:327
  147.9 2.0 %collective-permute-done.28.refs_1_ = bf16[128,512]{1,0:T(8,128)(2,1)S(1)} collective-permute-done((bf16[128,512]{1,0:T(8,128)(2,1)}, bf16[128,512]{1,0:T(8,128)(2,1)S(1)}, u32[]{:S(2)}, u32[]{:S(2)}) %collective-permute-start.28) | collective-permute-done | bytes 131104 | tf_op jit(solution)/shard_map/ppermute | solution.py:511
  149.9 3.2 %collective-permute-done.25.refs_1_ = f32[80,1024]{1,0:T(8,128)S(1)} collective-permute-done((f32[80,1024]{1,0:T(8,128)}, f32[80,1024]{1,0:T(8,128)S(1)}, u32[]{:S(2)}, u32[]{:S(2)}) %collective-permute-start.25) | collective-permute-done | bytes 327712 | tf_op jit(solution)/shard_map/ppermute | solution.py:511
  155.3 2.0 %split_sum.1 = (f32[80,256]{1,0:T(8,128)}, f32[80,256]{1,0:T(8,128)}, f32[80,256]{1,0:T(8,128)}, f32[80,256]{1,0:T(8,128)}) custom-call(s32[1]{0:T(128)} %bitcast.place_ref, f32[80,1024]{1,0:T(8,128)} %get-tuple-element.211.refs_0_, f32[80,1024]{1,0:T(8,128)} %copy-done.12, f32[80,1024]{1,0:T(8,128)} %copy-done.13, f32[80,1024]{1,0:T(8,128)} %collective-permute-done.27.refs_3_), custom_call_target="tpu_custom_call" | custom-call | flops 1000 | bytes 2000 | tf_op jit(solution)/shard_map/split_sum/pallas_call | solution.py:354
  159.4 2.3 %collective-permute-start.33 = (f32[80,256]{1,0:T(8,128)}, f32[80,256]{1,0:T(8,128)}, u32[]{:S(2)}, u32[]{:S(2)}) collective-permute-start(f32[80,256]{1,0:T(8,128)} %get-tuple-element.239), channel_id=1, source_target_pairs={{0,24},{4,28},{8,16},{12,20},{16,8},{20,12},{24,0},{28,4},{1,25},{... | collective-permute-start | bytes 245768 | tf_op jit(solution)/shard_map/ppermute | solution.py:511
  163.0 5.5 %layer_output.1 = bf16[864,1024]{1,0:T(8,128)(2,1)} custom-call(s32[3,6]{1,0:T(4,128)} %bitcast.30, bf16[864,1024]{1,0:T(8,128)(2,1)} %copy-done.2, bf16[864,1024]{1,0:T(8,128)(2,1)} %bitcast.23, bf16[1728,1024]{1,0:T(8,128)(2,1)} %get-tuple-element.174.refs_0_, bf16[1728,1024]{1,0:T(8,128)(2,1)} %get-tuple-element.215.refs_1_, ...), custom_call_target="tpu_custom_call" | custom-call | flops 5000000 | bytes 10000 | tf_op jit(solution)/shard_map/layer_output/pallas_call | solution.py:497
  171.7 1.7 collective-permute-start.37
  178.1 2.0 %collective-permute-done.37 = bf16[80,256]{1,0:T(8,128)(2,1)S(1)} collective-permute-done((bf16[80,256]{1,0:T(8,128)(2,1)S(1)}, bf16[80,256]{1,0:T(8,128)(2,1)S(1)}, u32[]{:S(2)}, u32[]{:S(2)}) %collective-permute-start.37) | collective-permute-done | bytes 40992 | tf_op jit(solution)/shard_map/ppermute | solution.py:511
  180.2 1.8 collective-permute-start.41
  183.8 2.3 %collective-permute-start.44 = (bf16[128,512]{1,0:T(8,128)(2,1)}, bf16[128,512]{1,0:T(8,128)(2,1)S(1)}, u32[]{:S(2)}, u32[]{:S(2)}) collective-permute-start(bf16[128,512]{1,0:T(8,128)(2,1)} %get-tuple-element.269), channel_id=1, source_target_pairs={{0,24},{4,28},{8,16},{12,20},{16,8},{20,12},{24,0},{28,4},{1,25},{... | collective-permute-start | bytes 393224 | tf_op jit(solution)/shard_map/ppermute | solution.py:511
  186.1 4.7 %collective-permute-done.44.refs_7_ = bf16[128,512]{1,0:T(8,128)(2,1)S(1)} collective-permute-done((bf16[128,512]{1,0:T(8,128)(2,1)}, bf16[128,512]{1,0:T(8,128)(2,1)S(1)}, u32[]{:S(2)}, u32[]{:S(2)}) %collective-permute-start.44) | collective-permute-done | bytes 131104 | tf_op jit(solution)/shard_map/ppermute | solution.py:511
  191.5 2.3 %weight_results.1 = (f32[3,128,256]{2,1,0:T(8,128)}, f32[256,128]{1,0:T(8,128)}) custom-call(f32[128,512]{1,0:T(8,128)} %get-tuple-element.274.refs_0_, bf16[128,512]{1,0:T(8,128)(2,1)} %copy-done.18, bf16[128,512]{1,0:T(8,128)(2,1)} %copy-done.19, f32[128,512]{1,0:T(8,128)} %collective-permute-done.35.refs_3_, f32[128,512]{1,0:T(8,128)} %get-tuple-element.278.refs_4_, ...), custom_call_target="tpu_custom_call" | custom-call | flops 1000 | bytes 2000 | tf_op jit(solution)/shard_map/weight_results/pallas_call | solution.py:377
  (141 shorter events, 48.3 us)
Async XLA Ops:
  2.3 11.9 %collective-permute-start.1 = (bf16[128,1024]{1,0:T(8,128)(2,1)}, bf16[128,1024]{1,0:T(8,128)(2,1)}, u32[]{:S(2)}, u32[]{:S(2)}) collective-permute-start(bf16[128,1024]{1,0:T(8,128)(2,1)} %pack_weights.1.refs_2_), channel_id=1, source_target_pairs={{0,2},{1,3},{2,0},{3,1},{4,6},{5,7},{6,4},{7,5},{8,10},{9,11},{10,... | collective-permute-start | bytes 786440 | tf_op jit(solution)/shard_map/ppermute | solution.py:511
  5.3 8.3 %collective-permute-start = (s32[3,6]{1,0:T(4,128)}, s32[3,6]{1,0:T(4,128)S(1)}, u32[]{:S(2)}, u32[]{:S(2)}) collective-permute-start(s32[3,6]{1,0:T(4,128)} %bitcast.28), channel_id=1, source_target_pairs={{0,1},{1,0},{2,3},{3,2},{4,5},{5,4},{6,7},{7,6},{8,9},{9,8},{10,11... | collective-permute-start | bytes 224 | tf_op jit(solution)/shard_map/ppermute | solution.py:511
  14.2 10.3 %collective-permute-start.4 = (bf16[2,864,1024]{2,1,0:T(8,128)(2,1)}, bf16[2,864,1024]{2,1,0:T(8,128)(2,1)S(1)}, u32[]{:S(2)}, u32[]{:S(2)}) collective-permute-start(bf16[2,864,1024]{2,1,0:T(8,128)(2,1)} %bitcast.16), channel_id=1, source_target_pairs={{0,1},{1,0},{2,3},{3,2},{4,5},{5,4},{6,7},{7,6},{8,9},{9,8},{10,11... | collective-permute-start | bytes 10616840 | tf_op jit(solution)/shard_map/ppermute | solution.py:511
  14.7 8.5 %collective-permute-start.2 = (bf16[128,1024]{1,0:T(8,128)(2,1)}, bf16[128,1024]{1,0:T(8,128)(2,1)}, u32[]{:S(2)}, u32[]{:S(2)}) collective-permute-start(bf16[128,1024]{1,0:T(8,128)(2,1)} %collective-permute-done.1.refs_0_), channel_id=1, source_target_pairs={{0,8},{8,16},{16,24},{24,28},{28,20},{20,12},{12,4},{4,0},{1,9},{9... | collective-permute-start | bytes 786440 | tf_op jit(solution)/shard_map/ppermute | solution.py:527
  16.3 8.2 %collective-permute-start.3 = (bf16[128,1024]{1,0:T(8,128)(2,1)}, bf16[128,1024]{1,0:T(8,128)(2,1)}, u32[]{:S(2)}, u32[]{:S(2)}) collective-permute-start(bf16[128,1024]{1,0:T(8,128)(2,1)} %collective-permute-done.1.refs_0_), channel_id=1, source_target_pairs={{8,0},{16,8},{24,16},{28,24},{20,28},{12,20},{4,12},{0,4},{9,1},{1... | collective-permute-start | bytes 786440 | tf_op jit(solution)/shard_map/ppermute | solution.py:529
  26.6 9.2 %collective-permute-start.9 = (bf16[128,1024]{1,0:T(8,128)(2,1)}, bf16[128,1024]{1,0:T(8,128)(2,1)}, u32[]{:S(2)}, u32[]{:S(2)}) collective-permute-start(bf16[128,1024]{1,0:T(8,128)(2,1)} %collective-permute-done.2.refs_1_), channel_id=1, source_target_pairs={{0,2},{1,3},{2,0},{3,1},{4,6},{5,7},{6,4},{7,5},{8,10},{9,11},{10,... | collective-permute-start | bytes 786440 | tf_op jit(solution)/shard_map/ppermute | solution.py:511
  35.3 10.3 %collective-permute-start.11 = (bf16[128,1024]{1,0:T(8,128)(2,1)S(1)}, bf16[128,1024]{1,0:T(8,128)(2,1)}, u32[]{:S(2)}, u32[]{:S(2)}) collective-permute-start(bf16[128,1024]{1,0:T(8,128)(2,1)S(1)} %collective-permute-done.5.refs_2_), channel_id=1, source_target_pairs={{0,2},{1,3},{2,0},{3,1},{4,6},{5,7},{6,4},{7,5},{8,10},{9,11},{10,... | collective-permute-start | bytes 786440 | tf_op jit(solution)/shard_map/ppermute | solution.py:511
  43.0 29.2 %collective-permute-start.14 = (bf16[128,1024]{1,0:T(8,128)(2,1)}, bf16[128,1024]{1,0:T(8,128)(2,1)S(1)}, u32[]{:S(2)}, u32[]{:S(2)}) collective-permute-start(bf16[128,1024]{1,0:T(8,128)(2,1)} %collective-permute-done.3.refs_5_), channel_id=1, source_target_pairs={{0,2},{1,3},{2,0},{3,1},{4,6},{5,7},{6,4},{7,5},{8,10},{9,11},{10,... | collective-permute-start | bytes 786440 | tf_op jit(solution)/shard_map/ppermute | solution.py:511
  43.6 28.7 %collective-permute-start.15 = (bf16[128,1024]{1,0:T(8,128)(2,1)}, bf16[128,1024]{1,0:T(8,128)(2,1)S(1)}, u32[]{:S(2)}, u32[]{:S(2)}) collective-permute-start(bf16[128,1024]{1,0:T(8,128)(2,1)} %collective-permute-done.6.refs_6_), channel_id=1, source_target_pairs={{0,2},{1,3},{2,0},{3,1},{4,6},{5,7},{6,4},{7,5},{8,10},{9,11},{10,... | collective-permute-start | bytes 786440 | tf_op jit(solution)/shard_map/ppermute | solution.py:511
  45.0 27.2 %collective-permute-start.12 = (bf16[128,1024]{1,0:T(8,128)(2,1)}, bf16[128,1024]{1,0:T(8,128)(2,1)}, u32[]{:S(2)}, u32[]{:S(2)}) collective-permute-start(bf16[128,1024]{1,0:T(8,128)(2,1)} %collective-permute-done.7.refs_3_), channel_id=1, source_target_pairs={{0,2},{1,3},{2,0},{3,1},{4,6},{5,7},{6,4},{7,5},{8,10},{9,11},{10,... | collective-permute-start | bytes 786440 | tf_op jit(solution)/shard_map/ppermute | solution.py:511
  48.2 24.1 %collective-permute-start.13 = (bf16[128,1024]{1,0:T(8,128)(2,1)}, bf16[128,1024]{1,0:T(8,128)(2,1)}, u32[]{:S(2)}, u32[]{:S(2)}) collective-permute-start(bf16[128,1024]{1,0:T(8,128)(2,1)} %collective-permute-done.10.refs_4_), channel_id=1, source_target_pairs={{0,2},{1,3},{2,0},{3,1},{4,6},{5,7},{6,4},{7,5},{8,10},{9,11},{10,... | collective-permute-start | bytes 786440 | tf_op jit(solution)/shard_map/ppermute | solution.py:511
  48.7 23.5 %collective-permute-start.16 = (bf16[128,1024]{1,0:T(8,128)(2,1)}, bf16[128,1024]{1,0:T(8,128)(2,1)}, u32[]{:S(2)}, u32[]{:S(2)}) collective-permute-start(bf16[128,1024]{1,0:T(8,128)(2,1)} %collective-permute-done.8.refs_7_), channel_id=1, source_target_pairs={{0,2},{1,3},{2,0},{3,1},{4,6},{5,7},{6,4},{7,5},{8,10},{9,11},{10,... | collective-permute-start | bytes 786440 | tf_op jit(solution)/shard_map/ppermute | solution.py:511
  73.0 33.7 %collective-permute-start.17 = (bf16[512,512]{1,0:T(8,128)(2,1)}, bf16[512,512]{1,0:T(8,128)(2,1)S(1)}, u32[]{:S(2)}, u32[]{:S(2)}) collective-permute-start(bf16[512,512]{1,0:T(8,128)(2,1)} %get-tuple-element.191), channel_id=1, source_target_pairs={{0,2},{1,3},{2,0},{3,1},{4,6},{5,7},{6,4},{7,5},{8,10},{9,11},{10,... | collective-permute-start | bytes 1572872 | tf_op jit(solution)/shard_map/ppermute | solution.py:511
  73.6 33.2 %collective-permute-start.18 = (bf16[512,512]{1,0:T(8,128)(2,1)}, bf16[512,512]{1,0:T(8,128)(2,1)S(1)}, u32[]{:S(2)}, u32[]{:S(2)}) collective-permute-start(bf16[512,512]{1,0:T(8,128)(2,1)} %get-tuple-element.192), channel_id=1, source_target_pairs={{0,2},{1,3},{2,0},{3,1},{4,6},{5,7},{6,4},{7,5},{8,10},{9,11},{10,... | collective-permute-start | bytes 1572872 | tf_op jit(solution)/shard_map/ppermute | solution.py:511
  75.0 31.7 %collective-permute-start.19 = (bf16[512,512]{1,0:T(8,128)(2,1)}, bf16[512,512]{1,0:T(8,128)(2,1)S(1)}, u32[]{:S(2)}, u32[]{:S(2)}) collective-permute-start(bf16[512,512]{1,0:T(8,128)(2,1)} %get-tuple-element.193), channel_id=1, source_target_pairs={{0,2},{1,3},{2,0},{3,1},{4,6},{5,7},{6,4},{7,5},{8,10},{9,11},{10,... | collective-permute-start | bytes 1572872 | tf_op jit(solution)/shard_map/ppermute | solution.py:511
  109.7 14.7 %collective-permute-start.21 = (bf16[512,512]{1,0:T(8,128)(2,1)}, bf16[512,512]{1,0:T(8,128)(2,1)}, u32[]{:S(2)}, u32[]{:S(2)}) collective-permute-start(bf16[512,512]{1,0:T(8,128)(2,1)} %add_convert_fusion.1), channel_id=1, source_target_pairs={{0,4},{4,0},{8,12},{12,8},{16,20},{20,16},{24,28},{28,24},{1,5},{5... | collective-permute-start | bytes 1572872 | tf_op jit(solution)/shard_map/ppermute | solution.py:511
  110.1 14.4 %collective-permute-start.22 = (bf16[512,512]{1,0:T(8,128)(2,1)}, bf16[512,512]{1,0:T(8,128)(2,1)}, u32[]{:S(2)}, u32[]{:S(2)}) collective-permute-start(bf16[512,512]{1,0:T(8,128)(2,1)} %get-tuple-element.205), channel_id=1, source_target_pairs={{0,2},{1,3},{2,0},{3,1},{4,6},{5,7},{6,4},{7,5},{8,10},{9,11},{10,... | collective-permute-start | bytes 1572872 | tf_op jit(solution)/shard_map/ppermute | solution.py:511
  125.2 14.9 %collective-permute-start.30 = (bf16[512,512]{1,0:T(8,128)(2,1)S(1)}, bf16[512,512]{1,0:T(8,128)(2,1)S(1)}, u32[]{:S(2)}, u32[]{:S(2)}) collective-permute-start(bf16[512,512]{1,0:T(8,128)(2,1)S(1)} %add_convert_fusion), channel_id=1, source_target_pairs={{0,4},{4,0},{8,12},{12,8},{16,20},{20,16},{24,28},{28,24},{1,5},{5... | collective-permute-start | bytes 1572872 | tf_op jit(solution)/shard_map/ppermute | solution.py:511
  131.6 21.6 %collective-permute-start.25 = (f32[80,1024]{1,0:T(8,128)}, f32[80,1024]{1,0:T(8,128)S(1)}, u32[]{:S(2)}, u32[]{:S(2)}) collective-permute-start(f32[80,1024]{1,0:T(8,128)} %get-tuple-element.212), channel_id=1, source_target_pairs={{0,4},{4,0},{8,12},{12,8},{16,20},{20,16},{24,28},{28,24},{1,5},{5... | collective-permute-start | bytes 983048 | tf_op jit(solution)/shard_map/ppermute | solution.py:511
  133.1 20.0 %collective-permute-start.26 = (f32[80,1024]{1,0:T(8,128)}, f32[80,1024]{1,0:T(8,128)S(1)}, u32[]{:S(2)}, u32[]{:S(2)}) collective-permute-start(f32[80,1024]{1,0:T(8,128)} %get-tuple-element.213), channel_id=1, source_target_pairs={{0,2},{1,3},{2,0},{3,1},{4,6},{5,7},{6,4},{7,5},{8,10},{9,11},{10,... | collective-permute-start | bytes 983048 | tf_op jit(solution)/shard_map/ppermute | solution.py:576
  134.6 18.5 %collective-permute-start.27 = (f32[80,1024]{1,0:T(8,128)}, f32[80,1024]{1,0:T(8,128)}, u32[]{:S(2)}, u32[]{:S(2)}) collective-permute-start(f32[80,1024]{1,0:T(8,128)} %get-tuple-element.214), channel_id=1, source_target_pairs={{0,6},{1,7},{2,4},{3,5},{4,2},{5,3},{6,0},{7,1},{8,14},{9,15},{10,... | collective-permute-start | bytes 983048 | tf_op jit(solution)/shard_map/ppermute | solution.py:576
  137.5 12.4 %collective-permute-start.28 = (bf16[128,512]{1,0:T(8,128)(2,1)}, bf16[128,512]{1,0:T(8,128)(2,1)S(1)}, u32[]{:S(2)}, u32[]{:S(2)}) collective-permute-start(bf16[128,512]{1,0:T(8,128)(2,1)} %get-tuple-element.226), channel_id=1, source_target_pairs={{0,16},{4,20},{8,24},{12,28},{16,0},{20,4},{24,8},{28,12},{1,17},{... | collective-permute-start | bytes 393224 | tf_op jit(solution)/shard_map/ppermute | solution.py:511
  140.0 9.9 %collective-permute-start.29 = (bf16[128,512]{1,0:T(8,128)(2,1)}, bf16[128,512]{1,0:T(8,128)(2,1)S(1)}, u32[]{:S(2)}, u32[]{:S(2)}) collective-permute-start(bf16[128,512]{1,0:T(8,128)(2,1)} %get-tuple-element.227), channel_id=1, source_target_pairs={{0,24},{4,28},{8,16},{12,20},{16,8},{20,12},{24,0},{28,4},{1,25},{... | collective-permute-start | bytes 393224 | tf_op jit(solution)/shard_map/ppermute | solution.py:511
  153.9 7.8 %collective-permute-start.34 = (bf16[864,1024]{1,0:T(8,128)(2,1)S(1)}, bf16[864,1024]{1,0:T(8,128)(2,1)S(1)}, u32[]{:S(2)}, u32[]{:S(2)}) collective-permute-start(bf16[864,1024]{1,0:T(8,128)(2,1)S(1)} %copy-done.3), channel_id=1, source_target_pairs={{0,1},{1,0},{2,3},{3,2},{4,5},{5,4},{6,7},{7,6},{8,9},{9,8},{10,11... | collective-permute-start | bytes 5308424 | tf_op jit(solution)/shard_map/ppermute | solution.py:511
  153.9 14.5 %collective-permute-start.35 = (f32[128,512]{1,0:T(8,128)}, f32[128,512]{1,0:T(8,128)}, u32[]{:S(2)}, u32[]{:S(2)}) collective-permute-start(f32[128,512]{1,0:T(8,128)} %get-tuple-element.244), channel_id=1, source_target_pairs={{0,8},{4,12},{8,0},{12,4},{16,24},{20,28},{24,16},{28,20},{1,9},{5... | collective-permute-start | bytes 786440 | tf_op jit(solution)/shard_map/ppermute | solution.py:511
  157.3 12.1 %collective-permute-start.31 = (f32[80,256]{1,0:T(8,128)}, f32[80,256]{1,0:T(8,128)}, u32[]{:S(2)}, u32[]{:S(2)}) collective-permute-start(f32[80,256]{1,0:T(8,128)} %get-tuple-element.237), channel_id=1, source_target_pairs={{0,8},{4,12},{8,0},{12,4},{16,24},{20,28},{24,16},{28,20},{1,9},{5... | collective-permute-start | bytes 245768 | tf_op jit(solution)/shard_map/ppermute | solution.py:511
  158.0 11.5 %collective-permute-start.32 = (f32[80,256]{1,0:T(8,128)}, f32[80,256]{1,0:T(8,128)}, u32[]{:S(2)}, u32[]{:S(2)}) collective-permute-start(f32[80,256]{1,0:T(8,128)} %get-tuple-element.238), channel_id=1, source_target_pairs={{0,16},{4,20},{8,24},{12,28},{16,0},{20,4},{24,8},{28,12},{1,17},{... | collective-permute-start | bytes 245768 | tf_op jit(solution)/shard_map/ppermute | solution.py:511
  159.4 10.0 %collective-permute-start.33 = (f32[80,256]{1,0:T(8,128)}, f32[80,256]{1,0:T(8,128)}, u32[]{:S(2)}, u32[]{:S(2)}) collective-permute-start(f32[80,256]{1,0:T(8,128)} %get-tuple-element.239), channel_id=1, source_target_pairs={{0,24},{4,28},{8,16},{12,20},{16,8},{20,12},{24,0},{28,4},{1,25},{... | collective-permute-start | bytes 245768 | tf_op jit(solution)/shard_map/ppermute | solution.py:511
  161.7 15.6 %collective-permute-start.39 = (f32[128,512]{1,0:T(8,128)}, f32[128,512]{1,0:T(8,128)S(1)}, u32[]{:S(2)}, u32[]{:S(2)}) collective-permute-start(f32[128,512]{1,0:T(8,128)} %get-tuple-element.255), channel_id=1, source_target_pairs={{0,8},{4,12},{8,0},{12,4},{16,24},{20,28},{24,16},{28,20},{1,9},{5... | collective-permute-start | bytes 786440 | tf_op jit(solution)/shard_map/ppermute | solution.py:511
  171.7 8.4 %collective-permute-start.37 = (bf16[80,256]{1,0:T(8,128)(2,1)S(1)}, bf16[80,256]{1,0:T(8,128)(2,1)S(1)}, u32[]{:S(2)}, u32[]{:S(2)}) collective-permute-start(bf16[80,256]{1,0:T(8,128)(2,1)S(1)} %get-tuple-element.285), channel_id=1, source_target_pairs={{0,16},{4,20},{8,24},{12,28},{16,0},{20,4},{24,8},{28,12},{1,17},{... | collective-permute-start | bytes 122888 | tf_op jit(solution)/shard_map/ppermute | solution.py:511
  180.2 10.6 %collective-permute-start.41 = (bf16[80,1024]{1,0:T(8,128)(2,1)S(1)}, bf16[80,1024]{1,0:T(8,128)(2,1)S(1)}, u32[]{:S(2)}, u32[]{:S(2)}) collective-permute-start(bf16[80,1024]{1,0:T(8,128)(2,1)S(1)} %constant_dynamic-update-slice_fusion.4), channel_id=1, source_target_pairs={{0,4},{4,0},{8,12},{12,8},{16,20},{20,16},{24,28},{28,24},{1,5},{5... | collective-permute-start | bytes 491528 | tf_op jit(solution)/shard_map/ppermute | solution.py:511
  182.0 8.8 %collective-permute-start.42 = (bf16[80,1024]{1,0:T(8,128)(2,1)S(1)}, bf16[80,1024]{1,0:T(8,128)(2,1)S(1)}, u32[]{:S(2)}, u32[]{:S(2)}) collective-permute-start(bf16[80,1024]{1,0:T(8,128)(2,1)S(1)} %constant_dynamic-update-slice_fusion.4), channel_id=1, source_target_pairs={{0,2},{1,3},{2,0},{3,1},{4,6},{5,7},{6,4},{7,5},{8,10},{9,11},{10,... | collective-permute-start | bytes 491528 | tf_op jit(solution)/shard_map/ppermute | solution.py:576
  (40 other events, 258.8 us)

commit v19 on v18

--- a/solution.py
+++ b/solution.py
@@ -22,6 +22,7 @@
 F32 = jnp.float32
 BF16 = jnp.bfloat16
 VMEM_LIMIT = 60 * 1024 * 1024
+SMALL_LIMIT = 16 * 1024 * 1024
 
 
 def dot_nn(a, b):
@@ -45,8 +46,8 @@
     )
 
 
-def params():
-    return pltpu.CompilerParams(vmem_limit_bytes=VMEM_LIMIT)
+def params(limit=VMEM_LIMIT):
+    return pltpu.CompilerParams(vmem_limit_bytes=limit)
 
 
 def cost(flops, nbytes):
@@ -329,7 +330,7 @@
         in_specs=[SCALARS] + [whole(a) for a in ins],
         out_specs=[pl.BlockSpec((rows, cols), lambda: (0, 0))] * len(dtypes),
         out_shape=[jax.ShapeDtypeStruct((rows, cols), d) for d in dtypes],
-        compiler_params=params(),
+        compiler_params=params(SMALL_LIMIT),
         cost_estimate=cost(1e6, 5e6),
         name="combine",
     )(place, *ins)
@@ -356,7 +357,7 @@
         in_specs=[SCALARS] + [pl.BlockSpec((rows, cols), lambda: (0, 0))] * len(parts),
         out_specs=[pl.BlockSpec((rows, cols // blocks), lambda: (0, 0))] * blocks,
         out_shape=[jax.ShapeDtypeStruct((rows, cols // blocks), F32)] * blocks,
-        compiler_params=params(),
+        compiler_params=params(SMALL_LIMIT),
         cost_estimate=cost(1e6, 2e6),
         name="split_sum",
     )(place, *parts)
@@ -380,7 +381,7 @@
             jax.ShapeDtypeStruct((3, rows, cols // 2), F32),
             jax.ShapeDtypeStruct((cols // 2, rows), F32),
         ],
-        compiler_params=params(),
+        compiler_params=params(SMALL_LIMIT),
         cost_estimate=cost(1e6, 2e6),
         name="weight_results",
     )(*first, *second)
@@ -649,7 +650,7 @@
         jnp.asarray(genc),
         out_grad.reshape(scenes, TOK, D),
     )
-    stem, both_counts, far_shards = together(stem, jnp.stack([counts, counts_far]), far_shards)
+    stem, counts_far, far_shards = together(stem, counts_far, far_shards)
     rings = [Ring(x, "dp", dp) for x in far_shards]
     ring = rings[0]
     owners = ring.owners(dp // 2 + 1, dp // 2)
@@ -658,7 +659,7 @@
     cols = stem[2].reshape(tokens, stem[2].shape[2])
     both.append(swap(both[0], "group", group, 1))
     own_ahead, own_behind = [], []
-    both, owners = step_all(rings, both, owners)
+    both, owners, both_counts = step_all(rings, both, owners, jnp.stack([counts, counts_far]))
     while ring.steps < dp // 2:
         a, b = len(own_ahead), len(own_behind)
         own_ahead.append(cross(ring.ahead[-1], 1))

time: 196 us -> 197 us (level)
  waiting for transfers between devices: 41.7 us -> 48.6 us
  Pallas kernels: 93.5 us -> 87.2 us
  local copies, waits for them, and re-layouts: 8 us -> 5.76 us
    ppermute x35, waiting for transfers between devices: 20.1 us -> 27.6 us  [swap(): return lax.ppermute(x, axis, [(i, i ^ bit) for i in range(size)])]
    pallas_call x3, Pallas kernels: 8.02 us -> 4.25 us  [combine_call(): pl.pallas_call(functools.partial(combine_kernel, [len(part) for part in p...]
    unnamed x52 -> x44, local copies, waits for them, and re-layouts: 7.51 us -> 5.27 us
  transfers between devices with their start and end apart: 46 -> 46, of which waited for: 18 -> 17; matrix products, arithmetic and copies ran while one was open for 3% -> 3% of each run, Pallas kernels for 47% -> 44%
where the time goes in v19:
time: 197 us
  Pallas kernels  87.2 us (44%)
  waiting for transfers between devices  48.6 us (25%)
  starting transfers between devices  47.8 us (24%)
  other arithmetic  6.19 us (3%)
  local copies, waits for them, and re-layouts  5.76 us (3%)
    pallas_call x2, Pallas kernels, attention_call(): pl.pallas_call(functools.partial(attention_kernel, packs, len(blocks), dp...  53.2 us
    ppermute x35, starting transfers between devices, swap(): return lax.ppermute(x, axis, [(i, i ^ bit) for i in range(size)])  35.3 us
    ppermute x35, waiting for transfers between devices, swap(): return lax.ppermute(x, axis, [(i, i ^ bit) for i in range(size)])  27.6 us
    ppermute x4, waiting for transfers between devices, send(): moved = [lax.ppermute(self.ahead[-1], self.axis, self.forward)]  16.5 us
    pallas_call x1, Pallas kernels, tail_call(): pl.pallas_call(tail_kernel, grid=(tokens // rows,), in_specs=[SCALARS, pe...  8.71 us
    pallas_call x1, Pallas kernels, stem_call(): pl.pallas_call(stem_kernel, grid=(scenes // block,), in_specs=[pl.BlockSp...  8.28 us
    ppermute x4, starting transfers between devices, send(): moved = [lax.ppermute(self.ahead[-1], self.axis, self.forward)]  6.3 us
    pallas_call x1, Pallas kernels, output_call(): pl.pallas_call(functools.partial(output_kernel, len(packs)), grid=(tokens...  5.44 us
  transfers between devices with their start and end apart: 46, of which 17 were waited for; matrix products, arithmetic and copies ran while one was open for 3% of the time, Pallas kernels for 44%

profile of v19, /device:TPU:0, one launch (start us, length us, event | category | flops | bytes accessed | tf_op | source)
XLA Modules:
  0.0 196.6 jit_solution(2979178512688200182)
XLA Ops:
  0.6 1.7 pack_weights.1.refs_2_
  2.3 2.9 %collective-permute-start.1 = (bf16[128,1024]{1,0:T(8,128)(2,1)}, bf16[128,1024]{1,0:T(8,128)(2,1)}, u32[]{:S(2)}, u32[]{:S(2)}) collective-permute-start(bf16[128,1024]{1,0:T(8,128)(2,1)} %pack_weights.1.refs_2_), channel_id=1, source_target_pairs={{0,2},{1,3},{2,0},{3,1},{4,6},{5,7},{6,4},{7,5},{8,10},{9,11},{10,... | collective-permute-start | bytes 786440 | tf_op jit(solution)/shard_map/ppermute | solution.py:512
  5.3 8.3 %stem_norm.1 = (bf16[6,144,1024]{2,1,0:T(8,128)(2,1)}, bf16[2,6,144,1024]{3,2,1,0:T(8,128)(2,1)}, bf16[6,144,256]{2,1,0:T(8,128)(2,1)}) custom-call(s32[3,6]{1,0:T(4,128)} %bitcast.29, s32[6,3,48]{2,1,0:T(4,128)} %idx_ref.1, bf16[6,144,640]{2,1,0:T(8,128)(2,1)} %patch_ref.1, bf16[640,1024]{1,0:T(8,128)(2,1)} %w_ref.1, f32[1,1024]{1,0:T(1,128)} %bitcast.32, ...), custom_call_target="tpu_custom_call" | custom-call | flops 8000000 | bytes 12000 | tf_op jit(solution)/shard_map/stem_norm/pallas_call | solution.py:99
  14.2 1.6 collective-permute-start.2
  17.3 5.4 %collective-permute-done.2.refs_1_ = bf16[128,1024]{1,0:T(8,128)(2,1)S(1)} collective-permute-done((bf16[128,1024]{1,0:T(8,128)(2,1)}, bf16[128,1024]{1,0:T(8,128)(2,1)S(1)}, u32[]{:S(2)}, u32[]{:S(2)}) %collective-permute-start.2) | collective-permute-done | bytes 262176 | tf_op jit(solution)/shard_map/ppermute | solution.py:528
  24.0 1.6 collective-permute-start.5
  26.6 4.6 %collective-permute-done.5.refs_2_ = bf16[128,1024]{1,0:T(8,128)(2,1)S(1)} collective-permute-done((bf16[128,1024]{1,0:T(8,128)(2,1)S(1)}, bf16[128,1024]{1,0:T(8,128)(2,1)S(1)}, u32[]{:S(2)}, u32[]{:S(2)}) %collective-permute-start.5) | collective-permute-done | bytes 262176 | tf_op jit(solution)/shard_map/ppermute | solution.py:528
  32.6 1.6 collective-permute-start.7
  35.1 3.9 %collective-permute-done.7.refs_3_ = bf16[128,1024]{1,0:T(8,128)(2,1)} collective-permute-done((bf16[128,1024]{1,0:T(8,128)(2,1)S(1)}, bf16[128,1024]{1,0:T(8,128)(2,1)}, u32[]{:S(2)}, u32[]{:S(2)}) %collective-permute-start.7) | collective-permute-done | bytes 262176 | tf_op jit(solution)/shard_map/ppermute | solution.py:528
  39.1 1.8 collective-permute-done.8.refs_7_
  40.9 1.5 collective-permute-start.10
  44.9 2.6 %collective-permute-done.10.refs_4_ = bf16[128,1024]{1,0:T(8,128)(2,1)} collective-permute-done((bf16[128,1024]{1,0:T(8,128)(2,1)}, bf16[128,1024]{1,0:T(8,128)(2,1)}, u32[]{:S(2)}, u32[]{:S(2)}) %collective-permute-start.10) | collective-permute-done | bytes 262176 | tf_op jit(solution)/shard_map/ppermute | solution.py:528
  49.6 22.0 %attention.2 = (bf16[1728,1024]{1,0:T(8,128)(2,1)}, bf16[1024,1024]{1,0:T(8,128)(2,1)}, bf16[512,512]{1,0:T(8,128)(2,1)}, bf16[512,512]{1,0:T(8,128)(2,1)}, bf16...) custom-call(s32[2,3,6]{2,1,0:T(4,128)} %pad_add_fusion.cnt_ref, s32[8]{0:T(128)} %compare_select_fusion.2.owner_ref, ...), custom_call_target="tpu_custom_call" | custom-call | flops 20000000 | bytes 14000 | tf_op jit(solution)/shard_map/attention/pallas_call | solution.py:279
  74.3 31.1 %attention.3 = (bf16[1728,1024]{1,0:T(8,128)(2,1)}, bf16[1024,1024]{1,0:T(8,128)(2,1)}, f32[512,512]{1,0:T(8,128)}, f32[512,512]{1,0:T(8,128)}, f32[512,512]{1,0...) custom-call(s32[2,3,6]{2,1,0:T(4,128)} %pad_add_fusion.cnt_ref, ...), custom_call_target="tpu_custom_call" | custom-call | flops 20000000 | bytes 14000 | tf_op jit(solution)/shard_map/attention/pallas_call | solution.py:279
  109.6 8.7 %tail.1 = (f32[320,1024]{1,0:T(8,128)}, f32[320,512]{1,0:T(8,128)}, f32[320,512]{1,0:T(8,128)}) custom-call(s32[1]{0:T(128)} %bitcast.2.core_ref, f32[864,1024]{1,0:T(8,128)} %get-tuple-element.196.own_ref, bf16[864,1024]{1,0:T(8,128)(2,1)} %collective-permute-done.20.recv_ref, bf16[864,1024]{1,0:T(8,128)(2,1)} %bitcast.22, bf16[2,864,1024]{2,1,0:T(8,128)(2,1)} %bitcast.21, ...), custom_call_target="tpu_custom_call" | custom-call | flops 10000000 | bytes 12000 | tf_op jit(solution)/shard_map/tail/pallas_call | solution.py:467
  118.3 3.1 %collective-permute-done.21.refs_2_ = bf16[512,512]{1,0:T(8,128)(2,1)S(1)} collective-permute-done((bf16[512,512]{1,0:T(8,128)(2,1)S(1)}, bf16[512,512]{1,0:T(8,128)(2,1)S(1)}, u32[]{:S(2)}, u32[]{:S(2)}) %collective-permute-start.21) | collective-permute-done | bytes 524320 | tf_op jit(solution)/shard_map/ppermute | solution.py:512
  123.5 2.2 %add_convert_fusion = bf16[512,512]{1,0:T(8,128)(2,1)} fusion(f32[512,512]{1,0:T(8,128)} %get-tuple-element.232, bf16[512,512]{1,0:T(8,128)(2,1)S(1)} %copy-done.16), kind=kLoop, calls=%fused_computation.2 | loop fusion | flops 786432 | bytes 2097152 | tf_op jit(solution)/shard_map/convert_element_type | solution.py:698
  126.8 2.2 %combine.3 = (f32[80,1024]{1,0:T(8,128)S(1)}, f32[80,1024]{1,0:T(8,128)}, f32[80,1024]{1,0:T(8,128)}, f32[80,1024]{1,0:T(8,128)}) custom-call(s32[1]{0:T(128)} %bitcast.1.place_ref, f32[320,1024]{1,0:T(8,128)S(1)} %copy-done, f32[320,512]{1,0:T(8,128)S(1)} %collective-permute-done.23.refs_1_, f32[320,512]{1,0:T(8,128)} %collective-permute-done.24.refs_2_), custom_call_target="tpu_custom_call" | custom-call | flops 1000 | bytes 5000 | tf_op jit(solution)/shard_map/combine/pallas_call | solution.py:328
  130.6 1.5 collective-permute-start.26
  134.8 1.6 collective-permute-start.28
  136.4 11.4 %collective-permute-done.30.refs_2_ = bf16[512,512]{1,0:T(8,128)(2,1)} collective-permute-done((bf16[512,512]{1,0:T(8,128)(2,1)}, bf16[512,512]{1,0:T(8,128)(2,1)}, u32[]{:S(2)}, u32[]{:S(2)}) %collective-permute-start.30) | collective-permute-done | bytes 524320 | tf_op jit(solution)/shard_map/ppermute | solution.py:512
  149.3 3.7 %mixed.1 = bf16[864,1024]{1,0:T(8,128)(2,1)} custom-call(bf16[1728,1024]{1,0:T(8,128)(2,1)} %get-tuple-element.176.refs_0_, bf16[1728,1024]{1,0:T(8,128)(2,1)} %get-tuple-element.217.refs_1_, bf16[1024,1024]{1,0:T(8,128)(2,1)} %get-tuple-element.177.refs_1_.refs_2_, bf16[1024,1024]{1,0:T(8,128)(2,1)} %get-tuple-element.218.refs_3_), custom_call_target="tpu_custom_call" | custom-call | flops 2000000 | bytes 5000 | tf_op jit(solution)/shard_map/mixed/pallas_call | solution.py:413
  158.2 1.5 collective-permute-start.32
  159.7 1.8 collective-permute-start.33
  161.7 5.4 %layer_output.1 = bf16[864,1024]{1,0:T(8,128)(2,1)} custom-call(s32[3,6]{1,0:T(4,128)} %bitcast.30, bf16[864,1024]{1,0:T(8,128)(2,1)} %collective-permute-done.34.recv_ref, bf16[864,1024]{1,0:T(8,128)(2,1)} %bitcast.23, bf16[1728,1024]{1,0:T(8,128)(2,1)} %get-tuple-element.176.refs_0_, bf16[1728,1024]{1,0:T(8,128)(2,1)} %get-tuple-element.217.refs_1_, ...), custom_call_target="tpu_custom_call" | custom-call | flops 5000000 | bytes 10000 | tf_op jit(solution)/shard_map/layer_output/pallas_call | solution.py:498
  167.2 2.5 %collective-permute-start.40 = (bf16[128,512]{1,0:T(8,128)(2,1)S(1)}, bf16[128,512]{1,0:T(8,128)(2,1)S(1)}, u32[]{:S(2)}, u32[]{:S(2)}) collective-permute-start(bf16[128,512]{1,0:T(8,128)(2,1)S(1)} %copy-done.12), channel_id=1, source_target_pairs={{0,16},{4,20},{8,24},{12,28},{16,0},{20,4},{24,8},{28,12},{1,17},{... | collective-permute-start | bytes 393224 | tf_op jit(solution)/shard_map/ppermute | solution.py:512
  170.6 2.4 %collective-permute-start.37 = (bf16[80,256]{1,0:T(8,128)(2,1)S(1)}, bf16[80,256]{1,0:T(8,128)(2,1)S(1)}, u32[]{:S(2)}, u32[]{:S(2)}) collective-permute-start(bf16[80,256]{1,0:T(8,128)(2,1)S(1)} %get-tuple-element.287), channel_id=1, source_target_pairs={{0,16},{4,20},{8,24},{12,28},{16,0},{20,4},{24,8},{28,12},{1,17},{... | collective-permute-start | bytes 122888 | tf_op jit(solution)/shard_map/ppermute | solution.py:512
  172.9 2.0 %collective-permute-start.38 = (bf16[80,256]{1,0:T(8,128)(2,1)S(1)}, bf16[80,256]{1,0:T(8,128)(2,1)S(1)}, u32[]{:S(2)}, u32[]{:S(2)}) collective-permute-start(bf16[80,256]{1,0:T(8,128)(2,1)S(1)} %get-tuple-element.287), channel_id=1, source_target_pairs={{0,24},{4,28},{8,16},{12,20},{16,8},{20,12},{24,0},{28,4},{1,25},{... | collective-permute-start | bytes 122888 | tf_op jit(solution)/shard_map/ppermute | solution.py:512
  176.4 2.3 %collective-permute-done.39.refs_5_ = f32[128,512]{1,0:T(8,128)S(1)} collective-permute-done((f32[128,512]{1,0:T(8,128)S(1)}, f32[128,512]{1,0:T(8,128)S(1)}, u32[]{:S(2)}, u32[]{:S(2)}) %collective-permute-start.39) | collective-permute-done | bytes 262176 | tf_op jit(solution)/shard_map/ppermute | solution.py:512
  179.2 1.9 collective-permute-done.38
  184.6 1.8 collective-permute-start.44
  186.6 5.0 %collective-permute-done.44.refs_7_ = bf16[128,512]{1,0:T(8,128)(2,1)S(1)} collective-permute-done((bf16[128,512]{1,0:T(8,128)(2,1)S(1)}, bf16[128,512]{1,0:T(8,128)(2,1)S(1)}, u32[]{:S(2)}, u32[]{:S(2)}) %collective-permute-start.44) | collective-permute-done | bytes 131104 | tf_op jit(solution)/shard_map/ppermute | solution.py:512
  (133 shorter events, 44.0 us)
Async XLA Ops:
  2.3 11.2 %collective-permute-start.1 = (bf16[128,1024]{1,0:T(8,128)(2,1)}, bf16[128,1024]{1,0:T(8,128)(2,1)}, u32[]{:S(2)}, u32[]{:S(2)}) collective-permute-start(bf16[128,1024]{1,0:T(8,128)(2,1)} %pack_weights.1.refs_2_), channel_id=1, source_target_pairs={{0,2},{1,3},{2,0},{3,1},{4,6},{5,7},{6,4},{7,5},{8,10},{9,11},{10,... | collective-permute-start | bytes 786440 | tf_op jit(solution)/shard_map/ppermute | solution.py:512
  5.3 8.3 %collective-permute-start = (s32[3,6]{1,0:T(4,128)}, s32[3,6]{1,0:T(4,128)S(1)}, u32[]{:S(2)}, u32[]{:S(2)}) collective-permute-start(s32[3,6]{1,0:T(4,128)} %bitcast.28), channel_id=1, source_target_pairs={{0,1},{1,0},{2,3},{3,2},{4,5},{5,4},{6,7},{7,6},{8,9},{9,8},{10,11... | collective-permute-start | bytes 224 | tf_op jit(solution)/shard_map/ppermute | solution.py:512
  13.6 10.4 %collective-permute-start.4 = (bf16[2,864,1024]{2,1,0:T(8,128)(2,1)}, bf16[2,864,1024]{2,1,0:T(8,128)(2,1)S(1)}, u32[]{:S(2)}, u32[]{:S(2)}) collective-permute-start(bf16[2,864,1024]{2,1,0:T(8,128)(2,1)} %bitcast.16), channel_id=1, source_target_pairs={{0,1},{1,0},{2,3},{3,2},{4,5},{5,4},{6,7},{7,6},{8,9},{9,8},{10,11... | collective-permute-start | bytes 10616840 | tf_op jit(solution)/shard_map/ppermute | solution.py:512
  14.2 8.5 %collective-permute-start.2 = (bf16[128,1024]{1,0:T(8,128)(2,1)}, bf16[128,1024]{1,0:T(8,128)(2,1)S(1)}, u32[]{:S(2)}, u32[]{:S(2)}) collective-permute-start(bf16[128,1024]{1,0:T(8,128)(2,1)} %collective-permute-done.1.refs_0_), channel_id=1, source_target_pairs={{0,8},{8,16},{16,24},{24,28},{28,20},{20,12},{12,4},{4,0},{1,9},{9... | collective-permute-start | bytes 786440 | tf_op jit(solution)/shard_map/ppermute | solution.py:528
  15.7 8.2 %collective-permute-start.3 = (bf16[128,1024]{1,0:T(8,128)(2,1)}, bf16[128,1024]{1,0:T(8,128)(2,1)S(1)}, u32[]{:S(2)}, u32[]{:S(2)}) collective-permute-start(bf16[128,1024]{1,0:T(8,128)(2,1)} %collective-permute-done.1.refs_0_), channel_id=1, source_target_pairs={{8,0},{16,8},{24,16},{28,24},{20,28},{12,20},{4,12},{0,4},{9,1},{1... | collective-permute-start | bytes 786440 | tf_op jit(solution)/shard_map/ppermute | solution.py:530
  26.1 9.1 %collective-permute-start.9 = (bf16[128,1024]{1,0:T(8,128)(2,1)S(1)}, bf16[128,1024]{1,0:T(8,128)(2,1)}, u32[]{:S(2)}, u32[]{:S(2)}) collective-permute-start(bf16[128,1024]{1,0:T(8,128)(2,1)S(1)} %collective-permute-done.2.refs_1_), channel_id=1, source_target_pairs={{0,2},{1,3},{2,0},{3,1},{4,6},{5,7},{6,4},{7,5},{8,10},{9,11},{10,... | collective-permute-start | bytes 786440 | tf_op jit(solution)/shard_map/ppermute | solution.py:512
  34.6 10.3 %collective-permute-start.11 = (bf16[128,1024]{1,0:T(8,128)(2,1)S(1)}, bf16[128,1024]{1,0:T(8,128)(2,1)}, u32[]{:S(2)}, u32[]{:S(2)}) collective-permute-start(bf16[128,1024]{1,0:T(8,128)(2,1)S(1)} %collective-permute-done.5.refs_2_), channel_id=1, source_target_pairs={{0,2},{1,3},{2,0},{3,1},{4,6},{5,7},{6,4},{7,5},{8,10},{9,11},{10,... | collective-permute-start | bytes 786440 | tf_op jit(solution)/shard_map/ppermute | solution.py:512
  42.4 29.2 %collective-permute-start.14 = (bf16[128,1024]{1,0:T(8,128)(2,1)S(1)}, bf16[128,1024]{1,0:T(8,128)(2,1)}, u32[]{:S(2)}, u32[]{:S(2)}) collective-permute-start(bf16[128,1024]{1,0:T(8,128)(2,1)S(1)} %collective-permute-done.3.refs_5_), channel_id=1, source_target_pairs={{0,2},{1,3},{2,0},{3,1},{4,6},{5,7},{6,4},{7,5},{8,10},{9,11},{10,... | collective-permute-start | bytes 786440 | tf_op jit(solution)/shard_map/ppermute | solution.py:512
  42.9 28.7 %collective-permute-start.15 = (bf16[128,1024]{1,0:T(8,128)(2,1)}, bf16[128,1024]{1,0:T(8,128)(2,1)}, u32[]{:S(2)}, u32[]{:S(2)}) collective-permute-start(bf16[128,1024]{1,0:T(8,128)(2,1)} %collective-permute-done.6.refs_6_), channel_id=1, source_target_pairs={{0,2},{1,3},{2,0},{3,1},{4,6},{5,7},{6,4},{7,5},{8,10},{9,11},{10,... | collective-permute-start | bytes 786440 | tf_op jit(solution)/shard_map/ppermute | solution.py:512
  44.4 27.2 %collective-permute-start.12 = (bf16[128,1024]{1,0:T(8,128)(2,1)}, bf16[128,1024]{1,0:T(8,128)(2,1)}, u32[]{:S(2)}, u32[]{:S(2)}) collective-permute-start(bf16[128,1024]{1,0:T(8,128)(2,1)} %collective-permute-done.7.refs_3_), channel_id=1, source_target_pairs={{0,2},{1,3},{2,0},{3,1},{4,6},{5,7},{6,4},{7,5},{8,10},{9,11},{10,... | collective-permute-start | bytes 786440 | tf_op jit(solution)/shard_map/ppermute | solution.py:512
  47.5 24.1 %collective-permute-start.13 = (bf16[128,1024]{1,0:T(8,128)(2,1)}, bf16[128,1024]{1,0:T(8,128)(2,1)}, u32[]{:S(2)}, u32[]{:S(2)}) collective-permute-start(bf16[128,1024]{1,0:T(8,128)(2,1)} %collective-permute-done.10.refs_4_), channel_id=1, source_target_pairs={{0,2},{1,3},{2,0},{3,1},{4,6},{5,7},{6,4},{7,5},{8,10},{9,11},{10,... | collective-permute-start | bytes 786440 | tf_op jit(solution)/shard_map/ppermute | solution.py:512
  48.1 23.6 %collective-permute-start.16 = (bf16[128,1024]{1,0:T(8,128)(2,1)}, bf16[128,1024]{1,0:T(8,128)(2,1)}, u32[]{:S(2)}, u32[]{:S(2)}) collective-permute-start(bf16[128,1024]{1,0:T(8,128)(2,1)} %collective-permute-done.8.refs_7_), channel_id=1, source_target_pairs={{0,2},{1,3},{2,0},{3,1},{4,6},{5,7},{6,4},{7,5},{8,10},{9,11},{10,... | collective-permute-start | bytes 786440 | tf_op jit(solution)/shard_map/ppermute | solution.py:512
  71.7 33.8 %collective-permute-start.17 = (bf16[512,512]{1,0:T(8,128)(2,1)}, bf16[512,512]{1,0:T(8,128)(2,1)S(1)}, u32[]{:S(2)}, u32[]{:S(2)}) collective-permute-start(bf16[512,512]{1,0:T(8,128)(2,1)} %get-tuple-element.193), channel_id=1, source_target_pairs={{0,2},{1,3},{2,0},{3,1},{4,6},{5,7},{6,4},{7,5},{8,10},{9,11},{10,... | collective-permute-start | bytes 1572872 | tf_op jit(solution)/shard_map/ppermute | solution.py:512
  72.3 33.2 %collective-permute-start.18 = (bf16[512,512]{1,0:T(8,128)(2,1)}, bf16[512,512]{1,0:T(8,128)(2,1)S(1)}, u32[]{:S(2)}, u32[]{:S(2)}) collective-permute-start(bf16[512,512]{1,0:T(8,128)(2,1)} %get-tuple-element.194), channel_id=1, source_target_pairs={{0,2},{1,3},{2,0},{3,1},{4,6},{5,7},{6,4},{7,5},{8,10},{9,11},{10,... | collective-permute-start | bytes 1572872 | tf_op jit(solution)/shard_map/ppermute | solution.py:512
  73.8 31.7 %collective-permute-start.19 = (bf16[512,512]{1,0:T(8,128)(2,1)}, bf16[512,512]{1,0:T(8,128)(2,1)S(1)}, u32[]{:S(2)}, u32[]{:S(2)}) collective-permute-start(bf16[512,512]{1,0:T(8,128)(2,1)} %get-tuple-element.195), channel_id=1, source_target_pairs={{0,2},{1,3},{2,0},{3,1},{4,6},{5,7},{6,4},{7,5},{8,10},{9,11},{10,... | collective-permute-start | bytes 1572872 | tf_op jit(solution)/shard_map/ppermute | solution.py:512
  107.0 14.3 %collective-permute-start.21 = (bf16[512,512]{1,0:T(8,128)(2,1)S(1)}, bf16[512,512]{1,0:T(8,128)(2,1)S(1)}, u32[]{:S(2)}, u32[]{:S(2)}) collective-permute-start(bf16[512,512]{1,0:T(8,128)(2,1)S(1)} %add_convert_fusion.1), channel_id=1, source_target_pairs={{0,4},{4,0},{8,12},{12,8},{16,20},{20,16},{24,28},{28,24},{1,5},{5... | collective-permute-start | bytes 1572872 | tf_op jit(solution)/shard_map/ppermute | solution.py:512
  107.6 14.5 %collective-permute-start.22 = (bf16[512,512]{1,0:T(8,128)(2,1)}, bf16[512,512]{1,0:T(8,128)(2,1)S(1)}, u32[]{:S(2)}, u32[]{:S(2)}) collective-permute-start(bf16[512,512]{1,0:T(8,128)(2,1)} %get-tuple-element.207), channel_id=1, source_target_pairs={{0,2},{1,3},{2,0},{3,1},{4,6},{5,7},{6,4},{7,5},{8,10},{9,11},{10,... | collective-permute-start | bytes 1572872 | tf_op jit(solution)/shard_map/ppermute | solution.py:512
  125.7 22.1 %collective-permute-start.30 = (bf16[512,512]{1,0:T(8,128)(2,1)}, bf16[512,512]{1,0:T(8,128)(2,1)}, u32[]{:S(2)}, u32[]{:S(2)}) collective-permute-start(bf16[512,512]{1,0:T(8,128)(2,1)} %add_convert_fusion), channel_id=1, source_target_pairs={{0,4},{4,0},{8,12},{12,8},{16,20},{20,16},{24,28},{28,24},{1,5},{5... | collective-permute-start | bytes 1572872 | tf_op jit(solution)/shard_map/ppermute | solution.py:512
  129.7 25.2 %collective-permute-start.25 = (f32[80,1024]{1,0:T(8,128)}, f32[80,1024]{1,0:T(8,128)S(1)}, u32[]{:S(2)}, u32[]{:S(2)}) collective-permute-start(f32[80,1024]{1,0:T(8,128)} %get-tuple-element.214), channel_id=1, source_target_pairs={{0,4},{4,0},{8,12},{12,8},{16,20},{20,16},{24,28},{28,24},{1,5},{5... | collective-permute-start | bytes 983048 | tf_op jit(solution)/shard_map/ppermute | solution.py:512
  130.6 24.3 %collective-permute-start.26 = (f32[80,1024]{1,0:T(8,128)}, f32[80,1024]{1,0:T(8,128)S(1)}, u32[]{:S(2)}, u32[]{:S(2)}) collective-permute-start(f32[80,1024]{1,0:T(8,128)} %get-tuple-element.215), channel_id=1, source_target_pairs={{0,2},{1,3},{2,0},{3,1},{4,6},{5,7},{6,4},{7,5},{8,10},{9,11},{10,... | collective-permute-start | bytes 983048 | tf_op jit(solution)/shard_map/ppermute | solution.py:577
  132.1 22.8 %collective-permute-start.27 = (f32[80,1024]{1,0:T(8,128)}, f32[80,1024]{1,0:T(8,128)}, u32[]{:S(2)}, u32[]{:S(2)}) collective-permute-start(f32[80,1024]{1,0:T(8,128)} %get-tuple-element.216), channel_id=1, source_target_pairs={{0,6},{1,7},{2,4},{3,5},{4,2},{5,3},{6,0},{7,1},{8,14},{9,15},{10,... | collective-permute-start | bytes 983048 | tf_op jit(solution)/shard_map/ppermute | solution.py:577
  134.8 20.1 %collective-permute-start.28 = (bf16[128,512]{1,0:T(8,128)(2,1)}, bf16[128,512]{1,0:T(8,128)(2,1)S(1)}, u32[]{:S(2)}, u32[]{:S(2)}) collective-permute-start(bf16[128,512]{1,0:T(8,128)(2,1)} %get-tuple-element.228), channel_id=1, source_target_pairs={{0,16},{4,20},{8,24},{12,28},{16,0},{20,4},{24,8},{28,12},{1,17},{... | collective-permute-start | bytes 393224 | tf_op jit(solution)/shard_map/ppermute | solution.py:512
  155.0 12.2 %collective-permute-start.35 = (f32[128,512]{1,0:T(8,128)S(1)}, f32[128,512]{1,0:T(8,128)S(1)}, u32[]{:S(2)}, u32[]{:S(2)}) collective-permute-start(f32[128,512]{1,0:T(8,128)S(1)} %copy-done.10), channel_id=1, source_target_pairs={{0,8},{4,12},{8,0},{12,4},{16,24},{20,28},{24,16},{28,20},{1,9},{5... | collective-permute-start | bytes 786440 | tf_op jit(solution)/shard_map/ppermute | solution.py:512
  157.1 12.6 %collective-permute-start.31 = (f32[80,256]{1,0:T(8,128)S(1)}, f32[80,256]{1,0:T(8,128)S(1)}, u32[]{:S(2)}, u32[]{:S(2)}) collective-permute-start(f32[80,256]{1,0:T(8,128)S(1)} %get-tuple-element.239), channel_id=1, source_target_pairs={{0,8},{4,12},{8,0},{12,4},{16,24},{20,28},{24,16},{28,20},{1,9},{5... | collective-permute-start | bytes 245768 | tf_op jit(solution)/shard_map/ppermute | solution.py:512
  158.2 11.5 %collective-permute-start.32 = (f32[80,256]{1,0:T(8,128)S(1)}, f32[80,256]{1,0:T(8,128)S(1)}, u32[]{:S(2)}, u32[]{:S(2)}) collective-permute-start(f32[80,256]{1,0:T(8,128)S(1)} %get-tuple-element.240), channel_id=1, source_target_pairs={{0,16},{4,20},{8,24},{12,28},{16,0},{20,4},{24,8},{28,12},{1,17},{... | collective-permute-start | bytes 245768 | tf_op jit(solution)/shard_map/ppermute | solution.py:512
  159.7 10.7 %collective-permute-start.33 = (f32[80,256]{1,0:T(8,128)S(1)}, f32[80,256]{1,0:T(8,128)S(1)}, u32[]{:S(2)}, u32[]{:S(2)}) collective-permute-start(f32[80,256]{1,0:T(8,128)S(1)} %get-tuple-element.241), channel_id=1, source_target_pairs={{0,24},{4,28},{8,16},{12,20},{16,8},{20,12},{24,0},{28,4},{1,25},{... | collective-permute-start | bytes 245768 | tf_op jit(solution)/shard_map/ppermute | solution.py:512
  161.6 17.2 %collective-permute-start.39 = (f32[128,512]{1,0:T(8,128)S(1)}, f32[128,512]{1,0:T(8,128)S(1)}, u32[]{:S(2)}, u32[]{:S(2)}) collective-permute-start(f32[128,512]{1,0:T(8,128)S(1)} %get-tuple-element.257), channel_id=1, source_target_pairs={{0,8},{4,12},{8,0},{12,4},{16,24},{20,28},{24,16},{28,20},{1,9},{5... | collective-permute-start | bytes 786440 | tf_op jit(solution)/shard_map/ppermute | solution.py:512
  167.2 9.2 %collective-permute-start.40 = (bf16[128,512]{1,0:T(8,128)(2,1)S(1)}, bf16[128,512]{1,0:T(8,128)(2,1)S(1)}, u32[]{:S(2)}, u32[]{:S(2)}) collective-permute-start(bf16[128,512]{1,0:T(8,128)(2,1)S(1)} %copy-done.12), channel_id=1, source_target_pairs={{0,16},{4,20},{8,24},{12,28},{16,0},{20,4},{24,8},{28,12},{1,17},{... | collective-permute-start | bytes 393224 | tf_op jit(solution)/shard_map/ppermute | solution.py:512
  170.5 8.7 %collective-permute-start.36 = (bf16[80,256]{1,0:T(8,128)(2,1)S(1)}, bf16[80,256]{1,0:T(8,128)(2,1)S(1)}, u32[]{:S(2)}, u32[]{:S(2)}) collective-permute-start(bf16[80,256]{1,0:T(8,128)(2,1)S(1)} %get-tuple-element.287), channel_id=1, source_target_pairs={{0,8},{4,12},{8,0},{12,4},{16,24},{20,28},{24,16},{28,20},{1,9},{5... | collective-permute-start | bytes 122888 | tf_op jit(solution)/shard_map/ppermute | solution.py:512
  170.6 8.6 %collective-permute-start.37 = (bf16[80,256]{1,0:T(8,128)(2,1)S(1)}, bf16[80,256]{1,0:T(8,128)(2,1)S(1)}, u32[]{:S(2)}, u32[]{:S(2)}) collective-permute-start(bf16[80,256]{1,0:T(8,128)(2,1)S(1)} %get-tuple-element.287), channel_id=1, source_target_pairs={{0,16},{4,20},{8,24},{12,28},{16,0},{20,4},{24,8},{28,12},{1,17},{... | collective-permute-start | bytes 122888 | tf_op jit(solution)/shard_map/ppermute | solution.py:512
  181.1 10.4 %collective-permute-start.41 = (bf16[80,1024]{1,0:T(8,128)(2,1)S(1)}, bf16[80,1024]{1,0:T(8,128)(2,1)S(1)}, u32[]{:S(2)}, u32[]{:S(2)}) collective-permute-start(bf16[80,1024]{1,0:T(8,128)(2,1)S(1)} %constant_dynamic-update-slice_fusion.4), channel_id=1, source_target_pairs={{0,4},{4,0},{8,12},{12,8},{16,20},{20,16},{24,28},{28,24},{1,5},{5... | collective-permute-start | bytes 491528 | tf_op jit(solution)/shard_map/ppermute | solution.py:512
  182.3 9.2 %collective-permute-start.42 = (bf16[80,1024]{1,0:T(8,128)(2,1)S(1)}, bf16[80,1024]{1,0:T(8,128)(2,1)S(1)}, u32[]{:S(2)}, u32[]{:S(2)}) collective-permute-start(bf16[80,1024]{1,0:T(8,128)(2,1)S(1)} %constant_dynamic-update-slice_fusion.4), channel_id=1, source_target_pairs={{0,2},{1,3},{2,0},{3,1},{4,6},{5,7},{6,4},{7,5},{8,10},{9,11},{10,... | collective-permute-start | bytes 491528 | tf_op jit(solution)/shard_map/ppermute | solution.py:577
  (36 other events, 261.8 us)

commit v20 on v19

--- a/solution.py
+++ b/solution.py
@@ -714,12 +714,13 @@
     _, coming[0], keeps = together(stem_parts, coming[0], keeps)
     first = second_leg(0)
     first_rest = spread(first, rests[1:])
+    mixed, coming[1], first_rest[0] = together(mixed_call(packs, weights), coming[1], first_rest[0])
     second = second_leg(1)
     near = dp // 2 * 3 // 4
-    beside = [mixed_call(packs, weights), first[0], *first_rest, second[0]]
+    beside = [mixed, first[0], first_rest[0], second[0]]
     def after_first(mixed, *arrived):
         output = output_call(counts, swap(mixed, "group", group, 1), emb, packs, weights)
-        return [output, *arrived[:-1], *spread(first, [1]), arrived[-1]]
+        return [output, *arrived[:-1], *first_rest[1:], *spread(first, [1]), arrived[-1]]
 
     def after_second(*arrived):
         return [*arrived, *spread(second, [1, *range(2, near)]), second[near:]]

time: 197 us -> 199 us (1.010)
    unnamed x44 -> x46, local copies, waits for them, and re-layouts: 5.27 us -> 6.58 us
  transfers between devices with their start and end apart: 46 -> 46, of which waited for: 17 -> 17; matrix products, arithmetic and copies ran while one was open for 3% -> 3% of each run, Pallas kernels for 44% -> 43%
where the time goes in v20:
time: 199 us; the launch traced here: 198 us
  Pallas kernels  87.2 us (44%)
  starting transfers between devices  49.1 us (25%)
  waiting for transfers between devices  47.7 us (24%)
  local copies, waits for them, and re-layouts  7.06 us (4%)
  other arithmetic  6.27 us (3%)
    pallas_call x2, Pallas kernels, attention_call(): pl.pallas_call(functools.partial(attention_kernel, packs, len(blocks), dp...  53.1 us
    ppermute x35, starting transfers between devices, swap(): return lax.ppermute(x, axis, [(i, i ^ bit) for i in range(size)])  36.5 us
    ppermute x35, waiting for transfers between devices, swap(): return lax.ppermute(x, axis, [(i, i ^ bit) for i in range(size)])  26.8 us
    ppermute x4, waiting for transfers between devices, send(): moved = [lax.ppermute(self.ahead[-1], self.axis, self.forward)]  16.4 us
    pallas_call x1, Pallas kernels, tail_call(): pl.pallas_call(tail_kernel, grid=(tokens // rows,), in_specs=[SCALARS, pe...  8.72 us
    pallas_call x1, Pallas kernels, stem_call(): pl.pallas_call(stem_kernel, grid=(scenes // block,), in_specs=[pl.BlockSp...  8.29 us
    unnamed x46, local copies, waits for them, and re-layouts  6.58 us
    ppermute x4, starting transfers between devices, send(): moved = [lax.ppermute(self.ahead[-1], self.axis, self.forward)]  6.3 us
  transfers between devices with their start and end apart: 46, of which 17 were waited for; matrix products, arithmetic and copies ran while one was open for 3% of the time, Pallas kernels for 43%

profile of v20, /device:TPU:0, one launch (start us, length us, event | category | flops | bytes accessed | tf_op | source)
XLA Modules:
  0.0 198.3 jit_solution(4697466904139071725)
XLA Ops:
  0.6 1.7 pack_weights.1.refs_2_
  2.3 2.9 %collective-permute-start.1 = (bf16[128,1024]{1,0:T(8,128)(2,1)}, bf16[128,1024]{1,0:T(8,128)(2,1)}, u32[]{:S(2)}, u32[]{:S(2)}) collective-permute-start(bf16[128,1024]{1,0:T(8,128)(2,1)} %pack_weights.1.refs_2_), channel_id=1, source_target_pairs={{0,2},{1,3},{2,0},{3,1},{4,6},{5,7},{6,4},{7,5},{8,10},{9,11},{10,... | collective-permute-start | bytes 786440 | tf_op jit(solution)/shard_map/ppermute | solution.py:512
  5.3 8.3 %stem_norm.1 = (bf16[6,144,1024]{2,1,0:T(8,128)(2,1)}, bf16[2,6,144,1024]{3,2,1,0:T(8,128)(2,1)}, bf16[6,144,256]{2,1,0:T(8,128)(2,1)}) custom-call(s32[3,6]{1,0:T(4,128)} %bitcast.29, s32[6,3,48]{2,1,0:T(4,128)} %idx_ref.1, bf16[6,144,640]{2,1,0:T(8,128)(2,1)} %patch_ref.1, bf16[640,1024]{1,0:T(8,128)(2,1)} %w_ref.1, f32[1,1024]{1,0:T(1,128)} %bitcast.32, ...), custom_call_target="tpu_custom_call" | custom-call | flops 8000000 | bytes 12000 | tf_op jit(solution)/shard_map/stem_norm/pallas_call | solution.py:99
  14.2 1.6 collective-permute-start.2
  17.4 5.3 %collective-permute-done.2.refs_1_ = bf16[128,1024]{1,0:T(8,128)(2,1)S(1)} collective-permute-done((bf16[128,1024]{1,0:T(8,128)(2,1)}, bf16[128,1024]{1,0:T(8,128)(2,1)S(1)}, u32[]{:S(2)}, u32[]{:S(2)}) %collective-permute-start.2) | collective-permute-done | bytes 262176 | tf_op jit(solution)/shard_map/ppermute | solution.py:528
  24.0 1.6 collective-permute-start.5
  26.6 4.6 %collective-permute-done.5.refs_2_ = bf16[128,1024]{1,0:T(8,128)(2,1)S(1)} collective-permute-done((bf16[128,1024]{1,0:T(8,128)(2,1)S(1)}, bf16[128,1024]{1,0:T(8,128)(2,1)S(1)}, u32[]{:S(2)}, u32[]{:S(2)}) %collective-permute-start.5) | collective-permute-done | bytes 262176 | tf_op jit(solution)/shard_map/ppermute | solution.py:528
  32.6 1.6 collective-permute-start.7
  35.2 3.9 %collective-permute-done.7.refs_3_ = bf16[128,1024]{1,0:T(8,128)(2,1)} collective-permute-done((bf16[128,1024]{1,0:T(8,128)(2,1)S(1)}, bf16[128,1024]{1,0:T(8,128)(2,1)}, u32[]{:S(2)}, u32[]{:S(2)}) %collective-permute-start.7) | collective-permute-done | bytes 262176 | tf_op jit(solution)/shard_map/ppermute | solution.py:528
  39.1 1.8 collective-permute-done.8.refs_7_
  44.9 2.6 %collective-permute-done.10.refs_4_ = bf16[128,1024]{1,0:T(8,128)(2,1)} collective-permute-done((bf16[128,1024]{1,0:T(8,128)(2,1)}, bf16[128,1024]{1,0:T(8,128)(2,1)}, u32[]{:S(2)}, u32[]{:S(2)}) %collective-permute-start.10) | collective-permute-done | bytes 262176 | tf_op jit(solution)/shard_map/ppermute | solution.py:528
  49.6 22.0 %attention.2 = (bf16[1728,1024]{1,0:T(8,128)(2,1)}, bf16[1024,1024]{1,0:T(8,128)(2,1)}, bf16[512,512]{1,0:T(8,128)(2,1)}, bf16[512,512]{1,0:T(8,128)(2,1)}, bf16...) custom-call(s32[2,3,6]{2,1,0:T(4,128)} %pad_add_fusion.cnt_ref, s32[8]{0:T(128)} %compare_select_fusion.2.owner_ref, ...), custom_call_target="tpu_custom_call" | custom-call | flops 20000000 | bytes 14000 | tf_op jit(solution)/shard_map/attention/pallas_call | solution.py:279
  74.3 31.1 %attention.3 = (bf16[1728,1024]{1,0:T(8,128)(2,1)}, bf16[1024,1024]{1,0:T(8,128)(2,1)}, f32[512,512]{1,0:T(8,128)}, f32[512,512]{1,0:T(8,128)}, f32[512,512]{1,0...) custom-call(s32[2,3,6]{2,1,0:T(4,128)} %pad_add_fusion.cnt_ref, ...), custom_call_target="tpu_custom_call" | custom-call | flops 20000000 | bytes 14000 | tf_op jit(solution)/shard_map/attention/pallas_call | solution.py:279
  109.6 8.7 %tail.1 = (f32[320,1024]{1,0:T(8,128)}, f32[320,512]{1,0:T(8,128)}, f32[320,512]{1,0:T(8,128)}) custom-call(s32[1]{0:T(128)} %bitcast.2.core_ref, f32[864,1024]{1,0:T(8,128)} %get-tuple-element.198.own_ref, bf16[864,1024]{1,0:T(8,128)(2,1)} %collective-permute-done.20.recv_ref, bf16[864,1024]{1,0:T(8,128)(2,1)} %bitcast.22, bf16[2,864,1024]{2,1,0:T(8,128)(2,1)} %bitcast.21, ...), custom_call_target="tpu_custom_call" | custom-call | flops 10000000 | bytes 12000 | tf_op jit(solution)/shard_map/tail/pallas_call | solution.py:467
  118.3 3.0 %collective-permute-done.21.refs_2_ = bf16[512,512]{1,0:T(8,128)(2,1)S(1)} collective-permute-done((bf16[512,512]{1,0:T(8,128)(2,1)S(1)}, bf16[512,512]{1,0:T(8,128)(2,1)S(1)}, u32[]{:S(2)}, u32[]{:S(2)}) %collective-permute-start.21) | collective-permute-done | bytes 524320 | tf_op jit(solution)/shard_map/ppermute | solution.py:512
  123.5 2.2 %add_convert_fusion = bf16[512,512]{1,0:T(8,128)(2,1)} fusion(f32[512,512]{1,0:T(8,128)} %get-tuple-element.221, bf16[512,512]{1,0:T(8,128)(2,1)S(1)} %copy-done.17), kind=kLoop, calls=%fused_computation.2 | loop fusion | flops 786432 | bytes 2097152 | tf_op jit(solution)/shard_map/convert_element_type | solution.py:698
  126.8 2.2 %combine.3 = (f32[80,1024]{1,0:T(8,128)S(1)}, f32[80,1024]{1,0:T(8,128)}, f32[80,1024]{1,0:T(8,128)}, f32[80,1024]{1,0:T(8,128)}) custom-call(s32[1]{0:T(128)} %bitcast.1.place_ref, f32[320,1024]{1,0:T(8,128)S(1)} %copy-done, f32[320,512]{1,0:T(8,128)S(1)} %collective-permute-done.23.refs_1_, f32[320,512]{1,0:T(8,128)} %collective-permute-done.24.refs_2_), custom_call_target="tpu_custom_call" | custom-call | flops 1000 | bytes 5000 | tf_op jit(solution)/shard_map/combine/pallas_call | solution.py:328
  134.8 1.6 collective-permute-start.29
  136.4 3.7 %mixed.1 = bf16[864,1024]{1,0:T(8,128)(2,1)} custom-call(bf16[1728,1024]{1,0:T(8,128)(2,1)} %get-tuple-element.178.refs_0_, bf16[1728,1024]{1,0:T(8,128)(2,1)} %get-tuple-element.219.refs_1_, bf16[1024,1024]{1,0:T(8,128)(2,1)} %get-tuple-element.179.refs_1_.refs_2_, bf16[1024,1024]{1,0:T(8,128)(2,1)} %get-tuple-element.220.refs_3_), custom_call_target="tpu_custom_call" | custom-call | flops 2000000 | bytes 5000 | tf_op jit(solution)/shard_map/mixed/pallas_call | solution.py:413
  140.1 7.8 %collective-permute-done.28.refs_2_ = bf16[512,512]{1,0:T(8,128)(2,1)} collective-permute-done((bf16[512,512]{1,0:T(8,128)(2,1)}, bf16[512,512]{1,0:T(8,128)(2,1)}, u32[]{:S(2)}, u32[]{:S(2)}) %collective-permute-start.28) | collective-permute-done | bytes 524320 | tf_op jit(solution)/shard_map/ppermute | solution.py:512
  149.7 4.1 %collective-permute-done.25.refs_1_ = f32[80,1024]{1,0:T(8,128)S(1)} collective-permute-done((f32[80,1024]{1,0:T(8,128)}, f32[80,1024]{1,0:T(8,128)S(1)}, u32[]{:S(2)}, u32[]{:S(2)}) %collective-permute-start.25) | collective-permute-done | bytes 327712 | tf_op jit(solution)/shard_map/ppermute | solution.py:512
  153.8 1.6 collective-permute-start.35
  155.4 1.5 collective-permute-start.34
  158.1 2.9 %collective-permute-start.31 = (f32[80,256]{1,0:T(8,128)S(1)}, f32[80,256]{1,0:T(8,128)S(1)}, u32[]{:S(2)}, u32[]{:S(2)}) collective-permute-start(f32[80,256]{1,0:T(8,128)S(1)} %get-tuple-element.244), channel_id=1, source_target_pairs={{0,16},{4,20},{8,24},{12,28},{16,0},{20,4},{24,8},{28,12},{1,17},{... | collective-permute-start | bytes 245768 | tf_op jit(solution)/shard_map/ppermute | solution.py:512
  162.2 1.5 collective-permute-start.32
  163.7 5.5 %layer_output.1 = bf16[864,1024]{1,0:T(8,128)(2,1)} custom-call(s32[3,6]{1,0:T(4,128)} %bitcast.30, bf16[864,1024]{1,0:T(8,128)(2,1)} %copy-done.15, bf16[864,1024]{1,0:T(8,128)(2,1)} %bitcast.23, bf16[1728,1024]{1,0:T(8,128)(2,1)} %get-tuple-element.178.refs_0_, bf16[1728,1024]{1,0:T(8,128)(2,1)} %get-tuple-element.219.refs_1_, ...), custom_call_target="tpu_custom_call" | custom-call | flops 5000000 | bytes 10000 | tf_op jit(solution)/shard_map/layer_output/pallas_call | solution.py:498
  169.3 2.8 %collective-permute-start.40 = (bf16[128,512]{1,0:T(8,128)(2,1)S(1)}, bf16[128,512]{1,0:T(8,128)(2,1)S(1)}, u32[]{:S(2)}, u32[]{:S(2)}) collective-permute-start(bf16[128,512]{1,0:T(8,128)(2,1)S(1)} %copy-done.12), channel_id=1, source_target_pairs={{0,16},{4,20},{8,24},{12,28},{16,0},{20,4},{24,8},{28,12},{1,17},{... | collective-permute-start | bytes 393224 | tf_op jit(solution)/shard_map/ppermute | solution.py:512
  172.4 2.8 %collective-permute-start.37 = (bf16[80,256]{1,0:T(8,128)(2,1)S(1)}, bf16[80,256]{1,0:T(8,128)(2,1)S(1)}, u32[]{:S(2)}, u32[]{:S(2)}) collective-permute-start(bf16[80,256]{1,0:T(8,128)(2,1)S(1)} %get-tuple-element.291), channel_id=1, source_target_pairs={{0,16},{4,20},{8,24},{12,28},{16,0},{20,4},{24,8},{28,12},{1,17},{... | collective-permute-start | bytes 122888 | tf_op jit(solution)/shard_map/ppermute | solution.py:512
  176.7 2.2 %collective-permute-done.40.refs_6_ = bf16[128,512]{1,0:T(8,128)(2,1)S(1)} collective-permute-done((bf16[128,512]{1,0:T(8,128)(2,1)S(1)}, bf16[128,512]{1,0:T(8,128)(2,1)S(1)}, u32[]{:S(2)}, u32[]{:S(2)}) %collective-permute-start.40) | collective-permute-done | bytes 131104 | tf_op jit(solution)/shard_map/ppermute | solution.py:512
  178.9 2.8 %collective-permute-done.39.refs_5_ = f32[128,512]{1,0:T(8,128)S(1)} collective-permute-done((f32[128,512]{1,0:T(8,128)S(1)}, f32[128,512]{1,0:T(8,128)S(1)}, u32[]{:S(2)}, u32[]{:S(2)}) %collective-permute-start.39) | collective-permute-done | bytes 262176 | tf_op jit(solution)/shard_map/ppermute | solution.py:512
  186.4 2.3 %collective-permute-start.44 = (bf16[128,512]{1,0:T(8,128)(2,1)S(1)}, bf16[128,512]{1,0:T(8,128)(2,1)S(1)}, u32[]{:S(2)}, u32[]{:S(2)}) collective-permute-start(bf16[128,512]{1,0:T(8,128)(2,1)S(1)} %get-tuple-element.275), channel_id=1, source_target_pairs={{0,24},{4,28},{8,16},{12,20},{16,8},{20,12},{24,0},{28,4},{1,25},{... | collective-permute-start | bytes 393224 | tf_op jit(solution)/shard_map/ppermute | solution.py:512
  188.8 4.4 %collective-permute-done.44.refs_7_ = bf16[128,512]{1,0:T(8,128)(2,1)S(1)} collective-permute-done((bf16[128,512]{1,0:T(8,128)(2,1)S(1)}, bf16[128,512]{1,0:T(8,128)(2,1)S(1)}, u32[]{:S(2)}, u32[]{:S(2)}) %collective-permute-start.44) | collective-permute-done | bytes 131104 | tf_op jit(solution)/shard_map/ppermute | solution.py:512
  (135 shorter events, 44.6 us)
Async XLA Ops:
  2.3 11.2 %collective-permute-start.1 = (bf16[128,1024]{1,0:T(8,128)(2,1)}, bf16[128,1024]{1,0:T(8,128)(2,1)}, u32[]{:S(2)}, u32[]{:S(2)}) collective-permute-start(bf16[128,1024]{1,0:T(8,128)(2,1)} %pack_weights.1.refs_2_), channel_id=1, source_target_pairs={{0,2},{1,3},{2,0},{3,1},{4,6},{5,7},{6,4},{7,5},{8,10},{9,11},{10,... | collective-permute-start | bytes 786440 | tf_op jit(solution)/shard_map/ppermute | solution.py:512
  5.3 8.3 %collective-permute-start = (s32[3,6]{1,0:T(4,128)}, s32[3,6]{1,0:T(4,128)S(1)}, u32[]{:S(2)}, u32[]{:S(2)}) collective-permute-start(s32[3,6]{1,0:T(4,128)} %bitcast.28), channel_id=1, source_target_pairs={{0,1},{1,0},{2,3},{3,2},{4,5},{5,4},{6,7},{7,6},{8,9},{9,8},{10,11... | collective-permute-start | bytes 224 | tf_op jit(solution)/shard_map/ppermute | solution.py:512
  13.6 10.4 %collective-permute-start.4 = (bf16[2,864,1024]{2,1,0:T(8,128)(2,1)}, bf16[2,864,1024]{2,1,0:T(8,128)(2,1)S(1)}, u32[]{:S(2)}, u32[]{:S(2)}) collective-permute-start(bf16[2,864,1024]{2,1,0:T(8,128)(2,1)} %bitcast.16), channel_id=1, source_target_pairs={{0,1},{1,0},{2,3},{3,2},{4,5},{5,4},{6,7},{7,6},{8,9},{9,8},{10,11... | collective-permute-start | bytes 10616840 | tf_op jit(solution)/shard_map/ppermute | solution.py:512
  14.2 8.5 %collective-permute-start.2 = (bf16[128,1024]{1,0:T(8,128)(2,1)}, bf16[128,1024]{1,0:T(8,128)(2,1)S(1)}, u32[]{:S(2)}, u32[]{:S(2)}) collective-permute-start(bf16[128,1024]{1,0:T(8,128)(2,1)} %collective-permute-done.1.refs_0_), channel_id=1, source_target_pairs={{0,8},{8,16},{16,24},{24,28},{28,20},{20,12},{12,4},{4,0},{1,9},{9... | collective-permute-start | bytes 786440 | tf_op jit(solution)/shard_map/ppermute | solution.py:528
  26.1 9.1 %collective-permute-start.9 = (bf16[128,1024]{1,0:T(8,128)(2,1)S(1)}, bf16[128,1024]{1,0:T(8,128)(2,1)}, u32[]{:S(2)}, u32[]{:S(2)}) collective-permute-start(bf16[128,1024]{1,0:T(8,128)(2,1)S(1)} %collective-permute-done.2.refs_1_), channel_id=1, source_target_pairs={{0,2},{1,3},{2,0},{3,1},{4,6},{5,7},{6,4},{7,5},{8,10},{9,11},{10,... | collective-permute-start | bytes 786440 | tf_op jit(solution)/shard_map/ppermute | solution.py:512
  34.6 10.3 %collective-permute-start.11 = (bf16[128,1024]{1,0:T(8,128)(2,1)S(1)}, bf16[128,1024]{1,0:T(8,128)(2,1)}, u32[]{:S(2)}, u32[]{:S(2)}) collective-permute-start(bf16[128,1024]{1,0:T(8,128)(2,1)S(1)} %collective-permute-done.5.refs_2_), channel_id=1, source_target_pairs={{0,2},{1,3},{2,0},{3,1},{4,6},{5,7},{6,4},{7,5},{8,10},{9,11},{10,... | collective-permute-start | bytes 786440 | tf_op jit(solution)/shard_map/ppermute | solution.py:512
  42.4 29.2 %collective-permute-start.14 = (bf16[128,1024]{1,0:T(8,128)(2,1)S(1)}, bf16[128,1024]{1,0:T(8,128)(2,1)}, u32[]{:S(2)}, u32[]{:S(2)}) collective-permute-start(bf16[128,1024]{1,0:T(8,128)(2,1)S(1)} %collective-permute-done.3.refs_5_), channel_id=1, source_target_pairs={{0,2},{1,3},{2,0},{3,1},{4,6},{5,7},{6,4},{7,5},{8,10},{9,11},{10,... | collective-permute-start | bytes 786440 | tf_op jit(solution)/shard_map/ppermute | solution.py:512
  42.9 28.7 %collective-permute-start.15 = (bf16[128,1024]{1,0:T(8,128)(2,1)}, bf16[128,1024]{1,0:T(8,128)(2,1)}, u32[]{:S(2)}, u32[]{:S(2)}) collective-permute-start(bf16[128,1024]{1,0:T(8,128)(2,1)} %collective-permute-done.6.refs_6_), channel_id=1, source_target_pairs={{0,2},{1,3},{2,0},{3,1},{4,6},{5,7},{6,4},{7,5},{8,10},{9,11},{10,... | collective-permute-start | bytes 786440 | tf_op jit(solution)/shard_map/ppermute | solution.py:512
  44.4 27.2 %collective-permute-start.12 = (bf16[128,1024]{1,0:T(8,128)(2,1)}, bf16[128,1024]{1,0:T(8,128)(2,1)}, u32[]{:S(2)}, u32[]{:S(2)}) collective-permute-start(bf16[128,1024]{1,0:T(8,128)(2,1)} %collective-permute-done.7.refs_3_), channel_id=1, source_target_pairs={{0,2},{1,3},{2,0},{3,1},{4,6},{5,7},{6,4},{7,5},{8,10},{9,11},{10,... | collective-permute-start | bytes 786440 | tf_op jit(solution)/shard_map/ppermute | solution.py:512
  47.6 24.1 %collective-permute-start.13 = (bf16[128,1024]{1,0:T(8,128)(2,1)}, bf16[128,1024]{1,0:T(8,128)(2,1)}, u32[]{:S(2)}, u32[]{:S(2)}) collective-permute-start(bf16[128,1024]{1,0:T(8,128)(2,1)} %collective-permute-done.10.refs_4_), channel_id=1, source_target_pairs={{0,2},{1,3},{2,0},{3,1},{4,6},{5,7},{6,4},{7,5},{8,10},{9,11},{10,... | collective-permute-start | bytes 786440 | tf_op jit(solution)/shard_map/ppermute | solution.py:512
  48.1 23.6 %collective-permute-start.16 = (bf16[128,1024]{1,0:T(8,128)(2,1)}, bf16[128,1024]{1,0:T(8,128)(2,1)}, u32[]{:S(2)}, u32[]{:S(2)}) collective-permute-start(bf16[128,1024]{1,0:T(8,128)(2,1)} %collective-permute-done.8.refs_7_), channel_id=1, source_target_pairs={{0,2},{1,3},{2,0},{3,1},{4,6},{5,7},{6,4},{7,5},{8,10},{9,11},{10,... | collective-permute-start | bytes 786440 | tf_op jit(solution)/shard_map/ppermute | solution.py:512
  71.7 33.8 %collective-permute-start.17 = (bf16[512,512]{1,0:T(8,128)(2,1)}, bf16[512,512]{1,0:T(8,128)(2,1)S(1)}, u32[]{:S(2)}, u32[]{:S(2)}) collective-permute-start(bf16[512,512]{1,0:T(8,128)(2,1)} %get-tuple-element.195), channel_id=1, source_target_pairs={{0,2},{1,3},{2,0},{3,1},{4,6},{5,7},{6,4},{7,5},{8,10},{9,11},{10,... | collective-permute-start | bytes 1572872 | tf_op jit(solution)/shard_map/ppermute | solution.py:512
  72.2 33.2 %collective-permute-start.18 = (bf16[512,512]{1,0:T(8,128)(2,1)}, bf16[512,512]{1,0:T(8,128)(2,1)S(1)}, u32[]{:S(2)}, u32[]{:S(2)}) collective-permute-start(bf16[512,512]{1,0:T(8,128)(2,1)} %get-tuple-element.196), channel_id=1, source_target_pairs={{0,2},{1,3},{2,0},{3,1},{4,6},{5,7},{6,4},{7,5},{8,10},{9,11},{10,... | collective-permute-start | bytes 1572872 | tf_op jit(solution)/shard_map/ppermute | solution.py:512
  73.8 31.7 %collective-permute-start.19 = (bf16[512,512]{1,0:T(8,128)(2,1)}, bf16[512,512]{1,0:T(8,128)(2,1)S(1)}, u32[]{:S(2)}, u32[]{:S(2)}) collective-permute-start(bf16[512,512]{1,0:T(8,128)(2,1)} %get-tuple-element.197), channel_id=1, source_target_pairs={{0,2},{1,3},{2,0},{3,1},{4,6},{5,7},{6,4},{7,5},{8,10},{9,11},{10,... | collective-permute-start | bytes 1572872 | tf_op jit(solution)/shard_map/ppermute | solution.py:512
  107.0 14.3 %collective-permute-start.21 = (bf16[512,512]{1,0:T(8,128)(2,1)S(1)}, bf16[512,512]{1,0:T(8,128)(2,1)S(1)}, u32[]{:S(2)}, u32[]{:S(2)}) collective-permute-start(bf16[512,512]{1,0:T(8,128)(2,1)S(1)} %add_convert_fusion.1), channel_id=1, source_target_pairs={{0,4},{4,0},{8,12},{12,8},{16,20},{20,16},{24,28},{28,24},{1,5},{5... | collective-permute-start | bytes 1572872 | tf_op jit(solution)/shard_map/ppermute | solution.py:512
  107.6 14.6 %collective-permute-start.22 = (bf16[512,512]{1,0:T(8,128)(2,1)}, bf16[512,512]{1,0:T(8,128)(2,1)S(1)}, u32[]{:S(2)}, u32[]{:S(2)}) collective-permute-start(bf16[512,512]{1,0:T(8,128)(2,1)} %get-tuple-element.209), channel_id=1, source_target_pairs={{0,2},{1,3},{2,0},{3,1},{4,6},{5,7},{6,4},{7,5},{8,10},{9,11},{10,... | collective-permute-start | bytes 1572872 | tf_op jit(solution)/shard_map/ppermute | solution.py:512
  125.7 22.1 %collective-permute-start.28 = (bf16[512,512]{1,0:T(8,128)(2,1)}, bf16[512,512]{1,0:T(8,128)(2,1)}, u32[]{:S(2)}, u32[]{:S(2)}) collective-permute-start(bf16[512,512]{1,0:T(8,128)(2,1)} %add_convert_fusion), channel_id=1, source_target_pairs={{0,4},{4,0},{8,12},{12,8},{16,20},{20,16},{24,28},{28,24},{1,5},{5... | collective-permute-start | bytes 1572872 | tf_op jit(solution)/shard_map/ppermute | solution.py:512
  129.8 24.1 %collective-permute-start.25 = (f32[80,1024]{1,0:T(8,128)}, f32[80,1024]{1,0:T(8,128)S(1)}, u32[]{:S(2)}, u32[]{:S(2)}) collective-permute-start(f32[80,1024]{1,0:T(8,128)} %get-tuple-element.216), channel_id=1, source_target_pairs={{0,4},{4,0},{8,12},{12,8},{16,20},{20,16},{24,28},{28,24},{1,5},{5... | collective-permute-start | bytes 983048 | tf_op jit(solution)/shard_map/ppermute | solution.py:512
  130.7 23.1 %collective-permute-start.26 = (f32[80,1024]{1,0:T(8,128)}, f32[80,1024]{1,0:T(8,128)S(1)}, u32[]{:S(2)}, u32[]{:S(2)}) collective-permute-start(f32[80,1024]{1,0:T(8,128)} %get-tuple-element.217), channel_id=1, source_target_pairs={{0,2},{1,3},{2,0},{3,1},{4,6},{5,7},{6,4},{7,5},{8,10},{9,11},{10,... | collective-permute-start | bytes 983048 | tf_op jit(solution)/shard_map/ppermute | solution.py:577
  132.2 21.6 %collective-permute-start.27 = (f32[80,1024]{1,0:T(8,128)}, f32[80,1024]{1,0:T(8,128)}, u32[]{:S(2)}, u32[]{:S(2)}) collective-permute-start(f32[80,1024]{1,0:T(8,128)} %get-tuple-element.218), channel_id=1, source_target_pairs={{0,6},{1,7},{2,4},{3,5},{4,2},{5,3},{6,0},{7,1},{8,14},{9,15},{10,... | collective-permute-start | bytes 983048 | tf_op jit(solution)/shard_map/ppermute | solution.py:577
  134.8 13.1 %collective-permute-start.29 = (bf16[128,512]{1,0:T(8,128)(2,1)}, bf16[128,512]{1,0:T(8,128)(2,1)S(1)}, u32[]{:S(2)}, u32[]{:S(2)}) collective-permute-start(bf16[128,512]{1,0:T(8,128)(2,1)} %get-tuple-element.231), channel_id=1, source_target_pairs={{0,16},{4,20},{8,24},{12,28},{16,0},{20,4},{24,8},{28,12},{1,17},{... | collective-permute-start | bytes 393224 | tf_op jit(solution)/shard_map/ppermute | solution.py:512
  153.8 15.5 %collective-permute-start.35 = (f32[128,512]{1,0:T(8,128)S(1)}, f32[128,512]{1,0:T(8,128)S(1)}, u32[]{:S(2)}, u32[]{:S(2)}) collective-permute-start(f32[128,512]{1,0:T(8,128)S(1)} %copy-done.10), channel_id=1, source_target_pairs={{0,8},{4,12},{8,0},{12,4},{16,24},{20,28},{24,16},{28,20},{1,9},{5... | collective-permute-start | bytes 786440 | tf_op jit(solution)/shard_map/ppermute | solution.py:512
  155.4 13.8 %collective-permute-start.34 = (bf16[128,512]{1,0:T(8,128)(2,1)}, bf16[128,512]{1,0:T(8,128)(2,1)S(1)}, u32[]{:S(2)}, u32[]{:S(2)}) collective-permute-start(bf16[128,512]{1,0:T(8,128)(2,1)} %get-tuple-element.249), channel_id=1, source_target_pairs={{0,24},{4,28},{8,16},{12,20},{16,8},{20,12},{24,0},{28,4},{1,25},{... | collective-permute-start | bytes 393224 | tf_op jit(solution)/shard_map/ppermute | solution.py:512
  158.0 14.2 %collective-permute-start.30 = (f32[80,256]{1,0:T(8,128)S(1)}, f32[80,256]{1,0:T(8,128)S(1)}, u32[]{:S(2)}, u32[]{:S(2)}) collective-permute-start(f32[80,256]{1,0:T(8,128)S(1)} %get-tuple-element.243), channel_id=1, source_target_pairs={{0,8},{4,12},{8,0},{12,4},{16,24},{20,28},{24,16},{28,20},{1,9},{5... | collective-permute-start | bytes 245768 | tf_op jit(solution)/shard_map/ppermute | solution.py:512
  158.1 14.1 %collective-permute-start.31 = (f32[80,256]{1,0:T(8,128)S(1)}, f32[80,256]{1,0:T(8,128)S(1)}, u32[]{:S(2)}, u32[]{:S(2)}) collective-permute-start(f32[80,256]{1,0:T(8,128)S(1)} %get-tuple-element.244), channel_id=1, source_target_pairs={{0,16},{4,20},{8,24},{12,28},{16,0},{20,4},{24,8},{28,12},{1,17},{... | collective-permute-start | bytes 245768 | tf_op jit(solution)/shard_map/ppermute | solution.py:512
  162.2 10.0 %collective-permute-start.32 = (f32[80,256]{1,0:T(8,128)S(1)}, f32[80,256]{1,0:T(8,128)S(1)}, u32[]{:S(2)}, u32[]{:S(2)}) collective-permute-start(f32[80,256]{1,0:T(8,128)S(1)} %get-tuple-element.245), channel_id=1, source_target_pairs={{0,24},{4,28},{8,16},{12,20},{16,8},{20,12},{24,0},{28,4},{1,25},{... | collective-permute-start | bytes 245768 | tf_op jit(solution)/shard_map/ppermute | solution.py:512
  169.2 12.5 %collective-permute-start.39 = (f32[128,512]{1,0:T(8,128)S(1)}, f32[128,512]{1,0:T(8,128)S(1)}, u32[]{:S(2)}, u32[]{:S(2)}) collective-permute-start(f32[128,512]{1,0:T(8,128)S(1)} %get-tuple-element.261), channel_id=1, source_target_pairs={{0,8},{4,12},{8,0},{12,4},{16,24},{20,28},{24,16},{28,20},{1,9},{5... | collective-permute-start | bytes 786440 | tf_op jit(solution)/shard_map/ppermute | solution.py:512
  169.3 9.6 %collective-permute-start.40 = (bf16[128,512]{1,0:T(8,128)(2,1)S(1)}, bf16[128,512]{1,0:T(8,128)(2,1)S(1)}, u32[]{:S(2)}, u32[]{:S(2)}) collective-permute-start(bf16[128,512]{1,0:T(8,128)(2,1)S(1)} %copy-done.12), channel_id=1, source_target_pairs={{0,16},{4,20},{8,24},{12,28},{16,0},{20,4},{24,8},{28,12},{1,17},{... | collective-permute-start | bytes 393224 | tf_op jit(solution)/shard_map/ppermute | solution.py:512
  172.2 10.1 %collective-permute-start.36 = (bf16[80,256]{1,0:T(8,128)(2,1)S(1)}, bf16[80,256]{1,0:T(8,128)(2,1)S(1)}, u32[]{:S(2)}, u32[]{:S(2)}) collective-permute-start(bf16[80,256]{1,0:T(8,128)(2,1)S(1)} %get-tuple-element.291), channel_id=1, source_target_pairs={{0,8},{4,12},{8,0},{12,4},{16,24},{20,28},{24,16},{28,20},{1,9},{5... | collective-permute-start | bytes 122888 | tf_op jit(solution)/shard_map/ppermute | solution.py:512
  172.4 9.9 %collective-permute-start.37 = (bf16[80,256]{1,0:T(8,128)(2,1)S(1)}, bf16[80,256]{1,0:T(8,128)(2,1)S(1)}, u32[]{:S(2)}, u32[]{:S(2)}) collective-permute-start(bf16[80,256]{1,0:T(8,128)(2,1)S(1)} %get-tuple-element.291), channel_id=1, source_target_pairs={{0,16},{4,20},{8,24},{12,28},{16,0},{20,4},{24,8},{28,12},{1,17},{... | collective-permute-start | bytes 122888 | tf_op jit(solution)/shard_map/ppermute | solution.py:512
  182.8 10.4 %collective-permute-start.41 = (bf16[80,1024]{1,0:T(8,128)(2,1)S(1)}, bf16[80,1024]{1,0:T(8,128)(2,1)S(1)}, u32[]{:S(2)}, u32[]{:S(2)}) collective-permute-start(bf16[80,1024]{1,0:T(8,128)(2,1)S(1)} %constant_dynamic-update-slice_fusion.4), channel_id=1, source_target_pairs={{0,4},{4,0},{8,12},{12,8},{16,20},{20,16},{24,28},{28,24},{1,5},{5... | collective-permute-start | bytes 491528 | tf_op jit(solution)/shard_map/ppermute | solution.py:512
  184.0 9.3 %collective-permute-start.42 = (bf16[80,1024]{1,0:T(8,128)(2,1)S(1)}, bf16[80,1024]{1,0:T(8,128)(2,1)S(1)}, u32[]{:S(2)}, u32[]{:S(2)}) collective-permute-start(bf16[80,1024]{1,0:T(8,128)(2,1)S(1)} %constant_dynamic-update-slice_fusion.4), channel_id=1, source_target_pairs={{0,2},{1,3},{2,0},{3,1},{4,6},{5,7},{6,4},{7,5},{8,10},{9,11},{10,... | collective-permute-start | bytes 491528 | tf_op jit(solution)/shard_map/ppermute | solution.py:577
  (37 other events, 305.6 us)
